TPU v7x, 32 devices: a whole 2x2x4 slice. The times are simulated.
32 devices in a mesh: groups: 2 (over y), mesh: 4 (over z), mp: 2 (over x), batch: 2 (over core).
Axes of the slice: x: 2, y: 2, z: 4, core: 2. Of those that a mesh axis runs over, the one named last changes fastest.
Arguments:
- g_nodes: bfloat16 [4, 4096, 512], P(('groups', 'batch'), 'mesh', 'mp'), parts along dimension 0, may hold values from -6 to 6
- r_nodes: bfloat16 [4, 4096, 512], P(('groups', 'batch'), 'mesh', 'mp'), parts along dimension 0, may hold values from -6 to 6
- g_nbr: int32 [4096, 8], P('mesh'), may hold values from 0 to 2047, as said below
- g_count: int32 [4096], P('mesh'), may hold values from 1 to 8
- r_nbr: int32 [4096, 8], P('mesh'), may hold values from 0 to 2047, as said below
- r_count: int32 [4096], P('mesh'), may hold values from 1 to 8
- bnd_src: int32 [2048], P('mesh'), may hold values from 0 to 1023
- bnd_part: int32 [2048, 1], P('mesh'), may hold values from 0 to 3; in each aligned block of 512 rows (0 to 511, 512 to 1023, ...) at most 256 rows name the same one
- bnd_node: int32 [2048], P('mesh'), may hold values from 0 to 1023
- g_ws: bfloat16 [2, 512, 512], P(None, None, 'mp'), may hold values from -0.25 to 0.25
- g_wd: bfloat16 [2, 512, 512], P(None, None, 'mp'), may hold values from -0.25 to 0.25
- g_b1: bfloat16 [2, 512], P(None, 'mp'), may hold values from -4 to 4
- g_w2: bfloat16 [2, 512, 512], P(None, 'mp'), may hold values from -0.09375 to 0.09375
- r_ws: bfloat16 [2, 512, 512], P(None, None, 'mp'), may hold values from -0.25 to 0.25
- r_wd: bfloat16 [2, 512, 512], P(None, None, 'mp'), may hold values from -0.25 to 0.25
- r_b1: bfloat16 [2, 512], P(None, 'mp'), may hold values from -4 to 4
- r_w2: bfloat16 [2, 512, 512], P(None, 'mp'), may hold values from -0.09375 to 0.09375
Outputs:
- g_out: bfloat16 [4, 4096, 512], P(('groups', 'batch'), 'mesh', 'mp'), parts along dimension 0
- r_out: bfloat16 [4, 4096, 512], P(('groups', 'batch'), 'mesh', 'mp'), parts along dimension 0
There are 2 independent parts, one for each index of `groups`. A program takes and returns all parts, laid end to end along the dimension named above; an argument that names none is the same for every part. Nothing has to cross between parts.
Inputs may be any that keep to these rules, and one draw needn't show every extreme that they name: `g_nbr`: row i of partition m points into the padded block of m at a row within 512 of its own row i + 512; both ends of the range are used. `r_nbr`: row i of partition m points into the padded block of m at a row within 512 of its own row i + 512; both ends of the range are used. `bnd_part`: among the boundary-zone rows of one partition, no regional partition is named by more than 256 rows, a bound that some block reaches.
All inputs are finite; a program needn't handle non-finite values.
Results may differ from a plain program's by a relative error of at most 0.015.
Values may be sent and summed in bfloat16 or wider, within the bound.
No kernel may reach another device: no remote copies, remote signals or barrier semaphores. Data moves between devices by JAX's collectives and lax.ppermute only.
A program may use at most 64 MiB of HBM per device.

v0:
```python
import jax
import jax.numpy as jnp
from jax import lax
from jax.sharding import PartitionSpec as P


def padded_2(shard, sides, width):
    for axis, dim in sides:
        size, length = (lax.axis_size(axis), shard.shape[dim])
        up = [(i, (i + 1) % size) for i in range(size)]
        down = [(j, i) for i, j in up]
        last = lax.slice_in_dim(shard, length - width, length, axis=dim)
        leading = lax.slice_in_dim(shard, 0, width, axis=dim)
        before = lax.ppermute(last, axis, up)
        after = lax.ppermute(leading, axis, down)
        shard = jnp.concatenate([before, shard, after], axis=dim)
    return shard


def edge_sums(proj, near, nbr, count):
    slots = nbr.shape[1]
    live = jnp.arange(slots, dtype=jnp.int32)[None, :] < count[:, None]
    pre = proj[:, nbr].astype(jnp.float32) + near[:, :, None]
    acts = jnp.where(live[None, :, :, None], jax.nn.silu(pre), 0.0)
    return jnp.sum(acts, axis=2).astype(jnp.bfloat16)


def clear_ends(padded, rows, rim, wrap):
    if wrap:
        return padded
    mine = lax.axis_index("mesh")
    parts = lax.axis_size("mesh")
    place = jnp.arange(padded.shape[1], dtype=jnp.int32)
    dropped = (place < rim) & (mine == 0) | (place >= rim + rows) & (mine == parts - 1)
    return jnp.where(dropped[None, :, None], jnp.zeros((), padded.dtype), padded)


def graph_layer(latent, nbr, count, w_send, w_recv, bias, w_out, wrap):
    rows = latent.shape[1]
    rim = rows // 2
    own_full = lax.all_gather(latent, "mp", axis=2, tiled=True)
    padded_full = padded_2(own_full, (("mesh", 1),), rim)
    padded_full = clear_ends(padded_full, rows, rim, wrap)
    proj = jnp.dot(padded_full, w_send, preferred_element_type=jnp.float32).astype(jnp.bfloat16)
    near = jnp.dot(own_full, w_recv, preferred_element_type=jnp.float32) + bias.astype(jnp.float32)
    summed = edge_sums(proj, near, nbr, count)
    partial_prod = jnp.dot(summed, w_out, preferred_element_type=jnp.float32)
    update = lax.psum_scatter(
        partial_prod.astype(jnp.bfloat16), "mp", scatter_dimension=2, tiled=True
    ).astype(jnp.float32)
    return (latent.astype(jnp.float32) + update).astype(jnp.bfloat16)


def on_device(
    g_nodes,
    r_nodes,
    g_nbr,
    g_count,
    r_nbr,
    r_count,
    bnd_src,
    bnd_part,
    bnd_node,
    g_ws,
    g_wd,
    g_b1,
    g_w2,
    r_ws,
    r_wd,
    r_b1,
    r_w2,
):
    batch_rows, reg_rows, feats = r_nodes.shape
    dest = bnd_part[:, 0]
    outgoing = jnp.moveaxis(g_nodes[:, bnd_src], 1, 0)
    init = jnp.zeros((reg_rows + 1, batch_rows, feats), jnp.float32)
    target = dest * reg_rows + bnd_node
    mine = lax.axis_index("mesh")
    piece_rows = lax.all_gather(outgoing, "mesh", axis=0, tiled=True)
    piece_target = lax.all_gather(target, "mesh", axis=0, tiled=True)
    local = jnp.where(piece_target // reg_rows == mine, piece_target % reg_rows + 1, 0)
    landed = init.at[local].add(piece_rows.astype(jnp.float32))
    force = jnp.moveaxis(landed[1:], 1, 0)
    regional = (r_nodes.astype(jnp.float32) + force).astype(jnp.bfloat16)
    planet = g_nodes
    for layer in range(g_ws.shape[0]):
        planet = graph_layer(
            planet, g_nbr, g_count, g_ws[layer], g_wd[layer], g_b1[layer], g_w2[layer], True
        )
    for layer in range(r_ws.shape[0]):
        regional = graph_layer(
            regional, r_nbr, r_count, r_ws[layer], r_wd[layer], r_b1[layer], r_w2[layer], False
        )
    return (planet, regional)


def solution(mesh):
    in_specs = (
        P(("groups", "batch"), "mesh", "mp"),
        P(("groups", "batch"), "mesh", "mp"),
        P("mesh", None),
        P("mesh"),
        P("mesh", None),
        P("mesh"),
        P("mesh"),
        P("mesh", None),
        P("mesh"),
        P(None, None, "mp"),
        P(None, None, "mp"),
        P(None, "mp"),
        P(None, "mp", None),
        P(None, None, "mp"),
        P(None, None, "mp"),
        P(None, "mp"),
        P(None, "mp", None),
    )
    out_specs = (P(("groups", "batch"), "mesh", "mp"), P(("groups", "batch"), "mesh", "mp"))
    return jax.shard_map(
        on_device, mesh=mesh, in_specs=in_specs, out_specs=out_specs, check_vma=False
    )
```

profile of v0, /device:TPU:1, one launch (start us, length us, event | category | flops | bytes accessed | tf_op | source)
XLA Modules:
  0.0 405.5 jit_solution(8681668976846762309)
XLA Ops:
  8.0 3.3 gather_fusion.2
  13.5 10.3 %all-gather.1 = s32[4,1,512]{2,1,0:T(1,128)S(1)} all-gather(s32[1,1,512]{2,1,0:T(1,128)S(1)} %bitcast.108), channel_id=1, replica_groups=mesh['groups'=2,'mesh'=4,'mp'=2,'batch'=2] {'mesh'}, dimensions={0}, use_global_device_ids=true | all-gather | bytes 10240 | tf_op jit(solution)/shard_map/all_gather | solution.py:80
  28.1 13.3 %all-gather.16.cloned.1.call-done = bf16[2048,256]{1,0:T(8,128)(2,1)} async-done(((bf16[512,256]{1,0:T(8,128)(2,1)}), bf16[2048,256]{1,0:T(8,128)(2,1)}) %all-gather.16.cloned.1.call-update) | async-done | bytes 1048592 | tf_op jit(solution)/shard_map/all_gather | solution.py:79
  41.4 13.6 %scatter_custom_fusion = f32[1025,256]{1,0:T(8,128)S(1)} fusion(s32[2048]{0:T(1024)S(1)} %compare_select_fusion.2, bf16[2048,256]{1,0:T(8,128)(2,1)} %all-gather.16.cloned.1.call-done, f32[]{:T(128)} %constant.47.clone.1), kind=kCustom, calls=%fused_computation.64 | custom fusion | flops 1048576 | bytes 2098180 | tf_op jit(solution)/shard_map/scatter-add | solution.py:82
  56.1 7.7 %all-gather.8.cloned.1.call-done = bf16[1,1024,512]{2,1,0:T(8,128)(2,1)} async-done(((bf16[1,1024,256]{2,1,0:T(8,128)(2,1)}), bf16[1,1024,512]{2,1,0:T(8,128)(2,1)}) %all-gather.8.cloned.1.call-update) | async-done | bytes 1048592 | tf_op jit(solution)/shard_map/all_gather | solution.py:41
  63.8 1.4 fusion.110
  65.2 1.3 collective-permute-start
  66.4 2.1 collective-permute-start.1
  68.7 1.7 convolution_add_fusion.3
  70.4 9.5 %collective-permute-done = bf16[1,512,512]{2,1,0:T(8,128)(2,1)S(1)} collective-permute-done((bf16[1,512,512]{2,1,0:T(8,128)(2,1)S(1)}, bf16[1,512,512]{2,1,0:T(8,128)(2,1)S(1)}, u32[]{:S(2)}, u32[]{:S(2)}) %collective-permute-start) | collective-permute-done | bytes 524320 | tf_op jit(solution)/shard_map/ppermute | solution.py:14
  79.9 11.0 %collective-permute-done.1 = bf16[1,512,512]{2,1,0:T(8,128)(2,1)S(1)} collective-permute-done((bf16[1,512,512]{2,1,0:T(8,128)(2,1)S(1)}, bf16[1,512,512]{2,1,0:T(8,128)(2,1)S(1)}, u32[]{:S(2)}, u32[]{:S(2)}) %collective-permute-start.1) | collective-permute-done | bytes 524320 | tf_op jit(solution)/shard_map/ppermute | solution.py:15
  90.9 1.7 convolution_convert_fusion.3
  92.5 33.1 %gather_fusion = bf16[8192,256]{1,0:T(8,128)(2,1)} fusion(bf16[2048,256]{1,0:T(8,128)(2,1)S(1)} %convolution_convert_fusion.3, s32[8192]{0:T(1024)S(1)} %broadcast_clamp_fusion.1), kind=kCustom, calls=%fused_computation | custom fusion | bytes 8421376 | tf_op jit(solution)/shard_map/gather | solution.py:23
  125.7 2.3 fusion.108
  128.0 1.5 collective-permute-start.4
  129.5 1.7 collective-permute-start.5
  131.2 8.1 %fusion.24 = bf16[1024,256]{1,0:T(8,128)(2,1)S(1)} fusion(bf16[8192,256]{1,0:T(8,128)(2,1)} %gather_fusion, f32[1024,256]{1,0:T(8,128)S(1)} %convolution_add_fusion.3, pred[1024,8]{1,0:T(8,128)(4,1)S(1)} %iota_compare_fusion.1), kind=kLoop, calls=%fused_computation.34 | loop fusion | flops 16515072 | bytes 5775360 | tf_op jit(solution)/shard_map/reduce_sum | solution.py:25
  139.3 1.4 fusion.52
  140.9 1.4 convolution_add_fusion.1
  142.4 12.1 %collective-permute-done.5 = bf16[1,512,512]{2,1,0:T(8,128)(2,1)} collective-permute-done((bf16[1,512,512]{2,1,0:T(8,128)(2,1)}, bf16[1,512,512]{2,1,0:T(8,128)(2,1)}, u32[]{:S(2)}, u32[]{:S(2)}) %collective-permute-start.5) | collective-permute-done | bytes 524320 | tf_op jit(solution)/shard_map/ppermute | solution.py:15
  154.5 2.0 convolution_convert_fusion.1
  156.5 33.1 %gather_fusion.3 = bf16[8192,256]{1,0:T(8,128)(2,1)} fusion(bf16[2048,256]{1,0:T(8,128)(2,1)S(1)} %convolution_convert_fusion.1, s32[8192]{0:T(1024)S(1)} %broadcast_clamp_fusion), kind=kCustom, calls=%fused_computation.3 | custom fusion | bytes 8421376 | tf_op jit(solution)/shard_map/gather | solution.py:23
  189.7 8.2 %fusion.26 = bf16[1024,256]{1,0:T(8,128)(2,1)S(1)} fusion(bf16[8192,256]{1,0:T(8,128)(2,1)} %gather_fusion.3, f32[1024,256]{1,0:T(8,128)S(1)} %convolution_add_fusion.1, pred[1024,8]{1,0:T(8,128)(4,1)S(1)} %iota_compare_fusion), kind=kLoop, calls=%fused_computation.36 | loop fusion | flops 16515072 | bytes 5775360 | tf_op jit(solution)/shard_map/reduce_sum | solution.py:25
  197.9 1.4 fusion.54
  199.4 2.0 add_convert_fusion.3
  201.5 17.3 %reduce-scatter.9.cloned.1.call-done = bf16[1,1024,256]{2,1,0:T(8,128)(2,1)} async-done(((bf16[1,1024,512]{2,1,0:T(8,128)(2,1)}), bf16[1,1024,256]{2,1,0:T(8,128)(2,1)}) %reduce-scatter.9.cloned.1.call-update) | async-done | bytes 524304 | tf_op jit(solution)/shard_map/reduce_scatter | solution.py:48
  218.8 2.0 add_convert_fusion.1
  220.8 21.2 %all-gather.10.cloned.1.call-done = bf16[1,1024,512]{2,1,0:T(8,128)(2,1)} async-done(((bf16[1,1024,256]{2,1,0:T(8,128)(2,1)}), bf16[1,1024,512]{2,1,0:T(8,128)(2,1)}) %all-gather.10.cloned.1.call-update) | async-done | bytes 1048592 | tf_op jit(solution)/shard_map/all_gather | solution.py:41
  242.0 1.4 fusion.109
  244.6 2.1 collective-permute-start.3
  246.7 1.7 convolution_add_fusion.2
  248.4 9.7 %collective-permute-done.2 = bf16[1,512,512]{2,1,0:T(8,128)(2,1)S(1)} collective-permute-done((bf16[1,512,512]{2,1,0:T(8,128)(2,1)S(1)}, bf16[1,512,512]{2,1,0:T(8,128)(2,1)S(1)}, u32[]{:S(2)}, u32[]{:S(2)}) %collective-permute-start.2) | collective-permute-done | bytes 524320 | tf_op jit(solution)/shard_map/ppermute | solution.py:14
  258.1 11.0 %collective-permute-done.3 = bf16[1,512,512]{2,1,0:T(8,128)(2,1)S(1)} collective-permute-done((bf16[1,512,512]{2,1,0:T(8,128)(2,1)S(1)}, bf16[1,512,512]{2,1,0:T(8,128)(2,1)S(1)}, u32[]{:S(2)}, u32[]{:S(2)}) %collective-permute-start.3) | collective-permute-done | bytes 524320 | tf_op jit(solution)/shard_map/ppermute | solution.py:15
  269.1 1.6 convolution_convert_fusion.2
  270.7 33.1 %gather_fusion.1 = bf16[8192,256]{1,0:T(8,128)(2,1)} fusion(bf16[2048,256]{1,0:T(8,128)(2,1)S(1)} %convolution_convert_fusion.2, s32[8192]{0:T(1024)S(1)} %broadcast_clamp_fusion.1), kind=kCustom, calls=%fused_computation.1 | custom fusion | bytes 8421376 | tf_op jit(solution)/shard_map/gather | solution.py:23
  303.9 2.3 fusion.107
  306.2 1.5 collective-permute-start.6
  307.7 1.7 collective-permute-start.7
  309.4 8.1 %fusion.25 = bf16[1024,256]{1,0:T(8,128)(2,1)S(1)} fusion(bf16[8192,256]{1,0:T(8,128)(2,1)} %gather_fusion.1, f32[1024,256]{1,0:T(8,128)S(1)} %convolution_add_fusion.2, pred[1024,8]{1,0:T(8,128)(4,1)S(1)} %iota_compare_fusion.1), kind=kLoop, calls=%fused_computation.35 | loop fusion | flops 16515072 | bytes 5775360 | tf_op jit(solution)/shard_map/reduce_sum | solution.py:25
  317.6 1.4 fusion.53
  320.7 12.1 %collective-permute-done.7 = bf16[1,512,512]{2,1,0:T(8,128)(2,1)} collective-permute-done((bf16[1,512,512]{2,1,0:T(8,128)(2,1)}, bf16[1,512,512]{2,1,0:T(8,128)(2,1)}, u32[]{:S(2)}, u32[]{:S(2)}) %collective-permute-start.7) | collective-permute-done | bytes 524320 | tf_op jit(solution)/shard_map/ppermute | solution.py:15
  332.8 2.0 convolution_convert_fusion
  334.8 33.1 %gather_fusion.4 = bf16[8192,256]{1,0:T(8,128)(2,1)} fusion(bf16[2048,256]{1,0:T(8,128)(2,1)S(1)} %convolution_convert_fusion, s32[8192]{0:T(1024)S(1)} %broadcast_clamp_fusion), kind=kCustom, calls=%fused_computation.4 | custom fusion | bytes 8421376 | tf_op jit(solution)/shard_map/gather | solution.py:23
  367.9 8.2 %fusion.27 = bf16[1024,256]{1,0:T(8,128)(2,1)S(1)} fusion(bf16[8192,256]{1,0:T(8,128)(2,1)} %gather_fusion.4, f32[1024,256]{1,0:T(8,128)S(1)} %convolution_add_fusion, pred[1024,8]{1,0:T(8,128)(4,1)S(1)} %iota_compare_fusion), kind=kLoop, calls=%fused_computation.37 | loop fusion | flops 16515072 | bytes 5775360 | tf_op jit(solution)/shard_map/reduce_sum | solution.py:25
  376.1 1.4 fusion.55
  377.6 2.0 add_convert_fusion.2
  379.6 17.4 %reduce-scatter.11.cloned.1.call-done = bf16[1,1024,256]{2,1,0:T(8,128)(2,1)} async-done(((bf16[1,1024,512]{2,1,0:T(8,128)(2,1)}), bf16[1,1024,256]{2,1,0:T(8,128)(2,1)}) %reduce-scatter.11.cloned.1.call-update) | async-done | bytes 524304 | tf_op jit(solution)/shard_map/reduce_scatter | solution.py:48
  397.0 2.0 add_convert_fusion
  (81 shorter events, 11.8 us)
Async XLA Ops:
  7.2 20.7 %copy-start.16 = (s32[1024]{0:T(1024)S(1)}, s32[1024]{0:T(1024)}, u32[]{:S(2)}) copy-start(s32[1024]{0:T(1024)} %param.22) | copy-start | bytes 12292
  7.2 47.8 %copy-start.15 = (bf16[1,1024,256]{2,1,0:T(8,128)(2,1)S(1)}, bf16[1,1024,256]{2,1,0:T(8,128)(2,1)}, u32[]{:S(2)}) copy-start(bf16[1,1024,256]{2,1,0:T(8,128)(2,1)} %param.18) | copy-start | bytes 1572868
  7.2 34.2 %all-gather.16.cloned.1.call-start = ((), (), s32[]{:S(2)}) async-start(), calls=%async_computation.12 | async-start | bytes 1310720 | tf_op jit(solution)/shard_map/all_gather | solution.py:79
  11.3 52.5 %all-gather.8.cloned.1.call-start = ((), (), s32[]{:S(2)}) async-start(), calls=%async_computation.4 | async-start | bytes 1572864 | tf_op jit(solution)/shard_map/all_gather | solution.py:41
  12.1 113.6 %all-gather.12.cloned.1.call-start = ((), (), s32[]{:S(2)}) async-start(), calls=%async_computation.8 | async-start | bytes 1572864 | tf_op jit(solution)/shard_map/all_gather | solution.py:41
  27.3 41.2 %copy-start.17 = (s32[1024]{0:T(1024)S(1)}, s32[1024]{0:T(1024)}, u32[]{:S(2)}) copy-start(s32[1024]{0:T(1024)} %param.20) | copy-start | bytes 12292
  27.3 41.4 %copy-start.8 = (bf16[2,512,256]{2,1,0:T(8,128)(2,1)S(1)}, bf16[2,512,256]{2,1,0:T(8,128)(2,1)}, u32[]{:S(2)}) copy-start(bf16[2,512,256]{2,1,0:T(8,128)(2,1)} %param.27) | copy-start | bytes 1572868
  56.0 143.4 %reduce-scatter.5.cloned.1.call-start = ((), (), s32[]{:S(2)}) async-start(), calls=%async_computation.5 | async-start | bytes 1572864 | tf_op jit(solution)/shard_map/reduce_scatter | solution.py:48
  63.8 27.1 %copy-start.4 = (bf16[1,1024,512]{2,1,0:T(8,128)(2,1)S(1)}, bf16[1,1024,512]{2,1,0:T(8,128)(2,1)}, u32[]{:S(2)}) copy-start(bf16[1,1024,512]{2,1,0:T(8,128)(2,1)} %all-gather.8.cloned.1.call-done) | copy-start | bytes 3145732
  65.2 14.7 %collective-permute-start = (bf16[1,512,512]{2,1,0:T(8,128)(2,1)S(1)}, bf16[1,512,512]{2,1,0:T(8,128)(2,1)S(1)}, u32[]{:S(2)}, u32[]{:S(2)}) collective-permute-start(bf16[1,512,512]{2,1,0:T(8,128)(2,1)S(1)} %get-tuple-element.8), channel_id=1, source_target_pairs={{0,4},{4,8},{8,12},{12,0},{1,5},{5,9},{9,13},{13,1},{2,6},{6,10},{... | collective-permute-start | bytes 1572872 | tf_op jit(solution)/shard_map/ppermute | solution.py:14
  66.4 24.4 %collective-permute-start.1 = (bf16[1,512,512]{2,1,0:T(8,128)(2,1)S(1)}, bf16[1,512,512]{2,1,0:T(8,128)(2,1)S(1)}, u32[]{:S(2)}, u32[]{:S(2)}) collective-permute-start(bf16[1,512,512]{2,1,0:T(8,128)(2,1)S(1)} %get-tuple-element.9), channel_id=1, source_target_pairs={{4,0},{8,4},{12,8},{0,12},{5,1},{9,5},{13,9},{1,13},{6,2},{10,6},{... | collective-permute-start | bytes 1572872 | tf_op jit(solution)/shard_map/ppermute | solution.py:15
  125.7 13.7 %copy-start.10 = (bf16[2,256,512]{2,1,0:T(8,128)(2,1)S(1)}, bf16[2,256,512]{2,1,0:T(8,128)(2,1)}, u32[]{:S(2)}) copy-start(bf16[2,256,512]{2,1,0:T(8,128)(2,1)} %param.29) | copy-start | bytes 1572868
  128.0 14.5 %collective-permute-start.4 = (bf16[1,512,512]{2,1,0:T(8,128)(2,1)}, bf16[1,512,512]{2,1,0:T(8,128)(2,1)}, u32[]{:S(2)}, u32[]{:S(2)}) collective-permute-start(bf16[1,512,512]{2,1,0:T(8,128)(2,1)} %get-tuple-element.4), channel_id=1, source_target_pairs={{0,4},{4,8},{8,12},{12,0},{1,5},{5,9},{9,13},{13,1},{2,6},{6,10},{... | collective-permute-start | bytes 1572872 | tf_op jit(solution)/shard_map/ppermute | solution.py:14
  129.5 11.4 %copy-start.6 = (bf16[1,1024,512]{2,1,0:T(8,128)(2,1)S(1)}, bf16[1,1024,512]{2,1,0:T(8,128)(2,1)}, u32[]{:S(2)}) copy-start(bf16[1,1024,512]{2,1,0:T(8,128)(2,1)} %all-gather.12.cloned.1.call-done) | copy-start | bytes 3145732
  129.5 25.0 %collective-permute-start.5 = (bf16[1,512,512]{2,1,0:T(8,128)(2,1)}, bf16[1,512,512]{2,1,0:T(8,128)(2,1)}, u32[]{:S(2)}, u32[]{:S(2)}) collective-permute-start(bf16[1,512,512]{2,1,0:T(8,128)(2,1)} %get-tuple-element.5), channel_id=1, source_target_pairs={{4,0},{8,4},{12,8},{0,12},{5,1},{9,5},{13,9},{1,13},{6,2},{10,6},{... | collective-permute-start | bytes 1572872 | tf_op jit(solution)/shard_map/ppermute | solution.py:15
  140.8 77.9 %reduce-scatter.9.cloned.1.call-start = ((), (), s32[]{:S(2)}) async-start(), calls=%async_computation.9 | async-start | bytes 1572864 | tf_op jit(solution)/shard_map/reduce_scatter | solution.py:48
  189.7 8.2 %copy-start.13 = (bf16[2,256,512]{2,1,0:T(8,128)(2,1)S(1)}, bf16[2,256,512]{2,1,0:T(8,128)(2,1)}, u32[]{:S(2)}) copy-start(bf16[2,256,512]{2,1,0:T(8,128)(2,1)} %param.33) | copy-start | bytes 1572868
  189.7 9.7 %copy-start = (bf16[1,1024,256]{2,1,0:T(8,128)(2,1)S(1)}, bf16[1,1024,256]{2,1,0:T(8,128)(2,1)}, u32[]{:S(2)}) copy-start(bf16[1,1024,256]{2,1,0:T(8,128)(2,1)} %param.17) | copy-start | bytes 1572868
  189.7 29.1 %copy-start.3 = (bf16[1,1024,256]{2,1,0:T(8,128)(2,1)S(1)}, bf16[1,1024,256]{2,1,0:T(8,128)(2,1)}, u32[]{:S(2)}) copy-start(bf16[1,1024,256]{2,1,0:T(8,128)(2,1)} %fusion.57) | copy-start | bytes 1572868
  199.3 47.4 %copy-start.9 = (bf16[2,512,256]{2,1,0:T(8,128)(2,1)S(1)}, bf16[2,512,256]{2,1,0:T(8,128)(2,1)}, u32[]{:S(2)}) copy-start(bf16[2,512,256]{2,1,0:T(8,128)(2,1)} %param.27) | copy-start | bytes 1572868
  199.3 42.7 %all-gather.10.cloned.1.call-start = ((), (), s32[]{:S(2)}) async-start(), calls=%async_computation.6 | async-start | bytes 1572864 | tf_op jit(solution)/shard_map/all_gather | solution.py:41
  201.4 102.4 %all-gather.14.cloned.1.call-start = ((), (), s32[]{:S(2)}) async-start(), calls=%async_computation.10 | async-start | bytes 1572864 | tf_op jit(solution)/shard_map/all_gather | solution.py:41
  220.8 156.8 %reduce-scatter.7.cloned.1.call-start = ((), (), s32[]{:S(2)}) async-start(), calls=%async_computation.7 | async-start | bytes 1572864 | tf_op jit(solution)/shard_map/reduce_scatter | solution.py:48
  242.0 27.1 %copy-start.7 = (bf16[1,1024,512]{2,1,0:T(8,128)(2,1)S(1)}, bf16[1,1024,512]{2,1,0:T(8,128)(2,1)}, u32[]{:S(2)}) copy-start(bf16[1,1024,512]{2,1,0:T(8,128)(2,1)} %all-gather.10.cloned.1.call-done) | copy-start | bytes 3145732
  243.4 14.7 %collective-permute-start.2 = (bf16[1,512,512]{2,1,0:T(8,128)(2,1)S(1)}, bf16[1,512,512]{2,1,0:T(8,128)(2,1)S(1)}, u32[]{:S(2)}, u32[]{:S(2)}) collective-permute-start(bf16[1,512,512]{2,1,0:T(8,128)(2,1)S(1)} %get-tuple-element.6), channel_id=1, source_target_pairs={{0,4},{4,8},{8,12},{12,0},{1,5},{5,9},{9,13},{13,1},{2,6},{6,10},{... | collective-permute-start | bytes 1572872 | tf_op jit(solution)/shard_map/ppermute | solution.py:14
  244.6 24.4 %collective-permute-start.3 = (bf16[1,512,512]{2,1,0:T(8,128)(2,1)S(1)}, bf16[1,512,512]{2,1,0:T(8,128)(2,1)S(1)}, u32[]{:S(2)}, u32[]{:S(2)}) collective-permute-start(bf16[1,512,512]{2,1,0:T(8,128)(2,1)S(1)} %get-tuple-element.7), channel_id=1, source_target_pairs={{4,0},{8,4},{12,8},{0,12},{5,1},{9,5},{13,9},{1,13},{6,2},{10,6},{... | collective-permute-start | bytes 1572872 | tf_op jit(solution)/shard_map/ppermute | solution.py:15
  303.9 13.7 %copy-start.11 = (bf16[2,256,512]{2,1,0:T(8,128)(2,1)S(1)}, bf16[2,256,512]{2,1,0:T(8,128)(2,1)}, u32[]{:S(2)}) copy-start(bf16[2,256,512]{2,1,0:T(8,128)(2,1)} %param.29) | copy-start | bytes 1572868
  306.2 14.5 %collective-permute-start.6 = (bf16[1,512,512]{2,1,0:T(8,128)(2,1)}, bf16[1,512,512]{2,1,0:T(8,128)(2,1)}, u32[]{:S(2)}, u32[]{:S(2)}) collective-permute-start(bf16[1,512,512]{2,1,0:T(8,128)(2,1)} %get-tuple-element.2), channel_id=1, source_target_pairs={{0,4},{4,8},{8,12},{12,0},{1,5},{5,9},{9,13},{13,1},{2,6},{6,10},{... | collective-permute-start | bytes 1572872 | tf_op jit(solution)/shard_map/ppermute | solution.py:14
  307.7 11.4 %copy-start.5 = (bf16[1,1024,512]{2,1,0:T(8,128)(2,1)S(1)}, bf16[1,1024,512]{2,1,0:T(8,128)(2,1)}, u32[]{:S(2)}) copy-start(bf16[1,1024,512]{2,1,0:T(8,128)(2,1)} %all-gather.14.cloned.1.call-done) | copy-start | bytes 3145732
  307.7 11.4 %copy-start.12 = (bf16[2,512,256]{2,1,0:T(8,128)(2,1)S(1)}, bf16[2,512,256]{2,1,0:T(8,128)(2,1)}, u32[]{:S(2)}) copy-start(bf16[2,512,256]{2,1,0:T(8,128)(2,1)} %param.31) | copy-start | bytes 1572868
  307.7 25.0 %collective-permute-start.7 = (bf16[1,512,512]{2,1,0:T(8,128)(2,1)}, bf16[1,512,512]{2,1,0:T(8,128)(2,1)}, u32[]{:S(2)}, u32[]{:S(2)}) collective-permute-start(bf16[1,512,512]{2,1,0:T(8,128)(2,1)} %get-tuple-element.3), channel_id=1, source_target_pairs={{4,0},{8,4},{12,8},{0,12},{5,1},{9,5},{13,9},{1,13},{6,2},{10,6},{... | collective-permute-start | bytes 1572872 | tf_op jit(solution)/shard_map/ppermute | solution.py:15
  319.0 77.9 %reduce-scatter.11.cloned.1.call-start = ((), (), s32[]{:S(2)}) async-start(), calls=%async_computation.11 | async-start | bytes 1572864 | tf_op jit(solution)/shard_map/reduce_scatter | solution.py:48
  367.9 8.2 %copy-start.14 = (bf16[2,256,512]{2,1,0:T(8,128)(2,1)S(1)}, bf16[2,256,512]{2,1,0:T(8,128)(2,1)}, u32[]{:S(2)}) copy-start(bf16[2,256,512]{2,1,0:T(8,128)(2,1)} %param.33) | copy-start | bytes 1572868
  367.9 9.7 %copy-start.1 = (bf16[1,1024,256]{2,1,0:T(8,128)(2,1)S(1)}, bf16[1,1024,256]{2,1,0:T(8,128)(2,1)}, u32[]{:S(2)}) copy-start(bf16[1,1024,256]{2,1,0:T(8,128)(2,1)} %add_convert_fusion.3) | copy-start | bytes 1572868
  367.9 29.1 %copy-start.2 = (bf16[1,1024,256]{2,1,0:T(8,128)(2,1)S(1)}, bf16[1,1024,256]{2,1,0:T(8,128)(2,1)}, u32[]{:S(2)}) copy-start(bf16[1,1024,256]{2,1,0:T(8,128)(2,1)} %add_convert_fusion.1) | copy-start | bytes 1572868
Sparse Core Ops, SparseCore 0:
  11.4 29.8 all-gather.15
  42.9 20.8 all-gather.7
  65.9 21.2 all-gather.11
  140.9 18.5 reduce-scatter.4
  199.4 19.2 reduce-scatter.8
  220.7 21.2 all-gather.9
  243.5 21.2 all-gather.13
  319.1 18.5 reduce-scatter.6
  377.7 19.2 reduce-scatter.10
where the time goes:
time: 408 us; the launch traced here: 405 us
  local copies, waits for them, and re-layouts  144 us (35%)
  waiting for transfers between devices  144 us (35%)
  other arithmetic  60.8 us (15%)
  matrix products  18.2 us (4%)
  between operations  14.2 us (3%)
  starting transfers between devices  13.6 us (3%)
  blocking collectives  10.3 us (3%)
    gather x4, local copies, waits for them, and re-layouts, edge_sums(): pre = proj[:, nbr].astype(jnp.float32) + near[:, :, None]  132 us
    ppermute x4, waiting for transfers between devices, padded_2(): after = lax.ppermute(leading, axis, down)  46.2 us
    reduce_scatter x4, waiting for transfers between devices, graph_layer(): lax.psum_scatter(partial_prod.astype(jnp.bfloat16), 'mp', scatter_dimensi...  34.7 us
    reduce_sum x4, other arithmetic, edge_sums(): return jnp.sum(acts, axis=2).astype(jnp.bfloat16)  32.6 us
    all_gather x4, waiting for transfers between devices, graph_layer(): own_full = lax.all_gather(latent, 'mp', axis=2, tiled=True)  28.9 us
    ppermute x4, waiting for transfers between devices, padded_2(): before = lax.ppermute(last, axis, up)  20.4 us
    scatter-add x1, other arithmetic, on_device(): landed = init.at[local].add(piece_rows.astype(jnp.float32))  13.6 us
    all_gather x1, waiting for transfers between devices, on_device(): piece_rows = lax.all_gather(outgoing, 'mesh', axis=0, tiled=True)  13.3 us
  transfers between devices with their start and end apart: 17, of which 13 were waited for; matrix products, arithmetic and copies ran while one was open for 52% of the time, Pallas kernels for 0%

commit v1 on v0

--- a/solution.py
+++ b/solution.py
@@ -1,13 +1,20 @@
+import functools
+
 import jax
 import jax.numpy as jnp
 from jax import lax
+from jax.experimental import pallas as pl
+from jax.experimental.pallas import tpu as pltpu
 from jax.sharding import PartitionSpec as P
 
-
-def padded_2(shard, sides, width):
+LANES = 128
+DEAD = -1e30
+
+
+def padded_2(shard, sides, width, wrap):
     for axis, dim in sides:
         size, length = (lax.axis_size(axis), shard.shape[dim])
-        up = [(i, (i + 1) % size) for i in range(size)]
+        up = [(i, (i + 1) % size) for i in range(size if wrap else size - 1)]
         down = [(j, i) for i, j in up]
         last = lax.slice_in_dim(shard, length - width, length, axis=dim)
         leading = lax.slice_in_dim(shard, 0, width, axis=dim)
@@ -25,22 +32,10 @@
     return jnp.sum(acts, axis=2).astype(jnp.bfloat16)
 
 
-def clear_ends(padded, rows, rim, wrap):
-    if wrap:
-        return padded
-    mine = lax.axis_index("mesh")
-    parts = lax.axis_size("mesh")
-    place = jnp.arange(padded.shape[1], dtype=jnp.int32)
-    dropped = (place < rim) & (mine == 0) | (place >= rim + rows) & (mine == parts - 1)
-    return jnp.where(dropped[None, :, None], jnp.zeros((), padded.dtype), padded)
-
-
 def graph_layer(latent, nbr, count, w_send, w_recv, bias, w_out, wrap):
-    rows = latent.shape[1]
-    rim = rows // 2
+    rim = latent.shape[1] // 2
     own_full = lax.all_gather(latent, "mp", axis=2, tiled=True)
-    padded_full = padded_2(own_full, (("mesh", 1),), rim)
-    padded_full = clear_ends(padded_full, rows, rim, wrap)
+    padded_full = padded_2(own_full, (("mesh", 1),), rim, wrap)
     proj = jnp.dot(padded_full, w_send, preferred_element_type=jnp.float32).astype(jnp.bfloat16)
     near = jnp.dot(own_full, w_recv, preferred_element_type=jnp.float32) + bias.astype(jnp.float32)
     summed = edge_sums(proj, near, nbr, count)
@@ -51,24 +46,9 @@
     return (latent.astype(jnp.float32) + update).astype(jnp.bfloat16)
 
 
-def on_device(
-    g_nodes,
-    r_nodes,
-    g_nbr,
-    g_count,
-    r_nbr,
-    r_count,
-    bnd_src,
-    bnd_part,
-    bnd_node,
-    g_ws,
-    g_wd,
-    g_b1,
-    g_w2,
-    r_ws,
-    r_wd,
-    r_b1,
-    r_w2,
+def by_features(
+    g_nodes, r_nodes, g_nbr, g_count, r_nbr, r_count, bnd_src, bnd_part, bnd_node,
+    g_ws, g_wd, g_b1, g_w2, r_ws, r_wd, r_b1, r_w2,
 ):
     batch_rows, reg_rows, feats = r_nodes.shape
     dest = bnd_part[:, 0]
@@ -94,6 +74,333 @@
     return (planet, regional)
 
 
+def one_hot(flags):
+    return jnp.where(flags, 1.0, 0.0).astype(jnp.bfloat16)
+
+
+def pick_kernel(parts, cap, me_ref, bnd_ref, g_ref, *out_refs):
+    rows = g_ref.shape[0]
+    total = bnd_ref.shape[1]
+    me = me_ref[0]
+    src, part, node = (bnd_ref[i:i + 1, :] for i in range(3))
+    lines = -(-parts // 8) * 8
+    target = lax.rem(lax.broadcasted_iota(jnp.int32, (lines, total), 0) + me, parts)
+    named = part == target
+    before = one_hot(
+        lax.broadcasted_iota(jnp.int32, (total, total), 0) < lax.broadcasted_iota(jnp.int32, (total, total), 1)
+    )
+    rank = jnp.dot(one_hot(named), before, preferred_element_type=jnp.float32)
+    rank = jnp.where(named, rank, -1.0)
+    source = one_hot(lax.broadcasted_iota(jnp.int32, (rows, total), 0) == src)
+    line = lax.broadcasted_iota(jnp.int32, (16, total), 0)
+    high = lax.shift_right_logical(node, 7)
+    facts = jnp.where(line == 0, high, jnp.where(line == 1, node - high * 128, jnp.where(line == 2, 1, 0)))
+    facts = facts.astype(jnp.float32).astype(jnp.bfloat16)
+    place = lax.broadcasted_iota(jnp.int32, (cap, total), 0).astype(jnp.float32)
+    across = (((1,), (1,)), ((), ()))
+    for k in range(parts):
+        chosen = one_hot(place == rank[k:k + 1, :])
+        pick = lax.dot_general(chosen, source, across, preferred_element_type=jnp.float32).astype(jnp.bfloat16)
+        out_refs[k][:cap, :] = jnp.dot(pick, g_ref[...], preferred_element_type=jnp.float32).astype(jnp.bfloat16)
+        told = lax.dot_general(facts, chosen, across, preferred_element_type=jnp.float32)
+        out_refs[k][cap:, :] = told.astype(jnp.bfloat16)
+
+
+def pick_rows(me, bnd, nodes, parts, cap):
+    vmem = pl.BlockSpec(memory_space=pltpu.VMEM)
+    rows, feats = nodes.shape
+    total = bnd.shape[1]
+    piece = jax.ShapeDtypeStruct((cap + 16, feats), jnp.bfloat16)
+    return pl.pallas_call(
+        functools.partial(pick_kernel, parts, cap),
+        out_shape=(piece,) * parts,
+        in_specs=[pl.BlockSpec(memory_space=pltpu.SMEM), vmem, vmem],
+        out_specs=(vmem,) * parts,
+        compiler_params=pltpu.CompilerParams(vmem_limit_bytes=32 << 20),
+        cost_estimate=pl.CostEstimate(
+            flops=2 * parts * cap * rows * (total + feats), bytes_accessed=4 * rows * feats, transcendentals=0
+        ),
+        name="pick_rows",
+    )(me, bnd, nodes)
+
+
+def force_kernel(cap, first_ref, r_ref, *refs):
+    pieces, (same_ref, other_ref) = refs[:-2], refs[-2:]
+    half = same_ref.shape[0]
+    first = first_ref[0]
+    for out_ref, start in ((same_ref, first * half), (other_ref, (1 - first) * half)):
+        start = pl.multiple_of(start, 16)
+        row = (lax.broadcasted_iota(jnp.int32, (half, cap), 0) + start).astype(jnp.float32)
+        total = r_ref[pl.ds(start, half), :].astype(jnp.float32)
+        for piece in pieces:
+            facts = piece[cap:, :].astype(jnp.float32)
+            node = jnp.where(facts[2:3, :] > 0.5, facts[0:1, :] * 128.0 + facts[1:2, :], -1.0)
+            total += jnp.dot(one_hot(row == node), piece[:cap, :], preferred_element_type=jnp.float32)
+        out_ref[...] = total.astype(jnp.bfloat16)
+
+
+def add_force(first, nodes, pieces, cap):
+    vmem = pl.BlockSpec(memory_space=pltpu.VMEM)
+    rows, feats = nodes.shape
+    block = jax.ShapeDtypeStruct((rows // 2, feats), jnp.bfloat16)
+    return pl.pallas_call(
+        functools.partial(force_kernel, cap),
+        out_shape=(block, block),
+        in_specs=[pl.BlockSpec(memory_space=pltpu.SMEM)] + [vmem] * (1 + len(pieces)),
+        out_specs=(vmem, vmem),
+        compiler_params=pltpu.CompilerParams(vmem_limit_bytes=32 << 20),
+        cost_estimate=pl.CostEstimate(
+            flops=2 * len(pieces) * cap * rows * feats, bytes_accessed=6 * rows * feats, transcendentals=0
+        ),
+        name="add_force",
+    )(first, nodes, *pieces)
+
+
+def layer_kernel(
+    layer, slots, last, core_ref, idx_ref, own_hbm, sib_hbm, rim_hbm, ws_hbm, wd_hbm, w2_hbm, b_hbm, near_hbm, far_hbm,
+    *refs,
+):
+    outs, refs = (refs[:2], refs[2:]) if last else (refs[:1], refs[1:])
+    own, sib, rim, ws, wd, w2, bias, near_w, far_w, ws_x, wd_x, w2_x, proj, near, summed, sems = refs
+    rows, width = own.shape
+    share = width // 2
+    chunks = width // LANES
+    core = core_ref[0]
+    pairs = (
+        (own_hbm, own), (wd_hbm.at[layer], wd), (ws_hbm.at[layer], ws), (b_hbm, bias),
+        (near_hbm, near_w), (far_hbm, far_w), (sib_hbm, sib), (rim_hbm, rim), (w2_hbm.at[layer], w2),
+    )
+    copies = [pltpu.make_async_copy(src, dst, sems.at[i]) for i, (src, dst) in enumerate(pairs)]
+    for copy in copies:
+        copy.start()
+    window = 3 * rows
+    proj[0:8, :] = jnp.full((8, LANES), DEAD, jnp.float32)
+    proj[4 * window + 4:4 * window + 16, :] = jnp.full((12, LANES), DEAD, jnp.float32)
+
+    def put(dst, base, first, values):
+        for c in range(values.shape[1] // LANES):
+            dst[pl.ds(base * chunks + first + c, rows, stride=chunks), :] = values[:, c * LANES:(c + 1) * LANES]
+
+    for i in (0, 1, 2, 3):
+        copies[i].wait()
+    part = share // LANES
+    b_own = bias[layer:layer + 1, :].astype(jnp.float32)
+    put(near, 0, 0, (jnp.dot(own[...], wd[...], preferred_element_type=jnp.float32) + b_own) * 0.5)
+    put(proj, 1, 0, jnp.dot(own[...], ws[...], preferred_element_type=jnp.float32) * 0.5)
+    for i in (4, 5):
+        copies[i].wait()
+    here, there = pl.multiple_of(core * share, 16), pl.multiple_of((1 - core) * share, 16)
+    for spot, piece in ((here, near_w), (there, far_w)):
+        ws_x[pl.ds(spot, share), :] = piece[0:share, :]
+        wd_x[pl.ds(spot, share), :] = piece[share:2 * share, :]
+
+    @pl.when(core == 0)
+    def _():
+        w2_x[:, :share] = near_w[2 * share:3 * share, :]
+        w2_x[:, share:] = far_w[2 * share:3 * share, :]
+
+    @pl.when(core != 0)
+    def _():
+        w2_x[:, share:] = near_w[2 * share:3 * share, :]
+        w2_x[:, :share] = far_w[2 * share:3 * share, :]
+
+    b_other = near_w[3 * share:3 * share + 1, :].astype(jnp.float32)
+    put(near, 0, part, (jnp.dot(own[...], wd_x[...], preferred_element_type=jnp.float32) + b_other) * 0.5)
+    put(proj, 1, part, jnp.dot(own[...], ws_x[...], preferred_element_type=jnp.float32) * 0.5)
+    for i, ref, base in ((6, sib, rows + 1), (7, rim, 2 * rows + 1)):
+        copies[i].wait()
+        put(proj, base, 0, jnp.dot(ref[...], ws[...], preferred_element_type=jnp.float32) * 0.5)
+        put(proj, base, part, jnp.dot(ref[...], ws_x[...], preferred_element_type=jnp.float32) * 0.5)
+    low = lax.broadcasted_iota(jnp.int32, (8, LANES), 0) < chunks
+
+    def nodes(q, carry):
+        spot = pl.ds(pl.multiple_of(8 * q, 8), 8)
+        mine = near[spot, :]
+        total = None
+        for j in range(slots):
+            upper = proj[pl.ds(pl.multiple_of(idx_ref[2 * q * slots + j], 4), 8), :]
+            lower = proj[pl.ds(pl.multiple_of(idx_ref[(2 * q + 1) * slots + j], 4), 8), :]
+            y = jnp.where(low, upper, lower) + mine
+            act = y * jnp.tanh(y) + y
+            total = act if total is None else total + act
+        summed[spot, :] = total
+        return carry
+
+    lax.fori_loop(0, rows // 2, nodes, 0, unroll=8)
+    copies[8].wait()
+    update = None
+    for c in range(chunks):
+        values = summed[pl.ds(c, rows, stride=chunks), :].astype(jnp.bfloat16)
+        if c < part:
+            w_rows = w2[c * LANES:(c + 1) * LANES, :]
+        else:
+            w_rows = w2_x[(c - part) * LANES:(c - part + 1) * LANES, :]
+        term = jnp.dot(values, w_rows, preferred_element_type=jnp.float32)
+        update = term if update is None else update + term
+    result = (own[...].astype(jnp.float32) + update).astype(jnp.bfloat16)
+    if not last:
+        outs[0][...] = result
+    else:
+        @pl.when(core == 0)
+        def _():
+            outs[0][...] = result[:, :share]
+            outs[1][...] = result[:, share:]
+
+        @pl.when(core != 0)
+        def _():
+            outs[0][...] = result[:, share:]
+            outs[1][...] = result[:, :share]
+
+
+def run_layer(layer, slots, last, core, idx, own, sib, rim, ws, wd, w2, bias, near_w, far_w):
+    rows, width = own.shape
+    share = width // 2
+    chunks = width // LANES
+    anywhere = pl.BlockSpec(memory_space=pl.ANY)
+    smem = pl.BlockSpec(memory_space=pltpu.SMEM)
+    vmem = pl.BlockSpec(memory_space=pltpu.VMEM)
+    bf16, f32 = jnp.bfloat16, jnp.float32
+    if last:
+        out_shape = (jax.ShapeDtypeStruct((rows, share), bf16),) * 2
+        out_specs = (vmem, vmem)
+    else:
+        out_shape, out_specs = jax.ShapeDtypeStruct((rows, width), bf16), vmem
+    edges = rows * slots
+    return pl.pallas_call(
+        functools.partial(layer_kernel, layer, slots, last),
+        out_shape=out_shape,
+        in_specs=[smem, smem] + [anywhere] * 9,
+        out_specs=out_specs,
+        scratch_shapes=[
+            pltpu.VMEM((rows, width), bf16),
+            pltpu.VMEM((rows, width), bf16),
+            pltpu.VMEM((rows, width), bf16),
+            pltpu.VMEM((width, share), bf16),
+            pltpu.VMEM((width, share), bf16),
+            pltpu.VMEM((share, width), bf16),
+            pltpu.VMEM(bias.shape, bf16),
+            pltpu.VMEM(near_w.shape, bf16),
+            pltpu.VMEM(far_w.shape, bf16),
+            pltpu.VMEM((width, share), bf16),
+            pltpu.VMEM((width, share), bf16),
+            pltpu.VMEM((share, width), bf16),
+            pltpu.VMEM((3 * rows * chunks + 96, LANES), f32),
+            pltpu.VMEM((rows * chunks, LANES), f32),
+            pltpu.VMEM((rows * chunks, LANES), f32),
+            pltpu.SemaphoreType.DMA((9,)),
+        ],
+        compiler_params=pltpu.CompilerParams(vmem_limit_bytes=32 << 20),
+        cost_estimate=pl.CostEstimate(
+            flops=2 * 5 * rows * width * width, bytes_accessed=10 * rows * width, transcendentals=edges * width
+        ),
+        name="graph_layer",
+    )(core, idx, own, sib, rim, ws, wd, w2, bias, near_w, far_w)
+
+
+def edge_offsets(nbr, count, core):
+    rows, slots = nbr.shape
+    half = rows // 2
+    nbr = lax.dynamic_slice(nbr, (core * half, 0), (half, slots)) - core * half
+    count = lax.dynamic_slice(count, (core * half,), (half,))
+    low = nbr + jnp.where(core == 0, 2 * half, half)
+    high = nbr - jnp.where(core == 0, half, 0)
+    place = jnp.where(nbr < half, low, jnp.where(nbr < 2 * half, nbr - half, high))
+    live = jnp.arange(slots, dtype=jnp.int32)[None, :] < count[:, None]
+    place = jnp.where(live, place, 3 * half)
+    odd = jnp.arange(half, dtype=jnp.int32)[:, None] % 2
+    return (4 * (place + 1 - odd)).reshape(half * slots)
+
+
+def spread_rows(same, other):
+    a = lax.ppermute(same, ("mp", "batch"), [(0, 0), (1, 2), (2, 1), (3, 3)])
+    b = lax.ppermute(other, ("mp", "batch"), [(0, 1), (1, 3), (2, 0), (3, 2)])
+    return a, b
+
+
+def gather_rows(a, b):
+    same = lax.ppermute(a, ("mp", "batch"), [(0, 0), (1, 2), (2, 1), (3, 3)])
+    other = lax.ppermute(b, ("mp", "batch"), [(0, 2), (1, 0), (2, 3), (3, 1)])
+    return same, other
+
+
+def ordered(which, a, b, axis):
+    return jnp.where(which == 0, jnp.concatenate([a, b], axis), jnp.concatenate([b, a], axis))
+
+
+def swap(values, axis):
+    return lax.ppermute(values, axis, [(0, 1), (1, 0)])
+
+
+def rims(own, wrap):
+    size = lax.axis_size("mesh")
+    pairs = []
+    for m in range(size):
+        if wrap or m + 1 < size:
+            pairs.append((2 * m + 1, 2 * ((m + 1) % size)))
+        if wrap or m > 0:
+            pairs.append((2 * m, 2 * ((m - 1) % size) + 1))
+    return lax.ppermute(own, ("mesh", "batch"), pairs)
+
+
+def other_weights(layer, core, ws, wd, w2, bias):
+    share = ws.shape[2]
+    picked = [
+        lax.dynamic_slice(ws, (layer, core * share, 0), (1, share, share))[0],
+        lax.dynamic_slice(wd, (layer, core * share, 0), (1, share, share))[0],
+        lax.dynamic_slice(w2, (layer, 0, core * share), (1, share, share))[0],
+        jnp.broadcast_to(bias[layer][None], (16, share)),
+    ]
+    near_w = swap(jnp.concatenate(picked, 0), "mp")
+    return near_w, swap(near_w, "batch")
+
+
+def by_rows(
+    g_nodes, r_nodes, g_nbr, g_count, r_nbr, r_count, bnd_src, bnd_part, bnd_node,
+    g_ws, g_wd, g_b1, g_w2, r_ws, r_wd, r_b1, r_w2,
+):
+    part = lax.axis_index("mp")
+    core = lax.axis_index("batch")
+    parts = lax.axis_size("mesh")
+    slots = g_nbr.shape[1]
+    layers = g_ws.shape[0]
+    rows = g_nodes.shape[1]
+    half = rows // 2
+    cap = 2 * bnd_src.shape[0] // parts
+    me = lax.axis_index("mesh").reshape(1)
+    core1 = core.reshape(1)
+    g_own, r_own = g_nodes[0], r_nodes[0]
+
+    same = lax.dynamic_slice(g_own, (part * half, 0), (half, g_own.shape[1]))
+    other = lax.dynamic_slice(g_own, ((1 - part) * half, 0), (half, g_own.shape[1]))
+    g_a, g_b = spread_rows(same, other)
+    bnd = jnp.stack([bnd_src, bnd_part[:, 0], bnd_node])
+    pieces = pick_rows(me, bnd, g_own, parts, cap)
+    landed = [pieces[0]]
+    for k in range(1, parts):
+        landed.append(lax.ppermute(pieces[k], "mesh", [(i, (i + k) % parts) for i in range(parts)]))
+    g_idx = edge_offsets(g_nbr, g_count, core)
+    r_idx = edge_offsets(r_nbr, r_count, core)
+    r_a, r_b = spread_rows(*add_force(part.reshape(1), r_own, landed, cap))
+
+    planet = ordered(core, g_a, g_b, 1)
+    regional = ordered(core, r_a, r_b, 1)
+    for layer in range(layers):
+        last = layer == layers - 1
+        g_w = other_weights(layer, core, g_ws, g_wd, g_w2, g_b1)
+        planet = run_layer(
+            layer, slots, last, core1, g_idx, planet, swap(planet, "batch"), rims(planet, True),
+            g_ws, g_wd, g_w2, g_b1, *g_w,
+        )
+        r_w = other_weights(layer, core, r_ws, r_wd, r_w2, r_b1)
+        regional = run_layer(
+            layer, slots, last, core1, r_idx, regional, swap(regional, "batch"), rims(regional, False),
+            r_ws, r_wd, r_w2, r_b1, *r_w,
+        )
+    g_out = ordered(part, *gather_rows(*planet), 0)
+    r_out = ordered(part, *gather_rows(*regional), 0)
+    return g_out[None], r_out[None]
+
+
 def solution(mesh):
     in_specs = (
         P(("groups", "batch"), "mesh", "mp"),
@@ -115,6 +422,7 @@
         P(None, "mp", None),
     )
     out_specs = (P(("groups", "batch"), "mesh", "mp"), P(("groups", "batch"), "mesh", "mp"))
+    square = mesh.shape["mp"] == 2 and mesh.shape["batch"] == 2
     return jax.shard_map(
-        on_device, mesh=mesh, in_specs=in_specs, out_specs=out_specs, check_vma=False
+        by_rows if square else by_features, mesh=mesh, in_specs=in_specs, out_specs=out_specs, check_vma=False
     )

time: 408 us -> 128 us (0.31)
  local copies, waits for them, and re-layouts: 144 us -> 15.4 us
  waiting for transfers between devices: 144 us -> 27.2 us
  other arithmetic: 60.8 us -> 8.43 us
  Pallas kernels: 0 us -> 36.1 us
  starting transfers between devices: 13.6 us -> 38.6 us
  matrix products: 18.2 us -> 0 us
  between operations: 14.2 us -> 1.1 us
  blocking collectives: 10.3 us -> 0 us
    gather x5 -> x0, local copies, waits for them, and re-layouts: 136 us -> none  [the longest x4 132 us: edge_sums(): pre = proj[:, nbr].astype(jnp.float32) + near[:, :, None]]
    all_gather x5 -> x0, waiting for transfers between devices: 42.2 us -> none  [the longest x4 28.9 us: graph_layer(): own_full = lax.all_gather(latent, 'mp', axis=2, tiled=True)]
    ppermute x8 -> x27, waiting for transfers between devices: 66.6 us -> 27.2 us  [the longest x2 8.91 us: spread_rows(): b = lax.ppermute(other, ('mp', 'batch'), [(0, 1), (1, 3), (2, 0), (3, 2)])]
    pallas_call x0 -> x6, Pallas kernels: none -> 36.1 us  [the longest x4 33.2 us: run_layer(): pl.pallas_call(functools.partial(layer_kernel, layer, slots, last), out_s...]
    reduce_scatter x4 -> x0, waiting for transfers between devices: 34.7 us -> none  [graph_layer(): lax.psum_scatter(partial_prod.astype(jnp.bfloat16), 'mp', scatter_dimensi...]
    reduce_sum x4 -> x0, other arithmetic: 32.6 us -> none  [edge_sums(): return jnp.sum(acts, axis=2).astype(jnp.bfloat16)]
    ppermute x8 -> x27, starting transfers between devices: 13.2 us -> 38.6 us  [the longest x4 11.8 us: rims(): return lax.ppermute(own, ('mesh', 'batch'), pairs)]
    dot_general x12 -> x0, matrix products: 18.2 us -> none  [the longest x4 7.33 us: graph_layer(): jnp.dot(padded_full, w_send, preferred_element_type=jnp.float32)]
  transfers between devices with their start and end apart: 17 -> 27, of which waited for: 13 -> 5; matrix products, arithmetic and copies ran while one was open for 52% -> 11% of each run, Pallas kernels for 0% -> 27%
where the time goes in v1:
time: 128 us; the launch traced here: 127 us
  starting transfers between devices  38.6 us (30%)
  Pallas kernels  36.1 us (28%)
  waiting for transfers between devices  27.2 us (21%)
  local copies, waits for them, and re-layouts  15.4 us (12%)
  other arithmetic  8.43 us (7%)
    pallas_call x4, Pallas kernels, run_layer(): pl.pallas_call(functools.partial(layer_kernel, layer, slots, last), out_s...  33.2 us
    ppermute x4, starting transfers between devices, rims(): return lax.ppermute(own, ('mesh', 'batch'), pairs)  11.8 us
    unnamed x58, local copies, waits for them, and re-layouts  9.15 us
    ppermute x2, waiting for transfers between devices, spread_rows(): b = lax.ppermute(other, ('mp', 'batch'), [(0, 1), (1, 3), (2, 0), (3, 2)])  8.91 us
    ppermute x2, waiting for transfers between devices, spread_rows(): a = lax.ppermute(same, ('mp', 'batch'), [(0, 0), (1, 2), (2, 1), (3, 3)])  8.68 us
    ppermute x2, starting transfers between devices, spread_rows(): a = lax.ppermute(same, ('mp', 'batch'), [(0, 0), (1, 2), (2, 1), (3, 3)])  8.35 us
    ppermute x2, waiting for transfers between devices, gather_rows(): same = lax.ppermute(a, ('mp', 'batch'), [(0, 0), (1, 2), (2, 1), (3, 3)])  6.97 us
    ppermute x2, starting transfers between devices, gather_rows(): same = lax.ppermute(a, ('mp', 'batch'), [(0, 0), (1, 2), (2, 1), (3, 3)])  6.12 us
  transfers between devices with their start and end apart: 27, of which 5 were waited for; matrix products, arithmetic and copies ran while one was open for 11% of the time, Pallas kernels for 27%

profile of v1, /device:TPU:1, one launch (start us, length us, event | category | flops | bytes accessed | tf_op | source)
XLA Modules:
  0.0 126.8 jit_solution(16583800782895359365)
XLA Ops:
  0.7 0.7 copy-done.26
  1.4 1.0 copy-done
  2.4 2.2 %pick_rows.1 = (bf16[272,256]{1,0:T(8,128)(2,1)S(1)}, bf16[272,256]{1,0:T(8,128)(2,1)S(1)}, bf16[272,256]{1,0:T(8,128)(2,1)S(1)}, bf16[272,256]{1,0:T(8,128)(2,1)S(1)}) custom-call(s32[1]{0:T(128)} %bitcast.13.me_ref, s32[3,512]{1,0:T(4,128)S(1)} %pad_add_fusion.bnd_ref, bf16[1024,256]{1,0:T(8,128)(2,1)S(1)} %bitcast.40), custom_call_target="tpu_custom_call" | custom-call | flops 1610612736 | bytes 1048576 | tf_op jit(solution)/shard_map/pick_rows/pallas_call | solution.py:114
  4.6 2.2 %collective-permute-start.12 = (bf16[272,256]{1,0:T(8,128)(2,1)S(1)}, bf16[272,256]{1,0:T(8,128)(2,1)S(1)}, u32[]{:S(2)}, u32[]{:S(2)}) collective-permute-start(bf16[272,256]{1,0:T(8,128)(2,1)S(1)} %get-tuple-element.15), channel_id=1, source_target_pairs={{0,4},{4,8},{8,12},{12,0},{1,5},{5,9},{9,13},{13,1},{2,6},{6,10},{... | collective-permute-start | bytes 417800 | tf_op jit(solution)/shard_map/ppermute | solution.py:380
  6.8 2.3 %collective-permute-start.13 = (bf16[272,256]{1,0:T(8,128)(2,1)S(1)}, bf16[272,256]{1,0:T(8,128)(2,1)S(1)}, u32[]{:S(2)}, u32[]{:S(2)}) collective-permute-start(bf16[272,256]{1,0:T(8,128)(2,1)S(1)} %get-tuple-element.16), channel_id=1, source_target_pairs={{0,8},{4,12},{8,0},{12,4},{1,9},{5,13},{9,1},{13,5},{2,10},{6,14},... | collective-permute-start | bytes 417800 | tf_op jit(solution)/shard_map/ppermute | solution.py:380
  9.1 1.1 collective-permute-start.14
  10.2 0.8 dynamic-slice_bitcast_fusion.1
  11.1 4.5 %collective-permute-start = (bf16[512,256]{1,0:T(8,128)(2,1)}, bf16[512,256]{1,0:T(8,128)(2,1)}, u32[]{:S(2)}, u32[]{:S(2)}) collective-permute-start(bf16[512,256]{1,0:T(8,128)(2,1)} %get-tuple-element.38), channel_id=1, source_target_pairs={{0,0},{1,2},{2,1},{3,3},{4,4},{5,6},{6,5},{7,7},{8,8},{9,10},{10,9... | collective-permute-start | bytes 786440 | tf_op jit(solution)/shard_map/ppermute | solution.py:315
  15.8 0.7 copy-done.11
  17.1 0.8 dynamic-slice_bitcast_fusion.4
  18.4 0.7 dynamic-slice_bitcast_fusion.2
  19.6 0.7 dynamic-slice_bitcast_fusion.9
  20.4 0.8 pad_maximum_fusion.2
  21.8 0.7 add_force.1
  22.5 3.8 %collective-permute-start.15 = (bf16[512,256]{1,0:T(8,128)(2,1)S(1)}, bf16[512,256]{1,0:T(8,128)(2,1)}, u32[]{:S(2)}, u32[]{:S(2)}) collective-permute-start(bf16[512,256]{1,0:T(8,128)(2,1)S(1)} %get-tuple-element.18), channel_id=1, source_target_pairs={{0,0},{1,2},{2,1},{3,3},{4,4},{5,6},{6,5},{7,7},{8,8},{9,10},{10,9... | collective-permute-start | bytes 786440 | tf_op jit(solution)/shard_map/ppermute | solution.py:315
  26.3 0.8 pad_maximum_fusion
  27.1 1.5 %collective-permute-start.16 = (bf16[512,256]{1,0:T(8,128)(2,1)S(1)}, bf16[512,256]{1,0:T(8,128)(2,1)S(1)}, u32[]{:S(2)}, u32[]{:S(2)}) collective-permute-start(bf16[512,256]{1,0:T(8,128)(2,1)S(1)} %get-tuple-element.19), channel_id=1, source_target_pairs={{0,1},{1,3},{2,0},{3,2},{4,5},{5,7},{6,4},{7,6},{8,9},{9,11},{10,8... | collective-permute-start | bytes 786440 | tf_op jit(solution)/shard_map/ppermute | solution.py:316
  28.6 1.3 %maximum_select_fusion.own_hbm = bf16[512,512]{1,0:T(8,128)(2,1)S(1)} fusion(bf16[512,256]{1,0:T(8,128)(2,1)} %collective-permute-done.1, bf16[512,256]{1,0:T(8,128)(2,1)} %collective-permute-done, pred[]{:T(512)S(6)} %eq.8), kind=kLoop, calls=%fused_computation | loop fusion | flops 2359296 | bytes 1048577 | tf_op jit(solution)/shard_map/jit(_where)/select_n | solution.py:327
  30.0 0.6 copy-done.28
  30.7 8.7 %collective-permute-done.15 = bf16[512,256]{1,0:T(8,128)(2,1)} collective-permute-done((bf16[512,256]{1,0:T(8,128)(2,1)S(1)}, bf16[512,256]{1,0:T(8,128)(2,1)}, u32[]{:S(2)}, u32[]{:S(2)}) %collective-permute-start.15) | collective-permute-done | bytes 262176 | tf_op jit(solution)/shard_map/ppermute | solution.py:315
  39.4 8.9 %collective-permute-done.16 = bf16[512,256]{1,0:T(8,128)(2,1)S(1)} collective-permute-done((bf16[512,256]{1,0:T(8,128)(2,1)S(1)}, bf16[512,256]{1,0:T(8,128)(2,1)S(1)}, u32[]{:S(2)}, u32[]{:S(2)}) %collective-permute-start.16) | collective-permute-done | bytes 262176 | tf_op jit(solution)/shard_map/ppermute | solution.py:316
  48.3 4.1 %collective-permute-start.3 = (bf16[512,512]{1,0:T(8,128)(2,1)S(1)}, bf16[512,512]{1,0:T(8,128)(2,1)}, u32[]{:S(2)}, u32[]{:S(2)}) collective-permute-start(bf16[512,512]{1,0:T(8,128)(2,1)S(1)} %maximum_select_fusion.own_hbm), channel_id=1, source_target_pairs={{1,4},{0,13},{5,8},{4,1},{9,12},{8,5},{13,0},{12,9},{3,6},{2,15},{... | collective-permute-start | bytes 1572872 | tf_op jit(solution)/shard_map/ppermute | solution.py:342
  52.5 1.3 %maximum_select_fusion.2.own_hbm = bf16[512,512]{1,0:T(8,128)(2,1)S(1)} fusion(bf16[512,256]{1,0:T(8,128)(2,1)S(1)} %collective-permute-done.16, bf16[512,256]{1,0:T(8,128)(2,1)} %collective-permute-done.15, pred[]{:T(512)S(6)} %eq.8), kind=kLoop, calls=%fused_computation.2 | loop fusion | flops 2359296 | bytes 1048577 | tf_op jit(solution)/shard_map/jit(_where)/select_n | solution.py:327
  54.2 4.5 %collective-permute-start.18 = (bf16[512,512]{1,0:T(8,128)(2,1)S(1)}, bf16[512,512]{1,0:T(8,128)(2,1)}, u32[]{:S(2)}, u32[]{:S(2)}) collective-permute-start(bf16[512,512]{1,0:T(8,128)(2,1)S(1)} %maximum_select_fusion.2.own_hbm), channel_id=1, source_target_pairs={{1,4},{5,8},{4,1},{9,12},{8,5},{12,9},{3,6},{7,10},{6,3},{11,14},{... | collective-permute-start | bytes 1572872 | tf_op jit(solution)/shard_map/ppermute | solution.py:342
  58.8 0.6 copy-done.27
  59.4 0.8 pad_maximum_fusion.3
  60.2 0.8 copy-done.13
  61.0 0.6 add_select_fusion
  61.6 0.8 dynamic_slice.58
  62.3 0.8 dynamic_slice.70
  63.1 1.1 collective-permute-done.3.rim_hbm
  64.2 4.2 %collective-permute-start.9 = (bf16[784,256]{1,0:T(8,128)(2,1)}, bf16[784,256]{1,0:T(8,128)(2,1)}, u32[]{:S(2)}, u32[]{:S(2)}) collective-permute-start(bf16[784,256]{1,0:T(8,128)(2,1)} %collective-permute-done.8.near_hbm), channel_id=1, source_target_pairs={{0,1},{1,0},{2,3},{3,2},{4,5},{5,4},{6,7},{7,6},{8,9},{9,8},{10,11... | collective-permute-start | bytes 1204232 | tf_op jit(solution)/shard_map/ppermute | solution.py:331
  68.4 0.8 subtract_multiply_fusion
  69.4 1.0 copy-done.14
  70.5 1.0 copy-done.16
  71.5 8.7 %graph_layer.4.own_hbm = bf16[512,512]{1,0:T(8,128)(2,1)} custom-call(s32[1]{0:T(128)} %bitcast.core_ref, s32[4096]{0:T(1024)S(1)} %reshape.149.idx_ref, bf16[512,512]{1,0:T(8,128)(2,1)S(1)} %maximum_select_fusion.own_hbm, bf16[512,512]{1,0:T(8,128)(2,1)S(1)} %copy-done.14, bf16[512,512]{1,0:T(8,128)(2,1)} %collective-permute-done.3.rim_hbm, ...), custom_call_target="tpu_custom_call" | custom-call | flops 1342177280 | bytes 2621440 | tf_op jit(solution)/shard_map/graph_layer/pallas_call | solution.py:269
  80.7 0.6 copy-done.7
  81.2 1.0 copy-done.9
  82.3 7.8 %graph_layer.6.own_hbm = bf16[512,512]{1,0:T(8,128)(2,1)S(1)} custom-call(s32[1]{0:T(128)} %bitcast.core_ref, s32[4096]{0:T(1024)S(1)} %reshape.150.idx_ref, bf16[512,512]{1,0:T(8,128)(2,1)S(1)} %maximum_select_fusion.2.own_hbm, bf16[512,512]{1,0:T(8,128)(2,1)} %collective-permute-done.17.sib_hbm, bf16[512,512]{1,0:T(8,128)(2,1)} %collective-permute-done.18.rim_hbm, ...), custom_call_target="tpu_custom_call" | custom-call | flops 1342177280 | bytes 2621440 | tf_op jit(solution)/shard_map/graph_layer/pallas_call | solution.py:269
  90.2 3.1 %collective-permute-start.22 = (bf16[512,512]{1,0:T(8,128)(2,1)S(1)}, bf16[512,512]{1,0:T(8,128)(2,1)S(1)}, u32[]{:S(2)}, u32[]{:S(2)}) collective-permute-start(bf16[512,512]{1,0:T(8,128)(2,1)S(1)} %graph_layer.6.own_hbm), channel_id=1, source_target_pairs={{1,4},{5,8},{4,1},{9,12},{8,5},{12,9},{3,6},{7,10},{6,3},{11,14},{... | collective-permute-start | bytes 1572872 | tf_op jit(solution)/shard_map/ppermute | solution.py:342
  93.4 1.5 %collective-permute-done.7.rim_hbm = bf16[512,512]{1,0:T(8,128)(2,1)} collective-permute-done((bf16[512,512]{1,0:T(8,128)(2,1)}, bf16[512,512]{1,0:T(8,128)(2,1)}, u32[]{:S(2)}, u32[]{:S(2)}) %collective-permute-start.7) | collective-permute-done | bytes 524320 | tf_op jit(solution)/shard_map/ppermute | solution.py:342
  94.9 8.9 %graph_layer.5 = (bf16[512,256]{1,0:T(8,128)(2,1)S(1)}, bf16[512,256]{1,0:T(8,128)(2,1)}) custom-call(s32[1]{0:T(128)} %bitcast.core_ref, s32[4096]{0:T(1024)S(1)} %reshape.149.idx_ref, bf16[512,512]{1,0:T(8,128)(2,1)} %graph_layer.4.own_hbm, bf16[512,512]{1,0:T(8,128)(2,1)} %collective-permute-done.6.sib_hbm, ...), custom_call_target="tpu_custom_call" | custom-call | flops 1342177280 | bytes 2621440 | tf_op jit(solution)/shard_map/graph_layer/pallas_call | solution.py:269
  103.8 4.2 %collective-permute-start.10 = (bf16[512,256]{1,0:T(8,128)(2,1)S(1)}, bf16[512,256]{1,0:T(8,128)(2,1)S(1)}, u32[]{:S(2)}, u32[]{:S(2)}) collective-permute-start(bf16[512,256]{1,0:T(8,128)(2,1)S(1)} %get-tuple-element.12), channel_id=1, source_target_pairs={{0,0},{1,2},{2,1},{3,3},{4,4},{5,6},{6,5},{7,7},{8,8},{9,10},{10,9... | collective-permute-start | bytes 786440 | tf_op jit(solution)/shard_map/ppermute | solution.py:321
  108.0 7.8 %graph_layer.7 = (bf16[512,256]{1,0:T(8,128)(2,1)S(1)}, bf16[512,256]{1,0:T(8,128)(2,1)S(1)}) custom-call(s32[1]{0:T(128)} %bitcast.core_ref, s32[4096]{0:T(1024)S(1)} %reshape.150.idx_ref, bf16[512,512]{1,0:T(8,128)(2,1)S(1)} %graph_layer.6.own_hbm, bf16[512,512]{1,0:T(8,128)(2,1)S(1)} %collective-permute-done.21.sib_hbm, ...), custom_call_target="tpu_custom_call" | custom-call | flops 1342177280 | bytes 2621440 | tf_op jit(solution)/shard_map/graph_layer/pallas_call | solution.py:269
  115.8 1.9 %collective-permute-start.25 = (bf16[512,256]{1,0:T(8,128)(2,1)S(1)}, bf16[512,256]{1,0:T(8,128)(2,1)S(1)}, u32[]{:S(2)}, u32[]{:S(2)}) collective-permute-start(bf16[512,256]{1,0:T(8,128)(2,1)S(1)} %get-tuple-element.20), channel_id=1, source_target_pairs={{0,0},{1,2},{2,1},{3,3},{4,4},{5,6},{6,5},{7,7},{8,8},{9,10},{10,9... | collective-permute-start | bytes 786440 | tf_op jit(solution)/shard_map/ppermute | solution.py:321
  117.8 1.0 maximum_select_fusion.1
  118.8 7.0 %collective-permute-done.25 = bf16[512,256]{1,0:T(8,128)(2,1)S(1)} collective-permute-done((bf16[512,256]{1,0:T(8,128)(2,1)S(1)}, bf16[512,256]{1,0:T(8,128)(2,1)S(1)}, u32[]{:S(2)}, u32[]{:S(2)}) %collective-permute-start.25) | collective-permute-done | bytes 262176 | tf_op jit(solution)/shard_map/ppermute | solution.py:321
  125.8 1.0 maximum_select_fusion.3
  (97 shorter events, 4.1 us)
Async XLA Ops:
  1.4 1.0 copy-start
  2.4 7.8 %copy-start.1 = (bf16[1,1024,256]{2,1,0:T(8,128)(2,1)S(1)}, bf16[1,1024,256]{2,1,0:T(8,128)(2,1)}, u32[]{:S(2)}) copy-start(bf16[1,1024,256]{2,1,0:T(8,128)(2,1)} %param.17) | copy-start | bytes 1572868
  4.6 17.1 %collective-permute-start.12 = (bf16[272,256]{1,0:T(8,128)(2,1)S(1)}, bf16[272,256]{1,0:T(8,128)(2,1)S(1)}, u32[]{:S(2)}, u32[]{:S(2)}) collective-permute-start(bf16[272,256]{1,0:T(8,128)(2,1)S(1)} %get-tuple-element.15), channel_id=1, source_target_pairs={{0,4},{4,8},{8,12},{12,0},{1,5},{5,9},{9,13},{13,1},{2,6},{6,10},{... | collective-permute-start | bytes 417800 | tf_op jit(solution)/shard_map/ppermute | solution.py:380
  6.8 14.9 %collective-permute-start.13 = (bf16[272,256]{1,0:T(8,128)(2,1)S(1)}, bf16[272,256]{1,0:T(8,128)(2,1)S(1)}, u32[]{:S(2)}, u32[]{:S(2)}) collective-permute-start(bf16[272,256]{1,0:T(8,128)(2,1)S(1)} %get-tuple-element.16), channel_id=1, source_target_pairs={{0,8},{4,12},{8,0},{12,4},{1,9},{5,13},{9,1},{13,5},{2,10},{6,14},... | collective-permute-start | bytes 417800 | tf_op jit(solution)/shard_map/ppermute | solution.py:380
  9.1 12.6 %collective-permute-start.14 = (bf16[272,256]{1,0:T(8,128)(2,1)S(1)}, bf16[272,256]{1,0:T(8,128)(2,1)S(1)}, u32[]{:S(2)}, u32[]{:S(2)}) collective-permute-start(bf16[272,256]{1,0:T(8,128)(2,1)S(1)} %get-tuple-element.17), channel_id=1, source_target_pairs={{0,12},{4,0},{8,4},{12,8},{1,13},{5,1},{9,5},{13,9},{2,14},{6,2},{... | collective-permute-start | bytes 417800 | tf_op jit(solution)/shard_map/ppermute | solution.py:380
  10.2 6.8 %copy-start.4 = (bf16[2,256,512]{2,1,0:T(8,128)(2,1)S(1)}, bf16[2,256,512]{2,1,0:T(8,128)(2,1)}, u32[]{:S(2)}) copy-start(bf16[2,256,512]{2,1,0:T(8,128)(2,1)} %w2_hbm.5) | copy-start | bytes 1572868
  10.2 6.9 %copy-start.5 = (bf16[2,512,256]{2,1,0:T(8,128)(2,1)S(1)}, bf16[2,512,256]{2,1,0:T(8,128)(2,1)}, u32[]{:S(2)}) copy-start(bf16[2,512,256]{2,1,0:T(8,128)(2,1)} %ws_hbm.7) | copy-start | bytes 1572868
  11.1 16.1 %collective-permute-start = (bf16[512,256]{1,0:T(8,128)(2,1)}, bf16[512,256]{1,0:T(8,128)(2,1)}, u32[]{:S(2)}, u32[]{:S(2)}) collective-permute-start(bf16[512,256]{1,0:T(8,128)(2,1)} %get-tuple-element.38), channel_id=1, source_target_pairs={{0,0},{1,2},{2,1},{3,3},{4,4},{5,6},{6,5},{7,7},{8,8},{9,10},{10,9... | collective-permute-start | bytes 786440 | tf_op jit(solution)/shard_map/ppermute | solution.py:315
  15.6 13.0 %collective-permute-start.1 = (bf16[512,256]{1,0:T(8,128)(2,1)}, bf16[512,256]{1,0:T(8,128)(2,1)}, u32[]{:S(2)}, u32[]{:S(2)}) collective-permute-start(bf16[512,256]{1,0:T(8,128)(2,1)} %get-tuple-element.39), channel_id=1, source_target_pairs={{0,1},{1,3},{2,0},{3,2},{4,5},{5,7},{6,4},{7,6},{8,9},{9,11},{10,8... | collective-permute-start | bytes 786440 | tf_op jit(solution)/shard_map/ppermute | solution.py:316
  17.1 1.1 copy-start.6
  17.1 1.3 %copy-start.8 = (bf16[2,256,512]{2,1,0:T(8,128)(2,1)S(1)}, bf16[2,256,512]{2,1,0:T(8,128)(2,1)}, u32[]{:S(2)}) copy-start(bf16[2,256,512]{2,1,0:T(8,128)(2,1)} %w2_hbm.7) | copy-start | bytes 1572868
  18.4 1.1 copy-start.2
  18.4 1.3 %copy-start.3 = (bf16[2,512,256]{2,1,0:T(8,128)(2,1)S(1)}, bf16[2,512,256]{2,1,0:T(8,128)(2,1)}, u32[]{:S(2)}) copy-start(bf16[2,512,256]{2,1,0:T(8,128)(2,1)} %wd_hbm.5) | copy-start | bytes 1572868
  20.4 1.4 %copy-start.12 = (bf16[1,1024,256]{2,1,0:T(8,128)(2,1)S(1)}, bf16[1,1024,256]{2,1,0:T(8,128)(2,1)}, u32[]{:S(2)}) copy-start(bf16[1,1024,256]{2,1,0:T(8,128)(2,1)} %param.18) | copy-start | bytes 1572868
  21.7 32.0 %collective-permute-start.19 = (bf16[784,256]{1,0:T(8,128)(2,1)}, bf16[784,256]{1,0:T(8,128)(2,1)}, u32[]{:S(2)}, u32[]{:S(2)}) collective-permute-start(bf16[784,256]{1,0:T(8,128)(2,1)} %pad_maximum_fusion.2), channel_id=1, source_target_pairs={{0,2},{2,0},{1,3},{3,1},{4,6},{6,4},{5,7},{7,5},{8,10},{10,8},{9,1... | collective-permute-start | bytes 1204232 | tf_op jit(solution)/shard_map/ppermute | solution.py:331
  22.5 16.9 %collective-permute-start.15 = (bf16[512,256]{1,0:T(8,128)(2,1)S(1)}, bf16[512,256]{1,0:T(8,128)(2,1)}, u32[]{:S(2)}, u32[]{:S(2)}) collective-permute-start(bf16[512,256]{1,0:T(8,128)(2,1)S(1)} %get-tuple-element.18), channel_id=1, source_target_pairs={{0,0},{1,2},{2,1},{3,3},{4,4},{5,6},{6,5},{7,7},{8,8},{9,10},{10,9... | collective-permute-start | bytes 786440 | tf_op jit(solution)/shard_map/ppermute | solution.py:315
  27.1 25.3 %collective-permute-start.4 = (bf16[784,256]{1,0:T(8,128)(2,1)}, bf16[784,256]{1,0:T(8,128)(2,1)S(1)}, u32[]{:S(2)}, u32[]{:S(2)}) collective-permute-start(bf16[784,256]{1,0:T(8,128)(2,1)} %pad_maximum_fusion), channel_id=1, source_target_pairs={{0,2},{2,0},{1,3},{3,1},{4,6},{6,4},{5,7},{7,5},{8,10},{10,8},{9,1... | collective-permute-start | bytes 1204232 | tf_op jit(solution)/shard_map/ppermute | solution.py:331
  27.1 3.5 %copy-start.20 = (bf16[256,256]{1,0:T(8,128)(2,1)S(1)}, bf16[256,256]{1,0:T(8,128)(2,1)}, u32[]{:S(2)}) copy-start(bf16[256,256]{1,0:T(8,128)(2,1)} %get-tuple-element.45) | copy-start | bytes 393220
  27.1 3.5 %copy-start.21 = (bf16[256,256]{1,0:T(8,128)(2,1)S(1)}, bf16[256,256]{1,0:T(8,128)(2,1)}, u32[]{:S(2)}) copy-start(bf16[256,256]{1,0:T(8,128)(2,1)} %get-tuple-element.34) | copy-start | bytes 393220
  27.1 3.5 %copy-start.22 = (bf16[256,256]{1,0:T(8,128)(2,1)S(1)}, bf16[256,256]{1,0:T(8,128)(2,1)}, u32[]{:S(2)}) copy-start(bf16[256,256]{1,0:T(8,128)(2,1)} %get-tuple-element.47) | copy-start | bytes 393220
  27.1 21.2 %collective-permute-start.16 = (bf16[512,256]{1,0:T(8,128)(2,1)S(1)}, bf16[512,256]{1,0:T(8,128)(2,1)S(1)}, u32[]{:S(2)}, u32[]{:S(2)}) collective-permute-start(bf16[512,256]{1,0:T(8,128)(2,1)S(1)} %get-tuple-element.19), channel_id=1, source_target_pairs={{0,1},{1,3},{2,0},{3,2},{4,5},{5,7},{6,4},{7,6},{8,9},{9,11},{10,8... | collective-permute-start | bytes 786440 | tf_op jit(solution)/shard_map/ppermute | solution.py:316
  30.0 30.2 %collective-permute-start.2 = (bf16[512,512]{1,0:T(8,128)(2,1)S(1)}, bf16[512,512]{1,0:T(8,128)(2,1)S(1)}, u32[]{:S(2)}, u32[]{:S(2)}) collective-permute-start(bf16[512,512]{1,0:T(8,128)(2,1)S(1)} %maximum_select_fusion.own_hbm), channel_id=1, source_target_pairs={{0,1},{1,0},{2,3},{3,2},{4,5},{5,4},{6,7},{7,6},{8,9},{9,8},{10,11... | collective-permute-start | bytes 1572872 | tf_op jit(solution)/shard_map/ppermute | solution.py:331
  30.7 28.7 %copy-start.17 = (bf16[256,256]{1,0:T(8,128)(2,1)S(1)}, bf16[256,256]{1,0:T(8,128)(2,1)}, u32[]{:S(2)}) copy-start(bf16[256,256]{1,0:T(8,128)(2,1)} %get-tuple-element.26) | copy-start | bytes 393220
  30.7 28.7 %copy-start.18 = (bf16[256,256]{1,0:T(8,128)(2,1)S(1)}, bf16[256,256]{1,0:T(8,128)(2,1)}, u32[]{:S(2)}) copy-start(bf16[256,256]{1,0:T(8,128)(2,1)} %get-tuple-element.30) | copy-start | bytes 393220
  30.7 28.6 %copy-start.19 = (bf16[256,256]{1,0:T(8,128)(2,1)S(1)}, bf16[256,256]{1,0:T(8,128)(2,1)}, u32[]{:S(2)}) copy-start(bf16[256,256]{1,0:T(8,128)(2,1)} %get-tuple-element.43) | copy-start | bytes 393220
  39.4 14.8 %collective-permute-start.8 = (bf16[784,256]{1,0:T(8,128)(2,1)S(1)}, bf16[784,256]{1,0:T(8,128)(2,1)}, u32[]{:S(2)}, u32[]{:S(2)}) collective-permute-start(bf16[784,256]{1,0:T(8,128)(2,1)S(1)} %pad_maximum_fusion.1), channel_id=1, source_target_pairs={{0,2},{2,0},{1,3},{3,1},{4,6},{6,4},{5,7},{7,5},{8,10},{10,8},{9,1... | collective-permute-start | bytes 1204232 | tf_op jit(solution)/shard_map/ppermute | solution.py:331
  48.3 15.9 %collective-permute-start.3 = (bf16[512,512]{1,0:T(8,128)(2,1)S(1)}, bf16[512,512]{1,0:T(8,128)(2,1)}, u32[]{:S(2)}, u32[]{:S(2)}) collective-permute-start(bf16[512,512]{1,0:T(8,128)(2,1)S(1)} %maximum_select_fusion.own_hbm), channel_id=1, source_target_pairs={{1,4},{0,13},{5,8},{4,1},{9,12},{8,5},{13,0},{12,9},{3,6},{2,15},{... | collective-permute-start | bytes 1572872 | tf_op jit(solution)/shard_map/ppermute | solution.py:342
  52.5 1.3 %copy-start.15 = (bf16[784,256]{1,0:T(8,128)(2,1)}, bf16[784,256]{1,0:T(8,128)(2,1)S(1)}, u32[]{:S(2)}) copy-start(bf16[784,256]{1,0:T(8,128)(2,1)S(1)} %collective-permute-done.4.near_hbm) | copy-start | bytes 1204228
  52.5 11.7 %collective-permute-start.5 = (bf16[784,256]{1,0:T(8,128)(2,1)S(1)}, bf16[784,256]{1,0:T(8,128)(2,1)}, u32[]{:S(2)}, u32[]{:S(2)}) collective-permute-start(bf16[784,256]{1,0:T(8,128)(2,1)S(1)} %collective-permute-done.4.near_hbm), channel_id=1, source_target_pairs={{0,1},{1,0},{2,3},{3,2},{4,5},{5,4},{6,7},{7,6},{8,9},{9,8},{10,11... | collective-permute-start | bytes 1204232 | tf_op jit(solution)/shard_map/ppermute | solution.py:331
  53.8 26.5 %collective-permute-start.17 = (bf16[512,512]{1,0:T(8,128)(2,1)S(1)}, bf16[512,512]{1,0:T(8,128)(2,1)}, u32[]{:S(2)}, u32[]{:S(2)}) collective-permute-start(bf16[512,512]{1,0:T(8,128)(2,1)S(1)} %maximum_select_fusion.2.own_hbm), channel_id=1, source_target_pairs={{0,1},{1,0},{2,3},{3,2},{4,5},{5,4},{6,7},{7,6},{8,9},{9,8},{10,11... | collective-permute-start | bytes 1572872 | tf_op jit(solution)/shard_map/ppermute | solution.py:331
  54.2 26.4 %collective-permute-start.18 = (bf16[512,512]{1,0:T(8,128)(2,1)S(1)}, bf16[512,512]{1,0:T(8,128)(2,1)}, u32[]{:S(2)}, u32[]{:S(2)}) collective-permute-start(bf16[512,512]{1,0:T(8,128)(2,1)S(1)} %maximum_select_fusion.2.own_hbm), channel_id=1, source_target_pairs={{1,4},{5,8},{4,1},{9,12},{8,5},{12,9},{3,6},{7,10},{6,3},{11,14},{... | collective-permute-start | bytes 1572872 | tf_op jit(solution)/shard_map/ppermute | solution.py:342
  61.0 19.2 %collective-permute-start.20 = (bf16[784,256]{1,0:T(8,128)(2,1)}, bf16[784,256]{1,0:T(8,128)(2,1)}, u32[]{:S(2)}, u32[]{:S(2)}) collective-permute-start(bf16[784,256]{1,0:T(8,128)(2,1)} %collective-permute-done.19.near_hbm), channel_id=1, source_target_pairs={{0,1},{1,0},{2,3},{3,2},{4,5},{5,4},{6,7},{7,6},{8,9},{9,8},{10,11... | collective-permute-start | bytes 1204232 | tf_op jit(solution)/shard_map/ppermute | solution.py:331
  62.3 6.1 %copy-start.23 = (s32[512]{0:T(512)S(1)}, s32[512]{0:T(512)}, u32[]{:S(2)}) copy-start(s32[512]{0:T(512)} %add_select_fusion) | copy-start | bytes 6148
  64.2 26.0 %collective-permute-start.23 = (bf16[784,256]{1,0:T(8,128)(2,1)}, bf16[784,256]{1,0:T(8,128)(2,1)}, u32[]{:S(2)}, u32[]{:S(2)}) collective-permute-start(bf16[784,256]{1,0:T(8,128)(2,1)} %pad_maximum_fusion.3), channel_id=1, source_target_pairs={{0,2},{2,0},{1,3},{3,1},{4,6},{6,4},{5,7},{7,5},{8,10},{10,8},{9,1... | collective-permute-start | bytes 1204232 | tf_op jit(solution)/shard_map/ppermute | solution.py:331
  64.2 29.1 %collective-permute-start.9 = (bf16[784,256]{1,0:T(8,128)(2,1)}, bf16[784,256]{1,0:T(8,128)(2,1)}, u32[]{:S(2)}, u32[]{:S(2)}) collective-permute-start(bf16[784,256]{1,0:T(8,128)(2,1)} %collective-permute-done.8.near_hbm), channel_id=1, source_target_pairs={{0,1},{1,0},{2,3},{3,2},{4,5},{5,4},{6,7},{7,6},{8,9},{9,8},{10,11... | collective-permute-start | bytes 1204232 | tf_op jit(solution)/shard_map/ppermute | solution.py:331
  69.4 1.0 copy-start.14
  70.5 1.0 copy-start.16
  80.2 1.0 copy-start.7
  80.2 13.2 %collective-permute-start.6 = (bf16[512,512]{1,0:T(8,128)(2,1)}, bf16[512,512]{1,0:T(8,128)(2,1)}, u32[]{:S(2)}, u32[]{:S(2)}) collective-permute-start(bf16[512,512]{1,0:T(8,128)(2,1)} %graph_layer.4.own_hbm), channel_id=1, source_target_pairs={{0,1},{1,0},{2,3},{3,2},{4,5},{5,4},{6,7},{7,6},{8,9},{9,8},{10,11... | collective-permute-start | bytes 1572872 | tf_op jit(solution)/shard_map/ppermute | solution.py:331
  80.3 14.6 %collective-permute-start.7 = (bf16[512,512]{1,0:T(8,128)(2,1)}, bf16[512,512]{1,0:T(8,128)(2,1)}, u32[]{:S(2)}, u32[]{:S(2)}) collective-permute-start(bf16[512,512]{1,0:T(8,128)(2,1)} %graph_layer.4.own_hbm), channel_id=1, source_target_pairs={{1,4},{0,13},{5,8},{4,1},{9,12},{8,5},{13,0},{12,9},{3,6},{2,15},{... | collective-permute-start | bytes 1572872 | tf_op jit(solution)/shard_map/ppermute | solution.py:342
  81.2 1.0 copy-start.9
  90.1 17.9 %collective-permute-start.21 = (bf16[512,512]{1,0:T(8,128)(2,1)S(1)}, bf16[512,512]{1,0:T(8,128)(2,1)S(1)}, u32[]{:S(2)}, u32[]{:S(2)}) collective-permute-start(bf16[512,512]{1,0:T(8,128)(2,1)S(1)} %graph_layer.6.own_hbm), channel_id=1, source_target_pairs={{0,1},{1,0},{2,3},{3,2},{4,5},{5,4},{6,7},{7,6},{8,9},{9,8},{10,11... | collective-permute-start | bytes 1572872 | tf_op jit(solution)/shard_map/ppermute | solution.py:331
  90.2 17.8 %collective-permute-start.22 = (bf16[512,512]{1,0:T(8,128)(2,1)S(1)}, bf16[512,512]{1,0:T(8,128)(2,1)S(1)}, u32[]{:S(2)}, u32[]{:S(2)}) collective-permute-start(bf16[512,512]{1,0:T(8,128)(2,1)S(1)} %graph_layer.6.own_hbm), channel_id=1, source_target_pairs={{1,4},{5,8},{4,1},{9,12},{8,5},{12,9},{3,6},{7,10},{6,3},{11,14},{... | collective-permute-start | bytes 1572872 | tf_op jit(solution)/shard_map/ppermute | solution.py:342
  93.3 14.7 %collective-permute-start.24 = (bf16[784,256]{1,0:T(8,128)(2,1)}, bf16[784,256]{1,0:T(8,128)(2,1)S(1)}, u32[]{:S(2)}, u32[]{:S(2)}) collective-permute-start(bf16[784,256]{1,0:T(8,128)(2,1)} %collective-permute-done.23.near_hbm), channel_id=1, source_target_pairs={{0,1},{1,0},{2,3},{3,2},{4,5},{5,4},{6,7},{7,6},{8,9},{9,8},{10,11... | collective-permute-start | bytes 1204232 | tf_op jit(solution)/shard_map/ppermute | solution.py:331
  103.8 14.0 %collective-permute-start.11 = (bf16[512,256]{1,0:T(8,128)(2,1)}, bf16[512,256]{1,0:T(8,128)(2,1)S(1)}, u32[]{:S(2)}, u32[]{:S(2)}) collective-permute-start(bf16[512,256]{1,0:T(8,128)(2,1)} %get-tuple-element.13), channel_id=1, source_target_pairs={{0,2},{1,0},{2,3},{3,1},{4,6},{5,4},{6,7},{7,5},{8,10},{9,8},{10,1... | collective-permute-start | bytes 786440 | tf_op jit(solution)/shard_map/ppermute | solution.py:322
  103.8 14.0 %collective-permute-start.10 = (bf16[512,256]{1,0:T(8,128)(2,1)S(1)}, bf16[512,256]{1,0:T(8,128)(2,1)S(1)}, u32[]{:S(2)}, u32[]{:S(2)}) collective-permute-start(bf16[512,256]{1,0:T(8,128)(2,1)S(1)} %get-tuple-element.12), channel_id=1, source_target_pairs={{0,0},{1,2},{2,1},{3,3},{4,4},{5,6},{6,5},{7,7},{8,8},{9,10},{10,9... | collective-permute-start | bytes 786440 | tf_op jit(solution)/shard_map/ppermute | solution.py:321
  115.8 10.0 %collective-permute-start.25 = (bf16[512,256]{1,0:T(8,128)(2,1)S(1)}, bf16[512,256]{1,0:T(8,128)(2,1)S(1)}, u32[]{:S(2)}, u32[]{:S(2)}) collective-permute-start(bf16[512,256]{1,0:T(8,128)(2,1)S(1)} %get-tuple-element.20), channel_id=1, source_target_pairs={{0,0},{1,2},{2,1},{3,3},{4,4},{5,6},{6,5},{7,7},{8,8},{9,10},{10,9... | collective-permute-start | bytes 786440 | tf_op jit(solution)/shard_map/ppermute | solution.py:321
  117.7 8.0 %collective-permute-start.26 = (bf16[512,256]{1,0:T(8,128)(2,1)S(1)}, bf16[512,256]{1,0:T(8,128)(2,1)S(1)}, u32[]{:S(2)}, u32[]{:S(2)}) collective-permute-start(bf16[512,256]{1,0:T(8,128)(2,1)S(1)} %get-tuple-element.21), channel_id=1, source_target_pairs={{0,2},{1,0},{2,3},{3,1},{4,6},{5,4},{6,7},{7,5},{8,10},{9,8},{10,1... | collective-permute-start | bytes 786440 | tf_op jit(solution)/shard_map/ppermute | solution.py:322
  (8 other events, 5.5 us)

commit v2 on v1

--- a/solution.py
+++ b/solution.py
@@ -9,6 +9,7 @@
 
 LANES = 128
 DEAD = -1e30
+SMALL = pl.CostEstimate(flops=1, bytes_accessed=1, transcendentals=0)
 
 
 def padded_2(shard, sides, width, wrap):
@@ -117,9 +118,7 @@
         in_specs=[pl.BlockSpec(memory_space=pltpu.SMEM), vmem, vmem],
         out_specs=(vmem,) * parts,
         compiler_params=pltpu.CompilerParams(vmem_limit_bytes=32 << 20),
-        cost_estimate=pl.CostEstimate(
-            flops=2 * parts * cap * rows * (total + feats), bytes_accessed=4 * rows * feats, transcendentals=0
-        ),
+        cost_estimate=SMALL,
         name="pick_rows",
     )(me, bnd, nodes)
 
@@ -149,15 +148,13 @@
         in_specs=[pl.BlockSpec(memory_space=pltpu.SMEM)] + [vmem] * (1 + len(pieces)),
         out_specs=(vmem, vmem),
         compiler_params=pltpu.CompilerParams(vmem_limit_bytes=32 << 20),
-        cost_estimate=pl.CostEstimate(
-            flops=2 * len(pieces) * cap * rows * feats, bytes_accessed=6 * rows * feats, transcendentals=0
-        ),
+        cost_estimate=SMALL,
         name="add_force",
     )(first, nodes, *pieces)
 
 
 def layer_kernel(
-    layer, slots, last, core_ref, idx_ref, own_hbm, sib_hbm, rim_hbm, ws_hbm, wd_hbm, w2_hbm, b_hbm, near_hbm, far_hbm,
+    layer, slots, last, spot, core_ref, idx_ref, own_hbm, sib_hbm, rim_hbm, ws_hbm, wd_hbm, w2_hbm, b_hbm, near_hbm, far_hbm,
     *refs,
 ):
     outs, refs = (refs[:2], refs[2:]) if last else (refs[:1], refs[1:])
@@ -168,7 +165,7 @@
     core = core_ref[0]
     pairs = (
         (own_hbm, own), (wd_hbm.at[layer], wd), (ws_hbm.at[layer], ws), (b_hbm, bias),
-        (near_hbm, near_w), (far_hbm, far_w), (sib_hbm, sib), (rim_hbm, rim), (w2_hbm.at[layer], w2),
+        (near_hbm.at[spot:spot + near_w.shape[0], :], near_w), (far_hbm.at[spot:spot + far_w.shape[0], :], far_w), (sib_hbm, sib), (rim_hbm, rim), (w2_hbm.at[layer], w2),
     )
     copies = [pltpu.make_async_copy(src, dst, sems.at[i]) for i, (src, dst) in enumerate(pairs)]
     for copy in copies:
@@ -218,8 +215,8 @@
         mine = near[spot, :]
         total = None
         for j in range(slots):
-            upper = proj[pl.ds(pl.multiple_of(idx_ref[2 * q * slots + j], 4), 8), :]
-            lower = proj[pl.ds(pl.multiple_of(idx_ref[(2 * q + 1) * slots + j], 4), 8), :]
+            upper = proj[pl.ds(pl.multiple_of(idx_ref[j * rows + 2 * q], 4), 8), :]
+            lower = proj[pl.ds(pl.multiple_of(idx_ref[j * rows + 2 * q + 1], 4), 8), :]
             y = jnp.where(low, upper, lower) + mine
             act = y * jnp.tanh(y) + y
             total = act if total is None else total + act
@@ -252,9 +249,10 @@
             outs[1][...] = result[:, :share]
 
 
-def run_layer(layer, slots, last, core, idx, own, sib, rim, ws, wd, w2, bias, near_w, far_w):
+def run_layer(layer, slots, last, core, idx, own, sib, rim, ws, wd, w2, bias, near_w, far_w, spot):
     rows, width = own.shape
     share = width // 2
+    pack = 3 * share + 16
     chunks = width // LANES
     anywhere = pl.BlockSpec(memory_space=pl.ANY)
     smem = pl.BlockSpec(memory_space=pltpu.SMEM)
@@ -267,9 +265,9 @@
         out_shape, out_specs = jax.ShapeDtypeStruct((rows, width), bf16), vmem
     edges = rows * slots
     return pl.pallas_call(
-        functools.partial(layer_kernel, layer, slots, last),
+        functools.partial(layer_kernel, layer, slots, last, spot * pack),
         out_shape=out_shape,
-        in_specs=[smem, smem] + [anywhere] * 9,
+        in_specs=[smem, smem] + [anywhere] * 3 + [pl.BlockSpec(memory_space=pltpu.HBM)] * 3 + [anywhere] * 3,
         out_specs=out_specs,
         scratch_shapes=[
             pltpu.VMEM((rows, width), bf16),
@@ -279,8 +277,8 @@
             pltpu.VMEM((width, share), bf16),
             pltpu.VMEM((share, width), bf16),
             pltpu.VMEM(bias.shape, bf16),
-            pltpu.VMEM(near_w.shape, bf16),
-            pltpu.VMEM(far_w.shape, bf16),
+            pltpu.VMEM((pack, share), bf16),
+            pltpu.VMEM((pack, share), bf16),
             pltpu.VMEM((width, share), bf16),
             pltpu.VMEM((width, share), bf16),
             pltpu.VMEM((share, width), bf16),
@@ -290,25 +288,23 @@
             pltpu.SemaphoreType.DMA((9,)),
         ],
         compiler_params=pltpu.CompilerParams(vmem_limit_bytes=32 << 20),
-        cost_estimate=pl.CostEstimate(
-            flops=2 * 5 * rows * width * width, bytes_accessed=10 * rows * width, transcendentals=edges * width
-        ),
+        cost_estimate=pl.CostEstimate(flops=64 * rows * width * width, bytes_accessed=10 * rows * width, transcendentals=0),
         name="graph_layer",
     )(core, idx, own, sib, rim, ws, wd, w2, bias, near_w, far_w)
 
 
-def edge_offsets(nbr, count, core):
-    rows, slots = nbr.shape
+def edge_offsets(nbrs, counts, core):
+    graphs, rows, slots = nbrs.shape
     half = rows // 2
-    nbr = lax.dynamic_slice(nbr, (core * half, 0), (half, slots)) - core * half
-    count = lax.dynamic_slice(count, (core * half,), (half,))
+    nbr = lax.dynamic_slice(nbrs.transpose(0, 2, 1), (0, 0, core * half), (graphs, slots, half)) - core * half
+    count = lax.dynamic_slice(counts, (0, core * half), (graphs, half))
     low = nbr + jnp.where(core == 0, 2 * half, half)
     high = nbr - jnp.where(core == 0, half, 0)
     place = jnp.where(nbr < half, low, jnp.where(nbr < 2 * half, nbr - half, high))
-    live = jnp.arange(slots, dtype=jnp.int32)[None, :] < count[:, None]
+    live = jnp.arange(slots, dtype=jnp.int32)[None, :, None] < count[:, None, :]
     place = jnp.where(live, place, 3 * half)
-    odd = jnp.arange(half, dtype=jnp.int32)[:, None] % 2
-    return (4 * (place + 1 - odd)).reshape(half * slots)
+    odd = jnp.arange(half, dtype=jnp.int32) % 2
+    return (4 * (place + 1 - odd)).reshape(graphs, slots * half)
 
 
 def spread_rows(same, other):
@@ -342,16 +338,48 @@
     return lax.ppermute(own, ("mesh", "batch"), pairs)
 
 
-def other_weights(layer, core, ws, wd, w2, bias):
-    share = ws.shape[2]
-    picked = [
-        lax.dynamic_slice(ws, (layer, core * share, 0), (1, share, share))[0],
-        lax.dynamic_slice(wd, (layer, core * share, 0), (1, share, share))[0],
-        lax.dynamic_slice(w2, (layer, 0, core * share), (1, share, share))[0],
-        jnp.broadcast_to(bias[layer][None], (16, share)),
-    ]
-    near_w = swap(jnp.concatenate(picked, 0), "mp")
-    return near_w, swap(near_w, "batch")
+def pack_kernel(plan, core_ref, g_bias, r_bias, *refs):
+    weights, refs = (refs[:3], refs[3:6]), refs[6:]
+    outs, (lines, sems) = refs[:-2], refs[-2:]
+    share = g_bias.shape[1]
+    here = pl.multiple_of(core_ref[0] * share, share)
+    count = 0
+    copies = []
+    for out, members in zip(outs, plan):
+        for place, (graph, layer) in enumerate(members):
+            base = place * (3 * share + 16)
+            ws, wd, w2 = weights[graph]
+            bias = (g_bias, r_bias)[graph][layer:layer + 1, :]
+            lines[16 * count:16 * count + 16, :] = jnp.broadcast_to(bias, (16, share))
+            sources = (
+                (ws.at[layer, pl.ds(here, share), :], share),
+                (wd.at[layer, pl.ds(here, share), :], share),
+                (w2.at[layer, :, pl.ds(here, share)], share),
+                (lines.at[16 * count:16 * count + 16, :], 16),
+            )
+            for i, (source, size) in enumerate(sources):
+                copies.append(pltpu.make_async_copy(source, out.at[base:base + size, :], sems.at[4 * count + i]))
+                copies[-1].start()
+                base += size
+            count += 1
+    for copy in copies:
+        copy.wait()
+
+
+def pack_weights(plan, core, g_weights, g_bias, r_weights, r_bias):
+    share = g_bias.shape[1]
+    sizes = [len(members) for members in plan]
+    hbm = pl.BlockSpec(memory_space=pltpu.HBM)
+    vmem = pl.BlockSpec(memory_space=pltpu.VMEM)
+    return pl.pallas_call(
+        functools.partial(pack_kernel, plan),
+        out_shape=tuple(jax.ShapeDtypeStruct((n * (3 * share + 16), share), jnp.bfloat16) for n in sizes),
+        in_specs=[pl.BlockSpec(memory_space=pltpu.SMEM), vmem, vmem] + [hbm] * 6,
+        out_specs=(hbm,) * len(plan),
+        scratch_shapes=[pltpu.VMEM((16 * sum(sizes), share), jnp.bfloat16), pltpu.SemaphoreType.DMA((4 * sum(sizes),))],
+        cost_estimate=SMALL,
+        name="pack_weights",
+    )(core, g_bias, r_bias, *g_weights, *r_weights)
 
 
 def by_rows(
@@ -369,33 +397,63 @@
     me = lax.axis_index("mesh").reshape(1)
     core1 = core.reshape(1)
     g_own, r_own = g_nodes[0], r_nodes[0]
+    g_weights, r_weights = (g_ws, g_wd, g_w2), (r_ws, r_wd, r_w2)
+    after = lax.optimization_barrier
 
     same = lax.dynamic_slice(g_own, (part * half, 0), (half, g_own.shape[1]))
     other = lax.dynamic_slice(g_own, ((1 - part) * half, 0), (half, g_own.shape[1]))
+    same, other, bnd_src = after((same, other, bnd_src))
     g_a, g_b = spread_rows(same, other)
     bnd = jnp.stack([bnd_src, bnd_part[:, 0], bnd_node])
     pieces = pick_rows(me, bnd, g_own, parts, cap)
     landed = [pieces[0]]
     for k in range(1, parts):
         landed.append(lax.ppermute(pieces[k], "mesh", [(i, (i + k) % parts) for i in range(parts)]))
-    g_idx = edge_offsets(g_nbr, g_count, core)
-    r_idx = edge_offsets(r_nbr, r_count, core)
+    idx = edge_offsets(jnp.stack([g_nbr, r_nbr]), jnp.stack([g_count, r_count]), core)
+
+    rest = tuple((graph, layer) for layer in range(1, layers) for graph in (0, 1))
+    plan = (((0, 0),), ((1, 0),)) + ((rest,) if rest else ())
+    g_a, g_b, g_idx, r_idx, core1, landed[0] = after((g_a, g_b, idx[0], idx[1], core1, landed[0]))
+    packs = pack_weights(plan, core1, g_weights, g_b1, r_weights, r_b1)
+    planet = ordered(core, g_a, g_b, 1)
+    near_w = [swap(packs[0], "mp")]
+    g_sib, g_rim = swap(planet, "batch"), rims(planet, True)
+    g_sib, r_own = after((g_sib, r_own))
     r_a, r_b = spread_rows(*add_force(part.reshape(1), r_own, landed, cap))
-
-    planet = ordered(core, g_a, g_b, 1)
+    r_a, r_b, sent, g_rim = after((r_a, r_b, packs[1], g_rim))
+    near_w.append(swap(sent, "mp"))
     regional = ordered(core, r_a, r_b, 1)
+    r_sib, r_rim = swap(regional, "batch"), rims(regional, False)
+    far_w = [swap(near_w[0], "batch")]
     for layer in range(layers):
         last = layer == layers - 1
-        g_w = other_weights(layer, core, g_ws, g_wd, g_w2, g_b1)
+        if layer:
+            g_sib, g_rim = swap(planet, "batch"), rims(planet, True)
+        spot = (0, 0) if layer == 0 else (2, 2 * layer - 2)
         planet = run_layer(
-            layer, slots, last, core1, g_idx, planet, swap(planet, "batch"), rims(planet, True),
-            g_ws, g_wd, g_w2, g_b1, *g_w,
+            layer, slots, last, core1, g_idx, planet, g_sib, g_rim,
+            g_ws, g_wd, g_w2, g_b1, near_w[spot[0]], far_w[spot[0]], spot[1],
         )
-        r_w = other_weights(layer, core, r_ws, r_wd, r_w2, r_b1)
+        *planet, core1 = after((*(planet if last else (planet,)), core1))
+        planet = planet if last else planet[0]
+        if layer == 0:
+            planet, near_w[1] = after((planet, near_w[1])) if rest else (planet, near_w[1])
+            far_w.append(swap(near_w[1], "batch"))
+            if rest:
+                sent, near_w[1] = after((packs[2], near_w[1]))
+                near_w.append(swap(sent, "mp"))
+        else:
+            r_sib, r_rim = swap(regional, "batch"), rims(regional, False)
+        spot = (1, 0) if layer == 0 else (2, 2 * layer - 1)
         regional = run_layer(
-            layer, slots, last, core1, r_idx, regional, swap(regional, "batch"), rims(regional, False),
-            r_ws, r_wd, r_w2, r_b1, *r_w,
+            layer, slots, last, core1, r_idx, regional, r_sib, r_rim,
+            r_ws, r_wd, r_w2, r_b1, near_w[spot[0]], far_w[spot[0]], spot[1],
         )
+        if not last:
+            regional, core1 = after((regional, core1))
+            if layer == 0:
+                regional, near_w[2] = after((regional, near_w[2]))
+                far_w.append(swap(near_w[2], "batch"))
     g_out = ordered(part, *gather_rows(*planet), 0)
     r_out = ordered(part, *gather_rows(*regional), 0)
     return g_out[None], r_out[None]

time: 128 us -> 183 us (1.43)
  Pallas kernels: 36.1 us -> 83.2 us
  waiting for transfers between devices: 27.2 us -> 47.8 us
  local copies, waits for them, and re-layouts: 15.4 us -> 1.91 us
  starting transfers between devices: 38.6 us -> 46.6 us
  other arithmetic: 8.43 us -> 2.42 us
    pallas_call x4 -> x5, Pallas kernels: 33.2 us -> 80.3 us  [the longest x1 49.6 us: pack_weights(): pl.pallas_call(functools.partial(pack_kernel, plan), out_shape=tuple((jax...]
    ppermute x12 -> x10, waiting for transfers between devices: 0.03 us -> 15.6 us  [swap(): return lax.ppermute(values, axis, [(0, 1), (1, 0)])]
    unnamed x58 -> x41, local copies, waits for them, and re-layouts: 9.15 us -> 0.78 us
    ppermute x3, waiting for transfers between devices: 0.01 us -> 6.21 us  [by_rows(): lax.ppermute(pieces[k], 'mesh', [(i, (i + k) % parts) for i in range(part...]
    ppermute x2, starting transfers between devices: 8.35 us -> 13.9 us  [spread_rows(): a = lax.ppermute(same, ('mp', 'batch'), [(0, 0), (1, 2), (2, 1), (3, 3)])]
    ppermute x4, waiting for transfers between devices: 2.63 us -> 7.92 us  [rims(): return lax.ppermute(own, ('mesh', 'batch'), pairs)]
    ppermute x2, waiting for transfers between devices: 8.91 us -> 4.12 us  [spread_rows(): b = lax.ppermute(other, ('mp', 'batch'), [(0, 1), (1, 3), (2, 0), (3, 2)])]
    ppermute x2, waiting for transfers between devices: 8.68 us -> 4.82 us  [spread_rows(): a = lax.ppermute(same, ('mp', 'batch'), [(0, 0), (1, 2), (2, 1), (3, 3)])]
  transfers between devices with their start and end apart: 27 -> 25, of which waited for: 5 -> 13; matrix products, arithmetic and copies ran while one was open for 11% -> 1% of each run, Pallas kernels for 27% -> 14%
where the time goes in v2:
time: 183 us
  Pallas kernels  83.2 us (45%)
  waiting for transfers between devices  47.8 us (26%)
  starting transfers between devices  46.6 us (25%)
  other arithmetic  2.42 us (1%)
  local copies, waits for them, and re-layouts  1.91 us (1%)
    pallas_call x1, Pallas kernels, pack_weights(): pl.pallas_call(functools.partial(pack_kernel, plan), out_shape=tuple((jax...  49.6 us
    pallas_call x4, Pallas kernels, run_layer(): pl.pallas_call(functools.partial(layer_kernel, layer, slots, last, spot *...  30.7 us
    ppermute x10, waiting for transfers between devices, swap(): return lax.ppermute(values, axis, [(0, 1), (1, 0)])  15.6 us
    ppermute x2, starting transfers between devices, spread_rows(): a = lax.ppermute(same, ('mp', 'batch'), [(0, 0), (1, 2), (2, 1), (3, 3)])  13.9 us
    ppermute x4, starting transfers between devices, rims(): return lax.ppermute(own, ('mesh', 'batch'), pairs)  12.9 us
    ppermute x2, waiting for transfers between devices, gather_rows(): same = lax.ppermute(a, ('mp', 'batch'), [(0, 0), (1, 2), (2, 1), (3, 3)])  9.03 us
    ppermute x10, starting transfers between devices, swap(): return lax.ppermute(values, axis, [(0, 1), (1, 0)])  8.55 us
    ppermute x4, waiting for transfers between devices, rims(): return lax.ppermute(own, ('mesh', 'batch'), pairs)  7.92 us
  transfers between devices with their start and end apart: 25, of which 13 were waited for; matrix products, arithmetic and copies ran while one was open for 1% of the time, Pallas kernels for 14%

profile of v2, /device:TPU:1, one launch (start us, length us, event | category | flops | bytes accessed | tf_op | source)
XLA Modules:
  0.0 183.0 jit_solution(5371179738363387982)
XLA Ops:
  0.7 1.1 dynamic-slice_bitcast_fusion
  1.8 4.5 %collective-permute-start = (bf16[512,256]{1,0:T(8,128)(2,1)S(1)}, bf16[512,256]{1,0:T(8,128)(2,1)S(1)}, u32[]{:S(2)}, u32[]{:S(2)}) collective-permute-start(bf16[512,256]{1,0:T(8,128)(2,1)S(1)} %get-tuple-element.43), channel_id=1, source_target_pairs={{0,0},{1,2},{2,1},{3,3},{4,4},{5,6},{6,5},{7,7},{8,8},{9,10},{10,9... | collective-permute-start | bytes 786440 | tf_op jit(solution)/shard_map/ppermute | solution.py:311
  6.4 0.1 fusion.5
  6.6 0.6 copy-done.16
  7.2 0.0 copy-done.15
  7.3 2.2 %pick_rows.1 = (bf16[272,256]{1,0:T(8,128)(2,1)S(1)}, bf16[272,256]{1,0:T(8,128)(2,1)S(1)}, bf16[272,256]{1,0:T(8,128)(2,1)S(1)}, bf16[272,256]{1,0:T(8,128)(2,1)S(1)}) custom-call(s32[1]{0:T(128)} %bitcast.8.me_ref, s32[3,512]{1,0:T(4,128)S(1)} %pad_add_fusion.bnd_ref, bf16[1024,256]{1,0:T(8,128)(2,1)S(1)} %bitcast.34), custom_call_target="tpu_custom_call" | custom-call | flops 1 | bytes 1 | tf_op jit(solution)/shard_map/pick_rows/pallas_call | solution.py:115
  9.6 0.8 collective-permute-done
  10.4 2.1 %collective-permute-done.1 = bf16[512,256]{1,0:T(8,128)(2,1)S(1)} collective-permute-done((bf16[512,256]{1,0:T(8,128)(2,1)S(1)}, bf16[512,256]{1,0:T(8,128)(2,1)S(1)}, u32[]{:S(2)}, u32[]{:S(2)}) %collective-permute-start.1) | collective-permute-done | bytes 262176 | tf_op jit(solution)/shard_map/ppermute | solution.py:312
  12.4 49.6 %pack_weights.1 = (bf16[784,256]{1,0:T(8,128)(2,1)}, bf16[784,256]{1,0:T(8,128)(2,1)}, bf16[1568,256]{1,0:T(8,128)(2,1)}) custom-call(s32[1]{0:T(128)} %bitcast.7.core_ref, bf16[2,256]{1,0:T(2,128)(2,1)} %b_hbm.6, bf16[2,256]{1,0:T(2,128)(2,1)} %b_hbm.7, bf16[2,512,256]{2,1,0:T(8,128)(2,1)} %ws_hbm.6, bf16[2,512,256]{2,1,0:T(8,128)(2,1)} %wd_hbm.6, ...), custom_call_target="tpu_custom_call" | custom-call | flops 1 | bytes 1 | tf_op jit(solution)/shard_map/pack_weights/pallas_call | solution.py:374
  62.1 2.0 %collective-permute-start.9 = (bf16[784,256]{1,0:T(8,128)(2,1)}, bf16[784,256]{1,0:T(8,128)(2,1)S(1)}, u32[]{:S(2)}, u32[]{:S(2)}) collective-permute-start(bf16[784,256]{1,0:T(8,128)(2,1)} %get-tuple-element.61), channel_id=1, source_target_pairs={{0,2},{2,0},{1,3},{3,1},{4,6},{6,4},{5,7},{7,5},{8,10},{10,8},{9,1... | collective-permute-start | bytes 1204232 | tf_op jit(solution)/shard_map/ppermute | solution.py:327
  64.0 0.1 maximum_select_fusion.own_hbm
  64.2 0.1 collective-permute-start.2
  64.2 1.7 collective-permute-start.8
  65.9 1.3 collective-permute-start.3
  67.2 1.0 collective-permute-start.4
  68.2 4.9 %collective-permute-done.9.near_hbm = bf16[784,256]{1,0:T(8,128)(2,1)S(1)} collective-permute-done((bf16[784,256]{1,0:T(8,128)(2,1)}, bf16[784,256]{1,0:T(8,128)(2,1)S(1)}, u32[]{:S(2)}, u32[]{:S(2)}) %collective-permute-start.9) | collective-permute-done | bytes 401440 | tf_op jit(solution)/shard_map/ppermute | solution.py:327
  73.2 3.3 %collective-permute-start.5 = (bf16[272,256]{1,0:T(8,128)(2,1)S(1)}, bf16[272,256]{1,0:T(8,128)(2,1)S(1)}, u32[]{:S(2)}, u32[]{:S(2)}) collective-permute-start(bf16[272,256]{1,0:T(8,128)(2,1)S(1)} %get-tuple-element.56), channel_id=1, source_target_pairs={{0,12},{4,0},{8,4},{12,8},{1,13},{5,1},{9,5},{13,9},{2,14},{6,2},{... | collective-permute-start | bytes 417800 | tf_op jit(solution)/shard_map/ppermute | solution.py:411
  76.5 1.6 collective-permute-start.10
  78.1 4.8 %collective-permute-done.3.refs_1_ = bf16[272,256]{1,0:T(8,128)(2,1)S(1)} collective-permute-done((bf16[272,256]{1,0:T(8,128)(2,1)S(1)}, bf16[272,256]{1,0:T(8,128)(2,1)S(1)}, u32[]{:S(2)}, u32[]{:S(2)}) %collective-permute-start.3) | collective-permute-done | bytes 139296 | tf_op jit(solution)/shard_map/ppermute | solution.py:411
  82.9 1.4 collective-permute-done.5.refs_3_
  84.3 0.7 add_force.1
  85.0 9.4 %collective-permute-start.6 = (bf16[512,256]{1,0:T(8,128)(2,1)S(1)}, bf16[512,256]{1,0:T(8,128)(2,1)S(1)}, u32[]{:S(2)}, u32[]{:S(2)}) collective-permute-start(bf16[512,256]{1,0:T(8,128)(2,1)S(1)} %get-tuple-element.57), channel_id=1, source_target_pairs={{0,0},{1,2},{2,1},{3,3},{4,4},{5,6},{6,5},{7,7},{8,8},{9,10},{10,9... | collective-permute-start | bytes 786440 | tf_op jit(solution)/shard_map/ppermute | solution.py:311
  94.5 4.0 %collective-permute-done.6 = bf16[512,256]{1,0:T(8,128)(2,1)S(1)} collective-permute-done((bf16[512,256]{1,0:T(8,128)(2,1)S(1)}, bf16[512,256]{1,0:T(8,128)(2,1)S(1)}, u32[]{:S(2)}, u32[]{:S(2)}) %collective-permute-start.6) | collective-permute-done | bytes 262176 | tf_op jit(solution)/shard_map/ppermute | solution.py:311
  98.5 2.1 %collective-permute-done.7 = bf16[512,256]{1,0:T(8,128)(2,1)S(1)} collective-permute-done((bf16[512,256]{1,0:T(8,128)(2,1)S(1)}, bf16[512,256]{1,0:T(8,128)(2,1)S(1)}, u32[]{:S(2)}, u32[]{:S(2)}) %collective-permute-start.7) | collective-permute-done | bytes 262176 | tf_op jit(solution)/shard_map/ppermute | solution.py:312
  100.5 0.1 maximum_select_fusion.1.own_hbm
  100.7 1.5 collective-permute-start.11
  102.2 3.7 %collective-permute-start.12 = (bf16[512,512]{1,0:T(8,128)(2,1)S(1)}, bf16[512,512]{1,0:T(8,128)(2,1)S(1)}, u32[]{:S(2)}, u32[]{:S(2)}) collective-permute-start(bf16[512,512]{1,0:T(8,128)(2,1)S(1)} %maximum_select_fusion.1.own_hbm), channel_id=1, source_target_pairs={{1,4},{5,8},{4,1},{9,12},{8,5},{12,9},{3,6},{7,10},{6,3},{11,14},{... | collective-permute-start | bytes 1572872 | tf_op jit(solution)/shard_map/ppermute | solution.py:338
  105.9 0.9 collective-permute-start.13
  106.8 7.6 %graph_layer.4.own_hbm = bf16[512,512]{1,0:T(8,128)(2,1)S(1)} custom-call(s32[1]{0:T(128)} %bitcast.7.core_ref, s32[4096]{0:T(1024)S(1)} %bitcast.38, bf16[512,512]{1,0:T(8,128)(2,1)S(1)} %maximum_select_fusion.own_hbm, bf16[512,512]{1,0:T(8,128)(2,1)S(1)} %collective-permute-done.2.sib_hbm, bf16[512,512]{1,0:T(8,128)(2,1)S(1)} %collective-permute-done.8.rim_hbm, ...), custom_call_target="tpu_custom_call" | custom-call | flops 8589934592 | bytes 2621440 | tf_op jit(solution)/shard_map/graph_layer/pallas_call | solution.py:267
  114.5 0.1 collective-permute-done.13.near_hbm
  114.6 0.8 collective-permute-start.17
  115.4 0.9 collective-permute-done.14.far_hbm
  116.4 7.6 %graph_layer.5.own_hbm = bf16[512,512]{1,0:T(8,128)(2,1)S(1)} custom-call(s32[1]{0:T(128)} %bitcast.7.core_ref, s32[4096]{0:T(1024)S(1)} %bitcast.36, bf16[512,512]{1,0:T(8,128)(2,1)S(1)} %maximum_select_fusion.1.own_hbm, bf16[512,512]{1,0:T(8,128)(2,1)S(1)} %collective-permute-done.11.sib_hbm, bf16[512,512]{1,0:T(8,128)(2,1)S(1)} %collective-permute-done.12.rim_hbm, ...), custom_call_target="tpu_custom_call" | custom-call | flops 8589934592 | bytes 2621440 | tf_op jit(solution)/shard_map/graph_layer/pallas_call | solution.py:267
  124.0 9.7 %collective-permute-done.17.near_hbm = bf16[1568,256]{1,0:T(8,128)(2,1)S(1)} collective-permute-done((bf16[1568,256]{1,0:T(8,128)(2,1)S(1)}, bf16[1568,256]{1,0:T(8,128)(2,1)S(1)}, u32[]{:S(2)}, u32[]{:S(2)}) %collective-permute-start.17) | collective-permute-done | bytes 802848 | tf_op jit(solution)/shard_map/ppermute | solution.py:327
  133.7 1.3 collective-permute-start.18
  135.0 3.4 %collective-permute-start.16 = (bf16[512,512]{1,0:T(8,128)(2,1)S(1)}, bf16[512,512]{1,0:T(8,128)(2,1)S(1)}, u32[]{:S(2)}, u32[]{:S(2)}) collective-permute-start(bf16[512,512]{1,0:T(8,128)(2,1)S(1)} %graph_layer.4.own_hbm), channel_id=1, source_target_pairs={{1,4},{0,13},{5,8},{4,1},{9,12},{8,5},{13,0},{12,9},{3,6},{2,15},{... | collective-permute-start | bytes 1572872 | tf_op jit(solution)/shard_map/ppermute | solution.py:338
  138.4 0.4 collective-permute-start.21
  138.8 4.1 %collective-permute-start.22 = (bf16[512,512]{1,0:T(8,128)(2,1)S(1)}, bf16[512,512]{1,0:T(8,128)(2,1)S(1)}, u32[]{:S(2)}, u32[]{:S(2)}) collective-permute-start(bf16[512,512]{1,0:T(8,128)(2,1)S(1)} %graph_layer.5.own_hbm), channel_id=1, source_target_pairs={{1,4},{5,8},{4,1},{9,12},{8,5},{12,9},{3,6},{7,10},{6,3},{11,14},{... | collective-permute-start | bytes 1572872 | tf_op jit(solution)/shard_map/ppermute | solution.py:338
  142.9 7.9 %collective-permute-done.16.rim_hbm = bf16[512,512]{1,0:T(8,128)(2,1)S(1)} collective-permute-done((bf16[512,512]{1,0:T(8,128)(2,1)S(1)}, bf16[512,512]{1,0:T(8,128)(2,1)S(1)}, u32[]{:S(2)}, u32[]{:S(2)}) %collective-permute-start.16) | collective-permute-done | bytes 524320 | tf_op jit(solution)/shard_map/ppermute | solution.py:338
  150.8 7.7 %graph_layer.6 = (bf16[512,256]{1,0:T(8,128)(2,1)S(1)}, bf16[512,256]{1,0:T(8,128)(2,1)S(1)}) custom-call(s32[1]{0:T(128)} %bitcast.7.core_ref, s32[4096]{0:T(1024)S(1)} %bitcast.39, bf16[512,512]{1,0:T(8,128)(2,1)S(1)} %graph_layer.4.own_hbm, bf16[512,512]{1,0:T(8,128)(2,1)S(1)} %collective-permute-done.15.sib_hbm, ...), custom_call_target="tpu_custom_call" | custom-call | flops 8589934592 | bytes 2621440 | tf_op jit(solution)/shard_map/graph_layer/pallas_call | solution.py:267
  158.6 7.7 %graph_layer.7 = (bf16[512,256]{1,0:T(8,128)(2,1)S(1)}, bf16[512,256]{1,0:T(8,128)(2,1)S(1)}) custom-call(s32[1]{0:T(128)} %bitcast.7.core_ref, s32[4096]{0:T(1024)S(1)} %bitcast.37, bf16[512,512]{1,0:T(8,128)(2,1)S(1)} %graph_layer.5.own_hbm, bf16[512,512]{1,0:T(8,128)(2,1)S(1)} %collective-permute-done.21.sib_hbm, ...), custom_call_target="tpu_custom_call" | custom-call | flops 8589934592 | bytes 2621440 | tf_op jit(solution)/shard_map/graph_layer/pallas_call | solution.py:267
  166.3 2.0 %collective-permute-start.23 = (bf16[512,256]{1,0:T(8,128)(2,1)S(1)}, bf16[512,256]{1,0:T(8,128)(2,1)S(1)}, u32[]{:S(2)}, u32[]{:S(2)}) collective-permute-start(bf16[512,256]{1,0:T(8,128)(2,1)S(1)} %get-tuple-element.82), channel_id=1, source_target_pairs={{0,0},{1,2},{2,1},{3,3},{4,4},{5,6},{6,5},{7,7},{8,8},{9,10},{10,9... | collective-permute-start | bytes 786440 | tf_op jit(solution)/shard_map/ppermute | solution.py:317
  168.3 0.0 collective-permute-start.24
  168.3 3.5 %collective-permute-start.19 = (bf16[512,256]{1,0:T(8,128)(2,1)S(1)}, bf16[512,256]{1,0:T(8,128)(2,1)S(1)}, u32[]{:S(2)}, u32[]{:S(2)}) collective-permute-start(bf16[512,256]{1,0:T(8,128)(2,1)S(1)} %get-tuple-element.78), channel_id=1, source_target_pairs={{0,0},{1,2},{2,1},{3,3},{4,4},{5,6},{6,5},{7,7},{8,8},{9,10},{10,9... | collective-permute-start | bytes 786440 | tf_op jit(solution)/shard_map/ppermute | solution.py:317
  171.9 4.8 %collective-permute-done.23 = bf16[512,256]{1,0:T(8,128)(2,1)S(1)} collective-permute-done((bf16[512,256]{1,0:T(8,128)(2,1)S(1)}, bf16[512,256]{1,0:T(8,128)(2,1)S(1)}, u32[]{:S(2)}, u32[]{:S(2)}) %collective-permute-start.23) | collective-permute-done | bytes 262176 | tf_op jit(solution)/shard_map/ppermute | solution.py:317
  176.7 1.0 maximum_select_fusion.3
  177.7 4.3 %collective-permute-done.19 = bf16[512,256]{1,0:T(8,128)(2,1)S(1)} collective-permute-done((bf16[512,256]{1,0:T(8,128)(2,1)S(1)}, bf16[512,256]{1,0:T(8,128)(2,1)S(1)}, u32[]{:S(2)}, u32[]{:S(2)}) %collective-permute-start.19) | collective-permute-done | bytes 262176 | tf_op jit(solution)/shard_map/ppermute | solution.py:317
  182.0 1.0 maximum_select_fusion.2
  (59 shorter events, 0.3 us)
Async XLA Ops:
  0.6 5.8 %copy-start.12 = (s32[1024]{0:T(1024)S(1)}, s32[1024]{0:T(1024)}, u32[]{:S(2)}) copy-start(s32[1024]{0:T(1024)} %param.20) | copy-start | bytes 12292
  0.6 5.8 %copy-start.13 = (s32[1024]{0:T(1024)S(1)}, s32[1024]{0:T(1024)}, u32[]{:S(2)}) copy-start(s32[1024]{0:T(1024)} %param.22) | copy-start | bytes 12292
  0.7 5.8 %copy-start.11 = (s32[1024,8]{0,1:T(8,128)S(1)}, s32[1024,8]{0,1:T(8,128)}, u32[]{:S(2)}) copy-start(s32[1024,8]{0,1:T(8,128)} %param.19) | copy-start | bytes 98308
  0.7 6.6 %copy-start = (bf16[1,1024,256]{2,1,0:T(8,128)(2,1)S(1)}, bf16[1,1024,256]{2,1,0:T(8,128)(2,1)}, u32[]{:S(2)}) copy-start(bf16[1,1024,256]{2,1,0:T(8,128)(2,1)} %param.17) | copy-start | bytes 1572868
  1.8 4.7 %copy-start.10 = (s32[1024,8]{0,1:T(8,128)S(1)}, s32[1024,8]{0,1:T(8,128)}, u32[]{:S(2)}) copy-start(s32[1024,8]{0,1:T(8,128)} %param.21) | copy-start | bytes 98308
  1.8 8.6 %collective-permute-start = (bf16[512,256]{1,0:T(8,128)(2,1)S(1)}, bf16[512,256]{1,0:T(8,128)(2,1)S(1)}, u32[]{:S(2)}, u32[]{:S(2)}) collective-permute-start(bf16[512,256]{1,0:T(8,128)(2,1)S(1)} %get-tuple-element.43), channel_id=1, source_target_pairs={{0,0},{1,2},{2,1},{3,3},{4,4},{5,6},{6,5},{7,7},{8,8},{9,10},{10,9... | collective-permute-start | bytes 786440 | tf_op jit(solution)/shard_map/ppermute | solution.py:311
  6.3 6.1 %collective-permute-start.1 = (bf16[512,256]{1,0:T(8,128)(2,1)S(1)}, bf16[512,256]{1,0:T(8,128)(2,1)S(1)}, u32[]{:S(2)}, u32[]{:S(2)}) collective-permute-start(bf16[512,256]{1,0:T(8,128)(2,1)S(1)} %get-tuple-element.44), channel_id=1, source_target_pairs={{0,1},{1,3},{2,0},{3,2},{4,5},{5,7},{6,4},{7,6},{8,9},{9,11},{10,8... | collective-permute-start | bytes 786440 | tf_op jit(solution)/shard_map/ppermute | solution.py:312
  6.5 0.7 copy-start.16
  6.6 0.7 copy-start.15
  6.6 0.7 copy-start.14
  62.0 22.3 %copy-start.1 = (bf16[1,1024,256]{2,1,0:T(8,128)(2,1)S(1)}, bf16[1,1024,256]{2,1,0:T(8,128)(2,1)}, u32[]{:S(2)}) copy-start(bf16[1,1024,256]{2,1,0:T(8,128)(2,1)} %param.18) | copy-start | bytes 1572868
  62.1 11.1 %collective-permute-start.9 = (bf16[784,256]{1,0:T(8,128)(2,1)}, bf16[784,256]{1,0:T(8,128)(2,1)S(1)}, u32[]{:S(2)}, u32[]{:S(2)}) collective-permute-start(bf16[784,256]{1,0:T(8,128)(2,1)} %get-tuple-element.61), channel_id=1, source_target_pairs={{0,2},{2,0},{1,3},{3,1},{4,6},{6,4},{5,7},{7,5},{8,10},{10,8},{9,1... | collective-permute-start | bytes 1204232 | tf_op jit(solution)/shard_map/ppermute | solution.py:327
  64.2 12.3 %collective-permute-start.2 = (bf16[512,512]{1,0:T(8,128)(2,1)S(1)}, bf16[512,512]{1,0:T(8,128)(2,1)S(1)}, u32[]{:S(2)}, u32[]{:S(2)}) collective-permute-start(bf16[512,512]{1,0:T(8,128)(2,1)S(1)} %maximum_select_fusion.own_hbm), channel_id=1, source_target_pairs={{0,1},{1,0},{2,3},{3,2},{4,5},{5,4},{6,7},{7,6},{8,9},{9,8},{10,11... | collective-permute-start | bytes 1572872 | tf_op jit(solution)/shard_map/ppermute | solution.py:327
  64.2 30.2 %collective-permute-start.8 = (bf16[512,512]{1,0:T(8,128)(2,1)S(1)}, bf16[512,512]{1,0:T(8,128)(2,1)S(1)}, u32[]{:S(2)}, u32[]{:S(2)}) collective-permute-start(bf16[512,512]{1,0:T(8,128)(2,1)S(1)} %maximum_select_fusion.own_hbm), channel_id=1, source_target_pairs={{1,4},{0,13},{5,8},{4,1},{9,12},{8,5},{13,0},{12,9},{3,6},{2,15},{... | collective-permute-start | bytes 1572872 | tf_op jit(solution)/shard_map/ppermute | solution.py:338
  65.9 17.0 %collective-permute-start.3 = (bf16[272,256]{1,0:T(8,128)(2,1)S(1)}, bf16[272,256]{1,0:T(8,128)(2,1)S(1)}, u32[]{:S(2)}, u32[]{:S(2)}) collective-permute-start(bf16[272,256]{1,0:T(8,128)(2,1)S(1)} %get-tuple-element.54), channel_id=1, source_target_pairs={{0,4},{4,8},{8,12},{12,0},{1,5},{5,9},{9,13},{13,1},{2,6},{6,10},{... | collective-permute-start | bytes 417800 | tf_op jit(solution)/shard_map/ppermute | solution.py:411
  67.2 15.7 %collective-permute-start.4 = (bf16[272,256]{1,0:T(8,128)(2,1)S(1)}, bf16[272,256]{1,0:T(8,128)(2,1)S(1)}, u32[]{:S(2)}, u32[]{:S(2)}) collective-permute-start(bf16[272,256]{1,0:T(8,128)(2,1)S(1)} %get-tuple-element.55), channel_id=1, source_target_pairs={{0,8},{4,12},{8,0},{12,4},{1,9},{5,13},{9,1},{13,5},{2,10},{6,14},... | collective-permute-start | bytes 417800 | tf_op jit(solution)/shard_map/ppermute | solution.py:411
  73.2 11.1 %collective-permute-start.5 = (bf16[272,256]{1,0:T(8,128)(2,1)S(1)}, bf16[272,256]{1,0:T(8,128)(2,1)S(1)}, u32[]{:S(2)}, u32[]{:S(2)}) collective-permute-start(bf16[272,256]{1,0:T(8,128)(2,1)S(1)} %get-tuple-element.56), channel_id=1, source_target_pairs={{0,12},{4,0},{8,4},{12,8},{1,13},{5,1},{9,5},{13,9},{2,14},{6,2},{... | collective-permute-start | bytes 417800 | tf_op jit(solution)/shard_map/ppermute | solution.py:411
  76.5 30.3 %collective-permute-start.10 = (bf16[784,256]{1,0:T(8,128)(2,1)S(1)}, bf16[784,256]{1,0:T(8,128)(2,1)S(1)}, u32[]{:S(2)}, u32[]{:S(2)}) collective-permute-start(bf16[784,256]{1,0:T(8,128)(2,1)S(1)} %collective-permute-done.9.near_hbm), channel_id=1, source_target_pairs={{0,1},{1,0},{2,3},{3,2},{4,5},{5,4},{6,7},{7,6},{8,9},{9,8},{10,11... | collective-permute-start | bytes 1204232 | tf_op jit(solution)/shard_map/ppermute | solution.py:327
  84.3 21.6 %copy-start.18 = (bf16[784,256]{1,0:T(8,128)(2,1)S(1)}, bf16[784,256]{1,0:T(8,128)(2,1)}, u32[]{:S(2)}) copy-start(bf16[784,256]{1,0:T(8,128)(2,1)} %get-tuple-element.68) | copy-start | bytes 1204228
  84.3 22.5 %copy-start.4 = (bf16[2,256,512]{2,1,0:T(8,128)(2,1)S(1)}, bf16[2,256,512]{2,1,0:T(8,128)(2,1)}, u32[]{:S(2)}) copy-start(bf16[2,256,512]{2,1,0:T(8,128)(2,1)} %w2_hbm.6) | copy-start | bytes 1572868
  84.3 22.5 %copy-start.8 = (bf16[2,256]{1,0:T(2,128)(2,1)S(1)}, bf16[2,256]{1,0:T(2,128)(2,1)}, u32[]{:S(2)}) copy-start(bf16[2,256]{1,0:T(2,128)(2,1)} %b_hbm.6) | copy-start | bytes 3076
  85.0 13.4 %collective-permute-start.6 = (bf16[512,256]{1,0:T(8,128)(2,1)S(1)}, bf16[512,256]{1,0:T(8,128)(2,1)S(1)}, u32[]{:S(2)}, u32[]{:S(2)}) collective-permute-start(bf16[512,256]{1,0:T(8,128)(2,1)S(1)} %get-tuple-element.57), channel_id=1, source_target_pairs={{0,0},{1,2},{2,1},{3,3},{4,4},{5,6},{6,5},{7,7},{8,8},{9,10},{10,9... | collective-permute-start | bytes 786440 | tf_op jit(solution)/shard_map/ppermute | solution.py:311
  94.4 6.1 %collective-permute-start.7 = (bf16[512,256]{1,0:T(8,128)(2,1)S(1)}, bf16[512,256]{1,0:T(8,128)(2,1)S(1)}, u32[]{:S(2)}, u32[]{:S(2)}) collective-permute-start(bf16[512,256]{1,0:T(8,128)(2,1)S(1)} %get-tuple-element.58), channel_id=1, source_target_pairs={{0,1},{1,3},{2,0},{3,2},{4,5},{5,7},{6,4},{7,6},{8,9},{9,11},{10,8... | collective-permute-start | bytes 786440 | tf_op jit(solution)/shard_map/ppermute | solution.py:312
  100.5 6.3 %copy-start.2 = (bf16[2,512,256]{2,1,0:T(8,128)(2,1)S(1)}, bf16[2,512,256]{2,1,0:T(8,128)(2,1)}, u32[]{:S(2)}) copy-start(bf16[2,512,256]{2,1,0:T(8,128)(2,1)} %ws_hbm.6) | copy-start | bytes 1572868
  100.5 6.3 %copy-start.3 = (bf16[2,512,256]{2,1,0:T(8,128)(2,1)S(1)}, bf16[2,512,256]{2,1,0:T(8,128)(2,1)}, u32[]{:S(2)}) copy-start(bf16[2,512,256]{2,1,0:T(8,128)(2,1)} %wd_hbm.6) | copy-start | bytes 1572868
  100.7 14.0 %copy-start.17 = (bf16[1568,256]{1,0:T(8,128)(2,1)S(1)}, bf16[1568,256]{1,0:T(8,128)(2,1)}, u32[]{:S(2)}) copy-start(bf16[1568,256]{1,0:T(8,128)(2,1)} %get-tuple-element.74) | copy-start | bytes 2408452
  100.7 15.7 %copy-start.5 = (bf16[2,512,256]{2,1,0:T(8,128)(2,1)S(1)}, bf16[2,512,256]{2,1,0:T(8,128)(2,1)}, u32[]{:S(2)}) copy-start(bf16[2,512,256]{2,1,0:T(8,128)(2,1)} %ws_hbm.7) | copy-start | bytes 1572868
  100.7 15.7 %copy-start.6 = (bf16[2,512,256]{2,1,0:T(8,128)(2,1)S(1)}, bf16[2,512,256]{2,1,0:T(8,128)(2,1)}, u32[]{:S(2)}) copy-start(bf16[2,512,256]{2,1,0:T(8,128)(2,1)} %wd_hbm.7) | copy-start | bytes 1572868
  100.7 15.7 %copy-start.7 = (bf16[2,256,512]{2,1,0:T(8,128)(2,1)S(1)}, bf16[2,256,512]{2,1,0:T(8,128)(2,1)}, u32[]{:S(2)}) copy-start(bf16[2,256,512]{2,1,0:T(8,128)(2,1)} %w2_hbm.7) | copy-start | bytes 1572868
  100.7 14.7 %collective-permute-start.11 = (bf16[512,512]{1,0:T(8,128)(2,1)S(1)}, bf16[512,512]{1,0:T(8,128)(2,1)S(1)}, u32[]{:S(2)}, u32[]{:S(2)}) collective-permute-start(bf16[512,512]{1,0:T(8,128)(2,1)S(1)} %maximum_select_fusion.1.own_hbm), channel_id=1, source_target_pairs={{0,1},{1,0},{2,3},{3,2},{4,5},{5,4},{6,7},{7,6},{8,9},{9,8},{10,11... | collective-permute-start | bytes 1572872 | tf_op jit(solution)/shard_map/ppermute | solution.py:327
  102.2 13.2 %collective-permute-start.12 = (bf16[512,512]{1,0:T(8,128)(2,1)S(1)}, bf16[512,512]{1,0:T(8,128)(2,1)S(1)}, u32[]{:S(2)}, u32[]{:S(2)}) collective-permute-start(bf16[512,512]{1,0:T(8,128)(2,1)S(1)} %maximum_select_fusion.1.own_hbm), channel_id=1, source_target_pairs={{1,4},{5,8},{4,1},{9,12},{8,5},{12,9},{3,6},{7,10},{6,3},{11,14},{... | collective-permute-start | bytes 1572872 | tf_op jit(solution)/shard_map/ppermute | solution.py:338
  105.9 8.7 %collective-permute-start.13 = (bf16[784,256]{1,0:T(8,128)(2,1)S(1)}, bf16[784,256]{1,0:T(8,128)(2,1)S(1)}, u32[]{:S(2)}, u32[]{:S(2)}) collective-permute-start(bf16[784,256]{1,0:T(8,128)(2,1)S(1)} %copy-done.18), channel_id=1, source_target_pairs={{0,2},{2,0},{1,3},{3,1},{4,6},{6,4},{5,7},{7,5},{8,10},{10,8},{9,1... | collective-permute-start | bytes 1204232 | tf_op jit(solution)/shard_map/ppermute | solution.py:327
  114.5 1.9 %copy-start.9 = (bf16[2,256]{1,0:T(2,128)(2,1)S(1)}, bf16[2,256]{1,0:T(2,128)(2,1)}, u32[]{:S(2)}) copy-start(bf16[2,256]{1,0:T(2,128)(2,1)} %b_hbm.7) | copy-start | bytes 3076
  114.6 1.7 collective-permute-start.14
  114.6 19.1 %collective-permute-start.17 = (bf16[1568,256]{1,0:T(8,128)(2,1)S(1)}, bf16[1568,256]{1,0:T(8,128)(2,1)S(1)}, u32[]{:S(2)}, u32[]{:S(2)}) collective-permute-start(bf16[1568,256]{1,0:T(8,128)(2,1)S(1)} %copy-done.17), channel_id=1, source_target_pairs={{0,2},{2,0},{1,3},{3,1},{4,6},{6,4},{5,7},{7,5},{8,10},{10,8},{9,1... | collective-permute-start | bytes 2408456 | tf_op jit(solution)/shard_map/ppermute | solution.py:327
  133.7 17.1 %collective-permute-start.18 = (bf16[1568,256]{1,0:T(8,128)(2,1)S(1)}, bf16[1568,256]{1,0:T(8,128)(2,1)S(1)}, u32[]{:S(2)}, u32[]{:S(2)}) collective-permute-start(bf16[1568,256]{1,0:T(8,128)(2,1)S(1)} %collective-permute-done.17.near_hbm), channel_id=1, source_target_pairs={{0,1},{1,0},{2,3},{3,2},{4,5},{5,4},{6,7},{7,6},{8,9},{9,8},{10,11... | collective-permute-start | bytes 2408456 | tf_op jit(solution)/shard_map/ppermute | solution.py:327
  135.0 7.9 %collective-permute-start.15 = (bf16[512,512]{1,0:T(8,128)(2,1)S(1)}, bf16[512,512]{1,0:T(8,128)(2,1)S(1)}, u32[]{:S(2)}, u32[]{:S(2)}) collective-permute-start(bf16[512,512]{1,0:T(8,128)(2,1)S(1)} %graph_layer.4.own_hbm), channel_id=1, source_target_pairs={{0,1},{1,0},{2,3},{3,2},{4,5},{5,4},{6,7},{7,6},{8,9},{9,8},{10,11... | collective-permute-start | bytes 1572872 | tf_op jit(solution)/shard_map/ppermute | solution.py:327
  135.0 15.8 %collective-permute-start.16 = (bf16[512,512]{1,0:T(8,128)(2,1)S(1)}, bf16[512,512]{1,0:T(8,128)(2,1)S(1)}, u32[]{:S(2)}, u32[]{:S(2)}) collective-permute-start(bf16[512,512]{1,0:T(8,128)(2,1)S(1)} %graph_layer.4.own_hbm), channel_id=1, source_target_pairs={{1,4},{0,13},{5,8},{4,1},{9,12},{8,5},{13,0},{12,9},{3,6},{2,15},{... | collective-permute-start | bytes 1572872 | tf_op jit(solution)/shard_map/ppermute | solution.py:338
  138.4 20.2 %collective-permute-start.21 = (bf16[512,512]{1,0:T(8,128)(2,1)S(1)}, bf16[512,512]{1,0:T(8,128)(2,1)S(1)}, u32[]{:S(2)}, u32[]{:S(2)}) collective-permute-start(bf16[512,512]{1,0:T(8,128)(2,1)S(1)} %graph_layer.5.own_hbm), channel_id=1, source_target_pairs={{0,1},{1,0},{2,3},{3,2},{4,5},{5,4},{6,7},{7,6},{8,9},{9,8},{10,11... | collective-permute-start | bytes 1572872 | tf_op jit(solution)/shard_map/ppermute | solution.py:327
  138.8 19.8 %collective-permute-start.22 = (bf16[512,512]{1,0:T(8,128)(2,1)S(1)}, bf16[512,512]{1,0:T(8,128)(2,1)S(1)}, u32[]{:S(2)}, u32[]{:S(2)}) collective-permute-start(bf16[512,512]{1,0:T(8,128)(2,1)S(1)} %graph_layer.5.own_hbm), channel_id=1, source_target_pairs={{1,4},{5,8},{4,1},{9,12},{8,5},{12,9},{3,6},{7,10},{6,3},{11,14},{... | collective-permute-start | bytes 1572872 | tf_op jit(solution)/shard_map/ppermute | solution.py:338
  166.3 10.4 %collective-permute-start.23 = (bf16[512,256]{1,0:T(8,128)(2,1)S(1)}, bf16[512,256]{1,0:T(8,128)(2,1)S(1)}, u32[]{:S(2)}, u32[]{:S(2)}) collective-permute-start(bf16[512,256]{1,0:T(8,128)(2,1)S(1)} %get-tuple-element.82), channel_id=1, source_target_pairs={{0,0},{1,2},{2,1},{3,3},{4,4},{5,6},{6,5},{7,7},{8,8},{9,10},{10,9... | collective-permute-start | bytes 786440 | tf_op jit(solution)/shard_map/ppermute | solution.py:317
  168.3 8.4 %collective-permute-start.24 = (bf16[512,256]{1,0:T(8,128)(2,1)S(1)}, bf16[512,256]{1,0:T(8,128)(2,1)S(1)}, u32[]{:S(2)}, u32[]{:S(2)}) collective-permute-start(bf16[512,256]{1,0:T(8,128)(2,1)S(1)} %get-tuple-element.83), channel_id=1, source_target_pairs={{0,2},{1,0},{2,3},{3,1},{4,6},{5,4},{6,7},{7,5},{8,10},{9,8},{10,1... | collective-permute-start | bytes 786440 | tf_op jit(solution)/shard_map/ppermute | solution.py:318
  168.3 13.6 %collective-permute-start.19 = (bf16[512,256]{1,0:T(8,128)(2,1)S(1)}, bf16[512,256]{1,0:T(8,128)(2,1)S(1)}, u32[]{:S(2)}, u32[]{:S(2)}) collective-permute-start(bf16[512,256]{1,0:T(8,128)(2,1)S(1)} %get-tuple-element.78), channel_id=1, source_target_pairs={{0,0},{1,2},{2,1},{3,3},{4,4},{5,6},{6,5},{7,7},{8,8},{9,10},{10,9... | collective-permute-start | bytes 786440 | tf_op jit(solution)/shard_map/ppermute | solution.py:317
  171.9 10.1 %collective-permute-start.20 = (bf16[512,256]{1,0:T(8,128)(2,1)S(1)}, bf16[512,256]{1,0:T(8,128)(2,1)S(1)}, u32[]{:S(2)}, u32[]{:S(2)}) collective-permute-start(bf16[512,256]{1,0:T(8,128)(2,1)S(1)} %get-tuple-element.79), channel_id=1, source_target_pairs={{0,2},{1,0},{2,3},{3,1},{4,6},{5,4},{6,7},{7,5},{8,10},{9,8},{10,1... | collective-permute-start | bytes 786440 | tf_op jit(solution)/shard_map/ppermute | solution.py:318

commit v3 on v1

--- a/solution.py
+++ b/solution.py
@@ -9,6 +9,7 @@
 
 LANES = 128
 DEAD = -1e30
+SMALL = pl.CostEstimate(flops=1, bytes_accessed=1, transcendentals=0)
 
 
 def padded_2(shard, sides, width, wrap):
@@ -117,9 +118,7 @@
         in_specs=[pl.BlockSpec(memory_space=pltpu.SMEM), vmem, vmem],
         out_specs=(vmem,) * parts,
         compiler_params=pltpu.CompilerParams(vmem_limit_bytes=32 << 20),
-        cost_estimate=pl.CostEstimate(
-            flops=2 * parts * cap * rows * (total + feats), bytes_accessed=4 * rows * feats, transcendentals=0
-        ),
+        cost_estimate=SMALL,
         name="pick_rows",
     )(me, bnd, nodes)
 
@@ -149,9 +148,7 @@
         in_specs=[pl.BlockSpec(memory_space=pltpu.SMEM)] + [vmem] * (1 + len(pieces)),
         out_specs=(vmem, vmem),
         compiler_params=pltpu.CompilerParams(vmem_limit_bytes=32 << 20),
-        cost_estimate=pl.CostEstimate(
-            flops=2 * len(pieces) * cap * rows * feats, bytes_accessed=6 * rows * feats, transcendentals=0
-        ),
+        cost_estimate=SMALL,
         name="add_force",
     )(first, nodes, *pieces)
 
@@ -218,8 +215,8 @@
         mine = near[spot, :]
         total = None
         for j in range(slots):
-            upper = proj[pl.ds(pl.multiple_of(idx_ref[2 * q * slots + j], 4), 8), :]
-            lower = proj[pl.ds(pl.multiple_of(idx_ref[(2 * q + 1) * slots + j], 4), 8), :]
+            upper = proj[pl.ds(pl.multiple_of(idx_ref[j * rows + 2 * q], 4), 8), :]
+            lower = proj[pl.ds(pl.multiple_of(idx_ref[j * rows + 2 * q + 1], 4), 8), :]
             y = jnp.where(low, upper, lower) + mine
             act = y * jnp.tanh(y) + y
             total = act if total is None else total + act
@@ -269,7 +266,7 @@
     return pl.pallas_call(
         functools.partial(layer_kernel, layer, slots, last),
         out_shape=out_shape,
-        in_specs=[smem, smem] + [anywhere] * 9,
+        in_specs=[smem, smem] + [anywhere] * 3 + [pl.BlockSpec(memory_space=pltpu.HBM)] * 3 + [anywhere] * 3,
         out_specs=out_specs,
         scratch_shapes=[
             pltpu.VMEM((rows, width), bf16),
@@ -290,25 +287,23 @@
             pltpu.SemaphoreType.DMA((9,)),
         ],
         compiler_params=pltpu.CompilerParams(vmem_limit_bytes=32 << 20),
-        cost_estimate=pl.CostEstimate(
-            flops=2 * 5 * rows * width * width, bytes_accessed=10 * rows * width, transcendentals=edges * width
-        ),
+        cost_estimate=pl.CostEstimate(flops=64 * rows * width * width, bytes_accessed=10 * rows * width, transcendentals=0),
         name="graph_layer",
     )(core, idx, own, sib, rim, ws, wd, w2, bias, near_w, far_w)
 
 
-def edge_offsets(nbr, count, core):
-    rows, slots = nbr.shape
+def edge_offsets(nbrs, counts, core):
+    graphs, rows, slots = nbrs.shape
     half = rows // 2
-    nbr = lax.dynamic_slice(nbr, (core * half, 0), (half, slots)) - core * half
-    count = lax.dynamic_slice(count, (core * half,), (half,))
+    nbr = lax.dynamic_slice(nbrs.transpose(0, 2, 1), (0, 0, core * half), (graphs, slots, half)) - core * half
+    count = lax.dynamic_slice(counts, (0, core * half), (graphs, half))
     low = nbr + jnp.where(core == 0, 2 * half, half)
     high = nbr - jnp.where(core == 0, half, 0)
     place = jnp.where(nbr < half, low, jnp.where(nbr < 2 * half, nbr - half, high))
-    live = jnp.arange(slots, dtype=jnp.int32)[None, :] < count[:, None]
+    live = jnp.arange(slots, dtype=jnp.int32)[None, :, None] < count[:, None, :]
     place = jnp.where(live, place, 3 * half)
-    odd = jnp.arange(half, dtype=jnp.int32)[:, None] % 2
-    return (4 * (place + 1 - odd)).reshape(half * slots)
+    odd = jnp.arange(half, dtype=jnp.int32) % 2
+    return (4 * (place + 1 - odd)).reshape(graphs, slots * half)
 
 
 def spread_rows(same, other):
@@ -342,16 +337,31 @@
     return lax.ppermute(own, ("mesh", "batch"), pairs)
 
 
-def other_weights(layer, core, ws, wd, w2, bias):
-    share = ws.shape[2]
-    picked = [
-        lax.dynamic_slice(ws, (layer, core * share, 0), (1, share, share))[0],
-        lax.dynamic_slice(wd, (layer, core * share, 0), (1, share, share))[0],
-        lax.dynamic_slice(w2, (layer, 0, core * share), (1, share, share))[0],
-        jnp.broadcast_to(bias[layer][None], (16, share)),
-    ]
-    near_w = swap(jnp.concatenate(picked, 0), "mp")
-    return near_w, swap(near_w, "batch")
+def pack_kernel(order, core_ref, g_bias, r_bias, *refs):
+    weights, outs = (refs[:3], refs[3:6]), refs[6:]
+    share = g_bias.shape[1]
+    here = pl.multiple_of(core_ref[0] * share, share)
+    for (graph, layer), out in zip(order, outs):
+        ws, wd, w2 = weights[graph]
+        bias = (g_bias, r_bias)[graph][layer:layer + 1, :]
+        out[0:share, :] = ws[layer, pl.ds(here, share), :]
+        out[share:2 * share, :] = wd[layer, pl.ds(here, share), :]
+        out[2 * share:3 * share, :] = w2[layer, :, pl.ds(here, share)]
+        out[3 * share:, :] = jnp.broadcast_to(bias, (16, share))
+
+
+def pack_weights(order, core, g_weights, g_bias, r_weights, r_bias):
+    share = g_bias.shape[1]
+    vmem = pl.BlockSpec(memory_space=pltpu.VMEM)
+    return pl.pallas_call(
+        functools.partial(pack_kernel, order),
+        out_shape=(jax.ShapeDtypeStruct((3 * share + 16, share), jnp.bfloat16),) * len(order),
+        in_specs=[pl.BlockSpec(memory_space=pltpu.SMEM)] + [vmem] * 8,
+        out_specs=(vmem,) * len(order),
+        compiler_params=pltpu.CompilerParams(vmem_limit_bytes=32 << 20),
+        cost_estimate=SMALL,
+        name="pack_weights",
+    )(core, g_bias, r_bias, *g_weights, *r_weights)
 
 
 def by_rows(
@@ -369,33 +379,59 @@
     me = lax.axis_index("mesh").reshape(1)
     core1 = core.reshape(1)
     g_own, r_own = g_nodes[0], r_nodes[0]
+    g_weights, r_weights = (g_ws, g_wd, g_w2), (r_ws, r_wd, r_w2)
+    after = lax.optimization_barrier
 
     same = lax.dynamic_slice(g_own, (part * half, 0), (half, g_own.shape[1]))
     other = lax.dynamic_slice(g_own, ((1 - part) * half, 0), (half, g_own.shape[1]))
+    same, other, bnd_src = after((same, other, bnd_src))
     g_a, g_b = spread_rows(same, other)
     bnd = jnp.stack([bnd_src, bnd_part[:, 0], bnd_node])
     pieces = pick_rows(me, bnd, g_own, parts, cap)
     landed = [pieces[0]]
     for k in range(1, parts):
         landed.append(lax.ppermute(pieces[k], "mesh", [(i, (i + k) % parts) for i in range(parts)]))
-    g_idx = edge_offsets(g_nbr, g_count, core)
-    r_idx = edge_offsets(r_nbr, r_count, core)
-    r_a, r_b = spread_rows(*add_force(part.reshape(1), r_own, landed, cap))
-
+    idx = edge_offsets(jnp.stack([g_nbr, r_nbr]), jnp.stack([g_count, r_count]), core)
+
+    order = [(graph, layer) for layer in range(layers) for graph in (0, 1)]
+    packs = pack_weights(order, core1, g_weights, g_b1, r_weights, r_b1)
+    g_a, g_b, g_idx, r_idx, core1, landed[0], sent = after((g_a, g_b, idx[0], idx[1], core1, landed[0], packs[0]))
+    near_w = [swap(sent, "mp")]
     planet = ordered(core, g_a, g_b, 1)
-    regional = ordered(core, r_a, r_b, 1)
+    g_sib, g_rim = swap(planet, "batch"), rims(planet, True)
+    g_sib, r_own = after((g_sib, r_own))
+    r_pair = add_force(part.reshape(1), r_own, landed, cap)
+    *r_pair, g_idx, near_w[0] = after((*r_pair, g_idx, near_w[0]))
+    r_a, r_b = spread_rows(*r_pair)
+    regional, g_idx = after((ordered(core, r_a, r_b, 1), g_idx))
+    r_sib, r_rim = swap(regional, "batch"), rims(regional, False)
+    far_w = []
     for layer in range(layers):
         last = layer == layers - 1
-        g_w = other_weights(layer, core, g_ws, g_wd, g_w2, g_b1)
-        planet = run_layer(
-            layer, slots, last, core1, g_idx, planet, swap(planet, "batch"), rims(planet, True),
-            g_ws, g_wd, g_w2, g_b1, *g_w,
-        )
-        r_w = other_weights(layer, core, r_ws, r_wd, r_w2, r_b1)
-        regional = run_layer(
-            layer, slots, last, core1, r_idx, regional, swap(regional, "batch"), rims(regional, False),
-            r_ws, r_wd, r_w2, r_b1, *r_w,
-        )
+        for graph in (0, 1):
+            i = 2 * layer + graph
+            far_w.append(swap(near_w[i], "batch"))
+            if i + 1 < len(order):
+                sent, near_w[i] = after((packs[i + 1], near_w[i]))
+                near_w.append(swap(sent, "mp"))
+            if graph == 0:
+                planet = run_layer(
+                    layer, slots, last, core1, g_idx, planet, g_sib, g_rim,
+                    g_ws, g_wd, g_w2, g_b1, near_w[i], far_w[i],
+                )
+                *planet, core1, near_w[i + 1] = after((*(planet if last else (planet,)), core1, near_w[i + 1]))
+                if not last:
+                    planet = planet[0]
+                    g_sib, g_rim = swap(planet, "batch"), rims(planet, True)
+                if layer:
+                    r_sib, r_rim = swap(regional, "batch"), rims(regional, False)
+            else:
+                regional = run_layer(
+                    layer, slots, last, core1, r_idx, regional, r_sib, r_rim,
+                    r_ws, r_wd, r_w2, r_b1, near_w[i], far_w[i],
+                )
+                if not last:
+                    regional, core1, near_w[i + 1] = after((regional, core1, near_w[i + 1]))
     g_out = ordered(part, *gather_rows(*planet), 0)
     r_out = ordered(part, *gather_rows(*regional), 0)
     return g_out[None], r_out[None]

time: 128 us -> 111 us (0.87)
  local copies, waits for them, and re-layouts: 15.4 us -> 6.06 us
  other arithmetic: 8.43 us -> 3.12 us
  Pallas kernels: 36.1 us -> 33.7 us
  starting transfers between devices: 38.6 us -> 40 us
    ppermute x3, waiting for transfers between devices: 0.01 us -> 7.94 us  [by_rows(): lax.ppermute(pieces[k], 'mesh', [(i, (i + k) % parts) for i in range(part...]
    ppermute x2, waiting for transfers between devices: 8.91 us -> 3.99 us  [spread_rows(): b = lax.ppermute(other, ('mp', 'batch'), [(0, 1), (1, 3), (2, 0), (3, 2)])]
    unnamed x58 -> x41, local copies, waits for them, and re-layouts: 9.15 us -> 4.9 us
    ppermute x12, starting transfers between devices: 4.94 us -> 8.03 us  [swap(): return lax.ppermute(values, axis, [(0, 1), (1, 0)])]
    ppermute x2, waiting for transfers between devices: 8.68 us -> 5.86 us  [spread_rows(): a = lax.ppermute(same, ('mp', 'batch'), [(0, 0), (1, 2), (2, 1), (3, 3)])]
    ppermute x4, waiting for transfers between devices: 2.63 us -> 0.01 us  [rims(): return lax.ppermute(own, ('mesh', 'batch'), pairs)]
    pallas_call x4, Pallas kernels: 33.2 us -> 30.7 us  [run_layer(): pl.pallas_call(functools.partial(layer_kernel, layer, slots, last), out_s...]
    select_n x4, other arithmetic: 4.69 us -> 2.29 us  [ordered(): jnp.where(which == 0, jnp.concatenate([a, b], axis), jnp.concatenate([b,...]
  transfers between devices with their start and end apart: 27 -> 27, of which waited for: 5 -> 8; matrix products, arithmetic and copies ran while one was open for 11% -> 2% of each run, Pallas kernels for 27% -> 31%
where the time goes in v3:
time: 111 us; the launch traced here: 110 us
  starting transfers between devices  40 us (36%)
  Pallas kernels  33.7 us (30%)
  waiting for transfers between devices  26 us (23%)
  local copies, waits for them, and re-layouts  6.06 us (5%)
  other arithmetic  3.12 us (3%)
  between operations  1.16 us (1%)
    pallas_call x4, Pallas kernels, run_layer(): pl.pallas_call(functools.partial(layer_kernel, layer, slots, last), out_s...  30.7 us
    ppermute x4, starting transfers between devices, rims(): return lax.ppermute(own, ('mesh', 'batch'), pairs)  13.8 us
    ppermute x12, starting transfers between devices, swap(): return lax.ppermute(values, axis, [(0, 1), (1, 0)])  8.03 us
    ppermute x3, waiting for transfers between devices, by_rows(): lax.ppermute(pieces[k], 'mesh', [(i, (i + k) % parts) for i in range(part...  7.94 us
    ppermute x2, starting transfers between devices, spread_rows(): a = lax.ppermute(same, ('mp', 'batch'), [(0, 0), (1, 2), (2, 1), (3, 3)])  7.84 us
    ppermute x2, waiting for transfers between devices, gather_rows(): same = lax.ppermute(a, ('mp', 'batch'), [(0, 0), (1, 2), (2, 1), (3, 3)])  6.97 us
    ppermute x2, waiting for transfers between devices, spread_rows(): a = lax.ppermute(same, ('mp', 'batch'), [(0, 0), (1, 2), (2, 1), (3, 3)])  5.86 us
    ppermute x2, starting transfers between devices, gather_rows(): same = lax.ppermute(a, ('mp', 'batch'), [(0, 0), (1, 2), (2, 1), (3, 3)])  5.55 us
  transfers between devices with their start and end apart: 27, of which 8 were waited for; matrix products, arithmetic and copies ran while one was open for 2% of the time, Pallas kernels for 31%

profile of v3, /device:TPU:1, one launch (start us, length us, event | category | flops | bytes accessed | tf_op | source)
XLA Modules:
  0.0 110.0 jit_solution(8940643214802414365)
XLA Ops:
  0.7 1.2 %dynamic-slice_bitcast_fusion = (bf16[512,256]{1,0:T(8,128)(2,1)S(1)}, bf16[512,256]{1,0:T(8,128)(2,1)S(1)}) fusion(bf16[1,1024,256]{2,1,0:T(8,128)(2,1)} %param.17, s32[]{:T(128)S(6)} %select_n.83, s32[]{:T(128)S(6)} %select_n.82), kind=kLoop, calls=%fused_computation.4 | loop fusion | bytes 1048584 | tf_op jit(solution)/shard_map/dynamic_slice | solution.py:386
  1.9 4.6 %collective-permute-start = (bf16[512,256]{1,0:T(8,128)(2,1)S(1)}, bf16[512,256]{1,0:T(8,128)(2,1)S(1)}, u32[]{:S(2)}, u32[]{:S(2)}) collective-permute-start(bf16[512,256]{1,0:T(8,128)(2,1)S(1)} %get-tuple-element.50), channel_id=1, source_target_pairs={{0,0},{1,2},{2,1},{3,3},{4,4},{5,6},{6,5},{7,7},{8,8},{9,10},{10,9... | collective-permute-start | bytes 786440 | tf_op jit(solution)/shard_map/ppermute | solution.py:310
  6.5 0.0 collective-permute-start.1
  6.6 0.8 fusion.5
  7.5 2.2 %pick_rows.1 = (bf16[272,256]{1,0:T(8,128)(2,1)S(1)}, bf16[272,256]{1,0:T(8,128)(2,1)S(1)}, bf16[272,256]{1,0:T(8,128)(2,1)S(1)}, bf16[272,256]{1,0:T(8,128)(2,1)S(1)}) custom-call(s32[1]{0:T(128)} %bitcast.8.me_ref, s32[3,512]{1,0:T(4,128)S(1)} %pad_add_fusion.bnd_ref, bf16[1024,256]{1,0:T(8,128)(2,1)S(1)} %bitcast.34), custom_call_target="tpu_custom_call" | custom-call | flops 1 | bytes 1 | tf_op jit(solution)/shard_map/pick_rows/pallas_call | solution.py:115
  9.8 0.6 copy-done.12
  10.4 1.0 copy-done.4
  11.4 1.0 copy-done.6
  12.5 1.0 copy-done.8
  13.5 1.0 copy-done.10
  14.6 0.1 pack_weights.1
  14.8 0.1 maximum_select_fusion.own_hbm
  14.9 0.5 collective-permute-start.2
  15.4 1.3 %collective-permute-start.3 = (bf16[272,256]{1,0:T(8,128)(2,1)S(1)}, bf16[272,256]{1,0:T(8,128)(2,1)S(1)}, u32[]{:S(2)}, u32[]{:S(2)}) collective-permute-start(bf16[272,256]{1,0:T(8,128)(2,1)S(1)} %get-tuple-element.60), channel_id=1, source_target_pairs={{0,4},{4,8},{8,12},{12,0},{1,5},{5,9},{9,13},{13,1},{2,6},{6,10},{... | collective-permute-start | bytes 417800 | tf_op jit(solution)/shard_map/ppermute | solution.py:393
  16.7 2.3 %collective-permute-start.4 = (bf16[272,256]{1,0:T(8,128)(2,1)S(1)}, bf16[272,256]{1,0:T(8,128)(2,1)S(1)}, u32[]{:S(2)}, u32[]{:S(2)}) collective-permute-start(bf16[272,256]{1,0:T(8,128)(2,1)S(1)} %get-tuple-element.61), channel_id=1, source_target_pairs={{0,8},{4,12},{8,0},{12,4},{1,9},{5,13},{9,1},{13,5},{2,10},{6,14},... | collective-permute-start | bytes 417800 | tf_op jit(solution)/shard_map/ppermute | solution.py:393
  19.0 1.1 collective-permute-start.5
  20.1 1.5 %collective-permute-start.9 = (bf16[512,512]{1,0:T(8,128)(2,1)S(1)}, bf16[512,512]{1,0:T(8,128)(2,1)S(1)}, u32[]{:S(2)}, u32[]{:S(2)}) collective-permute-start(bf16[512,512]{1,0:T(8,128)(2,1)S(1)} %maximum_select_fusion.own_hbm), channel_id=1, source_target_pairs={{1,4},{0,13},{5,8},{4,1},{9,12},{8,5},{13,0},{12,9},{3,6},{2,15},{... | collective-permute-start | bytes 1572872 | tf_op jit(solution)/shard_map/ppermute | solution.py:337
  21.6 0.6 collective-permute-done.3.refs_1_
  22.2 7.3 %collective-permute-done.4.refs_2_ = bf16[272,256]{1,0:T(8,128)(2,1)S(1)} collective-permute-done((bf16[272,256]{1,0:T(8,128)(2,1)S(1)}, bf16[272,256]{1,0:T(8,128)(2,1)S(1)}, u32[]{:S(2)}, u32[]{:S(2)}) %collective-permute-start.4) | collective-permute-done | bytes 139296 | tf_op jit(solution)/shard_map/ppermute | solution.py:393
  29.6 0.7 add_force.1
  30.3 0.9 collective-permute-start.10
  31.1 3.2 %collective-permute-start.7 = (bf16[512,256]{1,0:T(8,128)(2,1)S(1)}, bf16[512,256]{1,0:T(8,128)(2,1)S(1)}, u32[]{:S(2)}, u32[]{:S(2)}) collective-permute-start(bf16[512,256]{1,0:T(8,128)(2,1)S(1)} %get-tuple-element.67), channel_id=1, source_target_pairs={{0,0},{1,2},{2,1},{3,3},{4,4},{5,6},{6,5},{7,7},{8,8},{9,10},{10,9... | collective-permute-start | bytes 786440 | tf_op jit(solution)/shard_map/ppermute | solution.py:310
  34.4 0.0 collective-permute-start.8
  34.4 0.6 collective-permute-start.11
  34.9 5.9 %collective-permute-done.7 = bf16[512,256]{1,0:T(8,128)(2,1)S(1)} collective-permute-done((bf16[512,256]{1,0:T(8,128)(2,1)S(1)}, bf16[512,256]{1,0:T(8,128)(2,1)S(1)}, u32[]{:S(2)}, u32[]{:S(2)}) %collective-permute-start.7) | collective-permute-done | bytes 262176 | tf_op jit(solution)/shard_map/ppermute | solution.py:310
  40.8 4.0 %collective-permute-done.8 = bf16[512,256]{1,0:T(8,128)(2,1)S(1)} collective-permute-done((bf16[512,256]{1,0:T(8,128)(2,1)S(1)}, bf16[512,256]{1,0:T(8,128)(2,1)S(1)}, u32[]{:S(2)}, u32[]{:S(2)}) %collective-permute-start.8) | collective-permute-done | bytes 262176 | tf_op jit(solution)/shard_map/ppermute | solution.py:311
  44.8 0.1 maximum_select_fusion.1.own_hbm
  45.0 1.9 %collective-permute-start.12 = (bf16[512,512]{1,0:T(8,128)(2,1)S(1)}, bf16[512,512]{1,0:T(8,128)(2,1)S(1)}, u32[]{:S(2)}, u32[]{:S(2)}) collective-permute-start(bf16[512,512]{1,0:T(8,128)(2,1)S(1)} %maximum_select_fusion.1.own_hbm), channel_id=1, source_target_pairs={{0,1},{1,0},{2,3},{3,2},{4,5},{5,4},{6,7},{7,6},{8,9},{9,8},{10,11... | collective-permute-start | bytes 1572872 | tf_op jit(solution)/shard_map/ppermute | solution.py:326
  46.9 8.0 %collective-permute-start.13 = (bf16[512,512]{1,0:T(8,128)(2,1)S(1)}, bf16[512,512]{1,0:T(8,128)(2,1)S(1)}, u32[]{:S(2)}, u32[]{:S(2)}) collective-permute-start(bf16[512,512]{1,0:T(8,128)(2,1)S(1)} %maximum_select_fusion.1.own_hbm), channel_id=1, source_target_pairs={{1,4},{5,8},{4,1},{9,12},{8,5},{12,9},{3,6},{7,10},{6,3},{11,14},{... | collective-permute-start | bytes 1572872 | tf_op jit(solution)/shard_map/ppermute | solution.py:337
  54.9 7.7 %graph_layer.4.own_hbm = bf16[512,512]{1,0:T(8,128)(2,1)S(1)} custom-call(s32[1]{0:T(128)} %bitcast.7.core_ref, s32[4096]{0:T(1024)S(1)} %bitcast.38, bf16[512,512]{1,0:T(8,128)(2,1)S(1)} %maximum_select_fusion.own_hbm, bf16[512,512]{1,0:T(8,128)(2,1)S(1)} %collective-permute-done.2.sib_hbm, bf16[512,512]{1,0:T(8,128)(2,1)S(1)} %collective-permute-done.9.rim_hbm, ...), custom_call_target="tpu_custom_call" | custom-call | flops 8589934592 | bytes 2621440 | tf_op jit(solution)/shard_map/graph_layer/pallas_call | solution.py:266
  62.5 0.1 collective-permute-start.14
  62.6 0.5 collective-permute-start.16
  63.1 0.5 collective-permute-start.15
  63.7 0.7 collective-permute-done.14.far_hbm
  64.4 7.6 %graph_layer.5.own_hbm = bf16[512,512]{1,0:T(8,128)(2,1)S(1)} custom-call(s32[1]{0:T(128)} %bitcast.7.core_ref, s32[4096]{0:T(1024)S(1)} %bitcast.36, bf16[512,512]{1,0:T(8,128)(2,1)S(1)} %maximum_select_fusion.1.own_hbm, bf16[512,512]{1,0:T(8,128)(2,1)S(1)} %collective-permute-done.12.sib_hbm, bf16[512,512]{1,0:T(8,128)(2,1)S(1)} %collective-permute-done.13.rim_hbm, ...), custom_call_target="tpu_custom_call" | custom-call | flops 8589934592 | bytes 2621440 | tf_op jit(solution)/shard_map/graph_layer/pallas_call | solution.py:266
  72.0 0.4 collective-permute-done.15.near_hbm
  72.4 2.5 %collective-permute-start.18 = (bf16[784,256]{1,0:T(8,128)(2,1)S(1)}, bf16[784,256]{1,0:T(8,128)(2,1)S(1)}, u32[]{:S(2)}, u32[]{:S(2)}) collective-permute-start(bf16[784,256]{1,0:T(8,128)(2,1)S(1)} %collective-permute-done.15.near_hbm), channel_id=1, source_target_pairs={{0,1},{1,0},{2,3},{3,2},{4,5},{5,4},{6,7},{7,6},{8,9},{9,8},{10,11... | collective-permute-start | bytes 1204232 | tf_op jit(solution)/shard_map/ppermute | solution.py:326
  74.8 4.3 %collective-permute-start.23 = (bf16[512,512]{1,0:T(8,128)(2,1)S(1)}, bf16[512,512]{1,0:T(8,128)(2,1)S(1)}, u32[]{:S(2)}, u32[]{:S(2)}) collective-permute-start(bf16[512,512]{1,0:T(8,128)(2,1)S(1)} %graph_layer.5.own_hbm), channel_id=1, source_target_pairs={{1,4},{5,8},{4,1},{9,12},{8,5},{12,9},{3,6},{7,10},{6,3},{11,14},{... | collective-permute-start | bytes 1572872 | tf_op jit(solution)/shard_map/ppermute | solution.py:337
  79.1 0.6 collective-permute-start.19
  79.7 7.7 %graph_layer.6 = (bf16[512,256]{1,0:T(8,128)(2,1)S(1)}, bf16[512,256]{1,0:T(8,128)(2,1)S(1)}) custom-call(s32[1]{0:T(128)} %bitcast.7.core_ref, s32[4096]{0:T(1024)S(1)} %bitcast.39, bf16[512,512]{1,0:T(8,128)(2,1)S(1)} %graph_layer.4.own_hbm, bf16[512,512]{1,0:T(8,128)(2,1)S(1)} %collective-permute-done.16.sib_hbm, ...), custom_call_target="tpu_custom_call" | custom-call | flops 8589934592 | bytes 2621440 | tf_op jit(solution)/shard_map/graph_layer/pallas_call | solution.py:266
  87.4 0.1 collective-permute-done.19.near_hbm
  87.6 3.2 %collective-permute-start.20 = (bf16[512,256]{1,0:T(8,128)(2,1)S(1)}, bf16[512,256]{1,0:T(8,128)(2,1)S(1)}, u32[]{:S(2)}, u32[]{:S(2)}) collective-permute-start(bf16[512,256]{1,0:T(8,128)(2,1)S(1)} %get-tuple-element.91), channel_id=1, source_target_pairs={{0,0},{1,2},{2,1},{3,3},{4,4},{5,6},{6,5},{7,7},{8,8},{9,10},{10,9... | collective-permute-start | bytes 786440 | tf_op jit(solution)/shard_map/ppermute | solution.py:316
  90.8 0.0 collective-permute-start.21
  90.8 7.7 %graph_layer.7 = (bf16[512,256]{1,0:T(8,128)(2,1)S(1)}, bf16[512,256]{1,0:T(8,128)(2,1)S(1)}) custom-call(s32[1]{0:T(128)} %bitcast.7.core_ref, s32[4096]{0:T(1024)S(1)} %bitcast.37, bf16[512,512]{1,0:T(8,128)(2,1)S(1)} %graph_layer.5.own_hbm, bf16[512,512]{1,0:T(8,128)(2,1)S(1)} %collective-permute-done.22.sib_hbm, ...), custom_call_target="tpu_custom_call" | custom-call | flops 8589934592 | bytes 2621440 | tf_op jit(solution)/shard_map/graph_layer/pallas_call | solution.py:266
  98.5 2.4 %collective-permute-start.25 = (bf16[512,256]{1,0:T(8,128)(2,1)S(1)}, bf16[512,256]{1,0:T(8,128)(2,1)S(1)}, u32[]{:S(2)}, u32[]{:S(2)}) collective-permute-start(bf16[512,256]{1,0:T(8,128)(2,1)S(1)} %get-tuple-element.96), channel_id=1, source_target_pairs={{0,0},{1,2},{2,1},{3,3},{4,4},{5,6},{6,5},{7,7},{8,8},{9,10},{10,9... | collective-permute-start | bytes 786440 | tf_op jit(solution)/shard_map/ppermute | solution.py:316
  101.0 1.0 maximum_select_fusion.2
  102.0 7.0 %collective-permute-done.25 = bf16[512,256]{1,0:T(8,128)(2,1)S(1)} collective-permute-done((bf16[512,256]{1,0:T(8,128)(2,1)S(1)}, bf16[512,256]{1,0:T(8,128)(2,1)S(1)}, u32[]{:S(2)}, u32[]{:S(2)}) %collective-permute-start.25) | collective-permute-done | bytes 262176 | tf_op jit(solution)/shard_map/ppermute | solution.py:316
  109.0 1.0 maximum_select_fusion.3
  (63 shorter events, 0.2 us)
Async XLA Ops:
  0.6 6.7 %copy-start.15 = (s32[1024,8]{0,1:T(8,128)S(1)}, s32[1024,8]{0,1:T(8,128)}, u32[]{:S(2)}) copy-start(s32[1024,8]{0,1:T(8,128)} %param.19) | copy-start | bytes 98308
  0.6 6.7 %copy-start.14 = (s32[1024,8]{0,1:T(8,128)S(1)}, s32[1024,8]{0,1:T(8,128)}, u32[]{:S(2)}) copy-start(s32[1024,8]{0,1:T(8,128)} %param.21) | copy-start | bytes 98308
  0.7 6.8 %copy-start.16 = (s32[512]{0:T(512)S(1)}, s32[512]{0:T(512)}, u32[]{:S(2)}) copy-start(s32[512]{0:T(512)} %param.25) | copy-start | bytes 6148
  0.7 6.8 %copy-start.17 = (s32[512,1]{0,1:T(1,128)S(1)}, s32[512,1]{0,1:T(1,128)}, u32[]{:S(2)}) copy-start(s32[512,1]{0,1:T(1,128)} %param.24) | copy-start | bytes 6148
  0.7 6.8 %copy-start.18 = (s32[512]{0:T(512)S(1)}, s32[512]{0:T(512)}, u32[]{:S(2)}) copy-start(s32[512]{0:T(512)} %param.23) | copy-start | bytes 6148
  0.7 6.8 %copy-start = (bf16[1,1024,256]{2,1,0:T(8,128)(2,1)S(1)}, bf16[1,1024,256]{2,1,0:T(8,128)(2,1)}, u32[]{:S(2)}) copy-start(bf16[1,1024,256]{2,1,0:T(8,128)(2,1)} %param.17) | copy-start | bytes 1572868
  0.7 9.0 %copy-start.3 = (bf16[2,512,256]{2,1,0:T(8,128)(2,1)S(1)}, bf16[2,512,256]{2,1,0:T(8,128)(2,1)}, u32[]{:S(2)}) copy-start(bf16[2,512,256]{2,1,0:T(8,128)(2,1)} %wd_hbm.6) | copy-start | bytes 1572868
  1.9 7.9 %copy-start.2 = (bf16[2,512,256]{2,1,0:T(8,128)(2,1)S(1)}, bf16[2,512,256]{2,1,0:T(8,128)(2,1)}, u32[]{:S(2)}) copy-start(bf16[2,512,256]{2,1,0:T(8,128)(2,1)} %ws_hbm.6) | copy-start | bytes 1572868
  1.9 12.8 %collective-permute-start = (bf16[512,256]{1,0:T(8,128)(2,1)S(1)}, bf16[512,256]{1,0:T(8,128)(2,1)S(1)}, u32[]{:S(2)}, u32[]{:S(2)}) collective-permute-start(bf16[512,256]{1,0:T(8,128)(2,1)S(1)} %get-tuple-element.50), channel_id=1, source_target_pairs={{0,0},{1,2},{2,1},{3,3},{4,4},{5,6},{6,5},{7,7},{8,8},{9,10},{10,9... | collective-permute-start | bytes 786440 | tf_op jit(solution)/shard_map/ppermute | solution.py:310
  6.5 8.2 %collective-permute-start.1 = (bf16[512,256]{1,0:T(8,128)(2,1)S(1)}, bf16[512,256]{1,0:T(8,128)(2,1)S(1)}, u32[]{:S(2)}, u32[]{:S(2)}) collective-permute-start(bf16[512,256]{1,0:T(8,128)(2,1)S(1)} %get-tuple-element.51), channel_id=1, source_target_pairs={{0,1},{1,3},{2,0},{3,2},{4,5},{5,7},{6,4},{7,6},{8,9},{9,11},{10,8... | collective-permute-start | bytes 786440 | tf_op jit(solution)/shard_map/ppermute | solution.py:311
  7.5 2.3 %copy-start.13 = (bf16[2,256]{1,0:T(2,128)(2,1)S(1)}, bf16[2,256]{1,0:T(2,128)(2,1)}, u32[]{:S(2)}) copy-start(bf16[2,256]{1,0:T(2,128)(2,1)} %b_hbm.7) | copy-start | bytes 3076
  9.7 0.7 copy-start.12
  10.4 1.0 copy-start.4
  11.4 1.0 copy-start.6
  12.5 1.0 copy-start.8
  13.5 1.0 copy-start.10
  14.7 14.8 %copy-start.1 = (bf16[1,1024,256]{2,1,0:T(8,128)(2,1)S(1)}, bf16[1,1024,256]{2,1,0:T(8,128)(2,1)}, u32[]{:S(2)}) copy-start(bf16[1,1024,256]{2,1,0:T(8,128)(2,1)} %param.18) | copy-start | bytes 1572868
  14.9 5.2 %collective-permute-start.2 = (bf16[512,512]{1,0:T(8,128)(2,1)S(1)}, bf16[512,512]{1,0:T(8,128)(2,1)S(1)}, u32[]{:S(2)}, u32[]{:S(2)}) collective-permute-start(bf16[512,512]{1,0:T(8,128)(2,1)S(1)} %maximum_select_fusion.own_hbm), channel_id=1, source_target_pairs={{0,1},{1,0},{2,3},{3,2},{4,5},{5,4},{6,7},{7,6},{8,9},{9,8},{10,11... | collective-permute-start | bytes 1572872 | tf_op jit(solution)/shard_map/ppermute | solution.py:326
  15.4 14.9 %collective-permute-start.6 = (bf16[784,256]{1,0:T(8,128)(2,1)S(1)}, bf16[784,256]{1,0:T(8,128)(2,1)S(1)}, u32[]{:S(2)}, u32[]{:S(2)}) collective-permute-start(bf16[784,256]{1,0:T(8,128)(2,1)S(1)} %get-tuple-element.66), channel_id=1, source_target_pairs={{0,2},{2,0},{1,3},{3,1},{4,6},{6,4},{5,7},{7,5},{8,10},{10,8},{9,1... | collective-permute-start | bytes 1204232 | tf_op jit(solution)/shard_map/ppermute | solution.py:326
  15.4 6.8 %collective-permute-start.3 = (bf16[272,256]{1,0:T(8,128)(2,1)S(1)}, bf16[272,256]{1,0:T(8,128)(2,1)S(1)}, u32[]{:S(2)}, u32[]{:S(2)}) collective-permute-start(bf16[272,256]{1,0:T(8,128)(2,1)S(1)} %get-tuple-element.60), channel_id=1, source_target_pairs={{0,4},{4,8},{8,12},{12,0},{1,5},{5,9},{9,13},{13,1},{2,6},{6,10},{... | collective-permute-start | bytes 417800 | tf_op jit(solution)/shard_map/ppermute | solution.py:393
  16.7 12.8 %collective-permute-start.4 = (bf16[272,256]{1,0:T(8,128)(2,1)S(1)}, bf16[272,256]{1,0:T(8,128)(2,1)S(1)}, u32[]{:S(2)}, u32[]{:S(2)}) collective-permute-start(bf16[272,256]{1,0:T(8,128)(2,1)S(1)} %get-tuple-element.61), channel_id=1, source_target_pairs={{0,8},{4,12},{8,0},{12,4},{1,9},{5,13},{9,1},{13,5},{2,10},{6,14},... | collective-permute-start | bytes 417800 | tf_op jit(solution)/shard_map/ppermute | solution.py:393
  19.0 10.5 %collective-permute-start.5 = (bf16[272,256]{1,0:T(8,128)(2,1)S(1)}, bf16[272,256]{1,0:T(8,128)(2,1)S(1)}, u32[]{:S(2)}, u32[]{:S(2)}) collective-permute-start(bf16[272,256]{1,0:T(8,128)(2,1)S(1)} %get-tuple-element.62), channel_id=1, source_target_pairs={{0,12},{4,0},{8,4},{12,8},{1,13},{5,1},{9,5},{13,9},{2,14},{6,2},{... | collective-permute-start | bytes 417800 | tf_op jit(solution)/shard_map/ppermute | solution.py:393
  20.1 34.8 %collective-permute-start.9 = (bf16[512,512]{1,0:T(8,128)(2,1)S(1)}, bf16[512,512]{1,0:T(8,128)(2,1)S(1)}, u32[]{:S(2)}, u32[]{:S(2)}) collective-permute-start(bf16[512,512]{1,0:T(8,128)(2,1)S(1)} %maximum_select_fusion.own_hbm), channel_id=1, source_target_pairs={{1,4},{0,13},{5,8},{4,1},{9,12},{8,5},{13,0},{12,9},{3,6},{2,15},{... | collective-permute-start | bytes 1572872 | tf_op jit(solution)/shard_map/ppermute | solution.py:337
  30.3 24.6 %collective-permute-start.10 = (bf16[784,256]{1,0:T(8,128)(2,1)S(1)}, bf16[784,256]{1,0:T(8,128)(2,1)S(1)}, u32[]{:S(2)}, u32[]{:S(2)}) collective-permute-start(bf16[784,256]{1,0:T(8,128)(2,1)S(1)} %collective-permute-done.6.near_hbm), channel_id=1, source_target_pairs={{0,1},{1,0},{2,3},{3,2},{4,5},{5,4},{6,7},{7,6},{8,9},{9,8},{10,11... | collective-permute-start | bytes 1204232 | tf_op jit(solution)/shard_map/ppermute | solution.py:326
  31.1 9.7 %collective-permute-start.7 = (bf16[512,256]{1,0:T(8,128)(2,1)S(1)}, bf16[512,256]{1,0:T(8,128)(2,1)S(1)}, u32[]{:S(2)}, u32[]{:S(2)}) collective-permute-start(bf16[512,256]{1,0:T(8,128)(2,1)S(1)} %get-tuple-element.67), channel_id=1, source_target_pairs={{0,0},{1,2},{2,1},{3,3},{4,4},{5,6},{6,5},{7,7},{8,8},{9,10},{10,9... | collective-permute-start | bytes 786440 | tf_op jit(solution)/shard_map/ppermute | solution.py:310
  34.4 10.4 %collective-permute-start.8 = (bf16[512,256]{1,0:T(8,128)(2,1)S(1)}, bf16[512,256]{1,0:T(8,128)(2,1)S(1)}, u32[]{:S(2)}, u32[]{:S(2)}) collective-permute-start(bf16[512,256]{1,0:T(8,128)(2,1)S(1)} %get-tuple-element.68), channel_id=1, source_target_pairs={{0,1},{1,3},{2,0},{3,2},{4,5},{5,7},{6,4},{7,6},{8,9},{9,11},{10,8... | collective-permute-start | bytes 786440 | tf_op jit(solution)/shard_map/ppermute | solution.py:311
  34.4 20.5 %copy-start.5 = (bf16[2,256,512]{2,1,0:T(8,128)(2,1)S(1)}, bf16[2,256,512]{2,1,0:T(8,128)(2,1)}, u32[]{:S(2)}) copy-start(bf16[2,256,512]{2,1,0:T(8,128)(2,1)} %w2_hbm.6) | copy-start | bytes 1572868
  34.4 28.1 %collective-permute-start.11 = (bf16[784,256]{1,0:T(8,128)(2,1)S(1)}, bf16[784,256]{1,0:T(8,128)(2,1)S(1)}, u32[]{:S(2)}, u32[]{:S(2)}) collective-permute-start(bf16[784,256]{1,0:T(8,128)(2,1)S(1)} %get-tuple-element.75), channel_id=1, source_target_pairs={{0,2},{2,0},{1,3},{3,1},{4,6},{6,4},{5,7},{7,5},{8,10},{10,8},{9,1... | collective-permute-start | bytes 1204232 | tf_op jit(solution)/shard_map/ppermute | solution.py:326
  44.9 19.4 %copy-start.7 = (bf16[2,512,256]{2,1,0:T(8,128)(2,1)S(1)}, bf16[2,512,256]{2,1,0:T(8,128)(2,1)}, u32[]{:S(2)}) copy-start(bf16[2,512,256]{2,1,0:T(8,128)(2,1)} %ws_hbm.7) | copy-start | bytes 1572868
  44.9 19.4 %copy-start.9 = (bf16[2,512,256]{2,1,0:T(8,128)(2,1)S(1)}, bf16[2,512,256]{2,1,0:T(8,128)(2,1)}, u32[]{:S(2)}) copy-start(bf16[2,512,256]{2,1,0:T(8,128)(2,1)} %wd_hbm.7) | copy-start | bytes 1572868
  44.9 19.4 %copy-start.11 = (bf16[2,256,512]{2,1,0:T(8,128)(2,1)S(1)}, bf16[2,256,512]{2,1,0:T(8,128)(2,1)}, u32[]{:S(2)}) copy-start(bf16[2,256,512]{2,1,0:T(8,128)(2,1)} %w2_hbm.7) | copy-start | bytes 1572868
  45.0 18.2 %collective-permute-start.12 = (bf16[512,512]{1,0:T(8,128)(2,1)S(1)}, bf16[512,512]{1,0:T(8,128)(2,1)S(1)}, u32[]{:S(2)}, u32[]{:S(2)}) collective-permute-start(bf16[512,512]{1,0:T(8,128)(2,1)S(1)} %maximum_select_fusion.1.own_hbm), channel_id=1, source_target_pairs={{0,1},{1,0},{2,3},{3,2},{4,5},{5,4},{6,7},{7,6},{8,9},{9,8},{10,11... | collective-permute-start | bytes 1572872 | tf_op jit(solution)/shard_map/ppermute | solution.py:326
  46.9 16.8 %collective-permute-start.13 = (bf16[512,512]{1,0:T(8,128)(2,1)S(1)}, bf16[512,512]{1,0:T(8,128)(2,1)S(1)}, u32[]{:S(2)}, u32[]{:S(2)}) collective-permute-start(bf16[512,512]{1,0:T(8,128)(2,1)S(1)} %maximum_select_fusion.1.own_hbm), channel_id=1, source_target_pairs={{1,4},{5,8},{4,1},{9,12},{8,5},{12,9},{3,6},{7,10},{6,3},{11,14},{... | collective-permute-start | bytes 1572872 | tf_op jit(solution)/shard_map/ppermute | solution.py:337
  62.5 1.8 %collective-permute-start.14 = (bf16[784,256]{1,0:T(8,128)(2,1)S(1)}, bf16[784,256]{1,0:T(8,128)(2,1)S(1)}, u32[]{:S(2)}, u32[]{:S(2)}) collective-permute-start(bf16[784,256]{1,0:T(8,128)(2,1)S(1)} %collective-permute-done.11.near_hbm), channel_id=1, source_target_pairs={{0,1},{1,0},{2,3},{3,2},{4,5},{5,4},{6,7},{7,6},{8,9},{9,8},{10,11... | collective-permute-start | bytes 1204232 | tf_op jit(solution)/shard_map/ppermute | solution.py:326
  62.6 16.5 %collective-permute-start.16 = (bf16[512,512]{1,0:T(8,128)(2,1)S(1)}, bf16[512,512]{1,0:T(8,128)(2,1)S(1)}, u32[]{:S(2)}, u32[]{:S(2)}) collective-permute-start(bf16[512,512]{1,0:T(8,128)(2,1)S(1)} %graph_layer.4.own_hbm), channel_id=1, source_target_pairs={{0,1},{1,0},{2,3},{3,2},{4,5},{5,4},{6,7},{7,6},{8,9},{9,8},{10,11... | collective-permute-start | bytes 1572872 | tf_op jit(solution)/shard_map/ppermute | solution.py:326
  63.1 16.6 %collective-permute-start.17 = (bf16[512,512]{1,0:T(8,128)(2,1)S(1)}, bf16[512,512]{1,0:T(8,128)(2,1)S(1)}, u32[]{:S(2)}, u32[]{:S(2)}) collective-permute-start(bf16[512,512]{1,0:T(8,128)(2,1)S(1)} %graph_layer.4.own_hbm), channel_id=1, source_target_pairs={{1,4},{0,13},{5,8},{4,1},{9,12},{8,5},{13,0},{12,9},{3,6},{2,15},{... | collective-permute-start | bytes 1572872 | tf_op jit(solution)/shard_map/ppermute | solution.py:337
  63.1 9.2 %collective-permute-start.15 = (bf16[784,256]{1,0:T(8,128)(2,1)S(1)}, bf16[784,256]{1,0:T(8,128)(2,1)S(1)}, u32[]{:S(2)}, u32[]{:S(2)}) collective-permute-start(bf16[784,256]{1,0:T(8,128)(2,1)S(1)} %get-tuple-element.82), channel_id=1, source_target_pairs={{0,2},{2,0},{1,3},{3,1},{4,6},{6,4},{5,7},{7,5},{8,10},{10,8},{9,1... | collective-permute-start | bytes 1204232 | tf_op jit(solution)/shard_map/ppermute | solution.py:326
  72.4 7.4 %collective-permute-start.18 = (bf16[784,256]{1,0:T(8,128)(2,1)S(1)}, bf16[784,256]{1,0:T(8,128)(2,1)S(1)}, u32[]{:S(2)}, u32[]{:S(2)}) collective-permute-start(bf16[784,256]{1,0:T(8,128)(2,1)S(1)} %collective-permute-done.15.near_hbm), channel_id=1, source_target_pairs={{0,1},{1,0},{2,3},{3,2},{4,5},{5,4},{6,7},{7,6},{8,9},{9,8},{10,11... | collective-permute-start | bytes 1204232 | tf_op jit(solution)/shard_map/ppermute | solution.py:326
  74.8 15.9 %collective-permute-start.22 = (bf16[512,512]{1,0:T(8,128)(2,1)S(1)}, bf16[512,512]{1,0:T(8,128)(2,1)S(1)}, u32[]{:S(2)}, u32[]{:S(2)}) collective-permute-start(bf16[512,512]{1,0:T(8,128)(2,1)S(1)} %graph_layer.5.own_hbm), channel_id=1, source_target_pairs={{0,1},{1,0},{2,3},{3,2},{4,5},{5,4},{6,7},{7,6},{8,9},{9,8},{10,11... | collective-permute-start | bytes 1572872 | tf_op jit(solution)/shard_map/ppermute | solution.py:326
  74.8 16.0 %collective-permute-start.23 = (bf16[512,512]{1,0:T(8,128)(2,1)S(1)}, bf16[512,512]{1,0:T(8,128)(2,1)S(1)}, u32[]{:S(2)}, u32[]{:S(2)}) collective-permute-start(bf16[512,512]{1,0:T(8,128)(2,1)S(1)} %graph_layer.5.own_hbm), channel_id=1, source_target_pairs={{1,4},{5,8},{4,1},{9,12},{8,5},{12,9},{3,6},{7,10},{6,3},{11,14},{... | collective-permute-start | bytes 1572872 | tf_op jit(solution)/shard_map/ppermute | solution.py:337
  79.1 8.5 %collective-permute-start.19 = (bf16[784,256]{1,0:T(8,128)(2,1)S(1)}, bf16[784,256]{1,0:T(8,128)(2,1)S(1)}, u32[]{:S(2)}, u32[]{:S(2)}) collective-permute-start(bf16[784,256]{1,0:T(8,128)(2,1)S(1)} %get-tuple-element.90), channel_id=1, source_target_pairs={{0,2},{2,0},{1,3},{3,1},{4,6},{6,4},{5,7},{7,5},{8,10},{10,8},{9,1... | collective-permute-start | bytes 1204232 | tf_op jit(solution)/shard_map/ppermute | solution.py:326
  87.6 3.2 %collective-permute-start.24 = (bf16[784,256]{1,0:T(8,128)(2,1)S(1)}, bf16[784,256]{1,0:T(8,128)(2,1)S(1)}, u32[]{:S(2)}, u32[]{:S(2)}) collective-permute-start(bf16[784,256]{1,0:T(8,128)(2,1)S(1)} %collective-permute-done.19.near_hbm), channel_id=1, source_target_pairs={{0,1},{1,0},{2,3},{3,2},{4,5},{5,4},{6,7},{7,6},{8,9},{9,8},{10,11... | collective-permute-start | bytes 1204232 | tf_op jit(solution)/shard_map/ppermute | solution.py:326
  87.6 13.4 %collective-permute-start.20 = (bf16[512,256]{1,0:T(8,128)(2,1)S(1)}, bf16[512,256]{1,0:T(8,128)(2,1)S(1)}, u32[]{:S(2)}, u32[]{:S(2)}) collective-permute-start(bf16[512,256]{1,0:T(8,128)(2,1)S(1)} %get-tuple-element.91), channel_id=1, source_target_pairs={{0,0},{1,2},{2,1},{3,3},{4,4},{5,6},{6,5},{7,7},{8,8},{9,10},{10,9... | collective-permute-start | bytes 786440 | tf_op jit(solution)/shard_map/ppermute | solution.py:316
  90.8 10.2 %collective-permute-start.21 = (bf16[512,256]{1,0:T(8,128)(2,1)S(1)}, bf16[512,256]{1,0:T(8,128)(2,1)S(1)}, u32[]{:S(2)}, u32[]{:S(2)}) collective-permute-start(bf16[512,256]{1,0:T(8,128)(2,1)S(1)} %get-tuple-element.92), channel_id=1, source_target_pairs={{0,2},{1,0},{2,3},{3,1},{4,6},{5,4},{6,7},{7,5},{8,10},{9,8},{10,1... | collective-permute-start | bytes 786440 | tf_op jit(solution)/shard_map/ppermute | solution.py:317
  98.5 10.5 %collective-permute-start.25 = (bf16[512,256]{1,0:T(8,128)(2,1)S(1)}, bf16[512,256]{1,0:T(8,128)(2,1)S(1)}, u32[]{:S(2)}, u32[]{:S(2)}) collective-permute-start(bf16[512,256]{1,0:T(8,128)(2,1)S(1)} %get-tuple-element.96), channel_id=1, source_target_pairs={{0,0},{1,2},{2,1},{3,3},{4,4},{5,6},{6,5},{7,7},{8,8},{9,10},{10,9... | collective-permute-start | bytes 786440 | tf_op jit(solution)/shard_map/ppermute | solution.py:316
  100.9 8.0 %collective-permute-start.26 = (bf16[512,256]{1,0:T(8,128)(2,1)S(1)}, bf16[512,256]{1,0:T(8,128)(2,1)S(1)}, u32[]{:S(2)}, u32[]{:S(2)}) collective-permute-start(bf16[512,256]{1,0:T(8,128)(2,1)S(1)} %get-tuple-element.97), channel_id=1, source_target_pairs={{0,2},{1,0},{2,3},{3,1},{4,6},{5,4},{6,7},{7,5},{8,10},{9,8},{10,1... | collective-permute-start | bytes 786440 | tf_op jit(solution)/shard_map/ppermute | solution.py:317

commit v4 on v3

--- a/solution.py
+++ b/solution.py
@@ -338,26 +338,33 @@
 
 
 def pack_kernel(order, core_ref, g_bias, r_bias, *refs):
-    weights, outs = (refs[:3], refs[3:6]), refs[6:]
+    weights, outs, sems = (refs[:3], refs[3:6]), refs[6:-1], refs[-1]
     share = g_bias.shape[1]
     here = pl.multiple_of(core_ref[0] * share, share)
+    copies = []
     for (graph, layer), out in zip(order, outs):
         ws, wd, w2 = weights[graph]
+        sources = (ws.at[layer, pl.ds(here, share), :], wd.at[layer, pl.ds(here, share), :], w2.at[layer, :, pl.ds(here, share)])
+        for i, source in enumerate(sources):
+            copies.append(pltpu.make_async_copy(source, out.at[i * share:(i + 1) * share, :], sems.at[len(copies)]))
+            copies[-1].start()
+    for (graph, layer), out in zip(order, outs):
         bias = (g_bias, r_bias)[graph][layer:layer + 1, :]
-        out[0:share, :] = ws[layer, pl.ds(here, share), :]
-        out[share:2 * share, :] = wd[layer, pl.ds(here, share), :]
-        out[2 * share:3 * share, :] = w2[layer, :, pl.ds(here, share)]
         out[3 * share:, :] = jnp.broadcast_to(bias, (16, share))
+    for copy in copies:
+        copy.wait()
 
 
 def pack_weights(order, core, g_weights, g_bias, r_weights, r_bias):
     share = g_bias.shape[1]
     vmem = pl.BlockSpec(memory_space=pltpu.VMEM)
+    hbm = pl.BlockSpec(memory_space=pltpu.HBM)
     return pl.pallas_call(
         functools.partial(pack_kernel, order),
         out_shape=(jax.ShapeDtypeStruct((3 * share + 16, share), jnp.bfloat16),) * len(order),
-        in_specs=[pl.BlockSpec(memory_space=pltpu.SMEM)] + [vmem] * 8,
+        in_specs=[pl.BlockSpec(memory_space=pltpu.SMEM)] + [vmem] * 2 + [hbm] * 6,
         out_specs=(vmem,) * len(order),
+        scratch_shapes=[pltpu.SemaphoreType.DMA((3 * len(order),))],
         compiler_params=pltpu.CompilerParams(vmem_limit_bytes=32 << 20),
         cost_estimate=SMALL,
         name="pack_weights",
@@ -382,27 +389,27 @@
     g_weights, r_weights = (g_ws, g_wd, g_w2), (r_ws, r_wd, r_w2)
     after = lax.optimization_barrier
 
-    same = lax.dynamic_slice(g_own, (part * half, 0), (half, g_own.shape[1]))
-    other = lax.dynamic_slice(g_own, ((1 - part) * half, 0), (half, g_own.shape[1]))
-    same, other, bnd_src = after((same, other, bnd_src))
-    g_a, g_b = spread_rows(same, other)
     bnd = jnp.stack([bnd_src, bnd_part[:, 0], bnd_node])
     pieces = pick_rows(me, bnd, g_own, parts, cap)
     landed = [pieces[0]]
     for k in range(1, parts):
         landed.append(lax.ppermute(pieces[k], "mesh", [(i, (i + k) % parts) for i in range(parts)]))
+    landed[0], g_late = after((landed[0], g_own))
+    same = lax.dynamic_slice(g_late, (part * half, 0), (half, g_own.shape[1]))
+    other = lax.dynamic_slice(g_late, ((1 - part) * half, 0), (half, g_own.shape[1]))
+    same, other, core1 = after((same, other, core1))
+    g_a, g_b = spread_rows(same, other)
     idx = edge_offsets(jnp.stack([g_nbr, r_nbr]), jnp.stack([g_count, r_count]), core)
 
     order = [(graph, layer) for layer in range(layers) for graph in (0, 1)]
-    packs = pack_weights(order, core1, g_weights, g_b1, r_weights, r_b1)
-    g_a, g_b, g_idx, r_idx, core1, landed[0], sent = after((g_a, g_b, idx[0], idx[1], core1, landed[0], packs[0]))
-    near_w = [swap(sent, "mp")]
+    packs = list(pack_weights(order, core1, g_weights, g_b1, r_weights, r_b1))
+    near_w = [swap(packs[0], "mp")]
+    g_idx, r_idx = idx[0], idx[1]
+    g_a, g_b, g_idx, r_idx, packs[1], *landed = after((g_a, g_b, g_idx, r_idx, packs[1], *landed))
     planet = ordered(core, g_a, g_b, 1)
     g_sib, g_rim = swap(planet, "batch"), rims(planet, True)
-    g_sib, r_own = after((g_sib, r_own))
-    r_pair = add_force(part.reshape(1), r_own, landed, cap)
-    *r_pair, g_idx, near_w[0] = after((*r_pair, g_idx, near_w[0]))
-    r_a, r_b = spread_rows(*r_pair)
+    r_a, r_b = spread_rows(*add_force(part.reshape(1), r_own, landed, cap))
+    r_a, r_b, g_sib, near_w[0] = after((r_a, r_b, g_sib, near_w[0]))
     regional, g_idx = after((ordered(core, r_a, r_b, 1), g_idx))
     r_sib, r_rim = swap(regional, "batch"), rims(regional, False)
     far_w = []

time: 111 us -> 106 us (0.955)
  waiting for transfers between devices: 26 us -> 21 us
  starting transfers between devices: 40 us -> 38.2 us
  Pallas kernels: 33.7 us -> 35.1 us
    ppermute x12, waiting for transfers between devices: 1.21 us -> 8.71 us  [swap(): return lax.ppermute(values, axis, [(0, 1), (1, 0)])]
    ppermute x3, waiting for transfers between devices: 7.94 us -> 2.24 us  [by_rows(): lax.ppermute(pieces[k], 'mesh', [(i, (i + k) % parts) for i in range(part...]
    ppermute x2, waiting for transfers between devices: 3.99 us -> 0.65 us  [spread_rows(): b = lax.ppermute(other, ('mp', 'batch'), [(0, 1), (1, 3), (2, 0), (3, 2)])]
    ppermute x12, starting transfers between devices: 8.03 us -> 4.78 us  [swap(): return lax.ppermute(values, axis, [(0, 1), (1, 0)])]
    ppermute x2, waiting for transfers between devices: 5.86 us -> 3.27 us  [spread_rows(): a = lax.ppermute(same, ('mp', 'batch'), [(0, 0), (1, 2), (2, 1), (3, 3)])]
    unnamed x41 -> x47, local copies, waits for them, and re-layouts: 4.9 us -> 6.8 us
    ppermute x2, waiting for transfers between devices: 6.97 us -> 5.4 us  [gather_rows(): same = lax.ppermute(a, ('mp', 'batch'), [(0, 0), (1, 2), (2, 1), (3, 3)])]
    pallas_call x1, Pallas kernels: 0.11 us -> 1.49 us  [pack_weights(): pl.pallas_call(functools.partial(pack_kernel, order), out_shape=(jax.Shap...]
  transfers between devices with their start and end apart: 27 -> 27, of which waited for: 8 -> 8; matrix products, arithmetic and copies ran while one was open for 2% -> 1% of each run, Pallas kernels for 31% -> 31%
where the time goes in v4:
time: 106 us; the launch traced here: 105 us
  starting transfers between devices  38.2 us (36%)
  Pallas kernels  35.1 us (33%)
  waiting for transfers between devices  21 us (20%)
  local copies, waits for them, and re-layouts  6.85 us (6%)
  other arithmetic  2.41 us (2%)
  between operations  1.14 us (1%)
    pallas_call x4, Pallas kernels, run_layer(): pl.pallas_call(functools.partial(layer_kernel, layer, slots, last), out_s...  30.7 us
    ppermute x4, starting transfers between devices, rims(): return lax.ppermute(own, ('mesh', 'batch'), pairs)  15.1 us
    ppermute x12, waiting for transfers between devices, swap(): return lax.ppermute(values, axis, [(0, 1), (1, 0)])  8.71 us
    ppermute x2, starting transfers between devices, spread_rows(): a = lax.ppermute(same, ('mp', 'batch'), [(0, 0), (1, 2), (2, 1), (3, 3)])  8.01 us
    unnamed x47, local copies, waits for them, and re-layouts  6.8 us
    ppermute x2, starting transfers between devices, gather_rows(): same = lax.ppermute(a, ('mp', 'batch'), [(0, 0), (1, 2), (2, 1), (3, 3)])  5.55 us
    ppermute x2, waiting for transfers between devices, gather_rows(): same = lax.ppermute(a, ('mp', 'batch'), [(0, 0), (1, 2), (2, 1), (3, 3)])  5.4 us
    ppermute x12, starting transfers between devices, swap(): return lax.ppermute(values, axis, [(0, 1), (1, 0)])  4.78 us
  transfers between devices with their start and end apart: 27, of which 8 were waited for; matrix products, arithmetic and copies ran while one was open for 1% of the time, Pallas kernels for 31%

profile of v4, /device:TPU:1, one launch (start us, length us, event | category | flops | bytes accessed | tf_op | source)
XLA Modules:
  0.0 104.8 jit_solution(3669645739107217738)
XLA Ops:
  0.7 0.7 copy-done.21
  1.4 1.0 copy-done
  2.4 2.2 %pick_rows.1 = (bf16[272,256]{1,0:T(8,128)(2,1)S(1)}, bf16[272,256]{1,0:T(8,128)(2,1)S(1)}, bf16[272,256]{1,0:T(8,128)(2,1)S(1)}, bf16[272,256]{1,0:T(8,128)(2,1)S(1)}) custom-call(s32[1]{0:T(128)} %bitcast.me_ref, s32[3,512]{1,0:T(4,128)S(1)} %pad_add_fusion.bnd_ref, bf16[1024,256]{1,0:T(8,128)(2,1)S(1)} %bitcast.30), custom_call_target="tpu_custom_call" | custom-call | flops 1 | bytes 1 | tf_op jit(solution)/shard_map/pick_rows/pallas_call | solution.py:115
  4.8 4.6 %collective-permute-start = (bf16[512,256]{1,0:T(8,128)(2,1)S(1)}, bf16[512,256]{1,0:T(8,128)(2,1)S(1)}, u32[]{:S(2)}, u32[]{:S(2)}) collective-permute-start(bf16[512,256]{1,0:T(8,128)(2,1)S(1)} %get-tuple-element.55), channel_id=1, source_target_pairs={{0,0},{1,2},{2,1},{3,3},{4,4},{5,6},{6,5},{7,7},{8,8},{9,10},{10,9... | collective-permute-start | bytes 786440 | tf_op jit(solution)/shard_map/ppermute | solution.py:310
  9.5 1.3 %collective-permute-start.2 = (bf16[272,256]{1,0:T(8,128)(2,1)S(1)}, bf16[272,256]{1,0:T(8,128)(2,1)S(1)}, u32[]{:S(2)}, u32[]{:S(2)}) collective-permute-start(bf16[272,256]{1,0:T(8,128)(2,1)S(1)} %get-tuple-element.59), channel_id=1, source_target_pairs={{0,4},{4,8},{8,12},{12,0},{1,5},{5,9},{9,13},{13,1},{2,6},{6,10},{... | collective-permute-start | bytes 417800 | tf_op jit(solution)/shard_map/ppermute | solution.py:396
  10.8 2.3 %collective-permute-start.3 = (bf16[272,256]{1,0:T(8,128)(2,1)S(1)}, bf16[272,256]{1,0:T(8,128)(2,1)S(1)}, u32[]{:S(2)}, u32[]{:S(2)}) collective-permute-start(bf16[272,256]{1,0:T(8,128)(2,1)S(1)} %get-tuple-element.60), channel_id=1, source_target_pairs={{0,8},{4,12},{8,0},{12,4},{1,9},{5,13},{9,1},{13,5},{2,10},{6,14},... | collective-permute-start | bytes 417800 | tf_op jit(solution)/shard_map/ppermute | solution.py:396
  13.1 1.1 %collective-permute-start.4 = (bf16[272,256]{1,0:T(8,128)(2,1)S(1)}, bf16[272,256]{1,0:T(8,128)(2,1)S(1)}, u32[]{:S(2)}, u32[]{:S(2)}) collective-permute-start(bf16[272,256]{1,0:T(8,128)(2,1)S(1)} %get-tuple-element.61), channel_id=1, source_target_pairs={{0,12},{4,0},{8,4},{12,8},{1,13},{5,1},{9,5},{13,9},{2,14},{6,2},{... | collective-permute-start | bytes 417800 | tf_op jit(solution)/shard_map/ppermute | solution.py:396
  14.2 0.1 fusion.5
  14.4 0.6 copy-done.13
  15.0 1.0 copy-done.5
  16.0 1.0 copy-done.7
  17.1 1.0 copy-done.9
  18.1 1.0 copy-done.11
  19.1 1.5 %pack_weights.1 = (bf16[784,256]{1,0:T(8,128)(2,1)S(1)}, bf16[784,256]{1,0:T(8,128)(2,1)S(1)}, bf16[784,256]{1,0:T(8,128)(2,1)S(1)}, bf16[784,256]{1,0:T(8,128)(2,1)S(1)}) custom-call(s32[1]{0:T(128)} %bitcast.5.core_ref, bf16[2,256]{1,0:T(2,128)(2,1)S(1)} %copy-done.13, bf16[2,256]{1,0:T(2,128)(2,1)S(1)} %copy-done.14, bf16[2,512,256]{2,1,0:T(8,128)(2,1)S(1)} %copy-done.3, ...), custom_call_target="tpu_custom_call" | custom-call | flops 1 | bytes 1 | tf_op jit(solution)/shard_map/pack_weights/pallas_call | solution.py:362
  20.7 2.2 %collective-permute-done.3.refs_2_ = bf16[272,256]{1,0:T(8,128)(2,1)S(1)} collective-permute-done((bf16[272,256]{1,0:T(8,128)(2,1)S(1)}, bf16[272,256]{1,0:T(8,128)(2,1)S(1)}, u32[]{:S(2)}, u32[]{:S(2)}) %collective-permute-start.3) | collective-permute-done | bytes 139296 | tf_op jit(solution)/shard_map/ppermute | solution.py:396
  23.0 0.1 maximum_select_fusion.own_hbm
  23.1 0.7 collective-permute-start.7
  23.7 0.1 collective-permute-start.8
  23.8 0.2 copy-done.2
  24.0 0.7 add_force.1
  24.7 3.4 %collective-permute-start.5 = (bf16[512,256]{1,0:T(8,128)(2,1)S(1)}, bf16[512,256]{1,0:T(8,128)(2,1)S(1)}, u32[]{:S(2)}, u32[]{:S(2)}) collective-permute-start(bf16[512,256]{1,0:T(8,128)(2,1)S(1)} %get-tuple-element.66), channel_id=1, source_target_pairs={{0,0},{1,2},{2,1},{3,3},{4,4},{5,6},{6,5},{7,7},{8,8},{9,10},{10,9... | collective-permute-start | bytes 786440 | tf_op jit(solution)/shard_map/ppermute | solution.py:310
  28.1 3.5 %collective-permute-start.9 = (bf16[512,512]{1,0:T(8,128)(2,1)S(1)}, bf16[512,512]{1,0:T(8,128)(2,1)S(1)}, u32[]{:S(2)}, u32[]{:S(2)}) collective-permute-start(bf16[512,512]{1,0:T(8,128)(2,1)S(1)} %maximum_select_fusion.own_hbm), channel_id=1, source_target_pairs={{1,4},{0,13},{5,8},{4,1},{9,12},{8,5},{13,0},{12,9},{3,6},{2,15},{... | collective-permute-start | bytes 1572872 | tf_op jit(solution)/shard_map/ppermute | solution.py:337
  31.7 2.9 %collective-permute-done.8.near_hbm = bf16[784,256]{1,0:T(8,128)(2,1)S(1)} collective-permute-done((bf16[784,256]{1,0:T(8,128)(2,1)S(1)}, bf16[784,256]{1,0:T(8,128)(2,1)S(1)}, u32[]{:S(2)}, u32[]{:S(2)}) %collective-permute-start.8) | collective-permute-done | bytes 401440 | tf_op jit(solution)/shard_map/ppermute | solution.py:326
  34.6 3.3 %collective-permute-done.5 = bf16[512,256]{1,0:T(8,128)(2,1)S(1)} collective-permute-done((bf16[512,256]{1,0:T(8,128)(2,1)S(1)}, bf16[512,256]{1,0:T(8,128)(2,1)S(1)}, u32[]{:S(2)}, u32[]{:S(2)}) %collective-permute-start.5) | collective-permute-done | bytes 262176 | tf_op jit(solution)/shard_map/ppermute | solution.py:310
  37.9 0.6 collective-permute-done.6
  38.5 2.6 %collective-permute-start.10 = (bf16[784,256]{1,0:T(8,128)(2,1)S(1)}, bf16[784,256]{1,0:T(8,128)(2,1)S(1)}, u32[]{:S(2)}, u32[]{:S(2)}) collective-permute-start(bf16[784,256]{1,0:T(8,128)(2,1)S(1)} %collective-permute-done.8.near_hbm), channel_id=1, source_target_pairs={{0,1},{1,0},{2,3},{3,2},{4,5},{5,4},{6,7},{7,6},{8,9},{9,8},{10,11... | collective-permute-start | bytes 1204232 | tf_op jit(solution)/shard_map/ppermute | solution.py:326
  41.1 0.1 maximum_select_fusion.1.own_hbm
  41.2 0.1 collective-permute-start.12
  41.3 5.4 %collective-permute-start.13 = (bf16[512,512]{1,0:T(8,128)(2,1)S(1)}, bf16[512,512]{1,0:T(8,128)(2,1)S(1)}, u32[]{:S(2)}, u32[]{:S(2)}) collective-permute-start(bf16[512,512]{1,0:T(8,128)(2,1)S(1)} %maximum_select_fusion.1.own_hbm), channel_id=1, source_target_pairs={{1,4},{5,8},{4,1},{9,12},{8,5},{12,9},{3,6},{7,10},{6,3},{11,14},{... | collective-permute-start | bytes 1572872 | tf_op jit(solution)/shard_map/ppermute | solution.py:337
  46.8 0.1 collective-permute-start.11
  46.9 7.6 %graph_layer.4.own_hbm = bf16[512,512]{1,0:T(8,128)(2,1)S(1)} custom-call(s32[1]{0:T(128)} %bitcast.5.core_ref, s32[4096]{0:T(1024)S(1)} %bitcast.35, bf16[512,512]{1,0:T(8,128)(2,1)S(1)} %maximum_select_fusion.own_hbm, bf16[512,512]{1,0:T(8,128)(2,1)S(1)} %collective-permute-done.7.sib_hbm, bf16[512,512]{1,0:T(8,128)(2,1)S(1)} %collective-permute-done.9.rim_hbm, ...), custom_call_target="tpu_custom_call" | custom-call | flops 8589934592 | bytes 2621440 | tf_op jit(solution)/shard_map/graph_layer/pallas_call | solution.py:266
  54.5 0.1 collective-permute-start.14
  54.6 0.5 collective-permute-start.16
  55.1 3.6 %collective-permute-start.17 = (bf16[512,512]{1,0:T(8,128)(2,1)S(1)}, bf16[512,512]{1,0:T(8,128)(2,1)S(1)}, u32[]{:S(2)}, u32[]{:S(2)}) collective-permute-start(bf16[512,512]{1,0:T(8,128)(2,1)S(1)} %graph_layer.4.own_hbm), channel_id=1, source_target_pairs={{1,4},{0,13},{5,8},{4,1},{9,12},{8,5},{13,0},{12,9},{3,6},{2,15},{... | collective-permute-start | bytes 1572872 | tf_op jit(solution)/shard_map/ppermute | solution.py:337
  58.8 7.6 %graph_layer.5.own_hbm = bf16[512,512]{1,0:T(8,128)(2,1)S(1)} custom-call(s32[1]{0:T(128)} %bitcast.5.core_ref, s32[4096]{0:T(1024)S(1)} %bitcast.33, bf16[512,512]{1,0:T(8,128)(2,1)S(1)} %maximum_select_fusion.1.own_hbm, bf16[512,512]{1,0:T(8,128)(2,1)S(1)} %collective-permute-done.12.sib_hbm, bf16[512,512]{1,0:T(8,128)(2,1)S(1)} %collective-permute-done.13.rim_hbm, ...), custom_call_target="tpu_custom_call" | custom-call | flops 8589934592 | bytes 2621440 | tf_op jit(solution)/shard_map/graph_layer/pallas_call | solution.py:266
  66.4 3.3 %collective-permute-done.15.near_hbm = bf16[784,256]{1,0:T(8,128)(2,1)S(1)} collective-permute-done((bf16[784,256]{1,0:T(8,128)(2,1)S(1)}, bf16[784,256]{1,0:T(8,128)(2,1)S(1)}, u32[]{:S(2)}, u32[]{:S(2)}) %collective-permute-start.15) | collective-permute-done | bytes 401440 | tf_op jit(solution)/shard_map/ppermute | solution.py:326
  69.7 0.7 collective-permute-start.18
  70.4 2.5 %collective-permute-start.23 = (bf16[512,512]{1,0:T(8,128)(2,1)S(1)}, bf16[512,512]{1,0:T(8,128)(2,1)S(1)}, u32[]{:S(2)}, u32[]{:S(2)}) collective-permute-start(bf16[512,512]{1,0:T(8,128)(2,1)S(1)} %graph_layer.5.own_hbm), channel_id=1, source_target_pairs={{1,4},{5,8},{4,1},{9,12},{8,5},{12,9},{3,6},{7,10},{6,3},{11,14},{... | collective-permute-start | bytes 1572872 | tf_op jit(solution)/shard_map/ppermute | solution.py:337
  72.9 0.1 collective-permute-start.19
  73.0 7.7 %graph_layer.6 = (bf16[512,256]{1,0:T(8,128)(2,1)S(1)}, bf16[512,256]{1,0:T(8,128)(2,1)S(1)}) custom-call(s32[1]{0:T(128)} %bitcast.5.core_ref, s32[4096]{0:T(1024)S(1)} %bitcast.36, bf16[512,512]{1,0:T(8,128)(2,1)S(1)} %graph_layer.4.own_hbm, bf16[512,512]{1,0:T(8,128)(2,1)S(1)} %collective-permute-done.16.sib_hbm, ...), custom_call_target="tpu_custom_call" | custom-call | flops 8589934592 | bytes 2621440 | tf_op jit(solution)/shard_map/graph_layer/pallas_call | solution.py:266
  80.7 2.4 %collective-permute-done.19.near_hbm = bf16[784,256]{1,0:T(8,128)(2,1)S(1)} collective-permute-done((bf16[784,256]{1,0:T(8,128)(2,1)S(1)}, bf16[784,256]{1,0:T(8,128)(2,1)S(1)}, u32[]{:S(2)}, u32[]{:S(2)}) %collective-permute-start.19) | collective-permute-done | bytes 401440 | tf_op jit(solution)/shard_map/ppermute | solution.py:326
  83.2 2.3 %collective-permute-start.20 = (bf16[512,256]{1,0:T(8,128)(2,1)S(1)}, bf16[512,256]{1,0:T(8,128)(2,1)S(1)}, u32[]{:S(2)}, u32[]{:S(2)}) collective-permute-start(bf16[512,256]{1,0:T(8,128)(2,1)S(1)} %get-tuple-element.95), channel_id=1, source_target_pairs={{0,0},{1,2},{2,1},{3,3},{4,4},{5,6},{6,5},{7,7},{8,8},{9,10},{10,9... | collective-permute-start | bytes 786440 | tf_op jit(solution)/shard_map/ppermute | solution.py:316
  85.6 7.7 %graph_layer.7 = (bf16[512,256]{1,0:T(8,128)(2,1)S(1)}, bf16[512,256]{1,0:T(8,128)(2,1)S(1)}) custom-call(s32[1]{0:T(128)} %bitcast.5.core_ref, s32[4096]{0:T(1024)S(1)} %bitcast.34, bf16[512,512]{1,0:T(8,128)(2,1)S(1)} %graph_layer.5.own_hbm, bf16[512,512]{1,0:T(8,128)(2,1)S(1)} %collective-permute-done.22.sib_hbm, ...), custom_call_target="tpu_custom_call" | custom-call | flops 8589934592 | bytes 2621440 | tf_op jit(solution)/shard_map/graph_layer/pallas_call | solution.py:266
  93.3 3.2 %collective-permute-start.25 = (bf16[512,256]{1,0:T(8,128)(2,1)S(1)}, bf16[512,256]{1,0:T(8,128)(2,1)S(1)}, u32[]{:S(2)}, u32[]{:S(2)}) collective-permute-start(bf16[512,256]{1,0:T(8,128)(2,1)S(1)} %get-tuple-element.100), channel_id=1, source_target_pairs={{0,0},{1,2},{2,1},{3,3},{4,4},{5,6},{6,5},{7,7},{8,8},{9,10},{10,9... | collective-permute-start | bytes 786440 | tf_op jit(solution)/shard_map/ppermute | solution.py:316
  96.6 1.0 maximum_select_fusion.2
  97.6 5.4 %collective-permute-done.25 = bf16[512,256]{1,0:T(8,128)(2,1)S(1)} collective-permute-done((bf16[512,256]{1,0:T(8,128)(2,1)S(1)}, bf16[512,256]{1,0:T(8,128)(2,1)S(1)}, u32[]{:S(2)}, u32[]{:S(2)}) %collective-permute-start.25) | collective-permute-done | bytes 262176 | tf_op jit(solution)/shard_map/ppermute | solution.py:316
  103.0 0.8 collective-permute-done.26
  103.8 1.0 maximum_select_fusion.3
  (69 shorter events, 0.4 us)
Async XLA Ops:
  0.6 0.7 copy-start.21
  0.6 0.7 copy-start.20
  0.7 0.7 copy-start.19
  1.4 12.8 %copy-start.17 = (s32[1024]{0:T(1024)S(1)}, s32[1024]{0:T(1024)}, u32[]{:S(2)}) copy-start(s32[1024]{0:T(1024)} %param.20) | copy-start | bytes 12292
  1.4 12.8 %copy-start.18 = (s32[1024]{0:T(1024)S(1)}, s32[1024]{0:T(1024)}, u32[]{:S(2)}) copy-start(s32[1024]{0:T(1024)} %param.22) | copy-start | bytes 12292
  1.4 1.1 %copy-start = (bf16[1,1024,256]{2,1,0:T(8,128)(2,1)S(1)}, bf16[1,1024,256]{2,1,0:T(8,128)(2,1)}, u32[]{:S(2)}) copy-start(bf16[1,1024,256]{2,1,0:T(8,128)(2,1)} %param.17) | copy-start | bytes 1572868
  2.4 2.3 %copy-start.1 = (bf16[1,1024,256]{2,1,0:T(8,128)(2,1)S(1)}, bf16[1,1024,256]{2,1,0:T(8,128)(2,1)}, u32[]{:S(2)}) copy-start(bf16[1,1024,256]{2,1,0:T(8,128)(2,1)} %param.17) | copy-start | bytes 1572868
  2.4 11.8 %copy-start.16 = (s32[1024,8]{0,1:T(8,128)S(1)}, s32[1024,8]{0,1:T(8,128)}, u32[]{:S(2)}) copy-start(s32[1024,8]{0,1:T(8,128)} %param.19) | copy-start | bytes 98308
  4.7 9.7 %copy-start.3 = (bf16[2,512,256]{2,1,0:T(8,128)(2,1)S(1)}, bf16[2,512,256]{2,1,0:T(8,128)(2,1)}, u32[]{:S(2)}) copy-start(bf16[2,512,256]{2,1,0:T(8,128)(2,1)} %ws_hbm.6) | copy-start | bytes 1572868
  4.7 9.7 %copy-start.4 = (bf16[2,512,256]{2,1,0:T(8,128)(2,1)S(1)}, bf16[2,512,256]{2,1,0:T(8,128)(2,1)}, u32[]{:S(2)}) copy-start(bf16[2,512,256]{2,1,0:T(8,128)(2,1)} %wd_hbm.6) | copy-start | bytes 1572868
  4.8 9.5 %copy-start.15 = (s32[1024,8]{0,1:T(8,128)S(1)}, s32[1024,8]{0,1:T(8,128)}, u32[]{:S(2)}) copy-start(s32[1024,8]{0,1:T(8,128)} %param.21) | copy-start | bytes 98308
  4.8 18.2 %collective-permute-start = (bf16[512,256]{1,0:T(8,128)(2,1)S(1)}, bf16[512,256]{1,0:T(8,128)(2,1)S(1)}, u32[]{:S(2)}, u32[]{:S(2)}) collective-permute-start(bf16[512,256]{1,0:T(8,128)(2,1)S(1)} %get-tuple-element.55), channel_id=1, source_target_pairs={{0,0},{1,2},{2,1},{3,3},{4,4},{5,6},{6,5},{7,7},{8,8},{9,10},{10,9... | collective-permute-start | bytes 786440 | tf_op jit(solution)/shard_map/ppermute | solution.py:310
  9.4 13.5 %collective-permute-start.1 = (bf16[512,256]{1,0:T(8,128)(2,1)S(1)}, bf16[512,256]{1,0:T(8,128)(2,1)S(1)}, u32[]{:S(2)}, u32[]{:S(2)}) collective-permute-start(bf16[512,256]{1,0:T(8,128)(2,1)S(1)} %get-tuple-element.56), channel_id=1, source_target_pairs={{0,1},{1,3},{2,0},{3,2},{4,5},{5,7},{6,4},{7,6},{8,9},{9,11},{10,8... | collective-permute-start | bytes 786440 | tf_op jit(solution)/shard_map/ppermute | solution.py:311
  9.5 11.2 %collective-permute-start.2 = (bf16[272,256]{1,0:T(8,128)(2,1)S(1)}, bf16[272,256]{1,0:T(8,128)(2,1)S(1)}, u32[]{:S(2)}, u32[]{:S(2)}) collective-permute-start(bf16[272,256]{1,0:T(8,128)(2,1)S(1)} %get-tuple-element.59), channel_id=1, source_target_pairs={{0,4},{4,8},{8,12},{12,0},{1,5},{5,9},{9,13},{13,1},{2,6},{6,10},{... | collective-permute-start | bytes 417800 | tf_op jit(solution)/shard_map/ppermute | solution.py:396
  10.8 12.1 %collective-permute-start.3 = (bf16[272,256]{1,0:T(8,128)(2,1)S(1)}, bf16[272,256]{1,0:T(8,128)(2,1)S(1)}, u32[]{:S(2)}, u32[]{:S(2)}) collective-permute-start(bf16[272,256]{1,0:T(8,128)(2,1)S(1)} %get-tuple-element.60), channel_id=1, source_target_pairs={{0,8},{4,12},{8,0},{12,4},{1,9},{5,13},{9,1},{13,5},{2,10},{6,14},... | collective-permute-start | bytes 417800 | tf_op jit(solution)/shard_map/ppermute | solution.py:396
  13.1 9.8 %collective-permute-start.4 = (bf16[272,256]{1,0:T(8,128)(2,1)S(1)}, bf16[272,256]{1,0:T(8,128)(2,1)S(1)}, u32[]{:S(2)}, u32[]{:S(2)}) collective-permute-start(bf16[272,256]{1,0:T(8,128)(2,1)S(1)} %get-tuple-element.61), channel_id=1, source_target_pairs={{0,12},{4,0},{8,4},{12,8},{1,13},{5,1},{9,5},{13,9},{2,14},{6,2},{... | collective-permute-start | bytes 417800 | tf_op jit(solution)/shard_map/ppermute | solution.py:396
  14.3 0.7 copy-start.14
  15.0 1.0 copy-start.5
  16.0 1.0 copy-start.7
  17.1 1.0 copy-start.9
  18.1 1.0 copy-start.11
  22.9 1.0 copy-start.2
  23.1 15.4 %collective-permute-start.7 = (bf16[512,512]{1,0:T(8,128)(2,1)S(1)}, bf16[512,512]{1,0:T(8,128)(2,1)S(1)}, u32[]{:S(2)}, u32[]{:S(2)}) collective-permute-start(bf16[512,512]{1,0:T(8,128)(2,1)S(1)} %maximum_select_fusion.own_hbm), channel_id=1, source_target_pairs={{0,1},{1,0},{2,3},{3,2},{4,5},{5,4},{6,7},{7,6},{8,9},{9,8},{10,11... | collective-permute-start | bytes 1572872 | tf_op jit(solution)/shard_map/ppermute | solution.py:326
  23.7 10.9 %collective-permute-start.8 = (bf16[784,256]{1,0:T(8,128)(2,1)S(1)}, bf16[784,256]{1,0:T(8,128)(2,1)S(1)}, u32[]{:S(2)}, u32[]{:S(2)}) collective-permute-start(bf16[784,256]{1,0:T(8,128)(2,1)S(1)} %get-tuple-element.70), channel_id=1, source_target_pairs={{0,2},{2,0},{1,3},{3,1},{4,6},{6,4},{5,7},{7,5},{8,10},{10,8},{9,1... | collective-permute-start | bytes 1204232 | tf_op jit(solution)/shard_map/ppermute | solution.py:326
  24.7 13.2 %collective-permute-start.5 = (bf16[512,256]{1,0:T(8,128)(2,1)S(1)}, bf16[512,256]{1,0:T(8,128)(2,1)S(1)}, u32[]{:S(2)}, u32[]{:S(2)}) collective-permute-start(bf16[512,256]{1,0:T(8,128)(2,1)S(1)} %get-tuple-element.66), channel_id=1, source_target_pairs={{0,0},{1,2},{2,1},{3,3},{4,4},{5,6},{6,5},{7,7},{8,8},{9,10},{10,9... | collective-permute-start | bytes 786440 | tf_op jit(solution)/shard_map/ppermute | solution.py:310
  28.1 18.8 %copy-start.6 = (bf16[2,256,512]{2,1,0:T(8,128)(2,1)S(1)}, bf16[2,256,512]{2,1,0:T(8,128)(2,1)}, u32[]{:S(2)}) copy-start(bf16[2,256,512]{2,1,0:T(8,128)(2,1)} %w2_hbm.6) | copy-start | bytes 1572868
  28.1 10.4 %collective-permute-start.6 = (bf16[512,256]{1,0:T(8,128)(2,1)S(1)}, bf16[512,256]{1,0:T(8,128)(2,1)S(1)}, u32[]{:S(2)}, u32[]{:S(2)}) collective-permute-start(bf16[512,256]{1,0:T(8,128)(2,1)S(1)} %get-tuple-element.67), channel_id=1, source_target_pairs={{0,1},{1,3},{2,0},{3,2},{4,5},{5,7},{6,4},{7,6},{8,9},{9,11},{10,8... | collective-permute-start | bytes 786440 | tf_op jit(solution)/shard_map/ppermute | solution.py:311
  28.1 18.7 %collective-permute-start.9 = (bf16[512,512]{1,0:T(8,128)(2,1)S(1)}, bf16[512,512]{1,0:T(8,128)(2,1)S(1)}, u32[]{:S(2)}, u32[]{:S(2)}) collective-permute-start(bf16[512,512]{1,0:T(8,128)(2,1)S(1)} %maximum_select_fusion.own_hbm), channel_id=1, source_target_pairs={{1,4},{0,13},{5,8},{4,1},{9,12},{8,5},{13,0},{12,9},{3,6},{2,15},{... | collective-permute-start | bytes 1572872 | tf_op jit(solution)/shard_map/ppermute | solution.py:337
  38.5 8.3 %collective-permute-start.10 = (bf16[784,256]{1,0:T(8,128)(2,1)S(1)}, bf16[784,256]{1,0:T(8,128)(2,1)S(1)}, u32[]{:S(2)}, u32[]{:S(2)}) collective-permute-start(bf16[784,256]{1,0:T(8,128)(2,1)S(1)} %collective-permute-done.8.near_hbm), channel_id=1, source_target_pairs={{0,1},{1,0},{2,3},{3,2},{4,5},{5,4},{6,7},{7,6},{8,9},{9,8},{10,11... | collective-permute-start | bytes 1204232 | tf_op jit(solution)/shard_map/ppermute | solution.py:326
  41.2 17.5 %copy-start.8 = (bf16[2,512,256]{2,1,0:T(8,128)(2,1)S(1)}, bf16[2,512,256]{2,1,0:T(8,128)(2,1)}, u32[]{:S(2)}) copy-start(bf16[2,512,256]{2,1,0:T(8,128)(2,1)} %ws_hbm.7) | copy-start | bytes 1572868
  41.2 17.5 %copy-start.10 = (bf16[2,512,256]{2,1,0:T(8,128)(2,1)S(1)}, bf16[2,512,256]{2,1,0:T(8,128)(2,1)}, u32[]{:S(2)}) copy-start(bf16[2,512,256]{2,1,0:T(8,128)(2,1)} %wd_hbm.7) | copy-start | bytes 1572868
  41.2 17.5 %copy-start.12 = (bf16[2,256,512]{2,1,0:T(8,128)(2,1)S(1)}, bf16[2,256,512]{2,1,0:T(8,128)(2,1)}, u32[]{:S(2)}) copy-start(bf16[2,256,512]{2,1,0:T(8,128)(2,1)} %w2_hbm.7) | copy-start | bytes 1572868
  41.2 17.5 %collective-permute-start.12 = (bf16[512,512]{1,0:T(8,128)(2,1)S(1)}, bf16[512,512]{1,0:T(8,128)(2,1)S(1)}, u32[]{:S(2)}, u32[]{:S(2)}) collective-permute-start(bf16[512,512]{1,0:T(8,128)(2,1)S(1)} %maximum_select_fusion.1.own_hbm), channel_id=1, source_target_pairs={{0,1},{1,0},{2,3},{3,2},{4,5},{5,4},{6,7},{7,6},{8,9},{9,8},{10,11... | collective-permute-start | bytes 1572872 | tf_op jit(solution)/shard_map/ppermute | solution.py:326
  41.3 17.4 %collective-permute-start.13 = (bf16[512,512]{1,0:T(8,128)(2,1)S(1)}, bf16[512,512]{1,0:T(8,128)(2,1)S(1)}, u32[]{:S(2)}, u32[]{:S(2)}) collective-permute-start(bf16[512,512]{1,0:T(8,128)(2,1)S(1)} %maximum_select_fusion.1.own_hbm), channel_id=1, source_target_pairs={{1,4},{5,8},{4,1},{9,12},{8,5},{12,9},{3,6},{7,10},{6,3},{11,14},{... | collective-permute-start | bytes 1572872 | tf_op jit(solution)/shard_map/ppermute | solution.py:337
  46.8 7.8 %collective-permute-start.11 = (bf16[784,256]{1,0:T(8,128)(2,1)S(1)}, bf16[784,256]{1,0:T(8,128)(2,1)S(1)}, u32[]{:S(2)}, u32[]{:S(2)}) collective-permute-start(bf16[784,256]{1,0:T(8,128)(2,1)S(1)} %get-tuple-element.79), channel_id=1, source_target_pairs={{0,2},{2,0},{1,3},{3,1},{4,6},{6,4},{5,7},{7,5},{8,10},{10,8},{9,1... | collective-permute-start | bytes 1204232 | tf_op jit(solution)/shard_map/ppermute | solution.py:326
  54.5 4.2 %collective-permute-start.14 = (bf16[784,256]{1,0:T(8,128)(2,1)S(1)}, bf16[784,256]{1,0:T(8,128)(2,1)S(1)}, u32[]{:S(2)}, u32[]{:S(2)}) collective-permute-start(bf16[784,256]{1,0:T(8,128)(2,1)S(1)} %collective-permute-done.11.near_hbm), channel_id=1, source_target_pairs={{0,1},{1,0},{2,3},{3,2},{4,5},{5,4},{6,7},{7,6},{8,9},{9,8},{10,11... | collective-permute-start | bytes 1204232 | tf_op jit(solution)/shard_map/ppermute | solution.py:326
  54.6 18.3 %collective-permute-start.16 = (bf16[512,512]{1,0:T(8,128)(2,1)S(1)}, bf16[512,512]{1,0:T(8,128)(2,1)S(1)}, u32[]{:S(2)}, u32[]{:S(2)}) collective-permute-start(bf16[512,512]{1,0:T(8,128)(2,1)S(1)} %graph_layer.4.own_hbm), channel_id=1, source_target_pairs={{0,1},{1,0},{2,3},{3,2},{4,5},{5,4},{6,7},{7,6},{8,9},{9,8},{10,11... | collective-permute-start | bytes 1572872 | tf_op jit(solution)/shard_map/ppermute | solution.py:326
  55.1 17.9 %collective-permute-start.17 = (bf16[512,512]{1,0:T(8,128)(2,1)S(1)}, bf16[512,512]{1,0:T(8,128)(2,1)S(1)}, u32[]{:S(2)}, u32[]{:S(2)}) collective-permute-start(bf16[512,512]{1,0:T(8,128)(2,1)S(1)} %graph_layer.4.own_hbm), channel_id=1, source_target_pairs={{1,4},{0,13},{5,8},{4,1},{9,12},{8,5},{13,0},{12,9},{3,6},{2,15},{... | collective-permute-start | bytes 1572872 | tf_op jit(solution)/shard_map/ppermute | solution.py:337
  58.7 11.0 %collective-permute-start.15 = (bf16[784,256]{1,0:T(8,128)(2,1)S(1)}, bf16[784,256]{1,0:T(8,128)(2,1)S(1)}, u32[]{:S(2)}, u32[]{:S(2)}) collective-permute-start(bf16[784,256]{1,0:T(8,128)(2,1)S(1)} %get-tuple-element.86), channel_id=1, source_target_pairs={{0,2},{2,0},{1,3},{3,1},{4,6},{6,4},{5,7},{7,5},{8,10},{10,8},{9,1... | collective-permute-start | bytes 1204232 | tf_op jit(solution)/shard_map/ppermute | solution.py:326
  69.7 3.3 %collective-permute-start.18 = (bf16[784,256]{1,0:T(8,128)(2,1)S(1)}, bf16[784,256]{1,0:T(8,128)(2,1)S(1)}, u32[]{:S(2)}, u32[]{:S(2)}) collective-permute-start(bf16[784,256]{1,0:T(8,128)(2,1)S(1)} %collective-permute-done.15.near_hbm), channel_id=1, source_target_pairs={{0,1},{1,0},{2,3},{3,2},{4,5},{5,4},{6,7},{7,6},{8,9},{9,8},{10,11... | collective-permute-start | bytes 1204232 | tf_op jit(solution)/shard_map/ppermute | solution.py:326
  70.4 15.1 %collective-permute-start.22 = (bf16[512,512]{1,0:T(8,128)(2,1)S(1)}, bf16[512,512]{1,0:T(8,128)(2,1)S(1)}, u32[]{:S(2)}, u32[]{:S(2)}) collective-permute-start(bf16[512,512]{1,0:T(8,128)(2,1)S(1)} %graph_layer.5.own_hbm), channel_id=1, source_target_pairs={{0,1},{1,0},{2,3},{3,2},{4,5},{5,4},{6,7},{7,6},{8,9},{9,8},{10,11... | collective-permute-start | bytes 1572872 | tf_op jit(solution)/shard_map/ppermute | solution.py:326
  70.4 15.1 %collective-permute-start.23 = (bf16[512,512]{1,0:T(8,128)(2,1)S(1)}, bf16[512,512]{1,0:T(8,128)(2,1)S(1)}, u32[]{:S(2)}, u32[]{:S(2)}) collective-permute-start(bf16[512,512]{1,0:T(8,128)(2,1)S(1)} %graph_layer.5.own_hbm), channel_id=1, source_target_pairs={{1,4},{5,8},{4,1},{9,12},{8,5},{12,9},{3,6},{7,10},{6,3},{11,14},{... | collective-permute-start | bytes 1572872 | tf_op jit(solution)/shard_map/ppermute | solution.py:337
  72.9 10.3 %collective-permute-start.19 = (bf16[784,256]{1,0:T(8,128)(2,1)S(1)}, bf16[784,256]{1,0:T(8,128)(2,1)S(1)}, u32[]{:S(2)}, u32[]{:S(2)}) collective-permute-start(bf16[784,256]{1,0:T(8,128)(2,1)S(1)} %get-tuple-element.94), channel_id=1, source_target_pairs={{0,2},{2,0},{1,3},{3,1},{4,6},{6,4},{5,7},{7,5},{8,10},{10,8},{9,1... | collective-permute-start | bytes 1204232 | tf_op jit(solution)/shard_map/ppermute | solution.py:326
  83.2 2.4 %collective-permute-start.24 = (bf16[784,256]{1,0:T(8,128)(2,1)S(1)}, bf16[784,256]{1,0:T(8,128)(2,1)S(1)}, u32[]{:S(2)}, u32[]{:S(2)}) collective-permute-start(bf16[784,256]{1,0:T(8,128)(2,1)S(1)} %collective-permute-done.19.near_hbm), channel_id=1, source_target_pairs={{0,1},{1,0},{2,3},{3,2},{4,5},{5,4},{6,7},{7,6},{8,9},{9,8},{10,11... | collective-permute-start | bytes 1204232 | tf_op jit(solution)/shard_map/ppermute | solution.py:326
  83.2 13.4 %collective-permute-start.20 = (bf16[512,256]{1,0:T(8,128)(2,1)S(1)}, bf16[512,256]{1,0:T(8,128)(2,1)S(1)}, u32[]{:S(2)}, u32[]{:S(2)}) collective-permute-start(bf16[512,256]{1,0:T(8,128)(2,1)S(1)} %get-tuple-element.95), channel_id=1, source_target_pairs={{0,0},{1,2},{2,1},{3,3},{4,4},{5,6},{6,5},{7,7},{8,8},{9,10},{10,9... | collective-permute-start | bytes 786440 | tf_op jit(solution)/shard_map/ppermute | solution.py:316
  85.5 11.1 %collective-permute-start.21 = (bf16[512,256]{1,0:T(8,128)(2,1)S(1)}, bf16[512,256]{1,0:T(8,128)(2,1)S(1)}, u32[]{:S(2)}, u32[]{:S(2)}) collective-permute-start(bf16[512,256]{1,0:T(8,128)(2,1)S(1)} %get-tuple-element.96), channel_id=1, source_target_pairs={{0,2},{1,0},{2,3},{3,1},{4,6},{5,4},{6,7},{7,5},{8,10},{9,8},{10,1... | collective-permute-start | bytes 786440 | tf_op jit(solution)/shard_map/ppermute | solution.py:317
  93.3 9.7 %collective-permute-start.25 = (bf16[512,256]{1,0:T(8,128)(2,1)S(1)}, bf16[512,256]{1,0:T(8,128)(2,1)S(1)}, u32[]{:S(2)}, u32[]{:S(2)}) collective-permute-start(bf16[512,256]{1,0:T(8,128)(2,1)S(1)} %get-tuple-element.100), channel_id=1, source_target_pairs={{0,0},{1,2},{2,1},{3,3},{4,4},{5,6},{6,5},{7,7},{8,8},{9,10},{10,9... | collective-permute-start | bytes 786440 | tf_op jit(solution)/shard_map/ppermute | solution.py:316
  96.5 7.2 %collective-permute-start.26 = (bf16[512,256]{1,0:T(8,128)(2,1)S(1)}, bf16[512,256]{1,0:T(8,128)(2,1)S(1)}, u32[]{:S(2)}, u32[]{:S(2)}) collective-permute-start(bf16[512,256]{1,0:T(8,128)(2,1)S(1)} %get-tuple-element.101), channel_id=1, source_target_pairs={{0,2},{1,0},{2,3},{3,1},{4,6},{5,4},{6,7},{7,5},{8,10},{9,8},{10,1... | collective-permute-start | bytes 786440 | tf_op jit(solution)/shard_map/ppermute | solution.py:317
  (1 other events, 0.7 us)

commit v5 on v4

--- a/solution.py
+++ b/solution.py
@@ -154,38 +154,22 @@
 
 
 def layer_kernel(
-    layer, slots, last, core_ref, idx_ref, own_hbm, sib_hbm, rim_hbm, ws_hbm, wd_hbm, w2_hbm, b_hbm, near_hbm, far_hbm,
-    *refs,
+    layer, slots, last, core_ref, idx_ref, own, sib, rim, bias, near_w, far_w, ws_hbm, wd_hbm, w2_hbm, *refs
 ):
     outs, refs = (refs[:2], refs[2:]) if last else (refs[:1], refs[1:])
-    own, sib, rim, ws, wd, w2, bias, near_w, far_w, ws_x, wd_x, w2_x, proj, near, summed, sems = refs
+    ws, wd, w2, ws_x, wd_x, w2_x, proj, near, summed, sems = refs
     rows, width = own.shape
     share = width // 2
     chunks = width // LANES
+    part = chunks // 2
     core = core_ref[0]
-    pairs = (
-        (own_hbm, own), (wd_hbm.at[layer], wd), (ws_hbm.at[layer], ws), (b_hbm, bias),
-        (near_hbm, near_w), (far_hbm, far_w), (sib_hbm, sib), (rim_hbm, rim), (w2_hbm.at[layer], w2),
-    )
-    copies = [pltpu.make_async_copy(src, dst, sems.at[i]) for i, (src, dst) in enumerate(pairs)]
+    pairs = ((wd_hbm, wd), (ws_hbm, ws), (w2_hbm, w2))
+    copies = [pltpu.make_async_copy(src.at[layer], dst, sems.at[i]) for i, (src, dst) in enumerate(pairs)]
     for copy in copies:
         copy.start()
     window = 3 * rows
     proj[0:8, :] = jnp.full((8, LANES), DEAD, jnp.float32)
     proj[4 * window + 4:4 * window + 16, :] = jnp.full((12, LANES), DEAD, jnp.float32)
-
-    def put(dst, base, first, values):
-        for c in range(values.shape[1] // LANES):
-            dst[pl.ds(base * chunks + first + c, rows, stride=chunks), :] = values[:, c * LANES:(c + 1) * LANES]
-
-    for i in (0, 1, 2, 3):
-        copies[i].wait()
-    part = share // LANES
-    b_own = bias[layer:layer + 1, :].astype(jnp.float32)
-    put(near, 0, 0, (jnp.dot(own[...], wd[...], preferred_element_type=jnp.float32) + b_own) * 0.5)
-    put(proj, 1, 0, jnp.dot(own[...], ws[...], preferred_element_type=jnp.float32) * 0.5)
-    for i in (4, 5):
-        copies[i].wait()
     here, there = pl.multiple_of(core * share, 16), pl.multiple_of((1 - core) * share, 16)
     for spot, piece in ((here, near_w), (there, far_w)):
         ws_x[pl.ds(spot, share), :] = piece[0:share, :]
@@ -201,13 +185,24 @@
         w2_x[:, share:] = near_w[2 * share:3 * share, :]
         w2_x[:, :share] = far_w[2 * share:3 * share, :]
 
+    def put(dst, base, first, values):
+        for c in range(values.shape[1] // LANES):
+            dst[pl.ds(base * chunks + first + c, rows, stride=chunks), :] = values[:, c * LANES:(c + 1) * LANES] * 0.5
+
+    def product(values, weights):
+        return jnp.dot(values[...], weights[...], preferred_element_type=jnp.float32)
+
+    b_own = bias[layer:layer + 1, :].astype(jnp.float32)
     b_other = near_w[3 * share:3 * share + 1, :].astype(jnp.float32)
-    put(near, 0, part, (jnp.dot(own[...], wd_x[...], preferred_element_type=jnp.float32) + b_other) * 0.5)
-    put(proj, 1, part, jnp.dot(own[...], ws_x[...], preferred_element_type=jnp.float32) * 0.5)
-    for i, ref, base in ((6, sib, rows + 1), (7, rim, 2 * rows + 1)):
-        copies[i].wait()
-        put(proj, base, 0, jnp.dot(ref[...], ws[...], preferred_element_type=jnp.float32) * 0.5)
-        put(proj, base, part, jnp.dot(ref[...], ws_x[...], preferred_element_type=jnp.float32) * 0.5)
+    put(near, 0, part, product(own, wd_x) + b_other)
+    put(proj, 1, part, product(own, ws_x))
+    copies[0].wait()
+    copies[1].wait()
+    put(near, 0, 0, product(own, wd) + b_own)
+    put(proj, 1, 0, product(own, ws))
+    for ref, base in ((sib, rows + 1), (rim, 2 * rows + 1)):
+        put(proj, base, 0, product(ref, ws))
+        put(proj, base, part, product(ref, ws_x))
     low = lax.broadcasted_iota(jnp.int32, (8, LANES), 0) < chunks
 
     def nodes(q, carry):
@@ -223,17 +218,10 @@
         summed[spot, :] = total
         return carry
 
-    lax.fori_loop(0, rows // 2, nodes, 0, unroll=8)
-    copies[8].wait()
-    update = None
-    for c in range(chunks):
-        values = summed[pl.ds(c, rows, stride=chunks), :].astype(jnp.bfloat16)
-        if c < part:
-            w_rows = w2[c * LANES:(c + 1) * LANES, :]
-        else:
-            w_rows = w2_x[(c - part) * LANES:(c - part + 1) * LANES, :]
-        term = jnp.dot(values, w_rows, preferred_element_type=jnp.float32)
-        update = term if update is None else update + term
+    lax.fori_loop(0, rows // 2, nodes, 0, unroll=16)
+    copies[2].wait()
+    sums = [summed[pl.ds(c, rows, stride=chunks), :].astype(jnp.bfloat16) for c in range(chunks)]
+    update = product(jnp.concatenate(sums[:part], 1), w2) + product(jnp.concatenate(sums[part:], 1), w2_x)
     result = (own[...].astype(jnp.float32) + update).astype(jnp.bfloat16)
     if not last:
         outs[0][...] = result
@@ -253,7 +241,6 @@
     rows, width = own.shape
     share = width // 2
     chunks = width // LANES
-    anywhere = pl.BlockSpec(memory_space=pl.ANY)
     smem = pl.BlockSpec(memory_space=pltpu.SMEM)
     vmem = pl.BlockSpec(memory_space=pltpu.VMEM)
     bf16, f32 = jnp.bfloat16, jnp.float32
@@ -262,34 +249,27 @@
         out_specs = (vmem, vmem)
     else:
         out_shape, out_specs = jax.ShapeDtypeStruct((rows, width), bf16), vmem
-    edges = rows * slots
     return pl.pallas_call(
         functools.partial(layer_kernel, layer, slots, last),
         out_shape=out_shape,
-        in_specs=[smem, smem] + [anywhere] * 3 + [pl.BlockSpec(memory_space=pltpu.HBM)] * 3 + [anywhere] * 3,
+        in_specs=[smem] * 2 + [vmem] * 6 + [pl.BlockSpec(memory_space=pl.ANY)] * 3,
         out_specs=out_specs,
         scratch_shapes=[
-            pltpu.VMEM((rows, width), bf16),
-            pltpu.VMEM((rows, width), bf16),
-            pltpu.VMEM((rows, width), bf16),
             pltpu.VMEM((width, share), bf16),
             pltpu.VMEM((width, share), bf16),
             pltpu.VMEM((share, width), bf16),
-            pltpu.VMEM(bias.shape, bf16),
-            pltpu.VMEM(near_w.shape, bf16),
-            pltpu.VMEM(far_w.shape, bf16),
             pltpu.VMEM((width, share), bf16),
             pltpu.VMEM((width, share), bf16),
             pltpu.VMEM((share, width), bf16),
             pltpu.VMEM((3 * rows * chunks + 96, LANES), f32),
             pltpu.VMEM((rows * chunks, LANES), f32),
             pltpu.VMEM((rows * chunks, LANES), f32),
-            pltpu.SemaphoreType.DMA((9,)),
+            pltpu.SemaphoreType.DMA((3,)),
         ],
         compiler_params=pltpu.CompilerParams(vmem_limit_bytes=32 << 20),
         cost_estimate=pl.CostEstimate(flops=64 * rows * width * width, bytes_accessed=10 * rows * width, transcendentals=0),
         name="graph_layer",
-    )(core, idx, own, sib, rim, ws, wd, w2, bias, near_w, far_w)
+    )(core, idx, own, sib, rim, bias, near_w, far_w, ws, wd, w2)
 
 
 def edge_offsets(nbrs, counts, core):
@@ -365,7 +345,7 @@
         in_specs=[pl.BlockSpec(memory_space=pltpu.SMEM)] + [vmem] * 2 + [hbm] * 6,
         out_specs=(vmem,) * len(order),
         scratch_shapes=[pltpu.SemaphoreType.DMA((3 * len(order),))],
-        compiler_params=pltpu.CompilerParams(vmem_limit_bytes=32 << 20),
+        compiler_params=pltpu.CompilerParams(vmem_limit_bytes=60 << 20),
         cost_estimate=SMALL,
         name="pack_weights",
     )(core, g_bias, r_bias, *g_weights, *r_weights)

time: 106 us -> 104 us (0.981)
  waiting for transfers between devices: 21 us -> 27.2 us
  local copies, waits for them, and re-layouts: 6.85 us -> 2.17 us
  Pallas kernels: 35.1 us -> 31.5 us
    pallas_call x4, Pallas kernels: 30.7 us -> 25.2 us  [run_layer(): pl.pallas_call(functools.partial(layer_kernel, layer, slots, last), out_s...]
    unnamed x47, local copies, waits for them, and re-layouts: 6.8 us -> 2.12 us
    ppermute x3, waiting for transfers between devices: 2.24 us -> 5.16 us  [by_rows(): lax.ppermute(pieces[k], 'mesh', [(i, (i + k) % parts) for i in range(part...]
    ppermute x12, waiting for transfers between devices: 8.71 us -> 11.3 us  [swap(): return lax.ppermute(values, axis, [(0, 1), (1, 0)])]
    pallas_call x1, Pallas kernels: 1.49 us -> 3.4 us  [pack_weights(): pl.pallas_call(functools.partial(pack_kernel, order), out_shape=(jax.Shap...]
  transfers between devices with their start and end apart: 27 -> 27, of which waited for: 8 -> 9; matrix products, arithmetic and copies ran while one was open for 1% -> 1% of each run, Pallas kernels for 31% -> 28%
where the time goes in v5:
time: 104 us
  starting transfers between devices  39.2 us (38%)
  Pallas kernels  31.5 us (30%)
  waiting for transfers between devices  27.2 us (26%)
  other arithmetic  2.42 us (2%)
  local copies, waits for them, and re-layouts  2.17 us (2%)
  between operations  1.17 us (1%)
    pallas_call x4, Pallas kernels, run_layer(): pl.pallas_call(functools.partial(layer_kernel, layer, slots, last), out_s...  25.2 us
    ppermute x4, starting transfers between devices, rims(): return lax.ppermute(own, ('mesh', 'batch'), pairs)  15.7 us
    ppermute x12, waiting for transfers between devices, swap(): return lax.ppermute(values, axis, [(0, 1), (1, 0)])  11.3 us
    ppermute x2, starting transfers between devices, spread_rows(): a = lax.ppermute(same, ('mp', 'batch'), [(0, 0), (1, 2), (2, 1), (3, 3)])  8.48 us
    ppermute x2, starting transfers between devices, gather_rows(): same = lax.ppermute(a, ('mp', 'batch'), [(0, 0), (1, 2), (2, 1), (3, 3)])  5.55 us
    ppermute x2, waiting for transfers between devices, gather_rows(): same = lax.ppermute(a, ('mp', 'batch'), [(0, 0), (1, 2), (2, 1), (3, 3)])  5.39 us
    ppermute x3, waiting for transfers between devices, by_rows(): lax.ppermute(pieces[k], 'mesh', [(i, (i + k) % parts) for i in range(part...  5.16 us
    ppermute x3, starting transfers between devices, by_rows(): lax.ppermute(pieces[k], 'mesh', [(i, (i + k) % parts) for i in range(part...  4.72 us
  transfers between devices with their start and end apart: 27, of which 9 were waited for; matrix products, arithmetic and copies ran while one was open for 1% of the time, Pallas kernels for 28%

profile of v5, /device:TPU:1, one launch (start us, length us, event | category | flops | bytes accessed | tf_op | source)
XLA Modules:
  0.0 103.7 jit_solution(9447971753590043825)
XLA Ops:
  0.7 0.7 copy-done.17
  1.4 1.0 copy-done
  2.4 2.2 %pick_rows.1 = (bf16[272,256]{1,0:T(8,128)(2,1)S(1)}, bf16[272,256]{1,0:T(8,128)(2,1)S(1)}, bf16[272,256]{1,0:T(8,128)(2,1)S(1)}, bf16[272,256]{1,0:T(8,128)(2,1)S(1)}) custom-call(s32[1]{0:T(128)} %bitcast.me_ref, s32[3,512]{1,0:T(4,128)S(1)} %pad_add_fusion.bnd_ref, bf16[1024,256]{1,0:T(8,128)(2,1)S(1)} %bitcast.30), custom_call_target="tpu_custom_call" | custom-call | flops 1 | bytes 1 | tf_op jit(solution)/shard_map/pick_rows/pallas_call | solution.py:115
  4.8 4.5 %collective-permute-start = (bf16[512,256]{1,0:T(8,128)(2,1)S(1)}, bf16[512,256]{1,0:T(8,128)(2,1)S(1)}, u32[]{:S(2)}, u32[]{:S(2)}) collective-permute-start(bf16[512,256]{1,0:T(8,128)(2,1)S(1)} %get-tuple-element.55), channel_id=1, source_target_pairs={{0,0},{1,2},{2,1},{3,3},{4,4},{5,6},{6,5},{7,7},{8,8},{9,10},{10,9... | collective-permute-start | bytes 786440 | tf_op jit(solution)/shard_map/ppermute | solution.py:290
  9.3 0.0 collective-permute-start.1
  9.3 1.3 %collective-permute-start.2 = (bf16[272,256]{1,0:T(8,128)(2,1)S(1)}, bf16[272,256]{1,0:T(8,128)(2,1)S(1)}, u32[]{:S(2)}, u32[]{:S(2)}) collective-permute-start(bf16[272,256]{1,0:T(8,128)(2,1)S(1)} %get-tuple-element.59), channel_id=1, source_target_pairs={{0,4},{4,8},{8,12},{12,0},{1,5},{5,9},{9,13},{13,1},{2,6},{6,10},{... | collective-permute-start | bytes 417800 | tf_op jit(solution)/shard_map/ppermute | solution.py:376
  10.7 2.3 %collective-permute-start.3 = (bf16[272,256]{1,0:T(8,128)(2,1)S(1)}, bf16[272,256]{1,0:T(8,128)(2,1)S(1)}, u32[]{:S(2)}, u32[]{:S(2)}) collective-permute-start(bf16[272,256]{1,0:T(8,128)(2,1)S(1)} %get-tuple-element.60), channel_id=1, source_target_pairs={{0,8},{4,12},{8,0},{12,4},{1,9},{5,13},{9,1},{13,5},{2,10},{6,14},... | collective-permute-start | bytes 417800 | tf_op jit(solution)/shard_map/ppermute | solution.py:376
  13.0 1.1 %collective-permute-start.4 = (bf16[272,256]{1,0:T(8,128)(2,1)S(1)}, bf16[272,256]{1,0:T(8,128)(2,1)S(1)}, u32[]{:S(2)}, u32[]{:S(2)}) collective-permute-start(bf16[272,256]{1,0:T(8,128)(2,1)S(1)} %get-tuple-element.61), channel_id=1, source_target_pairs={{0,12},{4,0},{8,4},{12,8},{1,13},{5,1},{9,5},{13,9},{2,14},{6,2},{... | collective-permute-start | bytes 417800 | tf_op jit(solution)/shard_map/ppermute | solution.py:376
  14.1 0.1 fusion.5
  14.2 3.4 %pack_weights.1 = (bf16[784,256]{1,0:T(8,128)(2,1)}, bf16[784,256]{1,0:T(8,128)(2,1)}, bf16[784,256]{1,0:T(8,128)(2,1)}, bf16[784,256]{1,0:T(8,128)(2,1)}) custom-call(s32[1]{0:T(128)} %bitcast.5.core_ref, bf16[2,256]{1,0:T(2,128)(2,1)} %bias.6, bf16[2,256]{1,0:T(2,128)(2,1)} %bias.7, bf16[2,512,256]{2,1,0:T(8,128)(2,1)} %ws_hbm.6, ...), custom_call_target="tpu_custom_call" | custom-call | flops 1 | bytes 1 | tf_op jit(solution)/shard_map/pack_weights/pallas_call | solution.py:342
  17.6 5.2 %collective-permute-done.3.refs_2_ = bf16[272,256]{1,0:T(8,128)(2,1)S(1)} collective-permute-done((bf16[272,256]{1,0:T(8,128)(2,1)S(1)}, bf16[272,256]{1,0:T(8,128)(2,1)S(1)}, u32[]{:S(2)}, u32[]{:S(2)}) %collective-permute-start.3) | collective-permute-done | bytes 139296 | tf_op jit(solution)/shard_map/ppermute | solution.py:376
  22.8 0.1 maximum_select_fusion.own
  23.0 0.7 collective-permute-start.7
  23.6 0.2 copy-done.21
  23.8 0.1 collective-permute-start.8
  23.9 0.1 copy-done.2
  24.0 0.7 add_force.1
  24.7 4.0 %collective-permute-start.5 = (bf16[512,256]{1,0:T(8,128)(2,1)S(1)}, bf16[512,256]{1,0:T(8,128)(2,1)S(1)}, u32[]{:S(2)}, u32[]{:S(2)}) collective-permute-start(bf16[512,256]{1,0:T(8,128)(2,1)S(1)} %get-tuple-element.66), channel_id=1, source_target_pairs={{0,0},{1,2},{2,1},{3,3},{4,4},{5,6},{6,5},{7,7},{8,8},{9,10},{10,9... | collective-permute-start | bytes 786440 | tf_op jit(solution)/shard_map/ppermute | solution.py:290
  28.7 0.0 collective-permute-start.6
  28.7 3.5 %collective-permute-start.9 = (bf16[512,512]{1,0:T(8,128)(2,1)S(1)}, bf16[512,512]{1,0:T(8,128)(2,1)S(1)}, u32[]{:S(2)}, u32[]{:S(2)}) collective-permute-start(bf16[512,512]{1,0:T(8,128)(2,1)S(1)} %maximum_select_fusion.own), channel_id=1, source_target_pairs={{1,4},{0,13},{5,8},{4,1},{9,12},{8,5},{13,0},{12,9},{3,6},{2,15},{... | collective-permute-start | bytes 1572872 | tf_op jit(solution)/shard_map/ppermute | solution.py:317
  32.3 1.8 %collective-permute-done.8.near_w = bf16[784,256]{1,0:T(8,128)(2,1)S(1)} collective-permute-done((bf16[784,256]{1,0:T(8,128)(2,1)S(1)}, bf16[784,256]{1,0:T(8,128)(2,1)S(1)}, u32[]{:S(2)}, u32[]{:S(2)}) %collective-permute-start.8) | collective-permute-done | bytes 401440 | tf_op jit(solution)/shard_map/ppermute | solution.py:306
  34.1 3.9 %collective-permute-done.5 = bf16[512,256]{1,0:T(8,128)(2,1)S(1)} collective-permute-done((bf16[512,256]{1,0:T(8,128)(2,1)S(1)}, bf16[512,256]{1,0:T(8,128)(2,1)S(1)}, u32[]{:S(2)}, u32[]{:S(2)}) %collective-permute-start.5) | collective-permute-done | bytes 262176 | tf_op jit(solution)/shard_map/ppermute | solution.py:290
  37.9 0.7 collective-permute-done.6
  38.6 2.5 %collective-permute-start.10 = (bf16[784,256]{1,0:T(8,128)(2,1)S(1)}, bf16[784,256]{1,0:T(8,128)(2,1)S(1)}, u32[]{:S(2)}, u32[]{:S(2)}) collective-permute-start(bf16[784,256]{1,0:T(8,128)(2,1)S(1)} %collective-permute-done.8.near_w), channel_id=1, source_target_pairs={{0,1},{1,0},{2,3},{3,2},{4,5},{5,4},{6,7},{7,6},{8,9},{9,8},{10,11... | collective-permute-start | bytes 1204232 | tf_op jit(solution)/shard_map/ppermute | solution.py:306
  41.1 0.1 maximum_select_fusion.1.own
  41.3 0.1 collective-permute-start.12
  41.4 5.5 %collective-permute-start.13 = (bf16[512,512]{1,0:T(8,128)(2,1)S(1)}, bf16[512,512]{1,0:T(8,128)(2,1)S(1)}, u32[]{:S(2)}, u32[]{:S(2)}) collective-permute-start(bf16[512,512]{1,0:T(8,128)(2,1)S(1)} %maximum_select_fusion.1.own), channel_id=1, source_target_pairs={{1,4},{5,8},{4,1},{9,12},{8,5},{12,9},{3,6},{7,10},{6,3},{11,14},{... | collective-permute-start | bytes 1572872 | tf_op jit(solution)/shard_map/ppermute | solution.py:317
  46.9 0.1 collective-permute-start.11
  47.1 6.3 %graph_layer.4.own = bf16[512,512]{1,0:T(8,128)(2,1)S(1)} custom-call(s32[1]{0:T(128)} %bitcast.5.core_ref, s32[4096]{0:T(1024)S(1)} %bitcast.35, bf16[512,512]{1,0:T(8,128)(2,1)S(1)} %maximum_select_fusion.own, bf16[512,512]{1,0:T(8,128)(2,1)S(1)} %collective-permute-done.7.sib, bf16[512,512]{1,0:T(8,128)(2,1)S(1)} %collective-permute-done.9.rim, ...), custom_call_target="tpu_custom_call" | custom-call | flops 8589934592 | bytes 2621440 | tf_op jit(solution)/shard_map/graph_layer/pallas_call | solution.py:252
  53.4 0.7 collective-permute-done.11.near_w
  54.1 0.5 collective-permute-start.16
  54.6 4.2 %collective-permute-start.17 = (bf16[512,512]{1,0:T(8,128)(2,1)S(1)}, bf16[512,512]{1,0:T(8,128)(2,1)S(1)}, u32[]{:S(2)}, u32[]{:S(2)}) collective-permute-start(bf16[512,512]{1,0:T(8,128)(2,1)S(1)} %graph_layer.4.own), channel_id=1, source_target_pairs={{1,4},{0,13},{5,8},{4,1},{9,12},{8,5},{13,0},{12,9},{3,6},{2,15},{... | collective-permute-start | bytes 1572872 | tf_op jit(solution)/shard_map/ppermute | solution.py:317
  58.9 0.1 collective-permute-start.15
  59.0 6.3 %graph_layer.5.own = bf16[512,512]{1,0:T(8,128)(2,1)S(1)} custom-call(s32[1]{0:T(128)} %bitcast.5.core_ref, s32[4096]{0:T(1024)S(1)} %bitcast.33, bf16[512,512]{1,0:T(8,128)(2,1)S(1)} %maximum_select_fusion.1.own, bf16[512,512]{1,0:T(8,128)(2,1)S(1)} %collective-permute-done.12.sib, bf16[512,512]{1,0:T(8,128)(2,1)S(1)} %collective-permute-done.13.rim, ...), custom_call_target="tpu_custom_call" | custom-call | flops 8589934592 | bytes 2621440 | tf_op jit(solution)/shard_map/graph_layer/pallas_call | solution.py:252
  65.3 4.9 %collective-permute-done.15.near_w = bf16[784,256]{1,0:T(8,128)(2,1)S(1)} collective-permute-done((bf16[784,256]{1,0:T(8,128)(2,1)S(1)}, bf16[784,256]{1,0:T(8,128)(2,1)S(1)}, u32[]{:S(2)}, u32[]{:S(2)}) %collective-permute-start.15) | collective-permute-done | bytes 401440 | tf_op jit(solution)/shard_map/ppermute | solution.py:306
  70.2 0.4 collective-permute-start.18
  70.7 0.1 collective-permute-start.22
  70.8 2.4 %collective-permute-start.23 = (bf16[512,512]{1,0:T(8,128)(2,1)S(1)}, bf16[512,512]{1,0:T(8,128)(2,1)S(1)}, u32[]{:S(2)}, u32[]{:S(2)}) collective-permute-start(bf16[512,512]{1,0:T(8,128)(2,1)S(1)} %graph_layer.5.own), channel_id=1, source_target_pairs={{1,4},{5,8},{4,1},{9,12},{8,5},{12,9},{3,6},{7,10},{6,3},{11,14},{... | collective-permute-start | bytes 1572872 | tf_op jit(solution)/shard_map/ppermute | solution.py:317
  73.2 0.1 collective-permute-start.19
  73.3 6.3 %graph_layer.6 = (bf16[512,256]{1,0:T(8,128)(2,1)S(1)}, bf16[512,256]{1,0:T(8,128)(2,1)S(1)}) custom-call(s32[1]{0:T(128)} %bitcast.5.core_ref, s32[4096]{0:T(1024)S(1)} %bitcast.36, bf16[512,512]{1,0:T(8,128)(2,1)S(1)} %graph_layer.4.own, bf16[512,512]{1,0:T(8,128)(2,1)S(1)} %collective-permute-done.16.sib, ...), custom_call_target="tpu_custom_call" | custom-call | flops 8589934592 | bytes 2621440 | tf_op jit(solution)/shard_map/graph_layer/pallas_call | solution.py:252
  79.6 3.8 %collective-permute-done.19.near_w = bf16[784,256]{1,0:T(8,128)(2,1)S(1)} collective-permute-done((bf16[784,256]{1,0:T(8,128)(2,1)S(1)}, bf16[784,256]{1,0:T(8,128)(2,1)S(1)}, u32[]{:S(2)}, u32[]{:S(2)}) %collective-permute-start.19) | collective-permute-done | bytes 401440 | tf_op jit(solution)/shard_map/ppermute | solution.py:306
  83.4 2.3 %collective-permute-start.20 = (bf16[512,256]{1,0:T(8,128)(2,1)S(1)}, bf16[512,256]{1,0:T(8,128)(2,1)S(1)}, u32[]{:S(2)}, u32[]{:S(2)}) collective-permute-start(bf16[512,256]{1,0:T(8,128)(2,1)S(1)} %get-tuple-element.95), channel_id=1, source_target_pairs={{0,0},{1,2},{2,1},{3,3},{4,4},{5,6},{6,5},{7,7},{8,8},{9,10},{10,9... | collective-permute-start | bytes 786440 | tf_op jit(solution)/shard_map/ppermute | solution.py:296
  85.8 6.3 %graph_layer.7 = (bf16[512,256]{1,0:T(8,128)(2,1)S(1)}, bf16[512,256]{1,0:T(8,128)(2,1)S(1)}) custom-call(s32[1]{0:T(128)} %bitcast.5.core_ref, s32[4096]{0:T(1024)S(1)} %bitcast.34, bf16[512,512]{1,0:T(8,128)(2,1)S(1)} %graph_layer.5.own, bf16[512,512]{1,0:T(8,128)(2,1)S(1)} %collective-permute-done.22.sib, ...), custom_call_target="tpu_custom_call" | custom-call | flops 8589934592 | bytes 2621440 | tf_op jit(solution)/shard_map/graph_layer/pallas_call | solution.py:252
  92.1 3.2 %collective-permute-start.25 = (bf16[512,256]{1,0:T(8,128)(2,1)S(1)}, bf16[512,256]{1,0:T(8,128)(2,1)S(1)}, u32[]{:S(2)}, u32[]{:S(2)}) collective-permute-start(bf16[512,256]{1,0:T(8,128)(2,1)S(1)} %get-tuple-element.100), channel_id=1, source_target_pairs={{0,0},{1,2},{2,1},{3,3},{4,4},{5,6},{6,5},{7,7},{8,8},{9,10},{10,9... | collective-permute-start | bytes 786440 | tf_op jit(solution)/shard_map/ppermute | solution.py:296
  95.4 1.0 maximum_select_fusion.2
  96.5 5.4 %collective-permute-done.25 = bf16[512,256]{1,0:T(8,128)(2,1)S(1)} collective-permute-done((bf16[512,256]{1,0:T(8,128)(2,1)S(1)}, bf16[512,256]{1,0:T(8,128)(2,1)S(1)}, u32[]{:S(2)}, u32[]{:S(2)}) %collective-permute-start.25) | collective-permute-done | bytes 262176 | tf_op jit(solution)/shard_map/ppermute | solution.py:296
  101.9 0.8 collective-permute-done.26
  102.6 1.0 maximum_select_fusion.3
  (69 shorter events, 0.3 us)
Async XLA Ops:
  0.6 0.7 copy-start.16
  0.7 0.7 copy-start.15
  1.4 1.0 %copy-start = (bf16[1,1024,256]{2,1,0:T(8,128)(2,1)S(1)}, bf16[1,1024,256]{2,1,0:T(8,128)(2,1)}, u32[]{:S(2)}) copy-start(bf16[1,1024,256]{2,1,0:T(8,128)(2,1)} %param.17) | copy-start | bytes 1572868
  2.4 2.3 %copy-start.1 = (bf16[1,1024,256]{2,1,0:T(8,128)(2,1)S(1)}, bf16[1,1024,256]{2,1,0:T(8,128)(2,1)}, u32[]{:S(2)}) copy-start(bf16[1,1024,256]{2,1,0:T(8,128)(2,1)} %param.17) | copy-start | bytes 1572868
  4.7 9.4 %copy-start.13 = (s32[1024]{0:T(1024)S(1)}, s32[1024]{0:T(1024)}, u32[]{:S(2)}) copy-start(s32[1024]{0:T(1024)} %param.20) | copy-start | bytes 12292
  4.7 9.4 %copy-start.14 = (s32[1024]{0:T(1024)S(1)}, s32[1024]{0:T(1024)}, u32[]{:S(2)}) copy-start(s32[1024]{0:T(1024)} %param.22) | copy-start | bytes 12292
  4.7 9.4 %copy-start.12 = (s32[1024,8]{0,1:T(8,128)S(1)}, s32[1024,8]{0,1:T(8,128)}, u32[]{:S(2)}) copy-start(s32[1024,8]{0,1:T(8,128)} %param.19) | copy-start | bytes 98308
  4.8 9.4 %copy-start.11 = (s32[1024,8]{0,1:T(8,128)S(1)}, s32[1024,8]{0,1:T(8,128)}, u32[]{:S(2)}) copy-start(s32[1024,8]{0,1:T(8,128)} %param.21) | copy-start | bytes 98308
  4.8 18.0 %collective-permute-start = (bf16[512,256]{1,0:T(8,128)(2,1)S(1)}, bf16[512,256]{1,0:T(8,128)(2,1)S(1)}, u32[]{:S(2)}, u32[]{:S(2)}) collective-permute-start(bf16[512,256]{1,0:T(8,128)(2,1)S(1)} %get-tuple-element.55), channel_id=1, source_target_pairs={{0,0},{1,2},{2,1},{3,3},{4,4},{5,6},{6,5},{7,7},{8,8},{9,10},{10,9... | collective-permute-start | bytes 786440 | tf_op jit(solution)/shard_map/ppermute | solution.py:290
  9.3 13.5 %collective-permute-start.1 = (bf16[512,256]{1,0:T(8,128)(2,1)S(1)}, bf16[512,256]{1,0:T(8,128)(2,1)S(1)}, u32[]{:S(2)}, u32[]{:S(2)}) collective-permute-start(bf16[512,256]{1,0:T(8,128)(2,1)S(1)} %get-tuple-element.56), channel_id=1, source_target_pairs={{0,1},{1,3},{2,0},{3,2},{4,5},{5,7},{6,4},{7,6},{8,9},{9,11},{10,8... | collective-permute-start | bytes 786440 | tf_op jit(solution)/shard_map/ppermute | solution.py:291
  9.3 8.3 %collective-permute-start.2 = (bf16[272,256]{1,0:T(8,128)(2,1)S(1)}, bf16[272,256]{1,0:T(8,128)(2,1)S(1)}, u32[]{:S(2)}, u32[]{:S(2)}) collective-permute-start(bf16[272,256]{1,0:T(8,128)(2,1)S(1)} %get-tuple-element.59), channel_id=1, source_target_pairs={{0,4},{4,8},{8,12},{12,0},{1,5},{5,9},{9,13},{13,1},{2,6},{6,10},{... | collective-permute-start | bytes 417800 | tf_op jit(solution)/shard_map/ppermute | solution.py:376
  10.7 12.1 %collective-permute-start.3 = (bf16[272,256]{1,0:T(8,128)(2,1)S(1)}, bf16[272,256]{1,0:T(8,128)(2,1)S(1)}, u32[]{:S(2)}, u32[]{:S(2)}) collective-permute-start(bf16[272,256]{1,0:T(8,128)(2,1)S(1)} %get-tuple-element.60), channel_id=1, source_target_pairs={{0,8},{4,12},{8,0},{12,4},{1,9},{5,13},{9,1},{13,5},{2,10},{6,14},... | collective-permute-start | bytes 417800 | tf_op jit(solution)/shard_map/ppermute | solution.py:376
  13.0 9.8 %collective-permute-start.4 = (bf16[272,256]{1,0:T(8,128)(2,1)S(1)}, bf16[272,256]{1,0:T(8,128)(2,1)S(1)}, u32[]{:S(2)}, u32[]{:S(2)}) collective-permute-start(bf16[272,256]{1,0:T(8,128)(2,1)S(1)} %get-tuple-element.61), channel_id=1, source_target_pairs={{0,12},{4,0},{8,4},{12,8},{1,13},{5,1},{9,5},{13,9},{2,14},{6,2},{... | collective-permute-start | bytes 417800 | tf_op jit(solution)/shard_map/ppermute | solution.py:376
  22.8 1.0 copy-start.21
  22.8 1.2 %copy-start.2 = (bf16[1,1024,256]{2,1,0:T(8,128)(2,1)S(1)}, bf16[1,1024,256]{2,1,0:T(8,128)(2,1)}, u32[]{:S(2)}) copy-start(bf16[1,1024,256]{2,1,0:T(8,128)(2,1)} %param.18) | copy-start | bytes 1572868
  23.0 15.7 %collective-permute-start.7 = (bf16[512,512]{1,0:T(8,128)(2,1)S(1)}, bf16[512,512]{1,0:T(8,128)(2,1)S(1)}, u32[]{:S(2)}, u32[]{:S(2)}) collective-permute-start(bf16[512,512]{1,0:T(8,128)(2,1)S(1)} %maximum_select_fusion.own), channel_id=1, source_target_pairs={{0,1},{1,0},{2,3},{3,2},{4,5},{5,4},{6,7},{7,6},{8,9},{9,8},{10,11... | collective-permute-start | bytes 1572872 | tf_op jit(solution)/shard_map/ppermute | solution.py:306
  23.8 10.3 %collective-permute-start.8 = (bf16[784,256]{1,0:T(8,128)(2,1)S(1)}, bf16[784,256]{1,0:T(8,128)(2,1)S(1)}, u32[]{:S(2)}, u32[]{:S(2)}) collective-permute-start(bf16[784,256]{1,0:T(8,128)(2,1)S(1)} %copy-done.21), channel_id=1, source_target_pairs={{0,2},{2,0},{1,3},{3,1},{4,6},{6,4},{5,7},{7,5},{8,10},{10,8},{9,1... | collective-permute-start | bytes 1204232 | tf_op jit(solution)/shard_map/ppermute | solution.py:306
  24.0 23.0 %copy-start.20 = (bf16[784,256]{1,0:T(8,128)(2,1)S(1)}, bf16[784,256]{1,0:T(8,128)(2,1)}, u32[]{:S(2)}) copy-start(bf16[784,256]{1,0:T(8,128)(2,1)} %get-tuple-element.79) | copy-start | bytes 1204228
  24.0 23.1 %copy-start.5 = (bf16[2,256,512]{2,1,0:T(8,128)(2,1)S(1)}, bf16[2,256,512]{2,1,0:T(8,128)(2,1)}, u32[]{:S(2)}) copy-start(bf16[2,256,512]{2,1,0:T(8,128)(2,1)} %w2_hbm.6) | copy-start | bytes 1572868
  24.7 13.2 %collective-permute-start.5 = (bf16[512,256]{1,0:T(8,128)(2,1)S(1)}, bf16[512,256]{1,0:T(8,128)(2,1)S(1)}, u32[]{:S(2)}, u32[]{:S(2)}) collective-permute-start(bf16[512,256]{1,0:T(8,128)(2,1)S(1)} %get-tuple-element.66), channel_id=1, source_target_pairs={{0,0},{1,2},{2,1},{3,3},{4,4},{5,6},{6,5},{7,7},{8,8},{9,10},{10,9... | collective-permute-start | bytes 786440 | tf_op jit(solution)/shard_map/ppermute | solution.py:290
  28.7 18.4 %copy-start.9 = (bf16[2,256]{1,0:T(2,128)(2,1)S(1)}, bf16[2,256]{1,0:T(2,128)(2,1)}, u32[]{:S(2)}) copy-start(bf16[2,256]{1,0:T(2,128)(2,1)} %bias.6) | copy-start | bytes 3076
  28.7 18.4 %copy-start.3 = (bf16[2,512,256]{2,1,0:T(8,128)(2,1)S(1)}, bf16[2,512,256]{2,1,0:T(8,128)(2,1)}, u32[]{:S(2)}) copy-start(bf16[2,512,256]{2,1,0:T(8,128)(2,1)} %ws_hbm.6) | copy-start | bytes 1572868
  28.7 18.4 %copy-start.4 = (bf16[2,512,256]{2,1,0:T(8,128)(2,1)S(1)}, bf16[2,512,256]{2,1,0:T(8,128)(2,1)}, u32[]{:S(2)}) copy-start(bf16[2,512,256]{2,1,0:T(8,128)(2,1)} %wd_hbm.6) | copy-start | bytes 1572868
  28.7 9.9 %collective-permute-start.6 = (bf16[512,256]{1,0:T(8,128)(2,1)S(1)}, bf16[512,256]{1,0:T(8,128)(2,1)S(1)}, u32[]{:S(2)}, u32[]{:S(2)}) collective-permute-start(bf16[512,256]{1,0:T(8,128)(2,1)S(1)} %get-tuple-element.67), channel_id=1, source_target_pairs={{0,1},{1,3},{2,0},{3,2},{4,5},{5,7},{6,4},{7,6},{8,9},{9,11},{10,8... | collective-permute-start | bytes 786440 | tf_op jit(solution)/shard_map/ppermute | solution.py:291
  28.7 18.3 %collective-permute-start.9 = (bf16[512,512]{1,0:T(8,128)(2,1)S(1)}, bf16[512,512]{1,0:T(8,128)(2,1)S(1)}, u32[]{:S(2)}, u32[]{:S(2)}) collective-permute-start(bf16[512,512]{1,0:T(8,128)(2,1)S(1)} %maximum_select_fusion.own), channel_id=1, source_target_pairs={{1,4},{0,13},{5,8},{4,1},{9,12},{8,5},{13,0},{12,9},{3,6},{2,15},{... | collective-permute-start | bytes 1572872 | tf_op jit(solution)/shard_map/ppermute | solution.py:317
  38.6 8.4 %collective-permute-start.10 = (bf16[784,256]{1,0:T(8,128)(2,1)S(1)}, bf16[784,256]{1,0:T(8,128)(2,1)S(1)}, u32[]{:S(2)}, u32[]{:S(2)}) collective-permute-start(bf16[784,256]{1,0:T(8,128)(2,1)S(1)} %collective-permute-done.8.near_w), channel_id=1, source_target_pairs={{0,1},{1,0},{2,3},{3,2},{4,5},{5,4},{6,7},{7,6},{8,9},{9,8},{10,11... | collective-permute-start | bytes 1204232 | tf_op jit(solution)/shard_map/ppermute | solution.py:306
  41.3 17.6 %copy-start.19 = (bf16[784,256]{1,0:T(8,128)(2,1)S(1)}, bf16[784,256]{1,0:T(8,128)(2,1)}, u32[]{:S(2)}) copy-start(bf16[784,256]{1,0:T(8,128)(2,1)} %get-tuple-element.86) | copy-start | bytes 1204228
  41.3 17.7 %copy-start.6 = (bf16[2,512,256]{2,1,0:T(8,128)(2,1)S(1)}, bf16[2,512,256]{2,1,0:T(8,128)(2,1)}, u32[]{:S(2)}) copy-start(bf16[2,512,256]{2,1,0:T(8,128)(2,1)} %ws_hbm.7) | copy-start | bytes 1572868
  41.3 17.7 %copy-start.7 = (bf16[2,512,256]{2,1,0:T(8,128)(2,1)S(1)}, bf16[2,512,256]{2,1,0:T(8,128)(2,1)}, u32[]{:S(2)}) copy-start(bf16[2,512,256]{2,1,0:T(8,128)(2,1)} %wd_hbm.7) | copy-start | bytes 1572868
  41.3 17.7 %copy-start.8 = (bf16[2,256,512]{2,1,0:T(8,128)(2,1)S(1)}, bf16[2,256,512]{2,1,0:T(8,128)(2,1)}, u32[]{:S(2)}) copy-start(bf16[2,256,512]{2,1,0:T(8,128)(2,1)} %w2_hbm.7) | copy-start | bytes 1572868
  41.3 17.6 %collective-permute-start.12 = (bf16[512,512]{1,0:T(8,128)(2,1)S(1)}, bf16[512,512]{1,0:T(8,128)(2,1)S(1)}, u32[]{:S(2)}, u32[]{:S(2)}) collective-permute-start(bf16[512,512]{1,0:T(8,128)(2,1)S(1)} %maximum_select_fusion.1.own), channel_id=1, source_target_pairs={{0,1},{1,0},{2,3},{3,2},{4,5},{5,4},{6,7},{7,6},{8,9},{9,8},{10,11... | collective-permute-start | bytes 1572872 | tf_op jit(solution)/shard_map/ppermute | solution.py:306
  41.4 17.6 %collective-permute-start.13 = (bf16[512,512]{1,0:T(8,128)(2,1)S(1)}, bf16[512,512]{1,0:T(8,128)(2,1)S(1)}, u32[]{:S(2)}, u32[]{:S(2)}) collective-permute-start(bf16[512,512]{1,0:T(8,128)(2,1)S(1)} %maximum_select_fusion.1.own), channel_id=1, source_target_pairs={{1,4},{5,8},{4,1},{9,12},{8,5},{12,9},{3,6},{7,10},{6,3},{11,14},{... | collective-permute-start | bytes 1572872 | tf_op jit(solution)/shard_map/ppermute | solution.py:317
  46.9 7.2 %collective-permute-start.11 = (bf16[784,256]{1,0:T(8,128)(2,1)S(1)}, bf16[784,256]{1,0:T(8,128)(2,1)S(1)}, u32[]{:S(2)}, u32[]{:S(2)}) collective-permute-start(bf16[784,256]{1,0:T(8,128)(2,1)S(1)} %copy-done.20), channel_id=1, source_target_pairs={{0,2},{2,0},{1,3},{3,1},{4,6},{6,4},{5,7},{7,5},{8,10},{10,8},{9,1... | collective-permute-start | bytes 1204232 | tf_op jit(solution)/shard_map/ppermute | solution.py:306
  53.4 5.7 %copy-start.10 = (bf16[2,256]{1,0:T(2,128)(2,1)S(1)}, bf16[2,256]{1,0:T(2,128)(2,1)}, u32[]{:S(2)}) copy-start(bf16[2,256]{1,0:T(2,128)(2,1)} %bias.7) | copy-start | bytes 3076
  54.1 4.9 %collective-permute-start.14 = (bf16[784,256]{1,0:T(8,128)(2,1)S(1)}, bf16[784,256]{1,0:T(8,128)(2,1)S(1)}, u32[]{:S(2)}, u32[]{:S(2)}) collective-permute-start(bf16[784,256]{1,0:T(8,128)(2,1)S(1)} %collective-permute-done.11.near_w), channel_id=1, source_target_pairs={{0,1},{1,0},{2,3},{3,2},{4,5},{5,4},{6,7},{7,6},{8,9},{9,8},{10,11... | collective-permute-start | bytes 1204232 | tf_op jit(solution)/shard_map/ppermute | solution.py:306
  54.1 19.0 %collective-permute-start.16 = (bf16[512,512]{1,0:T(8,128)(2,1)S(1)}, bf16[512,512]{1,0:T(8,128)(2,1)S(1)}, u32[]{:S(2)}, u32[]{:S(2)}) collective-permute-start(bf16[512,512]{1,0:T(8,128)(2,1)S(1)} %graph_layer.4.own), channel_id=1, source_target_pairs={{0,1},{1,0},{2,3},{3,2},{4,5},{5,4},{6,7},{7,6},{8,9},{9,8},{10,11... | collective-permute-start | bytes 1572872 | tf_op jit(solution)/shard_map/ppermute | solution.py:306
  54.6 18.7 %collective-permute-start.17 = (bf16[512,512]{1,0:T(8,128)(2,1)S(1)}, bf16[512,512]{1,0:T(8,128)(2,1)S(1)}, u32[]{:S(2)}, u32[]{:S(2)}) collective-permute-start(bf16[512,512]{1,0:T(8,128)(2,1)S(1)} %graph_layer.4.own), channel_id=1, source_target_pairs={{1,4},{0,13},{5,8},{4,1},{9,12},{8,5},{13,0},{12,9},{3,6},{2,15},{... | collective-permute-start | bytes 1572872 | tf_op jit(solution)/shard_map/ppermute | solution.py:317
  58.9 14.3 %copy-start.18 = (bf16[784,256]{1,0:T(8,128)(2,1)S(1)}, bf16[784,256]{1,0:T(8,128)(2,1)}, u32[]{:S(2)}) copy-start(bf16[784,256]{1,0:T(8,128)(2,1)} %get-tuple-element.94) | copy-start | bytes 1204228
  58.9 11.3 %collective-permute-start.15 = (bf16[784,256]{1,0:T(8,128)(2,1)S(1)}, bf16[784,256]{1,0:T(8,128)(2,1)S(1)}, u32[]{:S(2)}, u32[]{:S(2)}) collective-permute-start(bf16[784,256]{1,0:T(8,128)(2,1)S(1)} %copy-done.19), channel_id=1, source_target_pairs={{0,2},{2,0},{1,3},{3,1},{4,6},{6,4},{5,7},{7,5},{8,10},{10,8},{9,1... | collective-permute-start | bytes 1204232 | tf_op jit(solution)/shard_map/ppermute | solution.py:306
  70.2 3.1 %collective-permute-start.18 = (bf16[784,256]{1,0:T(8,128)(2,1)S(1)}, bf16[784,256]{1,0:T(8,128)(2,1)S(1)}, u32[]{:S(2)}, u32[]{:S(2)}) collective-permute-start(bf16[784,256]{1,0:T(8,128)(2,1)S(1)} %collective-permute-done.15.near_w), channel_id=1, source_target_pairs={{0,1},{1,0},{2,3},{3,2},{4,5},{5,4},{6,7},{7,6},{8,9},{9,8},{10,11... | collective-permute-start | bytes 1204232 | tf_op jit(solution)/shard_map/ppermute | solution.py:306
  70.7 15.1 %collective-permute-start.22 = (bf16[512,512]{1,0:T(8,128)(2,1)S(1)}, bf16[512,512]{1,0:T(8,128)(2,1)S(1)}, u32[]{:S(2)}, u32[]{:S(2)}) collective-permute-start(bf16[512,512]{1,0:T(8,128)(2,1)S(1)} %graph_layer.5.own), channel_id=1, source_target_pairs={{0,1},{1,0},{2,3},{3,2},{4,5},{5,4},{6,7},{7,6},{8,9},{9,8},{10,11... | collective-permute-start | bytes 1572872 | tf_op jit(solution)/shard_map/ppermute | solution.py:306
  70.8 15.0 %collective-permute-start.23 = (bf16[512,512]{1,0:T(8,128)(2,1)S(1)}, bf16[512,512]{1,0:T(8,128)(2,1)S(1)}, u32[]{:S(2)}, u32[]{:S(2)}) collective-permute-start(bf16[512,512]{1,0:T(8,128)(2,1)S(1)} %graph_layer.5.own), channel_id=1, source_target_pairs={{1,4},{5,8},{4,1},{9,12},{8,5},{12,9},{3,6},{7,10},{6,3},{11,14},{... | collective-permute-start | bytes 1572872 | tf_op jit(solution)/shard_map/ppermute | solution.py:317
  73.2 10.2 %collective-permute-start.19 = (bf16[784,256]{1,0:T(8,128)(2,1)S(1)}, bf16[784,256]{1,0:T(8,128)(2,1)S(1)}, u32[]{:S(2)}, u32[]{:S(2)}) collective-permute-start(bf16[784,256]{1,0:T(8,128)(2,1)S(1)} %copy-done.18), channel_id=1, source_target_pairs={{0,2},{2,0},{1,3},{3,1},{4,6},{6,4},{5,7},{7,5},{8,10},{10,8},{9,1... | collective-permute-start | bytes 1204232 | tf_op jit(solution)/shard_map/ppermute | solution.py:306
  83.4 2.4 %collective-permute-start.24 = (bf16[784,256]{1,0:T(8,128)(2,1)S(1)}, bf16[784,256]{1,0:T(8,128)(2,1)S(1)}, u32[]{:S(2)}, u32[]{:S(2)}) collective-permute-start(bf16[784,256]{1,0:T(8,128)(2,1)S(1)} %collective-permute-done.19.near_w), channel_id=1, source_target_pairs={{0,1},{1,0},{2,3},{3,2},{4,5},{5,4},{6,7},{7,6},{8,9},{9,8},{10,11... | collective-permute-start | bytes 1204232 | tf_op jit(solution)/shard_map/ppermute | solution.py:306
  83.4 12.0 %collective-permute-start.20 = (bf16[512,256]{1,0:T(8,128)(2,1)S(1)}, bf16[512,256]{1,0:T(8,128)(2,1)S(1)}, u32[]{:S(2)}, u32[]{:S(2)}) collective-permute-start(bf16[512,256]{1,0:T(8,128)(2,1)S(1)} %get-tuple-element.95), channel_id=1, source_target_pairs={{0,0},{1,2},{2,1},{3,3},{4,4},{5,6},{6,5},{7,7},{8,8},{9,10},{10,9... | collective-permute-start | bytes 786440 | tf_op jit(solution)/shard_map/ppermute | solution.py:296
  85.7 9.7 %collective-permute-start.21 = (bf16[512,256]{1,0:T(8,128)(2,1)S(1)}, bf16[512,256]{1,0:T(8,128)(2,1)S(1)}, u32[]{:S(2)}, u32[]{:S(2)}) collective-permute-start(bf16[512,256]{1,0:T(8,128)(2,1)S(1)} %get-tuple-element.96), channel_id=1, source_target_pairs={{0,2},{1,0},{2,3},{3,1},{4,6},{5,4},{6,7},{7,5},{8,10},{9,8},{10,1... | collective-permute-start | bytes 786440 | tf_op jit(solution)/shard_map/ppermute | solution.py:297
  92.1 9.7 %collective-permute-start.25 = (bf16[512,256]{1,0:T(8,128)(2,1)S(1)}, bf16[512,256]{1,0:T(8,128)(2,1)S(1)}, u32[]{:S(2)}, u32[]{:S(2)}) collective-permute-start(bf16[512,256]{1,0:T(8,128)(2,1)S(1)} %get-tuple-element.100), channel_id=1, source_target_pairs={{0,0},{1,2},{2,1},{3,3},{4,4},{5,6},{6,5},{7,7},{8,8},{9,10},{10,9... | collective-permute-start | bytes 786440 | tf_op jit(solution)/shard_map/ppermute | solution.py:296
  95.4 7.2 %collective-permute-start.26 = (bf16[512,256]{1,0:T(8,128)(2,1)S(1)}, bf16[512,256]{1,0:T(8,128)(2,1)S(1)}, u32[]{:S(2)}, u32[]{:S(2)}) collective-permute-start(bf16[512,256]{1,0:T(8,128)(2,1)S(1)} %get-tuple-element.101), channel_id=1, source_target_pairs={{0,2},{1,0},{2,3},{3,1},{4,6},{5,4},{6,7},{7,5},{8,10},{9,8},{10,1... | collective-permute-start | bytes 786440 | tf_op jit(solution)/shard_map/ppermute | solution.py:297
  (1 other events, 0.7 us)

commit v6 on v5

--- a/solution.py
+++ b/solution.py
@@ -346,7 +346,7 @@
         out_specs=(vmem,) * len(order),
         scratch_shapes=[pltpu.SemaphoreType.DMA((3 * len(order),))],
         compiler_params=pltpu.CompilerParams(vmem_limit_bytes=60 << 20),
-        cost_estimate=SMALL,
+        cost_estimate=pl.CostEstimate(flops=256 * share**3, bytes_accessed=1, transcendentals=0),
         name="pack_weights",
     )(core, g_bias, r_bias, *g_weights, *r_weights)
 
@@ -383,42 +383,41 @@
 
     order = [(graph, layer) for layer in range(layers) for graph in (0, 1)]
     packs = list(pack_weights(order, core1, g_weights, g_b1, r_weights, r_b1))
+    landed[1], packs[0] = after((landed[1], packs[0]))
     near_w = [swap(packs[0], "mp")]
     g_idx, r_idx = idx[0], idx[1]
     g_a, g_b, g_idx, r_idx, packs[1], *landed = after((g_a, g_b, g_idx, r_idx, packs[1], *landed))
     planet = ordered(core, g_a, g_b, 1)
     g_sib, g_rim = swap(planet, "batch"), rims(planet, True)
-    r_a, r_b = spread_rows(*add_force(part.reshape(1), r_own, landed, cap))
-    r_a, r_b, g_sib, near_w[0] = after((r_a, r_b, g_sib, near_w[0]))
+    *r_pair, packs[1] = after((*add_force(part.reshape(1), r_own, landed, cap), packs[1]))
+    r_a, r_b = spread_rows(*r_pair)
+    near_w.append(swap(packs[1], "mp"))
+    r_a, r_b, g_sib, g_rim, near_w[0] = after((r_a, r_b, g_sib, g_rim, near_w[0]))
     regional, g_idx = after((ordered(core, r_a, r_b, 1), g_idx))
     r_sib, r_rim = swap(regional, "batch"), rims(regional, False)
-    far_w = []
-    for layer in range(layers):
+    for i, (graph, layer) in enumerate(order):
         last = layer == layers - 1
-        for graph in (0, 1):
-            i = 2 * layer + graph
-            far_w.append(swap(near_w[i], "batch"))
-            if i + 1 < len(order):
-                sent, near_w[i] = after((packs[i + 1], near_w[i]))
-                near_w.append(swap(sent, "mp"))
-            if graph == 0:
-                planet = run_layer(
-                    layer, slots, last, core1, g_idx, planet, g_sib, g_rim,
-                    g_ws, g_wd, g_w2, g_b1, near_w[i], far_w[i],
-                )
-                *planet, core1, near_w[i + 1] = after((*(planet if last else (planet,)), core1, near_w[i + 1]))
-                if not last:
-                    planet = planet[0]
-                    g_sib, g_rim = swap(planet, "batch"), rims(planet, True)
-                if layer:
-                    r_sib, r_rim = swap(regional, "batch"), rims(regional, False)
-            else:
-                regional = run_layer(
-                    layer, slots, last, core1, r_idx, regional, r_sib, r_rim,
-                    r_ws, r_wd, r_w2, r_b1, near_w[i], far_w[i],
-                )
-                if not last:
-                    regional, core1, near_w[i + 1] = after((regional, core1, near_w[i + 1]))
+        far_w = swap(near_w[i], "batch")
+        if i + 1 < len(order):
+            near_w[i + 1], core1 = after((near_w[i + 1], core1))
+        if i + 2 < len(order):
+            packs[i + 2], near_w[i + 1] = after((packs[i + 2], near_w[i + 1]))
+            near_w.append(swap(packs[i + 2], "mp"))
+        if graph == 0:
+            planet = run_layer(
+                layer, slots, last, core1, g_idx, planet, g_sib, g_rim, g_ws, g_wd, g_w2, g_b1, near_w[i], far_w
+            )
+            *planet, core1 = after((*(planet if last else (planet,)), core1))
+            if not last:
+                planet = planet[0]
+                g_sib, g_rim = swap(planet, "batch"), rims(planet, True)
+        else:
+            regional = run_layer(
+                layer, slots, last, core1, r_idx, regional, r_sib, r_rim, r_ws, r_wd, r_w2, r_b1, near_w[i], far_w
+            )
+            if not last:
+                regional, core1 = after((regional, core1))
+                r_sib, r_rim = swap(regional, "batch"), rims(regional, False)
     g_out = ordered(part, *gather_rows(*planet), 0)
     r_out = ordered(part, *gather_rows(*regional), 0)
     return g_out[None], r_out[None]

time: 104 us -> 104 us (level)
  waiting for transfers between devices: 27.2 us -> 26 us
    ppermute x4, starting transfers between devices: 15.7 us -> 11.3 us  [rims(): return lax.ppermute(own, ('mesh', 'batch'), pairs)]
    ppermute x2, waiting for transfers between devices: 3.86 us -> 8.02 us  [spread_rows(): a = lax.ppermute(same, ('mp', 'batch'), [(0, 0), (1, 2), (2, 1), (3, 3)])]
    ppermute x12, starting transfers between devices: 4.62 us -> 7.8 us  [swap(): return lax.ppermute(values, axis, [(0, 1), (1, 0)])]
    ppermute x12, waiting for transfers between devices: 11.3 us -> 8.12 us  [swap(): return lax.ppermute(values, axis, [(0, 1), (1, 0)])]
    ppermute x2, waiting for transfers between devices: 5.39 us -> 2.55 us  [gather_rows(): same = lax.ppermute(a, ('mp', 'batch'), [(0, 0), (1, 2), (2, 1), (3, 3)])]
    ppermute x2, waiting for transfers between devices: 0.78 us -> 1.93 us  [gather_rows(): other = lax.ppermute(b, ('mp', 'batch'), [(0, 2), (1, 0), (2, 3), (3, 1)])]
  transfers between devices with their start and end apart: 27 -> 27, of which waited for: 9 -> 7; matrix products, arithmetic and copies ran while one was open for 1% -> 1% of each run, Pallas kernels for 28% -> 28%
where the time goes in v6:
time: 104 us; the launch traced here: 103 us
  starting transfers between devices  39.5 us (38%)
  Pallas kernels  31.5 us (30%)
  waiting for transfers between devices  26 us (25%)
  local copies, waits for them, and re-layouts  2.57 us (2%)
  other arithmetic  2.42 us (2%)
  between operations  1.14 us (1%)
    pallas_call x4, Pallas kernels, run_layer(): pl.pallas_call(functools.partial(layer_kernel, layer, slots, last), out_s...  25.2 us
    ppermute x4, starting transfers between devices, rims(): return lax.ppermute(own, ('mesh', 'batch'), pairs)  11.3 us
    ppermute x2, starting transfers between devices, spread_rows(): a = lax.ppermute(same, ('mp', 'batch'), [(0, 0), (1, 2), (2, 1), (3, 3)])  9.5 us
    ppermute x12, waiting for transfers between devices, swap(): return lax.ppermute(values, axis, [(0, 1), (1, 0)])  8.12 us
    ppermute x2, waiting for transfers between devices, spread_rows(): a = lax.ppermute(same, ('mp', 'batch'), [(0, 0), (1, 2), (2, 1), (3, 3)])  8.02 us
    ppermute x12, starting transfers between devices, swap(): return lax.ppermute(values, axis, [(0, 1), (1, 0)])  7.8 us
    ppermute x2, starting transfers between devices, gather_rows(): same = lax.ppermute(a, ('mp', 'batch'), [(0, 0), (1, 2), (2, 1), (3, 3)])  5.55 us
    ppermute x3, starting transfers between devices, by_rows(): lax.ppermute(pieces[k], 'mesh', [(i, (i + k) % parts) for i in range(part...  4.72 us
  transfers between devices with their start and end apart: 27, of which 7 were waited for; matrix products, arithmetic and copies ran while one was open for 1% of the time, Pallas kernels for 28%

profile of v6, /device:TPU:1, one launch (start us, length us, event | category | flops | bytes accessed | tf_op | source)
XLA Modules:
  0.0 103.2 jit_solution(16909187082563266136)
XLA Ops:
  0.7 0.7 copy-done.17
  1.4 1.0 %copy-done = bf16[1,1024,256]{2,1,0:T(8,128)(2,1)S(1)} copy-done((bf16[1,1024,256]{2,1,0:T(8,128)(2,1)S(1)}, bf16[1,1024,256]{2,1,0:T(8,128)(2,1)}, u32[]{:S(2)}) %copy-start) | copy-done | bytes 524312
  2.4 2.2 %pick_rows.1 = (bf16[272,256]{1,0:T(8,128)(2,1)S(1)}, bf16[272,256]{1,0:T(8,128)(2,1)S(1)}, bf16[272,256]{1,0:T(8,128)(2,1)S(1)}, bf16[272,256]{1,0:T(8,128)(2,1)S(1)}) custom-call(s32[1]{0:T(128)} %bitcast.me_ref, s32[3,512]{1,0:T(4,128)S(1)} %pad_add_fusion.bnd_ref, bf16[1024,256]{1,0:T(8,128)(2,1)S(1)} %bitcast.30), custom_call_target="tpu_custom_call" | custom-call | flops 1 | bytes 1 | tf_op jit(solution)/shard_map/pick_rows/pallas_call | solution.py:115
  4.7 4.5 %collective-permute-start = (bf16[512,256]{1,0:T(8,128)(2,1)S(1)}, bf16[512,256]{1,0:T(8,128)(2,1)S(1)}, u32[]{:S(2)}, u32[]{:S(2)}) collective-permute-start(bf16[512,256]{1,0:T(8,128)(2,1)S(1)} %get-tuple-element.64), channel_id=1, source_target_pairs={{0,0},{1,2},{2,1},{3,3},{4,4},{5,6},{6,5},{7,7},{8,8},{9,10},{10,9... | collective-permute-start | bytes 786440 | tf_op jit(solution)/shard_map/ppermute | solution.py:290
  9.2 0.0 collective-permute-start.1
  9.3 1.3 %collective-permute-start.2 = (bf16[272,256]{1,0:T(8,128)(2,1)S(1)}, bf16[272,256]{1,0:T(8,128)(2,1)S(1)}, u32[]{:S(2)}, u32[]{:S(2)}) collective-permute-start(bf16[272,256]{1,0:T(8,128)(2,1)S(1)} %get-tuple-element.68), channel_id=1, source_target_pairs={{0,4},{4,8},{8,12},{12,0},{1,5},{5,9},{9,13},{13,1},{2,6},{6,10},{... | collective-permute-start | bytes 417800 | tf_op jit(solution)/shard_map/ppermute | solution.py:376
  10.6 2.3 %collective-permute-start.3 = (bf16[272,256]{1,0:T(8,128)(2,1)S(1)}, bf16[272,256]{1,0:T(8,128)(2,1)S(1)}, u32[]{:S(2)}, u32[]{:S(2)}) collective-permute-start(bf16[272,256]{1,0:T(8,128)(2,1)S(1)} %get-tuple-element.71), channel_id=1, source_target_pairs={{0,8},{4,12},{8,0},{12,4},{1,9},{5,13},{9,1},{13,5},{2,10},{6,14},... | collective-permute-start | bytes 417800 | tf_op jit(solution)/shard_map/ppermute | solution.py:376
  12.9 1.1 %collective-permute-start.4 = (bf16[272,256]{1,0:T(8,128)(2,1)S(1)}, bf16[272,256]{1,0:T(8,128)(2,1)S(1)}, u32[]{:S(2)}, u32[]{:S(2)}) collective-permute-start(bf16[272,256]{1,0:T(8,128)(2,1)S(1)} %get-tuple-element.72), channel_id=1, source_target_pairs={{0,12},{4,0},{8,4},{12,8},{1,13},{5,1},{9,5},{13,9},{2,14},{6,2},{... | collective-permute-start | bytes 417800 | tf_op jit(solution)/shard_map/ppermute | solution.py:376
  14.0 0.7 copy-done.14
  14.7 0.1 fusion.5
  14.8 3.4 %pack_weights.1 = (bf16[784,256]{1,0:T(8,128)(2,1)}, bf16[784,256]{1,0:T(8,128)(2,1)}, bf16[784,256]{1,0:T(8,128)(2,1)}, bf16[784,256]{1,0:T(8,128)(2,1)}) custom-call(s32[1]{0:T(128)} %bitcast.5.core_ref, bf16[2,256]{1,0:T(2,128)(2,1)} %bias.6, bf16[2,256]{1,0:T(2,128)(2,1)} %bias.7, bf16[2,512,256]{2,1,0:T(8,128)(2,1)} %ws_hbm.6, ...), custom_call_target="tpu_custom_call" | custom-call | flops 4294967296 | bytes 1 | tf_op jit(solution)/shard_map/pack_weights/pallas_call | solution.py:342
  18.3 4.4 %collective-permute-done.3.refs_2_ = bf16[272,256]{1,0:T(8,128)(2,1)S(1)} collective-permute-done((bf16[272,256]{1,0:T(8,128)(2,1)S(1)}, bf16[272,256]{1,0:T(8,128)(2,1)S(1)}, u32[]{:S(2)}, u32[]{:S(2)}) %collective-permute-start.3) | collective-permute-done | bytes 139296 | tf_op jit(solution)/shard_map/ppermute | solution.py:376
  22.8 0.1 maximum_select_fusion.own
  22.9 0.7 collective-permute-start.9
  23.6 3.1 %collective-permute-start.10 = (bf16[512,512]{1,0:T(8,128)(2,1)S(1)}, bf16[512,512]{1,0:T(8,128)(2,1)S(1)}, u32[]{:S(2)}, u32[]{:S(2)}) collective-permute-start(bf16[512,512]{1,0:T(8,128)(2,1)S(1)} %maximum_select_fusion.own), channel_id=1, source_target_pairs={{1,4},{0,13},{5,8},{4,1},{9,12},{8,5},{13,0},{12,9},{3,6},{2,15},{... | collective-permute-start | bytes 1572872 | tf_op jit(solution)/shard_map/ppermute | solution.py:317
  26.7 0.1 collective-permute-start.11
  26.8 0.7 add_force.1
  27.5 5.0 %collective-permute-start.7 = (bf16[512,256]{1,0:T(8,128)(2,1)S(1)}, bf16[512,256]{1,0:T(8,128)(2,1)S(1)}, u32[]{:S(2)}, u32[]{:S(2)}) collective-permute-start(bf16[512,256]{1,0:T(8,128)(2,1)S(1)} %get-tuple-element.84), channel_id=1, source_target_pairs={{0,0},{1,2},{2,1},{3,3},{4,4},{5,6},{6,5},{7,7},{8,8},{9,10},{10,9... | collective-permute-start | bytes 786440 | tf_op jit(solution)/shard_map/ppermute | solution.py:290
  32.5 8.0 %collective-permute-done.7 = bf16[512,256]{1,0:T(8,128)(2,1)S(1)} collective-permute-done((bf16[512,256]{1,0:T(8,128)(2,1)S(1)}, bf16[512,256]{1,0:T(8,128)(2,1)S(1)}, u32[]{:S(2)}, u32[]{:S(2)}) %collective-permute-start.7) | collective-permute-done | bytes 262176 | tf_op jit(solution)/shard_map/ppermute | solution.py:290
  40.5 1.0 collective-permute-done.8
  41.5 2.9 %collective-permute-start.12 = (bf16[784,256]{1,0:T(8,128)(2,1)S(1)}, bf16[784,256]{1,0:T(8,128)(2,1)S(1)}, u32[]{:S(2)}, u32[]{:S(2)}) collective-permute-start(bf16[784,256]{1,0:T(8,128)(2,1)S(1)} %collective-permute-done.11.near_w), channel_id=1, source_target_pairs={{0,1},{1,0},{2,3},{3,2},{4,5},{5,4},{6,7},{7,6},{8,9},{9,8},{10,11... | collective-permute-start | bytes 1204232 | tf_op jit(solution)/shard_map/ppermute | solution.py:306
  44.4 7.5 %collective-permute-done.5.near_w = bf16[784,256]{1,0:T(8,128)(2,1)S(1)} collective-permute-done((bf16[784,256]{1,0:T(8,128)(2,1)S(1)}, bf16[784,256]{1,0:T(8,128)(2,1)S(1)}, u32[]{:S(2)}, u32[]{:S(2)}) %collective-permute-start.5) | collective-permute-done | bytes 401440 | tf_op jit(solution)/shard_map/ppermute | solution.py:306
  51.9 0.1 collective-permute-start.6
  52.0 1.0 %collective-permute-start.16 = (bf16[784,256]{1,0:T(8,128)(2,1)S(1)}, bf16[784,256]{1,0:T(8,128)(2,1)S(1)}, u32[]{:S(2)}, u32[]{:S(2)}) collective-permute-start(bf16[784,256]{1,0:T(8,128)(2,1)S(1)} %collective-permute-done.5.near_w), channel_id=1, source_target_pairs={{0,1},{1,0},{2,3},{3,2},{4,5},{5,4},{6,7},{7,6},{8,9},{9,8},{10,11... | collective-permute-start | bytes 1204232 | tf_op jit(solution)/shard_map/ppermute | solution.py:306
  53.0 0.1 maximum_select_fusion.1.own
  53.2 0.1 collective-permute-start.14
  53.3 2.3 %collective-permute-start.15 = (bf16[512,512]{1,0:T(8,128)(2,1)S(1)}, bf16[512,512]{1,0:T(8,128)(2,1)S(1)}, u32[]{:S(2)}, u32[]{:S(2)}) collective-permute-start(bf16[512,512]{1,0:T(8,128)(2,1)S(1)} %maximum_select_fusion.1.own), channel_id=1, source_target_pairs={{1,4},{5,8},{4,1},{9,12},{8,5},{12,9},{3,6},{7,10},{6,3},{11,14},{... | collective-permute-start | bytes 1572872 | tf_op jit(solution)/shard_map/ppermute | solution.py:317
  55.7 6.3 %graph_layer.4.own = bf16[512,512]{1,0:T(8,128)(2,1)S(1)} custom-call(s32[1]{0:T(128)} %bitcast.5.core_ref, s32[4096]{0:T(1024)S(1)} %bitcast.35, bf16[512,512]{1,0:T(8,128)(2,1)S(1)} %maximum_select_fusion.own, bf16[512,512]{1,0:T(8,128)(2,1)S(1)} %collective-permute-done.9.sib, bf16[512,512]{1,0:T(8,128)(2,1)S(1)} %collective-permute-done.10.rim, ...), custom_call_target="tpu_custom_call" | custom-call | flops 8589934592 | bytes 2621440 | tf_op jit(solution)/shard_map/graph_layer/pallas_call | solution.py:252
  62.0 0.1 collective-permute-start.17
  62.0 0.0 collective-permute-done.6.near_w
  62.1 2.0 %collective-permute-start.18 = (bf16[512,512]{1,0:T(8,128)(2,1)S(1)}, bf16[512,512]{1,0:T(8,128)(2,1)S(1)}, u32[]{:S(2)}, u32[]{:S(2)}) collective-permute-start(bf16[512,512]{1,0:T(8,128)(2,1)S(1)} %graph_layer.4.own), channel_id=1, source_target_pairs={{1,4},{0,13},{5,8},{4,1},{9,12},{8,5},{13,0},{12,9},{3,6},{2,15},{... | collective-permute-start | bytes 1572872 | tf_op jit(solution)/shard_map/ppermute | solution.py:317
  64.0 1.4 %collective-permute-start.13 = (bf16[784,256]{1,0:T(8,128)(2,1)S(1)}, bf16[784,256]{1,0:T(8,128)(2,1)S(1)}, u32[]{:S(2)}, u32[]{:S(2)}) collective-permute-start(bf16[784,256]{1,0:T(8,128)(2,1)S(1)} %copy-done.18), channel_id=1, source_target_pairs={{0,2},{2,0},{1,3},{3,1},{4,6},{6,4},{5,7},{7,5},{8,10},{10,8},{9,1... | collective-permute-start | bytes 1204232 | tf_op jit(solution)/shard_map/ppermute | solution.py:306
  65.4 1.3 %collective-permute-start.19 = (bf16[784,256]{1,0:T(8,128)(2,1)S(1)}, bf16[784,256]{1,0:T(8,128)(2,1)S(1)}, u32[]{:S(2)}, u32[]{:S(2)}) collective-permute-start(bf16[784,256]{1,0:T(8,128)(2,1)S(1)} %collective-permute-done.6.near_w), channel_id=1, source_target_pairs={{0,1},{1,0},{2,3},{3,2},{4,5},{5,4},{6,7},{7,6},{8,9},{9,8},{10,11... | collective-permute-start | bytes 1204232 | tf_op jit(solution)/shard_map/ppermute | solution.py:306
  66.8 6.3 %graph_layer.5.own = bf16[512,512]{1,0:T(8,128)(2,1)S(1)} custom-call(s32[1]{0:T(128)} %bitcast.5.core_ref, s32[4096]{0:T(1024)S(1)} %bitcast.33, bf16[512,512]{1,0:T(8,128)(2,1)S(1)} %maximum_select_fusion.1.own, bf16[512,512]{1,0:T(8,128)(2,1)S(1)} %collective-permute-done.14.sib, bf16[512,512]{1,0:T(8,128)(2,1)S(1)} %collective-permute-done.15.rim, ...), custom_call_target="tpu_custom_call" | custom-call | flops 8589934592 | bytes 2621440 | tf_op jit(solution)/shard_map/graph_layer/pallas_call | solution.py:252
  73.1 0.1 collective-permute-start.22
  73.2 0.6 collective-permute-done.13.near_w
  73.8 3.9 %collective-permute-start.23 = (bf16[512,512]{1,0:T(8,128)(2,1)S(1)}, bf16[512,512]{1,0:T(8,128)(2,1)S(1)}, u32[]{:S(2)}, u32[]{:S(2)}) collective-permute-start(bf16[512,512]{1,0:T(8,128)(2,1)S(1)} %graph_layer.5.own), channel_id=1, source_target_pairs={{1,4},{5,8},{4,1},{9,12},{8,5},{12,9},{3,6},{7,10},{6,3},{11,14},{... | collective-permute-start | bytes 1572872 | tf_op jit(solution)/shard_map/ppermute | solution.py:317
  77.7 0.1 collective-permute-start.24
  77.8 6.3 %graph_layer.6 = (bf16[512,256]{1,0:T(8,128)(2,1)S(1)}, bf16[512,256]{1,0:T(8,128)(2,1)S(1)}) custom-call(s32[1]{0:T(128)} %bitcast.5.core_ref, s32[4096]{0:T(1024)S(1)} %bitcast.36, bf16[512,512]{1,0:T(8,128)(2,1)S(1)} %graph_layer.4.own, bf16[512,512]{1,0:T(8,128)(2,1)S(1)} %collective-permute-done.17.sib, ...), custom_call_target="tpu_custom_call" | custom-call | flops 8589934592 | bytes 2621440 | tf_op jit(solution)/shard_map/graph_layer/pallas_call | solution.py:252
  84.2 0.5 collective-permute-start.21
  84.7 3.1 %collective-permute-start.20 = (bf16[512,256]{1,0:T(8,128)(2,1)S(1)}, bf16[512,256]{1,0:T(8,128)(2,1)S(1)}, u32[]{:S(2)}, u32[]{:S(2)}) collective-permute-start(bf16[512,256]{1,0:T(8,128)(2,1)S(1)} %get-tuple-element.109), channel_id=1, source_target_pairs={{0,0},{1,2},{2,1},{3,3},{4,4},{5,6},{6,5},{7,7},{8,8},{9,10},{10,9... | collective-permute-start | bytes 786440 | tf_op jit(solution)/shard_map/ppermute | solution.py:296
  87.8 6.3 %graph_layer.7 = (bf16[512,256]{1,0:T(8,128)(2,1)S(1)}, bf16[512,256]{1,0:T(8,128)(2,1)S(1)}) custom-call(s32[1]{0:T(128)} %bitcast.5.core_ref, s32[4096]{0:T(1024)S(1)} %bitcast.34, bf16[512,512]{1,0:T(8,128)(2,1)S(1)} %graph_layer.5.own, bf16[512,512]{1,0:T(8,128)(2,1)S(1)} %collective-permute-done.22.sib, ...), custom_call_target="tpu_custom_call" | custom-call | flops 8589934592 | bytes 2621440 | tf_op jit(solution)/shard_map/graph_layer/pallas_call | solution.py:252
  94.1 0.0 collective-permute-start.26
  94.1 2.5 %collective-permute-start.25 = (bf16[512,256]{1,0:T(8,128)(2,1)S(1)}, bf16[512,256]{1,0:T(8,128)(2,1)S(1)}, u32[]{:S(2)}, u32[]{:S(2)}) collective-permute-start(bf16[512,256]{1,0:T(8,128)(2,1)S(1)} %get-tuple-element.114), channel_id=1, source_target_pairs={{0,0},{1,2},{2,1},{3,3},{4,4},{5,6},{6,5},{7,7},{8,8},{9,10},{10,9... | collective-permute-start | bytes 786440 | tf_op jit(solution)/shard_map/ppermute | solution.py:296
  96.7 1.0 maximum_select_fusion.2
  97.7 1.9 %collective-permute-done.26 = bf16[512,256]{1,0:T(8,128)(2,1)S(1)} collective-permute-done((bf16[512,256]{1,0:T(8,128)(2,1)S(1)}, bf16[512,256]{1,0:T(8,128)(2,1)S(1)}, u32[]{:S(2)}, u32[]{:S(2)}) %collective-permute-start.26) | collective-permute-done | bytes 262176 | tf_op jit(solution)/shard_map/ppermute | solution.py:297
  99.6 2.6 %collective-permute-done.25 = bf16[512,256]{1,0:T(8,128)(2,1)S(1)} collective-permute-done((bf16[512,256]{1,0:T(8,128)(2,1)S(1)}, bf16[512,256]{1,0:T(8,128)(2,1)S(1)}, u32[]{:S(2)}, u32[]{:S(2)}) %collective-permute-start.25) | collective-permute-done | bytes 262176 | tf_op jit(solution)/shard_map/ppermute | solution.py:296
  102.2 1.0 maximum_select_fusion.3
  (69 shorter events, 0.3 us)
Async XLA Ops:
  0.6 0.7 copy-start.16
  0.7 0.7 copy-start.15
  1.4 1.0 %copy-start = (bf16[1,1024,256]{2,1,0:T(8,128)(2,1)S(1)}, bf16[1,1024,256]{2,1,0:T(8,128)(2,1)}, u32[]{:S(2)}) copy-start(bf16[1,1024,256]{2,1,0:T(8,128)(2,1)} %param.17) | copy-start | bytes 1572868
  2.4 2.3 %copy-start.1 = (bf16[1,1024,256]{2,1,0:T(8,128)(2,1)S(1)}, bf16[1,1024,256]{2,1,0:T(8,128)(2,1)}, u32[]{:S(2)}) copy-start(bf16[1,1024,256]{2,1,0:T(8,128)(2,1)} %param.17) | copy-start | bytes 1572868
  4.7 18.0 %collective-permute-start = (bf16[512,256]{1,0:T(8,128)(2,1)S(1)}, bf16[512,256]{1,0:T(8,128)(2,1)S(1)}, u32[]{:S(2)}, u32[]{:S(2)}) collective-permute-start(bf16[512,256]{1,0:T(8,128)(2,1)S(1)} %get-tuple-element.64), channel_id=1, source_target_pairs={{0,0},{1,2},{2,1},{3,3},{4,4},{5,6},{6,5},{7,7},{8,8},{9,10},{10,9... | collective-permute-start | bytes 786440 | tf_op jit(solution)/shard_map/ppermute | solution.py:290
  9.2 13.5 %collective-permute-start.1 = (bf16[512,256]{1,0:T(8,128)(2,1)S(1)}, bf16[512,256]{1,0:T(8,128)(2,1)S(1)}, u32[]{:S(2)}, u32[]{:S(2)}) collective-permute-start(bf16[512,256]{1,0:T(8,128)(2,1)S(1)} %get-tuple-element.65), channel_id=1, source_target_pairs={{0,1},{1,3},{2,0},{3,2},{4,5},{5,7},{6,4},{7,6},{8,9},{9,11},{10,8... | collective-permute-start | bytes 786440 | tf_op jit(solution)/shard_map/ppermute | solution.py:291
  9.3 9.0 %collective-permute-start.2 = (bf16[272,256]{1,0:T(8,128)(2,1)S(1)}, bf16[272,256]{1,0:T(8,128)(2,1)S(1)}, u32[]{:S(2)}, u32[]{:S(2)}) collective-permute-start(bf16[272,256]{1,0:T(8,128)(2,1)S(1)} %get-tuple-element.68), channel_id=1, source_target_pairs={{0,4},{4,8},{8,12},{12,0},{1,5},{5,9},{9,13},{13,1},{2,6},{6,10},{... | collective-permute-start | bytes 417800 | tf_op jit(solution)/shard_map/ppermute | solution.py:376
  10.6 12.1 %collective-permute-start.3 = (bf16[272,256]{1,0:T(8,128)(2,1)S(1)}, bf16[272,256]{1,0:T(8,128)(2,1)S(1)}, u32[]{:S(2)}, u32[]{:S(2)}) collective-permute-start(bf16[272,256]{1,0:T(8,128)(2,1)S(1)} %get-tuple-element.71), channel_id=1, source_target_pairs={{0,8},{4,12},{8,0},{12,4},{1,9},{5,13},{9,1},{13,5},{2,10},{6,14},... | collective-permute-start | bytes 417800 | tf_op jit(solution)/shard_map/ppermute | solution.py:376
  12.9 9.8 %collective-permute-start.4 = (bf16[272,256]{1,0:T(8,128)(2,1)S(1)}, bf16[272,256]{1,0:T(8,128)(2,1)S(1)}, u32[]{:S(2)}, u32[]{:S(2)}) collective-permute-start(bf16[272,256]{1,0:T(8,128)(2,1)S(1)} %get-tuple-element.72), channel_id=1, source_target_pairs={{0,12},{4,0},{8,4},{12,8},{1,13},{5,1},{9,5},{13,9},{2,14},{6,2},{... | collective-permute-start | bytes 417800 | tf_op jit(solution)/shard_map/ppermute | solution.py:376
  14.0 0.7 copy-start.14
  14.0 0.7 copy-start.13
  14.8 3.4 %copy-start.11 = (s32[1024,8]{0,1:T(8,128)S(1)}, s32[1024,8]{0,1:T(8,128)}, u32[]{:S(2)}) copy-start(s32[1024,8]{0,1:T(8,128)} %param.21) | copy-start | bytes 98308
  14.8 3.4 %copy-start.12 = (s32[1024,8]{0,1:T(8,128)S(1)}, s32[1024,8]{0,1:T(8,128)}, u32[]{:S(2)}) copy-start(s32[1024,8]{0,1:T(8,128)} %param.19) | copy-start | bytes 98308
  18.3 8.4 %copy-start.21 = (bf16[784,256]{1,0:T(8,128)(2,1)S(1)}, bf16[784,256]{1,0:T(8,128)(2,1)}, u32[]{:S(2)}) copy-start(bf16[784,256]{1,0:T(8,128)(2,1)} %get-tuple-element.88) | copy-start | bytes 1204228
  22.8 4.0 %copy-start.2 = (bf16[1,1024,256]{2,1,0:T(8,128)(2,1)S(1)}, bf16[1,1024,256]{2,1,0:T(8,128)(2,1)}, u32[]{:S(2)}) copy-start(bf16[1,1024,256]{2,1,0:T(8,128)(2,1)} %param.18) | copy-start | bytes 1572868
  22.8 17.8 %copy-start.20 = (bf16[784,256]{1,0:T(8,128)(2,1)S(1)}, bf16[784,256]{1,0:T(8,128)(2,1)}, u32[]{:S(2)}) copy-start(bf16[784,256]{1,0:T(8,128)(2,1)} %get-tuple-element.80) | copy-start | bytes 1204228
  22.9 18.6 %collective-permute-start.9 = (bf16[512,512]{1,0:T(8,128)(2,1)S(1)}, bf16[512,512]{1,0:T(8,128)(2,1)S(1)}, u32[]{:S(2)}, u32[]{:S(2)}) collective-permute-start(bf16[512,512]{1,0:T(8,128)(2,1)S(1)} %maximum_select_fusion.own), channel_id=1, source_target_pairs={{0,1},{1,0},{2,3},{3,2},{4,5},{5,4},{6,7},{7,6},{8,9},{9,8},{10,11... | collective-permute-start | bytes 1572872 | tf_op jit(solution)/shard_map/ppermute | solution.py:306
  23.6 17.9 %collective-permute-start.10 = (bf16[512,512]{1,0:T(8,128)(2,1)S(1)}, bf16[512,512]{1,0:T(8,128)(2,1)S(1)}, u32[]{:S(2)}, u32[]{:S(2)}) collective-permute-start(bf16[512,512]{1,0:T(8,128)(2,1)S(1)} %maximum_select_fusion.own), channel_id=1, source_target_pairs={{1,4},{0,13},{5,8},{4,1},{9,12},{8,5},{13,0},{12,9},{3,6},{2,15},{... | collective-permute-start | bytes 1572872 | tf_op jit(solution)/shard_map/ppermute | solution.py:317
  26.7 14.8 %collective-permute-start.11 = (bf16[784,256]{1,0:T(8,128)(2,1)S(1)}, bf16[784,256]{1,0:T(8,128)(2,1)S(1)}, u32[]{:S(2)}, u32[]{:S(2)}) collective-permute-start(bf16[784,256]{1,0:T(8,128)(2,1)S(1)} %copy-done.21), channel_id=1, source_target_pairs={{0,2},{2,0},{1,3},{3,1},{4,6},{6,4},{5,7},{7,5},{8,10},{10,8},{9,1... | collective-permute-start | bytes 1204232 | tf_op jit(solution)/shard_map/ppermute | solution.py:306
  26.8 25.1 %copy-start.19 = (bf16[784,256]{1,0:T(8,128)(2,1)S(1)}, bf16[784,256]{1,0:T(8,128)(2,1)}, u32[]{:S(2)}) copy-start(bf16[784,256]{1,0:T(8,128)(2,1)} %get-tuple-element.82) | copy-start | bytes 1204228
  26.8 28.9 %copy-start.5 = (bf16[2,256,512]{2,1,0:T(8,128)(2,1)S(1)}, bf16[2,256,512]{2,1,0:T(8,128)(2,1)}, u32[]{:S(2)}) copy-start(bf16[2,256,512]{2,1,0:T(8,128)(2,1)} %w2_hbm.6) | copy-start | bytes 1572868
  27.5 13.0 %collective-permute-start.7 = (bf16[512,256]{1,0:T(8,128)(2,1)S(1)}, bf16[512,256]{1,0:T(8,128)(2,1)S(1)}, u32[]{:S(2)}, u32[]{:S(2)}) collective-permute-start(bf16[512,256]{1,0:T(8,128)(2,1)S(1)} %get-tuple-element.84), channel_id=1, source_target_pairs={{0,0},{1,2},{2,1},{3,3},{4,4},{5,6},{6,5},{7,7},{8,8},{9,10},{10,9... | collective-permute-start | bytes 786440 | tf_op jit(solution)/shard_map/ppermute | solution.py:290
  32.5 9.0 %collective-permute-start.8 = (bf16[512,256]{1,0:T(8,128)(2,1)S(1)}, bf16[512,256]{1,0:T(8,128)(2,1)S(1)}, u32[]{:S(2)}, u32[]{:S(2)}) collective-permute-start(bf16[512,256]{1,0:T(8,128)(2,1)S(1)} %get-tuple-element.85), channel_id=1, source_target_pairs={{0,1},{1,3},{2,0},{3,2},{4,5},{5,7},{6,4},{7,6},{8,9},{9,11},{10,8... | collective-permute-start | bytes 786440 | tf_op jit(solution)/shard_map/ppermute | solution.py:291
  40.5 11.4 %collective-permute-start.5 = (bf16[784,256]{1,0:T(8,128)(2,1)S(1)}, bf16[784,256]{1,0:T(8,128)(2,1)S(1)}, u32[]{:S(2)}, u32[]{:S(2)}) collective-permute-start(bf16[784,256]{1,0:T(8,128)(2,1)S(1)} %copy-done.20), channel_id=1, source_target_pairs={{0,2},{2,0},{1,3},{3,1},{4,6},{6,4},{5,7},{7,5},{8,10},{10,8},{9,1... | collective-permute-start | bytes 1204232 | tf_op jit(solution)/shard_map/ppermute | solution.py:306
  41.5 14.1 %collective-permute-start.12 = (bf16[784,256]{1,0:T(8,128)(2,1)S(1)}, bf16[784,256]{1,0:T(8,128)(2,1)S(1)}, u32[]{:S(2)}, u32[]{:S(2)}) collective-permute-start(bf16[784,256]{1,0:T(8,128)(2,1)S(1)} %collective-permute-done.11.near_w), channel_id=1, source_target_pairs={{0,1},{1,0},{2,3},{3,2},{4,5},{5,4},{6,7},{7,6},{8,9},{9,8},{10,11... | collective-permute-start | bytes 1204232 | tf_op jit(solution)/shard_map/ppermute | solution.py:306
  51.9 3.7 %copy-start.9 = (bf16[2,256]{1,0:T(2,128)(2,1)S(1)}, bf16[2,256]{1,0:T(2,128)(2,1)}, u32[]{:S(2)}) copy-start(bf16[2,256]{1,0:T(2,128)(2,1)} %bias.6) | copy-start | bytes 3076
  51.9 3.7 %copy-start.3 = (bf16[2,512,256]{2,1,0:T(8,128)(2,1)S(1)}, bf16[2,512,256]{2,1,0:T(8,128)(2,1)}, u32[]{:S(2)}) copy-start(bf16[2,512,256]{2,1,0:T(8,128)(2,1)} %ws_hbm.6) | copy-start | bytes 1572868
  51.9 3.8 %copy-start.4 = (bf16[2,512,256]{2,1,0:T(8,128)(2,1)S(1)}, bf16[2,512,256]{2,1,0:T(8,128)(2,1)}, u32[]{:S(2)}) copy-start(bf16[2,512,256]{2,1,0:T(8,128)(2,1)} %wd_hbm.6) | copy-start | bytes 1572868
  51.9 10.2 %collective-permute-start.6 = (bf16[784,256]{1,0:T(8,128)(2,1)S(1)}, bf16[784,256]{1,0:T(8,128)(2,1)S(1)}, u32[]{:S(2)}, u32[]{:S(2)}) collective-permute-start(bf16[784,256]{1,0:T(8,128)(2,1)S(1)} %copy-done.19), channel_id=1, source_target_pairs={{0,2},{2,0},{1,3},{3,1},{4,6},{6,4},{5,7},{7,5},{8,10},{10,8},{9,1... | collective-permute-start | bytes 1204232 | tf_op jit(solution)/shard_map/ppermute | solution.py:306
  52.0 12.0 %collective-permute-start.16 = (bf16[784,256]{1,0:T(8,128)(2,1)S(1)}, bf16[784,256]{1,0:T(8,128)(2,1)S(1)}, u32[]{:S(2)}, u32[]{:S(2)}) collective-permute-start(bf16[784,256]{1,0:T(8,128)(2,1)S(1)} %collective-permute-done.5.near_w), channel_id=1, source_target_pairs={{0,1},{1,0},{2,3},{3,2},{4,5},{5,4},{6,7},{7,6},{8,9},{9,8},{10,11... | collective-permute-start | bytes 1204232 | tf_op jit(solution)/shard_map/ppermute | solution.py:306
  53.2 10.9 %copy-start.18 = (bf16[784,256]{1,0:T(8,128)(2,1)S(1)}, bf16[784,256]{1,0:T(8,128)(2,1)}, u32[]{:S(2)}) copy-start(bf16[784,256]{1,0:T(8,128)(2,1)} %get-tuple-element.98) | copy-start | bytes 1204228
  53.2 13.6 %copy-start.6 = (bf16[2,512,256]{2,1,0:T(8,128)(2,1)S(1)}, bf16[2,512,256]{2,1,0:T(8,128)(2,1)}, u32[]{:S(2)}) copy-start(bf16[2,512,256]{2,1,0:T(8,128)(2,1)} %ws_hbm.7) | copy-start | bytes 1572868
  53.2 13.6 %copy-start.7 = (bf16[2,512,256]{2,1,0:T(8,128)(2,1)S(1)}, bf16[2,512,256]{2,1,0:T(8,128)(2,1)}, u32[]{:S(2)}) copy-start(bf16[2,512,256]{2,1,0:T(8,128)(2,1)} %wd_hbm.7) | copy-start | bytes 1572868
  53.2 13.6 %copy-start.8 = (bf16[2,256,512]{2,1,0:T(8,128)(2,1)S(1)}, bf16[2,256,512]{2,1,0:T(8,128)(2,1)}, u32[]{:S(2)}) copy-start(bf16[2,256,512]{2,1,0:T(8,128)(2,1)} %w2_hbm.7) | copy-start | bytes 1572868
  53.2 12.2 %collective-permute-start.14 = (bf16[512,512]{1,0:T(8,128)(2,1)S(1)}, bf16[512,512]{1,0:T(8,128)(2,1)S(1)}, u32[]{:S(2)}, u32[]{:S(2)}) collective-permute-start(bf16[512,512]{1,0:T(8,128)(2,1)S(1)} %maximum_select_fusion.1.own), channel_id=1, source_target_pairs={{0,1},{1,0},{2,3},{3,2},{4,5},{5,4},{6,7},{7,6},{8,9},{9,8},{10,11... | collective-permute-start | bytes 1572872 | tf_op jit(solution)/shard_map/ppermute | solution.py:306
  53.3 13.5 %collective-permute-start.15 = (bf16[512,512]{1,0:T(8,128)(2,1)S(1)}, bf16[512,512]{1,0:T(8,128)(2,1)S(1)}, u32[]{:S(2)}, u32[]{:S(2)}) collective-permute-start(bf16[512,512]{1,0:T(8,128)(2,1)S(1)} %maximum_select_fusion.1.own), channel_id=1, source_target_pairs={{1,4},{5,8},{4,1},{9,12},{8,5},{12,9},{3,6},{7,10},{6,3},{11,14},{... | collective-permute-start | bytes 1572872 | tf_op jit(solution)/shard_map/ppermute | solution.py:317
  61.9 4.9 %copy-start.10 = (bf16[2,256]{1,0:T(2,128)(2,1)S(1)}, bf16[2,256]{1,0:T(2,128)(2,1)}, u32[]{:S(2)}) copy-start(bf16[2,256]{1,0:T(2,128)(2,1)} %bias.7) | copy-start | bytes 3076
  62.0 15.9 %collective-permute-start.17 = (bf16[512,512]{1,0:T(8,128)(2,1)S(1)}, bf16[512,512]{1,0:T(8,128)(2,1)S(1)}, u32[]{:S(2)}, u32[]{:S(2)}) collective-permute-start(bf16[512,512]{1,0:T(8,128)(2,1)S(1)} %graph_layer.4.own), channel_id=1, source_target_pairs={{0,1},{1,0},{2,3},{3,2},{4,5},{5,4},{6,7},{7,6},{8,9},{9,8},{10,11... | collective-permute-start | bytes 1572872 | tf_op jit(solution)/shard_map/ppermute | solution.py:306
  62.1 15.7 %collective-permute-start.18 = (bf16[512,512]{1,0:T(8,128)(2,1)S(1)}, bf16[512,512]{1,0:T(8,128)(2,1)S(1)}, u32[]{:S(2)}, u32[]{:S(2)}) collective-permute-start(bf16[512,512]{1,0:T(8,128)(2,1)S(1)} %graph_layer.4.own), channel_id=1, source_target_pairs={{1,4},{0,13},{5,8},{4,1},{9,12},{8,5},{13,0},{12,9},{3,6},{2,15},{... | collective-permute-start | bytes 1572872 | tf_op jit(solution)/shard_map/ppermute | solution.py:317
  64.0 9.7 %collective-permute-start.13 = (bf16[784,256]{1,0:T(8,128)(2,1)S(1)}, bf16[784,256]{1,0:T(8,128)(2,1)S(1)}, u32[]{:S(2)}, u32[]{:S(2)}) collective-permute-start(bf16[784,256]{1,0:T(8,128)(2,1)S(1)} %copy-done.18), channel_id=1, source_target_pairs={{0,2},{2,0},{1,3},{3,1},{4,6},{6,4},{5,7},{7,5},{8,10},{10,8},{9,1... | collective-permute-start | bytes 1204232 | tf_op jit(solution)/shard_map/ppermute | solution.py:306
  65.4 12.3 %collective-permute-start.19 = (bf16[784,256]{1,0:T(8,128)(2,1)S(1)}, bf16[784,256]{1,0:T(8,128)(2,1)S(1)}, u32[]{:S(2)}, u32[]{:S(2)}) collective-permute-start(bf16[784,256]{1,0:T(8,128)(2,1)S(1)} %collective-permute-done.6.near_w), channel_id=1, source_target_pairs={{0,1},{1,0},{2,3},{3,2},{4,5},{5,4},{6,7},{7,6},{8,9},{9,8},{10,11... | collective-permute-start | bytes 1204232 | tf_op jit(solution)/shard_map/ppermute | solution.py:306
  73.1 14.6 %collective-permute-start.22 = (bf16[512,512]{1,0:T(8,128)(2,1)S(1)}, bf16[512,512]{1,0:T(8,128)(2,1)S(1)}, u32[]{:S(2)}, u32[]{:S(2)}) collective-permute-start(bf16[512,512]{1,0:T(8,128)(2,1)S(1)} %graph_layer.5.own), channel_id=1, source_target_pairs={{0,1},{1,0},{2,3},{3,2},{4,5},{5,4},{6,7},{7,6},{8,9},{9,8},{10,11... | collective-permute-start | bytes 1572872 | tf_op jit(solution)/shard_map/ppermute | solution.py:306
  73.8 14.0 %collective-permute-start.23 = (bf16[512,512]{1,0:T(8,128)(2,1)S(1)}, bf16[512,512]{1,0:T(8,128)(2,1)S(1)}, u32[]{:S(2)}, u32[]{:S(2)}) collective-permute-start(bf16[512,512]{1,0:T(8,128)(2,1)S(1)} %graph_layer.5.own), channel_id=1, source_target_pairs={{1,4},{5,8},{4,1},{9,12},{8,5},{12,9},{3,6},{7,10},{6,3},{11,14},{... | collective-permute-start | bytes 1572872 | tf_op jit(solution)/shard_map/ppermute | solution.py:317
  77.7 10.0 %collective-permute-start.24 = (bf16[784,256]{1,0:T(8,128)(2,1)S(1)}, bf16[784,256]{1,0:T(8,128)(2,1)S(1)}, u32[]{:S(2)}, u32[]{:S(2)}) collective-permute-start(bf16[784,256]{1,0:T(8,128)(2,1)S(1)} %collective-permute-done.13.near_w), channel_id=1, source_target_pairs={{0,1},{1,0},{2,3},{3,2},{4,5},{5,4},{6,7},{7,6},{8,9},{9,8},{10,11... | collective-permute-start | bytes 1204232 | tf_op jit(solution)/shard_map/ppermute | solution.py:306
  84.2 12.5 %collective-permute-start.21 = (bf16[512,256]{1,0:T(8,128)(2,1)S(1)}, bf16[512,256]{1,0:T(8,128)(2,1)S(1)}, u32[]{:S(2)}, u32[]{:S(2)}) collective-permute-start(bf16[512,256]{1,0:T(8,128)(2,1)S(1)} %get-tuple-element.110), channel_id=1, source_target_pairs={{0,2},{1,0},{2,3},{3,1},{4,6},{5,4},{6,7},{7,5},{8,10},{9,8},{10,1... | collective-permute-start | bytes 786440 | tf_op jit(solution)/shard_map/ppermute | solution.py:297
  84.7 12.0 %collective-permute-start.20 = (bf16[512,256]{1,0:T(8,128)(2,1)S(1)}, bf16[512,256]{1,0:T(8,128)(2,1)S(1)}, u32[]{:S(2)}, u32[]{:S(2)}) collective-permute-start(bf16[512,256]{1,0:T(8,128)(2,1)S(1)} %get-tuple-element.109), channel_id=1, source_target_pairs={{0,0},{1,2},{2,1},{3,3},{4,4},{5,6},{6,5},{7,7},{8,8},{9,10},{10,9... | collective-permute-start | bytes 786440 | tf_op jit(solution)/shard_map/ppermute | solution.py:296
  94.1 5.5 %collective-permute-start.26 = (bf16[512,256]{1,0:T(8,128)(2,1)S(1)}, bf16[512,256]{1,0:T(8,128)(2,1)S(1)}, u32[]{:S(2)}, u32[]{:S(2)}) collective-permute-start(bf16[512,256]{1,0:T(8,128)(2,1)S(1)} %get-tuple-element.115), channel_id=1, source_target_pairs={{0,2},{1,0},{2,3},{3,1},{4,6},{5,4},{6,7},{7,5},{8,10},{9,8},{10,1... | collective-permute-start | bytes 786440 | tf_op jit(solution)/shard_map/ppermute | solution.py:297
  94.1 8.0 %collective-permute-start.25 = (bf16[512,256]{1,0:T(8,128)(2,1)S(1)}, bf16[512,256]{1,0:T(8,128)(2,1)S(1)}, u32[]{:S(2)}, u32[]{:S(2)}) collective-permute-start(bf16[512,256]{1,0:T(8,128)(2,1)S(1)} %get-tuple-element.114), channel_id=1, source_target_pairs={{0,0},{1,2},{2,1},{3,3},{4,4},{5,6},{6,5},{7,7},{8,8},{9,10},{10,9... | collective-permute-start | bytes 786440 | tf_op jit(solution)/shard_map/ppermute | solution.py:296
  (1 other events, 0.7 us)

commit v7 on v6

--- a/solution.py
+++ b/solution.py
@@ -382,17 +382,17 @@
     idx = edge_offsets(jnp.stack([g_nbr, r_nbr]), jnp.stack([g_count, r_count]), core)
 
     order = [(graph, layer) for layer in range(layers) for graph in (0, 1)]
+    g_a, g_b, core1 = after((g_a, g_b, core1))
     packs = list(pack_weights(order, core1, g_weights, g_b1, r_weights, r_b1))
-    landed[1], packs[0] = after((landed[1], packs[0]))
     near_w = [swap(packs[0], "mp")]
     g_idx, r_idx = idx[0], idx[1]
-    g_a, g_b, g_idx, r_idx, packs[1], *landed = after((g_a, g_b, g_idx, r_idx, packs[1], *landed))
+    g_a, g_b, g_idx, r_idx, near_w[0], *landed = after((g_a, g_b, g_idx, r_idx, near_w[0], *landed))
     planet = ordered(core, g_a, g_b, 1)
     g_sib, g_rim = swap(planet, "batch"), rims(planet, True)
-    *r_pair, packs[1] = after((*add_force(part.reshape(1), r_own, landed, cap), packs[1]))
+    *r_pair, packs[1], g_sib = after((*add_force(part.reshape(1), r_own, landed, cap), packs[1], g_sib))
     r_a, r_b = spread_rows(*r_pair)
     near_w.append(swap(packs[1], "mp"))
-    r_a, r_b, g_sib, g_rim, near_w[0] = after((r_a, r_b, g_sib, g_rim, near_w[0]))
+    r_a, r_b, g_rim = after((r_a, r_b, g_rim))
     regional, g_idx = after((ordered(core, r_a, r_b, 1), g_idx))
     r_sib, r_rim = swap(regional, "batch"), rims(regional, False)
     for i, (graph, layer) in enumerate(order):

time: 104 us -> 106 us (1.019)
  starting transfers between devices: 39.5 us -> 42 us
    ppermute x4, waiting for transfers between devices: 0.01 us -> 6.33 us  [rims(): return lax.ppermute(own, ('mesh', 'batch'), pairs)]
    ppermute x2, waiting for transfers between devices: 8.02 us -> 1.77 us  [spread_rows(): a = lax.ppermute(same, ('mp', 'batch'), [(0, 0), (1, 2), (2, 1), (3, 3)])]
    ppermute x12, starting transfers between devices: 7.8 us -> 11.1 us  [swap(): return lax.ppermute(values, axis, [(0, 1), (1, 0)])]
    ppermute x3, waiting for transfers between devices: 4.43 us -> 1.66 us  [by_rows(): lax.ppermute(pieces[k], 'mesh', [(i, (i + k) % parts) for i in range(part...]
    ppermute x2, starting transfers between devices: 9.5 us -> 6.87 us  [spread_rows(): a = lax.ppermute(same, ('mp', 'batch'), [(0, 0), (1, 2), (2, 1), (3, 3)])]
    ppermute x12, waiting for transfers between devices: 8.12 us -> 10.6 us  [swap(): return lax.ppermute(values, axis, [(0, 1), (1, 0)])]
    ppermute x4, starting transfers between devices: 11.3 us -> 13.2 us  [rims(): return lax.ppermute(own, ('mesh', 'batch'), pairs)]
    ppermute x2, waiting for transfers between devices: 1.93 us -> 0.77 us  [gather_rows(): other = lax.ppermute(b, ('mp', 'batch'), [(0, 2), (1, 0), (2, 3), (3, 1)])]
  transfers between devices with their start and end apart: 27 -> 27, of which waited for: 7 -> 10; matrix products, arithmetic and copies ran while one was open for 1% -> 1% of each run, Pallas kernels for 28% -> 28%
where the time goes in v7:
time: 106 us
  starting transfers between devices  42 us (40%)
  Pallas kernels  31.5 us (30%)
  waiting for transfers between devices  26.2 us (25%)
  local copies, waits for them, and re-layouts  2.56 us (2%)
  other arithmetic  2.41 us (2%)
  between operations  1.14 us (1%)
    pallas_call x4, Pallas kernels, run_layer(): pl.pallas_call(functools.partial(layer_kernel, layer, slots, last), out_s...  25.2 us
    ppermute x4, starting transfers between devices, rims(): return lax.ppermute(own, ('mesh', 'batch'), pairs)  13.2 us
    ppermute x12, starting transfers between devices, swap(): return lax.ppermute(values, axis, [(0, 1), (1, 0)])  11.1 us
    ppermute x12, waiting for transfers between devices, swap(): return lax.ppermute(values, axis, [(0, 1), (1, 0)])  10.6 us
    ppermute x2, starting transfers between devices, spread_rows(): a = lax.ppermute(same, ('mp', 'batch'), [(0, 0), (1, 2), (2, 1), (3, 3)])  6.87 us
    ppermute x4, waiting for transfers between devices, rims(): return lax.ppermute(own, ('mesh', 'batch'), pairs)  6.33 us
    ppermute x2, starting transfers between devices, gather_rows(): same = lax.ppermute(a, ('mp', 'batch'), [(0, 0), (1, 2), (2, 1), (3, 3)])  5.55 us
    ppermute x3, starting transfers between devices, by_rows(): lax.ppermute(pieces[k], 'mesh', [(i, (i + k) % parts) for i in range(part...  4.72 us
  transfers between devices with their start and end apart: 27, of which 10 were waited for; matrix products, arithmetic and copies ran while one was open for 1% of the time, Pallas kernels for 28%

profile of v7, /device:TPU:1, one launch (start us, length us, event | category | flops | bytes accessed | tf_op | source)
XLA Modules:
  0.0 105.8 jit_solution(6660038470684943892)
XLA Ops:
  0.7 0.7 copy-done.17
  1.4 1.0 copy-done
  2.4 2.2 %pick_rows.1 = (bf16[272,256]{1,0:T(8,128)(2,1)S(1)}, bf16[272,256]{1,0:T(8,128)(2,1)S(1)}, bf16[272,256]{1,0:T(8,128)(2,1)S(1)}, bf16[272,256]{1,0:T(8,128)(2,1)S(1)}) custom-call(s32[1]{0:T(128)} %bitcast.me_ref, s32[3,512]{1,0:T(4,128)S(1)} %pad_add_fusion.bnd_ref, bf16[1024,256]{1,0:T(8,128)(2,1)S(1)} %bitcast.30), custom_call_target="tpu_custom_call" | custom-call | flops 1 | bytes 1 | tf_op jit(solution)/shard_map/pick_rows/pallas_call | solution.py:115
  4.7 4.5 %collective-permute-start = (bf16[512,256]{1,0:T(8,128)(2,1)S(1)}, bf16[512,256]{1,0:T(8,128)(2,1)S(1)}, u32[]{:S(2)}, u32[]{:S(2)}) collective-permute-start(bf16[512,256]{1,0:T(8,128)(2,1)S(1)} %get-tuple-element.61), channel_id=1, source_target_pairs={{0,0},{1,2},{2,1},{3,3},{4,4},{5,6},{6,5},{7,7},{8,8},{9,10},{10,9... | collective-permute-start | bytes 786440 | tf_op jit(solution)/shard_map/ppermute | solution.py:290
  9.2 0.0 collective-permute-start.1
  9.3 1.3 %collective-permute-start.3 = (bf16[272,256]{1,0:T(8,128)(2,1)S(1)}, bf16[272,256]{1,0:T(8,128)(2,1)S(1)}, u32[]{:S(2)}, u32[]{:S(2)}) collective-permute-start(bf16[272,256]{1,0:T(8,128)(2,1)S(1)} %get-tuple-element.71), channel_id=1, source_target_pairs={{0,4},{4,8},{8,12},{12,0},{1,5},{5,9},{9,13},{13,1},{2,6},{6,10},{... | collective-permute-start | bytes 417800 | tf_op jit(solution)/shard_map/ppermute | solution.py:376
  10.6 2.3 %collective-permute-start.4 = (bf16[272,256]{1,0:T(8,128)(2,1)S(1)}, bf16[272,256]{1,0:T(8,128)(2,1)S(1)}, u32[]{:S(2)}, u32[]{:S(2)}) collective-permute-start(bf16[272,256]{1,0:T(8,128)(2,1)S(1)} %get-tuple-element.72), channel_id=1, source_target_pairs={{0,8},{4,12},{8,0},{12,4},{1,9},{5,13},{9,1},{13,5},{2,10},{6,14},... | collective-permute-start | bytes 417800 | tf_op jit(solution)/shard_map/ppermute | solution.py:376
  12.9 1.1 %collective-permute-start.5 = (bf16[272,256]{1,0:T(8,128)(2,1)S(1)}, bf16[272,256]{1,0:T(8,128)(2,1)S(1)}, u32[]{:S(2)}, u32[]{:S(2)}) collective-permute-start(bf16[272,256]{1,0:T(8,128)(2,1)S(1)} %get-tuple-element.73), channel_id=1, source_target_pairs={{0,12},{4,0},{8,4},{12,8},{1,13},{5,1},{9,5},{13,9},{2,14},{6,2},{... | collective-permute-start | bytes 417800 | tf_op jit(solution)/shard_map/ppermute | solution.py:376
  14.0 0.7 copy-done.14
  14.7 0.1 fusion.5
  14.8 0.6 collective-permute-done.1
  15.4 3.4 %pack_weights.1 = (bf16[784,256]{1,0:T(8,128)(2,1)}, bf16[784,256]{1,0:T(8,128)(2,1)}, bf16[784,256]{1,0:T(8,128)(2,1)}, bf16[784,256]{1,0:T(8,128)(2,1)}) custom-call(s32[1]{0:T(128)} %bitcast.5.core_ref, bf16[2,256]{1,0:T(2,128)(2,1)} %bias.6, bf16[2,256]{1,0:T(2,128)(2,1)} %bias.7, bf16[2,512,256]{2,1,0:T(8,128)(2,1)} %ws_hbm.6, ...), custom_call_target="tpu_custom_call" | custom-call | flops 4294967296 | bytes 1 | tf_op jit(solution)/shard_map/pack_weights/pallas_call | solution.py:342
  18.7 2.3 %collective-permute-start.2 = (bf16[784,256]{1,0:T(8,128)(2,1)}, bf16[784,256]{1,0:T(8,128)(2,1)S(1)}, u32[]{:S(2)}, u32[]{:S(2)}) collective-permute-start(bf16[784,256]{1,0:T(8,128)(2,1)} %get-tuple-element.69), channel_id=1, source_target_pairs={{0,2},{2,0},{1,3},{3,1},{4,6},{6,4},{5,7},{7,5},{8,10},{10,8},{9,1... | collective-permute-start | bytes 1204232 | tf_op jit(solution)/shard_map/ppermute | solution.py:306
  21.1 1.7 %collective-permute-done.4.refs_2_ = bf16[272,256]{1,0:T(8,128)(2,1)S(1)} collective-permute-done((bf16[272,256]{1,0:T(8,128)(2,1)S(1)}, bf16[272,256]{1,0:T(8,128)(2,1)S(1)}, u32[]{:S(2)}, u32[]{:S(2)}) %collective-permute-start.4) | collective-permute-done | bytes 139296 | tf_op jit(solution)/shard_map/ppermute | solution.py:376
  22.8 7.1 %collective-permute-done.2.near_w = bf16[784,256]{1,0:T(8,128)(2,1)S(1)} collective-permute-done((bf16[784,256]{1,0:T(8,128)(2,1)}, bf16[784,256]{1,0:T(8,128)(2,1)S(1)}, u32[]{:S(2)}, u32[]{:S(2)}) %collective-permute-start.2) | collective-permute-done | bytes 401440 | tf_op jit(solution)/shard_map/ppermute | solution.py:306
  29.9 0.1 maximum_select_fusion.own
  30.0 1.6 %collective-permute-start.6 = (bf16[512,512]{1,0:T(8,128)(2,1)S(1)}, bf16[512,512]{1,0:T(8,128)(2,1)S(1)}, u32[]{:S(2)}, u32[]{:S(2)}) collective-permute-start(bf16[512,512]{1,0:T(8,128)(2,1)S(1)} %maximum_select_fusion.own), channel_id=1, source_target_pairs={{0,1},{1,0},{2,3},{3,2},{4,5},{5,4},{6,7},{7,6},{8,9},{9,8},{10,11... | collective-permute-start | bytes 1572872 | tf_op jit(solution)/shard_map/ppermute | solution.py:306
  31.7 1.3 %collective-permute-start.11 = (bf16[512,512]{1,0:T(8,128)(2,1)S(1)}, bf16[512,512]{1,0:T(8,128)(2,1)S(1)}, u32[]{:S(2)}, u32[]{:S(2)}) collective-permute-start(bf16[512,512]{1,0:T(8,128)(2,1)S(1)} %maximum_select_fusion.own), channel_id=1, source_target_pairs={{1,4},{0,13},{5,8},{4,1},{9,12},{8,5},{13,0},{12,9},{3,6},{2,15},{... | collective-permute-start | bytes 1572872 | tf_op jit(solution)/shard_map/ppermute | solution.py:317
  32.9 0.7 add_force.1
  33.7 0.7 collective-permute-start.7
  34.4 2.7 %collective-permute-start.12 = (bf16[784,256]{1,0:T(8,128)(2,1)S(1)}, bf16[784,256]{1,0:T(8,128)(2,1)S(1)}, u32[]{:S(2)}, u32[]{:S(2)}) collective-permute-start(bf16[784,256]{1,0:T(8,128)(2,1)S(1)} %collective-permute-done.2.near_w), channel_id=1, source_target_pairs={{0,1},{1,0},{2,3},{3,2},{4,5},{5,4},{6,7},{7,6},{8,9},{9,8},{10,11... | collective-permute-start | bytes 1204232 | tf_op jit(solution)/shard_map/ppermute | solution.py:306
  37.1 2.4 %collective-permute-start.9 = (bf16[512,256]{1,0:T(8,128)(2,1)S(1)}, bf16[512,256]{1,0:T(8,128)(2,1)S(1)}, u32[]{:S(2)}, u32[]{:S(2)}) collective-permute-start(bf16[512,256]{1,0:T(8,128)(2,1)S(1)} %get-tuple-element.87), channel_id=1, source_target_pairs={{0,0},{1,2},{2,1},{3,3},{4,4},{5,6},{6,5},{7,7},{8,8},{9,10},{10,9... | collective-permute-start | bytes 786440 | tf_op jit(solution)/shard_map/ppermute | solution.py:290
  39.5 6.3 %collective-permute-done.11.rim = bf16[512,512]{1,0:T(8,128)(2,1)S(1)} collective-permute-done((bf16[512,512]{1,0:T(8,128)(2,1)S(1)}, bf16[512,512]{1,0:T(8,128)(2,1)S(1)}, u32[]{:S(2)}, u32[]{:S(2)}) %collective-permute-start.11) | collective-permute-done | bytes 524320 | tf_op jit(solution)/shard_map/ppermute | solution.py:317
  45.8 1.8 %collective-permute-done.9 = bf16[512,256]{1,0:T(8,128)(2,1)S(1)} collective-permute-done((bf16[512,256]{1,0:T(8,128)(2,1)S(1)}, bf16[512,256]{1,0:T(8,128)(2,1)S(1)}, u32[]{:S(2)}, u32[]{:S(2)}) %collective-permute-start.9) | collective-permute-done | bytes 262176 | tf_op jit(solution)/shard_map/ppermute | solution.py:290
  47.6 1.5 %collective-permute-done.10 = bf16[512,256]{1,0:T(8,128)(2,1)S(1)} collective-permute-done((bf16[512,256]{1,0:T(8,128)(2,1)S(1)}, bf16[512,256]{1,0:T(8,128)(2,1)S(1)}, u32[]{:S(2)}, u32[]{:S(2)}) %collective-permute-start.10) | collective-permute-done | bytes 262176 | tf_op jit(solution)/shard_map/ppermute | solution.py:291
  49.1 0.1 maximum_select_fusion.1.own
  49.3 2.0 %collective-permute-start.14 = (bf16[512,512]{1,0:T(8,128)(2,1)S(1)}, bf16[512,512]{1,0:T(8,128)(2,1)S(1)}, u32[]{:S(2)}, u32[]{:S(2)}) collective-permute-start(bf16[512,512]{1,0:T(8,128)(2,1)S(1)} %maximum_select_fusion.1.own), channel_id=1, source_target_pairs={{0,1},{1,0},{2,3},{3,2},{4,5},{5,4},{6,7},{7,6},{8,9},{9,8},{10,11... | collective-permute-start | bytes 1572872 | tf_op jit(solution)/shard_map/ppermute | solution.py:306
  51.3 3.1 %collective-permute-start.15 = (bf16[512,512]{1,0:T(8,128)(2,1)S(1)}, bf16[512,512]{1,0:T(8,128)(2,1)S(1)}, u32[]{:S(2)}, u32[]{:S(2)}) collective-permute-start(bf16[512,512]{1,0:T(8,128)(2,1)S(1)} %maximum_select_fusion.1.own), channel_id=1, source_target_pairs={{1,4},{5,8},{4,1},{9,12},{8,5},{12,9},{3,6},{7,10},{6,3},{11,14},{... | collective-permute-start | bytes 1572872 | tf_op jit(solution)/shard_map/ppermute | solution.py:317
  54.5 0.5 collective-permute-start.8
  55.0 6.3 %graph_layer.4.own = bf16[512,512]{1,0:T(8,128)(2,1)S(1)} custom-call(s32[1]{0:T(128)} %bitcast.5.core_ref, s32[4096]{0:T(1024)S(1)} %bitcast.35, bf16[512,512]{1,0:T(8,128)(2,1)S(1)} %maximum_select_fusion.own, bf16[512,512]{1,0:T(8,128)(2,1)S(1)} %collective-permute-done.6.sib, bf16[512,512]{1,0:T(8,128)(2,1)S(1)} %collective-permute-done.11.rim, ...), custom_call_target="tpu_custom_call" | custom-call | flops 8589934592 | bytes 2621440 | tf_op jit(solution)/shard_map/graph_layer/pallas_call | solution.py:252
  61.3 0.6 collective-permute-start.17
  61.9 1.7 %collective-permute-done.8.near_w = bf16[784,256]{1,0:T(8,128)(2,1)S(1)} collective-permute-done((bf16[784,256]{1,0:T(8,128)(2,1)S(1)}, bf16[784,256]{1,0:T(8,128)(2,1)S(1)}, u32[]{:S(2)}, u32[]{:S(2)}) %collective-permute-start.8) | collective-permute-done | bytes 401440 | tf_op jit(solution)/shard_map/ppermute | solution.py:306
  63.6 3.5 %collective-permute-start.18 = (bf16[512,512]{1,0:T(8,128)(2,1)S(1)}, bf16[512,512]{1,0:T(8,128)(2,1)S(1)}, u32[]{:S(2)}, u32[]{:S(2)}) collective-permute-start(bf16[512,512]{1,0:T(8,128)(2,1)S(1)} %graph_layer.4.own), channel_id=1, source_target_pairs={{1,4},{0,13},{5,8},{4,1},{9,12},{8,5},{13,0},{12,9},{3,6},{2,15},{... | collective-permute-start | bytes 1572872 | tf_op jit(solution)/shard_map/ppermute | solution.py:317
  67.1 0.1 collective-permute-start.19
  67.3 6.3 %graph_layer.5.own = bf16[512,512]{1,0:T(8,128)(2,1)S(1)} custom-call(s32[1]{0:T(128)} %bitcast.5.core_ref, s32[4096]{0:T(1024)S(1)} %bitcast.33, bf16[512,512]{1,0:T(8,128)(2,1)S(1)} %maximum_select_fusion.1.own, bf16[512,512]{1,0:T(8,128)(2,1)S(1)} %collective-permute-done.14.sib, bf16[512,512]{1,0:T(8,128)(2,1)S(1)} %collective-permute-done.15.rim, ...), custom_call_target="tpu_custom_call" | custom-call | flops 8589934592 | bytes 2621440 | tf_op jit(solution)/shard_map/graph_layer/pallas_call | solution.py:252
  73.5 0.5 collective-permute-start.22
  74.1 1.7 %collective-permute-done.13.near_w = bf16[784,256]{1,0:T(8,128)(2,1)S(1)} collective-permute-done((bf16[784,256]{1,0:T(8,128)(2,1)S(1)}, bf16[784,256]{1,0:T(8,128)(2,1)S(1)}, u32[]{:S(2)}, u32[]{:S(2)}) %collective-permute-start.13) | collective-permute-done | bytes 401440 | tf_op jit(solution)/shard_map/ppermute | solution.py:306
  75.8 5.3 %collective-permute-start.23 = (bf16[512,512]{1,0:T(8,128)(2,1)S(1)}, bf16[512,512]{1,0:T(8,128)(2,1)S(1)}, u32[]{:S(2)}, u32[]{:S(2)}) collective-permute-start(bf16[512,512]{1,0:T(8,128)(2,1)S(1)} %graph_layer.5.own), channel_id=1, source_target_pairs={{1,4},{5,8},{4,1},{9,12},{8,5},{12,9},{3,6},{7,10},{6,3},{11,14},{... | collective-permute-start | bytes 1572872 | tf_op jit(solution)/shard_map/ppermute | solution.py:317
  81.2 0.1 collective-permute-start.24
  81.3 6.3 %graph_layer.6 = (bf16[512,256]{1,0:T(8,128)(2,1)S(1)}, bf16[512,256]{1,0:T(8,128)(2,1)S(1)}) custom-call(s32[1]{0:T(128)} %bitcast.5.core_ref, s32[4096]{0:T(1024)S(1)} %bitcast.36, bf16[512,512]{1,0:T(8,128)(2,1)S(1)} %graph_layer.4.own, bf16[512,512]{1,0:T(8,128)(2,1)S(1)} %collective-permute-done.17.sib, ...), custom_call_target="tpu_custom_call" | custom-call | flops 8589934592 | bytes 2621440 | tf_op jit(solution)/shard_map/graph_layer/pallas_call | solution.py:252
  87.6 0.5 collective-permute-start.21
  88.1 1.9 %collective-permute-start.20 = (bf16[512,256]{1,0:T(8,128)(2,1)S(1)}, bf16[512,256]{1,0:T(8,128)(2,1)S(1)}, u32[]{:S(2)}, u32[]{:S(2)}) collective-permute-start(bf16[512,256]{1,0:T(8,128)(2,1)S(1)} %get-tuple-element.109), channel_id=1, source_target_pairs={{0,0},{1,2},{2,1},{3,3},{4,4},{5,6},{6,5},{7,7},{8,8},{9,10},{10,9... | collective-permute-start | bytes 786440 | tf_op jit(solution)/shard_map/ppermute | solution.py:296
  90.0 6.3 %graph_layer.7 = (bf16[512,256]{1,0:T(8,128)(2,1)S(1)}, bf16[512,256]{1,0:T(8,128)(2,1)S(1)}) custom-call(s32[1]{0:T(128)} %bitcast.5.core_ref, s32[4096]{0:T(1024)S(1)} %bitcast.34, bf16[512,512]{1,0:T(8,128)(2,1)S(1)} %graph_layer.5.own, bf16[512,512]{1,0:T(8,128)(2,1)S(1)} %collective-permute-done.22.sib, ...), custom_call_target="tpu_custom_call" | custom-call | flops 8589934592 | bytes 2621440 | tf_op jit(solution)/shard_map/graph_layer/pallas_call | solution.py:252
  96.4 3.6 %collective-permute-start.25 = (bf16[512,256]{1,0:T(8,128)(2,1)S(1)}, bf16[512,256]{1,0:T(8,128)(2,1)S(1)}, u32[]{:S(2)}, u32[]{:S(2)}) collective-permute-start(bf16[512,256]{1,0:T(8,128)(2,1)S(1)} %get-tuple-element.114), channel_id=1, source_target_pairs={{0,0},{1,2},{2,1},{3,3},{4,4},{5,6},{6,5},{7,7},{8,8},{9,10},{10,9... | collective-permute-start | bytes 786440 | tf_op jit(solution)/shard_map/ppermute | solution.py:296
  100.1 1.0 maximum_select_fusion.2
  101.1 0.8 collective-permute-done.26
  101.9 3.0 %collective-permute-done.25 = bf16[512,256]{1,0:T(8,128)(2,1)S(1)} collective-permute-done((bf16[512,256]{1,0:T(8,128)(2,1)S(1)}, bf16[512,256]{1,0:T(8,128)(2,1)S(1)}, u32[]{:S(2)}, u32[]{:S(2)}) %collective-permute-start.25) | collective-permute-done | bytes 262176 | tf_op jit(solution)/shard_map/ppermute | solution.py:296
  104.8 1.0 maximum_select_fusion.3
  (67 shorter events, 0.3 us)
Async XLA Ops:
  0.6 0.7 copy-start.17
  0.6 0.7 copy-start.16
  0.7 0.7 copy-start.15
  1.4 1.0 copy-start
  2.4 2.3 %copy-start.1 = (bf16[1,1024,256]{2,1,0:T(8,128)(2,1)S(1)}, bf16[1,1024,256]{2,1,0:T(8,128)(2,1)}, u32[]{:S(2)}) copy-start(bf16[1,1024,256]{2,1,0:T(8,128)(2,1)} %param.17) | copy-start | bytes 1572868
  4.7 10.1 %collective-permute-start = (bf16[512,256]{1,0:T(8,128)(2,1)S(1)}, bf16[512,256]{1,0:T(8,128)(2,1)S(1)}, u32[]{:S(2)}, u32[]{:S(2)}) collective-permute-start(bf16[512,256]{1,0:T(8,128)(2,1)S(1)} %get-tuple-element.61), channel_id=1, source_target_pairs={{0,0},{1,2},{2,1},{3,3},{4,4},{5,6},{6,5},{7,7},{8,8},{9,10},{10,9... | collective-permute-start | bytes 786440 | tf_op jit(solution)/shard_map/ppermute | solution.py:290
  9.2 6.1 %collective-permute-start.1 = (bf16[512,256]{1,0:T(8,128)(2,1)S(1)}, bf16[512,256]{1,0:T(8,128)(2,1)S(1)}, u32[]{:S(2)}, u32[]{:S(2)}) collective-permute-start(bf16[512,256]{1,0:T(8,128)(2,1)S(1)} %get-tuple-element.62), channel_id=1, source_target_pairs={{0,1},{1,3},{2,0},{3,2},{4,5},{5,7},{6,4},{7,6},{8,9},{9,11},{10,8... | collective-permute-start | bytes 786440 | tf_op jit(solution)/shard_map/ppermute | solution.py:291
  9.3 11.8 %collective-permute-start.3 = (bf16[272,256]{1,0:T(8,128)(2,1)S(1)}, bf16[272,256]{1,0:T(8,128)(2,1)S(1)}, u32[]{:S(2)}, u32[]{:S(2)}) collective-permute-start(bf16[272,256]{1,0:T(8,128)(2,1)S(1)} %get-tuple-element.71), channel_id=1, source_target_pairs={{0,4},{4,8},{8,12},{12,0},{1,5},{5,9},{9,13},{13,1},{2,6},{6,10},{... | collective-permute-start | bytes 417800 | tf_op jit(solution)/shard_map/ppermute | solution.py:376
  10.6 12.1 %collective-permute-start.4 = (bf16[272,256]{1,0:T(8,128)(2,1)S(1)}, bf16[272,256]{1,0:T(8,128)(2,1)S(1)}, u32[]{:S(2)}, u32[]{:S(2)}) collective-permute-start(bf16[272,256]{1,0:T(8,128)(2,1)S(1)} %get-tuple-element.72), channel_id=1, source_target_pairs={{0,8},{4,12},{8,0},{12,4},{1,9},{5,13},{9,1},{13,5},{2,10},{6,14},... | collective-permute-start | bytes 417800 | tf_op jit(solution)/shard_map/ppermute | solution.py:376
  12.9 9.8 %collective-permute-start.5 = (bf16[272,256]{1,0:T(8,128)(2,1)S(1)}, bf16[272,256]{1,0:T(8,128)(2,1)S(1)}, u32[]{:S(2)}, u32[]{:S(2)}) collective-permute-start(bf16[272,256]{1,0:T(8,128)(2,1)S(1)} %get-tuple-element.73), channel_id=1, source_target_pairs={{0,12},{4,0},{8,4},{12,8},{1,13},{5,1},{9,5},{13,9},{2,14},{6,2},{... | collective-permute-start | bytes 417800 | tf_op jit(solution)/shard_map/ppermute | solution.py:376
  14.0 0.7 copy-start.14
  14.0 0.7 copy-start.13
  14.8 6.2 %copy-start.11 = (s32[1024,8]{0,1:T(8,128)S(1)}, s32[1024,8]{0,1:T(8,128)}, u32[]{:S(2)}) copy-start(s32[1024,8]{0,1:T(8,128)} %param.21) | copy-start | bytes 98308
  14.8 6.2 %copy-start.12 = (s32[1024,8]{0,1:T(8,128)S(1)}, s32[1024,8]{0,1:T(8,128)}, u32[]{:S(2)}) copy-start(s32[1024,8]{0,1:T(8,128)} %param.19) | copy-start | bytes 98308
  18.7 11.1 %collective-permute-start.2 = (bf16[784,256]{1,0:T(8,128)(2,1)}, bf16[784,256]{1,0:T(8,128)(2,1)S(1)}, u32[]{:S(2)}, u32[]{:S(2)}) collective-permute-start(bf16[784,256]{1,0:T(8,128)(2,1)} %get-tuple-element.69), channel_id=1, source_target_pairs={{0,2},{2,0},{1,3},{3,1},{4,6},{6,4},{5,7},{7,5},{8,10},{10,8},{9,1... | collective-permute-start | bytes 1204232 | tf_op jit(solution)/shard_map/ppermute | solution.py:306
  29.9 3.0 %copy-start.2 = (bf16[1,1024,256]{2,1,0:T(8,128)(2,1)S(1)}, bf16[1,1024,256]{2,1,0:T(8,128)(2,1)}, u32[]{:S(2)}) copy-start(bf16[1,1024,256]{2,1,0:T(8,128)(2,1)} %param.18) | copy-start | bytes 1572868
  29.9 3.8 %copy-start.20 = (bf16[784,256]{1,0:T(8,128)(2,1)S(1)}, bf16[784,256]{1,0:T(8,128)(2,1)}, u32[]{:S(2)}) copy-start(bf16[784,256]{1,0:T(8,128)(2,1)} %get-tuple-element.83) | copy-start | bytes 1204228
  30.0 3.6 %collective-permute-start.6 = (bf16[512,512]{1,0:T(8,128)(2,1)S(1)}, bf16[512,512]{1,0:T(8,128)(2,1)S(1)}, u32[]{:S(2)}, u32[]{:S(2)}) collective-permute-start(bf16[512,512]{1,0:T(8,128)(2,1)S(1)} %maximum_select_fusion.own), channel_id=1, source_target_pairs={{0,1},{1,0},{2,3},{3,2},{4,5},{5,4},{6,7},{7,6},{8,9},{9,8},{10,11... | collective-permute-start | bytes 1572872 | tf_op jit(solution)/shard_map/ppermute | solution.py:306
  31.7 14.1 %collective-permute-start.11 = (bf16[512,512]{1,0:T(8,128)(2,1)S(1)}, bf16[512,512]{1,0:T(8,128)(2,1)S(1)}, u32[]{:S(2)}, u32[]{:S(2)}) collective-permute-start(bf16[512,512]{1,0:T(8,128)(2,1)S(1)} %maximum_select_fusion.own), channel_id=1, source_target_pairs={{1,4},{0,13},{5,8},{4,1},{9,12},{8,5},{13,0},{12,9},{3,6},{2,15},{... | collective-permute-start | bytes 1572872 | tf_op jit(solution)/shard_map/ppermute | solution.py:317
  32.9 21.5 %copy-start.19 = (bf16[784,256]{1,0:T(8,128)(2,1)S(1)}, bf16[784,256]{1,0:T(8,128)(2,1)}, u32[]{:S(2)}) copy-start(bf16[784,256]{1,0:T(8,128)(2,1)} %get-tuple-element.85) | copy-start | bytes 1204228
  32.9 22.0 %copy-start.5 = (bf16[2,256,512]{2,1,0:T(8,128)(2,1)S(1)}, bf16[2,256,512]{2,1,0:T(8,128)(2,1)}, u32[]{:S(2)}) copy-start(bf16[2,256,512]{2,1,0:T(8,128)(2,1)} %w2_hbm.6) | copy-start | bytes 1572868
  33.7 21.3 %copy-start.3 = (bf16[2,512,256]{2,1,0:T(8,128)(2,1)S(1)}, bf16[2,512,256]{2,1,0:T(8,128)(2,1)}, u32[]{:S(2)}) copy-start(bf16[2,512,256]{2,1,0:T(8,128)(2,1)} %ws_hbm.6) | copy-start | bytes 1572868
  33.7 21.3 %copy-start.4 = (bf16[2,512,256]{2,1,0:T(8,128)(2,1)S(1)}, bf16[2,512,256]{2,1,0:T(8,128)(2,1)}, u32[]{:S(2)}) copy-start(bf16[2,512,256]{2,1,0:T(8,128)(2,1)} %wd_hbm.6) | copy-start | bytes 1572868
  33.7 20.7 %collective-permute-start.7 = (bf16[784,256]{1,0:T(8,128)(2,1)S(1)}, bf16[784,256]{1,0:T(8,128)(2,1)S(1)}, u32[]{:S(2)}, u32[]{:S(2)}) collective-permute-start(bf16[784,256]{1,0:T(8,128)(2,1)S(1)} %copy-done.20), channel_id=1, source_target_pairs={{0,2},{2,0},{1,3},{3,1},{4,6},{6,4},{5,7},{7,5},{8,10},{10,8},{9,1... | collective-permute-start | bytes 1204232 | tf_op jit(solution)/shard_map/ppermute | solution.py:306
  34.4 20.6 %collective-permute-start.12 = (bf16[784,256]{1,0:T(8,128)(2,1)S(1)}, bf16[784,256]{1,0:T(8,128)(2,1)S(1)}, u32[]{:S(2)}, u32[]{:S(2)}) collective-permute-start(bf16[784,256]{1,0:T(8,128)(2,1)S(1)} %collective-permute-done.2.near_w), channel_id=1, source_target_pairs={{0,1},{1,0},{2,3},{3,2},{4,5},{5,4},{6,7},{7,6},{8,9},{9,8},{10,11... | collective-permute-start | bytes 1204232 | tf_op jit(solution)/shard_map/ppermute | solution.py:306
  37.1 10.5 %collective-permute-start.9 = (bf16[512,256]{1,0:T(8,128)(2,1)S(1)}, bf16[512,256]{1,0:T(8,128)(2,1)S(1)}, u32[]{:S(2)}, u32[]{:S(2)}) collective-permute-start(bf16[512,256]{1,0:T(8,128)(2,1)S(1)} %get-tuple-element.87), channel_id=1, source_target_pairs={{0,0},{1,2},{2,1},{3,3},{4,4},{5,6},{6,5},{7,7},{8,8},{9,10},{10,9... | collective-permute-start | bytes 786440 | tf_op jit(solution)/shard_map/ppermute | solution.py:290
  39.5 9.7 %collective-permute-start.10 = (bf16[512,256]{1,0:T(8,128)(2,1)S(1)}, bf16[512,256]{1,0:T(8,128)(2,1)S(1)}, u32[]{:S(2)}, u32[]{:S(2)}) collective-permute-start(bf16[512,256]{1,0:T(8,128)(2,1)S(1)} %get-tuple-element.88), channel_id=1, source_target_pairs={{0,1},{1,3},{2,0},{3,2},{4,5},{5,7},{6,4},{7,6},{8,9},{9,11},{10,8... | collective-permute-start | bytes 786440 | tf_op jit(solution)/shard_map/ppermute | solution.py:291
  49.2 5.7 %copy-start.9 = (bf16[2,256]{1,0:T(2,128)(2,1)S(1)}, bf16[2,256]{1,0:T(2,128)(2,1)}, u32[]{:S(2)}) copy-start(bf16[2,256]{1,0:T(2,128)(2,1)} %bias.6) | copy-start | bytes 3076
  49.3 17.9 %collective-permute-start.14 = (bf16[512,512]{1,0:T(8,128)(2,1)S(1)}, bf16[512,512]{1,0:T(8,128)(2,1)S(1)}, u32[]{:S(2)}, u32[]{:S(2)}) collective-permute-start(bf16[512,512]{1,0:T(8,128)(2,1)S(1)} %maximum_select_fusion.1.own), channel_id=1, source_target_pairs={{0,1},{1,0},{2,3},{3,2},{4,5},{5,4},{6,7},{7,6},{8,9},{9,8},{10,11... | collective-permute-start | bytes 1572872 | tf_op jit(solution)/shard_map/ppermute | solution.py:306
  51.3 15.9 %collective-permute-start.15 = (bf16[512,512]{1,0:T(8,128)(2,1)S(1)}, bf16[512,512]{1,0:T(8,128)(2,1)S(1)}, u32[]{:S(2)}, u32[]{:S(2)}) collective-permute-start(bf16[512,512]{1,0:T(8,128)(2,1)S(1)} %maximum_select_fusion.1.own), channel_id=1, source_target_pairs={{1,4},{5,8},{4,1},{9,12},{8,5},{12,9},{3,6},{7,10},{6,3},{11,14},{... | collective-permute-start | bytes 1572872 | tf_op jit(solution)/shard_map/ppermute | solution.py:317
  54.4 12.7 %copy-start.18 = (bf16[784,256]{1,0:T(8,128)(2,1)S(1)}, bf16[784,256]{1,0:T(8,128)(2,1)}, u32[]{:S(2)}) copy-start(bf16[784,256]{1,0:T(8,128)(2,1)} %get-tuple-element.98) | copy-start | bytes 1204228
  54.4 12.8 %copy-start.6 = (bf16[2,512,256]{2,1,0:T(8,128)(2,1)S(1)}, bf16[2,512,256]{2,1,0:T(8,128)(2,1)}, u32[]{:S(2)}) copy-start(bf16[2,512,256]{2,1,0:T(8,128)(2,1)} %ws_hbm.7) | copy-start | bytes 1572868
  54.4 12.8 %copy-start.7 = (bf16[2,512,256]{2,1,0:T(8,128)(2,1)S(1)}, bf16[2,512,256]{2,1,0:T(8,128)(2,1)}, u32[]{:S(2)}) copy-start(bf16[2,512,256]{2,1,0:T(8,128)(2,1)} %wd_hbm.7) | copy-start | bytes 1572868
  54.5 12.8 %copy-start.8 = (bf16[2,256,512]{2,1,0:T(8,128)(2,1)S(1)}, bf16[2,256,512]{2,1,0:T(8,128)(2,1)}, u32[]{:S(2)}) copy-start(bf16[2,256,512]{2,1,0:T(8,128)(2,1)} %w2_hbm.7) | copy-start | bytes 1572868
  54.5 9.1 %collective-permute-start.8 = (bf16[784,256]{1,0:T(8,128)(2,1)S(1)}, bf16[784,256]{1,0:T(8,128)(2,1)S(1)}, u32[]{:S(2)}, u32[]{:S(2)}) collective-permute-start(bf16[784,256]{1,0:T(8,128)(2,1)S(1)} %copy-done.19), channel_id=1, source_target_pairs={{0,2},{2,0},{1,3},{3,1},{4,6},{6,4},{5,7},{7,5},{8,10},{10,8},{9,1... | collective-permute-start | bytes 1204232 | tf_op jit(solution)/shard_map/ppermute | solution.py:306
  54.9 12.3 %collective-permute-start.16 = (bf16[784,256]{1,0:T(8,128)(2,1)S(1)}, bf16[784,256]{1,0:T(8,128)(2,1)S(1)}, u32[]{:S(2)}, u32[]{:S(2)}) collective-permute-start(bf16[784,256]{1,0:T(8,128)(2,1)S(1)} %collective-permute-done.7.near_w), channel_id=1, source_target_pairs={{0,1},{1,0},{2,3},{3,2},{4,5},{5,4},{6,7},{7,6},{8,9},{9,8},{10,11... | collective-permute-start | bytes 1204232 | tf_op jit(solution)/shard_map/ppermute | solution.py:306
  61.3 6.0 %copy-start.10 = (bf16[2,256]{1,0:T(2,128)(2,1)S(1)}, bf16[2,256]{1,0:T(2,128)(2,1)}, u32[]{:S(2)}) copy-start(bf16[2,256]{1,0:T(2,128)(2,1)} %bias.7) | copy-start | bytes 3076
  61.3 19.9 %collective-permute-start.17 = (bf16[512,512]{1,0:T(8,128)(2,1)S(1)}, bf16[512,512]{1,0:T(8,128)(2,1)S(1)}, u32[]{:S(2)}, u32[]{:S(2)}) collective-permute-start(bf16[512,512]{1,0:T(8,128)(2,1)S(1)} %graph_layer.4.own), channel_id=1, source_target_pairs={{0,1},{1,0},{2,3},{3,2},{4,5},{5,4},{6,7},{7,6},{8,9},{9,8},{10,11... | collective-permute-start | bytes 1572872 | tf_op jit(solution)/shard_map/ppermute | solution.py:306
  63.6 17.6 %collective-permute-start.18 = (bf16[512,512]{1,0:T(8,128)(2,1)S(1)}, bf16[512,512]{1,0:T(8,128)(2,1)S(1)}, u32[]{:S(2)}, u32[]{:S(2)}) collective-permute-start(bf16[512,512]{1,0:T(8,128)(2,1)S(1)} %graph_layer.4.own), channel_id=1, source_target_pairs={{1,4},{0,13},{5,8},{4,1},{9,12},{8,5},{13,0},{12,9},{3,6},{2,15},{... | collective-permute-start | bytes 1572872 | tf_op jit(solution)/shard_map/ppermute | solution.py:317
  67.1 8.7 %collective-permute-start.13 = (bf16[784,256]{1,0:T(8,128)(2,1)S(1)}, bf16[784,256]{1,0:T(8,128)(2,1)S(1)}, u32[]{:S(2)}, u32[]{:S(2)}) collective-permute-start(bf16[784,256]{1,0:T(8,128)(2,1)S(1)} %copy-done.18), channel_id=1, source_target_pairs={{0,2},{2,0},{1,3},{3,1},{4,6},{6,4},{5,7},{7,5},{8,10},{10,8},{9,1... | collective-permute-start | bytes 1204232 | tf_op jit(solution)/shard_map/ppermute | solution.py:306
  67.1 14.1 %collective-permute-start.19 = (bf16[784,256]{1,0:T(8,128)(2,1)S(1)}, bf16[784,256]{1,0:T(8,128)(2,1)S(1)}, u32[]{:S(2)}, u32[]{:S(2)}) collective-permute-start(bf16[784,256]{1,0:T(8,128)(2,1)S(1)} %collective-permute-done.8.near_w), channel_id=1, source_target_pairs={{0,1},{1,0},{2,3},{3,2},{4,5},{5,4},{6,7},{7,6},{8,9},{9,8},{10,11... | collective-permute-start | bytes 1204232 | tf_op jit(solution)/shard_map/ppermute | solution.py:306
  73.5 16.5 %collective-permute-start.22 = (bf16[512,512]{1,0:T(8,128)(2,1)S(1)}, bf16[512,512]{1,0:T(8,128)(2,1)S(1)}, u32[]{:S(2)}, u32[]{:S(2)}) collective-permute-start(bf16[512,512]{1,0:T(8,128)(2,1)S(1)} %graph_layer.5.own), channel_id=1, source_target_pairs={{0,1},{1,0},{2,3},{3,2},{4,5},{5,4},{6,7},{7,6},{8,9},{9,8},{10,11... | collective-permute-start | bytes 1572872 | tf_op jit(solution)/shard_map/ppermute | solution.py:306
  75.8 14.2 %collective-permute-start.23 = (bf16[512,512]{1,0:T(8,128)(2,1)S(1)}, bf16[512,512]{1,0:T(8,128)(2,1)S(1)}, u32[]{:S(2)}, u32[]{:S(2)}) collective-permute-start(bf16[512,512]{1,0:T(8,128)(2,1)S(1)} %graph_layer.5.own), channel_id=1, source_target_pairs={{1,4},{5,8},{4,1},{9,12},{8,5},{12,9},{3,6},{7,10},{6,3},{11,14},{... | collective-permute-start | bytes 1572872 | tf_op jit(solution)/shard_map/ppermute | solution.py:317
  81.2 8.9 %collective-permute-start.24 = (bf16[784,256]{1,0:T(8,128)(2,1)S(1)}, bf16[784,256]{1,0:T(8,128)(2,1)S(1)}, u32[]{:S(2)}, u32[]{:S(2)}) collective-permute-start(bf16[784,256]{1,0:T(8,128)(2,1)S(1)} %collective-permute-done.13.near_w), channel_id=1, source_target_pairs={{0,1},{1,0},{2,3},{3,2},{4,5},{5,4},{6,7},{7,6},{8,9},{9,8},{10,11... | collective-permute-start | bytes 1204232 | tf_op jit(solution)/shard_map/ppermute | solution.py:306
  87.6 12.5 %collective-permute-start.21 = (bf16[512,256]{1,0:T(8,128)(2,1)S(1)}, bf16[512,256]{1,0:T(8,128)(2,1)S(1)}, u32[]{:S(2)}, u32[]{:S(2)}) collective-permute-start(bf16[512,256]{1,0:T(8,128)(2,1)S(1)} %get-tuple-element.110), channel_id=1, source_target_pairs={{0,2},{1,0},{2,3},{3,1},{4,6},{5,4},{6,7},{7,5},{8,10},{9,8},{10,1... | collective-permute-start | bytes 786440 | tf_op jit(solution)/shard_map/ppermute | solution.py:297
  88.1 12.0 %collective-permute-start.20 = (bf16[512,256]{1,0:T(8,128)(2,1)S(1)}, bf16[512,256]{1,0:T(8,128)(2,1)S(1)}, u32[]{:S(2)}, u32[]{:S(2)}) collective-permute-start(bf16[512,256]{1,0:T(8,128)(2,1)S(1)} %get-tuple-element.109), channel_id=1, source_target_pairs={{0,0},{1,2},{2,1},{3,3},{4,4},{5,6},{6,5},{7,7},{8,8},{9,10},{10,9... | collective-permute-start | bytes 786440 | tf_op jit(solution)/shard_map/ppermute | solution.py:296
  96.4 5.5 %collective-permute-start.26 = (bf16[512,256]{1,0:T(8,128)(2,1)S(1)}, bf16[512,256]{1,0:T(8,128)(2,1)S(1)}, u32[]{:S(2)}, u32[]{:S(2)}) collective-permute-start(bf16[512,256]{1,0:T(8,128)(2,1)S(1)} %get-tuple-element.115), channel_id=1, source_target_pairs={{0,2},{1,0},{2,3},{3,1},{4,6},{5,4},{6,7},{7,5},{8,10},{9,8},{10,1... | collective-permute-start | bytes 786440 | tf_op jit(solution)/shard_map/ppermute | solution.py:297
  96.4 8.4 %collective-permute-start.25 = (bf16[512,256]{1,0:T(8,128)(2,1)S(1)}, bf16[512,256]{1,0:T(8,128)(2,1)S(1)}, u32[]{:S(2)}, u32[]{:S(2)}) collective-permute-start(bf16[512,256]{1,0:T(8,128)(2,1)S(1)} %get-tuple-element.114), channel_id=1, source_target_pairs={{0,0},{1,2},{2,1},{3,3},{4,4},{5,6},{6,5},{7,7},{8,8},{9,10},{10,9... | collective-permute-start | bytes 786440 | tf_op jit(solution)/shard_map/ppermute | solution.py:296

commit v8 on v6

--- a/solution.py
+++ b/solution.py
@@ -398,16 +398,11 @@
     for i, (graph, layer) in enumerate(order):
         last = layer == layers - 1
         far_w = swap(near_w[i], "batch")
-        if i + 1 < len(order):
-            near_w[i + 1], core1 = after((near_w[i + 1], core1))
-        if i + 2 < len(order):
-            packs[i + 2], near_w[i + 1] = after((packs[i + 2], near_w[i + 1]))
-            near_w.append(swap(packs[i + 2], "mp"))
         if graph == 0:
             planet = run_layer(
                 layer, slots, last, core1, g_idx, planet, g_sib, g_rim, g_ws, g_wd, g_w2, g_b1, near_w[i], far_w
             )
-            *planet, core1 = after((*(planet if last else (planet,)), core1))
+            *planet, core1, near_w[i + 1] = after((*(planet if last else (planet,)), core1, near_w[i + 1]))
             if not last:
                 planet = planet[0]
                 g_sib, g_rim = swap(planet, "batch"), rims(planet, True)
@@ -416,8 +411,11 @@
                 layer, slots, last, core1, r_idx, regional, r_sib, r_rim, r_ws, r_wd, r_w2, r_b1, near_w[i], far_w
             )
             if not last:
-                regional, core1 = after((regional, core1))
+                regional, core1, near_w[i + 1] = after((regional, core1, near_w[i + 1]))
                 r_sib, r_rim = swap(regional, "batch"), rims(regional, False)
+        if i + 2 < len(order):
+            packs[i + 2], near_w[i + 1] = after((packs[i + 2], near_w[i + 1]))
+            near_w.append(swap(packs[i + 2], "mp"))
     g_out = ordered(part, *gather_rows(*planet), 0)
     r_out = ordered(part, *gather_rows(*regional), 0)
     return g_out[None], r_out[None]

time: 104 us -> 101 us (0.971)
  waiting for transfers between devices: 26 us -> 22.1 us
    ppermute x2, waiting for transfers between devices: 2.55 us -> 6.97 us  [gather_rows(): same = lax.ppermute(a, ('mp', 'batch'), [(0, 0), (1, 2), (2, 1), (3, 3)])]
    ppermute x3, waiting for transfers between devices: 4.43 us -> 1.02 us  [by_rows(): lax.ppermute(pieces[k], 'mesh', [(i, (i + k) % parts) for i in range(part...]
    ppermute x4, starting transfers between devices: 11.3 us -> 8.88 us  [rims(): return lax.ppermute(own, ('mesh', 'batch'), pairs)]
    ppermute x12, waiting for transfers between devices: 8.12 us -> 5.85 us  [swap(): return lax.ppermute(values, axis, [(0, 1), (1, 0)])]
    ppermute x12, starting transfers between devices: 7.8 us -> 9.92 us  [swap(): return lax.ppermute(values, axis, [(0, 1), (1, 0)])]
    ppermute x2, waiting for transfers between devices: 1.93 us -> 0.01 us  [gather_rows(): other = lax.ppermute(b, ('mp', 'batch'), [(0, 2), (1, 0), (2, 3), (3, 1)])]
  transfers between devices with their start and end apart: 27 -> 27, of which waited for: 7 -> 7; matrix products, arithmetic and copies ran while one was open for 1% -> 1% of each run, Pallas kernels for 28% -> 29%
where the time goes in v8:
time: 101 us; the launch traced here: 99.4 us
  starting transfers between devices  39.7 us (39%)
  Pallas kernels  31.6 us (31%)
  waiting for transfers between devices  22.1 us (22%)
  local copies, waits for them, and re-layouts  2.56 us (3%)
  other arithmetic  2.42 us (2%)
  between operations  1.11 us (1%)
    pallas_call x4, Pallas kernels, run_layer(): pl.pallas_call(functools.partial(layer_kernel, layer, slots, last), out_s...  25.2 us
    ppermute x12, starting transfers between devices, swap(): return lax.ppermute(values, axis, [(0, 1), (1, 0)])  9.92 us
    ppermute x2, starting transfers between devices, spread_rows(): a = lax.ppermute(same, ('mp', 'batch'), [(0, 0), (1, 2), (2, 1), (3, 3)])  9.65 us
    ppermute x4, starting transfers between devices, rims(): return lax.ppermute(own, ('mesh', 'batch'), pairs)  8.88 us
    ppermute x2, waiting for transfers between devices, spread_rows(): a = lax.ppermute(same, ('mp', 'batch'), [(0, 0), (1, 2), (2, 1), (3, 3)])  7.36 us
    ppermute x2, waiting for transfers between devices, gather_rows(): same = lax.ppermute(a, ('mp', 'batch'), [(0, 0), (1, 2), (2, 1), (3, 3)])  6.97 us
    ppermute x12, waiting for transfers between devices, swap(): return lax.ppermute(values, axis, [(0, 1), (1, 0)])  5.85 us
    ppermute x3, starting transfers between devices, by_rows(): lax.ppermute(pieces[k], 'mesh', [(i, (i + k) % parts) for i in range(part...  5.61 us
  transfers between devices with their start and end apart: 27, of which 7 were waited for; matrix products, arithmetic and copies ran while one was open for 1% of the time, Pallas kernels for 29%

profile of v8, /device:TPU:1, one launch (start us, length us, event | category | flops | bytes accessed | tf_op | source)
XLA Modules:
  0.0 99.4 jit_solution(12427214502845237672)
XLA Ops:
  0.7 0.7 copy-done.17
  1.3 0.0 copy-done.16
  1.3 0.0 copy-done.15
  1.4 1.0 %copy-done = bf16[1,1024,256]{2,1,0:T(8,128)(2,1)S(1)} copy-done((bf16[1,1024,256]{2,1,0:T(8,128)(2,1)S(1)}, bf16[1,1024,256]{2,1,0:T(8,128)(2,1)}, u32[]{:S(2)}) %copy-start) | copy-done | bytes 524312
  2.4 2.2 %pick_rows.1 = (bf16[272,256]{1,0:T(8,128)(2,1)S(1)}, bf16[272,256]{1,0:T(8,128)(2,1)S(1)}, bf16[272,256]{1,0:T(8,128)(2,1)S(1)}, bf16[272,256]{1,0:T(8,128)(2,1)S(1)}) custom-call(s32[1]{0:T(128)} %bitcast.me_ref, s32[3,512]{1,0:T(4,128)S(1)} %pad_add_fusion.bnd_ref, bf16[1024,256]{1,0:T(8,128)(2,1)S(1)} %bitcast.30), custom_call_target="tpu_custom_call" | custom-call | flops 1 | bytes 1 | tf_op jit(solution)/shard_map/pick_rows/pallas_call | solution.py:115
  4.7 2.2 %collective-permute-start.2 = (bf16[272,256]{1,0:T(8,128)(2,1)S(1)}, bf16[272,256]{1,0:T(8,128)(2,1)S(1)}, u32[]{:S(2)}, u32[]{:S(2)}) collective-permute-start(bf16[272,256]{1,0:T(8,128)(2,1)S(1)} %get-tuple-element.63), channel_id=1, source_target_pairs={{0,4},{4,8},{8,12},{12,0},{1,5},{5,9},{9,13},{13,1},{2,6},{6,10},{... | collective-permute-start | bytes 417800 | tf_op jit(solution)/shard_map/ppermute | solution.py:376
  6.9 4.0 %collective-permute-start = (bf16[512,256]{1,0:T(8,128)(2,1)S(1)}, bf16[512,256]{1,0:T(8,128)(2,1)S(1)}, u32[]{:S(2)}, u32[]{:S(2)}) collective-permute-start(bf16[512,256]{1,0:T(8,128)(2,1)S(1)} %get-tuple-element.59), channel_id=1, source_target_pairs={{0,0},{1,2},{2,1},{3,3},{4,4},{5,6},{6,5},{7,7},{8,8},{9,10},{10,9... | collective-permute-start | bytes 786440 | tf_op jit(solution)/shard_map/ppermute | solution.py:290
  10.9 0.0 collective-permute-start.1
  10.9 2.4 %collective-permute-start.3 = (bf16[272,256]{1,0:T(8,128)(2,1)S(1)}, bf16[272,256]{1,0:T(8,128)(2,1)S(1)}, u32[]{:S(2)}, u32[]{:S(2)}) collective-permute-start(bf16[272,256]{1,0:T(8,128)(2,1)S(1)} %get-tuple-element.66), channel_id=1, source_target_pairs={{0,8},{4,12},{8,0},{12,4},{1,9},{5,13},{9,1},{13,5},{2,10},{6,14},... | collective-permute-start | bytes 417800 | tf_op jit(solution)/shard_map/ppermute | solution.py:376
  13.2 1.1 %collective-permute-start.4 = (bf16[272,256]{1,0:T(8,128)(2,1)S(1)}, bf16[272,256]{1,0:T(8,128)(2,1)S(1)}, u32[]{:S(2)}, u32[]{:S(2)}) collective-permute-start(bf16[272,256]{1,0:T(8,128)(2,1)S(1)} %get-tuple-element.67), channel_id=1, source_target_pairs={{0,12},{4,0},{8,4},{12,8},{1,13},{5,1},{9,5},{13,9},{2,14},{6,2},{... | collective-permute-start | bytes 417800 | tf_op jit(solution)/shard_map/ppermute | solution.py:376
  14.3 0.7 copy-done.14
  15.0 0.0 copy-done.13
  15.0 0.1 fusion.5
  15.1 3.4 %pack_weights.1 = (bf16[784,256]{1,0:T(8,128)(2,1)}, bf16[784,256]{1,0:T(8,128)(2,1)}, bf16[784,256]{1,0:T(8,128)(2,1)}, bf16[784,256]{1,0:T(8,128)(2,1)}) custom-call(s32[1]{0:T(128)} %bitcast.5.core_ref, bf16[2,256]{1,0:T(2,128)(2,1)} %bias.6, bf16[2,256]{1,0:T(2,128)(2,1)} %bias.7, bf16[2,512,256]{2,1,0:T(8,128)(2,1)} %ws_hbm.6, ...), custom_call_target="tpu_custom_call" | custom-call | flops 4294967296 | bytes 1 | tf_op jit(solution)/shard_map/pack_weights/pallas_call | solution.py:342
  18.6 1.0 %collective-permute-done.3.refs_2_ = bf16[272,256]{1,0:T(8,128)(2,1)S(1)} collective-permute-done((bf16[272,256]{1,0:T(8,128)(2,1)S(1)}, bf16[272,256]{1,0:T(8,128)(2,1)S(1)}, u32[]{:S(2)}, u32[]{:S(2)}) %collective-permute-start.3) | collective-permute-done | bytes 139296 | tf_op jit(solution)/shard_map/ppermute | solution.py:376
  19.7 0.1 maximum_select_fusion.own
  19.8 2.2 %collective-permute-start.7 = (bf16[512,512]{1,0:T(8,128)(2,1)S(1)}, bf16[512,512]{1,0:T(8,128)(2,1)S(1)}, u32[]{:S(2)}, u32[]{:S(2)}) collective-permute-start(bf16[512,512]{1,0:T(8,128)(2,1)S(1)} %maximum_select_fusion.own), channel_id=1, source_target_pairs={{0,1},{1,0},{2,3},{3,2},{4,5},{5,4},{6,7},{7,6},{8,9},{9,8},{10,11... | collective-permute-start | bytes 1572872 | tf_op jit(solution)/shard_map/ppermute | solution.py:306
  22.0 2.3 %collective-permute-start.8 = (bf16[512,512]{1,0:T(8,128)(2,1)S(1)}, bf16[512,512]{1,0:T(8,128)(2,1)S(1)}, u32[]{:S(2)}, u32[]{:S(2)}) collective-permute-start(bf16[512,512]{1,0:T(8,128)(2,1)S(1)} %maximum_select_fusion.own), channel_id=1, source_target_pairs={{1,4},{0,13},{5,8},{4,1},{9,12},{8,5},{13,0},{12,9},{3,6},{2,15},{... | collective-permute-start | bytes 1572872 | tf_op jit(solution)/shard_map/ppermute | solution.py:317
  24.4 0.1 collective-permute-start.9
  24.5 0.7 add_force.1
  25.2 5.7 %collective-permute-start.5 = (bf16[512,256]{1,0:T(8,128)(2,1)S(1)}, bf16[512,256]{1,0:T(8,128)(2,1)S(1)}, u32[]{:S(2)}, u32[]{:S(2)}) collective-permute-start(bf16[512,256]{1,0:T(8,128)(2,1)S(1)} %get-tuple-element.75), channel_id=1, source_target_pairs={{0,0},{1,2},{2,1},{3,3},{4,4},{5,6},{6,5},{7,7},{8,8},{9,10},{10,9... | collective-permute-start | bytes 786440 | tf_op jit(solution)/shard_map/ppermute | solution.py:290
  30.9 0.0 collective-permute-start.6
  31.0 7.4 %collective-permute-done.5 = bf16[512,256]{1,0:T(8,128)(2,1)S(1)} collective-permute-done((bf16[512,256]{1,0:T(8,128)(2,1)S(1)}, bf16[512,256]{1,0:T(8,128)(2,1)S(1)}, u32[]{:S(2)}, u32[]{:S(2)}) %collective-permute-start.5) | collective-permute-done | bytes 262176 | tf_op jit(solution)/shard_map/ppermute | solution.py:290
  38.3 0.9 collective-permute-done.6
  39.2 2.6 %collective-permute-start.10 = (bf16[784,256]{1,0:T(8,128)(2,1)S(1)}, bf16[784,256]{1,0:T(8,128)(2,1)S(1)}, u32[]{:S(2)}, u32[]{:S(2)}) collective-permute-start(bf16[784,256]{1,0:T(8,128)(2,1)S(1)} %collective-permute-done.9.near_w), channel_id=1, source_target_pairs={{0,1},{1,0},{2,3},{3,2},{4,5},{5,4},{6,7},{7,6},{8,9},{9,8},{10,11... | collective-permute-start | bytes 1204232 | tf_op jit(solution)/shard_map/ppermute | solution.py:306
  41.8 0.1 maximum_select_fusion.1.own
  42.0 0.3 collective-permute-start.12
  42.2 2.3 %collective-permute-start.13 = (bf16[512,512]{1,0:T(8,128)(2,1)S(1)}, bf16[512,512]{1,0:T(8,128)(2,1)S(1)}, u32[]{:S(2)}, u32[]{:S(2)}) collective-permute-start(bf16[512,512]{1,0:T(8,128)(2,1)S(1)} %maximum_select_fusion.1.own), channel_id=1, source_target_pairs={{1,4},{5,8},{4,1},{9,12},{8,5},{12,9},{3,6},{7,10},{6,3},{11,14},{... | collective-permute-start | bytes 1572872 | tf_op jit(solution)/shard_map/ppermute | solution.py:317
  44.5 6.3 %graph_layer.4.own = bf16[512,512]{1,0:T(8,128)(2,1)S(1)} custom-call(s32[1]{0:T(128)} %bitcast.5.core_ref, s32[4096]{0:T(1024)S(1)} %bitcast.35, bf16[512,512]{1,0:T(8,128)(2,1)S(1)} %maximum_select_fusion.own, bf16[512,512]{1,0:T(8,128)(2,1)S(1)} %collective-permute-done.7.sib, bf16[512,512]{1,0:T(8,128)(2,1)S(1)} %collective-permute-done.8.rim, ...), custom_call_target="tpu_custom_call" | custom-call | flops 8589934592 | bytes 2621440 | tf_op jit(solution)/shard_map/graph_layer/pallas_call | solution.py:252
  50.8 1.8 %collective-permute-done.11.near_w = bf16[784,256]{1,0:T(8,128)(2,1)S(1)} collective-permute-done((bf16[784,256]{1,0:T(8,128)(2,1)S(1)}, bf16[784,256]{1,0:T(8,128)(2,1)S(1)}, u32[]{:S(2)}, u32[]{:S(2)}) %collective-permute-start.11) | collective-permute-done | bytes 401440 | tf_op jit(solution)/shard_map/ppermute | solution.py:306
  52.6 0.9 collective-permute-start.14
  53.5 0.4 collective-permute-start.17
  53.9 1.2 %collective-permute-start.15 = (bf16[784,256]{1,0:T(8,128)(2,1)S(1)}, bf16[784,256]{1,0:T(8,128)(2,1)S(1)}, u32[]{:S(2)}, u32[]{:S(2)}) collective-permute-start(bf16[784,256]{1,0:T(8,128)(2,1)S(1)} %copy-done.19), channel_id=1, source_target_pairs={{0,2},{2,0},{1,3},{3,1},{4,6},{6,4},{5,7},{7,5},{8,10},{10,8},{9,1... | collective-permute-start | bytes 1204232 | tf_op jit(solution)/shard_map/ppermute | solution.py:306
  55.1 6.3 %graph_layer.5.own = bf16[512,512]{1,0:T(8,128)(2,1)S(1)} custom-call(s32[1]{0:T(128)} %bitcast.5.core_ref, s32[4096]{0:T(1024)S(1)} %bitcast.33, bf16[512,512]{1,0:T(8,128)(2,1)S(1)} %maximum_select_fusion.1.own, bf16[512,512]{1,0:T(8,128)(2,1)S(1)} %collective-permute-done.12.sib, bf16[512,512]{1,0:T(8,128)(2,1)S(1)} %collective-permute-done.13.rim, ...), custom_call_target="tpu_custom_call" | custom-call | flops 8589934592 | bytes 2621440 | tf_op jit(solution)/shard_map/graph_layer/pallas_call | solution.py:252
  61.4 1.6 %collective-permute-done.15.near_w = bf16[784,256]{1,0:T(8,128)(2,1)S(1)} collective-permute-done((bf16[784,256]{1,0:T(8,128)(2,1)S(1)}, bf16[784,256]{1,0:T(8,128)(2,1)S(1)}, u32[]{:S(2)}, u32[]{:S(2)}) %collective-permute-start.15) | collective-permute-done | bytes 401440 | tf_op jit(solution)/shard_map/ppermute | solution.py:306
  63.0 2.6 %collective-permute-start.18 = (bf16[784,256]{1,0:T(8,128)(2,1)S(1)}, bf16[784,256]{1,0:T(8,128)(2,1)S(1)}, u32[]{:S(2)}, u32[]{:S(2)}) collective-permute-start(bf16[784,256]{1,0:T(8,128)(2,1)S(1)} %collective-permute-done.15.near_w), channel_id=1, source_target_pairs={{0,1},{1,0},{2,3},{3,2},{4,5},{5,4},{6,7},{7,6},{8,9},{9,8},{10,11... | collective-permute-start | bytes 1204232 | tf_op jit(solution)/shard_map/ppermute | solution.py:306
  65.7 3.8 %collective-permute-start.23 = (bf16[512,512]{1,0:T(8,128)(2,1)S(1)}, bf16[512,512]{1,0:T(8,128)(2,1)S(1)}, u32[]{:S(2)}, u32[]{:S(2)}) collective-permute-start(bf16[512,512]{1,0:T(8,128)(2,1)S(1)} %graph_layer.5.own), channel_id=1, source_target_pairs={{1,4},{5,8},{4,1},{9,12},{8,5},{12,9},{3,6},{7,10},{6,3},{11,14},{... | collective-permute-start | bytes 1572872 | tf_op jit(solution)/shard_map/ppermute | solution.py:317
  69.5 0.1 collective-permute-start.19
  69.7 6.3 %graph_layer.6 = (bf16[512,256]{1,0:T(8,128)(2,1)S(1)}, bf16[512,256]{1,0:T(8,128)(2,1)S(1)}) custom-call(s32[1]{0:T(128)} %bitcast.5.core_ref, s32[4096]{0:T(1024)S(1)} %bitcast.36, bf16[512,512]{1,0:T(8,128)(2,1)S(1)} %graph_layer.4.own, bf16[512,512]{1,0:T(8,128)(2,1)S(1)} %collective-permute-done.16.sib, ...), custom_call_target="tpu_custom_call" | custom-call | flops 8589934592 | bytes 2621440 | tf_op jit(solution)/shard_map/graph_layer/pallas_call | solution.py:252
  76.0 2.4 %collective-permute-done.19.near_w = bf16[784,256]{1,0:T(8,128)(2,1)S(1)} collective-permute-done((bf16[784,256]{1,0:T(8,128)(2,1)S(1)}, bf16[784,256]{1,0:T(8,128)(2,1)S(1)}, u32[]{:S(2)}, u32[]{:S(2)}) %collective-permute-start.19) | collective-permute-done | bytes 401440 | tf_op jit(solution)/shard_map/ppermute | solution.py:306
  78.4 3.4 %collective-permute-start.20 = (bf16[512,256]{1,0:T(8,128)(2,1)S(1)}, bf16[512,256]{1,0:T(8,128)(2,1)S(1)}, u32[]{:S(2)}, u32[]{:S(2)}) collective-permute-start(bf16[512,256]{1,0:T(8,128)(2,1)S(1)} %get-tuple-element.103), channel_id=1, source_target_pairs={{0,0},{1,2},{2,1},{3,3},{4,4},{5,6},{6,5},{7,7},{8,8},{9,10},{10,9... | collective-permute-start | bytes 786440 | tf_op jit(solution)/shard_map/ppermute | solution.py:296
  81.9 0.0 collective-permute-start.21
  81.9 6.3 %graph_layer.7 = (bf16[512,256]{1,0:T(8,128)(2,1)S(1)}, bf16[512,256]{1,0:T(8,128)(2,1)S(1)}) custom-call(s32[1]{0:T(128)} %bitcast.5.core_ref, s32[4096]{0:T(1024)S(1)} %bitcast.34, bf16[512,512]{1,0:T(8,128)(2,1)S(1)} %graph_layer.5.own, bf16[512,512]{1,0:T(8,128)(2,1)S(1)} %collective-permute-done.22.sib, ...), custom_call_target="tpu_custom_call" | custom-call | flops 8589934592 | bytes 2621440 | tf_op jit(solution)/shard_map/graph_layer/pallas_call | solution.py:252
  88.3 2.1 %collective-permute-start.25 = (bf16[512,256]{1,0:T(8,128)(2,1)S(1)}, bf16[512,256]{1,0:T(8,128)(2,1)S(1)}, u32[]{:S(2)}, u32[]{:S(2)}) collective-permute-start(bf16[512,256]{1,0:T(8,128)(2,1)S(1)} %get-tuple-element.108), channel_id=1, source_target_pairs={{0,0},{1,2},{2,1},{3,3},{4,4},{5,6},{6,5},{7,7},{8,8},{9,10},{10,9... | collective-permute-start | bytes 786440 | tf_op jit(solution)/shard_map/ppermute | solution.py:296
  90.4 0.0 collective-permute-start.26
  90.4 1.0 %maximum_select_fusion.2 = bf16[1,1024,256]{2,1,0:T(8,128)(2,1)} fusion(bf16[1,512,256]{2,1,0:T(8,128)(2,1)S(1)} %bitcast.38, bf16[1,512,256]{2,1,0:T(8,128)(2,1)S(1)} %bitcast.37, pred[]{:T(512)S(6)} %eq.6), kind=kLoop, calls=%fused_computation.2 | loop fusion | flops 2359296 | bytes 1048577 | tf_op jit(solution)/shard_map/jit(_where)/select_n | solution.py:302
  91.5 7.0 %collective-permute-done.25 = bf16[512,256]{1,0:T(8,128)(2,1)S(1)} collective-permute-done((bf16[512,256]{1,0:T(8,128)(2,1)S(1)}, bf16[512,256]{1,0:T(8,128)(2,1)S(1)}, u32[]{:S(2)}, u32[]{:S(2)}) %collective-permute-start.25) | collective-permute-done | bytes 262176 | tf_op jit(solution)/shard_map/ppermute | solution.py:296
  98.4 1.0 %maximum_select_fusion.3 = bf16[1,1024,256]{2,1,0:T(8,128)(2,1)} fusion(bf16[1,512,256]{2,1,0:T(8,128)(2,1)S(1)} %bitcast.40, bf16[1,512,256]{2,1,0:T(8,128)(2,1)S(1)} %bitcast.39, pred[]{:T(512)S(6)} %eq.6), kind=kLoop, calls=%fused_computation.3 | loop fusion | flops 2359296 | bytes 1048577 | tf_op jit(solution)/shard_map/jit(_where)/select_n | solution.py:302
  (69 shorter events, 0.3 us)
Async XLA Ops:
  0.6 0.7 copy-start.16
  0.7 0.7 copy-start.15
  1.4 1.0 %copy-start = (bf16[1,1024,256]{2,1,0:T(8,128)(2,1)S(1)}, bf16[1,1024,256]{2,1,0:T(8,128)(2,1)}, u32[]{:S(2)}) copy-start(bf16[1,1024,256]{2,1,0:T(8,128)(2,1)} %param.17) | copy-start | bytes 1572868
  2.4 4.4 %copy-start.1 = (bf16[1,1024,256]{2,1,0:T(8,128)(2,1)S(1)}, bf16[1,1024,256]{2,1,0:T(8,128)(2,1)}, u32[]{:S(2)}) copy-start(bf16[1,1024,256]{2,1,0:T(8,128)(2,1)} %param.17) | copy-start | bytes 1572868
  4.7 14.0 %collective-permute-start.2 = (bf16[272,256]{1,0:T(8,128)(2,1)S(1)}, bf16[272,256]{1,0:T(8,128)(2,1)S(1)}, u32[]{:S(2)}, u32[]{:S(2)}) collective-permute-start(bf16[272,256]{1,0:T(8,128)(2,1)S(1)} %get-tuple-element.63), channel_id=1, source_target_pairs={{0,4},{4,8},{8,12},{12,0},{1,5},{5,9},{9,13},{13,1},{2,6},{6,10},{... | collective-permute-start | bytes 417800 | tf_op jit(solution)/shard_map/ppermute | solution.py:376
  6.9 12.8 %collective-permute-start = (bf16[512,256]{1,0:T(8,128)(2,1)S(1)}, bf16[512,256]{1,0:T(8,128)(2,1)S(1)}, u32[]{:S(2)}, u32[]{:S(2)}) collective-permute-start(bf16[512,256]{1,0:T(8,128)(2,1)S(1)} %get-tuple-element.59), channel_id=1, source_target_pairs={{0,0},{1,2},{2,1},{3,3},{4,4},{5,6},{6,5},{7,7},{8,8},{9,10},{10,9... | collective-permute-start | bytes 786440 | tf_op jit(solution)/shard_map/ppermute | solution.py:290
  10.9 8.8 %collective-permute-start.1 = (bf16[512,256]{1,0:T(8,128)(2,1)S(1)}, bf16[512,256]{1,0:T(8,128)(2,1)S(1)}, u32[]{:S(2)}, u32[]{:S(2)}) collective-permute-start(bf16[512,256]{1,0:T(8,128)(2,1)S(1)} %get-tuple-element.60), channel_id=1, source_target_pairs={{0,1},{1,3},{2,0},{3,2},{4,5},{5,7},{6,4},{7,6},{8,9},{9,11},{10,8... | collective-permute-start | bytes 786440 | tf_op jit(solution)/shard_map/ppermute | solution.py:291
  10.9 8.8 %collective-permute-start.3 = (bf16[272,256]{1,0:T(8,128)(2,1)S(1)}, bf16[272,256]{1,0:T(8,128)(2,1)S(1)}, u32[]{:S(2)}, u32[]{:S(2)}) collective-permute-start(bf16[272,256]{1,0:T(8,128)(2,1)S(1)} %get-tuple-element.66), channel_id=1, source_target_pairs={{0,8},{4,12},{8,0},{12,4},{1,9},{5,13},{9,1},{13,5},{2,10},{6,14},... | collective-permute-start | bytes 417800 | tf_op jit(solution)/shard_map/ppermute | solution.py:376
  13.2 6.4 %collective-permute-start.4 = (bf16[272,256]{1,0:T(8,128)(2,1)S(1)}, bf16[272,256]{1,0:T(8,128)(2,1)S(1)}, u32[]{:S(2)}, u32[]{:S(2)}) collective-permute-start(bf16[272,256]{1,0:T(8,128)(2,1)S(1)} %get-tuple-element.67), channel_id=1, source_target_pairs={{0,12},{4,0},{8,4},{12,8},{1,13},{5,1},{9,5},{13,9},{2,14},{6,2},{... | collective-permute-start | bytes 417800 | tf_op jit(solution)/shard_map/ppermute | solution.py:376
  14.3 0.7 copy-start.14
  14.3 0.7 copy-start.13
  15.1 3.4 %copy-start.11 = (s32[1024,8]{0,1:T(8,128)S(1)}, s32[1024,8]{0,1:T(8,128)}, u32[]{:S(2)}) copy-start(s32[1024,8]{0,1:T(8,128)} %param.21) | copy-start | bytes 98308
  15.1 3.4 %copy-start.12 = (s32[1024,8]{0,1:T(8,128)S(1)}, s32[1024,8]{0,1:T(8,128)}, u32[]{:S(2)}) copy-start(s32[1024,8]{0,1:T(8,128)} %param.19) | copy-start | bytes 98308
  19.7 4.7 %copy-start.21 = (bf16[784,256]{1,0:T(8,128)(2,1)S(1)}, bf16[784,256]{1,0:T(8,128)(2,1)}, u32[]{:S(2)}) copy-start(bf16[784,256]{1,0:T(8,128)(2,1)} %get-tuple-element.79) | copy-start | bytes 1204228
  19.7 4.8 %copy-start.2 = (bf16[1,1024,256]{2,1,0:T(8,128)(2,1)S(1)}, bf16[1,1024,256]{2,1,0:T(8,128)(2,1)}, u32[]{:S(2)}) copy-start(bf16[1,1024,256]{2,1,0:T(8,128)(2,1)} %param.18) | copy-start | bytes 1572868
  19.8 19.4 %collective-permute-start.7 = (bf16[512,512]{1,0:T(8,128)(2,1)S(1)}, bf16[512,512]{1,0:T(8,128)(2,1)S(1)}, u32[]{:S(2)}, u32[]{:S(2)}) collective-permute-start(bf16[512,512]{1,0:T(8,128)(2,1)S(1)} %maximum_select_fusion.own), channel_id=1, source_target_pairs={{0,1},{1,0},{2,3},{3,2},{4,5},{5,4},{6,7},{7,6},{8,9},{9,8},{10,11... | collective-permute-start | bytes 1572872 | tf_op jit(solution)/shard_map/ppermute | solution.py:306
  22.0 17.2 %collective-permute-start.8 = (bf16[512,512]{1,0:T(8,128)(2,1)S(1)}, bf16[512,512]{1,0:T(8,128)(2,1)S(1)}, u32[]{:S(2)}, u32[]{:S(2)}) collective-permute-start(bf16[512,512]{1,0:T(8,128)(2,1)S(1)} %maximum_select_fusion.own), channel_id=1, source_target_pairs={{1,4},{0,13},{5,8},{4,1},{9,12},{8,5},{13,0},{12,9},{3,6},{2,15},{... | collective-permute-start | bytes 1572872 | tf_op jit(solution)/shard_map/ppermute | solution.py:317
  24.4 14.8 %collective-permute-start.9 = (bf16[784,256]{1,0:T(8,128)(2,1)S(1)}, bf16[784,256]{1,0:T(8,128)(2,1)S(1)}, u32[]{:S(2)}, u32[]{:S(2)}) collective-permute-start(bf16[784,256]{1,0:T(8,128)(2,1)S(1)} %copy-done.21), channel_id=1, source_target_pairs={{0,2},{2,0},{1,3},{3,1},{4,6},{6,4},{5,7},{7,5},{8,10},{10,8},{9,1... | collective-permute-start | bytes 1204232 | tf_op jit(solution)/shard_map/ppermute | solution.py:306
  24.5 17.3 %copy-start.20 = (bf16[784,256]{1,0:T(8,128)(2,1)S(1)}, bf16[784,256]{1,0:T(8,128)(2,1)}, u32[]{:S(2)}) copy-start(bf16[784,256]{1,0:T(8,128)(2,1)} %get-tuple-element.87) | copy-start | bytes 1204228
  24.5 20.0 %copy-start.5 = (bf16[2,256,512]{2,1,0:T(8,128)(2,1)S(1)}, bf16[2,256,512]{2,1,0:T(8,128)(2,1)}, u32[]{:S(2)}) copy-start(bf16[2,256,512]{2,1,0:T(8,128)(2,1)} %w2_hbm.6) | copy-start | bytes 1572868
  25.2 19.3 %copy-start.9 = (bf16[2,256]{1,0:T(2,128)(2,1)S(1)}, bf16[2,256]{1,0:T(2,128)(2,1)}, u32[]{:S(2)}) copy-start(bf16[2,256]{1,0:T(2,128)(2,1)} %bias.6) | copy-start | bytes 3076
  25.2 19.3 %copy-start.3 = (bf16[2,512,256]{2,1,0:T(8,128)(2,1)S(1)}, bf16[2,512,256]{2,1,0:T(8,128)(2,1)}, u32[]{:S(2)}) copy-start(bf16[2,512,256]{2,1,0:T(8,128)(2,1)} %ws_hbm.6) | copy-start | bytes 1572868
  25.2 19.3 %copy-start.4 = (bf16[2,512,256]{2,1,0:T(8,128)(2,1)S(1)}, bf16[2,512,256]{2,1,0:T(8,128)(2,1)}, u32[]{:S(2)}) copy-start(bf16[2,512,256]{2,1,0:T(8,128)(2,1)} %wd_hbm.6) | copy-start | bytes 1572868
  25.2 13.1 %collective-permute-start.5 = (bf16[512,256]{1,0:T(8,128)(2,1)S(1)}, bf16[512,256]{1,0:T(8,128)(2,1)S(1)}, u32[]{:S(2)}, u32[]{:S(2)}) collective-permute-start(bf16[512,256]{1,0:T(8,128)(2,1)S(1)} %get-tuple-element.75), channel_id=1, source_target_pairs={{0,0},{1,2},{2,1},{3,3},{4,4},{5,6},{6,5},{7,7},{8,8},{9,10},{10,9... | collective-permute-start | bytes 786440 | tf_op jit(solution)/shard_map/ppermute | solution.py:290
  30.9 8.3 %collective-permute-start.6 = (bf16[512,256]{1,0:T(8,128)(2,1)S(1)}, bf16[512,256]{1,0:T(8,128)(2,1)S(1)}, u32[]{:S(2)}, u32[]{:S(2)}) collective-permute-start(bf16[512,256]{1,0:T(8,128)(2,1)S(1)} %get-tuple-element.76), channel_id=1, source_target_pairs={{0,1},{1,3},{2,0},{3,2},{4,5},{5,7},{6,4},{7,6},{8,9},{9,11},{10,8... | collective-permute-start | bytes 786440 | tf_op jit(solution)/shard_map/ppermute | solution.py:291
  39.2 5.3 %collective-permute-start.10 = (bf16[784,256]{1,0:T(8,128)(2,1)S(1)}, bf16[784,256]{1,0:T(8,128)(2,1)S(1)}, u32[]{:S(2)}, u32[]{:S(2)}) collective-permute-start(bf16[784,256]{1,0:T(8,128)(2,1)S(1)} %collective-permute-done.9.near_w), channel_id=1, source_target_pairs={{0,1},{1,0},{2,3},{3,2},{4,5},{5,4},{6,7},{7,6},{8,9},{9,8},{10,11... | collective-permute-start | bytes 1204232 | tf_op jit(solution)/shard_map/ppermute | solution.py:306
  41.8 10.9 %collective-permute-start.11 = (bf16[784,256]{1,0:T(8,128)(2,1)S(1)}, bf16[784,256]{1,0:T(8,128)(2,1)S(1)}, u32[]{:S(2)}, u32[]{:S(2)}) collective-permute-start(bf16[784,256]{1,0:T(8,128)(2,1)S(1)} %copy-done.20), channel_id=1, source_target_pairs={{0,2},{2,0},{1,3},{3,1},{4,6},{6,4},{5,7},{7,5},{8,10},{10,8},{9,1... | collective-permute-start | bytes 1204232 | tf_op jit(solution)/shard_map/ppermute | solution.py:306
  41.9 12.0 %copy-start.19 = (bf16[784,256]{1,0:T(8,128)(2,1)S(1)}, bf16[784,256]{1,0:T(8,128)(2,1)}, u32[]{:S(2)}) copy-start(bf16[784,256]{1,0:T(8,128)(2,1)} %get-tuple-element.94) | copy-start | bytes 1204228
  41.9 13.2 %copy-start.6 = (bf16[2,512,256]{2,1,0:T(8,128)(2,1)S(1)}, bf16[2,512,256]{2,1,0:T(8,128)(2,1)}, u32[]{:S(2)}) copy-start(bf16[2,512,256]{2,1,0:T(8,128)(2,1)} %ws_hbm.7) | copy-start | bytes 1572868
  41.9 13.2 %copy-start.7 = (bf16[2,512,256]{2,1,0:T(8,128)(2,1)S(1)}, bf16[2,512,256]{2,1,0:T(8,128)(2,1)}, u32[]{:S(2)}) copy-start(bf16[2,512,256]{2,1,0:T(8,128)(2,1)} %wd_hbm.7) | copy-start | bytes 1572868
  41.9 13.2 %copy-start.8 = (bf16[2,256,512]{2,1,0:T(8,128)(2,1)S(1)}, bf16[2,256,512]{2,1,0:T(8,128)(2,1)}, u32[]{:S(2)}) copy-start(bf16[2,256,512]{2,1,0:T(8,128)(2,1)} %w2_hbm.7) | copy-start | bytes 1572868
  42.0 12.0 %collective-permute-start.12 = (bf16[512,512]{1,0:T(8,128)(2,1)S(1)}, bf16[512,512]{1,0:T(8,128)(2,1)S(1)}, u32[]{:S(2)}, u32[]{:S(2)}) collective-permute-start(bf16[512,512]{1,0:T(8,128)(2,1)S(1)} %maximum_select_fusion.1.own), channel_id=1, source_target_pairs={{0,1},{1,0},{2,3},{3,2},{4,5},{5,4},{6,7},{7,6},{8,9},{9,8},{10,11... | collective-permute-start | bytes 1572872 | tf_op jit(solution)/shard_map/ppermute | solution.py:306
  42.2 12.9 %collective-permute-start.13 = (bf16[512,512]{1,0:T(8,128)(2,1)S(1)}, bf16[512,512]{1,0:T(8,128)(2,1)S(1)}, u32[]{:S(2)}, u32[]{:S(2)}) collective-permute-start(bf16[512,512]{1,0:T(8,128)(2,1)S(1)} %maximum_select_fusion.1.own), channel_id=1, source_target_pairs={{1,4},{5,8},{4,1},{9,12},{8,5},{12,9},{3,6},{7,10},{6,3},{11,14},{... | collective-permute-start | bytes 1572872 | tf_op jit(solution)/shard_map/ppermute | solution.py:317
  50.8 4.3 %copy-start.10 = (bf16[2,256]{1,0:T(2,128)(2,1)S(1)}, bf16[2,256]{1,0:T(2,128)(2,1)}, u32[]{:S(2)}) copy-start(bf16[2,256]{1,0:T(2,128)(2,1)} %bias.7) | copy-start | bytes 3076
  52.6 16.9 %copy-start.18 = (bf16[784,256]{1,0:T(8,128)(2,1)S(1)}, bf16[784,256]{1,0:T(8,128)(2,1)}, u32[]{:S(2)}) copy-start(bf16[784,256]{1,0:T(8,128)(2,1)} %get-tuple-element.102) | copy-start | bytes 1204228
  52.6 2.5 %collective-permute-start.14 = (bf16[784,256]{1,0:T(8,128)(2,1)S(1)}, bf16[784,256]{1,0:T(8,128)(2,1)S(1)}, u32[]{:S(2)}, u32[]{:S(2)}) collective-permute-start(bf16[784,256]{1,0:T(8,128)(2,1)S(1)} %collective-permute-done.11.near_w), channel_id=1, source_target_pairs={{0,1},{1,0},{2,3},{3,2},{4,5},{5,4},{6,7},{7,6},{8,9},{9,8},{10,11... | collective-permute-start | bytes 1204232 | tf_op jit(solution)/shard_map/ppermute | solution.py:306
  53.5 16.0 %collective-permute-start.16 = (bf16[512,512]{1,0:T(8,128)(2,1)S(1)}, bf16[512,512]{1,0:T(8,128)(2,1)S(1)}, u32[]{:S(2)}, u32[]{:S(2)}) collective-permute-start(bf16[512,512]{1,0:T(8,128)(2,1)S(1)} %graph_layer.4.own), channel_id=1, source_target_pairs={{0,1},{1,0},{2,3},{3,2},{4,5},{5,4},{6,7},{7,6},{8,9},{9,8},{10,11... | collective-permute-start | bytes 1572872 | tf_op jit(solution)/shard_map/ppermute | solution.py:306
  53.5 16.2 %collective-permute-start.17 = (bf16[512,512]{1,0:T(8,128)(2,1)S(1)}, bf16[512,512]{1,0:T(8,128)(2,1)S(1)}, u32[]{:S(2)}, u32[]{:S(2)}) collective-permute-start(bf16[512,512]{1,0:T(8,128)(2,1)S(1)} %graph_layer.4.own), channel_id=1, source_target_pairs={{1,4},{0,13},{5,8},{4,1},{9,12},{8,5},{13,0},{12,9},{3,6},{2,15},{... | collective-permute-start | bytes 1572872 | tf_op jit(solution)/shard_map/ppermute | solution.py:317
  53.9 9.1 %collective-permute-start.15 = (bf16[784,256]{1,0:T(8,128)(2,1)S(1)}, bf16[784,256]{1,0:T(8,128)(2,1)S(1)}, u32[]{:S(2)}, u32[]{:S(2)}) collective-permute-start(bf16[784,256]{1,0:T(8,128)(2,1)S(1)} %copy-done.19), channel_id=1, source_target_pairs={{0,2},{2,0},{1,3},{3,1},{4,6},{6,4},{5,7},{7,5},{8,10},{10,8},{9,1... | collective-permute-start | bytes 1204232 | tf_op jit(solution)/shard_map/ppermute | solution.py:306
  63.0 6.6 %collective-permute-start.18 = (bf16[784,256]{1,0:T(8,128)(2,1)S(1)}, bf16[784,256]{1,0:T(8,128)(2,1)S(1)}, u32[]{:S(2)}, u32[]{:S(2)}) collective-permute-start(bf16[784,256]{1,0:T(8,128)(2,1)S(1)} %collective-permute-done.15.near_w), channel_id=1, source_target_pairs={{0,1},{1,0},{2,3},{3,2},{4,5},{5,4},{6,7},{7,6},{8,9},{9,8},{10,11... | collective-permute-start | bytes 1204232 | tf_op jit(solution)/shard_map/ppermute | solution.py:306
  65.6 16.3 %collective-permute-start.22 = (bf16[512,512]{1,0:T(8,128)(2,1)S(1)}, bf16[512,512]{1,0:T(8,128)(2,1)S(1)}, u32[]{:S(2)}, u32[]{:S(2)}) collective-permute-start(bf16[512,512]{1,0:T(8,128)(2,1)S(1)} %graph_layer.5.own), channel_id=1, source_target_pairs={{0,1},{1,0},{2,3},{3,2},{4,5},{5,4},{6,7},{7,6},{8,9},{9,8},{10,11... | collective-permute-start | bytes 1572872 | tf_op jit(solution)/shard_map/ppermute | solution.py:306
  65.7 16.3 %collective-permute-start.23 = (bf16[512,512]{1,0:T(8,128)(2,1)S(1)}, bf16[512,512]{1,0:T(8,128)(2,1)S(1)}, u32[]{:S(2)}, u32[]{:S(2)}) collective-permute-start(bf16[512,512]{1,0:T(8,128)(2,1)S(1)} %graph_layer.5.own), channel_id=1, source_target_pairs={{1,4},{5,8},{4,1},{9,12},{8,5},{12,9},{3,6},{7,10},{6,3},{11,14},{... | collective-permute-start | bytes 1572872 | tf_op jit(solution)/shard_map/ppermute | solution.py:317
  69.5 8.9 %collective-permute-start.19 = (bf16[784,256]{1,0:T(8,128)(2,1)S(1)}, bf16[784,256]{1,0:T(8,128)(2,1)S(1)}, u32[]{:S(2)}, u32[]{:S(2)}) collective-permute-start(bf16[784,256]{1,0:T(8,128)(2,1)S(1)} %copy-done.18), channel_id=1, source_target_pairs={{0,2},{2,0},{1,3},{3,1},{4,6},{6,4},{5,7},{7,5},{8,10},{10,8},{9,1... | collective-permute-start | bytes 1204232 | tf_op jit(solution)/shard_map/ppermute | solution.py:306
  78.4 3.5 %collective-permute-start.24 = (bf16[784,256]{1,0:T(8,128)(2,1)S(1)}, bf16[784,256]{1,0:T(8,128)(2,1)S(1)}, u32[]{:S(2)}, u32[]{:S(2)}) collective-permute-start(bf16[784,256]{1,0:T(8,128)(2,1)S(1)} %collective-permute-done.19.near_w), channel_id=1, source_target_pairs={{0,1},{1,0},{2,3},{3,2},{4,5},{5,4},{6,7},{7,6},{8,9},{9,8},{10,11... | collective-permute-start | bytes 1204232 | tf_op jit(solution)/shard_map/ppermute | solution.py:306
  78.4 12.0 %collective-permute-start.20 = (bf16[512,256]{1,0:T(8,128)(2,1)S(1)}, bf16[512,256]{1,0:T(8,128)(2,1)S(1)}, u32[]{:S(2)}, u32[]{:S(2)}) collective-permute-start(bf16[512,256]{1,0:T(8,128)(2,1)S(1)} %get-tuple-element.103), channel_id=1, source_target_pairs={{0,0},{1,2},{2,1},{3,3},{4,4},{5,6},{6,5},{7,7},{8,8},{9,10},{10,9... | collective-permute-start | bytes 786440 | tf_op jit(solution)/shard_map/ppermute | solution.py:296
  81.9 8.6 %collective-permute-start.21 = (bf16[512,256]{1,0:T(8,128)(2,1)S(1)}, bf16[512,256]{1,0:T(8,128)(2,1)S(1)}, u32[]{:S(2)}, u32[]{:S(2)}) collective-permute-start(bf16[512,256]{1,0:T(8,128)(2,1)S(1)} %get-tuple-element.104), channel_id=1, source_target_pairs={{0,2},{1,0},{2,3},{3,1},{4,6},{5,4},{6,7},{7,5},{8,10},{9,8},{10,1... | collective-permute-start | bytes 786440 | tf_op jit(solution)/shard_map/ppermute | solution.py:297
  88.3 10.2 %collective-permute-start.25 = (bf16[512,256]{1,0:T(8,128)(2,1)S(1)}, bf16[512,256]{1,0:T(8,128)(2,1)S(1)}, u32[]{:S(2)}, u32[]{:S(2)}) collective-permute-start(bf16[512,256]{1,0:T(8,128)(2,1)S(1)} %get-tuple-element.108), channel_id=1, source_target_pairs={{0,0},{1,2},{2,1},{3,3},{4,4},{5,6},{6,5},{7,7},{8,8},{9,10},{10,9... | collective-permute-start | bytes 786440 | tf_op jit(solution)/shard_map/ppermute | solution.py:296
  90.4 8.0 %collective-permute-start.26 = (bf16[512,256]{1,0:T(8,128)(2,1)S(1)}, bf16[512,256]{1,0:T(8,128)(2,1)S(1)}, u32[]{:S(2)}, u32[]{:S(2)}) collective-permute-start(bf16[512,256]{1,0:T(8,128)(2,1)S(1)} %get-tuple-element.109), channel_id=1, source_target_pairs={{0,2},{1,0},{2,3},{3,1},{4,6},{5,4},{6,7},{7,5},{8,10},{9,8},{10,1... | collective-permute-start | bytes 786440 | tf_op jit(solution)/shard_map/ppermute | solution.py:297
  (1 other events, 0.7 us)

commit v9 on v8

--- a/solution.py
+++ b/solution.py
@@ -154,7 +154,7 @@
 
 
 def layer_kernel(
-    layer, slots, last, core_ref, idx_ref, own, sib, rim, bias, near_w, far_w, ws_hbm, wd_hbm, w2_hbm, *refs
+    layer, graph, slots, last, spot_ref, idx_ref, own, sib, rim, bias, w_a, w_b, w_c, w_d, ws_hbm, wd_hbm, w2_hbm, *refs
 ):
     outs, refs = (refs[:2], refs[2:]) if last else (refs[:1], refs[1:])
     ws, wd, w2, ws_x, wd_x, w2_x, proj, near, summed, sems = refs
@@ -162,7 +162,7 @@
     share = width // 2
     chunks = width // LANES
     part = chunks // 2
-    core = core_ref[0]
+    group, core = spot_ref[0], spot_ref[1]
     pairs = ((wd_hbm, wd), (ws_hbm, ws), (w2_hbm, w2))
     copies = [pltpu.make_async_copy(src.at[layer], dst, sems.at[i]) for i, (src, dst) in enumerate(pairs)]
     for copy in copies:
@@ -170,20 +170,27 @@
     window = 3 * rows
     proj[0:8, :] = jnp.full((8, LANES), DEAD, jnp.float32)
     proj[4 * window + 4:4 * window + 16, :] = jnp.full((12, LANES), DEAD, jnp.float32)
-    here, there = pl.multiple_of(core * share, 16), pl.multiple_of((1 - core) * share, 16)
-    for spot, piece in ((here, near_w), (there, far_w)):
-        ws_x[pl.ds(spot, share), :] = piece[0:share, :]
-        wd_x[pl.ds(spot, share), :] = piece[share:2 * share, :]
+    half = share // 2
+    base = graph * (3 * half + 16)
+    pieces = ((group, core, w_a), (1 - group, core, w_b), (group, 1 - core, w_c), (1 - group, 1 - core, w_d))
+    for y, c, piece in pieces:
+        spot = pl.ds(pl.multiple_of((2 * c + y) * half, half), half)
+        ws_x[spot, :] = piece[base:base + half, :]
+        wd_x[spot, :] = piece[base + half:base + 2 * half, :]
+
+    def place(left, right):
+        for here, there, y in ((left[0], right[0], group), (left[1], right[1], 1 - group)):
+            spot = pl.ds(pl.multiple_of(y * half, half), half)
+            w2_x[spot, :share] = here[base + 2 * half:base + 3 * half, :]
+            w2_x[spot, share:] = there[base + 2 * half:base + 3 * half, :]
 
     @pl.when(core == 0)
     def _():
-        w2_x[:, :share] = near_w[2 * share:3 * share, :]
-        w2_x[:, share:] = far_w[2 * share:3 * share, :]
+        place((w_a, w_b), (w_c, w_d))
 
     @pl.when(core != 0)
     def _():
-        w2_x[:, share:] = near_w[2 * share:3 * share, :]
-        w2_x[:, :share] = far_w[2 * share:3 * share, :]
+        place((w_c, w_d), (w_a, w_b))
 
     def put(dst, base, first, values):
         for c in range(values.shape[1] // LANES):
@@ -193,7 +200,7 @@
         return jnp.dot(values[...], weights[...], preferred_element_type=jnp.float32)
 
     b_own = bias[layer:layer + 1, :].astype(jnp.float32)
-    b_other = near_w[3 * share:3 * share + 1, :].astype(jnp.float32)
+    b_other = w_a[base + 3 * half:base + 3 * half + 1, :].astype(jnp.float32)
     put(near, 0, part, product(own, wd_x) + b_other)
     put(proj, 1, part, product(own, ws_x))
     copies[0].wait()
@@ -237,7 +244,7 @@
             outs[1][...] = result[:, :share]
 
 
-def run_layer(layer, slots, last, core, idx, own, sib, rim, ws, wd, w2, bias, near_w, far_w):
+def run_layer(layer, graph, slots, last, spot, idx, own, sib, rim, ws, wd, w2, bias, pieces):
     rows, width = own.shape
     share = width // 2
     chunks = width // LANES
@@ -250,9 +257,9 @@
     else:
         out_shape, out_specs = jax.ShapeDtypeStruct((rows, width), bf16), vmem
     return pl.pallas_call(
-        functools.partial(layer_kernel, layer, slots, last),
+        functools.partial(layer_kernel, layer, graph, slots, last),
         out_shape=out_shape,
-        in_specs=[smem] * 2 + [vmem] * 6 + [pl.BlockSpec(memory_space=pl.ANY)] * 3,
+        in_specs=[smem] * 2 + [vmem] * 8 + [pl.BlockSpec(memory_space=pl.ANY)] * 3,
         out_specs=out_specs,
         scratch_shapes=[
             pltpu.VMEM((width, share), bf16),
@@ -269,7 +276,7 @@
         compiler_params=pltpu.CompilerParams(vmem_limit_bytes=32 << 20),
         cost_estimate=pl.CostEstimate(flops=64 * rows * width * width, bytes_accessed=10 * rows * width, transcendentals=0),
         name="graph_layer",
-    )(core, idx, own, sib, rim, bias, near_w, far_w, ws, wd, w2)
+    )(spot, idx, own, sib, rim, bias, *pieces, ws, wd, w2)
 
 
 def edge_offsets(nbrs, counts, core):
@@ -317,38 +324,55 @@
     return lax.ppermute(own, ("mesh", "batch"), pairs)
 
 
-def pack_kernel(order, core_ref, g_bias, r_bias, *refs):
+def all_pieces(near_w, across):
+    return near_w, across, swap(near_w, "batch"), swap(across, "batch")
+
+
+def pack_kernel(graphs, spot_ref, g_bias, r_bias, *refs):
     weights, outs, sems = (refs[:3], refs[3:6]), refs[6:-1], refs[-1]
     share = g_bias.shape[1]
-    here = pl.multiple_of(core_ref[0] * share, share)
+    half = share // 2
+    group, core = spot_ref[0], spot_ref[1]
+    rows = pl.ds(pl.multiple_of((2 * core + group) * half, half), half)
+    columns = pl.ds(pl.multiple_of(core * share, share), share)
     copies = []
-    for (graph, layer), out in zip(order, outs):
-        ws, wd, w2 = weights[graph]
-        sources = (ws.at[layer, pl.ds(here, share), :], wd.at[layer, pl.ds(here, share), :], w2.at[layer, :, pl.ds(here, share)])
-        for i, source in enumerate(sources):
-            copies.append(pltpu.make_async_copy(source, out.at[i * share:(i + 1) * share, :], sems.at[len(copies)]))
-            copies[-1].start()
-    for (graph, layer), out in zip(order, outs):
-        bias = (g_bias, r_bias)[graph][layer:layer + 1, :]
-        out[3 * share:, :] = jnp.broadcast_to(bias, (16, share))
+    for layer, out in enumerate(outs):
+        for graph in range(graphs):
+            ws, wd, w2 = weights[graph]
+            base = graph * (3 * half + 16)
+            sources = (
+                ws.at[layer, rows, :], wd.at[layer, rows, :],
+                w2.at[layer, pl.ds(pl.multiple_of(group * half, half), half), columns],
+            )
+            for i, source in enumerate(sources):
+                spot = base + i * half
+                copies.append(pltpu.make_async_copy(source, out.at[spot:spot + half, :], sems.at[len(copies)]))
+                copies[-1].start()
+    for layer, out in enumerate(outs):
+        for graph in range(graphs):
+            base = graph * (3 * half + 16) + 3 * half
+            bias = (g_bias, r_bias)[graph][layer:layer + 1, :]
+            out[base:base + 16, :] = jnp.broadcast_to(bias, (16, share))
     for copy in copies:
         copy.wait()
 
 
-def pack_weights(order, core, g_weights, g_bias, r_weights, r_bias):
-    share = g_bias.shape[1]
+def pack_weights(spot, g_weights, g_bias, r_weights, r_bias):
+    layers, share = g_bias.shape
+    graphs = 2
     vmem = pl.BlockSpec(memory_space=pltpu.VMEM)
     hbm = pl.BlockSpec(memory_space=pltpu.HBM)
+    size = graphs * (3 * share // 2 + 16)
     return pl.pallas_call(
-        functools.partial(pack_kernel, order),
-        out_shape=(jax.ShapeDtypeStruct((3 * share + 16, share), jnp.bfloat16),) * len(order),
+        functools.partial(pack_kernel, graphs),
+        out_shape=(jax.ShapeDtypeStruct((size, share), jnp.bfloat16),) * layers,
         in_specs=[pl.BlockSpec(memory_space=pltpu.SMEM)] + [vmem] * 2 + [hbm] * 6,
-        out_specs=(vmem,) * len(order),
-        scratch_shapes=[pltpu.SemaphoreType.DMA((3 * len(order),))],
+        out_specs=(vmem,) * layers,
+        scratch_shapes=[pltpu.SemaphoreType.DMA((3 * graphs * layers,))],
         compiler_params=pltpu.CompilerParams(vmem_limit_bytes=60 << 20),
         cost_estimate=pl.CostEstimate(flops=256 * share**3, bytes_accessed=1, transcendentals=0),
         name="pack_weights",
-    )(core, g_bias, r_bias, *g_weights, *r_weights)
+    )(spot, g_bias, r_bias, *g_weights, *r_weights)
 
 
 def by_rows(
@@ -364,7 +388,7 @@
     half = rows // 2
     cap = 2 * bnd_src.shape[0] // parts
     me = lax.axis_index("mesh").reshape(1)
-    core1 = core.reshape(1)
+    spot = jnp.stack([lax.axis_index("groups"), core])
     g_own, r_own = g_nodes[0], r_nodes[0]
     g_weights, r_weights = (g_ws, g_wd, g_w2), (r_ws, r_wd, r_w2)
     after = lax.optimization_barrier
@@ -377,47 +401,45 @@
     landed[0], g_late = after((landed[0], g_own))
     same = lax.dynamic_slice(g_late, (part * half, 0), (half, g_own.shape[1]))
     other = lax.dynamic_slice(g_late, ((1 - part) * half, 0), (half, g_own.shape[1]))
-    same, other, core1 = after((same, other, core1))
+    same, other, spot = after((same, other, spot))
     g_a, g_b = spread_rows(same, other)
     idx = edge_offsets(jnp.stack([g_nbr, r_nbr]), jnp.stack([g_count, r_count]), core)
 
-    order = [(graph, layer) for layer in range(layers) for graph in (0, 1)]
-    packs = list(pack_weights(order, core1, g_weights, g_b1, r_weights, r_b1))
-    landed[1], packs[0] = after((landed[1], packs[0]))
-    near_w = [swap(packs[0], "mp")]
+    g_a, g_b, spot = after((g_a, g_b, spot))
+    packs = list(pack_weights(spot, g_weights, g_b1, r_weights, r_b1))
+    near_w = swap(packs[0], "mp")
     g_idx, r_idx = idx[0], idx[1]
-    g_a, g_b, g_idx, r_idx, packs[1], *landed = after((g_a, g_b, g_idx, r_idx, packs[1], *landed))
+    g_a, g_b, g_idx, r_idx, *landed = after((g_a, g_b, g_idx, r_idx, *landed))
     planet = ordered(core, g_a, g_b, 1)
     g_sib, g_rim = swap(planet, "batch"), rims(planet, True)
-    *r_pair, packs[1] = after((*add_force(part.reshape(1), r_own, landed, cap), packs[1]))
+    *r_pair, near_w, packs[1:] = after((*add_force(part.reshape(1), r_own, landed, cap), near_w, packs[1:]))
+    across = swap(near_w, "groups")
     r_a, r_b = spread_rows(*r_pair)
-    near_w.append(swap(packs[1], "mp"))
-    r_a, r_b, g_sib, g_rim, near_w[0] = after((r_a, r_b, g_sib, g_rim, near_w[0]))
-    regional, g_idx = after((ordered(core, r_a, r_b, 1), g_idx))
+    r_a, r_b, g_sib, g_rim, across = after((r_a, r_b, g_sib, g_rim, across))
+    pieces = all_pieces(near_w, across)
+    later = [swap(pack, "mp") for pack in packs[1:]]
+    regional, g_idx, later = after((ordered(core, r_a, r_b, 1), g_idx, later))
     r_sib, r_rim = swap(regional, "batch"), rims(regional, False)
-    for i, (graph, layer) in enumerate(order):
+    for layer in range(layers):
         last = layer == layers - 1
-        far_w = swap(near_w[i], "batch")
-        if graph == 0:
-            planet = run_layer(
-                layer, slots, last, core1, g_idx, planet, g_sib, g_rim, g_ws, g_wd, g_w2, g_b1, near_w[i], far_w
-            )
-            *planet, core1, near_w[i + 1] = after((*(planet if last else (planet,)), core1, near_w[i + 1]))
-            if not last:
-                planet = planet[0]
-                g_sib, g_rim = swap(planet, "batch"), rims(planet, True)
-        else:
-            regional = run_layer(
-                layer, slots, last, core1, r_idx, regional, r_sib, r_rim, r_ws, r_wd, r_w2, r_b1, near_w[i], far_w
-            )
-            if not last:
-                regional, core1, near_w[i + 1] = after((regional, core1, near_w[i + 1]))
-                r_sib, r_rim = swap(regional, "batch"), rims(regional, False)
-        if i + 2 < len(order):
-            packs[i + 2], near_w[i + 1] = after((packs[i + 2], near_w[i + 1]))
-            near_w.append(swap(packs[i + 2], "mp"))
+        planet = run_layer(
+            layer, 0, slots, last, spot, g_idx, planet, g_sib, g_rim, g_ws, g_wd, g_w2, g_b1, pieces
+        )
+        *planet, spot = after((*(planet if last else (planet,)), spot))
+        if not last:
+            planet = planet[0]
+            g_sib, g_rim = swap(planet, "batch"), rims(planet, True)
+            across = swap(later[layer], "groups")
+        regional = run_layer(
+            layer, 1, slots, last, spot, r_idx, regional, r_sib, r_rim, r_ws, r_wd, r_w2, r_b1, pieces
+        )
+        if not last:
+            regional, spot = after((regional, spot))
+            r_sib, r_rim = swap(regional, "batch"), rims(regional, False)
+            pieces = all_pieces(later[layer], across)
     g_out = ordered(part, *gather_rows(*planet), 0)
-    r_out = ordered(part, *gather_rows(*regional), 0)
+    g_out, *regional_rows = after((g_out, *gather_rows(*regional)))
+    r_out = ordered(part, *regional_rows, 0)
     return g_out[None], r_out[None]
 
 
@@ -442,7 +464,7 @@
         P(None, "mp", None),
     )
     out_specs = (P(("groups", "batch"), "mesh", "mp"), P(("groups", "batch"), "mesh", "mp"))
-    square = mesh.shape["mp"] == 2 and mesh.shape["batch"] == 2
+    square = mesh.shape["mp"] == 2 and mesh.shape["batch"] == 2 and mesh.shape["groups"] == 2
     return jax.shard_map(
         by_rows if square else by_features, mesh=mesh, in_specs=in_specs, out_specs=out_specs, check_vma=False
     )

time: 101 us -> 105 us (1.040)
  waiting for transfers between devices: 22.1 us -> 25.9 us
  starting transfers between devices: 39.7 us -> 41.5 us
    ppermute x2, waiting for transfers between devices: 7.36 us -> 0.28 us  [spread_rows(): a = lax.ppermute(same, ('mp', 'batch'), [(0, 0), (1, 2), (2, 1), (3, 3)])]
    ppermute x2, waiting for transfers between devices: 0.89 us -> 5.88 us  [spread_rows(): b = lax.ppermute(other, ('mp', 'batch'), [(0, 1), (1, 3), (2, 0), (3, 2)])]
    ppermute x4, waiting for transfers between devices: 0.01 us -> 4.55 us  [rims(): return lax.ppermute(own, ('mesh', 'batch'), pairs)]
    ppermute x4, starting transfers between devices: 8.88 us -> 12.7 us  [rims(): return lax.ppermute(own, ('mesh', 'batch'), pairs)]
    ppermute x2, waiting for transfers between devices: 6.97 us -> 4.54 us  [gather_rows(): same = lax.ppermute(a, ('mp', 'batch'), [(0, 0), (1, 2), (2, 1), (3, 3)])]
    ppermute x12, waiting for transfers between devices: 5.85 us -> 7.16 us  [swap(): return lax.ppermute(values, axis, [(0, 1), (1, 0)])]
    ppermute x2, waiting for transfers between devices: 0.01 us -> 1.23 us  [gather_rows(): other = lax.ppermute(b, ('mp', 'batch'), [(0, 2), (1, 0), (2, 3), (3, 1)])]
    ppermute x3, waiting for transfers between devices: 1.02 us -> 2.25 us  [by_rows(): lax.ppermute(pieces[k], 'mesh', [(i, (i + k) % parts) for i in range(part...]
  transfers between devices with their start and end apart: 27 -> 27, of which waited for: 7 -> 11; matrix products, arithmetic and copies ran while one was open for 1% -> 1% of each run, Pallas kernels for 29% -> 28%
where the time goes in v9:
time: 105 us; the launch traced here: 104 us
  starting transfers between devices  41.5 us (40%)
  Pallas kernels  31 us (30%)
  waiting for transfers between devices  25.9 us (25%)
  other arithmetic  3.07 us (3%)
  local copies, waits for them, and re-layouts  1.86 us (2%)
  between operations  1.09 us (1%)
    pallas_call x4, Pallas kernels, run_layer(): pl.pallas_call(functools.partial(layer_kernel, layer, graph, slots, last)...  25.2 us
    ppermute x4, starting transfers between devices, rims(): return lax.ppermute(own, ('mesh', 'batch'), pairs)  12.7 us
    ppermute x12, starting transfers between devices, swap(): return lax.ppermute(values, axis, [(0, 1), (1, 0)])  9.99 us
    ppermute x2, starting transfers between devices, spread_rows(): a = lax.ppermute(same, ('mp', 'batch'), [(0, 0), (1, 2), (2, 1), (3, 3)])  8.51 us
    ppermute x12, waiting for transfers between devices, swap(): return lax.ppermute(values, axis, [(0, 1), (1, 0)])  7.16 us
    ppermute x2, waiting for transfers between devices, spread_rows(): b = lax.ppermute(other, ('mp', 'batch'), [(0, 1), (1, 3), (2, 0), (3, 2)])  5.88 us
    ppermute x2, starting transfers between devices, gather_rows(): same = lax.ppermute(a, ('mp', 'batch'), [(0, 0), (1, 2), (2, 1), (3, 3)])  5.56 us
    ppermute x3, starting transfers between devices, by_rows(): lax.ppermute(pieces[k], 'mesh', [(i, (i + k) % parts) for i in range(part...  4.73 us
  transfers between devices with their start and end apart: 27, of which 11 were waited for; matrix products, arithmetic and copies ran while one was open for 1% of the time, Pallas kernels for 28%

profile of v9, /device:TPU:1, one launch (start us, length us, event | category | flops | bytes accessed | tf_op | source)
XLA Modules:
  0.0 104.4 jit_solution(17773622912301359155)
XLA Ops:
  0.7 0.7 copy-done.18
  1.4 1.0 copy-done
  2.4 2.2 %pick_rows.1 = (bf16[272,256]{1,0:T(8,128)(2,1)S(1)}, bf16[272,256]{1,0:T(8,128)(2,1)S(1)}, bf16[272,256]{1,0:T(8,128)(2,1)S(1)}, bf16[272,256]{1,0:T(8,128)(2,1)S(1)}) custom-call(s32[1]{0:T(128)} %bitcast.me_ref, s32[3,512]{1,0:T(4,128)S(1)} %pad_add_fusion.bnd_ref, bf16[1024,256]{1,0:T(8,128)(2,1)S(1)} %bitcast.30), custom_call_target="tpu_custom_call" | custom-call | flops 1 | bytes 1 | tf_op jit(solution)/shard_map/pick_rows/pallas_call | solution.py:115
  4.7 0.7 pad_add_fusion.1.spot_ref
  5.4 4.5 %collective-permute-start = (bf16[512,256]{1,0:T(8,128)(2,1)S(1)}, bf16[512,256]{1,0:T(8,128)(2,1)S(1)}, u32[]{:S(2)}, u32[]{:S(2)}) collective-permute-start(bf16[512,256]{1,0:T(8,128)(2,1)S(1)} %get-tuple-element.54), channel_id=1, source_target_pairs={{0,0},{1,2},{2,1},{3,3},{4,4},{5,6},{6,5},{7,7},{8,8},{9,10},{10,9... | collective-permute-start | bytes 786440 | tf_op jit(solution)/shard_map/ppermute | solution.py:297
  9.9 1.4 %collective-permute-start.2 = (bf16[272,256]{1,0:T(8,128)(2,1)S(1)}, bf16[272,256]{1,0:T(8,128)(2,1)S(1)}, u32[]{:S(2)}, u32[]{:S(2)}) collective-permute-start(bf16[272,256]{1,0:T(8,128)(2,1)S(1)} %get-tuple-element.61), channel_id=1, source_target_pairs={{0,4},{4,8},{8,12},{12,0},{1,5},{5,9},{9,13},{13,1},{2,6},{6,10},{... | collective-permute-start | bytes 417800 | tf_op jit(solution)/shard_map/ppermute | solution.py:400
  11.3 2.3 %collective-permute-start.3 = (bf16[272,256]{1,0:T(8,128)(2,1)S(1)}, bf16[272,256]{1,0:T(8,128)(2,1)S(1)}, u32[]{:S(2)}, u32[]{:S(2)}) collective-permute-start(bf16[272,256]{1,0:T(8,128)(2,1)S(1)} %get-tuple-element.62), channel_id=1, source_target_pairs={{0,8},{4,12},{8,0},{12,4},{1,9},{5,13},{9,1},{13,5},{2,10},{6,14},... | collective-permute-start | bytes 417800 | tf_op jit(solution)/shard_map/ppermute | solution.py:400
  13.6 1.1 %collective-permute-start.4 = (bf16[272,256]{1,0:T(8,128)(2,1)S(1)}, bf16[272,256]{1,0:T(8,128)(2,1)S(1)}, u32[]{:S(2)}, u32[]{:S(2)}) collective-permute-start(bf16[272,256]{1,0:T(8,128)(2,1)S(1)} %get-tuple-element.63), channel_id=1, source_target_pairs={{0,12},{4,0},{8,4},{12,8},{1,13},{5,1},{9,5},{13,9},{2,14},{6,2},{... | collective-permute-start | bytes 417800 | tf_op jit(solution)/shard_map/ppermute | solution.py:400
  14.7 0.1 fusion.5
  14.8 1.2 %collective-permute-done.1 = bf16[512,256]{1,0:T(8,128)(2,1)S(1)} collective-permute-done((bf16[512,256]{1,0:T(8,128)(2,1)S(1)}, bf16[512,256]{1,0:T(8,128)(2,1)S(1)}, u32[]{:S(2)}, u32[]{:S(2)}) %collective-permute-start.1) | collective-permute-done | bytes 262176 | tf_op jit(solution)/shard_map/ppermute | solution.py:298
  16.0 2.9 %pack_weights.1 = (bf16[800,256]{1,0:T(8,128)(2,1)}, bf16[800,256]{1,0:T(8,128)(2,1)}) custom-call(s32[2]{0:T(128)} %pad_add_fusion.1.spot_ref, bf16[2,256]{1,0:T(2,128)(2,1)} %bias.6, bf16[2,256]{1,0:T(2,128)(2,1)} %bias.7, bf16[2,512,256]{2,1,0:T(8,128)(2,1)} %ws_hbm.6, bf16[2,512,256]{2,1,0:T(8,128)(2,1)} %wd_hbm.6, bf16[2,256,512]{2,1,0:T(8,128)(2,1)} %w2_hbm.6, ...), custom_call_target="tpu_custom_call" | custom-call | flops 4294967296 | bytes 1 | tf_op jit(solution)/shard_map/pack_weights/pallas_call | solution.py:366
  18.9 2.3 %collective-permute-start.5 = (bf16[800,256]{1,0:T(8,128)(2,1)}, bf16[800,256]{1,0:T(8,128)(2,1)S(1)}, u32[]{:S(2)}, u32[]{:S(2)}) collective-permute-start(bf16[800,256]{1,0:T(8,128)(2,1)} %get-tuple-element.70), channel_id=1, source_target_pairs={{0,2},{2,0},{1,3},{3,1},{4,6},{6,4},{5,7},{7,5},{8,10},{10,8},{9,1... | collective-permute-start | bytes 1228808 | tf_op jit(solution)/shard_map/ppermute | solution.py:313
  21.2 2.2 %collective-permute-done.3.refs_2_ = bf16[272,256]{1,0:T(8,128)(2,1)S(1)} collective-permute-done((bf16[272,256]{1,0:T(8,128)(2,1)S(1)}, bf16[272,256]{1,0:T(8,128)(2,1)S(1)}, u32[]{:S(2)}, u32[]{:S(2)}) %collective-permute-start.3) | collective-permute-done | bytes 139296 | tf_op jit(solution)/shard_map/ppermute | solution.py:400
  23.4 0.1 maximum_select_fusion.own
  23.6 0.7 collective-permute-start.8
  24.2 3.1 %collective-permute-start.9 = (bf16[512,512]{1,0:T(8,128)(2,1)S(1)}, bf16[512,512]{1,0:T(8,128)(2,1)S(1)}, u32[]{:S(2)}, u32[]{:S(2)}) collective-permute-start(bf16[512,512]{1,0:T(8,128)(2,1)S(1)} %maximum_select_fusion.own), channel_id=1, source_target_pairs={{1,4},{0,13},{5,8},{4,1},{9,12},{8,5},{13,0},{12,9},{3,6},{2,15},{... | collective-permute-start | bytes 1572872 | tf_op jit(solution)/shard_map/ppermute | solution.py:324
  27.3 0.7 add_force.1
  28.1 2.1 %collective-permute-done.5.w_a = bf16[800,256]{1,0:T(8,128)(2,1)S(1)} collective-permute-done((bf16[800,256]{1,0:T(8,128)(2,1)}, bf16[800,256]{1,0:T(8,128)(2,1)S(1)}, u32[]{:S(2)}, u32[]{:S(2)}) %collective-permute-start.5) | collective-permute-done | bytes 409632 | tf_op jit(solution)/shard_map/ppermute | solution.py:313
  30.2 1.3 %collective-permute-start.10 = (bf16[800,256]{1,0:T(8,128)(2,1)S(1)}, bf16[800,256]{1,0:T(8,128)(2,1)S(1)}, u32[]{:S(2)}, u32[]{:S(2)}) collective-permute-start(bf16[800,256]{1,0:T(8,128)(2,1)S(1)} %collective-permute-done.5.w_a), channel_id=1, source_target_pairs={{0,16},{16,0},{1,17},{17,1},{2,18},{18,2},{3,19},{19,3},{4,20},{20... | collective-permute-start | bytes 1228808 | tf_op jit(solution)/shard_map/ppermute | solution.py:313
  31.5 4.0 %collective-permute-start.6 = (bf16[512,256]{1,0:T(8,128)(2,1)S(1)}, bf16[512,256]{1,0:T(8,128)(2,1)S(1)}, u32[]{:S(2)}, u32[]{:S(2)}) collective-permute-start(bf16[512,256]{1,0:T(8,128)(2,1)S(1)} %get-tuple-element.72), channel_id=1, source_target_pairs={{0,0},{1,2},{2,1},{3,3},{4,4},{5,6},{6,5},{7,7},{8,8},{9,10},{10,9... | collective-permute-start | bytes 786440 | tf_op jit(solution)/shard_map/ppermute | solution.py:297
  35.5 0.0 collective-permute-start.7
  35.6 0.1 collective-permute-start.11
  35.7 3.9 %collective-permute-done.9.rim = bf16[512,512]{1,0:T(8,128)(2,1)S(1)} collective-permute-done((bf16[512,512]{1,0:T(8,128)(2,1)S(1)}, bf16[512,512]{1,0:T(8,128)(2,1)S(1)}, u32[]{:S(2)}, u32[]{:S(2)}) %collective-permute-start.9) | collective-permute-done | bytes 524320 | tf_op jit(solution)/shard_map/ppermute | solution.py:324
  39.6 1.5 %collective-permute-start.12 = (bf16[800,256]{1,0:T(8,128)(2,1)S(1)}, bf16[800,256]{1,0:T(8,128)(2,1)S(1)}, u32[]{:S(2)}, u32[]{:S(2)}) collective-permute-start(bf16[800,256]{1,0:T(8,128)(2,1)S(1)} %collective-permute-done.5.w_a), channel_id=1, source_target_pairs={{0,1},{1,0},{2,3},{3,2},{4,5},{5,4},{6,7},{7,6},{8,9},{9,8},{10,11... | collective-permute-start | bytes 1228808 | tf_op jit(solution)/shard_map/ppermute | solution.py:313
  41.1 0.3 collective-permute-done.6
  41.3 4.7 %collective-permute-done.7 = bf16[512,256]{1,0:T(8,128)(2,1)S(1)} collective-permute-done((bf16[512,256]{1,0:T(8,128)(2,1)S(1)}, bf16[512,256]{1,0:T(8,128)(2,1)S(1)}, u32[]{:S(2)}, u32[]{:S(2)}) %collective-permute-start.7) | collective-permute-done | bytes 262176 | tf_op jit(solution)/shard_map/ppermute | solution.py:298
  46.0 1.3 %collective-permute-start.13 = (bf16[800,256]{1,0:T(8,128)(2,1)S(1)}, bf16[800,256]{1,0:T(8,128)(2,1)S(1)}, u32[]{:S(2)}, u32[]{:S(2)}) collective-permute-start(bf16[800,256]{1,0:T(8,128)(2,1)S(1)} %collective-permute-done.10.w_b), channel_id=1, source_target_pairs={{0,1},{1,0},{2,3},{3,2},{4,5},{5,4},{6,7},{7,6},{8,9},{9,8},{10,11... | collective-permute-start | bytes 1228808 | tf_op jit(solution)/shard_map/ppermute | solution.py:313
  47.3 0.1 maximum_select_fusion.1.own
  47.5 2.9 %collective-permute-done.11.w_a = bf16[800,256]{1,0:T(8,128)(2,1)S(1)} collective-permute-done((bf16[800,256]{1,0:T(8,128)(2,1)S(1)}, bf16[800,256]{1,0:T(8,128)(2,1)S(1)}, u32[]{:S(2)}, u32[]{:S(2)}) %collective-permute-start.11) | collective-permute-done | bytes 409632 | tf_op jit(solution)/shard_map/ppermute | solution.py:313
  50.4 1.4 %collective-permute-start.14 = (bf16[512,512]{1,0:T(8,128)(2,1)S(1)}, bf16[512,512]{1,0:T(8,128)(2,1)S(1)}, u32[]{:S(2)}, u32[]{:S(2)}) collective-permute-start(bf16[512,512]{1,0:T(8,128)(2,1)S(1)} %maximum_select_fusion.1.own), channel_id=1, source_target_pairs={{0,1},{1,0},{2,3},{3,2},{4,5},{5,4},{6,7},{7,6},{8,9},{9,8},{10,11... | collective-permute-start | bytes 1572872 | tf_op jit(solution)/shard_map/ppermute | solution.py:313
  51.8 3.1 %collective-permute-start.15 = (bf16[512,512]{1,0:T(8,128)(2,1)S(1)}, bf16[512,512]{1,0:T(8,128)(2,1)S(1)}, u32[]{:S(2)}, u32[]{:S(2)}) collective-permute-start(bf16[512,512]{1,0:T(8,128)(2,1)S(1)} %maximum_select_fusion.1.own), channel_id=1, source_target_pairs={{1,4},{5,8},{4,1},{9,12},{8,5},{12,9},{3,6},{7,10},{6,3},{11,14},{... | collective-permute-start | bytes 1572872 | tf_op jit(solution)/shard_map/ppermute | solution.py:324
  54.9 0.3 collective-permute-start.18
  55.3 6.3 %graph_layer.4.own = bf16[512,512]{1,0:T(8,128)(2,1)S(1)} custom-call(s32[2]{0:T(128)S(1)} %copy-done.11, s32[4096]{0:T(1024)S(1)} %bitcast.35, bf16[512,512]{1,0:T(8,128)(2,1)S(1)} %maximum_select_fusion.own, bf16[512,512]{1,0:T(8,128)(2,1)S(1)} %collective-permute-done.8.sib, bf16[512,512]{1,0:T(8,128)(2,1)S(1)} %collective-permute-done.9.rim, ...), custom_call_target="tpu_custom_call" | custom-call | flops 8589934592 | bytes 2621440 | tf_op jit(solution)/shard_map/graph_layer/pallas_call | solution.py:259
  61.6 0.6 collective-permute-start.16
  62.1 2.1 %collective-permute-done.18.w_b = bf16[800,256]{1,0:T(8,128)(2,1)S(1)} collective-permute-done((bf16[800,256]{1,0:T(8,128)(2,1)S(1)}, bf16[800,256]{1,0:T(8,128)(2,1)S(1)}, u32[]{:S(2)}, u32[]{:S(2)}) %collective-permute-start.18) | collective-permute-done | bytes 409632 | tf_op jit(solution)/shard_map/ppermute | solution.py:313
  64.3 3.5 %collective-permute-start.17 = (bf16[512,512]{1,0:T(8,128)(2,1)S(1)}, bf16[512,512]{1,0:T(8,128)(2,1)S(1)}, u32[]{:S(2)}, u32[]{:S(2)}) collective-permute-start(bf16[512,512]{1,0:T(8,128)(2,1)S(1)} %graph_layer.4.own), channel_id=1, source_target_pairs={{1,4},{0,13},{5,8},{4,1},{9,12},{8,5},{13,0},{12,9},{3,6},{2,15},{... | collective-permute-start | bytes 1572872 | tf_op jit(solution)/shard_map/ppermute | solution.py:324
  67.8 6.3 %graph_layer.5.own = bf16[512,512]{1,0:T(8,128)(2,1)S(1)} custom-call(s32[2]{0:T(128)S(1)} %copy-done.11, s32[4096]{0:T(1024)S(1)} %bitcast.33, bf16[512,512]{1,0:T(8,128)(2,1)S(1)} %maximum_select_fusion.1.own, bf16[512,512]{1,0:T(8,128)(2,1)S(1)} %collective-permute-done.14.sib, bf16[512,512]{1,0:T(8,128)(2,1)S(1)} %collective-permute-done.15.rim, ...), custom_call_target="tpu_custom_call" | custom-call | flops 8589934592 | bytes 2621440 | tf_op jit(solution)/shard_map/graph_layer/pallas_call | solution.py:259
  74.1 0.6 collective-permute-start.23
  74.6 3.0 %collective-permute-start.24 = (bf16[512,512]{1,0:T(8,128)(2,1)S(1)}, bf16[512,512]{1,0:T(8,128)(2,1)S(1)}, u32[]{:S(2)}, u32[]{:S(2)}) collective-permute-start(bf16[512,512]{1,0:T(8,128)(2,1)S(1)} %graph_layer.5.own), channel_id=1, source_target_pairs={{1,4},{5,8},{4,1},{9,12},{8,5},{12,9},{3,6},{7,10},{6,3},{11,14},{... | collective-permute-start | bytes 1572872 | tf_op jit(solution)/shard_map/ppermute | solution.py:324
  77.6 0.6 collective-permute-done.17.rim
  78.3 6.3 %graph_layer.6 = (bf16[512,256]{1,0:T(8,128)(2,1)S(1)}, bf16[512,256]{1,0:T(8,128)(2,1)S(1)}) custom-call(s32[2]{0:T(128)S(1)} %copy-done.11, s32[4096]{0:T(1024)S(1)} %bitcast.36, bf16[512,512]{1,0:T(8,128)(2,1)S(1)} %graph_layer.4.own, bf16[512,512]{1,0:T(8,128)(2,1)S(1)} %collective-permute-done.16.sib, bf16[512,512]{1,0:T(8,128)(2,1)S(1)} %collective-permute-done.17.rim, ...), custom_call_target="tpu_custom_call" | custom-call | flops 8589934592 | bytes 2621440 | tf_op jit(solution)/shard_map/graph_layer/pallas_call | solution.py:259
  84.6 1.9 %collective-permute-start.21 = (bf16[512,256]{1,0:T(8,128)(2,1)S(1)}, bf16[512,256]{1,0:T(8,128)(2,1)S(1)}, u32[]{:S(2)}, u32[]{:S(2)}) collective-permute-start(bf16[512,256]{1,0:T(8,128)(2,1)S(1)} %get-tuple-element.93), channel_id=1, source_target_pairs={{0,0},{1,2},{2,1},{3,3},{4,4},{5,6},{6,5},{7,7},{8,8},{9,10},{10,9... | collective-permute-start | bytes 786440 | tf_op jit(solution)/shard_map/ppermute | solution.py:303
  86.6 6.3 %graph_layer.7 = (bf16[512,256]{1,0:T(8,128)(2,1)S(1)}, bf16[512,256]{1,0:T(8,128)(2,1)S(1)}) custom-call(s32[2]{0:T(128)S(1)} %copy-done.11, s32[4096]{0:T(1024)S(1)} %bitcast.34, bf16[512,512]{1,0:T(8,128)(2,1)S(1)} %graph_layer.5.own, bf16[512,512]{1,0:T(8,128)(2,1)S(1)} %collective-permute-done.23.sib, bf16[512,512]{1,0:T(8,128)(2,1)S(1)} %collective-permute-done.24.rim, ...), custom_call_target="tpu_custom_call" | custom-call | flops 8589934592 | bytes 2621440 | tf_op jit(solution)/shard_map/graph_layer/pallas_call | solution.py:259
  92.9 3.6 %collective-permute-start.25 = (bf16[512,256]{1,0:T(8,128)(2,1)S(1)}, bf16[512,256]{1,0:T(8,128)(2,1)S(1)}, u32[]{:S(2)}, u32[]{:S(2)}) collective-permute-start(bf16[512,256]{1,0:T(8,128)(2,1)S(1)} %get-tuple-element.97), channel_id=1, source_target_pairs={{0,0},{1,2},{2,1},{3,3},{4,4},{5,6},{6,5},{7,7},{8,8},{9,10},{10,9... | collective-permute-start | bytes 786440 | tf_op jit(solution)/shard_map/ppermute | solution.py:303
  96.6 1.0 maximum_select_fusion.2
  97.7 4.5 %collective-permute-done.25 = bf16[512,256]{1,0:T(8,128)(2,1)S(1)} collective-permute-done((bf16[512,256]{1,0:T(8,128)(2,1)S(1)}, bf16[512,256]{1,0:T(8,128)(2,1)S(1)}, u32[]{:S(2)}, u32[]{:S(2)}) %collective-permute-start.25) | collective-permute-done | bytes 262176 | tf_op jit(solution)/shard_map/ppermute | solution.py:303
  102.2 1.2 %collective-permute-done.26 = bf16[512,256]{1,0:T(8,128)(2,1)S(1)} collective-permute-done((bf16[512,256]{1,0:T(8,128)(2,1)S(1)}, bf16[512,256]{1,0:T(8,128)(2,1)S(1)}, u32[]{:S(2)}, u32[]{:S(2)}) %collective-permute-start.26) | collective-permute-done | bytes 262176 | tf_op jit(solution)/shard_map/ppermute | solution.py:304
  103.4 1.0 maximum_select_fusion.3
  (66 shorter events, 0.3 us)
Async XLA Ops:
  0.6 0.7 copy-start.18
  0.7 0.7 copy-start.17
  0.7 0.7 copy-start.16
  1.4 1.0 %copy-start = (bf16[1,1024,256]{2,1,0:T(8,128)(2,1)S(1)}, bf16[1,1024,256]{2,1,0:T(8,128)(2,1)}, u32[]{:S(2)}) copy-start(bf16[1,1024,256]{2,1,0:T(8,128)(2,1)} %param.17) | copy-start | bytes 1572868
  2.4 2.9 %copy-start.1 = (bf16[1,1024,256]{2,1,0:T(8,128)(2,1)S(1)}, bf16[1,1024,256]{2,1,0:T(8,128)(2,1)}, u32[]{:S(2)}) copy-start(bf16[1,1024,256]{2,1,0:T(8,128)(2,1)} %param.17) | copy-start | bytes 1572868
  5.3 9.4 %copy-start.14 = (s32[1024]{0:T(1024)S(1)}, s32[1024]{0:T(1024)}, u32[]{:S(2)}) copy-start(s32[1024]{0:T(1024)} %param.20) | copy-start | bytes 12292
  5.3 9.4 %copy-start.15 = (s32[1024]{0:T(1024)S(1)}, s32[1024]{0:T(1024)}, u32[]{:S(2)}) copy-start(s32[1024]{0:T(1024)} %param.22) | copy-start | bytes 12292
  5.3 9.4 %copy-start.13 = (s32[1024,8]{0,1:T(8,128)S(1)}, s32[1024,8]{0,1:T(8,128)}, u32[]{:S(2)}) copy-start(s32[1024,8]{0,1:T(8,128)} %param.19) | copy-start | bytes 98308
  5.4 9.4 %copy-start.12 = (s32[1024,8]{0,1:T(8,128)S(1)}, s32[1024,8]{0,1:T(8,128)}, u32[]{:S(2)}) copy-start(s32[1024,8]{0,1:T(8,128)} %param.21) | copy-start | bytes 98308
  5.4 9.4 %collective-permute-start = (bf16[512,256]{1,0:T(8,128)(2,1)S(1)}, bf16[512,256]{1,0:T(8,128)(2,1)S(1)}, u32[]{:S(2)}, u32[]{:S(2)}) collective-permute-start(bf16[512,256]{1,0:T(8,128)(2,1)S(1)} %get-tuple-element.54), channel_id=1, source_target_pairs={{0,0},{1,2},{2,1},{3,3},{4,4},{5,6},{6,5},{7,7},{8,8},{9,10},{10,9... | collective-permute-start | bytes 786440 | tf_op jit(solution)/shard_map/ppermute | solution.py:297
  9.9 6.1 %collective-permute-start.1 = (bf16[512,256]{1,0:T(8,128)(2,1)S(1)}, bf16[512,256]{1,0:T(8,128)(2,1)S(1)}, u32[]{:S(2)}, u32[]{:S(2)}) collective-permute-start(bf16[512,256]{1,0:T(8,128)(2,1)S(1)} %get-tuple-element.55), channel_id=1, source_target_pairs={{0,1},{1,3},{2,0},{3,2},{4,5},{5,7},{6,4},{7,6},{8,9},{9,11},{10,8... | collective-permute-start | bytes 786440 | tf_op jit(solution)/shard_map/ppermute | solution.py:298
  9.9 11.2 %collective-permute-start.2 = (bf16[272,256]{1,0:T(8,128)(2,1)S(1)}, bf16[272,256]{1,0:T(8,128)(2,1)S(1)}, u32[]{:S(2)}, u32[]{:S(2)}) collective-permute-start(bf16[272,256]{1,0:T(8,128)(2,1)S(1)} %get-tuple-element.61), channel_id=1, source_target_pairs={{0,4},{4,8},{8,12},{12,0},{1,5},{5,9},{9,13},{13,1},{2,6},{6,10},{... | collective-permute-start | bytes 417800 | tf_op jit(solution)/shard_map/ppermute | solution.py:400
  11.3 12.1 %collective-permute-start.3 = (bf16[272,256]{1,0:T(8,128)(2,1)S(1)}, bf16[272,256]{1,0:T(8,128)(2,1)S(1)}, u32[]{:S(2)}, u32[]{:S(2)}) collective-permute-start(bf16[272,256]{1,0:T(8,128)(2,1)S(1)} %get-tuple-element.62), channel_id=1, source_target_pairs={{0,8},{4,12},{8,0},{12,4},{1,9},{5,13},{9,1},{13,5},{2,10},{6,14},... | collective-permute-start | bytes 417800 | tf_op jit(solution)/shard_map/ppermute | solution.py:400
  13.6 9.8 %collective-permute-start.4 = (bf16[272,256]{1,0:T(8,128)(2,1)S(1)}, bf16[272,256]{1,0:T(8,128)(2,1)S(1)}, u32[]{:S(2)}, u32[]{:S(2)}) collective-permute-start(bf16[272,256]{1,0:T(8,128)(2,1)S(1)} %get-tuple-element.63), channel_id=1, source_target_pairs={{0,12},{4,0},{8,4},{12,8},{1,13},{5,1},{9,5},{13,9},{2,14},{6,2},{... | collective-permute-start | bytes 417800 | tf_op jit(solution)/shard_map/ppermute | solution.py:400
  18.9 11.3 %collective-permute-start.5 = (bf16[800,256]{1,0:T(8,128)(2,1)}, bf16[800,256]{1,0:T(8,128)(2,1)S(1)}, u32[]{:S(2)}, u32[]{:S(2)}) collective-permute-start(bf16[800,256]{1,0:T(8,128)(2,1)} %get-tuple-element.70), channel_id=1, source_target_pairs={{0,2},{2,0},{1,3},{3,1},{4,6},{6,4},{5,7},{7,5},{8,10},{10,8},{9,1... | collective-permute-start | bytes 1228808 | tf_op jit(solution)/shard_map/ppermute | solution.py:313
  23.4 3.9 %copy-start.2 = (bf16[1,1024,256]{2,1,0:T(8,128)(2,1)S(1)}, bf16[1,1024,256]{2,1,0:T(8,128)(2,1)}, u32[]{:S(2)}) copy-start(bf16[1,1024,256]{2,1,0:T(8,128)(2,1)} %param.18) | copy-start | bytes 1572868
  23.6 12.0 %collective-permute-start.8 = (bf16[512,512]{1,0:T(8,128)(2,1)S(1)}, bf16[512,512]{1,0:T(8,128)(2,1)S(1)}, u32[]{:S(2)}, u32[]{:S(2)}) collective-permute-start(bf16[512,512]{1,0:T(8,128)(2,1)S(1)} %maximum_select_fusion.own), channel_id=1, source_target_pairs={{0,1},{1,0},{2,3},{3,2},{4,5},{5,4},{6,7},{7,6},{8,9},{9,8},{10,11... | collective-permute-start | bytes 1572872 | tf_op jit(solution)/shard_map/ppermute | solution.py:313
  24.2 15.4 %collective-permute-start.9 = (bf16[512,512]{1,0:T(8,128)(2,1)S(1)}, bf16[512,512]{1,0:T(8,128)(2,1)S(1)}, u32[]{:S(2)}, u32[]{:S(2)}) collective-permute-start(bf16[512,512]{1,0:T(8,128)(2,1)S(1)} %maximum_select_fusion.own), channel_id=1, source_target_pairs={{1,4},{0,13},{5,8},{4,1},{9,12},{8,5},{13,0},{12,9},{3,6},{2,15},{... | collective-permute-start | bytes 1572872 | tf_op jit(solution)/shard_map/ppermute | solution.py:324
  27.3 8.2 %copy-start.19 = (bf16[800,256]{1,0:T(8,128)(2,1)S(1)}, bf16[800,256]{1,0:T(8,128)(2,1)}, u32[]{:S(2)}) copy-start(bf16[800,256]{1,0:T(8,128)(2,1)} %get-tuple-element.80) | copy-start | bytes 1228804
  27.3 27.9 %copy-start.5 = (bf16[2,256,512]{2,1,0:T(8,128)(2,1)S(1)}, bf16[2,256,512]{2,1,0:T(8,128)(2,1)}, u32[]{:S(2)}) copy-start(bf16[2,256,512]{2,1,0:T(8,128)(2,1)} %w2_hbm.6) | copy-start | bytes 1572868
  30.2 25.0 %copy-start.9 = (bf16[2,256]{1,0:T(2,128)(2,1)S(1)}, bf16[2,256]{1,0:T(2,128)(2,1)}, u32[]{:S(2)}) copy-start(bf16[2,256]{1,0:T(2,128)(2,1)} %bias.6) | copy-start | bytes 3076
  30.2 25.1 %copy-start.3 = (bf16[2,512,256]{2,1,0:T(8,128)(2,1)S(1)}, bf16[2,512,256]{2,1,0:T(8,128)(2,1)}, u32[]{:S(2)}) copy-start(bf16[2,512,256]{2,1,0:T(8,128)(2,1)} %ws_hbm.6) | copy-start | bytes 1572868
  30.2 25.1 %copy-start.4 = (bf16[2,512,256]{2,1,0:T(8,128)(2,1)S(1)}, bf16[2,512,256]{2,1,0:T(8,128)(2,1)}, u32[]{:S(2)}) copy-start(bf16[2,512,256]{2,1,0:T(8,128)(2,1)} %wd_hbm.6) | copy-start | bytes 1572868
  30.2 25.1 %copy-start.11 = (s32[2]{0:T(128)S(1)}, s32[2]{0:T(128)}, u32[]{:S(2)}) copy-start(s32[2]{0:T(128)} %pad_add_fusion.1.spot_ref) | copy-start | bytes 28
  30.2 15.8 %collective-permute-start.10 = (bf16[800,256]{1,0:T(8,128)(2,1)S(1)}, bf16[800,256]{1,0:T(8,128)(2,1)S(1)}, u32[]{:S(2)}, u32[]{:S(2)}) collective-permute-start(bf16[800,256]{1,0:T(8,128)(2,1)S(1)} %collective-permute-done.5.w_a), channel_id=1, source_target_pairs={{0,16},{16,0},{1,17},{17,1},{2,18},{18,2},{3,19},{19,3},{4,20},{20... | collective-permute-start | bytes 1228808 | tf_op jit(solution)/shard_map/ppermute | solution.py:313
  31.5 9.8 %collective-permute-start.6 = (bf16[512,256]{1,0:T(8,128)(2,1)S(1)}, bf16[512,256]{1,0:T(8,128)(2,1)S(1)}, u32[]{:S(2)}, u32[]{:S(2)}) collective-permute-start(bf16[512,256]{1,0:T(8,128)(2,1)S(1)} %get-tuple-element.72), channel_id=1, source_target_pairs={{0,0},{1,2},{2,1},{3,3},{4,4},{5,6},{6,5},{7,7},{8,8},{9,10},{10,9... | collective-permute-start | bytes 786440 | tf_op jit(solution)/shard_map/ppermute | solution.py:297
  35.5 10.5 %collective-permute-start.7 = (bf16[512,256]{1,0:T(8,128)(2,1)S(1)}, bf16[512,256]{1,0:T(8,128)(2,1)S(1)}, u32[]{:S(2)}, u32[]{:S(2)}) collective-permute-start(bf16[512,256]{1,0:T(8,128)(2,1)S(1)} %get-tuple-element.73), channel_id=1, source_target_pairs={{0,1},{1,3},{2,0},{3,2},{4,5},{5,7},{6,4},{7,6},{8,9},{9,11},{10,8... | collective-permute-start | bytes 786440 | tf_op jit(solution)/shard_map/ppermute | solution.py:298
  35.6 14.8 %collective-permute-start.11 = (bf16[800,256]{1,0:T(8,128)(2,1)S(1)}, bf16[800,256]{1,0:T(8,128)(2,1)S(1)}, u32[]{:S(2)}, u32[]{:S(2)}) collective-permute-start(bf16[800,256]{1,0:T(8,128)(2,1)S(1)} %copy-done.19), channel_id=1, source_target_pairs={{0,2},{2,0},{1,3},{3,1},{4,6},{6,4},{5,7},{7,5},{8,10},{10,8},{9,1... | collective-permute-start | bytes 1228808 | tf_op jit(solution)/shard_map/ppermute | solution.py:313
  39.6 15.7 %collective-permute-start.12 = (bf16[800,256]{1,0:T(8,128)(2,1)S(1)}, bf16[800,256]{1,0:T(8,128)(2,1)S(1)}, u32[]{:S(2)}, u32[]{:S(2)}) collective-permute-start(bf16[800,256]{1,0:T(8,128)(2,1)S(1)} %collective-permute-done.5.w_a), channel_id=1, source_target_pairs={{0,1},{1,0},{2,3},{3,2},{4,5},{5,4},{6,7},{7,6},{8,9},{9,8},{10,11... | collective-permute-start | bytes 1228808 | tf_op jit(solution)/shard_map/ppermute | solution.py:313
  46.0 9.2 %collective-permute-start.13 = (bf16[800,256]{1,0:T(8,128)(2,1)S(1)}, bf16[800,256]{1,0:T(8,128)(2,1)S(1)}, u32[]{:S(2)}, u32[]{:S(2)}) collective-permute-start(bf16[800,256]{1,0:T(8,128)(2,1)S(1)} %collective-permute-done.10.w_b), channel_id=1, source_target_pairs={{0,1},{1,0},{2,3},{3,2},{4,5},{5,4},{6,7},{7,6},{8,9},{9,8},{10,11... | collective-permute-start | bytes 1228808 | tf_op jit(solution)/shard_map/ppermute | solution.py:313
  47.5 20.3 %copy-start.6 = (bf16[2,512,256]{2,1,0:T(8,128)(2,1)S(1)}, bf16[2,512,256]{2,1,0:T(8,128)(2,1)}, u32[]{:S(2)}) copy-start(bf16[2,512,256]{2,1,0:T(8,128)(2,1)} %ws_hbm.7) | copy-start | bytes 1572868
  47.5 20.3 %copy-start.7 = (bf16[2,512,256]{2,1,0:T(8,128)(2,1)S(1)}, bf16[2,512,256]{2,1,0:T(8,128)(2,1)}, u32[]{:S(2)}) copy-start(bf16[2,512,256]{2,1,0:T(8,128)(2,1)} %wd_hbm.7) | copy-start | bytes 1572868
  47.5 20.3 %copy-start.8 = (bf16[2,256,512]{2,1,0:T(8,128)(2,1)S(1)}, bf16[2,256,512]{2,1,0:T(8,128)(2,1)}, u32[]{:S(2)}) copy-start(bf16[2,256,512]{2,1,0:T(8,128)(2,1)} %w2_hbm.7) | copy-start | bytes 1572868
  47.5 20.3 %copy-start.10 = (bf16[2,256]{1,0:T(2,128)(2,1)S(1)}, bf16[2,256]{1,0:T(2,128)(2,1)}, u32[]{:S(2)}) copy-start(bf16[2,256]{1,0:T(2,128)(2,1)} %bias.7) | copy-start | bytes 3076
  50.4 17.3 %collective-permute-start.14 = (bf16[512,512]{1,0:T(8,128)(2,1)S(1)}, bf16[512,512]{1,0:T(8,128)(2,1)S(1)}, u32[]{:S(2)}, u32[]{:S(2)}) collective-permute-start(bf16[512,512]{1,0:T(8,128)(2,1)S(1)} %maximum_select_fusion.1.own), channel_id=1, source_target_pairs={{0,1},{1,0},{2,3},{3,2},{4,5},{5,4},{6,7},{7,6},{8,9},{9,8},{10,11... | collective-permute-start | bytes 1572872 | tf_op jit(solution)/shard_map/ppermute | solution.py:313
  51.8 15.9 %collective-permute-start.15 = (bf16[512,512]{1,0:T(8,128)(2,1)S(1)}, bf16[512,512]{1,0:T(8,128)(2,1)S(1)}, u32[]{:S(2)}, u32[]{:S(2)}) collective-permute-start(bf16[512,512]{1,0:T(8,128)(2,1)S(1)} %maximum_select_fusion.1.own), channel_id=1, source_target_pairs={{1,4},{5,8},{4,1},{9,12},{8,5},{12,9},{3,6},{7,10},{6,3},{11,14},{... | collective-permute-start | bytes 1572872 | tf_op jit(solution)/shard_map/ppermute | solution.py:324
  54.9 9.3 %collective-permute-start.18 = (bf16[800,256]{1,0:T(8,128)(2,1)S(1)}, bf16[800,256]{1,0:T(8,128)(2,1)S(1)}, u32[]{:S(2)}, u32[]{:S(2)}) collective-permute-start(bf16[800,256]{1,0:T(8,128)(2,1)S(1)} %collective-permute-done.11.w_a), channel_id=1, source_target_pairs={{0,16},{16,0},{1,17},{17,1},{2,18},{18,2},{3,19},{19,3},{4,20},{20... | collective-permute-start | bytes 1228808 | tf_op jit(solution)/shard_map/ppermute | solution.py:313
  55.2 19.4 %collective-permute-start.19 = (bf16[800,256]{1,0:T(8,128)(2,1)S(1)}, bf16[800,256]{1,0:T(8,128)(2,1)S(1)}, u32[]{:S(2)}, u32[]{:S(2)}) collective-permute-start(bf16[800,256]{1,0:T(8,128)(2,1)S(1)} %collective-permute-done.11.w_a), channel_id=1, source_target_pairs={{0,1},{1,0},{2,3},{3,2},{4,5},{5,4},{6,7},{7,6},{8,9},{9,8},{10,11... | collective-permute-start | bytes 1228808 | tf_op jit(solution)/shard_map/ppermute | solution.py:313
  61.6 16.0 %collective-permute-start.16 = (bf16[512,512]{1,0:T(8,128)(2,1)S(1)}, bf16[512,512]{1,0:T(8,128)(2,1)S(1)}, u32[]{:S(2)}, u32[]{:S(2)}) collective-permute-start(bf16[512,512]{1,0:T(8,128)(2,1)S(1)} %graph_layer.4.own), channel_id=1, source_target_pairs={{0,1},{1,0},{2,3},{3,2},{4,5},{5,4},{6,7},{7,6},{8,9},{9,8},{10,11... | collective-permute-start | bytes 1572872 | tf_op jit(solution)/shard_map/ppermute | solution.py:313
  64.3 14.0 %collective-permute-start.17 = (bf16[512,512]{1,0:T(8,128)(2,1)S(1)}, bf16[512,512]{1,0:T(8,128)(2,1)S(1)}, u32[]{:S(2)}, u32[]{:S(2)}) collective-permute-start(bf16[512,512]{1,0:T(8,128)(2,1)S(1)} %graph_layer.4.own), channel_id=1, source_target_pairs={{1,4},{0,13},{5,8},{4,1},{9,12},{8,5},{13,0},{12,9},{3,6},{2,15},{... | collective-permute-start | bytes 1572872 | tf_op jit(solution)/shard_map/ppermute | solution.py:324
  67.7 9.9 %collective-permute-start.20 = (bf16[800,256]{1,0:T(8,128)(2,1)S(1)}, bf16[800,256]{1,0:T(8,128)(2,1)S(1)}, u32[]{:S(2)}, u32[]{:S(2)}) collective-permute-start(bf16[800,256]{1,0:T(8,128)(2,1)S(1)} %collective-permute-done.18.w_b), channel_id=1, source_target_pairs={{0,1},{1,0},{2,3},{3,2},{4,5},{5,4},{6,7},{7,6},{8,9},{9,8},{10,11... | collective-permute-start | bytes 1228808 | tf_op jit(solution)/shard_map/ppermute | solution.py:313
  74.1 12.5 %collective-permute-start.23 = (bf16[512,512]{1,0:T(8,128)(2,1)S(1)}, bf16[512,512]{1,0:T(8,128)(2,1)S(1)}, u32[]{:S(2)}, u32[]{:S(2)}) collective-permute-start(bf16[512,512]{1,0:T(8,128)(2,1)S(1)} %graph_layer.5.own), channel_id=1, source_target_pairs={{0,1},{1,0},{2,3},{3,2},{4,5},{5,4},{6,7},{7,6},{8,9},{9,8},{10,11... | collective-permute-start | bytes 1572872 | tf_op jit(solution)/shard_map/ppermute | solution.py:313
  74.6 11.9 %collective-permute-start.24 = (bf16[512,512]{1,0:T(8,128)(2,1)S(1)}, bf16[512,512]{1,0:T(8,128)(2,1)S(1)}, u32[]{:S(2)}, u32[]{:S(2)}) collective-permute-start(bf16[512,512]{1,0:T(8,128)(2,1)S(1)} %graph_layer.5.own), channel_id=1, source_target_pairs={{1,4},{5,8},{4,1},{9,12},{8,5},{12,9},{3,6},{7,10},{6,3},{11,14},{... | collective-permute-start | bytes 1572872 | tf_op jit(solution)/shard_map/ppermute | solution.py:324
  84.6 12.0 %collective-permute-start.21 = (bf16[512,256]{1,0:T(8,128)(2,1)S(1)}, bf16[512,256]{1,0:T(8,128)(2,1)S(1)}, u32[]{:S(2)}, u32[]{:S(2)}) collective-permute-start(bf16[512,256]{1,0:T(8,128)(2,1)S(1)} %get-tuple-element.93), channel_id=1, source_target_pairs={{0,0},{1,2},{2,1},{3,3},{4,4},{5,6},{6,5},{7,7},{8,8},{9,10},{10,9... | collective-permute-start | bytes 786440 | tf_op jit(solution)/shard_map/ppermute | solution.py:303
  86.5 10.1 %collective-permute-start.22 = (bf16[512,256]{1,0:T(8,128)(2,1)S(1)}, bf16[512,256]{1,0:T(8,128)(2,1)S(1)}, u32[]{:S(2)}, u32[]{:S(2)}) collective-permute-start(bf16[512,256]{1,0:T(8,128)(2,1)S(1)} %get-tuple-element.94), channel_id=1, source_target_pairs={{0,2},{1,0},{2,3},{3,1},{4,6},{5,4},{6,7},{7,5},{8,10},{9,8},{10,1... | collective-permute-start | bytes 786440 | tf_op jit(solution)/shard_map/ppermute | solution.py:304
  92.9 9.3 %collective-permute-start.25 = (bf16[512,256]{1,0:T(8,128)(2,1)S(1)}, bf16[512,256]{1,0:T(8,128)(2,1)S(1)}, u32[]{:S(2)}, u32[]{:S(2)}) collective-permute-start(bf16[512,256]{1,0:T(8,128)(2,1)S(1)} %get-tuple-element.97), channel_id=1, source_target_pairs={{0,0},{1,2},{2,1},{3,3},{4,4},{5,6},{6,5},{7,7},{8,8},{9,10},{10,9... | collective-permute-start | bytes 786440 | tf_op jit(solution)/shard_map/ppermute | solution.py:303
  96.6 6.8 %collective-permute-start.26 = (bf16[512,256]{1,0:T(8,128)(2,1)S(1)}, bf16[512,256]{1,0:T(8,128)(2,1)S(1)}, u32[]{:S(2)}, u32[]{:S(2)}) collective-permute-start(bf16[512,256]{1,0:T(8,128)(2,1)S(1)} %get-tuple-element.98), channel_id=1, source_target_pairs={{0,2},{1,0},{2,3},{3,1},{4,6},{5,4},{6,7},{7,5},{8,10},{9,8},{10,1... | collective-permute-start | bytes 786440 | tf_op jit(solution)/shard_map/ppermute | solution.py:304

commit v10 on v6

--- a/solution.py
+++ b/solution.py
@@ -118,7 +118,7 @@
         in_specs=[pl.BlockSpec(memory_space=pltpu.SMEM), vmem, vmem],
         out_specs=(vmem,) * parts,
         compiler_params=pltpu.CompilerParams(vmem_limit_bytes=32 << 20),
-        cost_estimate=SMALL,
+        cost_estimate=pl.CostEstimate(flops=32 * rows**2 * feats, bytes_accessed=1, transcendentals=0),
         name="pick_rows",
     )(me, bnd, nodes)
 
@@ -369,28 +369,29 @@
     g_weights, r_weights = (g_ws, g_wd, g_w2), (r_ws, r_wd, r_w2)
     after = lax.optimization_barrier
 
+    same = lax.dynamic_slice(g_own, (part * half, 0), (half, g_own.shape[1]))
+    other = lax.dynamic_slice(g_own, ((1 - part) * half, 0), (half, g_own.shape[1]))
+    g_a, g_b = spread_rows(same, other)
+    order = [(graph, layer) for layer in range(layers) for graph in (0, 1)]
+    packs = list(pack_weights(order[:1], core1, g_weights, g_b1, r_weights, r_b1))
+    near_w = [swap(packs[0], "mp")]
     bnd = jnp.stack([bnd_src, bnd_part[:, 0], bnd_node])
+    bnd, packs[0], same, other = after((bnd, packs[0], same, other))
     pieces = pick_rows(me, bnd, g_own, parts, cap)
     landed = [pieces[0]]
     for k in range(1, parts):
         landed.append(lax.ppermute(pieces[k], "mesh", [(i, (i + k) % parts) for i in range(parts)]))
-    landed[0], g_late = after((landed[0], g_own))
-    same = lax.dynamic_slice(g_late, (part * half, 0), (half, g_own.shape[1]))
-    other = lax.dynamic_slice(g_late, ((1 - part) * half, 0), (half, g_own.shape[1]))
-    same, other, core1 = after((same, other, core1))
-    g_a, g_b = spread_rows(same, other)
+    landed[0], core1, g_a, g_b = after((landed[0], core1, g_a, g_b))
     idx = edge_offsets(jnp.stack([g_nbr, r_nbr]), jnp.stack([g_count, r_count]), core)
-
-    order = [(graph, layer) for layer in range(layers) for graph in (0, 1)]
-    packs = list(pack_weights(order, core1, g_weights, g_b1, r_weights, r_b1))
-    landed[1], packs[0] = after((landed[1], packs[0]))
-    near_w = [swap(packs[0], "mp")]
+    packs += pack_weights(order[1:], core1, g_weights, g_b1, r_weights, r_b1)
     g_idx, r_idx = idx[0], idx[1]
-    g_a, g_b, g_idx, r_idx, packs[1], *landed = after((g_a, g_b, g_idx, r_idx, packs[1], *landed))
+    g_a, g_b, g_idx, r_idx, packs[1], near_w[0], *landed = after(
+        (g_a, g_b, g_idx, r_idx, packs[1], near_w[0], *landed)
+    )
     planet = ordered(core, g_a, g_b, 1)
     g_sib, g_rim = swap(planet, "batch"), rims(planet, True)
-    *r_pair, packs[1] = after((*add_force(part.reshape(1), r_own, landed, cap), packs[1]))
-    r_a, r_b = spread_rows(*r_pair)
+    r_a, r_b = spread_rows(*add_force(part.reshape(1), r_own, landed, cap))
+    r_a, r_b, packs[1] = after((r_a, r_b, packs[1]))
     near_w.append(swap(packs[1], "mp"))
     r_a, r_b, g_sib, g_rim, near_w[0] = after((r_a, r_b, g_sib, g_rim, near_w[0]))
     regional, g_idx = after((ordered(core, r_a, r_b, 1), g_idx))
@@ -419,7 +420,8 @@
                 regional, core1 = after((regional, core1))
                 r_sib, r_rim = swap(regional, "batch"), rims(regional, False)
     g_out = ordered(part, *gather_rows(*planet), 0)
-    r_out = ordered(part, *gather_rows(*regional), 0)
+    g_out, *regional_rows = after((g_out, *gather_rows(*regional)))
+    r_out = ordered(part, *regional_rows, 0)
     return g_out[None], r_out[None]
 
 

time: 104 us -> 107 us (1.029)
  Pallas kernels: 31.5 us -> 33.8 us
  waiting for transfers between devices: 26 us -> 27.6 us
    ppermute x2, waiting for transfers between devices: 2.55 us -> 6.97 us  [gather_rows(): same = lax.ppermute(a, ('mp', 'batch'), [(0, 0), (1, 2), (2, 1), (3, 3)])]
    ppermute x2, waiting for transfers between devices: 8.02 us -> 4.29 us  [spread_rows(): a = lax.ppermute(same, ('mp', 'batch'), [(0, 0), (1, 2), (2, 1), (3, 3)])]
    pallas_call x1 -> x2, Pallas kernels: 3.41 us -> 5.68 us  [pack_weights(): pl.pallas_call(functools.partial(pack_kernel, order), out_shape=(jax.Shap...]
    ppermute x2, waiting for transfers between devices: 1.93 us -> 0.01 us  [gather_rows(): other = lax.ppermute(b, ('mp', 'batch'), [(0, 2), (1, 0), (2, 3), (3, 1)])]
    unnamed x47 -> x43, local copies, waits for them, and re-layouts: 2.52 us -> 0.81 us
    ppermute x12, waiting for transfers between devices: 8.12 us -> 9.23 us  [swap(): return lax.ppermute(values, axis, [(0, 1), (1, 0)])]
  transfers between devices with their start and end apart: 27 -> 27, of which waited for: 7 -> 7; matrix products, arithmetic and copies ran while one was open for 1% -> 1% of each run, Pallas kernels for 28% -> 32%
where the time goes in v10:
time: 107 us; the launch traced here: 106 us
  starting transfers between devices  39.3 us (37%)
  Pallas kernels  33.8 us (32%)
  waiting for transfers between devices  27.6 us (26%)
  other arithmetic  2.42 us (2%)
  local copies, waits for them, and re-layouts  1.88 us (2%)
  between operations  1.1 us (1%)
    pallas_call x4, Pallas kernels, run_layer(): pl.pallas_call(functools.partial(layer_kernel, layer, slots, last), out_s...  25.2 us
    ppermute x4, starting transfers between devices, rims(): return lax.ppermute(own, ('mesh', 'batch'), pairs)  10.7 us
    ppermute x12, waiting for transfers between devices, swap(): return lax.ppermute(values, axis, [(0, 1), (1, 0)])  9.23 us
    ppermute x2, starting transfers between devices, spread_rows(): a = lax.ppermute(same, ('mp', 'batch'), [(0, 0), (1, 2), (2, 1), (3, 3)])  9.2 us
    ppermute x12, starting transfers between devices, swap(): return lax.ppermute(values, axis, [(0, 1), (1, 0)])  8.52 us
    ppermute x2, waiting for transfers between devices, gather_rows(): same = lax.ppermute(a, ('mp', 'batch'), [(0, 0), (1, 2), (2, 1), (3, 3)])  6.97 us
    pallas_call x2, Pallas kernels, pack_weights(): pl.pallas_call(functools.partial(pack_kernel, order), out_shape=(jax.Shap...  5.68 us
    ppermute x2, starting transfers between devices, gather_rows(): same = lax.ppermute(a, ('mp', 'batch'), [(0, 0), (1, 2), (2, 1), (3, 3)])  5.55 us
  transfers between devices with their start and end apart: 27, of which 7 were waited for; matrix products, arithmetic and copies ran while one was open for 1% of the time, Pallas kernels for 32%

profile of v10, /device:TPU:1, one launch (start us, length us, event | category | flops | bytes accessed | tf_op | source)
XLA Modules:
  0.0 106.1 jit_solution(3492443149802034955)
XLA Ops:
  0.6 1.1 %dynamic-slice_bitcast_fusion = (bf16[512,256]{1,0:T(8,128)(2,1)S(1)}, bf16[512,256]{1,0:T(8,128)(2,1)S(1)}) fusion(bf16[1,1024,256]{2,1,0:T(8,128)(2,1)} %param.17, s32[]{:T(128)S(6)} %select_n.78, s32[]{:T(128)S(6)} %select_n.77), kind=kLoop, calls=%fused_computation.4 | loop fusion | bytes 1048584 | tf_op jit(solution)/shard_map/dynamic_slice | solution.py:373
  1.7 4.5 %collective-permute-start = (bf16[512,256]{1,0:T(8,128)(2,1)S(1)}, bf16[512,256]{1,0:T(8,128)(2,1)S(1)}, u32[]{:S(2)}, u32[]{:S(2)}) collective-permute-start(bf16[512,256]{1,0:T(8,128)(2,1)S(1)} %get-tuple-element.119), channel_id=1, source_target_pairs={{0,0},{1,2},{2,1},{3,3},{4,4},{5,6},{6,5},{7,7},{8,8},{9,10},{10,9... | collective-permute-start | bytes 786440 | tf_op jit(solution)/shard_map/ppermute | solution.py:290
  6.2 0.0 collective-permute-start.1
  6.3 2.6 %pack_weights.2 = bf16[784,256]{1,0:T(8,128)(2,1)} custom-call(s32[1]{0:T(128)} %bitcast.4.core_ref, bf16[2,256]{1,0:T(2,128)(2,1)} %bias.6, bf16[2,256]{1,0:T(2,128)(2,1)} %bias.7, bf16[2,512,256]{2,1,0:T(8,128)(2,1)} %ws_hbm.6, bf16[2,512,256]{2,1,0:T(8,128)(2,1)} %wd_hbm.6, bf16[2,256,512]{2,1,0:T(8,128)(2,1)} %w2_hbm.6, bf16[2,512,256]{2,1,0:T(8,128)(2,1)} %ws_hbm.7, ...), custom_call_target="tpu_custom_call" | custom-call | flops 4294967296 | bytes 1 | tf_op jit(solution)/shard_map/pack_weights/pallas_call | solution.py:342
  8.9 0.2 collective-permute-start.2
  9.0 0.7 copy-done.15
  9.8 2.2 %pick_rows.1 = (bf16[272,256]{1,0:T(8,128)(2,1)S(1)}, bf16[272,256]{1,0:T(8,128)(2,1)S(1)}, bf16[272,256]{1,0:T(8,128)(2,1)S(1)}, bf16[272,256]{1,0:T(8,128)(2,1)S(1)}) custom-call(s32[1]{0:T(128)} %bitcast.me_ref, s32[3,512]{1,0:T(4,128)S(1)} %pad_add_fusion.bnd_ref, bf16[1024,256]{1,0:T(8,128)(2,1)S(1)} %bitcast.33), custom_call_target="tpu_custom_call" | custom-call | flops 8589934592 | bytes 1 | tf_op jit(solution)/shard_map/pick_rows/pallas_call | solution.py:115
  12.0 1.4 %collective-permute-start.3 = (bf16[272,256]{1,0:T(8,128)(2,1)S(1)}, bf16[272,256]{1,0:T(8,128)(2,1)S(1)}, u32[]{:S(2)}, u32[]{:S(2)}) collective-permute-start(bf16[272,256]{1,0:T(8,128)(2,1)S(1)} %get-tuple-element.69), channel_id=1, source_target_pairs={{0,4},{4,8},{8,12},{12,0},{1,5},{5,9},{9,13},{13,1},{2,6},{6,10},{... | collective-permute-start | bytes 417800 | tf_op jit(solution)/shard_map/ppermute | solution.py:383
  13.4 2.3 %collective-permute-start.4 = (bf16[272,256]{1,0:T(8,128)(2,1)S(1)}, bf16[272,256]{1,0:T(8,128)(2,1)S(1)}, u32[]{:S(2)}, u32[]{:S(2)}) collective-permute-start(bf16[272,256]{1,0:T(8,128)(2,1)S(1)} %get-tuple-element.70), channel_id=1, source_target_pairs={{0,8},{4,12},{8,0},{12,4},{1,9},{5,13},{9,1},{13,5},{2,10},{6,14},... | collective-permute-start | bytes 417800 | tf_op jit(solution)/shard_map/ppermute | solution.py:383
  15.7 0.1 fusion.5
  15.9 1.1 %collective-permute-start.5 = (bf16[272,256]{1,0:T(8,128)(2,1)S(1)}, bf16[272,256]{1,0:T(8,128)(2,1)S(1)}, u32[]{:S(2)}, u32[]{:S(2)}) collective-permute-start(bf16[272,256]{1,0:T(8,128)(2,1)S(1)} %get-tuple-element.71), channel_id=1, source_target_pairs={{0,12},{4,0},{8,4},{12,8},{1,13},{5,1},{9,5},{13,9},{2,14},{6,2},{... | collective-permute-start | bytes 417800 | tf_op jit(solution)/shard_map/ppermute | solution.py:383
  17.0 3.1 %pack_weights.3 = (bf16[784,256]{1,0:T(8,128)(2,1)}, bf16[784,256]{1,0:T(8,128)(2,1)}, bf16[784,256]{1,0:T(8,128)(2,1)}) custom-call(s32[1]{0:T(128)} %bitcast.4.core_ref, bf16[2,256]{1,0:T(2,128)(2,1)} %bias.6, bf16[2,256]{1,0:T(2,128)(2,1)} %bias.7, bf16[2,512,256]{2,1,0:T(8,128)(2,1)} %ws_hbm.6, bf16[2,512,256]{2,1,0:T(8,128)(2,1)} %wd_hbm.6, ...), custom_call_target="tpu_custom_call" | custom-call | flops 4294967296 | bytes 1 | tf_op jit(solution)/shard_map/pack_weights/pallas_call | solution.py:342
  20.1 5.4 %collective-permute-done.4.refs_2_ = bf16[272,256]{1,0:T(8,128)(2,1)S(1)} collective-permute-done((bf16[272,256]{1,0:T(8,128)(2,1)S(1)}, bf16[272,256]{1,0:T(8,128)(2,1)S(1)}, u32[]{:S(2)}, u32[]{:S(2)}) %collective-permute-start.4) | collective-permute-done | bytes 139296 | tf_op jit(solution)/shard_map/ppermute | solution.py:383
  25.5 0.1 maximum_select_fusion.own
  25.6 0.7 collective-permute-start.10
  26.3 3.1 %collective-permute-start.11 = (bf16[512,512]{1,0:T(8,128)(2,1)S(1)}, bf16[512,512]{1,0:T(8,128)(2,1)S(1)}, u32[]{:S(2)}, u32[]{:S(2)}) collective-permute-start(bf16[512,512]{1,0:T(8,128)(2,1)S(1)} %maximum_select_fusion.own), channel_id=1, source_target_pairs={{1,4},{0,13},{5,8},{4,1},{9,12},{8,5},{13,0},{12,9},{3,6},{2,15},{... | collective-permute-start | bytes 1572872 | tf_op jit(solution)/shard_map/ppermute | solution.py:317
  29.4 0.7 add_force.1
  30.1 4.7 %collective-permute-start.6 = (bf16[512,256]{1,0:T(8,128)(2,1)S(1)}, bf16[512,256]{1,0:T(8,128)(2,1)S(1)}, u32[]{:S(2)}, u32[]{:S(2)}) collective-permute-start(bf16[512,256]{1,0:T(8,128)(2,1)S(1)} %get-tuple-element.76), channel_id=1, source_target_pairs={{0,0},{1,2},{2,1},{3,3},{4,4},{5,6},{6,5},{7,7},{8,8},{9,10},{10,9... | collective-permute-start | bytes 786440 | tf_op jit(solution)/shard_map/ppermute | solution.py:290
  34.9 0.0 collective-permute-start.7
  34.9 4.3 %collective-permute-done.6 = bf16[512,256]{1,0:T(8,128)(2,1)S(1)} collective-permute-done((bf16[512,256]{1,0:T(8,128)(2,1)S(1)}, bf16[512,256]{1,0:T(8,128)(2,1)S(1)}, u32[]{:S(2)}, u32[]{:S(2)}) %collective-permute-start.6) | collective-permute-done | bytes 262176 | tf_op jit(solution)/shard_map/ppermute | solution.py:290
  39.2 1.8 %collective-permute-done.7 = bf16[512,256]{1,0:T(8,128)(2,1)S(1)} collective-permute-done((bf16[512,256]{1,0:T(8,128)(2,1)S(1)}, bf16[512,256]{1,0:T(8,128)(2,1)S(1)}, u32[]{:S(2)}, u32[]{:S(2)}) %collective-permute-start.7) | collective-permute-done | bytes 262176 | tf_op jit(solution)/shard_map/ppermute | solution.py:291
  40.9 2.2 %collective-permute-start.8 = (bf16[784,256]{1,0:T(8,128)(2,1)S(1)}, bf16[784,256]{1,0:T(8,128)(2,1)S(1)}, u32[]{:S(2)}, u32[]{:S(2)}) collective-permute-start(bf16[784,256]{1,0:T(8,128)(2,1)S(1)} %copy-done.19), channel_id=1, source_target_pairs={{0,2},{2,0},{1,3},{3,1},{4,6},{6,4},{5,7},{7,5},{8,10},{10,8},{9,1... | collective-permute-start | bytes 1204232 | tf_op jit(solution)/shard_map/ppermute | solution.py:306
  43.2 0.1 maximum_select_fusion.1.own
  43.3 0.6 collective-permute-start.14
  43.9 1.9 %collective-permute-start.15 = (bf16[512,512]{1,0:T(8,128)(2,1)S(1)}, bf16[512,512]{1,0:T(8,128)(2,1)S(1)}, u32[]{:S(2)}, u32[]{:S(2)}) collective-permute-start(bf16[512,512]{1,0:T(8,128)(2,1)S(1)} %maximum_select_fusion.1.own), channel_id=1, source_target_pairs={{1,4},{5,8},{4,1},{9,12},{8,5},{12,9},{3,6},{7,10},{6,3},{11,14},{... | collective-permute-start | bytes 1572872 | tf_op jit(solution)/shard_map/ppermute | solution.py:317
  45.8 6.0 %collective-permute-done.8.near_w = bf16[784,256]{1,0:T(8,128)(2,1)S(1)} collective-permute-done((bf16[784,256]{1,0:T(8,128)(2,1)S(1)}, bf16[784,256]{1,0:T(8,128)(2,1)S(1)}, u32[]{:S(2)}, u32[]{:S(2)}) %collective-permute-start.8) | collective-permute-done | bytes 401440 | tf_op jit(solution)/shard_map/ppermute | solution.py:306
  51.8 1.8 %collective-permute-start.9 = (bf16[784,256]{1,0:T(8,128)(2,1)S(1)}, bf16[784,256]{1,0:T(8,128)(2,1)S(1)}, u32[]{:S(2)}, u32[]{:S(2)}) collective-permute-start(bf16[784,256]{1,0:T(8,128)(2,1)S(1)} %copy-done.18), channel_id=1, source_target_pairs={{0,2},{2,0},{1,3},{3,1},{4,6},{6,4},{5,7},{7,5},{8,10},{10,8},{9,1... | collective-permute-start | bytes 1204232 | tf_op jit(solution)/shard_map/ppermute | solution.py:306
  53.7 0.4 collective-permute-start.16
  54.1 6.3 %graph_layer.4.own = bf16[512,512]{1,0:T(8,128)(2,1)S(1)} custom-call(s32[1]{0:T(128)} %bitcast.4.core_ref, s32[4096]{0:T(1024)S(1)} %bitcast.37, bf16[512,512]{1,0:T(8,128)(2,1)S(1)} %maximum_select_fusion.own, bf16[512,512]{1,0:T(8,128)(2,1)S(1)} %collective-permute-done.10.sib, bf16[512,512]{1,0:T(8,128)(2,1)S(1)} %collective-permute-done.11.rim, ...), custom_call_target="tpu_custom_call" | custom-call | flops 8589934592 | bytes 2621440 | tf_op jit(solution)/shard_map/graph_layer/pallas_call | solution.py:252
  60.4 0.1 collective-permute-start.17
  60.6 1.6 %collective-permute-done.9.near_w = bf16[784,256]{1,0:T(8,128)(2,1)S(1)} collective-permute-done((bf16[784,256]{1,0:T(8,128)(2,1)S(1)}, bf16[784,256]{1,0:T(8,128)(2,1)S(1)}, u32[]{:S(2)}, u32[]{:S(2)}) %collective-permute-start.9) | collective-permute-done | bytes 401440 | tf_op jit(solution)/shard_map/ppermute | solution.py:306
  62.2 1.2 %collective-permute-start.18 = (bf16[512,512]{1,0:T(8,128)(2,1)S(1)}, bf16[512,512]{1,0:T(8,128)(2,1)S(1)}, u32[]{:S(2)}, u32[]{:S(2)}) collective-permute-start(bf16[512,512]{1,0:T(8,128)(2,1)S(1)} %graph_layer.4.own), channel_id=1, source_target_pairs={{1,4},{0,13},{5,8},{4,1},{9,12},{8,5},{13,0},{12,9},{3,6},{2,15},{... | collective-permute-start | bytes 1572872 | tf_op jit(solution)/shard_map/ppermute | solution.py:317
  63.5 1.5 %collective-permute-start.13 = (bf16[784,256]{1,0:T(8,128)(2,1)S(1)}, bf16[784,256]{1,0:T(8,128)(2,1)S(1)}, u32[]{:S(2)}, u32[]{:S(2)}) collective-permute-start(bf16[784,256]{1,0:T(8,128)(2,1)S(1)} %copy-done.17), channel_id=1, source_target_pairs={{0,2},{2,0},{1,3},{3,1},{4,6},{6,4},{5,7},{7,5},{8,10},{10,8},{9,1... | collective-permute-start | bytes 1204232 | tf_op jit(solution)/shard_map/ppermute | solution.py:306
  64.9 0.9 collective-permute-start.19
  65.9 6.3 %graph_layer.5.own = bf16[512,512]{1,0:T(8,128)(2,1)S(1)} custom-call(s32[1]{0:T(128)} %bitcast.4.core_ref, s32[4096]{0:T(1024)S(1)} %bitcast.35, bf16[512,512]{1,0:T(8,128)(2,1)S(1)} %maximum_select_fusion.1.own, bf16[512,512]{1,0:T(8,128)(2,1)S(1)} %collective-permute-done.14.sib, bf16[512,512]{1,0:T(8,128)(2,1)S(1)} %collective-permute-done.15.rim, ...), custom_call_target="tpu_custom_call" | custom-call | flops 8589934592 | bytes 2621440 | tf_op jit(solution)/shard_map/graph_layer/pallas_call | solution.py:252
  72.1 0.1 collective-permute-start.22
  72.2 1.5 %collective-permute-done.13.near_w = bf16[784,256]{1,0:T(8,128)(2,1)S(1)} collective-permute-done((bf16[784,256]{1,0:T(8,128)(2,1)S(1)}, bf16[784,256]{1,0:T(8,128)(2,1)S(1)}, u32[]{:S(2)}, u32[]{:S(2)}) %collective-permute-start.13) | collective-permute-done | bytes 401440 | tf_op jit(solution)/shard_map/ppermute | solution.py:306
  73.8 4.4 %collective-permute-start.23 = (bf16[512,512]{1,0:T(8,128)(2,1)S(1)}, bf16[512,512]{1,0:T(8,128)(2,1)S(1)}, u32[]{:S(2)}, u32[]{:S(2)}) collective-permute-start(bf16[512,512]{1,0:T(8,128)(2,1)S(1)} %graph_layer.5.own), channel_id=1, source_target_pairs={{1,4},{5,8},{4,1},{9,12},{8,5},{12,9},{3,6},{7,10},{6,3},{11,14},{... | collective-permute-start | bytes 1572872 | tf_op jit(solution)/shard_map/ppermute | solution.py:317
  78.2 0.1 collective-permute-start.24
  78.3 6.3 %graph_layer.6 = (bf16[512,256]{1,0:T(8,128)(2,1)S(1)}, bf16[512,256]{1,0:T(8,128)(2,1)S(1)}) custom-call(s32[1]{0:T(128)} %bitcast.4.core_ref, s32[4096]{0:T(1024)S(1)} %bitcast.38, bf16[512,512]{1,0:T(8,128)(2,1)S(1)} %graph_layer.4.own, bf16[512,512]{1,0:T(8,128)(2,1)S(1)} %collective-permute-done.17.sib, ...), custom_call_target="tpu_custom_call" | custom-call | flops 8589934592 | bytes 2621440 | tf_op jit(solution)/shard_map/graph_layer/pallas_call | solution.py:252
  84.6 0.5 collective-permute-start.21
  85.1 3.3 %collective-permute-start.20 = (bf16[512,256]{1,0:T(8,128)(2,1)S(1)}, bf16[512,256]{1,0:T(8,128)(2,1)S(1)}, u32[]{:S(2)}, u32[]{:S(2)}) collective-permute-start(bf16[512,256]{1,0:T(8,128)(2,1)S(1)} %get-tuple-element.108), channel_id=1, source_target_pairs={{0,0},{1,2},{2,1},{3,3},{4,4},{5,6},{6,5},{7,7},{8,8},{9,10},{10,9... | collective-permute-start | bytes 786440 | tf_op jit(solution)/shard_map/ppermute | solution.py:296
  88.5 6.3 %graph_layer.7 = (bf16[512,256]{1,0:T(8,128)(2,1)S(1)}, bf16[512,256]{1,0:T(8,128)(2,1)S(1)}) custom-call(s32[1]{0:T(128)} %bitcast.4.core_ref, s32[4096]{0:T(1024)S(1)} %bitcast.36, bf16[512,512]{1,0:T(8,128)(2,1)S(1)} %graph_layer.5.own, bf16[512,512]{1,0:T(8,128)(2,1)S(1)} %collective-permute-done.22.sib, ...), custom_call_target="tpu_custom_call" | custom-call | flops 8589934592 | bytes 2621440 | tf_op jit(solution)/shard_map/graph_layer/pallas_call | solution.py:252
  94.8 2.3 %collective-permute-start.25 = (bf16[512,256]{1,0:T(8,128)(2,1)S(1)}, bf16[512,256]{1,0:T(8,128)(2,1)S(1)}, u32[]{:S(2)}, u32[]{:S(2)}) collective-permute-start(bf16[512,256]{1,0:T(8,128)(2,1)S(1)} %get-tuple-element.113), channel_id=1, source_target_pairs={{0,0},{1,2},{2,1},{3,3},{4,4},{5,6},{6,5},{7,7},{8,8},{9,10},{10,9... | collective-permute-start | bytes 786440 | tf_op jit(solution)/shard_map/ppermute | solution.py:296
  97.1 0.0 collective-permute-start.26
  97.1 1.0 maximum_select_fusion.2
  98.1 7.0 %collective-permute-done.25 = bf16[512,256]{1,0:T(8,128)(2,1)S(1)} collective-permute-done((bf16[512,256]{1,0:T(8,128)(2,1)S(1)}, bf16[512,256]{1,0:T(8,128)(2,1)S(1)}, u32[]{:S(2)}, u32[]{:S(2)}) %collective-permute-start.25) | collective-permute-done | bytes 262176 | tf_op jit(solution)/shard_map/ppermute | solution.py:296
  105.1 1.0 maximum_select_fusion.3
  (66 shorter events, 0.2 us)
Async XLA Ops:
  1.7 14.1 %collective-permute-start = (bf16[512,256]{1,0:T(8,128)(2,1)S(1)}, bf16[512,256]{1,0:T(8,128)(2,1)S(1)}, u32[]{:S(2)}, u32[]{:S(2)}) collective-permute-start(bf16[512,256]{1,0:T(8,128)(2,1)S(1)} %get-tuple-element.119), channel_id=1, source_target_pairs={{0,0},{1,2},{2,1},{3,3},{4,4},{5,6},{6,5},{7,7},{8,8},{9,10},{10,9... | collective-permute-start | bytes 786440 | tf_op jit(solution)/shard_map/ppermute | solution.py:290
  6.2 10.8 %collective-permute-start.1 = (bf16[512,256]{1,0:T(8,128)(2,1)S(1)}, bf16[512,256]{1,0:T(8,128)(2,1)S(1)}, u32[]{:S(2)}, u32[]{:S(2)}) collective-permute-start(bf16[512,256]{1,0:T(8,128)(2,1)S(1)} %get-tuple-element.118), channel_id=1, source_target_pairs={{0,1},{1,3},{2,0},{3,2},{4,5},{5,7},{6,4},{7,6},{8,9},{9,11},{10,8... | collective-permute-start | bytes 786440 | tf_op jit(solution)/shard_map/ppermute | solution.py:291
  6.3 2.8 %copy-start.16 = (s32[512]{0:T(512)S(1)}, s32[512]{0:T(512)}, u32[]{:S(2)}) copy-start(s32[512]{0:T(512)} %param.23) | copy-start | bytes 6148
  6.3 3.4 %copy-start = (bf16[1,1024,256]{2,1,0:T(8,128)(2,1)S(1)}, bf16[1,1024,256]{2,1,0:T(8,128)(2,1)}, u32[]{:S(2)}) copy-start(bf16[1,1024,256]{2,1,0:T(8,128)(2,1)} %param.17) | copy-start | bytes 1572868
  8.9 16.6 %collective-permute-start.2 = (bf16[784,256]{1,0:T(8,128)(2,1)}, bf16[784,256]{1,0:T(8,128)(2,1)S(1)}, u32[]{:S(2)}, u32[]{:S(2)}) collective-permute-start(bf16[784,256]{1,0:T(8,128)(2,1)} %pack_weights.2), channel_id=1, source_target_pairs={{0,2},{2,0},{1,3},{3,1},{4,6},{6,4},{5,7},{7,5},{8,10},{10,8},{9,1... | collective-permute-start | bytes 1204232 | tf_op jit(solution)/shard_map/ppermute | solution.py:306
  9.0 0.7 copy-start.15
  9.0 0.7 copy-start.14
  9.7 5.9 %copy-start.12 = (s32[1024]{0:T(1024)S(1)}, s32[1024]{0:T(1024)}, u32[]{:S(2)}) copy-start(s32[1024]{0:T(1024)} %param.20) | copy-start | bytes 12292
  9.7 5.9 %copy-start.13 = (s32[1024]{0:T(1024)S(1)}, s32[1024]{0:T(1024)}, u32[]{:S(2)}) copy-start(s32[1024]{0:T(1024)} %param.22) | copy-start | bytes 12292
  9.8 6.0 %copy-start.11 = (s32[1024,8]{0,1:T(8,128)S(1)}, s32[1024,8]{0,1:T(8,128)}, u32[]{:S(2)}) copy-start(s32[1024,8]{0,1:T(8,128)} %param.19) | copy-start | bytes 98308
  12.0 3.8 %copy-start.10 = (s32[1024,8]{0,1:T(8,128)S(1)}, s32[1024,8]{0,1:T(8,128)}, u32[]{:S(2)}) copy-start(s32[1024,8]{0,1:T(8,128)} %param.21) | copy-start | bytes 98308
  12.0 8.1 %collective-permute-start.3 = (bf16[272,256]{1,0:T(8,128)(2,1)S(1)}, bf16[272,256]{1,0:T(8,128)(2,1)S(1)}, u32[]{:S(2)}, u32[]{:S(2)}) collective-permute-start(bf16[272,256]{1,0:T(8,128)(2,1)S(1)} %get-tuple-element.69), channel_id=1, source_target_pairs={{0,4},{4,8},{8,12},{12,0},{1,5},{5,9},{9,13},{13,1},{2,6},{6,10},{... | collective-permute-start | bytes 417800 | tf_op jit(solution)/shard_map/ppermute | solution.py:383
  13.4 12.1 %collective-permute-start.4 = (bf16[272,256]{1,0:T(8,128)(2,1)S(1)}, bf16[272,256]{1,0:T(8,128)(2,1)S(1)}, u32[]{:S(2)}, u32[]{:S(2)}) collective-permute-start(bf16[272,256]{1,0:T(8,128)(2,1)S(1)} %get-tuple-element.70), channel_id=1, source_target_pairs={{0,8},{4,12},{8,0},{12,4},{1,9},{5,13},{9,1},{13,5},{2,10},{6,14},... | collective-permute-start | bytes 417800 | tf_op jit(solution)/shard_map/ppermute | solution.py:383
  15.9 9.6 %collective-permute-start.5 = (bf16[272,256]{1,0:T(8,128)(2,1)S(1)}, bf16[272,256]{1,0:T(8,128)(2,1)S(1)}, u32[]{:S(2)}, u32[]{:S(2)}) collective-permute-start(bf16[272,256]{1,0:T(8,128)(2,1)S(1)} %get-tuple-element.71), channel_id=1, source_target_pairs={{0,12},{4,0},{8,4},{12,8},{1,13},{5,1},{9,5},{13,9},{2,14},{6,2},{... | collective-permute-start | bytes 417800 | tf_op jit(solution)/shard_map/ppermute | solution.py:383
  25.5 3.9 %copy-start.1 = (bf16[1,1024,256]{2,1,0:T(8,128)(2,1)S(1)}, bf16[1,1024,256]{2,1,0:T(8,128)(2,1)}, u32[]{:S(2)}) copy-start(bf16[1,1024,256]{2,1,0:T(8,128)(2,1)} %param.18) | copy-start | bytes 1572868
  25.5 15.4 %copy-start.19 = (bf16[784,256]{1,0:T(8,128)(2,1)S(1)}, bf16[784,256]{1,0:T(8,128)(2,1)}, u32[]{:S(2)}) copy-start(bf16[784,256]{1,0:T(8,128)(2,1)} %get-tuple-element.79) | copy-start | bytes 1204228
  25.6 17.5 %collective-permute-start.10 = (bf16[512,512]{1,0:T(8,128)(2,1)S(1)}, bf16[512,512]{1,0:T(8,128)(2,1)S(1)}, u32[]{:S(2)}, u32[]{:S(2)}) collective-permute-start(bf16[512,512]{1,0:T(8,128)(2,1)S(1)} %maximum_select_fusion.own), channel_id=1, source_target_pairs={{0,1},{1,0},{2,3},{3,2},{4,5},{5,4},{6,7},{7,6},{8,9},{9,8},{10,11... | collective-permute-start | bytes 1572872 | tf_op jit(solution)/shard_map/ppermute | solution.py:306
  26.3 16.9 %collective-permute-start.11 = (bf16[512,512]{1,0:T(8,128)(2,1)S(1)}, bf16[512,512]{1,0:T(8,128)(2,1)S(1)}, u32[]{:S(2)}, u32[]{:S(2)}) collective-permute-start(bf16[512,512]{1,0:T(8,128)(2,1)S(1)} %maximum_select_fusion.own), channel_id=1, source_target_pairs={{1,4},{0,13},{5,8},{4,1},{9,12},{8,5},{13,0},{12,9},{3,6},{2,15},{... | collective-permute-start | bytes 1572872 | tf_op jit(solution)/shard_map/ppermute | solution.py:317
  29.4 22.4 %copy-start.18 = (bf16[784,256]{1,0:T(8,128)(2,1)S(1)}, bf16[784,256]{1,0:T(8,128)(2,1)}, u32[]{:S(2)}) copy-start(bf16[784,256]{1,0:T(8,128)(2,1)} %get-tuple-element.81) | copy-start | bytes 1204228
  29.4 24.7 %copy-start.4 = (bf16[2,256,512]{2,1,0:T(8,128)(2,1)S(1)}, bf16[2,256,512]{2,1,0:T(8,128)(2,1)}, u32[]{:S(2)}) copy-start(bf16[2,256,512]{2,1,0:T(8,128)(2,1)} %w2_hbm.6) | copy-start | bytes 1572868
  30.1 9.0 %collective-permute-start.6 = (bf16[512,256]{1,0:T(8,128)(2,1)S(1)}, bf16[512,256]{1,0:T(8,128)(2,1)S(1)}, u32[]{:S(2)}, u32[]{:S(2)}) collective-permute-start(bf16[512,256]{1,0:T(8,128)(2,1)S(1)} %get-tuple-element.76), channel_id=1, source_target_pairs={{0,0},{1,2},{2,1},{3,3},{4,4},{5,6},{6,5},{7,7},{8,8},{9,10},{10,9... | collective-permute-start | bytes 786440 | tf_op jit(solution)/shard_map/ppermute | solution.py:290
  34.8 19.3 %copy-start.2 = (bf16[2,512,256]{2,1,0:T(8,128)(2,1)S(1)}, bf16[2,512,256]{2,1,0:T(8,128)(2,1)}, u32[]{:S(2)}) copy-start(bf16[2,512,256]{2,1,0:T(8,128)(2,1)} %ws_hbm.6) | copy-start | bytes 1572868
  34.8 19.3 %copy-start.3 = (bf16[2,512,256]{2,1,0:T(8,128)(2,1)S(1)}, bf16[2,512,256]{2,1,0:T(8,128)(2,1)}, u32[]{:S(2)}) copy-start(bf16[2,512,256]{2,1,0:T(8,128)(2,1)} %wd_hbm.6) | copy-start | bytes 1572868
  34.9 6.1 %collective-permute-start.7 = (bf16[512,256]{1,0:T(8,128)(2,1)S(1)}, bf16[512,256]{1,0:T(8,128)(2,1)S(1)}, u32[]{:S(2)}, u32[]{:S(2)}) collective-permute-start(bf16[512,256]{1,0:T(8,128)(2,1)S(1)} %get-tuple-element.77), channel_id=1, source_target_pairs={{0,1},{1,3},{2,0},{3,2},{4,5},{5,7},{6,4},{7,6},{8,9},{9,11},{10,8... | collective-permute-start | bytes 786440 | tf_op jit(solution)/shard_map/ppermute | solution.py:291
  40.9 10.9 %collective-permute-start.8 = (bf16[784,256]{1,0:T(8,128)(2,1)S(1)}, bf16[784,256]{1,0:T(8,128)(2,1)S(1)}, u32[]{:S(2)}, u32[]{:S(2)}) collective-permute-start(bf16[784,256]{1,0:T(8,128)(2,1)S(1)} %copy-done.19), channel_id=1, source_target_pairs={{0,2},{2,0},{1,3},{3,1},{4,6},{6,4},{5,7},{7,5},{8,10},{10,8},{9,1... | collective-permute-start | bytes 1204232 | tf_op jit(solution)/shard_map/ppermute | solution.py:306
  43.1 11.0 %collective-permute-start.12 = (bf16[784,256]{1,0:T(8,128)(2,1)S(1)}, bf16[784,256]{1,0:T(8,128)(2,1)S(1)}, u32[]{:S(2)}, u32[]{:S(2)}) collective-permute-start(bf16[784,256]{1,0:T(8,128)(2,1)S(1)} %collective-permute-done.2.near_w), channel_id=1, source_target_pairs={{0,1},{1,0},{2,3},{3,2},{4,5},{5,4},{6,7},{7,6},{8,9},{9,8},{10,11... | collective-permute-start | bytes 1204232 | tf_op jit(solution)/shard_map/ppermute | solution.py:306
  43.3 10.9 %copy-start.8 = (bf16[2,256]{1,0:T(2,128)(2,1)S(1)}, bf16[2,256]{1,0:T(2,128)(2,1)}, u32[]{:S(2)}) copy-start(bf16[2,256]{1,0:T(2,128)(2,1)} %bias.6) | copy-start | bytes 3076
  43.3 20.2 %collective-permute-start.14 = (bf16[512,512]{1,0:T(8,128)(2,1)S(1)}, bf16[512,512]{1,0:T(8,128)(2,1)S(1)}, u32[]{:S(2)}, u32[]{:S(2)}) collective-permute-start(bf16[512,512]{1,0:T(8,128)(2,1)S(1)} %maximum_select_fusion.1.own), channel_id=1, source_target_pairs={{0,1},{1,0},{2,3},{3,2},{4,5},{5,4},{6,7},{7,6},{8,9},{9,8},{10,11... | collective-permute-start | bytes 1572872 | tf_op jit(solution)/shard_map/ppermute | solution.py:306
  43.9 21.1 %collective-permute-start.15 = (bf16[512,512]{1,0:T(8,128)(2,1)S(1)}, bf16[512,512]{1,0:T(8,128)(2,1)S(1)}, u32[]{:S(2)}, u32[]{:S(2)}) collective-permute-start(bf16[512,512]{1,0:T(8,128)(2,1)S(1)} %maximum_select_fusion.1.own), channel_id=1, source_target_pairs={{1,4},{5,8},{4,1},{9,12},{8,5},{12,9},{3,6},{7,10},{6,3},{11,14},{... | collective-permute-start | bytes 1572872 | tf_op jit(solution)/shard_map/ppermute | solution.py:317
  51.8 11.7 %copy-start.17 = (bf16[784,256]{1,0:T(8,128)(2,1)S(1)}, bf16[784,256]{1,0:T(8,128)(2,1)}, u32[]{:S(2)}) copy-start(bf16[784,256]{1,0:T(8,128)(2,1)} %get-tuple-element.97) | copy-start | bytes 1204228
  51.8 14.0 %copy-start.5 = (bf16[2,512,256]{2,1,0:T(8,128)(2,1)S(1)}, bf16[2,512,256]{2,1,0:T(8,128)(2,1)}, u32[]{:S(2)}) copy-start(bf16[2,512,256]{2,1,0:T(8,128)(2,1)} %ws_hbm.7) | copy-start | bytes 1572868
  51.8 14.0 %copy-start.6 = (bf16[2,512,256]{2,1,0:T(8,128)(2,1)S(1)}, bf16[2,512,256]{2,1,0:T(8,128)(2,1)}, u32[]{:S(2)}) copy-start(bf16[2,512,256]{2,1,0:T(8,128)(2,1)} %wd_hbm.7) | copy-start | bytes 1572868
  51.8 14.0 %copy-start.7 = (bf16[2,256,512]{2,1,0:T(8,128)(2,1)S(1)}, bf16[2,256,512]{2,1,0:T(8,128)(2,1)}, u32[]{:S(2)}) copy-start(bf16[2,256,512]{2,1,0:T(8,128)(2,1)} %w2_hbm.7) | copy-start | bytes 1572868
  51.8 10.4 %collective-permute-start.9 = (bf16[784,256]{1,0:T(8,128)(2,1)S(1)}, bf16[784,256]{1,0:T(8,128)(2,1)S(1)}, u32[]{:S(2)}, u32[]{:S(2)}) collective-permute-start(bf16[784,256]{1,0:T(8,128)(2,1)S(1)} %copy-done.18), channel_id=1, source_target_pairs={{0,2},{2,0},{1,3},{3,1},{4,6},{6,4},{5,7},{7,5},{8,10},{10,8},{9,1... | collective-permute-start | bytes 1204232 | tf_op jit(solution)/shard_map/ppermute | solution.py:306
  53.7 12.2 %collective-permute-start.16 = (bf16[784,256]{1,0:T(8,128)(2,1)S(1)}, bf16[784,256]{1,0:T(8,128)(2,1)S(1)}, u32[]{:S(2)}, u32[]{:S(2)}) collective-permute-start(bf16[784,256]{1,0:T(8,128)(2,1)S(1)} %collective-permute-done.8.near_w), channel_id=1, source_target_pairs={{0,1},{1,0},{2,3},{3,2},{4,5},{5,4},{6,7},{7,6},{8,9},{9,8},{10,11... | collective-permute-start | bytes 1204232 | tf_op jit(solution)/shard_map/ppermute | solution.py:306
  60.4 5.4 %copy-start.9 = (bf16[2,256]{1,0:T(2,128)(2,1)S(1)}, bf16[2,256]{1,0:T(2,128)(2,1)}, u32[]{:S(2)}) copy-start(bf16[2,256]{1,0:T(2,128)(2,1)} %bias.7) | copy-start | bytes 3076
  60.4 17.8 %collective-permute-start.17 = (bf16[512,512]{1,0:T(8,128)(2,1)S(1)}, bf16[512,512]{1,0:T(8,128)(2,1)S(1)}, u32[]{:S(2)}, u32[]{:S(2)}) collective-permute-start(bf16[512,512]{1,0:T(8,128)(2,1)S(1)} %graph_layer.4.own), channel_id=1, source_target_pairs={{0,1},{1,0},{2,3},{3,2},{4,5},{5,4},{6,7},{7,6},{8,9},{9,8},{10,11... | collective-permute-start | bytes 1572872 | tf_op jit(solution)/shard_map/ppermute | solution.py:306
  62.2 16.1 %collective-permute-start.18 = (bf16[512,512]{1,0:T(8,128)(2,1)S(1)}, bf16[512,512]{1,0:T(8,128)(2,1)S(1)}, u32[]{:S(2)}, u32[]{:S(2)}) collective-permute-start(bf16[512,512]{1,0:T(8,128)(2,1)S(1)} %graph_layer.4.own), channel_id=1, source_target_pairs={{1,4},{0,13},{5,8},{4,1},{9,12},{8,5},{13,0},{12,9},{3,6},{2,15},{... | collective-permute-start | bytes 1572872 | tf_op jit(solution)/shard_map/ppermute | solution.py:317
  63.5 10.3 %collective-permute-start.13 = (bf16[784,256]{1,0:T(8,128)(2,1)S(1)}, bf16[784,256]{1,0:T(8,128)(2,1)S(1)}, u32[]{:S(2)}, u32[]{:S(2)}) collective-permute-start(bf16[784,256]{1,0:T(8,128)(2,1)S(1)} %copy-done.17), channel_id=1, source_target_pairs={{0,2},{2,0},{1,3},{3,1},{4,6},{6,4},{5,7},{7,5},{8,10},{10,8},{9,1... | collective-permute-start | bytes 1204232 | tf_op jit(solution)/shard_map/ppermute | solution.py:306
  64.9 13.4 %collective-permute-start.19 = (bf16[784,256]{1,0:T(8,128)(2,1)S(1)}, bf16[784,256]{1,0:T(8,128)(2,1)S(1)}, u32[]{:S(2)}, u32[]{:S(2)}) collective-permute-start(bf16[784,256]{1,0:T(8,128)(2,1)S(1)} %collective-permute-done.9.near_w), channel_id=1, source_target_pairs={{0,1},{1,0},{2,3},{3,2},{4,5},{5,4},{6,7},{7,6},{8,9},{9,8},{10,11... | collective-permute-start | bytes 1204232 | tf_op jit(solution)/shard_map/ppermute | solution.py:306
  72.1 16.3 %collective-permute-start.22 = (bf16[512,512]{1,0:T(8,128)(2,1)S(1)}, bf16[512,512]{1,0:T(8,128)(2,1)S(1)}, u32[]{:S(2)}, u32[]{:S(2)}) collective-permute-start(bf16[512,512]{1,0:T(8,128)(2,1)S(1)} %graph_layer.5.own), channel_id=1, source_target_pairs={{0,1},{1,0},{2,3},{3,2},{4,5},{5,4},{6,7},{7,6},{8,9},{9,8},{10,11... | collective-permute-start | bytes 1572872 | tf_op jit(solution)/shard_map/ppermute | solution.py:306
  73.8 14.7 %collective-permute-start.23 = (bf16[512,512]{1,0:T(8,128)(2,1)S(1)}, bf16[512,512]{1,0:T(8,128)(2,1)S(1)}, u32[]{:S(2)}, u32[]{:S(2)}) collective-permute-start(bf16[512,512]{1,0:T(8,128)(2,1)S(1)} %graph_layer.5.own), channel_id=1, source_target_pairs={{1,4},{5,8},{4,1},{9,12},{8,5},{12,9},{3,6},{7,10},{6,3},{11,14},{... | collective-permute-start | bytes 1572872 | tf_op jit(solution)/shard_map/ppermute | solution.py:317
  78.2 10.3 %collective-permute-start.24 = (bf16[784,256]{1,0:T(8,128)(2,1)S(1)}, bf16[784,256]{1,0:T(8,128)(2,1)S(1)}, u32[]{:S(2)}, u32[]{:S(2)}) collective-permute-start(bf16[784,256]{1,0:T(8,128)(2,1)S(1)} %collective-permute-done.13.near_w), channel_id=1, source_target_pairs={{0,1},{1,0},{2,3},{3,2},{4,5},{5,4},{6,7},{7,6},{8,9},{9,8},{10,11... | collective-permute-start | bytes 1204232 | tf_op jit(solution)/shard_map/ppermute | solution.py:306
  84.6 12.5 %collective-permute-start.21 = (bf16[512,256]{1,0:T(8,128)(2,1)S(1)}, bf16[512,256]{1,0:T(8,128)(2,1)S(1)}, u32[]{:S(2)}, u32[]{:S(2)}) collective-permute-start(bf16[512,256]{1,0:T(8,128)(2,1)S(1)} %get-tuple-element.109), channel_id=1, source_target_pairs={{0,2},{1,0},{2,3},{3,1},{4,6},{5,4},{6,7},{7,5},{8,10},{9,8},{10,1... | collective-permute-start | bytes 786440 | tf_op jit(solution)/shard_map/ppermute | solution.py:297
  85.1 12.0 %collective-permute-start.20 = (bf16[512,256]{1,0:T(8,128)(2,1)S(1)}, bf16[512,256]{1,0:T(8,128)(2,1)S(1)}, u32[]{:S(2)}, u32[]{:S(2)}) collective-permute-start(bf16[512,256]{1,0:T(8,128)(2,1)S(1)} %get-tuple-element.108), channel_id=1, source_target_pairs={{0,0},{1,2},{2,1},{3,3},{4,4},{5,6},{6,5},{7,7},{8,8},{9,10},{10,9... | collective-permute-start | bytes 786440 | tf_op jit(solution)/shard_map/ppermute | solution.py:296
  94.8 10.3 %collective-permute-start.25 = (bf16[512,256]{1,0:T(8,128)(2,1)S(1)}, bf16[512,256]{1,0:T(8,128)(2,1)S(1)}, u32[]{:S(2)}, u32[]{:S(2)}) collective-permute-start(bf16[512,256]{1,0:T(8,128)(2,1)S(1)} %get-tuple-element.113), channel_id=1, source_target_pairs={{0,0},{1,2},{2,1},{3,3},{4,4},{5,6},{6,5},{7,7},{8,8},{9,10},{10,9... | collective-permute-start | bytes 786440 | tf_op jit(solution)/shard_map/ppermute | solution.py:296
  97.1 8.0 %collective-permute-start.26 = (bf16[512,256]{1,0:T(8,128)(2,1)S(1)}, bf16[512,256]{1,0:T(8,128)(2,1)S(1)}, u32[]{:S(2)}, u32[]{:S(2)}) collective-permute-start(bf16[512,256]{1,0:T(8,128)(2,1)S(1)} %get-tuple-element.114), channel_id=1, source_target_pairs={{0,2},{1,0},{2,3},{3,1},{4,6},{5,4},{6,7},{7,5},{8,10},{9,8},{10,1... | collective-permute-start | bytes 786440 | tf_op jit(solution)/shard_map/ppermute | solution.py:297

commit v11 on v10

--- a/solution.py
+++ b/solution.py
@@ -390,12 +390,13 @@
     )
     planet = ordered(core, g_a, g_b, 1)
     g_sib, g_rim = swap(planet, "batch"), rims(planet, True)
-    r_a, r_b = spread_rows(*add_force(part.reshape(1), r_own, landed, cap))
-    r_a, r_b, packs[1] = after((r_a, r_b, packs[1]))
+    *r_pair, packs[1] = after((*add_force(part.reshape(1), r_own, landed, cap), packs[1]))
+    r_a, r_b = spread_rows(*r_pair)
     near_w.append(swap(packs[1], "mp"))
     r_a, r_b, g_sib, g_rim, near_w[0] = after((r_a, r_b, g_sib, g_rim, near_w[0]))
     regional, g_idx = after((ordered(core, r_a, r_b, 1), g_idx))
     r_sib, r_rim = swap(regional, "batch"), rims(regional, False)
+    r_sib, near_w[1] = after((r_sib, near_w[1]))
     for i, (graph, layer) in enumerate(order):
         last = layer == layers - 1
         far_w = swap(near_w[i], "batch")

time: 107 us -> 105 us (0.981)
  waiting for transfers between devices: 27.6 us -> 25.5 us
  starting transfers between devices: 39.3 us -> 40.4 us
    ppermute x12, starting transfers between devices: 8.52 us -> 10.4 us  [swap(): return lax.ppermute(values, axis, [(0, 1), (1, 0)])]
    ppermute x12, waiting for transfers between devices: 9.23 us -> 7.37 us  [swap(): return lax.ppermute(values, axis, [(0, 1), (1, 0)])]
    ppermute x2, waiting for transfers between devices: 6.97 us -> 5.31 us  [gather_rows(): same = lax.ppermute(a, ('mp', 'batch'), [(0, 0), (1, 2), (2, 1), (3, 3)])]
    ppermute x4, starting transfers between devices: 10.7 us -> 9.14 us  [rims(): return lax.ppermute(own, ('mesh', 'batch'), pairs)]
  transfers between devices with their start and end apart: 27 -> 27, of which waited for: 7 -> 8; matrix products, arithmetic and copies ran while one was open for 1% -> 1% of each run, Pallas kernels for 32% -> 32%
where the time goes in v11:
time: 105 us
  starting transfers between devices  40.4 us (38%)
  Pallas kernels  33.8 us (32%)
  waiting for transfers between devices  25.5 us (24%)
  other arithmetic  2.43 us (2%)
  local copies, waits for them, and re-layouts  1.88 us (2%)
  between operations  1.1 us (1%)
    pallas_call x4, Pallas kernels, run_layer(): pl.pallas_call(functools.partial(layer_kernel, layer, slots, last), out_s...  25.2 us
    ppermute x12, starting transfers between devices, swap(): return lax.ppermute(values, axis, [(0, 1), (1, 0)])  10.4 us
    ppermute x2, starting transfers between devices, spread_rows(): a = lax.ppermute(same, ('mp', 'batch'), [(0, 0), (1, 2), (2, 1), (3, 3)])  9.33 us
    ppermute x4, starting transfers between devices, rims(): return lax.ppermute(own, ('mesh', 'batch'), pairs)  9.14 us
    ppermute x12, waiting for transfers between devices, swap(): return lax.ppermute(values, axis, [(0, 1), (1, 0)])  7.37 us
    pallas_call x2, Pallas kernels, pack_weights(): pl.pallas_call(functools.partial(pack_kernel, order), out_shape=(jax.Shap...  5.68 us
    ppermute x2, starting transfers between devices, gather_rows(): same = lax.ppermute(a, ('mp', 'batch'), [(0, 0), (1, 2), (2, 1), (3, 3)])  5.55 us
    ppermute x3, waiting for transfers between devices, by_rows(): lax.ppermute(pieces[k], 'mesh', [(i, (i + k) % parts) for i in range(part...  5.38 us
  transfers between devices with their start and end apart: 27, of which 8 were waited for; matrix products, arithmetic and copies ran while one was open for 1% of the time, Pallas kernels for 32%

profile of v11, /device:TPU:1, one launch (start us, length us, event | category | flops | bytes accessed | tf_op | source)
XLA Modules:
  0.0 105.1 jit_solution(5858514570236499326)
XLA Ops:
  0.6 1.1 %dynamic-slice_bitcast_fusion = (bf16[512,256]{1,0:T(8,128)(2,1)S(1)}, bf16[512,256]{1,0:T(8,128)(2,1)S(1)}) fusion(bf16[1,1024,256]{2,1,0:T(8,128)(2,1)} %param.17, s32[]{:T(128)S(6)} %select_n.78, s32[]{:T(128)S(6)} %select_n.77), kind=kLoop, calls=%fused_computation.4 | loop fusion | bytes 1048584 | tf_op jit(solution)/shard_map/dynamic_slice | solution.py:373
  1.7 4.5 %collective-permute-start = (bf16[512,256]{1,0:T(8,128)(2,1)S(1)}, bf16[512,256]{1,0:T(8,128)(2,1)S(1)}, u32[]{:S(2)}, u32[]{:S(2)}) collective-permute-start(bf16[512,256]{1,0:T(8,128)(2,1)S(1)} %get-tuple-element.123), channel_id=1, source_target_pairs={{0,0},{1,2},{2,1},{3,3},{4,4},{5,6},{6,5},{7,7},{8,8},{9,10},{10,9... | collective-permute-start | bytes 786440 | tf_op jit(solution)/shard_map/ppermute | solution.py:290
  6.3 2.6 %pack_weights.2 = bf16[784,256]{1,0:T(8,128)(2,1)} custom-call(s32[1]{0:T(128)} %bitcast.4.core_ref, bf16[2,256]{1,0:T(2,128)(2,1)} %bias.6, bf16[2,256]{1,0:T(2,128)(2,1)} %bias.7, bf16[2,512,256]{2,1,0:T(8,128)(2,1)} %ws_hbm.6, bf16[2,512,256]{2,1,0:T(8,128)(2,1)} %wd_hbm.6, bf16[2,256,512]{2,1,0:T(8,128)(2,1)} %w2_hbm.6, bf16[2,512,256]{2,1,0:T(8,128)(2,1)} %ws_hbm.7, ...), custom_call_target="tpu_custom_call" | custom-call | flops 4294967296 | bytes 1 | tf_op jit(solution)/shard_map/pack_weights/pallas_call | solution.py:342
  8.9 0.2 collective-permute-start.2
  9.0 0.7 copy-done.15
  9.8 2.2 %pick_rows.1 = (bf16[272,256]{1,0:T(8,128)(2,1)S(1)}, bf16[272,256]{1,0:T(8,128)(2,1)S(1)}, bf16[272,256]{1,0:T(8,128)(2,1)S(1)}, bf16[272,256]{1,0:T(8,128)(2,1)S(1)}) custom-call(s32[1]{0:T(128)} %bitcast.me_ref, s32[3,512]{1,0:T(4,128)S(1)} %pad_add_fusion.bnd_ref, bf16[1024,256]{1,0:T(8,128)(2,1)S(1)} %bitcast.33), custom_call_target="tpu_custom_call" | custom-call | flops 8589934592 | bytes 1 | tf_op jit(solution)/shard_map/pick_rows/pallas_call | solution.py:115
  12.0 1.4 %collective-permute-start.3 = (bf16[272,256]{1,0:T(8,128)(2,1)S(1)}, bf16[272,256]{1,0:T(8,128)(2,1)S(1)}, u32[]{:S(2)}, u32[]{:S(2)}) collective-permute-start(bf16[272,256]{1,0:T(8,128)(2,1)S(1)} %get-tuple-element.71), channel_id=1, source_target_pairs={{0,4},{4,8},{8,12},{12,0},{1,5},{5,9},{9,13},{13,1},{2,6},{6,10},{... | collective-permute-start | bytes 417800 | tf_op jit(solution)/shard_map/ppermute | solution.py:383
  13.4 2.3 %collective-permute-start.4 = (bf16[272,256]{1,0:T(8,128)(2,1)S(1)}, bf16[272,256]{1,0:T(8,128)(2,1)S(1)}, u32[]{:S(2)}, u32[]{:S(2)}) collective-permute-start(bf16[272,256]{1,0:T(8,128)(2,1)S(1)} %get-tuple-element.72), channel_id=1, source_target_pairs={{0,8},{4,12},{8,0},{12,4},{1,9},{5,13},{9,1},{13,5},{2,10},{6,14},... | collective-permute-start | bytes 417800 | tf_op jit(solution)/shard_map/ppermute | solution.py:383
  15.7 0.1 fusion.5
  15.9 1.1 %collective-permute-start.5 = (bf16[272,256]{1,0:T(8,128)(2,1)S(1)}, bf16[272,256]{1,0:T(8,128)(2,1)S(1)}, u32[]{:S(2)}, u32[]{:S(2)}) collective-permute-start(bf16[272,256]{1,0:T(8,128)(2,1)S(1)} %get-tuple-element.73), channel_id=1, source_target_pairs={{0,12},{4,0},{8,4},{12,8},{1,13},{5,1},{9,5},{13,9},{2,14},{6,2},{... | collective-permute-start | bytes 417800 | tf_op jit(solution)/shard_map/ppermute | solution.py:383
  17.0 3.1 %pack_weights.3 = (bf16[784,256]{1,0:T(8,128)(2,1)}, bf16[784,256]{1,0:T(8,128)(2,1)}, bf16[784,256]{1,0:T(8,128)(2,1)}) custom-call(s32[1]{0:T(128)} %bitcast.4.core_ref, bf16[2,256]{1,0:T(2,128)(2,1)} %bias.6, bf16[2,256]{1,0:T(2,128)(2,1)} %bias.7, bf16[2,512,256]{2,1,0:T(8,128)(2,1)} %ws_hbm.6, bf16[2,512,256]{2,1,0:T(8,128)(2,1)} %wd_hbm.6, ...), custom_call_target="tpu_custom_call" | custom-call | flops 4294967296 | bytes 1 | tf_op jit(solution)/shard_map/pack_weights/pallas_call | solution.py:342
  20.1 5.4 %collective-permute-done.4.refs_2_ = bf16[272,256]{1,0:T(8,128)(2,1)S(1)} collective-permute-done((bf16[272,256]{1,0:T(8,128)(2,1)S(1)}, bf16[272,256]{1,0:T(8,128)(2,1)S(1)}, u32[]{:S(2)}, u32[]{:S(2)}) %collective-permute-start.4) | collective-permute-done | bytes 139296 | tf_op jit(solution)/shard_map/ppermute | solution.py:383
  25.5 0.1 maximum_select_fusion.own
  25.6 0.7 collective-permute-start.8
  26.3 3.1 %collective-permute-start.9 = (bf16[512,512]{1,0:T(8,128)(2,1)S(1)}, bf16[512,512]{1,0:T(8,128)(2,1)S(1)}, u32[]{:S(2)}, u32[]{:S(2)}) collective-permute-start(bf16[512,512]{1,0:T(8,128)(2,1)S(1)} %maximum_select_fusion.own), channel_id=1, source_target_pairs={{1,4},{0,13},{5,8},{4,1},{9,12},{8,5},{13,0},{12,9},{3,6},{2,15},{... | collective-permute-start | bytes 1572872 | tf_op jit(solution)/shard_map/ppermute | solution.py:317
  29.4 0.7 add_force.1
  30.2 4.8 %collective-permute-start.6 = (bf16[512,256]{1,0:T(8,128)(2,1)S(1)}, bf16[512,256]{1,0:T(8,128)(2,1)S(1)}, u32[]{:S(2)}, u32[]{:S(2)}) collective-permute-start(bf16[512,256]{1,0:T(8,128)(2,1)S(1)} %get-tuple-element.81), channel_id=1, source_target_pairs={{0,0},{1,2},{2,1},{3,3},{4,4},{5,6},{6,5},{7,7},{8,8},{9,10},{10,9... | collective-permute-start | bytes 786440 | tf_op jit(solution)/shard_map/ppermute | solution.py:290
  35.0 4.3 %collective-permute-done.6 = bf16[512,256]{1,0:T(8,128)(2,1)S(1)} collective-permute-done((bf16[512,256]{1,0:T(8,128)(2,1)S(1)}, bf16[512,256]{1,0:T(8,128)(2,1)S(1)}, u32[]{:S(2)}, u32[]{:S(2)}) %collective-permute-start.6) | collective-permute-done | bytes 262176 | tf_op jit(solution)/shard_map/ppermute | solution.py:290
  39.3 1.8 %collective-permute-done.7 = bf16[512,256]{1,0:T(8,128)(2,1)S(1)} collective-permute-done((bf16[512,256]{1,0:T(8,128)(2,1)S(1)}, bf16[512,256]{1,0:T(8,128)(2,1)S(1)}, u32[]{:S(2)}, u32[]{:S(2)}) %collective-permute-start.7) | collective-permute-done | bytes 262176 | tf_op jit(solution)/shard_map/ppermute | solution.py:291
  41.1 0.5 collective-permute-done.9.rim
  41.6 0.1 maximum_select_fusion.1.own
  41.8 1.6 %collective-permute-start.10 = (bf16[512,512]{1,0:T(8,128)(2,1)S(1)}, bf16[512,512]{1,0:T(8,128)(2,1)S(1)}, u32[]{:S(2)}, u32[]{:S(2)}) collective-permute-start(bf16[512,512]{1,0:T(8,128)(2,1)S(1)} %maximum_select_fusion.1.own), channel_id=1, source_target_pairs={{0,1},{1,0},{2,3},{3,2},{4,5},{5,4},{6,7},{7,6},{8,9},{9,8},{10,11... | collective-permute-start | bytes 1572872 | tf_op jit(solution)/shard_map/ppermute | solution.py:306
  43.4 1.4 %collective-permute-start.11 = (bf16[784,256]{1,0:T(8,128)(2,1)S(1)}, bf16[784,256]{1,0:T(8,128)(2,1)S(1)}, u32[]{:S(2)}, u32[]{:S(2)}) collective-permute-start(bf16[784,256]{1,0:T(8,128)(2,1)S(1)} %copy-done.19), channel_id=1, source_target_pairs={{0,2},{2,0},{1,3},{3,1},{4,6},{6,4},{5,7},{7,5},{8,10},{10,8},{9,1... | collective-permute-start | bytes 1204232 | tf_op jit(solution)/shard_map/ppermute | solution.py:306
  44.8 0.4 collective-permute-start.13
  45.1 2.3 %collective-permute-start.15 = (bf16[512,512]{1,0:T(8,128)(2,1)S(1)}, bf16[512,512]{1,0:T(8,128)(2,1)S(1)}, u32[]{:S(2)}, u32[]{:S(2)}) collective-permute-start(bf16[512,512]{1,0:T(8,128)(2,1)S(1)} %maximum_select_fusion.1.own), channel_id=1, source_target_pairs={{1,4},{5,8},{4,1},{9,12},{8,5},{12,9},{3,6},{7,10},{6,3},{11,14},{... | collective-permute-start | bytes 1572872 | tf_op jit(solution)/shard_map/ppermute | solution.py:317
  47.4 6.8 %collective-permute-done.11.near_w = bf16[784,256]{1,0:T(8,128)(2,1)S(1)} collective-permute-done((bf16[784,256]{1,0:T(8,128)(2,1)S(1)}, bf16[784,256]{1,0:T(8,128)(2,1)S(1)}, u32[]{:S(2)}, u32[]{:S(2)}) %collective-permute-start.11) | collective-permute-done | bytes 401440 | tf_op jit(solution)/shard_map/ppermute | solution.py:306
  54.3 1.4 %collective-permute-start.12 = (bf16[784,256]{1,0:T(8,128)(2,1)S(1)}, bf16[784,256]{1,0:T(8,128)(2,1)S(1)}, u32[]{:S(2)}, u32[]{:S(2)}) collective-permute-start(bf16[784,256]{1,0:T(8,128)(2,1)S(1)} %copy-done.18), channel_id=1, source_target_pairs={{0,2},{2,0},{1,3},{3,1},{4,6},{6,4},{5,7},{7,5},{8,10},{10,8},{9,1... | collective-permute-start | bytes 1204232 | tf_op jit(solution)/shard_map/ppermute | solution.py:306
  55.7 1.1 %collective-permute-start.16 = (bf16[784,256]{1,0:T(8,128)(2,1)S(1)}, bf16[784,256]{1,0:T(8,128)(2,1)S(1)}, u32[]{:S(2)}, u32[]{:S(2)}) collective-permute-start(bf16[784,256]{1,0:T(8,128)(2,1)S(1)} %collective-permute-done.11.near_w), channel_id=1, source_target_pairs={{0,1},{1,0},{2,3},{3,2},{4,5},{5,4},{6,7},{7,6},{8,9},{9,8},{10,11... | collective-permute-start | bytes 1204232 | tf_op jit(solution)/shard_map/ppermute | solution.py:306
  56.9 6.3 %graph_layer.4.own = bf16[512,512]{1,0:T(8,128)(2,1)S(1)} custom-call(s32[1]{0:T(128)} %bitcast.4.core_ref, s32[4096]{0:T(1024)S(1)} %bitcast.37, bf16[512,512]{1,0:T(8,128)(2,1)S(1)} %maximum_select_fusion.own, bf16[512,512]{1,0:T(8,128)(2,1)S(1)} %collective-permute-done.8.sib, bf16[512,512]{1,0:T(8,128)(2,1)S(1)} %collective-permute-done.9.rim, ...), custom_call_target="tpu_custom_call" | custom-call | flops 8589934592 | bytes 2621440 | tf_op jit(solution)/shard_map/graph_layer/pallas_call | solution.py:252
  63.2 0.1 collective-permute-start.17
  63.3 0.5 collective-permute-start.18
  63.8 0.5 collective-permute-done.12.near_w
  64.3 1.4 %collective-permute-start.14 = (bf16[784,256]{1,0:T(8,128)(2,1)S(1)}, bf16[784,256]{1,0:T(8,128)(2,1)S(1)}, u32[]{:S(2)}, u32[]{:S(2)}) collective-permute-start(bf16[784,256]{1,0:T(8,128)(2,1)S(1)} %copy-done.17), channel_id=1, source_target_pairs={{0,2},{2,0},{1,3},{3,1},{4,6},{6,4},{5,7},{7,5},{8,10},{10,8},{9,1... | collective-permute-start | bytes 1204232 | tf_op jit(solution)/shard_map/ppermute | solution.py:306
  65.7 2.0 %collective-permute-start.19 = (bf16[784,256]{1,0:T(8,128)(2,1)S(1)}, bf16[784,256]{1,0:T(8,128)(2,1)S(1)}, u32[]{:S(2)}, u32[]{:S(2)}) collective-permute-start(bf16[784,256]{1,0:T(8,128)(2,1)S(1)} %collective-permute-done.12.near_w), channel_id=1, source_target_pairs={{0,1},{1,0},{2,3},{3,2},{4,5},{5,4},{6,7},{7,6},{8,9},{9,8},{10,11... | collective-permute-start | bytes 1204232 | tf_op jit(solution)/shard_map/ppermute | solution.py:306
  67.7 6.3 %graph_layer.5.own = bf16[512,512]{1,0:T(8,128)(2,1)S(1)} custom-call(s32[1]{0:T(128)} %bitcast.4.core_ref, s32[4096]{0:T(1024)S(1)} %bitcast.35, bf16[512,512]{1,0:T(8,128)(2,1)S(1)} %maximum_select_fusion.1.own, bf16[512,512]{1,0:T(8,128)(2,1)S(1)} %collective-permute-done.10.sib, bf16[512,512]{1,0:T(8,128)(2,1)S(1)} %collective-permute-done.15.rim, ...), custom_call_target="tpu_custom_call" | custom-call | flops 8589934592 | bytes 2621440 | tf_op jit(solution)/shard_map/graph_layer/pallas_call | solution.py:252
  74.0 0.1 collective-permute-start.22
  74.1 3.2 %collective-permute-start.23 = (bf16[512,512]{1,0:T(8,128)(2,1)S(1)}, bf16[512,512]{1,0:T(8,128)(2,1)S(1)}, u32[]{:S(2)}, u32[]{:S(2)}) collective-permute-start(bf16[512,512]{1,0:T(8,128)(2,1)S(1)} %graph_layer.5.own), channel_id=1, source_target_pairs={{1,4},{5,8},{4,1},{9,12},{8,5},{12,9},{3,6},{7,10},{6,3},{11,14},{... | collective-permute-start | bytes 1572872 | tf_op jit(solution)/shard_map/ppermute | solution.py:317
  77.4 0.1 collective-permute-start.24
  77.5 6.3 %graph_layer.6 = (bf16[512,256]{1,0:T(8,128)(2,1)S(1)}, bf16[512,256]{1,0:T(8,128)(2,1)S(1)}) custom-call(s32[1]{0:T(128)} %bitcast.4.core_ref, s32[4096]{0:T(1024)S(1)} %bitcast.38, bf16[512,512]{1,0:T(8,128)(2,1)S(1)} %graph_layer.4.own, bf16[512,512]{1,0:T(8,128)(2,1)S(1)} %collective-permute-done.17.sib, ...), custom_call_target="tpu_custom_call" | custom-call | flops 8589934592 | bytes 2621440 | tf_op jit(solution)/shard_map/graph_layer/pallas_call | solution.py:252
  83.8 1.1 %collective-permute-start.21 = (bf16[512,256]{1,0:T(8,128)(2,1)S(1)}, bf16[512,256]{1,0:T(8,128)(2,1)S(1)}, u32[]{:S(2)}, u32[]{:S(2)}) collective-permute-start(bf16[512,256]{1,0:T(8,128)(2,1)S(1)} %get-tuple-element.113), channel_id=1, source_target_pairs={{0,2},{1,0},{2,3},{3,1},{4,6},{5,4},{6,7},{7,5},{8,10},{9,8},{10,1... | collective-permute-start | bytes 786440 | tf_op jit(solution)/shard_map/ppermute | solution.py:297
  85.0 2.3 %collective-permute-start.20 = (bf16[512,256]{1,0:T(8,128)(2,1)S(1)}, bf16[512,256]{1,0:T(8,128)(2,1)S(1)}, u32[]{:S(2)}, u32[]{:S(2)}) collective-permute-start(bf16[512,256]{1,0:T(8,128)(2,1)S(1)} %get-tuple-element.112), channel_id=1, source_target_pairs={{0,0},{1,2},{2,1},{3,3},{4,4},{5,6},{6,5},{7,7},{8,8},{9,10},{10,9... | collective-permute-start | bytes 786440 | tf_op jit(solution)/shard_map/ppermute | solution.py:296
  87.3 6.3 %graph_layer.7 = (bf16[512,256]{1,0:T(8,128)(2,1)S(1)}, bf16[512,256]{1,0:T(8,128)(2,1)S(1)}) custom-call(s32[1]{0:T(128)} %bitcast.4.core_ref, s32[4096]{0:T(1024)S(1)} %bitcast.36, bf16[512,512]{1,0:T(8,128)(2,1)S(1)} %graph_layer.5.own, bf16[512,512]{1,0:T(8,128)(2,1)S(1)} %collective-permute-done.22.sib, ...), custom_call_target="tpu_custom_call" | custom-call | flops 8589934592 | bytes 2621440 | tf_op jit(solution)/shard_map/graph_layer/pallas_call | solution.py:252
  93.6 3.3 %collective-permute-start.25 = (bf16[512,256]{1,0:T(8,128)(2,1)S(1)}, bf16[512,256]{1,0:T(8,128)(2,1)S(1)}, u32[]{:S(2)}, u32[]{:S(2)}) collective-permute-start(bf16[512,256]{1,0:T(8,128)(2,1)S(1)} %get-tuple-element.117), channel_id=1, source_target_pairs={{0,0},{1,2},{2,1},{3,3},{4,4},{5,6},{6,5},{7,7},{8,8},{9,10},{10,9... | collective-permute-start | bytes 786440 | tf_op jit(solution)/shard_map/ppermute | solution.py:296
  96.9 0.0 collective-permute-start.26
  96.9 1.0 maximum_select_fusion.2
  98.0 5.3 %collective-permute-done.25 = bf16[512,256]{1,0:T(8,128)(2,1)S(1)} collective-permute-done((bf16[512,256]{1,0:T(8,128)(2,1)S(1)}, bf16[512,256]{1,0:T(8,128)(2,1)S(1)}, u32[]{:S(2)}, u32[]{:S(2)}) %collective-permute-start.25) | collective-permute-done | bytes 262176 | tf_op jit(solution)/shard_map/ppermute | solution.py:296
  103.3 0.8 collective-permute-done.26
  104.1 1.0 maximum_select_fusion.3
  (66 shorter events, 0.3 us)
Async XLA Ops:
  1.7 14.1 %collective-permute-start = (bf16[512,256]{1,0:T(8,128)(2,1)S(1)}, bf16[512,256]{1,0:T(8,128)(2,1)S(1)}, u32[]{:S(2)}, u32[]{:S(2)}) collective-permute-start(bf16[512,256]{1,0:T(8,128)(2,1)S(1)} %get-tuple-element.123), channel_id=1, source_target_pairs={{0,0},{1,2},{2,1},{3,3},{4,4},{5,6},{6,5},{7,7},{8,8},{9,10},{10,9... | collective-permute-start | bytes 786440 | tf_op jit(solution)/shard_map/ppermute | solution.py:290
  6.2 10.8 %collective-permute-start.1 = (bf16[512,256]{1,0:T(8,128)(2,1)S(1)}, bf16[512,256]{1,0:T(8,128)(2,1)S(1)}, u32[]{:S(2)}, u32[]{:S(2)}) collective-permute-start(bf16[512,256]{1,0:T(8,128)(2,1)S(1)} %get-tuple-element.122), channel_id=1, source_target_pairs={{0,1},{1,3},{2,0},{3,2},{4,5},{5,7},{6,4},{7,6},{8,9},{9,11},{10,8... | collective-permute-start | bytes 786440 | tf_op jit(solution)/shard_map/ppermute | solution.py:291
  6.3 2.8 %copy-start.16 = (s32[512]{0:T(512)S(1)}, s32[512]{0:T(512)}, u32[]{:S(2)}) copy-start(s32[512]{0:T(512)} %param.23) | copy-start | bytes 6148
  6.3 3.4 %copy-start = (bf16[1,1024,256]{2,1,0:T(8,128)(2,1)S(1)}, bf16[1,1024,256]{2,1,0:T(8,128)(2,1)}, u32[]{:S(2)}) copy-start(bf16[1,1024,256]{2,1,0:T(8,128)(2,1)} %param.17) | copy-start | bytes 1572868
  8.9 16.6 %collective-permute-start.2 = (bf16[784,256]{1,0:T(8,128)(2,1)}, bf16[784,256]{1,0:T(8,128)(2,1)S(1)}, u32[]{:S(2)}, u32[]{:S(2)}) collective-permute-start(bf16[784,256]{1,0:T(8,128)(2,1)} %pack_weights.2), channel_id=1, source_target_pairs={{0,2},{2,0},{1,3},{3,1},{4,6},{6,4},{5,7},{7,5},{8,10},{10,8},{9,1... | collective-permute-start | bytes 1204232 | tf_op jit(solution)/shard_map/ppermute | solution.py:306
  9.0 0.7 copy-start.15
  9.0 0.7 copy-start.14
  9.7 5.9 %copy-start.12 = (s32[1024]{0:T(1024)S(1)}, s32[1024]{0:T(1024)}, u32[]{:S(2)}) copy-start(s32[1024]{0:T(1024)} %param.20) | copy-start | bytes 12292
  9.7 5.9 %copy-start.13 = (s32[1024]{0:T(1024)S(1)}, s32[1024]{0:T(1024)}, u32[]{:S(2)}) copy-start(s32[1024]{0:T(1024)} %param.22) | copy-start | bytes 12292
  9.8 6.0 %copy-start.11 = (s32[1024,8]{0,1:T(8,128)S(1)}, s32[1024,8]{0,1:T(8,128)}, u32[]{:S(2)}) copy-start(s32[1024,8]{0,1:T(8,128)} %param.19) | copy-start | bytes 98308
  12.0 3.8 %copy-start.10 = (s32[1024,8]{0,1:T(8,128)S(1)}, s32[1024,8]{0,1:T(8,128)}, u32[]{:S(2)}) copy-start(s32[1024,8]{0,1:T(8,128)} %param.21) | copy-start | bytes 98308
  12.0 8.1 %collective-permute-start.3 = (bf16[272,256]{1,0:T(8,128)(2,1)S(1)}, bf16[272,256]{1,0:T(8,128)(2,1)S(1)}, u32[]{:S(2)}, u32[]{:S(2)}) collective-permute-start(bf16[272,256]{1,0:T(8,128)(2,1)S(1)} %get-tuple-element.71), channel_id=1, source_target_pairs={{0,4},{4,8},{8,12},{12,0},{1,5},{5,9},{9,13},{13,1},{2,6},{6,10},{... | collective-permute-start | bytes 417800 | tf_op jit(solution)/shard_map/ppermute | solution.py:383
  13.4 12.1 %collective-permute-start.4 = (bf16[272,256]{1,0:T(8,128)(2,1)S(1)}, bf16[272,256]{1,0:T(8,128)(2,1)S(1)}, u32[]{:S(2)}, u32[]{:S(2)}) collective-permute-start(bf16[272,256]{1,0:T(8,128)(2,1)S(1)} %get-tuple-element.72), channel_id=1, source_target_pairs={{0,8},{4,12},{8,0},{12,4},{1,9},{5,13},{9,1},{13,5},{2,10},{6,14},... | collective-permute-start | bytes 417800 | tf_op jit(solution)/shard_map/ppermute | solution.py:383
  15.9 9.6 %collective-permute-start.5 = (bf16[272,256]{1,0:T(8,128)(2,1)S(1)}, bf16[272,256]{1,0:T(8,128)(2,1)S(1)}, u32[]{:S(2)}, u32[]{:S(2)}) collective-permute-start(bf16[272,256]{1,0:T(8,128)(2,1)S(1)} %get-tuple-element.73), channel_id=1, source_target_pairs={{0,12},{4,0},{8,4},{12,8},{1,13},{5,1},{9,5},{13,9},{2,14},{6,2},{... | collective-permute-start | bytes 417800 | tf_op jit(solution)/shard_map/ppermute | solution.py:383
  25.5 3.9 %copy-start.1 = (bf16[1,1024,256]{2,1,0:T(8,128)(2,1)S(1)}, bf16[1,1024,256]{2,1,0:T(8,128)(2,1)}, u32[]{:S(2)}) copy-start(bf16[1,1024,256]{2,1,0:T(8,128)(2,1)} %param.18) | copy-start | bytes 1572868
  25.5 17.9 %copy-start.19 = (bf16[784,256]{1,0:T(8,128)(2,1)S(1)}, bf16[784,256]{1,0:T(8,128)(2,1)}, u32[]{:S(2)}) copy-start(bf16[784,256]{1,0:T(8,128)(2,1)} %get-tuple-element.90) | copy-start | bytes 1204228
  25.6 15.5 %collective-permute-start.8 = (bf16[512,512]{1,0:T(8,128)(2,1)S(1)}, bf16[512,512]{1,0:T(8,128)(2,1)S(1)}, u32[]{:S(2)}, u32[]{:S(2)}) collective-permute-start(bf16[512,512]{1,0:T(8,128)(2,1)S(1)} %maximum_select_fusion.own), channel_id=1, source_target_pairs={{0,1},{1,0},{2,3},{3,2},{4,5},{5,4},{6,7},{7,6},{8,9},{9,8},{10,11... | collective-permute-start | bytes 1572872 | tf_op jit(solution)/shard_map/ppermute | solution.py:306
  26.3 15.3 %collective-permute-start.9 = (bf16[512,512]{1,0:T(8,128)(2,1)S(1)}, bf16[512,512]{1,0:T(8,128)(2,1)S(1)}, u32[]{:S(2)}, u32[]{:S(2)}) collective-permute-start(bf16[512,512]{1,0:T(8,128)(2,1)S(1)} %maximum_select_fusion.own), channel_id=1, source_target_pairs={{1,4},{0,13},{5,8},{4,1},{9,12},{8,5},{13,0},{12,9},{3,6},{2,15},{... | collective-permute-start | bytes 1572872 | tf_op jit(solution)/shard_map/ppermute | solution.py:317
  29.4 24.8 %copy-start.18 = (bf16[784,256]{1,0:T(8,128)(2,1)S(1)}, bf16[784,256]{1,0:T(8,128)(2,1)}, u32[]{:S(2)}) copy-start(bf16[784,256]{1,0:T(8,128)(2,1)} %get-tuple-element.93) | copy-start | bytes 1204228
  29.4 27.5 %copy-start.4 = (bf16[2,256,512]{2,1,0:T(8,128)(2,1)S(1)}, bf16[2,256,512]{2,1,0:T(8,128)(2,1)}, u32[]{:S(2)}) copy-start(bf16[2,256,512]{2,1,0:T(8,128)(2,1)} %w2_hbm.6) | copy-start | bytes 1572868
  30.1 26.7 %copy-start.2 = (bf16[2,512,256]{2,1,0:T(8,128)(2,1)S(1)}, bf16[2,512,256]{2,1,0:T(8,128)(2,1)}, u32[]{:S(2)}) copy-start(bf16[2,512,256]{2,1,0:T(8,128)(2,1)} %ws_hbm.6) | copy-start | bytes 1572868
  30.1 26.7 %copy-start.3 = (bf16[2,512,256]{2,1,0:T(8,128)(2,1)S(1)}, bf16[2,512,256]{2,1,0:T(8,128)(2,1)}, u32[]{:S(2)}) copy-start(bf16[2,512,256]{2,1,0:T(8,128)(2,1)} %wd_hbm.6) | copy-start | bytes 1572868
  30.2 9.2 %collective-permute-start.6 = (bf16[512,256]{1,0:T(8,128)(2,1)S(1)}, bf16[512,256]{1,0:T(8,128)(2,1)S(1)}, u32[]{:S(2)}, u32[]{:S(2)}) collective-permute-start(bf16[512,256]{1,0:T(8,128)(2,1)S(1)} %get-tuple-element.81), channel_id=1, source_target_pairs={{0,0},{1,2},{2,1},{3,3},{4,4},{5,6},{6,5},{7,7},{8,8},{9,10},{10,9... | collective-permute-start | bytes 786440 | tf_op jit(solution)/shard_map/ppermute | solution.py:290
  35.0 6.1 %collective-permute-start.7 = (bf16[512,256]{1,0:T(8,128)(2,1)S(1)}, bf16[512,256]{1,0:T(8,128)(2,1)S(1)}, u32[]{:S(2)}, u32[]{:S(2)}) collective-permute-start(bf16[512,256]{1,0:T(8,128)(2,1)S(1)} %get-tuple-element.82), channel_id=1, source_target_pairs={{0,1},{1,3},{2,0},{3,2},{4,5},{5,7},{6,4},{7,6},{8,9},{9,11},{10,8... | collective-permute-start | bytes 786440 | tf_op jit(solution)/shard_map/ppermute | solution.py:291
  41.8 15.1 %copy-start.8 = (bf16[2,256]{1,0:T(2,128)(2,1)S(1)}, bf16[2,256]{1,0:T(2,128)(2,1)}, u32[]{:S(2)}) copy-start(bf16[2,256]{1,0:T(2,128)(2,1)} %bias.6) | copy-start | bytes 3076
  41.8 12.5 %collective-permute-start.10 = (bf16[512,512]{1,0:T(8,128)(2,1)S(1)}, bf16[512,512]{1,0:T(8,128)(2,1)S(1)}, u32[]{:S(2)}, u32[]{:S(2)}) collective-permute-start(bf16[512,512]{1,0:T(8,128)(2,1)S(1)} %maximum_select_fusion.1.own), channel_id=1, source_target_pairs={{0,1},{1,0},{2,3},{3,2},{4,5},{5,4},{6,7},{7,6},{8,9},{9,8},{10,11... | collective-permute-start | bytes 1572872 | tf_op jit(solution)/shard_map/ppermute | solution.py:306
  43.4 10.9 %collective-permute-start.11 = (bf16[784,256]{1,0:T(8,128)(2,1)S(1)}, bf16[784,256]{1,0:T(8,128)(2,1)S(1)}, u32[]{:S(2)}, u32[]{:S(2)}) collective-permute-start(bf16[784,256]{1,0:T(8,128)(2,1)S(1)} %copy-done.19), channel_id=1, source_target_pairs={{0,2},{2,0},{1,3},{3,1},{4,6},{6,4},{5,7},{7,5},{8,10},{10,8},{9,1... | collective-permute-start | bytes 1204232 | tf_op jit(solution)/shard_map/ppermute | solution.py:306
  44.8 12.1 %collective-permute-start.13 = (bf16[784,256]{1,0:T(8,128)(2,1)S(1)}, bf16[784,256]{1,0:T(8,128)(2,1)S(1)}, u32[]{:S(2)}, u32[]{:S(2)}) collective-permute-start(bf16[784,256]{1,0:T(8,128)(2,1)S(1)} %collective-permute-done.2.near_w), channel_id=1, source_target_pairs={{0,1},{1,0},{2,3},{3,2},{4,5},{5,4},{6,7},{7,6},{8,9},{9,8},{10,11... | collective-permute-start | bytes 1204232 | tf_op jit(solution)/shard_map/ppermute | solution.py:306
  45.1 20.6 %collective-permute-start.15 = (bf16[512,512]{1,0:T(8,128)(2,1)S(1)}, bf16[512,512]{1,0:T(8,128)(2,1)S(1)}, u32[]{:S(2)}, u32[]{:S(2)}) collective-permute-start(bf16[512,512]{1,0:T(8,128)(2,1)S(1)} %maximum_select_fusion.1.own), channel_id=1, source_target_pairs={{1,4},{5,8},{4,1},{9,12},{8,5},{12,9},{3,6},{7,10},{6,3},{11,14},{... | collective-permute-start | bytes 1572872 | tf_op jit(solution)/shard_map/ppermute | solution.py:317
  54.2 10.1 %copy-start.17 = (bf16[784,256]{1,0:T(8,128)(2,1)S(1)}, bf16[784,256]{1,0:T(8,128)(2,1)}, u32[]{:S(2)}) copy-start(bf16[784,256]{1,0:T(8,128)(2,1)} %get-tuple-element.101) | copy-start | bytes 1204228
  54.2 13.5 %copy-start.5 = (bf16[2,512,256]{2,1,0:T(8,128)(2,1)S(1)}, bf16[2,512,256]{2,1,0:T(8,128)(2,1)}, u32[]{:S(2)}) copy-start(bf16[2,512,256]{2,1,0:T(8,128)(2,1)} %ws_hbm.7) | copy-start | bytes 1572868
  54.3 13.5 %copy-start.6 = (bf16[2,512,256]{2,1,0:T(8,128)(2,1)S(1)}, bf16[2,512,256]{2,1,0:T(8,128)(2,1)}, u32[]{:S(2)}) copy-start(bf16[2,512,256]{2,1,0:T(8,128)(2,1)} %wd_hbm.7) | copy-start | bytes 1572868
  54.3 13.5 %copy-start.7 = (bf16[2,256,512]{2,1,0:T(8,128)(2,1)S(1)}, bf16[2,256,512]{2,1,0:T(8,128)(2,1)}, u32[]{:S(2)}) copy-start(bf16[2,256,512]{2,1,0:T(8,128)(2,1)} %w2_hbm.7) | copy-start | bytes 1572868
  54.3 10.0 %collective-permute-start.12 = (bf16[784,256]{1,0:T(8,128)(2,1)S(1)}, bf16[784,256]{1,0:T(8,128)(2,1)S(1)}, u32[]{:S(2)}, u32[]{:S(2)}) collective-permute-start(bf16[784,256]{1,0:T(8,128)(2,1)S(1)} %copy-done.18), channel_id=1, source_target_pairs={{0,2},{2,0},{1,3},{3,1},{4,6},{6,4},{5,7},{7,5},{8,10},{10,8},{9,1... | collective-permute-start | bytes 1204232 | tf_op jit(solution)/shard_map/ppermute | solution.py:306
  55.7 12.0 %collective-permute-start.16 = (bf16[784,256]{1,0:T(8,128)(2,1)S(1)}, bf16[784,256]{1,0:T(8,128)(2,1)S(1)}, u32[]{:S(2)}, u32[]{:S(2)}) collective-permute-start(bf16[784,256]{1,0:T(8,128)(2,1)S(1)} %collective-permute-done.11.near_w), channel_id=1, source_target_pairs={{0,1},{1,0},{2,3},{3,2},{4,5},{5,4},{6,7},{7,6},{8,9},{9,8},{10,11... | collective-permute-start | bytes 1204232 | tf_op jit(solution)/shard_map/ppermute | solution.py:306
  63.2 4.6 %copy-start.9 = (bf16[2,256]{1,0:T(2,128)(2,1)S(1)}, bf16[2,256]{1,0:T(2,128)(2,1)}, u32[]{:S(2)}) copy-start(bf16[2,256]{1,0:T(2,128)(2,1)} %bias.7) | copy-start | bytes 3076
  63.2 14.2 %collective-permute-start.17 = (bf16[512,512]{1,0:T(8,128)(2,1)S(1)}, bf16[512,512]{1,0:T(8,128)(2,1)S(1)}, u32[]{:S(2)}, u32[]{:S(2)}) collective-permute-start(bf16[512,512]{1,0:T(8,128)(2,1)S(1)} %graph_layer.4.own), channel_id=1, source_target_pairs={{0,1},{1,0},{2,3},{3,2},{4,5},{5,4},{6,7},{7,6},{8,9},{9,8},{10,11... | collective-permute-start | bytes 1572872 | tf_op jit(solution)/shard_map/ppermute | solution.py:306
  63.3 14.2 %collective-permute-start.18 = (bf16[512,512]{1,0:T(8,128)(2,1)S(1)}, bf16[512,512]{1,0:T(8,128)(2,1)S(1)}, u32[]{:S(2)}, u32[]{:S(2)}) collective-permute-start(bf16[512,512]{1,0:T(8,128)(2,1)S(1)} %graph_layer.4.own), channel_id=1, source_target_pairs={{1,4},{0,13},{5,8},{4,1},{9,12},{8,5},{13,0},{12,9},{3,6},{2,15},{... | collective-permute-start | bytes 1572872 | tf_op jit(solution)/shard_map/ppermute | solution.py:317
  64.3 9.8 %collective-permute-start.14 = (bf16[784,256]{1,0:T(8,128)(2,1)S(1)}, bf16[784,256]{1,0:T(8,128)(2,1)S(1)}, u32[]{:S(2)}, u32[]{:S(2)}) collective-permute-start(bf16[784,256]{1,0:T(8,128)(2,1)S(1)} %copy-done.17), channel_id=1, source_target_pairs={{0,2},{2,0},{1,3},{3,1},{4,6},{6,4},{5,7},{7,5},{8,10},{10,8},{9,1... | collective-permute-start | bytes 1204232 | tf_op jit(solution)/shard_map/ppermute | solution.py:306
  65.7 11.8 %collective-permute-start.19 = (bf16[784,256]{1,0:T(8,128)(2,1)S(1)}, bf16[784,256]{1,0:T(8,128)(2,1)S(1)}, u32[]{:S(2)}, u32[]{:S(2)}) collective-permute-start(bf16[784,256]{1,0:T(8,128)(2,1)S(1)} %collective-permute-done.12.near_w), channel_id=1, source_target_pairs={{0,1},{1,0},{2,3},{3,2},{4,5},{5,4},{6,7},{7,6},{8,9},{9,8},{10,11... | collective-permute-start | bytes 1204232 | tf_op jit(solution)/shard_map/ppermute | solution.py:306
  74.0 13.2 %collective-permute-start.22 = (bf16[512,512]{1,0:T(8,128)(2,1)S(1)}, bf16[512,512]{1,0:T(8,128)(2,1)S(1)}, u32[]{:S(2)}, u32[]{:S(2)}) collective-permute-start(bf16[512,512]{1,0:T(8,128)(2,1)S(1)} %graph_layer.5.own), channel_id=1, source_target_pairs={{0,1},{1,0},{2,3},{3,2},{4,5},{5,4},{6,7},{7,6},{8,9},{9,8},{10,11... | collective-permute-start | bytes 1572872 | tf_op jit(solution)/shard_map/ppermute | solution.py:306
  74.1 13.1 %collective-permute-start.23 = (bf16[512,512]{1,0:T(8,128)(2,1)S(1)}, bf16[512,512]{1,0:T(8,128)(2,1)S(1)}, u32[]{:S(2)}, u32[]{:S(2)}) collective-permute-start(bf16[512,512]{1,0:T(8,128)(2,1)S(1)} %graph_layer.5.own), channel_id=1, source_target_pairs={{1,4},{5,8},{4,1},{9,12},{8,5},{12,9},{3,6},{7,10},{6,3},{11,14},{... | collective-permute-start | bytes 1572872 | tf_op jit(solution)/shard_map/ppermute | solution.py:317
  77.4 9.9 %collective-permute-start.24 = (bf16[784,256]{1,0:T(8,128)(2,1)S(1)}, bf16[784,256]{1,0:T(8,128)(2,1)S(1)}, u32[]{:S(2)}, u32[]{:S(2)}) collective-permute-start(bf16[784,256]{1,0:T(8,128)(2,1)S(1)} %collective-permute-done.14.near_w), channel_id=1, source_target_pairs={{0,1},{1,0},{2,3},{3,2},{4,5},{5,4},{6,7},{7,6},{8,9},{9,8},{10,11... | collective-permute-start | bytes 1204232 | tf_op jit(solution)/shard_map/ppermute | solution.py:306
  83.8 13.1 %collective-permute-start.21 = (bf16[512,256]{1,0:T(8,128)(2,1)S(1)}, bf16[512,256]{1,0:T(8,128)(2,1)S(1)}, u32[]{:S(2)}, u32[]{:S(2)}) collective-permute-start(bf16[512,256]{1,0:T(8,128)(2,1)S(1)} %get-tuple-element.113), channel_id=1, source_target_pairs={{0,2},{1,0},{2,3},{3,1},{4,6},{5,4},{6,7},{7,5},{8,10},{9,8},{10,1... | collective-permute-start | bytes 786440 | tf_op jit(solution)/shard_map/ppermute | solution.py:297
  85.0 12.0 %collective-permute-start.20 = (bf16[512,256]{1,0:T(8,128)(2,1)S(1)}, bf16[512,256]{1,0:T(8,128)(2,1)S(1)}, u32[]{:S(2)}, u32[]{:S(2)}) collective-permute-start(bf16[512,256]{1,0:T(8,128)(2,1)S(1)} %get-tuple-element.112), channel_id=1, source_target_pairs={{0,0},{1,2},{2,1},{3,3},{4,4},{5,6},{6,5},{7,7},{8,8},{9,10},{10,9... | collective-permute-start | bytes 786440 | tf_op jit(solution)/shard_map/ppermute | solution.py:296
  93.6 9.7 %collective-permute-start.25 = (bf16[512,256]{1,0:T(8,128)(2,1)S(1)}, bf16[512,256]{1,0:T(8,128)(2,1)S(1)}, u32[]{:S(2)}, u32[]{:S(2)}) collective-permute-start(bf16[512,256]{1,0:T(8,128)(2,1)S(1)} %get-tuple-element.117), channel_id=1, source_target_pairs={{0,0},{1,2},{2,1},{3,3},{4,4},{5,6},{6,5},{7,7},{8,8},{9,10},{10,9... | collective-permute-start | bytes 786440 | tf_op jit(solution)/shard_map/ppermute | solution.py:296
  96.9 7.2 %collective-permute-start.26 = (bf16[512,256]{1,0:T(8,128)(2,1)S(1)}, bf16[512,256]{1,0:T(8,128)(2,1)S(1)}, u32[]{:S(2)}, u32[]{:S(2)}) collective-permute-start(bf16[512,256]{1,0:T(8,128)(2,1)S(1)} %get-tuple-element.118), channel_id=1, source_target_pairs={{0,2},{1,0},{2,3},{3,1},{4,6},{5,4},{6,7},{7,5},{8,10},{9,8},{10,1... | collective-permute-start | bytes 786440 | tf_op jit(solution)/shard_map/ppermute | solution.py:297

commit v12 on v11

--- a/solution.py
+++ b/solution.py
@@ -154,7 +154,7 @@
 
 
 def layer_kernel(
-    layer, slots, last, core_ref, idx_ref, own, sib, rim, bias, near_w, far_w, ws_hbm, wd_hbm, w2_hbm, *refs
+    layer, graph, slots, last, core_ref, idx_ref, own, sib, rim, bias, near_w, far_w, ws_hbm, wd_hbm, w2_hbm, *refs
 ):
     outs, refs = (refs[:2], refs[2:]) if last else (refs[:1], refs[1:])
     ws, wd, w2, ws_x, wd_x, w2_x, proj, near, summed, sems = refs
@@ -170,20 +170,22 @@
     window = 3 * rows
     proj[0:8, :] = jnp.full((8, LANES), DEAD, jnp.float32)
     proj[4 * window + 4:4 * window + 16, :] = jnp.full((12, LANES), DEAD, jnp.float32)
+    pack = graph * (3 * share + 16)
     here, there = pl.multiple_of(core * share, 16), pl.multiple_of((1 - core) * share, 16)
     for spot, piece in ((here, near_w), (there, far_w)):
-        ws_x[pl.ds(spot, share), :] = piece[0:share, :]
-        wd_x[pl.ds(spot, share), :] = piece[share:2 * share, :]
+        ws_x[pl.ds(spot, share), :] = piece[pack:pack + share, :]
+        wd_x[pl.ds(spot, share), :] = piece[pack + share:pack + 2 * share, :]
+    third = slice(pack + 2 * share, pack + 3 * share)
 
     @pl.when(core == 0)
     def _():
-        w2_x[:, :share] = near_w[2 * share:3 * share, :]
-        w2_x[:, share:] = far_w[2 * share:3 * share, :]
+        w2_x[:, :share] = near_w[third, :]
+        w2_x[:, share:] = far_w[third, :]
 
     @pl.when(core != 0)
     def _():
-        w2_x[:, share:] = near_w[2 * share:3 * share, :]
-        w2_x[:, :share] = far_w[2 * share:3 * share, :]
+        w2_x[:, share:] = near_w[third, :]
+        w2_x[:, :share] = far_w[third, :]
 
     def put(dst, base, first, values):
         for c in range(values.shape[1] // LANES):
@@ -193,7 +195,7 @@
         return jnp.dot(values[...], weights[...], preferred_element_type=jnp.float32)
 
     b_own = bias[layer:layer + 1, :].astype(jnp.float32)
-    b_other = near_w[3 * share:3 * share + 1, :].astype(jnp.float32)
+    b_other = near_w[pack + 3 * share:pack + 3 * share + 1, :].astype(jnp.float32)
     put(near, 0, part, product(own, wd_x) + b_other)
     put(proj, 1, part, product(own, ws_x))
     copies[0].wait()
@@ -237,7 +239,7 @@
             outs[1][...] = result[:, :share]
 
 
-def run_layer(layer, slots, last, core, idx, own, sib, rim, ws, wd, w2, bias, near_w, far_w):
+def run_layer(layer, graph, slots, last, core, idx, own, sib, rim, ws, wd, w2, bias, near_w, far_w):
     rows, width = own.shape
     share = width // 2
     chunks = width // LANES
@@ -250,7 +252,7 @@
     else:
         out_shape, out_specs = jax.ShapeDtypeStruct((rows, width), bf16), vmem
     return pl.pallas_call(
-        functools.partial(layer_kernel, layer, slots, last),
+        functools.partial(layer_kernel, layer, graph, slots, last),
         out_shape=out_shape,
         in_specs=[smem] * 2 + [vmem] * 6 + [pl.BlockSpec(memory_space=pl.ANY)] * 3,
         out_specs=out_specs,
@@ -317,34 +319,39 @@
     return lax.ppermute(own, ("mesh", "batch"), pairs)
 
 
-def pack_kernel(order, core_ref, g_bias, r_bias, *refs):
+def pack_kernel(layers, core_ref, g_bias, r_bias, *refs):
     weights, outs, sems = (refs[:3], refs[3:6]), refs[6:-1], refs[-1]
     share = g_bias.shape[1]
     here = pl.multiple_of(core_ref[0] * share, share)
     copies = []
-    for (graph, layer), out in zip(order, outs):
-        ws, wd, w2 = weights[graph]
-        sources = (ws.at[layer, pl.ds(here, share), :], wd.at[layer, pl.ds(here, share), :], w2.at[layer, :, pl.ds(here, share)])
-        for i, source in enumerate(sources):
-            copies.append(pltpu.make_async_copy(source, out.at[i * share:(i + 1) * share, :], sems.at[len(copies)]))
-            copies[-1].start()
-    for (graph, layer), out in zip(order, outs):
-        bias = (g_bias, r_bias)[graph][layer:layer + 1, :]
-        out[3 * share:, :] = jnp.broadcast_to(bias, (16, share))
+    for layer, out in zip(layers, outs):
+        for graph, (ws, wd, w2) in enumerate(weights):
+            base = graph * (3 * share + 16)
+            sources = (
+                ws.at[layer, pl.ds(here, share), :], wd.at[layer, pl.ds(here, share), :], w2.at[layer, :, pl.ds(here, share)]
+            )
+            for i, source in enumerate(sources):
+                spot = base + i * share
+                copies.append(pltpu.make_async_copy(source, out.at[spot:spot + share, :], sems.at[len(copies)]))
+                copies[-1].start()
+    for layer, out in zip(layers, outs):
+        for graph, bias in enumerate((g_bias, r_bias)):
+            base = graph * (3 * share + 16) + 3 * share
+            out[base:base + 16, :] = jnp.broadcast_to(bias[layer:layer + 1, :], (16, share))
     for copy in copies:
         copy.wait()
 
 
-def pack_weights(order, core, g_weights, g_bias, r_weights, r_bias):
+def pack_weights(layers, core, g_weights, g_bias, r_weights, r_bias):
     share = g_bias.shape[1]
     vmem = pl.BlockSpec(memory_space=pltpu.VMEM)
     hbm = pl.BlockSpec(memory_space=pltpu.HBM)
     return pl.pallas_call(
-        functools.partial(pack_kernel, order),
-        out_shape=(jax.ShapeDtypeStruct((3 * share + 16, share), jnp.bfloat16),) * len(order),
+        functools.partial(pack_kernel, layers),
+        out_shape=(jax.ShapeDtypeStruct((2 * (3 * share + 16), share), jnp.bfloat16),) * len(layers),
         in_specs=[pl.BlockSpec(memory_space=pltpu.SMEM)] + [vmem] * 2 + [hbm] * 6,
-        out_specs=(vmem,) * len(order),
-        scratch_shapes=[pltpu.SemaphoreType.DMA((3 * len(order),))],
+        out_specs=(vmem,) * len(layers),
+        scratch_shapes=[pltpu.SemaphoreType.DMA((6 * len(layers),))],
         compiler_params=pltpu.CompilerParams(vmem_limit_bytes=60 << 20),
         cost_estimate=pl.CostEstimate(flops=256 * share**3, bytes_accessed=1, transcendentals=0),
         name="pack_weights",
@@ -372,8 +379,7 @@
     same = lax.dynamic_slice(g_own, (part * half, 0), (half, g_own.shape[1]))
     other = lax.dynamic_slice(g_own, ((1 - part) * half, 0), (half, g_own.shape[1]))
     g_a, g_b = spread_rows(same, other)
-    order = [(graph, layer) for layer in range(layers) for graph in (0, 1)]
-    packs = list(pack_weights(order[:1], core1, g_weights, g_b1, r_weights, r_b1))
+    packs = list(pack_weights((0,), core1, g_weights, g_b1, r_weights, r_b1))
     near_w = [swap(packs[0], "mp")]
     bnd = jnp.stack([bnd_src, bnd_part[:, 0], bnd_node])
     bnd, packs[0], same, other = after((bnd, packs[0], same, other))
@@ -383,43 +389,36 @@
         landed.append(lax.ppermute(pieces[k], "mesh", [(i, (i + k) % parts) for i in range(parts)]))
     landed[0], core1, g_a, g_b = after((landed[0], core1, g_a, g_b))
     idx = edge_offsets(jnp.stack([g_nbr, r_nbr]), jnp.stack([g_count, r_count]), core)
-    packs += pack_weights(order[1:], core1, g_weights, g_b1, r_weights, r_b1)
+    packs += pack_weights(tuple(range(1, layers)), core1, g_weights, g_b1, r_weights, r_b1)
     g_idx, r_idx = idx[0], idx[1]
-    g_a, g_b, g_idx, r_idx, packs[1], near_w[0], *landed = after(
-        (g_a, g_b, g_idx, r_idx, packs[1], near_w[0], *landed)
+    g_a, g_b, g_idx, r_idx, packs[1:], near_w[0], *landed = after(
+        (g_a, g_b, g_idx, r_idx, packs[1:], near_w[0], *landed)
     )
     planet = ordered(core, g_a, g_b, 1)
     g_sib, g_rim = swap(planet, "batch"), rims(planet, True)
-    *r_pair, packs[1] = after((*add_force(part.reshape(1), r_own, landed, cap), packs[1]))
+    *r_pair, packs[1:] = after((*add_force(part.reshape(1), r_own, landed, cap), packs[1:]))
     r_a, r_b = spread_rows(*r_pair)
-    near_w.append(swap(packs[1], "mp"))
-    r_a, r_b, g_sib, g_rim, near_w[0] = after((r_a, r_b, g_sib, g_rim, near_w[0]))
+    near_w += [swap(pack, "mp") for pack in packs[1:]]
+    r_a, r_b, g_sib, g_rim = after((r_a, r_b, g_sib, g_rim))
     regional, g_idx = after((ordered(core, r_a, r_b, 1), g_idx))
     r_sib, r_rim = swap(regional, "batch"), rims(regional, False)
-    r_sib, near_w[1] = after((r_sib, near_w[1]))
-    for i, (graph, layer) in enumerate(order):
+    for layer in range(layers):
         last = layer == layers - 1
-        far_w = swap(near_w[i], "batch")
-        if i + 1 < len(order):
-            near_w[i + 1], core1 = after((near_w[i + 1], core1))
-        if i + 2 < len(order):
-            packs[i + 2], near_w[i + 1] = after((packs[i + 2], near_w[i + 1]))
-            near_w.append(swap(packs[i + 2], "mp"))
-        if graph == 0:
-            planet = run_layer(
-                layer, slots, last, core1, g_idx, planet, g_sib, g_rim, g_ws, g_wd, g_w2, g_b1, near_w[i], far_w
-            )
-            *planet, core1 = after((*(planet if last else (planet,)), core1))
-            if not last:
-                planet = planet[0]
-                g_sib, g_rim = swap(planet, "batch"), rims(planet, True)
-        else:
-            regional = run_layer(
-                layer, slots, last, core1, r_idx, regional, r_sib, r_rim, r_ws, r_wd, r_w2, r_b1, near_w[i], far_w
-            )
-            if not last:
-                regional, core1 = after((regional, core1))
-                r_sib, r_rim = swap(regional, "batch"), rims(regional, False)
+        far_w = swap(near_w[layer], "batch")
+        planet = run_layer(
+            layer, 0, slots, last, core1, g_idx, planet, g_sib, g_rim, g_ws, g_wd, g_w2, g_b1, near_w[layer], far_w
+        )
+        *planet, core1 = after((*(planet if last else (planet,)), core1))
+        if not last:
+            planet = planet[0]
+            g_sib, g_rim = swap(planet, "batch"), rims(planet, True)
+            core1, near_w[layer + 1] = after((core1, near_w[layer + 1]))
+        regional = run_layer(
+            layer, 1, slots, last, core1, r_idx, regional, r_sib, r_rim, r_ws, r_wd, r_w2, r_b1, near_w[layer], far_w
+        )
+        if not last:
+            regional, core1 = after((regional, core1))
+            r_sib, r_rim = swap(regional, "batch"), rims(regional, False)
     g_out = ordered(part, *gather_rows(*planet), 0)
     g_out, *regional_rows = after((g_out, *gather_rows(*regional)))
     r_out = ordered(part, *regional_rows, 0)

time: 105 us -> 99.8 us (0.950)
  starting transfers between devices: 40.4 us -> 32.6 us
  waiting for transfers between devices: 25.5 us -> 27.4 us
    ppermute x12 -> x8, starting transfers between devices: 10.4 us -> 4.95 us  [swap(): return lax.ppermute(values, axis, [(0, 1), (1, 0)])]
    ppermute x12 -> x8, waiting for transfers between devices: 7.37 us -> 8.84 us  [swap(): return lax.ppermute(values, axis, [(0, 1), (1, 0)])]
    ppermute x2, waiting for transfers between devices: 5.31 us -> 6.75 us  [gather_rows(): same = lax.ppermute(a, ('mp', 'batch'), [(0, 0), (1, 2), (2, 1), (3, 3)])]
    ppermute x4, starting transfers between devices: 9.14 us -> 7.79 us  [rims(): return lax.ppermute(own, ('mesh', 'batch'), pairs)]
    ppermute x2, starting transfers between devices: 1.17 us -> 0.04 us  [gather_rows(): other = lax.ppermute(b, ('mp', 'batch'), [(0, 2), (1, 0), (2, 3), (3, 1)])]
  transfers between devices with their start and end apart: 27 -> 23, of which waited for: 8 -> 7; matrix products, arithmetic and copies ran while one was open for 1% -> 1% of each run, Pallas kernels for 32% -> 34%
where the time goes in v12:
time: 99.8 us; the launch traced here: 99.4 us
  Pallas kernels  33.9 us (34%)
  starting transfers between devices  32.6 us (33%)
  waiting for transfers between devices  27.4 us (27%)
  other arithmetic  2.43 us (2%)
  local copies, waits for them, and re-layouts  1.87 us (2%)
  between operations  1.13 us (1%)
    pallas_call x4, Pallas kernels, run_layer(): pl.pallas_call(functools.partial(layer_kernel, layer, graph, slots, last)...  25.2 us
    ppermute x2, starting transfers between devices, spread_rows(): a = lax.ppermute(same, ('mp', 'batch'), [(0, 0), (1, 2), (2, 1), (3, 3)])  9.45 us
    ppermute x8, waiting for transfers between devices, swap(): return lax.ppermute(values, axis, [(0, 1), (1, 0)])  8.84 us
    ppermute x4, starting transfers between devices, rims(): return lax.ppermute(own, ('mesh', 'batch'), pairs)  7.79 us
    ppermute x2, waiting for transfers between devices, gather_rows(): same = lax.ppermute(a, ('mp', 'batch'), [(0, 0), (1, 2), (2, 1), (3, 3)])  6.75 us
    pallas_call x2, Pallas kernels, pack_weights(): pl.pallas_call(functools.partial(pack_kernel, layers), out_shape=(jax.Sha...  5.78 us
    ppermute x3, waiting for transfers between devices, by_rows(): lax.ppermute(pieces[k], 'mesh', [(i, (i + k) % parts) for i in range(part...  5.64 us
    ppermute x2, starting transfers between devices, gather_rows(): same = lax.ppermute(a, ('mp', 'batch'), [(0, 0), (1, 2), (2, 1), (3, 3)])  5.56 us
  transfers between devices with their start and end apart: 23, of which 7 were waited for; matrix products, arithmetic and copies ran while one was open for 1% of the time, Pallas kernels for 34%

profile of v12, /device:TPU:1, one launch (start us, length us, event | category | flops | bytes accessed | tf_op | source)
XLA Modules:
  0.0 99.4 jit_solution(16888097289893357138)
XLA Ops:
  0.6 1.1 %dynamic-slice_bitcast_fusion = (bf16[512,256]{1,0:T(8,128)(2,1)S(1)}, bf16[512,256]{1,0:T(8,128)(2,1)S(1)}) fusion(bf16[1,1024,256]{2,1,0:T(8,128)(2,1)} %param.17, s32[]{:T(128)S(6)} %select_n.78, s32[]{:T(128)S(6)} %select_n.77), kind=kLoop, calls=%fused_computation.4 | loop fusion | bytes 1048584 | tf_op jit(solution)/shard_map/dynamic_slice | solution.py:380
  1.7 4.5 %collective-permute-start = (bf16[512,256]{1,0:T(8,128)(2,1)S(1)}, bf16[512,256]{1,0:T(8,128)(2,1)S(1)}, u32[]{:S(2)}, u32[]{:S(2)}) collective-permute-start(bf16[512,256]{1,0:T(8,128)(2,1)S(1)} %get-tuple-element.95), channel_id=1, source_target_pairs={{0,0},{1,2},{2,1},{3,3},{4,4},{5,6},{6,5},{7,7},{8,8},{9,10},{10,9... | collective-permute-start | bytes 786440 | tf_op jit(solution)/shard_map/ppermute | solution.py:292
  6.2 0.0 collective-permute-start.1
  6.3 0.0 copy-start
  6.3 2.9 %pack_weights.2 = bf16[1568,256]{1,0:T(8,128)(2,1)} custom-call(s32[1]{0:T(128)} %bitcast.4.core_ref, bf16[2,256]{1,0:T(2,128)(2,1)} %bias.6, bf16[2,256]{1,0:T(2,128)(2,1)} %bias.7, bf16[2,512,256]{2,1,0:T(8,128)(2,1)} %ws_hbm.6, bf16[2,512,256]{2,1,0:T(8,128)(2,1)} %wd_hbm.6, bf16[2,256,512]{2,1,0:T(8,128)(2,1)} %w2_hbm.6, bf16[2,512,256]{2,1,0:T(8,128)(2,1)} %ws_hbm.7, ...), custom_call_target="tpu_custom_call" | custom-call | flops 4294967296 | bytes 1 | tf_op jit(solution)/shard_map/pack_weights/pallas_call | solution.py:349
  9.2 0.2 collective-permute-start.2
  9.4 0.7 copy-done.15
  10.0 0.0 copy-done.14
  10.1 0.0 copy-start.12
  10.1 0.0 copy-start.11
  10.1 2.3 %pick_rows.1 = (bf16[272,256]{1,0:T(8,128)(2,1)S(1)}, bf16[272,256]{1,0:T(8,128)(2,1)S(1)}, bf16[272,256]{1,0:T(8,128)(2,1)S(1)}, bf16[272,256]{1,0:T(8,128)(2,1)S(1)}) custom-call(s32[1]{0:T(128)} %bitcast.me_ref, s32[3,512]{1,0:T(4,128)S(1)} %pad_add_fusion.bnd_ref, bf16[1024,256]{1,0:T(8,128)(2,1)S(1)} %bitcast.33), custom_call_target="tpu_custom_call" | custom-call | flops 8589934592 | bytes 1 | tf_op jit(solution)/shard_map/pick_rows/pallas_call | solution.py:115
  12.4 1.3 %collective-permute-start.3 = (bf16[272,256]{1,0:T(8,128)(2,1)S(1)}, bf16[272,256]{1,0:T(8,128)(2,1)S(1)}, u32[]{:S(2)}, u32[]{:S(2)}) collective-permute-start(bf16[272,256]{1,0:T(8,128)(2,1)S(1)} %get-tuple-element.54), channel_id=1, source_target_pairs={{0,4},{4,8},{8,12},{12,0},{1,5},{5,9},{9,13},{13,1},{2,6},{6,10},{... | collective-permute-start | bytes 417800 | tf_op jit(solution)/shard_map/ppermute | solution.py:389
  13.7 2.3 %collective-permute-start.4 = (bf16[272,256]{1,0:T(8,128)(2,1)S(1)}, bf16[272,256]{1,0:T(8,128)(2,1)S(1)}, u32[]{:S(2)}, u32[]{:S(2)}) collective-permute-start(bf16[272,256]{1,0:T(8,128)(2,1)S(1)} %get-tuple-element.55), channel_id=1, source_target_pairs={{0,8},{4,12},{8,0},{12,4},{1,9},{5,13},{9,1},{13,5},{2,10},{6,14},... | collective-permute-start | bytes 417800 | tf_op jit(solution)/shard_map/ppermute | solution.py:389
  16.1 0.1 fusion.5
  16.2 1.1 %collective-permute-start.5 = (bf16[272,256]{1,0:T(8,128)(2,1)S(1)}, bf16[272,256]{1,0:T(8,128)(2,1)S(1)}, u32[]{:S(2)}, u32[]{:S(2)}) collective-permute-start(bf16[272,256]{1,0:T(8,128)(2,1)S(1)} %get-tuple-element.56), channel_id=1, source_target_pairs={{0,12},{4,0},{8,4},{12,8},{1,13},{5,1},{9,5},{13,9},{2,14},{6,2},{... | collective-permute-start | bytes 417800 | tf_op jit(solution)/shard_map/ppermute | solution.py:389
  17.4 2.9 %pack_weights.3 = bf16[1568,256]{1,0:T(8,128)(2,1)} custom-call(s32[1]{0:T(128)} %bitcast.4.core_ref, bf16[2,256]{1,0:T(2,128)(2,1)} %bias.6, bf16[2,256]{1,0:T(2,128)(2,1)} %bias.7, bf16[2,512,256]{2,1,0:T(8,128)(2,1)} %ws_hbm.6, bf16[2,512,256]{2,1,0:T(8,128)(2,1)} %wd_hbm.6, bf16[2,256,512]{2,1,0:T(8,128)(2,1)} %w2_hbm.6, bf16[2,512,256]{2,1,0:T(8,128)(2,1)} %ws_hbm.7, ...), custom_call_target="tpu_custom_call" | custom-call | flops 4294967296 | bytes 1 | tf_op jit(solution)/shard_map/pack_weights/pallas_call | solution.py:349
  20.2 5.6 %collective-permute-done.4.refs_2_ = bf16[272,256]{1,0:T(8,128)(2,1)S(1)} collective-permute-done((bf16[272,256]{1,0:T(8,128)(2,1)S(1)}, bf16[272,256]{1,0:T(8,128)(2,1)S(1)}, u32[]{:S(2)}, u32[]{:S(2)}) %collective-permute-start.4) | collective-permute-done | bytes 139296 | tf_op jit(solution)/shard_map/ppermute | solution.py:389
  25.9 3.8 %collective-permute-done.2.near_w = bf16[1568,256]{1,0:T(8,128)(2,1)S(1)} collective-permute-done((bf16[1568,256]{1,0:T(8,128)(2,1)}, bf16[1568,256]{1,0:T(8,128)(2,1)S(1)}, u32[]{:S(2)}, u32[]{:S(2)}) %collective-permute-start.2) | collective-permute-done | bytes 802848 | tf_op jit(solution)/shard_map/ppermute | solution.py:308
  29.6 1.3 %collective-permute-start.10 = (bf16[1568,256]{1,0:T(8,128)(2,1)S(1)}, bf16[1568,256]{1,0:T(8,128)(2,1)S(1)}, u32[]{:S(2)}, u32[]{:S(2)}) collective-permute-start(bf16[1568,256]{1,0:T(8,128)(2,1)S(1)} %collective-permute-done.2.near_w), channel_id=1, source_target_pairs={{0,1},{1,0},{2,3},{3,2},{4,5},{5,4},{6,7},{7,6},{8,9},{9,8},{10,11... | collective-permute-start | bytes 2408456 | tf_op jit(solution)/shard_map/ppermute | solution.py:308
  31.0 0.1 maximum_select_fusion.own
  31.1 0.1 collective-permute-start.8
  31.2 1.7 %collective-permute-start.9 = (bf16[512,512]{1,0:T(8,128)(2,1)S(1)}, bf16[512,512]{1,0:T(8,128)(2,1)S(1)}, u32[]{:S(2)}, u32[]{:S(2)}) collective-permute-start(bf16[512,512]{1,0:T(8,128)(2,1)S(1)} %maximum_select_fusion.own), channel_id=1, source_target_pairs={{1,4},{0,13},{5,8},{4,1},{9,12},{8,5},{13,0},{12,9},{3,6},{2,15},{... | collective-permute-start | bytes 1572872 | tf_op jit(solution)/shard_map/ppermute | solution.py:319
  32.9 0.7 add_force.1
  33.6 4.9 %collective-permute-start.6 = (bf16[512,256]{1,0:T(8,128)(2,1)S(1)}, bf16[512,256]{1,0:T(8,128)(2,1)S(1)}, u32[]{:S(2)}, u32[]{:S(2)}) collective-permute-start(bf16[512,256]{1,0:T(8,128)(2,1)S(1)} %get-tuple-element.64), channel_id=1, source_target_pairs={{0,0},{1,2},{2,1},{3,3},{4,4},{5,6},{6,5},{7,7},{8,8},{9,10},{10,9... | collective-permute-start | bytes 786440 | tf_op jit(solution)/shard_map/ppermute | solution.py:292
  38.6 0.0 collective-permute-start.7
  38.6 4.3 %collective-permute-done.6 = bf16[512,256]{1,0:T(8,128)(2,1)S(1)} collective-permute-done((bf16[512,256]{1,0:T(8,128)(2,1)S(1)}, bf16[512,256]{1,0:T(8,128)(2,1)S(1)}, u32[]{:S(2)}, u32[]{:S(2)}) %collective-permute-start.6) | collective-permute-done | bytes 262176 | tf_op jit(solution)/shard_map/ppermute | solution.py:292
  42.9 1.8 %collective-permute-done.7 = bf16[512,256]{1,0:T(8,128)(2,1)S(1)} collective-permute-done((bf16[512,256]{1,0:T(8,128)(2,1)S(1)}, bf16[512,256]{1,0:T(8,128)(2,1)S(1)}, u32[]{:S(2)}, u32[]{:S(2)}) %collective-permute-start.7) | collective-permute-done | bytes 262176 | tf_op jit(solution)/shard_map/ppermute | solution.py:293
  44.7 0.1 maximum_select_fusion.1.own
  44.9 2.7 %collective-permute-start.12 = (bf16[512,512]{1,0:T(8,128)(2,1)S(1)}, bf16[512,512]{1,0:T(8,128)(2,1)S(1)}, u32[]{:S(2)}, u32[]{:S(2)}) collective-permute-start(bf16[512,512]{1,0:T(8,128)(2,1)S(1)} %maximum_select_fusion.1.own), channel_id=1, source_target_pairs={{0,1},{1,0},{2,3},{3,2},{4,5},{5,4},{6,7},{7,6},{8,9},{9,8},{10,11... | collective-permute-start | bytes 1572872 | tf_op jit(solution)/shard_map/ppermute | solution.py:308
  47.5 1.9 %collective-permute-start.13 = (bf16[512,512]{1,0:T(8,128)(2,1)S(1)}, bf16[512,512]{1,0:T(8,128)(2,1)S(1)}, u32[]{:S(2)}, u32[]{:S(2)}) collective-permute-start(bf16[512,512]{1,0:T(8,128)(2,1)S(1)} %maximum_select_fusion.1.own), channel_id=1, source_target_pairs={{1,4},{5,8},{4,1},{9,12},{8,5},{12,9},{3,6},{7,10},{6,3},{11,14},{... | collective-permute-start | bytes 1572872 | tf_op jit(solution)/shard_map/ppermute | solution.py:319
  49.5 6.3 %graph_layer.4.own = bf16[512,512]{1,0:T(8,128)(2,1)S(1)} custom-call(s32[1]{0:T(128)} %bitcast.4.core_ref, s32[4096]{0:T(1024)S(1)} %bitcast.37, bf16[512,512]{1,0:T(8,128)(2,1)S(1)} %maximum_select_fusion.own, bf16[512,512]{1,0:T(8,128)(2,1)S(1)} %collective-permute-done.8.sib, bf16[512,512]{1,0:T(8,128)(2,1)S(1)} %collective-permute-done.9.rim, ...), custom_call_target="tpu_custom_call" | custom-call | flops 8589934592 | bytes 2621440 | tf_op jit(solution)/shard_map/graph_layer/pallas_call | solution.py:254
  55.8 0.1 collective-permute-start.14
  55.9 1.8 %collective-permute-start.15 = (bf16[512,512]{1,0:T(8,128)(2,1)S(1)}, bf16[512,512]{1,0:T(8,128)(2,1)S(1)}, u32[]{:S(2)}, u32[]{:S(2)}) collective-permute-start(bf16[512,512]{1,0:T(8,128)(2,1)S(1)} %graph_layer.4.own), channel_id=1, source_target_pairs={{1,4},{0,13},{5,8},{4,1},{9,12},{8,5},{13,0},{12,9},{3,6},{2,15},{... | collective-permute-start | bytes 1572872 | tf_op jit(solution)/shard_map/ppermute | solution.py:319
  57.7 5.1 %collective-permute-done.11.near_w = bf16[1568,256]{1,0:T(8,128)(2,1)S(1)} collective-permute-done((bf16[1568,256]{1,0:T(8,128)(2,1)S(1)}, bf16[1568,256]{1,0:T(8,128)(2,1)S(1)}, u32[]{:S(2)}, u32[]{:S(2)}) %collective-permute-start.11) | collective-permute-done | bytes 802848 | tf_op jit(solution)/shard_map/ppermute | solution.py:308
  62.7 0.6 collective-permute-start.16
  63.4 6.3 %graph_layer.5.own = bf16[512,512]{1,0:T(8,128)(2,1)S(1)} custom-call(s32[1]{0:T(128)} %bitcast.4.core_ref, s32[4096]{0:T(1024)S(1)} %bitcast.35, bf16[512,512]{1,0:T(8,128)(2,1)S(1)} %maximum_select_fusion.1.own, bf16[512,512]{1,0:T(8,128)(2,1)S(1)} %collective-permute-done.12.sib, bf16[512,512]{1,0:T(8,128)(2,1)S(1)} %collective-permute-done.13.rim, ...), custom_call_target="tpu_custom_call" | custom-call | flops 8589934592 | bytes 2621440 | tf_op jit(solution)/shard_map/graph_layer/pallas_call | solution.py:254
  69.6 0.1 collective-permute-start.19
  69.7 2.4 %collective-permute-start.20 = (bf16[512,512]{1,0:T(8,128)(2,1)S(1)}, bf16[512,512]{1,0:T(8,128)(2,1)S(1)}, u32[]{:S(2)}, u32[]{:S(2)}) collective-permute-start(bf16[512,512]{1,0:T(8,128)(2,1)S(1)} %graph_layer.5.own), channel_id=1, source_target_pairs={{1,4},{5,8},{4,1},{9,12},{8,5},{12,9},{3,6},{7,10},{6,3},{11,14},{... | collective-permute-start | bytes 1572872 | tf_op jit(solution)/shard_map/ppermute | solution.py:319
  72.2 6.3 %graph_layer.6 = (bf16[512,256]{1,0:T(8,128)(2,1)S(1)}, bf16[512,256]{1,0:T(8,128)(2,1)S(1)}) custom-call(s32[1]{0:T(128)} %bitcast.4.core_ref, s32[4096]{0:T(1024)S(1)} %bitcast.38, bf16[512,512]{1,0:T(8,128)(2,1)S(1)} %graph_layer.4.own, bf16[512,512]{1,0:T(8,128)(2,1)S(1)} %collective-permute-done.14.sib, ...), custom_call_target="tpu_custom_call" | custom-call | flops 8589934592 | bytes 2621440 | tf_op jit(solution)/shard_map/graph_layer/pallas_call | solution.py:254
  78.5 3.0 %collective-permute-start.17 = (bf16[512,256]{1,0:T(8,128)(2,1)S(1)}, bf16[512,256]{1,0:T(8,128)(2,1)S(1)}, u32[]{:S(2)}, u32[]{:S(2)}) collective-permute-start(bf16[512,256]{1,0:T(8,128)(2,1)S(1)} %get-tuple-element.85), channel_id=1, source_target_pairs={{0,0},{1,2},{2,1},{3,3},{4,4},{5,6},{6,5},{7,7},{8,8},{9,10},{10,9... | collective-permute-start | bytes 786440 | tf_op jit(solution)/shard_map/ppermute | solution.py:298
  81.5 0.0 collective-permute-start.18
  81.5 6.3 %graph_layer.7 = (bf16[512,256]{1,0:T(8,128)(2,1)S(1)}, bf16[512,256]{1,0:T(8,128)(2,1)S(1)}) custom-call(s32[1]{0:T(128)} %bitcast.4.core_ref, s32[4096]{0:T(1024)S(1)} %bitcast.36, bf16[512,512]{1,0:T(8,128)(2,1)S(1)} %graph_layer.5.own, bf16[512,512]{1,0:T(8,128)(2,1)S(1)} %collective-permute-done.19.sib, ...), custom_call_target="tpu_custom_call" | custom-call | flops 8589934592 | bytes 2621440 | tf_op jit(solution)/shard_map/graph_layer/pallas_call | solution.py:254
  87.9 2.6 %collective-permute-start.21 = (bf16[512,256]{1,0:T(8,128)(2,1)S(1)}, bf16[512,256]{1,0:T(8,128)(2,1)S(1)}, u32[]{:S(2)}, u32[]{:S(2)}) collective-permute-start(bf16[512,256]{1,0:T(8,128)(2,1)S(1)} %get-tuple-element.89), channel_id=1, source_target_pairs={{0,0},{1,2},{2,1},{3,3},{4,4},{5,6},{6,5},{7,7},{8,8},{9,10},{10,9... | collective-permute-start | bytes 786440 | tf_op jit(solution)/shard_map/ppermute | solution.py:298
  90.4 0.0 collective-permute-start.22
  90.5 1.0 %maximum_select_fusion.2 = bf16[1024,256]{1,0:T(8,128)(2,1)} fusion(bf16[512,256]{1,0:T(8,128)(2,1)S(1)} %collective-permute-done.18, bf16[512,256]{1,0:T(8,128)(2,1)S(1)} %collective-permute-done.17, pred[]{:T(512)S(6)} %eq.6), kind=kLoop, calls=%fused_computation.2 | loop fusion | flops 2359296 | bytes 1048577 | tf_op jit(solution)/shard_map/jit(_where)/select_n | solution.py:304
  91.5 6.8 %collective-permute-done.21 = bf16[512,256]{1,0:T(8,128)(2,1)S(1)} collective-permute-done((bf16[512,256]{1,0:T(8,128)(2,1)S(1)}, bf16[512,256]{1,0:T(8,128)(2,1)S(1)}, u32[]{:S(2)}, u32[]{:S(2)}) %collective-permute-start.21) | collective-permute-done | bytes 262176 | tf_op jit(solution)/shard_map/ppermute | solution.py:298
  98.3 0.1 collective-permute-done.22
  98.4 1.0 %maximum_select_fusion.3 = bf16[1,1024,256]{2,1,0:T(8,128)(2,1)} fusion(bf16[1,512,256]{2,1,0:T(8,128)(2,1)S(1)} %bitcast.41, bf16[1,512,256]{2,1,0:T(8,128)(2,1)S(1)} %bitcast.40, pred[]{:T(512)S(6)} %eq.6), kind=kLoop, calls=%fused_computation.3 | loop fusion | flops 2359296 | bytes 1048577 | tf_op jit(solution)/shard_map/jit(_where)/select_n | solution.py:304
  (54 shorter events, 0.2 us)
Async XLA Ops:
  1.7 14.5 %collective-permute-start = (bf16[512,256]{1,0:T(8,128)(2,1)S(1)}, bf16[512,256]{1,0:T(8,128)(2,1)S(1)}, u32[]{:S(2)}, u32[]{:S(2)}) collective-permute-start(bf16[512,256]{1,0:T(8,128)(2,1)S(1)} %get-tuple-element.95), channel_id=1, source_target_pairs={{0,0},{1,2},{2,1},{3,3},{4,4},{5,6},{6,5},{7,7},{8,8},{9,10},{10,9... | collective-permute-start | bytes 786440 | tf_op jit(solution)/shard_map/ppermute | solution.py:292
  6.2 11.1 %collective-permute-start.1 = (bf16[512,256]{1,0:T(8,128)(2,1)S(1)}, bf16[512,256]{1,0:T(8,128)(2,1)S(1)}, u32[]{:S(2)}, u32[]{:S(2)}) collective-permute-start(bf16[512,256]{1,0:T(8,128)(2,1)S(1)} %get-tuple-element.94), channel_id=1, source_target_pairs={{0,1},{1,3},{2,0},{3,2},{4,5},{5,7},{6,4},{7,6},{8,9},{9,11},{10,8... | collective-permute-start | bytes 786440 | tf_op jit(solution)/shard_map/ppermute | solution.py:293
  6.3 3.1 %copy-start.16 = (s32[512]{0:T(512)S(1)}, s32[512]{0:T(512)}, u32[]{:S(2)}) copy-start(s32[512]{0:T(512)} %param.23) | copy-start | bytes 6148
  6.3 3.8 %copy-start = (bf16[1,1024,256]{2,1,0:T(8,128)(2,1)S(1)}, bf16[1,1024,256]{2,1,0:T(8,128)(2,1)}, u32[]{:S(2)}) copy-start(bf16[1,1024,256]{2,1,0:T(8,128)(2,1)} %param.17) | copy-start | bytes 1572868
  9.2 20.4 %collective-permute-start.2 = (bf16[1568,256]{1,0:T(8,128)(2,1)}, bf16[1568,256]{1,0:T(8,128)(2,1)S(1)}, u32[]{:S(2)}, u32[]{:S(2)}) collective-permute-start(bf16[1568,256]{1,0:T(8,128)(2,1)} %pack_weights.2), channel_id=1, source_target_pairs={{0,2},{2,0},{1,3},{3,1},{4,6},{6,4},{5,7},{7,5},{8,10},{10,8},{9,1... | collective-permute-start | bytes 2408456 | tf_op jit(solution)/shard_map/ppermute | solution.py:308
  9.4 0.7 copy-start.15
  9.4 0.7 copy-start.14
  10.1 6.0 %copy-start.12 = (s32[1024]{0:T(1024)S(1)}, s32[1024]{0:T(1024)}, u32[]{:S(2)}) copy-start(s32[1024]{0:T(1024)} %param.20) | copy-start | bytes 12292
  10.1 6.0 %copy-start.13 = (s32[1024]{0:T(1024)S(1)}, s32[1024]{0:T(1024)}, u32[]{:S(2)}) copy-start(s32[1024]{0:T(1024)} %param.22) | copy-start | bytes 12292
  10.1 6.0 %copy-start.11 = (s32[1024,8]{0,1:T(8,128)S(1)}, s32[1024,8]{0,1:T(8,128)}, u32[]{:S(2)}) copy-start(s32[1024,8]{0,1:T(8,128)} %param.19) | copy-start | bytes 98308
  12.4 3.8 %copy-start.10 = (s32[1024,8]{0,1:T(8,128)S(1)}, s32[1024,8]{0,1:T(8,128)}, u32[]{:S(2)}) copy-start(s32[1024,8]{0,1:T(8,128)} %param.21) | copy-start | bytes 98308
  12.4 7.8 %collective-permute-start.3 = (bf16[272,256]{1,0:T(8,128)(2,1)S(1)}, bf16[272,256]{1,0:T(8,128)(2,1)S(1)}, u32[]{:S(2)}, u32[]{:S(2)}) collective-permute-start(bf16[272,256]{1,0:T(8,128)(2,1)S(1)} %get-tuple-element.54), channel_id=1, source_target_pairs={{0,4},{4,8},{8,12},{12,0},{1,5},{5,9},{9,13},{13,1},{2,6},{6,10},{... | collective-permute-start | bytes 417800 | tf_op jit(solution)/shard_map/ppermute | solution.py:389
  13.7 12.1 %collective-permute-start.4 = (bf16[272,256]{1,0:T(8,128)(2,1)S(1)}, bf16[272,256]{1,0:T(8,128)(2,1)S(1)}, u32[]{:S(2)}, u32[]{:S(2)}) collective-permute-start(bf16[272,256]{1,0:T(8,128)(2,1)S(1)} %get-tuple-element.55), channel_id=1, source_target_pairs={{0,8},{4,12},{8,0},{12,4},{1,9},{5,13},{9,1},{13,5},{2,10},{6,14},... | collective-permute-start | bytes 417800 | tf_op jit(solution)/shard_map/ppermute | solution.py:389
  16.2 9.6 %collective-permute-start.5 = (bf16[272,256]{1,0:T(8,128)(2,1)S(1)}, bf16[272,256]{1,0:T(8,128)(2,1)S(1)}, u32[]{:S(2)}, u32[]{:S(2)}) collective-permute-start(bf16[272,256]{1,0:T(8,128)(2,1)S(1)} %get-tuple-element.56), channel_id=1, source_target_pairs={{0,12},{4,0},{8,4},{12,8},{1,13},{5,1},{9,5},{13,9},{2,14},{6,2},{... | collective-permute-start | bytes 417800 | tf_op jit(solution)/shard_map/ppermute | solution.py:389
  29.6 3.2 %copy-start.1 = (bf16[1,1024,256]{2,1,0:T(8,128)(2,1)S(1)}, bf16[1,1024,256]{2,1,0:T(8,128)(2,1)}, u32[]{:S(2)}) copy-start(bf16[1,1024,256]{2,1,0:T(8,128)(2,1)} %param.18) | copy-start | bytes 1572868
  29.6 19.9 %collective-permute-start.10 = (bf16[1568,256]{1,0:T(8,128)(2,1)S(1)}, bf16[1568,256]{1,0:T(8,128)(2,1)S(1)}, u32[]{:S(2)}, u32[]{:S(2)}) collective-permute-start(bf16[1568,256]{1,0:T(8,128)(2,1)S(1)} %collective-permute-done.2.near_w), channel_id=1, source_target_pairs={{0,1},{1,0},{2,3},{3,2},{4,5},{5,4},{6,7},{7,6},{8,9},{9,8},{10,11... | collective-permute-start | bytes 2408456 | tf_op jit(solution)/shard_map/ppermute | solution.py:308
  31.0 11.9 %copy-start.17 = (bf16[1568,256]{1,0:T(8,128)(2,1)S(1)}, bf16[1568,256]{1,0:T(8,128)(2,1)}, u32[]{:S(2)}) copy-start(bf16[1568,256]{1,0:T(8,128)(2,1)} %pack_weights.3) | copy-start | bytes 2408452
  31.1 13.6 %collective-permute-start.8 = (bf16[512,512]{1,0:T(8,128)(2,1)S(1)}, bf16[512,512]{1,0:T(8,128)(2,1)S(1)}, u32[]{:S(2)}, u32[]{:S(2)}) collective-permute-start(bf16[512,512]{1,0:T(8,128)(2,1)S(1)} %maximum_select_fusion.own), channel_id=1, source_target_pairs={{0,1},{1,0},{2,3},{3,2},{4,5},{5,4},{6,7},{7,6},{8,9},{9,8},{10,11... | collective-permute-start | bytes 1572872 | tf_op jit(solution)/shard_map/ppermute | solution.py:308
  31.2 13.5 %collective-permute-start.9 = (bf16[512,512]{1,0:T(8,128)(2,1)S(1)}, bf16[512,512]{1,0:T(8,128)(2,1)S(1)}, u32[]{:S(2)}, u32[]{:S(2)}) collective-permute-start(bf16[512,512]{1,0:T(8,128)(2,1)S(1)} %maximum_select_fusion.own), channel_id=1, source_target_pairs={{1,4},{0,13},{5,8},{4,1},{9,12},{8,5},{13,0},{12,9},{3,6},{2,15},{... | collective-permute-start | bytes 1572872 | tf_op jit(solution)/shard_map/ppermute | solution.py:319
  32.9 16.6 %copy-start.4 = (bf16[2,256,512]{2,1,0:T(8,128)(2,1)S(1)}, bf16[2,256,512]{2,1,0:T(8,128)(2,1)}, u32[]{:S(2)}) copy-start(bf16[2,256,512]{2,1,0:T(8,128)(2,1)} %w2_hbm.6) | copy-start | bytes 1572868
  33.6 15.9 %copy-start.8 = (bf16[2,256]{1,0:T(2,128)(2,1)S(1)}, bf16[2,256]{1,0:T(2,128)(2,1)}, u32[]{:S(2)}) copy-start(bf16[2,256]{1,0:T(2,128)(2,1)} %bias.6) | copy-start | bytes 3076
  33.6 15.9 %copy-start.2 = (bf16[2,512,256]{2,1,0:T(8,128)(2,1)S(1)}, bf16[2,512,256]{2,1,0:T(8,128)(2,1)}, u32[]{:S(2)}) copy-start(bf16[2,512,256]{2,1,0:T(8,128)(2,1)} %ws_hbm.6) | copy-start | bytes 1572868
  33.6 15.9 %copy-start.3 = (bf16[2,512,256]{2,1,0:T(8,128)(2,1)S(1)}, bf16[2,512,256]{2,1,0:T(8,128)(2,1)}, u32[]{:S(2)}) copy-start(bf16[2,512,256]{2,1,0:T(8,128)(2,1)} %wd_hbm.6) | copy-start | bytes 1572868
  33.6 9.3 %collective-permute-start.6 = (bf16[512,256]{1,0:T(8,128)(2,1)S(1)}, bf16[512,256]{1,0:T(8,128)(2,1)S(1)}, u32[]{:S(2)}, u32[]{:S(2)}) collective-permute-start(bf16[512,256]{1,0:T(8,128)(2,1)S(1)} %get-tuple-element.64), channel_id=1, source_target_pairs={{0,0},{1,2},{2,1},{3,3},{4,4},{5,6},{6,5},{7,7},{8,8},{9,10},{10,9... | collective-permute-start | bytes 786440 | tf_op jit(solution)/shard_map/ppermute | solution.py:292
  38.6 6.1 %collective-permute-start.7 = (bf16[512,256]{1,0:T(8,128)(2,1)S(1)}, bf16[512,256]{1,0:T(8,128)(2,1)S(1)}, u32[]{:S(2)}, u32[]{:S(2)}) collective-permute-start(bf16[512,256]{1,0:T(8,128)(2,1)S(1)} %get-tuple-element.65), channel_id=1, source_target_pairs={{0,1},{1,3},{2,0},{3,2},{4,5},{5,7},{6,4},{7,6},{8,9},{9,11},{10,8... | collective-permute-start | bytes 786440 | tf_op jit(solution)/shard_map/ppermute | solution.py:293
  42.9 19.8 %collective-permute-start.11 = (bf16[1568,256]{1,0:T(8,128)(2,1)S(1)}, bf16[1568,256]{1,0:T(8,128)(2,1)S(1)}, u32[]{:S(2)}, u32[]{:S(2)}) collective-permute-start(bf16[1568,256]{1,0:T(8,128)(2,1)S(1)} %copy-done.17), channel_id=1, source_target_pairs={{0,2},{2,0},{1,3},{3,1},{4,6},{6,4},{5,7},{7,5},{8,10},{10,8},{9,1... | collective-permute-start | bytes 2408456 | tf_op jit(solution)/shard_map/ppermute | solution.py:308
  44.8 18.5 %copy-start.5 = (bf16[2,512,256]{2,1,0:T(8,128)(2,1)S(1)}, bf16[2,512,256]{2,1,0:T(8,128)(2,1)}, u32[]{:S(2)}) copy-start(bf16[2,512,256]{2,1,0:T(8,128)(2,1)} %ws_hbm.7) | copy-start | bytes 1572868
  44.8 18.5 %copy-start.6 = (bf16[2,512,256]{2,1,0:T(8,128)(2,1)S(1)}, bf16[2,512,256]{2,1,0:T(8,128)(2,1)}, u32[]{:S(2)}) copy-start(bf16[2,512,256]{2,1,0:T(8,128)(2,1)} %wd_hbm.7) | copy-start | bytes 1572868
  44.8 18.5 %copy-start.7 = (bf16[2,256,512]{2,1,0:T(8,128)(2,1)S(1)}, bf16[2,256,512]{2,1,0:T(8,128)(2,1)}, u32[]{:S(2)}) copy-start(bf16[2,256,512]{2,1,0:T(8,128)(2,1)} %w2_hbm.7) | copy-start | bytes 1572868
  44.9 18.5 %copy-start.9 = (bf16[2,256]{1,0:T(2,128)(2,1)S(1)}, bf16[2,256]{1,0:T(2,128)(2,1)}, u32[]{:S(2)}) copy-start(bf16[2,256]{1,0:T(2,128)(2,1)} %bias.7) | copy-start | bytes 3076
  44.9 18.4 %collective-permute-start.12 = (bf16[512,512]{1,0:T(8,128)(2,1)S(1)}, bf16[512,512]{1,0:T(8,128)(2,1)S(1)}, u32[]{:S(2)}, u32[]{:S(2)}) collective-permute-start(bf16[512,512]{1,0:T(8,128)(2,1)S(1)} %maximum_select_fusion.1.own), channel_id=1, source_target_pairs={{0,1},{1,0},{2,3},{3,2},{4,5},{5,4},{6,7},{7,6},{8,9},{9,8},{10,11... | collective-permute-start | bytes 1572872 | tf_op jit(solution)/shard_map/ppermute | solution.py:308
  47.5 15.8 %collective-permute-start.13 = (bf16[512,512]{1,0:T(8,128)(2,1)S(1)}, bf16[512,512]{1,0:T(8,128)(2,1)S(1)}, u32[]{:S(2)}, u32[]{:S(2)}) collective-permute-start(bf16[512,512]{1,0:T(8,128)(2,1)S(1)} %maximum_select_fusion.1.own), channel_id=1, source_target_pairs={{1,4},{5,8},{4,1},{9,12},{8,5},{12,9},{3,6},{7,10},{6,3},{11,14},{... | collective-permute-start | bytes 1572872 | tf_op jit(solution)/shard_map/ppermute | solution.py:319
  55.8 16.3 %collective-permute-start.14 = (bf16[512,512]{1,0:T(8,128)(2,1)S(1)}, bf16[512,512]{1,0:T(8,128)(2,1)S(1)}, u32[]{:S(2)}, u32[]{:S(2)}) collective-permute-start(bf16[512,512]{1,0:T(8,128)(2,1)S(1)} %graph_layer.4.own), channel_id=1, source_target_pairs={{0,1},{1,0},{2,3},{3,2},{4,5},{5,4},{6,7},{7,6},{8,9},{9,8},{10,11... | collective-permute-start | bytes 1572872 | tf_op jit(solution)/shard_map/ppermute | solution.py:308
  55.9 16.2 %collective-permute-start.15 = (bf16[512,512]{1,0:T(8,128)(2,1)S(1)}, bf16[512,512]{1,0:T(8,128)(2,1)S(1)}, u32[]{:S(2)}, u32[]{:S(2)}) collective-permute-start(bf16[512,512]{1,0:T(8,128)(2,1)S(1)} %graph_layer.4.own), channel_id=1, source_target_pairs={{1,4},{0,13},{5,8},{4,1},{9,12},{8,5},{13,0},{12,9},{3,6},{2,15},{... | collective-permute-start | bytes 1572872 | tf_op jit(solution)/shard_map/ppermute | solution.py:319
  62.7 9.4 %collective-permute-start.16 = (bf16[1568,256]{1,0:T(8,128)(2,1)S(1)}, bf16[1568,256]{1,0:T(8,128)(2,1)S(1)}, u32[]{:S(2)}, u32[]{:S(2)}) collective-permute-start(bf16[1568,256]{1,0:T(8,128)(2,1)S(1)} %collective-permute-done.11.near_w), channel_id=1, source_target_pairs={{0,1},{1,0},{2,3},{3,2},{4,5},{5,4},{6,7},{7,6},{8,9},{9,8},{10,11... | collective-permute-start | bytes 2408456 | tf_op jit(solution)/shard_map/ppermute | solution.py:308
  69.6 11.9 %collective-permute-start.19 = (bf16[512,512]{1,0:T(8,128)(2,1)S(1)}, bf16[512,512]{1,0:T(8,128)(2,1)S(1)}, u32[]{:S(2)}, u32[]{:S(2)}) collective-permute-start(bf16[512,512]{1,0:T(8,128)(2,1)S(1)} %graph_layer.5.own), channel_id=1, source_target_pairs={{0,1},{1,0},{2,3},{3,2},{4,5},{5,4},{6,7},{7,6},{8,9},{9,8},{10,11... | collective-permute-start | bytes 1572872 | tf_op jit(solution)/shard_map/ppermute | solution.py:308
  69.7 11.8 %collective-permute-start.20 = (bf16[512,512]{1,0:T(8,128)(2,1)S(1)}, bf16[512,512]{1,0:T(8,128)(2,1)S(1)}, u32[]{:S(2)}, u32[]{:S(2)}) collective-permute-start(bf16[512,512]{1,0:T(8,128)(2,1)S(1)} %graph_layer.5.own), channel_id=1, source_target_pairs={{1,4},{5,8},{4,1},{9,12},{8,5},{12,9},{3,6},{7,10},{6,3},{11,14},{... | collective-permute-start | bytes 1572872 | tf_op jit(solution)/shard_map/ppermute | solution.py:319
  78.5 12.0 %collective-permute-start.17 = (bf16[512,256]{1,0:T(8,128)(2,1)S(1)}, bf16[512,256]{1,0:T(8,128)(2,1)S(1)}, u32[]{:S(2)}, u32[]{:S(2)}) collective-permute-start(bf16[512,256]{1,0:T(8,128)(2,1)S(1)} %get-tuple-element.85), channel_id=1, source_target_pairs={{0,0},{1,2},{2,1},{3,3},{4,4},{5,6},{6,5},{7,7},{8,8},{9,10},{10,9... | collective-permute-start | bytes 786440 | tf_op jit(solution)/shard_map/ppermute | solution.py:298
  81.5 9.0 %collective-permute-start.18 = (bf16[512,256]{1,0:T(8,128)(2,1)S(1)}, bf16[512,256]{1,0:T(8,128)(2,1)S(1)}, u32[]{:S(2)}, u32[]{:S(2)}) collective-permute-start(bf16[512,256]{1,0:T(8,128)(2,1)S(1)} %get-tuple-element.86), channel_id=1, source_target_pairs={{0,2},{1,0},{2,3},{3,1},{4,6},{5,4},{6,7},{7,5},{8,10},{9,8},{10,1... | collective-permute-start | bytes 786440 | tf_op jit(solution)/shard_map/ppermute | solution.py:299
  87.9 10.4 %collective-permute-start.21 = (bf16[512,256]{1,0:T(8,128)(2,1)S(1)}, bf16[512,256]{1,0:T(8,128)(2,1)S(1)}, u32[]{:S(2)}, u32[]{:S(2)}) collective-permute-start(bf16[512,256]{1,0:T(8,128)(2,1)S(1)} %get-tuple-element.89), channel_id=1, source_target_pairs={{0,0},{1,2},{2,1},{3,3},{4,4},{5,6},{6,5},{7,7},{8,8},{9,10},{10,9... | collective-permute-start | bytes 786440 | tf_op jit(solution)/shard_map/ppermute | solution.py:298
  90.4 7.9 %collective-permute-start.22 = (bf16[512,256]{1,0:T(8,128)(2,1)S(1)}, bf16[512,256]{1,0:T(8,128)(2,1)S(1)}, u32[]{:S(2)}, u32[]{:S(2)}) collective-permute-start(bf16[512,256]{1,0:T(8,128)(2,1)S(1)} %get-tuple-element.90), channel_id=1, source_target_pairs={{0,2},{1,0},{2,3},{3,1},{4,6},{5,4},{6,7},{7,5},{8,10},{9,8},{10,1... | collective-permute-start | bytes 786440 | tf_op jit(solution)/shard_map/ppermute | solution.py:299

commit v13 on v12

--- a/solution.py
+++ b/solution.py
@@ -154,7 +154,7 @@
 
 
 def layer_kernel(
-    layer, graph, slots, last, core_ref, idx_ref, own, sib, rim, bias, near_w, far_w, ws_hbm, wd_hbm, w2_hbm, *refs
+    layer, place, slots, last, core_ref, idx_ref, own, sib, rim, bias, near_w, far_w, ws_hbm, wd_hbm, w2_hbm, *refs
 ):
     outs, refs = (refs[:2], refs[2:]) if last else (refs[:1], refs[1:])
     ws, wd, w2, ws_x, wd_x, w2_x, proj, near, summed, sems = refs
@@ -170,7 +170,7 @@
     window = 3 * rows
     proj[0:8, :] = jnp.full((8, LANES), DEAD, jnp.float32)
     proj[4 * window + 4:4 * window + 16, :] = jnp.full((12, LANES), DEAD, jnp.float32)
-    pack = graph * (3 * share + 16)
+    pack = place * (3 * share + 16)
     here, there = pl.multiple_of(core * share, 16), pl.multiple_of((1 - core) * share, 16)
     for spot, piece in ((here, near_w), (there, far_w)):
         ws_x[pl.ds(spot, share), :] = piece[pack:pack + share, :]
@@ -239,7 +239,7 @@
             outs[1][...] = result[:, :share]
 
 
-def run_layer(layer, graph, slots, last, core, idx, own, sib, rim, ws, wd, w2, bias, near_w, far_w):
+def run_layer(layer, place, slots, last, core, idx, own, sib, rim, ws, wd, w2, bias, near_w, far_w):
     rows, width = own.shape
     share = width // 2
     chunks = width // LANES
@@ -252,7 +252,7 @@
     else:
         out_shape, out_specs = jax.ShapeDtypeStruct((rows, width), bf16), vmem
     return pl.pallas_call(
-        functools.partial(layer_kernel, layer, graph, slots, last),
+        functools.partial(layer_kernel, layer, place, slots, last),
         out_shape=out_shape,
         in_specs=[smem] * 2 + [vmem] * 6 + [pl.BlockSpec(memory_space=pl.ANY)] * 3,
         out_specs=out_specs,
@@ -319,14 +319,15 @@
     return lax.ppermute(own, ("mesh", "batch"), pairs)
 
 
-def pack_kernel(layers, core_ref, g_bias, r_bias, *refs):
+def pack_kernel(plan, core_ref, g_bias, r_bias, *refs):
     weights, outs, sems = (refs[:3], refs[3:6]), refs[6:-1], refs[-1]
     share = g_bias.shape[1]
     here = pl.multiple_of(core_ref[0] * share, share)
     copies = []
-    for layer, out in zip(layers, outs):
-        for graph, (ws, wd, w2) in enumerate(weights):
-            base = graph * (3 * share + 16)
+    for members, out in zip(plan, outs):
+        for place, (graph, layer) in enumerate(members):
+            ws, wd, w2 = weights[graph]
+            base = place * (3 * share + 16)
             sources = (
                 ws.at[layer, pl.ds(here, share), :], wd.at[layer, pl.ds(here, share), :], w2.at[layer, :, pl.ds(here, share)]
             )
@@ -334,24 +335,26 @@
                 spot = base + i * share
                 copies.append(pltpu.make_async_copy(source, out.at[spot:spot + share, :], sems.at[len(copies)]))
                 copies[-1].start()
-    for layer, out in zip(layers, outs):
-        for graph, bias in enumerate((g_bias, r_bias)):
-            base = graph * (3 * share + 16) + 3 * share
-            out[base:base + 16, :] = jnp.broadcast_to(bias[layer:layer + 1, :], (16, share))
+    for members, out in zip(plan, outs):
+        for place, (graph, layer) in enumerate(members):
+            base = place * (3 * share + 16) + 3 * share
+            bias = (g_bias, r_bias)[graph][layer:layer + 1, :]
+            out[base:base + 16, :] = jnp.broadcast_to(bias, (16, share))
     for copy in copies:
         copy.wait()
 
 
-def pack_weights(layers, core, g_weights, g_bias, r_weights, r_bias):
+def pack_weights(plan, core, g_weights, g_bias, r_weights, r_bias):
     share = g_bias.shape[1]
     vmem = pl.BlockSpec(memory_space=pltpu.VMEM)
     hbm = pl.BlockSpec(memory_space=pltpu.HBM)
+    sizes = [len(members) for members in plan]
     return pl.pallas_call(
-        functools.partial(pack_kernel, layers),
-        out_shape=(jax.ShapeDtypeStruct((2 * (3 * share + 16), share), jnp.bfloat16),) * len(layers),
+        functools.partial(pack_kernel, plan),
+        out_shape=tuple(jax.ShapeDtypeStruct((n * (3 * share + 16), share), jnp.bfloat16) for n in sizes),
         in_specs=[pl.BlockSpec(memory_space=pltpu.SMEM)] + [vmem] * 2 + [hbm] * 6,
-        out_specs=(vmem,) * len(layers),
-        scratch_shapes=[pltpu.SemaphoreType.DMA((6 * len(layers),))],
+        out_specs=(vmem,) * len(sizes),
+        scratch_shapes=[pltpu.SemaphoreType.DMA((3 * sum(sizes),))],
         compiler_params=pltpu.CompilerParams(vmem_limit_bytes=60 << 20),
         cost_estimate=pl.CostEstimate(flops=256 * share**3, bytes_accessed=1, transcendentals=0),
         name="pack_weights",
@@ -379,7 +382,7 @@
     same = lax.dynamic_slice(g_own, (part * half, 0), (half, g_own.shape[1]))
     other = lax.dynamic_slice(g_own, ((1 - part) * half, 0), (half, g_own.shape[1]))
     g_a, g_b = spread_rows(same, other)
-    packs = list(pack_weights((0,), core1, g_weights, g_b1, r_weights, r_b1))
+    packs = list(pack_weights((((0, 0), (1, 0)),), core1, g_weights, g_b1, r_weights, r_b1))
     near_w = [swap(packs[0], "mp")]
     bnd = jnp.stack([bnd_src, bnd_part[:, 0], bnd_node])
     bnd, packs[0], same, other = after((bnd, packs[0], same, other))
@@ -389,7 +392,8 @@
         landed.append(lax.ppermute(pieces[k], "mesh", [(i, (i + k) % parts) for i in range(parts)]))
     landed[0], core1, g_a, g_b = after((landed[0], core1, g_a, g_b))
     idx = edge_offsets(jnp.stack([g_nbr, r_nbr]), jnp.stack([g_count, r_count]), core)
-    packs += pack_weights(tuple(range(1, layers)), core1, g_weights, g_b1, r_weights, r_b1)
+    rest = tuple(((graph, layer),) for layer in range(1, layers) for graph in (0, 1))
+    packs += pack_weights(rest, core1, g_weights, g_b1, r_weights, r_b1)
     g_idx, r_idx = idx[0], idx[1]
     g_a, g_b, g_idx, r_idx, packs[1:], near_w[0], *landed = after(
         (g_a, g_b, g_idx, r_idx, packs[1:], near_w[0], *landed)
@@ -398,23 +402,36 @@
     g_sib, g_rim = swap(planet, "batch"), rims(planet, True)
     *r_pair, packs[1:] = after((*add_force(part.reshape(1), r_own, landed, cap), packs[1:]))
     r_a, r_b = spread_rows(*r_pair)
-    near_w += [swap(pack, "mp") for pack in packs[1:]]
+    near_w.append(swap(packs[1], "mp"))
     r_a, r_b, g_sib, g_rim = after((r_a, r_b, g_sib, g_rim))
     regional, g_idx = after((ordered(core, r_a, r_b, 1), g_idx))
     r_sib, r_rim = swap(regional, "batch"), rims(regional, False)
+    far_w = [swap(near_w[0], "batch")]
     for layer in range(layers):
         last = layer == layers - 1
-        far_w = swap(near_w[layer], "batch")
+        i = max(0, 2 * layer - 1)
+        if layer:
+            far_w.append(swap(near_w[i], "batch"))
         planet = run_layer(
-            layer, 0, slots, last, core1, g_idx, planet, g_sib, g_rim, g_ws, g_wd, g_w2, g_b1, near_w[layer], far_w
+            layer, 0, slots, last, core1, g_idx, planet, g_sib, g_rim, g_ws, g_wd, g_w2, g_b1, near_w[i], far_w[i]
         )
         *planet, core1 = after((*(planet if last else (planet,)), core1))
         if not last:
             planet = planet[0]
             g_sib, g_rim = swap(planet, "batch"), rims(planet, True)
-            core1, near_w[layer + 1] = after((core1, near_w[layer + 1]))
+        if layer:
+            i += 1
+            near_w[i], core1 = after((near_w[i], core1))
+            far_w.append(swap(near_w[i], "batch"))
+        for j in range(i + 1, min(i + 3, len(packs))):
+            if j == len(near_w):
+                packs[j], near_w[j - 1] = after((packs[j], near_w[j - 1]))
+                near_w.append(swap(packs[j], "mp"))
+            if j == i + 1:
+                core1, near_w[j] = after((core1, near_w[j]))
         regional = run_layer(
-            layer, 1, slots, last, core1, r_idx, regional, r_sib, r_rim, r_ws, r_wd, r_w2, r_b1, near_w[layer], far_w
+            layer, 1 - min(layer, 1), slots, last, core1, r_idx, regional, r_sib, r_rim, r_ws, r_wd, r_w2, r_b1,
+            near_w[i], far_w[i],
         )
         if not last:
             regional, core1 = after((regional, core1))

time: 99.8 us -> 99.9 us (level)
  starting transfers between devices: 32.6 us -> 36.8 us
  waiting for transfers between devices: 27.4 us -> 23.4 us
    ppermute x8 -> x10, waiting for transfers between devices: 8.84 us -> 3.79 us  [swap(): return lax.ppermute(values, axis, [(0, 1), (1, 0)])]
    ppermute x8 -> x10, starting transfers between devices: 4.95 us -> 9.27 us  [swap(): return lax.ppermute(values, axis, [(0, 1), (1, 0)])]
  transfers between devices with their start and end apart: 23 -> 25, of which waited for: 7 -> 6; matrix products, arithmetic and copies ran while one was open for 1% -> 1% of each run, Pallas kernels for 34% -> 34%
where the time goes in v13:
time: 99.9 us; the launch traced here: 99.5 us
  starting transfers between devices  36.8 us (37%)
  Pallas kernels  33.9 us (34%)
  waiting for transfers between devices  23.4 us (23%)
  other arithmetic  2.41 us (2%)
  local copies, waits for them, and re-layouts  1.88 us (2%)
  between operations  1.11 us (1%)
    pallas_call x4, Pallas kernels, run_layer(): pl.pallas_call(functools.partial(layer_kernel, layer, place, slots, last)...  25.2 us
    ppermute x2, starting transfers between devices, spread_rows(): a = lax.ppermute(same, ('mp', 'batch'), [(0, 0), (1, 2), (2, 1), (3, 3)])  9.45 us
    ppermute x10, starting transfers between devices, swap(): return lax.ppermute(values, axis, [(0, 1), (1, 0)])  9.27 us
    ppermute x4, starting transfers between devices, rims(): return lax.ppermute(own, ('mesh', 'batch'), pairs)  7.68 us
    ppermute x2, waiting for transfers between devices, gather_rows(): same = lax.ppermute(a, ('mp', 'batch'), [(0, 0), (1, 2), (2, 1), (3, 3)])  6.97 us
    pallas_call x2, Pallas kernels, pack_weights(): pl.pallas_call(functools.partial(pack_kernel, plan), out_shape=tuple((jax...  5.74 us
    ppermute x3, waiting for transfers between devices, by_rows(): lax.ppermute(pieces[k], 'mesh', [(i, (i + k) % parts) for i in range(part...  5.67 us
    ppermute x2, starting transfers between devices, gather_rows(): same = lax.ppermute(a, ('mp', 'batch'), [(0, 0), (1, 2), (2, 1), (3, 3)])  5.55 us
  transfers between devices with their start and end apart: 25, of which 6 were waited for; matrix products, arithmetic and copies ran while one was open for 1% of the time, Pallas kernels for 34%

profile of v13, /device:TPU:1, one launch (start us, length us, event | category | flops | bytes accessed | tf_op | source)
XLA Modules:
  0.0 99.5 jit_solution(12301065717607815147)
XLA Ops:
  0.6 1.1 %dynamic-slice_bitcast_fusion = (bf16[512,256]{1,0:T(8,128)(2,1)S(1)}, bf16[512,256]{1,0:T(8,128)(2,1)S(1)}) fusion(bf16[1,1024,256]{2,1,0:T(8,128)(2,1)} %param.17, s32[]{:T(128)S(6)} %select_n.78, s32[]{:T(128)S(6)} %select_n.77), kind=kLoop, calls=%fused_computation.4 | loop fusion | bytes 1048584 | tf_op jit(solution)/shard_map/dynamic_slice | solution.py:383
  1.7 4.5 %collective-permute-start = (bf16[512,256]{1,0:T(8,128)(2,1)S(1)}, bf16[512,256]{1,0:T(8,128)(2,1)S(1)}, u32[]{:S(2)}, u32[]{:S(2)}) collective-permute-start(bf16[512,256]{1,0:T(8,128)(2,1)S(1)} %get-tuple-element.111), channel_id=1, source_target_pairs={{0,0},{1,2},{2,1},{3,3},{4,4},{5,6},{6,5},{7,7},{8,8},{9,10},{10,9... | collective-permute-start | bytes 786440 | tf_op jit(solution)/shard_map/ppermute | solution.py:292
  6.2 0.0 collective-permute-start.1
  6.3 0.0 copy-start.16
  6.3 0.0 copy-start
  6.3 2.9 %pack_weights.2 = bf16[1568,256]{1,0:T(8,128)(2,1)} custom-call(s32[1]{0:T(128)} %bitcast.4.core_ref, bf16[2,256]{1,0:T(2,128)(2,1)} %bias.6, bf16[2,256]{1,0:T(2,128)(2,1)} %bias.7, bf16[2,512,256]{2,1,0:T(8,128)(2,1)} %ws_hbm.6, bf16[2,512,256]{2,1,0:T(8,128)(2,1)} %wd_hbm.6, bf16[2,256,512]{2,1,0:T(8,128)(2,1)} %w2_hbm.6, bf16[2,512,256]{2,1,0:T(8,128)(2,1)} %ws_hbm.7, ...), custom_call_target="tpu_custom_call" | custom-call | flops 4294967296 | bytes 1 | tf_op jit(solution)/shard_map/pack_weights/pallas_call | solution.py:352
  9.2 0.2 collective-permute-start.2
  9.4 0.7 copy-done.15
  10.0 0.0 copy-done.14
  10.1 2.3 %pick_rows.1 = (bf16[272,256]{1,0:T(8,128)(2,1)S(1)}, bf16[272,256]{1,0:T(8,128)(2,1)S(1)}, bf16[272,256]{1,0:T(8,128)(2,1)S(1)}, bf16[272,256]{1,0:T(8,128)(2,1)S(1)}) custom-call(s32[1]{0:T(128)} %bitcast.me_ref, s32[3,512]{1,0:T(4,128)S(1)} %pad_add_fusion.bnd_ref, bf16[1024,256]{1,0:T(8,128)(2,1)S(1)} %bitcast.33), custom_call_target="tpu_custom_call" | custom-call | flops 8589934592 | bytes 1 | tf_op jit(solution)/shard_map/pick_rows/pallas_call | solution.py:115
  12.4 1.3 %collective-permute-start.3 = (bf16[272,256]{1,0:T(8,128)(2,1)S(1)}, bf16[272,256]{1,0:T(8,128)(2,1)S(1)}, u32[]{:S(2)}, u32[]{:S(2)}) collective-permute-start(bf16[272,256]{1,0:T(8,128)(2,1)S(1)} %get-tuple-element.64), channel_id=1, source_target_pairs={{0,4},{4,8},{8,12},{12,0},{1,5},{5,9},{9,13},{13,1},{2,6},{6,10},{... | collective-permute-start | bytes 417800 | tf_op jit(solution)/shard_map/ppermute | solution.py:392
  13.7 2.3 %collective-permute-start.4 = (bf16[272,256]{1,0:T(8,128)(2,1)S(1)}, bf16[272,256]{1,0:T(8,128)(2,1)S(1)}, u32[]{:S(2)}, u32[]{:S(2)}) collective-permute-start(bf16[272,256]{1,0:T(8,128)(2,1)S(1)} %get-tuple-element.65), channel_id=1, source_target_pairs={{0,8},{4,12},{8,0},{12,4},{1,9},{5,13},{9,1},{13,5},{2,10},{6,14},... | collective-permute-start | bytes 417800 | tf_op jit(solution)/shard_map/ppermute | solution.py:392
  16.1 0.1 fusion.5
  16.2 1.1 %collective-permute-start.5 = (bf16[272,256]{1,0:T(8,128)(2,1)S(1)}, bf16[272,256]{1,0:T(8,128)(2,1)S(1)}, u32[]{:S(2)}, u32[]{:S(2)}) collective-permute-start(bf16[272,256]{1,0:T(8,128)(2,1)S(1)} %get-tuple-element.66), channel_id=1, source_target_pairs={{0,12},{4,0},{8,4},{12,8},{1,13},{5,1},{9,5},{13,9},{2,14},{6,2},{... | collective-permute-start | bytes 417800 | tf_op jit(solution)/shard_map/ppermute | solution.py:392
  17.4 2.8 %pack_weights.3 = (bf16[784,256]{1,0:T(8,128)(2,1)}, bf16[784,256]{1,0:T(8,128)(2,1)}) custom-call(s32[1]{0:T(128)} %bitcast.4.core_ref, bf16[2,256]{1,0:T(2,128)(2,1)} %bias.6, bf16[2,256]{1,0:T(2,128)(2,1)} %bias.7, bf16[2,512,256]{2,1,0:T(8,128)(2,1)} %ws_hbm.6, bf16[2,512,256]{2,1,0:T(8,128)(2,1)} %wd_hbm.6, bf16[2,256,512]{2,1,0:T(8,128)(2,1)} %w2_hbm.6, ...), custom_call_target="tpu_custom_call" | custom-call | flops 4294967296 | bytes 1 | tf_op jit(solution)/shard_map/pack_weights/pallas_call | solution.py:352
  20.2 5.7 %collective-permute-done.4.refs_2_ = bf16[272,256]{1,0:T(8,128)(2,1)S(1)} collective-permute-done((bf16[272,256]{1,0:T(8,128)(2,1)S(1)}, bf16[272,256]{1,0:T(8,128)(2,1)S(1)}, u32[]{:S(2)}, u32[]{:S(2)}) %collective-permute-start.4) | collective-permute-done | bytes 139296 | tf_op jit(solution)/shard_map/ppermute | solution.py:392
  25.9 3.8 %collective-permute-done.2.near_w = bf16[1568,256]{1,0:T(8,128)(2,1)S(1)} collective-permute-done((bf16[1568,256]{1,0:T(8,128)(2,1)}, bf16[1568,256]{1,0:T(8,128)(2,1)S(1)}, u32[]{:S(2)}, u32[]{:S(2)}) %collective-permute-start.2) | collective-permute-done | bytes 802848 | tf_op jit(solution)/shard_map/ppermute | solution.py:308
  29.6 1.3 %collective-permute-start.10 = (bf16[1568,256]{1,0:T(8,128)(2,1)S(1)}, bf16[1568,256]{1,0:T(8,128)(2,1)S(1)}, u32[]{:S(2)}, u32[]{:S(2)}) collective-permute-start(bf16[1568,256]{1,0:T(8,128)(2,1)S(1)} %collective-permute-done.2.near_w), channel_id=1, source_target_pairs={{0,1},{1,0},{2,3},{3,2},{4,5},{5,4},{6,7},{7,6},{8,9},{9,8},{10,11... | collective-permute-start | bytes 2408456 | tf_op jit(solution)/shard_map/ppermute | solution.py:308
  31.0 0.1 maximum_select_fusion.own
  31.1 0.1 collective-permute-start.8
  31.2 1.7 %collective-permute-start.9 = (bf16[512,512]{1,0:T(8,128)(2,1)S(1)}, bf16[512,512]{1,0:T(8,128)(2,1)S(1)}, u32[]{:S(2)}, u32[]{:S(2)}) collective-permute-start(bf16[512,512]{1,0:T(8,128)(2,1)S(1)} %maximum_select_fusion.own), channel_id=1, source_target_pairs={{1,4},{0,13},{5,8},{4,1},{9,12},{8,5},{13,0},{12,9},{3,6},{2,15},{... | collective-permute-start | bytes 1572872 | tf_op jit(solution)/shard_map/ppermute | solution.py:319
  32.9 0.7 add_force.1
  33.6 4.9 %collective-permute-start.6 = (bf16[512,256]{1,0:T(8,128)(2,1)S(1)}, bf16[512,256]{1,0:T(8,128)(2,1)S(1)}, u32[]{:S(2)}, u32[]{:S(2)}) collective-permute-start(bf16[512,256]{1,0:T(8,128)(2,1)S(1)} %get-tuple-element.75), channel_id=1, source_target_pairs={{0,0},{1,2},{2,1},{3,3},{4,4},{5,6},{6,5},{7,7},{8,8},{9,10},{10,9... | collective-permute-start | bytes 786440 | tf_op jit(solution)/shard_map/ppermute | solution.py:292
  38.6 0.0 collective-permute-start.7
  38.6 4.3 %collective-permute-done.6 = bf16[512,256]{1,0:T(8,128)(2,1)S(1)} collective-permute-done((bf16[512,256]{1,0:T(8,128)(2,1)S(1)}, bf16[512,256]{1,0:T(8,128)(2,1)S(1)}, u32[]{:S(2)}, u32[]{:S(2)}) %collective-permute-start.6) | collective-permute-done | bytes 262176 | tf_op jit(solution)/shard_map/ppermute | solution.py:292
  42.9 1.8 %collective-permute-done.7 = bf16[512,256]{1,0:T(8,128)(2,1)S(1)} collective-permute-done((bf16[512,256]{1,0:T(8,128)(2,1)S(1)}, bf16[512,256]{1,0:T(8,128)(2,1)S(1)}, u32[]{:S(2)}, u32[]{:S(2)}) %collective-permute-start.7) | collective-permute-done | bytes 262176 | tf_op jit(solution)/shard_map/ppermute | solution.py:293
  44.7 0.1 maximum_select_fusion.1.own
  44.9 2.7 %collective-permute-start.12 = (bf16[512,512]{1,0:T(8,128)(2,1)S(1)}, bf16[512,512]{1,0:T(8,128)(2,1)S(1)}, u32[]{:S(2)}, u32[]{:S(2)}) collective-permute-start(bf16[512,512]{1,0:T(8,128)(2,1)S(1)} %maximum_select_fusion.1.own), channel_id=1, source_target_pairs={{0,1},{1,0},{2,3},{3,2},{4,5},{5,4},{6,7},{7,6},{8,9},{9,8},{10,11... | collective-permute-start | bytes 1572872 | tf_op jit(solution)/shard_map/ppermute | solution.py:308
  47.5 1.9 %collective-permute-start.13 = (bf16[512,512]{1,0:T(8,128)(2,1)S(1)}, bf16[512,512]{1,0:T(8,128)(2,1)S(1)}, u32[]{:S(2)}, u32[]{:S(2)}) collective-permute-start(bf16[512,512]{1,0:T(8,128)(2,1)S(1)} %maximum_select_fusion.1.own), channel_id=1, source_target_pairs={{1,4},{5,8},{4,1},{9,12},{8,5},{12,9},{3,6},{7,10},{6,3},{11,14},{... | collective-permute-start | bytes 1572872 | tf_op jit(solution)/shard_map/ppermute | solution.py:319
  49.5 6.3 %graph_layer.4.own = bf16[512,512]{1,0:T(8,128)(2,1)S(1)} custom-call(s32[1]{0:T(128)} %bitcast.4.core_ref, s32[4096]{0:T(1024)S(1)} %bitcast.37, bf16[512,512]{1,0:T(8,128)(2,1)S(1)} %maximum_select_fusion.own, bf16[512,512]{1,0:T(8,128)(2,1)S(1)} %collective-permute-done.8.sib, bf16[512,512]{1,0:T(8,128)(2,1)S(1)} %collective-permute-done.9.rim, ...), custom_call_target="tpu_custom_call" | custom-call | flops 8589934592 | bytes 2621440 | tf_op jit(solution)/shard_map/graph_layer/pallas_call | solution.py:254
  55.8 0.1 collective-permute-start.14
  55.9 1.8 %collective-permute-start.15 = (bf16[512,512]{1,0:T(8,128)(2,1)S(1)}, bf16[512,512]{1,0:T(8,128)(2,1)S(1)}, u32[]{:S(2)}, u32[]{:S(2)}) collective-permute-start(bf16[512,512]{1,0:T(8,128)(2,1)S(1)} %graph_layer.4.own), channel_id=1, source_target_pairs={{1,4},{0,13},{5,8},{4,1},{9,12},{8,5},{13,0},{12,9},{3,6},{2,15},{... | collective-permute-start | bytes 1572872 | tf_op jit(solution)/shard_map/ppermute | solution.py:319
  57.7 1.1 %collective-permute-start.16 = (bf16[784,256]{1,0:T(8,128)(2,1)S(1)}, bf16[784,256]{1,0:T(8,128)(2,1)S(1)}, u32[]{:S(2)}, u32[]{:S(2)}) collective-permute-start(bf16[784,256]{1,0:T(8,128)(2,1)S(1)} %collective-permute-done.11.near_w), channel_id=1, source_target_pairs={{0,1},{1,0},{2,3},{3,2},{4,5},{5,4},{6,7},{7,6},{8,9},{9,8},{10,11... | collective-permute-start | bytes 1204232 | tf_op jit(solution)/shard_map/ppermute | solution.py:308
  58.7 0.6 collective-permute-start.19
  59.3 6.3 %graph_layer.5.own = bf16[512,512]{1,0:T(8,128)(2,1)S(1)} custom-call(s32[1]{0:T(128)} %bitcast.4.core_ref, s32[4096]{0:T(1024)S(1)} %bitcast.35, bf16[512,512]{1,0:T(8,128)(2,1)S(1)} %maximum_select_fusion.1.own, bf16[512,512]{1,0:T(8,128)(2,1)S(1)} %collective-permute-done.12.sib, bf16[512,512]{1,0:T(8,128)(2,1)S(1)} %collective-permute-done.13.rim, ...), custom_call_target="tpu_custom_call" | custom-call | flops 8589934592 | bytes 2621440 | tf_op jit(solution)/shard_map/graph_layer/pallas_call | solution.py:254
  65.6 0.4 collective-permute-start.20
  66.0 2.3 %collective-permute-start.21 = (bf16[512,512]{1,0:T(8,128)(2,1)S(1)}, bf16[512,512]{1,0:T(8,128)(2,1)S(1)}, u32[]{:S(2)}, u32[]{:S(2)}) collective-permute-start(bf16[512,512]{1,0:T(8,128)(2,1)S(1)} %graph_layer.5.own), channel_id=1, source_target_pairs={{1,4},{5,8},{4,1},{9,12},{8,5},{12,9},{3,6},{7,10},{6,3},{11,14},{... | collective-permute-start | bytes 1572872 | tf_op jit(solution)/shard_map/ppermute | solution.py:319
  68.3 0.9 collective-permute-done.15.rim
  69.2 6.3 %graph_layer.6 = (bf16[512,256]{1,0:T(8,128)(2,1)S(1)}, bf16[512,256]{1,0:T(8,128)(2,1)S(1)}) custom-call(s32[1]{0:T(128)} %bitcast.4.core_ref, s32[4096]{0:T(1024)S(1)} %bitcast.38, bf16[512,512]{1,0:T(8,128)(2,1)S(1)} %graph_layer.4.own, bf16[512,512]{1,0:T(8,128)(2,1)S(1)} %collective-permute-done.14.sib, ...), custom_call_target="tpu_custom_call" | custom-call | flops 8589934592 | bytes 2621440 | tf_op jit(solution)/shard_map/graph_layer/pallas_call | solution.py:254
  75.6 2.9 %collective-permute-start.22 = (bf16[784,256]{1,0:T(8,128)(2,1)S(1)}, bf16[784,256]{1,0:T(8,128)(2,1)S(1)}, u32[]{:S(2)}, u32[]{:S(2)}) collective-permute-start(bf16[784,256]{1,0:T(8,128)(2,1)S(1)} %collective-permute-done.19.near_w), channel_id=1, source_target_pairs={{0,1},{1,0},{2,3},{3,2},{4,5},{5,4},{6,7},{7,6},{8,9},{9,8},{10,11... | collective-permute-start | bytes 1204232 | tf_op jit(solution)/shard_map/ppermute | solution.py:308
  78.5 0.0 collective-permute-start.18
  78.5 3.6 %collective-permute-start.17 = (bf16[512,256]{1,0:T(8,128)(2,1)S(1)}, bf16[512,256]{1,0:T(8,128)(2,1)S(1)}, u32[]{:S(2)}, u32[]{:S(2)}) collective-permute-start(bf16[512,256]{1,0:T(8,128)(2,1)S(1)} %get-tuple-element.98), channel_id=1, source_target_pairs={{0,0},{1,2},{2,1},{3,3},{4,4},{5,6},{6,5},{7,7},{8,8},{9,10},{10,9... | collective-permute-start | bytes 786440 | tf_op jit(solution)/shard_map/ppermute | solution.py:298
  82.2 6.3 %graph_layer.7 = (bf16[512,256]{1,0:T(8,128)(2,1)S(1)}, bf16[512,256]{1,0:T(8,128)(2,1)S(1)}) custom-call(s32[1]{0:T(128)} %bitcast.4.core_ref, s32[4096]{0:T(1024)S(1)} %bitcast.36, bf16[512,512]{1,0:T(8,128)(2,1)S(1)} %graph_layer.5.own, bf16[512,512]{1,0:T(8,128)(2,1)S(1)} %collective-permute-done.20.sib, ...), custom_call_target="tpu_custom_call" | custom-call | flops 8589934592 | bytes 2621440 | tf_op jit(solution)/shard_map/graph_layer/pallas_call | solution.py:254
  88.5 1.9 %collective-permute-start.23 = (bf16[512,256]{1,0:T(8,128)(2,1)S(1)}, bf16[512,256]{1,0:T(8,128)(2,1)S(1)}, u32[]{:S(2)}, u32[]{:S(2)}) collective-permute-start(bf16[512,256]{1,0:T(8,128)(2,1)S(1)} %get-tuple-element.105), channel_id=1, source_target_pairs={{0,0},{1,2},{2,1},{3,3},{4,4},{5,6},{6,5},{7,7},{8,8},{9,10},{10,9... | collective-permute-start | bytes 786440 | tf_op jit(solution)/shard_map/ppermute | solution.py:298
  90.5 0.0 collective-permute-start.24
  90.5 1.0 %maximum_select_fusion.2 = bf16[1024,256]{1,0:T(8,128)(2,1)} fusion(bf16[512,256]{1,0:T(8,128)(2,1)S(1)} %collective-permute-done.18, bf16[512,256]{1,0:T(8,128)(2,1)S(1)} %collective-permute-done.17, pred[]{:T(512)S(6)} %eq.6), kind=kLoop, calls=%fused_computation.2 | loop fusion | flops 2359296 | bytes 1048577 | tf_op jit(solution)/shard_map/jit(_where)/select_n | solution.py:304
  91.5 7.0 %collective-permute-done.23 = bf16[512,256]{1,0:T(8,128)(2,1)S(1)} collective-permute-done((bf16[512,256]{1,0:T(8,128)(2,1)S(1)}, bf16[512,256]{1,0:T(8,128)(2,1)S(1)}, u32[]{:S(2)}, u32[]{:S(2)}) %collective-permute-start.23) | collective-permute-done | bytes 262176 | tf_op jit(solution)/shard_map/ppermute | solution.py:298
  98.5 1.0 %maximum_select_fusion.3 = bf16[1,1024,256]{2,1,0:T(8,128)(2,1)} fusion(bf16[1,512,256]{2,1,0:T(8,128)(2,1)S(1)} %bitcast.41, bf16[1,512,256]{2,1,0:T(8,128)(2,1)S(1)} %bitcast.40, pred[]{:T(512)S(6)} %eq.6), kind=kLoop, calls=%fused_computation.3 | loop fusion | flops 2359296 | bytes 1048577 | tf_op jit(solution)/shard_map/jit(_where)/select_n | solution.py:304
  (60 shorter events, 0.2 us)
Async XLA Ops:
  1.7 14.5 %collective-permute-start = (bf16[512,256]{1,0:T(8,128)(2,1)S(1)}, bf16[512,256]{1,0:T(8,128)(2,1)S(1)}, u32[]{:S(2)}, u32[]{:S(2)}) collective-permute-start(bf16[512,256]{1,0:T(8,128)(2,1)S(1)} %get-tuple-element.111), channel_id=1, source_target_pairs={{0,0},{1,2},{2,1},{3,3},{4,4},{5,6},{6,5},{7,7},{8,8},{9,10},{10,9... | collective-permute-start | bytes 786440 | tf_op jit(solution)/shard_map/ppermute | solution.py:292
  6.2 11.1 %collective-permute-start.1 = (bf16[512,256]{1,0:T(8,128)(2,1)S(1)}, bf16[512,256]{1,0:T(8,128)(2,1)S(1)}, u32[]{:S(2)}, u32[]{:S(2)}) collective-permute-start(bf16[512,256]{1,0:T(8,128)(2,1)S(1)} %get-tuple-element.110), channel_id=1, source_target_pairs={{0,1},{1,3},{2,0},{3,2},{4,5},{5,7},{6,4},{7,6},{8,9},{9,11},{10,8... | collective-permute-start | bytes 786440 | tf_op jit(solution)/shard_map/ppermute | solution.py:293
  6.3 3.1 %copy-start.16 = (s32[512]{0:T(512)S(1)}, s32[512]{0:T(512)}, u32[]{:S(2)}) copy-start(s32[512]{0:T(512)} %param.23) | copy-start | bytes 6148
  6.3 3.8 %copy-start = (bf16[1,1024,256]{2,1,0:T(8,128)(2,1)S(1)}, bf16[1,1024,256]{2,1,0:T(8,128)(2,1)}, u32[]{:S(2)}) copy-start(bf16[1,1024,256]{2,1,0:T(8,128)(2,1)} %param.17) | copy-start | bytes 1572868
  9.2 20.4 %collective-permute-start.2 = (bf16[1568,256]{1,0:T(8,128)(2,1)}, bf16[1568,256]{1,0:T(8,128)(2,1)S(1)}, u32[]{:S(2)}, u32[]{:S(2)}) collective-permute-start(bf16[1568,256]{1,0:T(8,128)(2,1)} %pack_weights.2), channel_id=1, source_target_pairs={{0,2},{2,0},{1,3},{3,1},{4,6},{6,4},{5,7},{7,5},{8,10},{10,8},{9,1... | collective-permute-start | bytes 2408456 | tf_op jit(solution)/shard_map/ppermute | solution.py:308
  9.4 0.7 copy-start.15
  9.4 0.7 copy-start.14
  10.1 6.0 %copy-start.12 = (s32[1024]{0:T(1024)S(1)}, s32[1024]{0:T(1024)}, u32[]{:S(2)}) copy-start(s32[1024]{0:T(1024)} %param.20) | copy-start | bytes 12292
  10.1 6.0 %copy-start.13 = (s32[1024]{0:T(1024)S(1)}, s32[1024]{0:T(1024)}, u32[]{:S(2)}) copy-start(s32[1024]{0:T(1024)} %param.22) | copy-start | bytes 12292
  10.1 6.0 %copy-start.11 = (s32[1024,8]{0,1:T(8,128)S(1)}, s32[1024,8]{0,1:T(8,128)}, u32[]{:S(2)}) copy-start(s32[1024,8]{0,1:T(8,128)} %param.19) | copy-start | bytes 98308
  12.4 3.8 %copy-start.10 = (s32[1024,8]{0,1:T(8,128)S(1)}, s32[1024,8]{0,1:T(8,128)}, u32[]{:S(2)}) copy-start(s32[1024,8]{0,1:T(8,128)} %param.21) | copy-start | bytes 98308
  12.4 7.8 %collective-permute-start.3 = (bf16[272,256]{1,0:T(8,128)(2,1)S(1)}, bf16[272,256]{1,0:T(8,128)(2,1)S(1)}, u32[]{:S(2)}, u32[]{:S(2)}) collective-permute-start(bf16[272,256]{1,0:T(8,128)(2,1)S(1)} %get-tuple-element.64), channel_id=1, source_target_pairs={{0,4},{4,8},{8,12},{12,0},{1,5},{5,9},{9,13},{13,1},{2,6},{6,10},{... | collective-permute-start | bytes 417800 | tf_op jit(solution)/shard_map/ppermute | solution.py:392
  13.7 12.1 %collective-permute-start.4 = (bf16[272,256]{1,0:T(8,128)(2,1)S(1)}, bf16[272,256]{1,0:T(8,128)(2,1)S(1)}, u32[]{:S(2)}, u32[]{:S(2)}) collective-permute-start(bf16[272,256]{1,0:T(8,128)(2,1)S(1)} %get-tuple-element.65), channel_id=1, source_target_pairs={{0,8},{4,12},{8,0},{12,4},{1,9},{5,13},{9,1},{13,5},{2,10},{6,14},... | collective-permute-start | bytes 417800 | tf_op jit(solution)/shard_map/ppermute | solution.py:392
  16.2 9.6 %collective-permute-start.5 = (bf16[272,256]{1,0:T(8,128)(2,1)S(1)}, bf16[272,256]{1,0:T(8,128)(2,1)S(1)}, u32[]{:S(2)}, u32[]{:S(2)}) collective-permute-start(bf16[272,256]{1,0:T(8,128)(2,1)S(1)} %get-tuple-element.66), channel_id=1, source_target_pairs={{0,12},{4,0},{8,4},{12,8},{1,13},{5,1},{9,5},{13,9},{2,14},{6,2},{... | collective-permute-start | bytes 417800 | tf_op jit(solution)/shard_map/ppermute | solution.py:392
  29.6 3.2 %copy-start.1 = (bf16[1,1024,256]{2,1,0:T(8,128)(2,1)S(1)}, bf16[1,1024,256]{2,1,0:T(8,128)(2,1)}, u32[]{:S(2)}) copy-start(bf16[1,1024,256]{2,1,0:T(8,128)(2,1)} %param.18) | copy-start | bytes 1572868
  29.6 19.8 %collective-permute-start.10 = (bf16[1568,256]{1,0:T(8,128)(2,1)S(1)}, bf16[1568,256]{1,0:T(8,128)(2,1)S(1)}, u32[]{:S(2)}, u32[]{:S(2)}) collective-permute-start(bf16[1568,256]{1,0:T(8,128)(2,1)S(1)} %collective-permute-done.2.near_w), channel_id=1, source_target_pairs={{0,1},{1,0},{2,3},{3,2},{4,5},{5,4},{6,7},{7,6},{8,9},{9,8},{10,11... | collective-permute-start | bytes 2408456 | tf_op jit(solution)/shard_map/ppermute | solution.py:308
  31.1 13.6 %collective-permute-start.8 = (bf16[512,512]{1,0:T(8,128)(2,1)S(1)}, bf16[512,512]{1,0:T(8,128)(2,1)S(1)}, u32[]{:S(2)}, u32[]{:S(2)}) collective-permute-start(bf16[512,512]{1,0:T(8,128)(2,1)S(1)} %maximum_select_fusion.own), channel_id=1, source_target_pairs={{0,1},{1,0},{2,3},{3,2},{4,5},{5,4},{6,7},{7,6},{8,9},{9,8},{10,11... | collective-permute-start | bytes 1572872 | tf_op jit(solution)/shard_map/ppermute | solution.py:308
  31.2 13.5 %collective-permute-start.9 = (bf16[512,512]{1,0:T(8,128)(2,1)S(1)}, bf16[512,512]{1,0:T(8,128)(2,1)S(1)}, u32[]{:S(2)}, u32[]{:S(2)}) collective-permute-start(bf16[512,512]{1,0:T(8,128)(2,1)S(1)} %maximum_select_fusion.own), channel_id=1, source_target_pairs={{1,4},{0,13},{5,8},{4,1},{9,12},{8,5},{13,0},{12,9},{3,6},{2,15},{... | collective-permute-start | bytes 1572872 | tf_op jit(solution)/shard_map/ppermute | solution.py:319
  32.9 10.0 %copy-start.18 = (bf16[784,256]{1,0:T(8,128)(2,1)S(1)}, bf16[784,256]{1,0:T(8,128)(2,1)}, u32[]{:S(2)}) copy-start(bf16[784,256]{1,0:T(8,128)(2,1)} %get-tuple-element.87) | copy-start | bytes 1204228
  32.9 16.6 %copy-start.4 = (bf16[2,256,512]{2,1,0:T(8,128)(2,1)S(1)}, bf16[2,256,512]{2,1,0:T(8,128)(2,1)}, u32[]{:S(2)}) copy-start(bf16[2,256,512]{2,1,0:T(8,128)(2,1)} %w2_hbm.6) | copy-start | bytes 1572868
  33.6 15.9 %copy-start.8 = (bf16[2,256]{1,0:T(2,128)(2,1)S(1)}, bf16[2,256]{1,0:T(2,128)(2,1)}, u32[]{:S(2)}) copy-start(bf16[2,256]{1,0:T(2,128)(2,1)} %bias.6) | copy-start | bytes 3076
  33.6 15.9 %copy-start.2 = (bf16[2,512,256]{2,1,0:T(8,128)(2,1)S(1)}, bf16[2,512,256]{2,1,0:T(8,128)(2,1)}, u32[]{:S(2)}) copy-start(bf16[2,512,256]{2,1,0:T(8,128)(2,1)} %ws_hbm.6) | copy-start | bytes 1572868
  33.6 15.9 %copy-start.3 = (bf16[2,512,256]{2,1,0:T(8,128)(2,1)S(1)}, bf16[2,512,256]{2,1,0:T(8,128)(2,1)}, u32[]{:S(2)}) copy-start(bf16[2,512,256]{2,1,0:T(8,128)(2,1)} %wd_hbm.6) | copy-start | bytes 1572868
  33.6 9.3 %collective-permute-start.6 = (bf16[512,256]{1,0:T(8,128)(2,1)S(1)}, bf16[512,256]{1,0:T(8,128)(2,1)S(1)}, u32[]{:S(2)}, u32[]{:S(2)}) collective-permute-start(bf16[512,256]{1,0:T(8,128)(2,1)S(1)} %get-tuple-element.75), channel_id=1, source_target_pairs={{0,0},{1,2},{2,1},{3,3},{4,4},{5,6},{6,5},{7,7},{8,8},{9,10},{10,9... | collective-permute-start | bytes 786440 | tf_op jit(solution)/shard_map/ppermute | solution.py:292
  38.6 6.1 %collective-permute-start.7 = (bf16[512,256]{1,0:T(8,128)(2,1)S(1)}, bf16[512,256]{1,0:T(8,128)(2,1)S(1)}, u32[]{:S(2)}, u32[]{:S(2)}) collective-permute-start(bf16[512,256]{1,0:T(8,128)(2,1)S(1)} %get-tuple-element.76), channel_id=1, source_target_pairs={{0,1},{1,3},{2,0},{3,2},{4,5},{5,7},{6,4},{7,6},{8,9},{9,11},{10,8... | collective-permute-start | bytes 786440 | tf_op jit(solution)/shard_map/ppermute | solution.py:293
  42.9 14.8 %collective-permute-start.11 = (bf16[784,256]{1,0:T(8,128)(2,1)S(1)}, bf16[784,256]{1,0:T(8,128)(2,1)S(1)}, u32[]{:S(2)}, u32[]{:S(2)}) collective-permute-start(bf16[784,256]{1,0:T(8,128)(2,1)S(1)} %copy-done.18), channel_id=1, source_target_pairs={{0,2},{2,0},{1,3},{3,1},{4,6},{6,4},{5,7},{7,5},{8,10},{10,8},{9,1... | collective-permute-start | bytes 1204232 | tf_op jit(solution)/shard_map/ppermute | solution.py:308
  44.8 13.9 %copy-start.17 = (bf16[784,256]{1,0:T(8,128)(2,1)S(1)}, bf16[784,256]{1,0:T(8,128)(2,1)}, u32[]{:S(2)}) copy-start(bf16[784,256]{1,0:T(8,128)(2,1)} %get-tuple-element.100) | copy-start | bytes 1204228
  44.8 14.5 %copy-start.5 = (bf16[2,512,256]{2,1,0:T(8,128)(2,1)S(1)}, bf16[2,512,256]{2,1,0:T(8,128)(2,1)}, u32[]{:S(2)}) copy-start(bf16[2,512,256]{2,1,0:T(8,128)(2,1)} %ws_hbm.7) | copy-start | bytes 1572868
  44.8 14.5 %copy-start.6 = (bf16[2,512,256]{2,1,0:T(8,128)(2,1)S(1)}, bf16[2,512,256]{2,1,0:T(8,128)(2,1)}, u32[]{:S(2)}) copy-start(bf16[2,512,256]{2,1,0:T(8,128)(2,1)} %wd_hbm.7) | copy-start | bytes 1572868
  44.8 14.5 %copy-start.7 = (bf16[2,256,512]{2,1,0:T(8,128)(2,1)S(1)}, bf16[2,256,512]{2,1,0:T(8,128)(2,1)}, u32[]{:S(2)}) copy-start(bf16[2,256,512]{2,1,0:T(8,128)(2,1)} %w2_hbm.7) | copy-start | bytes 1572868
  44.8 14.5 %copy-start.9 = (bf16[2,256]{1,0:T(2,128)(2,1)S(1)}, bf16[2,256]{1,0:T(2,128)(2,1)}, u32[]{:S(2)}) copy-start(bf16[2,256]{1,0:T(2,128)(2,1)} %bias.7) | copy-start | bytes 3076
  44.9 13.9 %collective-permute-start.12 = (bf16[512,512]{1,0:T(8,128)(2,1)S(1)}, bf16[512,512]{1,0:T(8,128)(2,1)S(1)}, u32[]{:S(2)}, u32[]{:S(2)}) collective-permute-start(bf16[512,512]{1,0:T(8,128)(2,1)S(1)} %maximum_select_fusion.1.own), channel_id=1, source_target_pairs={{0,1},{1,0},{2,3},{3,2},{4,5},{5,4},{6,7},{7,6},{8,9},{9,8},{10,11... | collective-permute-start | bytes 1572872 | tf_op jit(solution)/shard_map/ppermute | solution.py:308
  47.5 11.8 %collective-permute-start.13 = (bf16[512,512]{1,0:T(8,128)(2,1)S(1)}, bf16[512,512]{1,0:T(8,128)(2,1)S(1)}, u32[]{:S(2)}, u32[]{:S(2)}) collective-permute-start(bf16[512,512]{1,0:T(8,128)(2,1)S(1)} %maximum_select_fusion.1.own), channel_id=1, source_target_pairs={{1,4},{5,8},{4,1},{9,12},{8,5},{12,9},{3,6},{7,10},{6,3},{11,14},{... | collective-permute-start | bytes 1572872 | tf_op jit(solution)/shard_map/ppermute | solution.py:319
  55.8 12.5 %collective-permute-start.14 = (bf16[512,512]{1,0:T(8,128)(2,1)S(1)}, bf16[512,512]{1,0:T(8,128)(2,1)S(1)}, u32[]{:S(2)}, u32[]{:S(2)}) collective-permute-start(bf16[512,512]{1,0:T(8,128)(2,1)S(1)} %graph_layer.4.own), channel_id=1, source_target_pairs={{0,1},{1,0},{2,3},{3,2},{4,5},{5,4},{6,7},{7,6},{8,9},{9,8},{10,11... | collective-permute-start | bytes 1572872 | tf_op jit(solution)/shard_map/ppermute | solution.py:308
  55.9 13.3 %collective-permute-start.15 = (bf16[512,512]{1,0:T(8,128)(2,1)S(1)}, bf16[512,512]{1,0:T(8,128)(2,1)S(1)}, u32[]{:S(2)}, u32[]{:S(2)}) collective-permute-start(bf16[512,512]{1,0:T(8,128)(2,1)S(1)} %graph_layer.4.own), channel_id=1, source_target_pairs={{1,4},{0,13},{5,8},{4,1},{9,12},{8,5},{13,0},{12,9},{3,6},{2,15},{... | collective-permute-start | bytes 1572872 | tf_op jit(solution)/shard_map/ppermute | solution.py:319
  57.7 8.4 %collective-permute-start.16 = (bf16[784,256]{1,0:T(8,128)(2,1)S(1)}, bf16[784,256]{1,0:T(8,128)(2,1)S(1)}, u32[]{:S(2)}, u32[]{:S(2)}) collective-permute-start(bf16[784,256]{1,0:T(8,128)(2,1)S(1)} %collective-permute-done.11.near_w), channel_id=1, source_target_pairs={{0,1},{1,0},{2,3},{3,2},{4,5},{5,4},{6,7},{7,6},{8,9},{9,8},{10,11... | collective-permute-start | bytes 1204232 | tf_op jit(solution)/shard_map/ppermute | solution.py:308
  58.7 16.8 %collective-permute-start.19 = (bf16[784,256]{1,0:T(8,128)(2,1)S(1)}, bf16[784,256]{1,0:T(8,128)(2,1)S(1)}, u32[]{:S(2)}, u32[]{:S(2)}) collective-permute-start(bf16[784,256]{1,0:T(8,128)(2,1)S(1)} %copy-done.17), channel_id=1, source_target_pairs={{0,2},{2,0},{1,3},{3,1},{4,6},{6,4},{5,7},{7,5},{8,10},{10,8},{9,1... | collective-permute-start | bytes 1204232 | tf_op jit(solution)/shard_map/ppermute | solution.py:308
  65.6 16.5 %collective-permute-start.20 = (bf16[512,512]{1,0:T(8,128)(2,1)S(1)}, bf16[512,512]{1,0:T(8,128)(2,1)S(1)}, u32[]{:S(2)}, u32[]{:S(2)}) collective-permute-start(bf16[512,512]{1,0:T(8,128)(2,1)S(1)} %graph_layer.5.own), channel_id=1, source_target_pairs={{0,1},{1,0},{2,3},{3,2},{4,5},{5,4},{6,7},{7,6},{8,9},{9,8},{10,11... | collective-permute-start | bytes 1572872 | tf_op jit(solution)/shard_map/ppermute | solution.py:308
  66.0 16.1 %collective-permute-start.21 = (bf16[512,512]{1,0:T(8,128)(2,1)S(1)}, bf16[512,512]{1,0:T(8,128)(2,1)S(1)}, u32[]{:S(2)}, u32[]{:S(2)}) collective-permute-start(bf16[512,512]{1,0:T(8,128)(2,1)S(1)} %graph_layer.5.own), channel_id=1, source_target_pairs={{1,4},{5,8},{4,1},{9,12},{8,5},{12,9},{3,6},{7,10},{6,3},{11,14},{... | collective-permute-start | bytes 1572872 | tf_op jit(solution)/shard_map/ppermute | solution.py:319
  75.6 6.6 %collective-permute-start.22 = (bf16[784,256]{1,0:T(8,128)(2,1)S(1)}, bf16[784,256]{1,0:T(8,128)(2,1)S(1)}, u32[]{:S(2)}, u32[]{:S(2)}) collective-permute-start(bf16[784,256]{1,0:T(8,128)(2,1)S(1)} %collective-permute-done.19.near_w), channel_id=1, source_target_pairs={{0,1},{1,0},{2,3},{3,2},{4,5},{5,4},{6,7},{7,6},{8,9},{9,8},{10,11... | collective-permute-start | bytes 1204232 | tf_op jit(solution)/shard_map/ppermute | solution.py:308
  78.5 12.0 %collective-permute-start.18 = (bf16[512,256]{1,0:T(8,128)(2,1)S(1)}, bf16[512,256]{1,0:T(8,128)(2,1)S(1)}, u32[]{:S(2)}, u32[]{:S(2)}) collective-permute-start(bf16[512,256]{1,0:T(8,128)(2,1)S(1)} %get-tuple-element.99), channel_id=1, source_target_pairs={{0,2},{1,0},{2,3},{3,1},{4,6},{5,4},{6,7},{7,5},{8,10},{9,8},{10,1... | collective-permute-start | bytes 786440 | tf_op jit(solution)/shard_map/ppermute | solution.py:299
  78.5 12.0 %collective-permute-start.17 = (bf16[512,256]{1,0:T(8,128)(2,1)S(1)}, bf16[512,256]{1,0:T(8,128)(2,1)S(1)}, u32[]{:S(2)}, u32[]{:S(2)}) collective-permute-start(bf16[512,256]{1,0:T(8,128)(2,1)S(1)} %get-tuple-element.98), channel_id=1, source_target_pairs={{0,0},{1,2},{2,1},{3,3},{4,4},{5,6},{6,5},{7,7},{8,8},{9,10},{10,9... | collective-permute-start | bytes 786440 | tf_op jit(solution)/shard_map/ppermute | solution.py:298
  88.5 10.0 %collective-permute-start.23 = (bf16[512,256]{1,0:T(8,128)(2,1)S(1)}, bf16[512,256]{1,0:T(8,128)(2,1)S(1)}, u32[]{:S(2)}, u32[]{:S(2)}) collective-permute-start(bf16[512,256]{1,0:T(8,128)(2,1)S(1)} %get-tuple-element.105), channel_id=1, source_target_pairs={{0,0},{1,2},{2,1},{3,3},{4,4},{5,6},{6,5},{7,7},{8,8},{9,10},{10,9... | collective-permute-start | bytes 786440 | tf_op jit(solution)/shard_map/ppermute | solution.py:298
  90.5 8.0 %collective-permute-start.24 = (bf16[512,256]{1,0:T(8,128)(2,1)S(1)}, bf16[512,256]{1,0:T(8,128)(2,1)S(1)}, u32[]{:S(2)}, u32[]{:S(2)}) collective-permute-start(bf16[512,256]{1,0:T(8,128)(2,1)S(1)} %get-tuple-element.106), channel_id=1, source_target_pairs={{0,2},{1,0},{2,3},{3,1},{4,6},{5,4},{6,7},{7,5},{8,10},{9,8},{10,1... | collective-permute-start | bytes 786440 | tf_op jit(solution)/shard_map/ppermute | solution.py:299

commit v14 on v10

--- a/solution.py
+++ b/solution.py
@@ -399,16 +399,11 @@
     for i, (graph, layer) in enumerate(order):
         last = layer == layers - 1
         far_w = swap(near_w[i], "batch")
-        if i + 1 < len(order):
-            near_w[i + 1], core1 = after((near_w[i + 1], core1))
-        if i + 2 < len(order):
-            packs[i + 2], near_w[i + 1] = after((packs[i + 2], near_w[i + 1]))
-            near_w.append(swap(packs[i + 2], "mp"))
         if graph == 0:
             planet = run_layer(
                 layer, slots, last, core1, g_idx, planet, g_sib, g_rim, g_ws, g_wd, g_w2, g_b1, near_w[i], far_w
             )
-            *planet, core1 = after((*(planet if last else (planet,)), core1))
+            *planet, core1, near_w[i + 1] = after((*(planet if last else (planet,)), core1, near_w[i + 1]))
             if not last:
                 planet = planet[0]
                 g_sib, g_rim = swap(planet, "batch"), rims(planet, True)
@@ -417,8 +412,11 @@
                 layer, slots, last, core1, r_idx, regional, r_sib, r_rim, r_ws, r_wd, r_w2, r_b1, near_w[i], far_w
             )
             if not last:
-                regional, core1 = after((regional, core1))
+                regional, core1, near_w[i + 1] = after((regional, core1, near_w[i + 1]))
                 r_sib, r_rim = swap(regional, "batch"), rims(regional, False)
+        if i + 2 < len(order):
+            packs[i + 2], near_w[i + 1] = after((packs[i + 2], near_w[i + 1]))
+            near_w.append(swap(packs[i + 2], "mp"))
     g_out = ordered(part, *gather_rows(*planet), 0)
     g_out, *regional_rows = after((g_out, *gather_rows(*regional)))
     r_out = ordered(part, *regional_rows, 0)

time: 107 us -> 102 us (0.953)
  waiting for transfers between devices: 27.6 us -> 24.6 us
  starting transfers between devices: 39.3 us -> 37.4 us
    ppermute x12, waiting for transfers between devices: 9.23 us -> 5.53 us  [swap(): return lax.ppermute(values, axis, [(0, 1), (1, 0)])]
  transfers between devices with their start and end apart: 27 -> 27, of which waited for: 7 -> 8; matrix products, arithmetic and copies ran while one was open for 1% -> 1% of each run, Pallas kernels for 32% -> 33%
where the time goes in v14:
time: 102 us; the launch traced here: 101 us
  starting transfers between devices  37.4 us (37%)
  Pallas kernels  33.8 us (33%)
  waiting for transfers between devices  24.6 us (24%)
  other arithmetic  2.42 us (2%)
  local copies, waits for them, and re-layouts  1.88 us (2%)
  between operations  1.12 us (1%)
    pallas_call x4, Pallas kernels, run_layer(): pl.pallas_call(functools.partial(layer_kernel, layer, slots, last), out_s...  25.2 us
    ppermute x4, starting transfers between devices, rims(): return lax.ppermute(own, ('mesh', 'batch'), pairs)  9.77 us
    ppermute x2, starting transfers between devices, spread_rows(): a = lax.ppermute(same, ('mp', 'batch'), [(0, 0), (1, 2), (2, 1), (3, 3)])  9.2 us
    ppermute x12, starting transfers between devices, swap(): return lax.ppermute(values, axis, [(0, 1), (1, 0)])  8.04 us
    ppermute x2, waiting for transfers between devices, gather_rows(): same = lax.ppermute(a, ('mp', 'batch'), [(0, 0), (1, 2), (2, 1), (3, 3)])  6.97 us
    pallas_call x2, Pallas kernels, pack_weights(): pl.pallas_call(functools.partial(pack_kernel, order), out_shape=(jax.Shap...  5.68 us
    ppermute x2, starting transfers between devices, gather_rows(): same = lax.ppermute(a, ('mp', 'batch'), [(0, 0), (1, 2), (2, 1), (3, 3)])  5.55 us
    ppermute x12, waiting for transfers between devices, swap(): return lax.ppermute(values, axis, [(0, 1), (1, 0)])  5.53 us
  transfers between devices with their start and end apart: 27, of which 8 were waited for; matrix products, arithmetic and copies ran while one was open for 1% of the time, Pallas kernels for 33%

profile of v14, /device:TPU:1, one launch (start us, length us, event | category | flops | bytes accessed | tf_op | source)
XLA Modules:
  0.0 101.3 jit_solution(10025614646314704648)
XLA Ops:
  0.6 1.1 %dynamic-slice_bitcast_fusion = (bf16[512,256]{1,0:T(8,128)(2,1)S(1)}, bf16[512,256]{1,0:T(8,128)(2,1)S(1)}) fusion(bf16[1,1024,256]{2,1,0:T(8,128)(2,1)} %param.17, s32[]{:T(128)S(6)} %select_n.78, s32[]{:T(128)S(6)} %select_n.77), kind=kLoop, calls=%fused_computation.4 | loop fusion | bytes 1048584 | tf_op jit(solution)/shard_map/dynamic_slice | solution.py:373
  1.7 4.5 %collective-permute-start = (bf16[512,256]{1,0:T(8,128)(2,1)S(1)}, bf16[512,256]{1,0:T(8,128)(2,1)S(1)}, u32[]{:S(2)}, u32[]{:S(2)}) collective-permute-start(bf16[512,256]{1,0:T(8,128)(2,1)S(1)} %get-tuple-element.113), channel_id=1, source_target_pairs={{0,0},{1,2},{2,1},{3,3},{4,4},{5,6},{6,5},{7,7},{8,8},{9,10},{10,9... | collective-permute-start | bytes 786440 | tf_op jit(solution)/shard_map/ppermute | solution.py:290
  6.2 0.0 collective-permute-start.1
  6.3 2.6 %pack_weights.2 = bf16[784,256]{1,0:T(8,128)(2,1)} custom-call(s32[1]{0:T(128)} %bitcast.4.core_ref, bf16[2,256]{1,0:T(2,128)(2,1)} %bias.6, bf16[2,256]{1,0:T(2,128)(2,1)} %bias.7, bf16[2,512,256]{2,1,0:T(8,128)(2,1)} %ws_hbm.6, bf16[2,512,256]{2,1,0:T(8,128)(2,1)} %wd_hbm.6, bf16[2,256,512]{2,1,0:T(8,128)(2,1)} %w2_hbm.6, bf16[2,512,256]{2,1,0:T(8,128)(2,1)} %ws_hbm.7, ...), custom_call_target="tpu_custom_call" | custom-call | flops 4294967296 | bytes 1 | tf_op jit(solution)/shard_map/pack_weights/pallas_call | solution.py:342
  8.9 0.2 collective-permute-start.2
  9.0 0.7 copy-done.15
  9.7 0.0 copy-done.14
  9.8 2.2 %pick_rows.1 = (bf16[272,256]{1,0:T(8,128)(2,1)S(1)}, bf16[272,256]{1,0:T(8,128)(2,1)S(1)}, bf16[272,256]{1,0:T(8,128)(2,1)S(1)}, bf16[272,256]{1,0:T(8,128)(2,1)S(1)}) custom-call(s32[1]{0:T(128)} %bitcast.me_ref, s32[3,512]{1,0:T(4,128)S(1)} %pad_add_fusion.bnd_ref, bf16[1024,256]{1,0:T(8,128)(2,1)S(1)} %bitcast.33), custom_call_target="tpu_custom_call" | custom-call | flops 8589934592 | bytes 1 | tf_op jit(solution)/shard_map/pick_rows/pallas_call | solution.py:115
  12.0 1.4 %collective-permute-start.3 = (bf16[272,256]{1,0:T(8,128)(2,1)S(1)}, bf16[272,256]{1,0:T(8,128)(2,1)S(1)}, u32[]{:S(2)}, u32[]{:S(2)}) collective-permute-start(bf16[272,256]{1,0:T(8,128)(2,1)S(1)} %get-tuple-element.64), channel_id=1, source_target_pairs={{0,4},{4,8},{8,12},{12,0},{1,5},{5,9},{9,13},{13,1},{2,6},{6,10},{... | collective-permute-start | bytes 417800 | tf_op jit(solution)/shard_map/ppermute | solution.py:383
  13.4 2.3 %collective-permute-start.4 = (bf16[272,256]{1,0:T(8,128)(2,1)S(1)}, bf16[272,256]{1,0:T(8,128)(2,1)S(1)}, u32[]{:S(2)}, u32[]{:S(2)}) collective-permute-start(bf16[272,256]{1,0:T(8,128)(2,1)S(1)} %get-tuple-element.65), channel_id=1, source_target_pairs={{0,8},{4,12},{8,0},{12,4},{1,9},{5,13},{9,1},{13,5},{2,10},{6,14},... | collective-permute-start | bytes 417800 | tf_op jit(solution)/shard_map/ppermute | solution.py:383
  15.7 0.1 fusion.5
  15.9 1.1 %collective-permute-start.5 = (bf16[272,256]{1,0:T(8,128)(2,1)S(1)}, bf16[272,256]{1,0:T(8,128)(2,1)S(1)}, u32[]{:S(2)}, u32[]{:S(2)}) collective-permute-start(bf16[272,256]{1,0:T(8,128)(2,1)S(1)} %get-tuple-element.66), channel_id=1, source_target_pairs={{0,12},{4,0},{8,4},{12,8},{1,13},{5,1},{9,5},{13,9},{2,14},{6,2},{... | collective-permute-start | bytes 417800 | tf_op jit(solution)/shard_map/ppermute | solution.py:383
  17.0 3.1 %pack_weights.3 = (bf16[784,256]{1,0:T(8,128)(2,1)}, bf16[784,256]{1,0:T(8,128)(2,1)}, bf16[784,256]{1,0:T(8,128)(2,1)}) custom-call(s32[1]{0:T(128)} %bitcast.4.core_ref, bf16[2,256]{1,0:T(2,128)(2,1)} %bias.6, bf16[2,256]{1,0:T(2,128)(2,1)} %bias.7, bf16[2,512,256]{2,1,0:T(8,128)(2,1)} %ws_hbm.6, bf16[2,512,256]{2,1,0:T(8,128)(2,1)} %wd_hbm.6, ...), custom_call_target="tpu_custom_call" | custom-call | flops 4294967296 | bytes 1 | tf_op jit(solution)/shard_map/pack_weights/pallas_call | solution.py:342
  20.1 5.4 %collective-permute-done.4.refs_2_ = bf16[272,256]{1,0:T(8,128)(2,1)S(1)} collective-permute-done((bf16[272,256]{1,0:T(8,128)(2,1)S(1)}, bf16[272,256]{1,0:T(8,128)(2,1)S(1)}, u32[]{:S(2)}, u32[]{:S(2)}) %collective-permute-start.4) | collective-permute-done | bytes 139296 | tf_op jit(solution)/shard_map/ppermute | solution.py:383
  25.5 0.1 maximum_select_fusion.own
  25.6 0.7 collective-permute-start.8
  26.3 3.1 %collective-permute-start.9 = (bf16[512,512]{1,0:T(8,128)(2,1)S(1)}, bf16[512,512]{1,0:T(8,128)(2,1)S(1)}, u32[]{:S(2)}, u32[]{:S(2)}) collective-permute-start(bf16[512,512]{1,0:T(8,128)(2,1)S(1)} %maximum_select_fusion.own), channel_id=1, source_target_pairs={{1,4},{0,13},{5,8},{4,1},{9,12},{8,5},{13,0},{12,9},{3,6},{2,15},{... | collective-permute-start | bytes 1572872 | tf_op jit(solution)/shard_map/ppermute | solution.py:317
  29.4 0.7 add_force.1
  30.1 4.7 %collective-permute-start.6 = (bf16[512,256]{1,0:T(8,128)(2,1)S(1)}, bf16[512,256]{1,0:T(8,128)(2,1)S(1)}, u32[]{:S(2)}, u32[]{:S(2)}) collective-permute-start(bf16[512,256]{1,0:T(8,128)(2,1)S(1)} %get-tuple-element.71), channel_id=1, source_target_pairs={{0,0},{1,2},{2,1},{3,3},{4,4},{5,6},{6,5},{7,7},{8,8},{9,10},{10,9... | collective-permute-start | bytes 786440 | tf_op jit(solution)/shard_map/ppermute | solution.py:290
  34.9 0.0 collective-permute-start.7
  34.9 4.3 %collective-permute-done.6 = bf16[512,256]{1,0:T(8,128)(2,1)S(1)} collective-permute-done((bf16[512,256]{1,0:T(8,128)(2,1)S(1)}, bf16[512,256]{1,0:T(8,128)(2,1)S(1)}, u32[]{:S(2)}, u32[]{:S(2)}) %collective-permute-start.6) | collective-permute-done | bytes 262176 | tf_op jit(solution)/shard_map/ppermute | solution.py:290
  39.2 1.8 %collective-permute-done.7 = bf16[512,256]{1,0:T(8,128)(2,1)S(1)} collective-permute-done((bf16[512,256]{1,0:T(8,128)(2,1)S(1)}, bf16[512,256]{1,0:T(8,128)(2,1)S(1)}, u32[]{:S(2)}, u32[]{:S(2)}) %collective-permute-start.7) | collective-permute-done | bytes 262176 | tf_op jit(solution)/shard_map/ppermute | solution.py:291
  40.9 0.7 collective-permute-done.9.rim
  41.6 1.5 %collective-permute-start.10 = (bf16[784,256]{1,0:T(8,128)(2,1)S(1)}, bf16[784,256]{1,0:T(8,128)(2,1)S(1)}, u32[]{:S(2)}, u32[]{:S(2)}) collective-permute-start(bf16[784,256]{1,0:T(8,128)(2,1)S(1)} %collective-permute-done.2.near_w), channel_id=1, source_target_pairs={{0,1},{1,0},{2,3},{3,2},{4,5},{5,4},{6,7},{7,6},{8,9},{9,8},{10,11... | collective-permute-start | bytes 1204232 | tf_op jit(solution)/shard_map/ppermute | solution.py:306
  43.1 1.4 %collective-permute-start.11 = (bf16[784,256]{1,0:T(8,128)(2,1)S(1)}, bf16[784,256]{1,0:T(8,128)(2,1)S(1)}, u32[]{:S(2)}, u32[]{:S(2)}) collective-permute-start(bf16[784,256]{1,0:T(8,128)(2,1)S(1)} %copy-done.19), channel_id=1, source_target_pairs={{0,2},{2,0},{1,3},{3,1},{4,6},{6,4},{5,7},{7,5},{8,10},{10,8},{9,1... | collective-permute-start | bytes 1204232 | tf_op jit(solution)/shard_map/ppermute | solution.py:306
  44.5 0.1 maximum_select_fusion.1.own
  44.7 0.3 collective-permute-start.12
  45.0 2.5 %collective-permute-start.13 = (bf16[512,512]{1,0:T(8,128)(2,1)S(1)}, bf16[512,512]{1,0:T(8,128)(2,1)S(1)}, u32[]{:S(2)}, u32[]{:S(2)}) collective-permute-start(bf16[512,512]{1,0:T(8,128)(2,1)S(1)} %maximum_select_fusion.1.own), channel_id=1, source_target_pairs={{1,4},{5,8},{4,1},{9,12},{8,5},{12,9},{3,6},{7,10},{6,3},{11,14},{... | collective-permute-start | bytes 1572872 | tf_op jit(solution)/shard_map/ppermute | solution.py:317
  47.6 6.3 %graph_layer.4.own = bf16[512,512]{1,0:T(8,128)(2,1)S(1)} custom-call(s32[1]{0:T(128)} %bitcast.4.core_ref, s32[4096]{0:T(1024)S(1)} %bitcast.37, bf16[512,512]{1,0:T(8,128)(2,1)S(1)} %maximum_select_fusion.own, bf16[512,512]{1,0:T(8,128)(2,1)S(1)} %collective-permute-done.8.sib, bf16[512,512]{1,0:T(8,128)(2,1)S(1)} %collective-permute-done.9.rim, ...), custom_call_target="tpu_custom_call" | custom-call | flops 8589934592 | bytes 2621440 | tf_op jit(solution)/shard_map/graph_layer/pallas_call | solution.py:252
  53.9 0.2 collective-permute-done.11.near_w
  54.1 0.8 collective-permute-start.14
  54.9 0.9 collective-permute-start.17
  55.8 0.9 collective-permute-start.15
  56.7 6.3 %graph_layer.5.own = bf16[512,512]{1,0:T(8,128)(2,1)S(1)} custom-call(s32[1]{0:T(128)} %bitcast.4.core_ref, s32[4096]{0:T(1024)S(1)} %bitcast.35, bf16[512,512]{1,0:T(8,128)(2,1)S(1)} %maximum_select_fusion.1.own, bf16[512,512]{1,0:T(8,128)(2,1)S(1)} %collective-permute-done.12.sib, bf16[512,512]{1,0:T(8,128)(2,1)S(1)} %collective-permute-done.13.rim, ...), custom_call_target="tpu_custom_call" | custom-call | flops 8589934592 | bytes 2621440 | tf_op jit(solution)/shard_map/graph_layer/pallas_call | solution.py:252
  63.0 2.3 %collective-permute-done.15.near_w = bf16[784,256]{1,0:T(8,128)(2,1)S(1)} collective-permute-done((bf16[784,256]{1,0:T(8,128)(2,1)S(1)}, bf16[784,256]{1,0:T(8,128)(2,1)S(1)}, u32[]{:S(2)}, u32[]{:S(2)}) %collective-permute-start.15) | collective-permute-done | bytes 401440 | tf_op jit(solution)/shard_map/ppermute | solution.py:306
  65.3 2.1 %collective-permute-start.18 = (bf16[784,256]{1,0:T(8,128)(2,1)S(1)}, bf16[784,256]{1,0:T(8,128)(2,1)S(1)}, u32[]{:S(2)}, u32[]{:S(2)}) collective-permute-start(bf16[784,256]{1,0:T(8,128)(2,1)S(1)} %collective-permute-done.15.near_w), channel_id=1, source_target_pairs={{0,1},{1,0},{2,3},{3,2},{4,5},{5,4},{6,7},{7,6},{8,9},{9,8},{10,11... | collective-permute-start | bytes 1204232 | tf_op jit(solution)/shard_map/ppermute | solution.py:306
  67.5 3.2 %collective-permute-start.23 = (bf16[512,512]{1,0:T(8,128)(2,1)S(1)}, bf16[512,512]{1,0:T(8,128)(2,1)S(1)}, u32[]{:S(2)}, u32[]{:S(2)}) collective-permute-start(bf16[512,512]{1,0:T(8,128)(2,1)S(1)} %graph_layer.5.own), channel_id=1, source_target_pairs={{1,4},{5,8},{4,1},{9,12},{8,5},{12,9},{3,6},{7,10},{6,3},{11,14},{... | collective-permute-start | bytes 1572872 | tf_op jit(solution)/shard_map/ppermute | solution.py:317
  70.7 0.2 collective-permute-start.19
  70.9 6.3 %graph_layer.6 = (bf16[512,256]{1,0:T(8,128)(2,1)S(1)}, bf16[512,256]{1,0:T(8,128)(2,1)S(1)}) custom-call(s32[1]{0:T(128)} %bitcast.4.core_ref, s32[4096]{0:T(1024)S(1)} %bitcast.38, bf16[512,512]{1,0:T(8,128)(2,1)S(1)} %graph_layer.4.own, bf16[512,512]{1,0:T(8,128)(2,1)S(1)} %collective-permute-done.16.sib, ...), custom_call_target="tpu_custom_call" | custom-call | flops 8589934592 | bytes 2621440 | tf_op jit(solution)/shard_map/graph_layer/pallas_call | solution.py:252
  77.2 3.0 %collective-permute-done.19.near_w = bf16[784,256]{1,0:T(8,128)(2,1)S(1)} collective-permute-done((bf16[784,256]{1,0:T(8,128)(2,1)S(1)}, bf16[784,256]{1,0:T(8,128)(2,1)S(1)}, u32[]{:S(2)}, u32[]{:S(2)}) %collective-permute-start.19) | collective-permute-done | bytes 401440 | tf_op jit(solution)/shard_map/ppermute | solution.py:306
  80.2 3.2 %collective-permute-start.20 = (bf16[512,256]{1,0:T(8,128)(2,1)S(1)}, bf16[512,256]{1,0:T(8,128)(2,1)S(1)}, u32[]{:S(2)}, u32[]{:S(2)}) collective-permute-start(bf16[512,256]{1,0:T(8,128)(2,1)S(1)} %get-tuple-element.102), channel_id=1, source_target_pairs={{0,0},{1,2},{2,1},{3,3},{4,4},{5,6},{6,5},{7,7},{8,8},{9,10},{10,9... | collective-permute-start | bytes 786440 | tf_op jit(solution)/shard_map/ppermute | solution.py:296
  83.5 0.0 collective-permute-start.21
  83.5 6.3 %graph_layer.7 = (bf16[512,256]{1,0:T(8,128)(2,1)S(1)}, bf16[512,256]{1,0:T(8,128)(2,1)S(1)}) custom-call(s32[1]{0:T(128)} %bitcast.4.core_ref, s32[4096]{0:T(1024)S(1)} %bitcast.36, bf16[512,512]{1,0:T(8,128)(2,1)S(1)} %graph_layer.5.own, bf16[512,512]{1,0:T(8,128)(2,1)S(1)} %collective-permute-done.22.sib, ...), custom_call_target="tpu_custom_call" | custom-call | flops 8589934592 | bytes 2621440 | tf_op jit(solution)/shard_map/graph_layer/pallas_call | solution.py:252
  89.9 2.3 %collective-permute-start.25 = (bf16[512,256]{1,0:T(8,128)(2,1)S(1)}, bf16[512,256]{1,0:T(8,128)(2,1)S(1)}, u32[]{:S(2)}, u32[]{:S(2)}) collective-permute-start(bf16[512,256]{1,0:T(8,128)(2,1)S(1)} %get-tuple-element.107), channel_id=1, source_target_pairs={{0,0},{1,2},{2,1},{3,3},{4,4},{5,6},{6,5},{7,7},{8,8},{9,10},{10,9... | collective-permute-start | bytes 786440 | tf_op jit(solution)/shard_map/ppermute | solution.py:296
  92.2 0.0 collective-permute-start.26
  92.3 1.0 %maximum_select_fusion.2 = bf16[1024,256]{1,0:T(8,128)(2,1)} fusion(bf16[512,256]{1,0:T(8,128)(2,1)S(1)} %collective-permute-done.21, bf16[512,256]{1,0:T(8,128)(2,1)S(1)} %collective-permute-done.20, pred[]{:T(512)S(6)} %eq.6), kind=kLoop, calls=%fused_computation.2 | loop fusion | flops 2359296 | bytes 1048577 | tf_op jit(solution)/shard_map/jit(_where)/select_n | solution.py:302
  93.3 7.0 %collective-permute-done.25 = bf16[512,256]{1,0:T(8,128)(2,1)S(1)} collective-permute-done((bf16[512,256]{1,0:T(8,128)(2,1)S(1)}, bf16[512,256]{1,0:T(8,128)(2,1)S(1)}, u32[]{:S(2)}, u32[]{:S(2)}) %collective-permute-start.25) | collective-permute-done | bytes 262176 | tf_op jit(solution)/shard_map/ppermute | solution.py:296
  100.3 1.0 %maximum_select_fusion.3 = bf16[1,1024,256]{2,1,0:T(8,128)(2,1)} fusion(bf16[1,512,256]{2,1,0:T(8,128)(2,1)S(1)} %bitcast.41, bf16[1,512,256]{2,1,0:T(8,128)(2,1)S(1)} %bitcast.40, pred[]{:T(512)S(6)} %eq.6), kind=kLoop, calls=%fused_computation.3 | loop fusion | flops 2359296 | bytes 1048577 | tf_op jit(solution)/shard_map/jit(_where)/select_n | solution.py:302
  (66 shorter events, 0.2 us)
Async XLA Ops:
  1.7 14.1 %collective-permute-start = (bf16[512,256]{1,0:T(8,128)(2,1)S(1)}, bf16[512,256]{1,0:T(8,128)(2,1)S(1)}, u32[]{:S(2)}, u32[]{:S(2)}) collective-permute-start(bf16[512,256]{1,0:T(8,128)(2,1)S(1)} %get-tuple-element.113), channel_id=1, source_target_pairs={{0,0},{1,2},{2,1},{3,3},{4,4},{5,6},{6,5},{7,7},{8,8},{9,10},{10,9... | collective-permute-start | bytes 786440 | tf_op jit(solution)/shard_map/ppermute | solution.py:290
  6.2 10.8 %collective-permute-start.1 = (bf16[512,256]{1,0:T(8,128)(2,1)S(1)}, bf16[512,256]{1,0:T(8,128)(2,1)S(1)}, u32[]{:S(2)}, u32[]{:S(2)}) collective-permute-start(bf16[512,256]{1,0:T(8,128)(2,1)S(1)} %get-tuple-element.112), channel_id=1, source_target_pairs={{0,1},{1,3},{2,0},{3,2},{4,5},{5,7},{6,4},{7,6},{8,9},{9,11},{10,8... | collective-permute-start | bytes 786440 | tf_op jit(solution)/shard_map/ppermute | solution.py:291
  6.3 2.8 %copy-start.16 = (s32[512]{0:T(512)S(1)}, s32[512]{0:T(512)}, u32[]{:S(2)}) copy-start(s32[512]{0:T(512)} %param.23) | copy-start | bytes 6148
  6.3 3.5 %copy-start = (bf16[1,1024,256]{2,1,0:T(8,128)(2,1)S(1)}, bf16[1,1024,256]{2,1,0:T(8,128)(2,1)}, u32[]{:S(2)}) copy-start(bf16[1,1024,256]{2,1,0:T(8,128)(2,1)} %param.17) | copy-start | bytes 1572868
  8.9 16.6 %collective-permute-start.2 = (bf16[784,256]{1,0:T(8,128)(2,1)}, bf16[784,256]{1,0:T(8,128)(2,1)S(1)}, u32[]{:S(2)}, u32[]{:S(2)}) collective-permute-start(bf16[784,256]{1,0:T(8,128)(2,1)} %pack_weights.2), channel_id=1, source_target_pairs={{0,2},{2,0},{1,3},{3,1},{4,6},{6,4},{5,7},{7,5},{8,10},{10,8},{9,1... | collective-permute-start | bytes 1204232 | tf_op jit(solution)/shard_map/ppermute | solution.py:306
  9.0 0.7 copy-start.15
  9.0 0.7 copy-start.14
  9.7 5.9 %copy-start.12 = (s32[1024]{0:T(1024)S(1)}, s32[1024]{0:T(1024)}, u32[]{:S(2)}) copy-start(s32[1024]{0:T(1024)} %param.20) | copy-start | bytes 12292
  9.7 5.9 %copy-start.13 = (s32[1024]{0:T(1024)S(1)}, s32[1024]{0:T(1024)}, u32[]{:S(2)}) copy-start(s32[1024]{0:T(1024)} %param.22) | copy-start | bytes 12292
  9.8 6.0 %copy-start.11 = (s32[1024,8]{0,1:T(8,128)S(1)}, s32[1024,8]{0,1:T(8,128)}, u32[]{:S(2)}) copy-start(s32[1024,8]{0,1:T(8,128)} %param.19) | copy-start | bytes 98308
  12.0 3.8 %copy-start.10 = (s32[1024,8]{0,1:T(8,128)S(1)}, s32[1024,8]{0,1:T(8,128)}, u32[]{:S(2)}) copy-start(s32[1024,8]{0,1:T(8,128)} %param.21) | copy-start | bytes 98308
  12.0 8.1 %collective-permute-start.3 = (bf16[272,256]{1,0:T(8,128)(2,1)S(1)}, bf16[272,256]{1,0:T(8,128)(2,1)S(1)}, u32[]{:S(2)}, u32[]{:S(2)}) collective-permute-start(bf16[272,256]{1,0:T(8,128)(2,1)S(1)} %get-tuple-element.64), channel_id=1, source_target_pairs={{0,4},{4,8},{8,12},{12,0},{1,5},{5,9},{9,13},{13,1},{2,6},{6,10},{... | collective-permute-start | bytes 417800 | tf_op jit(solution)/shard_map/ppermute | solution.py:383
  13.4 12.1 %collective-permute-start.4 = (bf16[272,256]{1,0:T(8,128)(2,1)S(1)}, bf16[272,256]{1,0:T(8,128)(2,1)S(1)}, u32[]{:S(2)}, u32[]{:S(2)}) collective-permute-start(bf16[272,256]{1,0:T(8,128)(2,1)S(1)} %get-tuple-element.65), channel_id=1, source_target_pairs={{0,8},{4,12},{8,0},{12,4},{1,9},{5,13},{9,1},{13,5},{2,10},{6,14},... | collective-permute-start | bytes 417800 | tf_op jit(solution)/shard_map/ppermute | solution.py:383
  15.9 9.6 %collective-permute-start.5 = (bf16[272,256]{1,0:T(8,128)(2,1)S(1)}, bf16[272,256]{1,0:T(8,128)(2,1)S(1)}, u32[]{:S(2)}, u32[]{:S(2)}) collective-permute-start(bf16[272,256]{1,0:T(8,128)(2,1)S(1)} %get-tuple-element.66), channel_id=1, source_target_pairs={{0,12},{4,0},{8,4},{12,8},{1,13},{5,1},{9,5},{13,9},{2,14},{6,2},{... | collective-permute-start | bytes 417800 | tf_op jit(solution)/shard_map/ppermute | solution.py:383
  25.5 3.9 %copy-start.1 = (bf16[1,1024,256]{2,1,0:T(8,128)(2,1)S(1)}, bf16[1,1024,256]{2,1,0:T(8,128)(2,1)}, u32[]{:S(2)}) copy-start(bf16[1,1024,256]{2,1,0:T(8,128)(2,1)} %param.18) | copy-start | bytes 1572868
  25.6 15.3 %collective-permute-start.8 = (bf16[512,512]{1,0:T(8,128)(2,1)S(1)}, bf16[512,512]{1,0:T(8,128)(2,1)S(1)}, u32[]{:S(2)}, u32[]{:S(2)}) collective-permute-start(bf16[512,512]{1,0:T(8,128)(2,1)S(1)} %maximum_select_fusion.own), channel_id=1, source_target_pairs={{0,1},{1,0},{2,3},{3,2},{4,5},{5,4},{6,7},{7,6},{8,9},{9,8},{10,11... | collective-permute-start | bytes 1572872 | tf_op jit(solution)/shard_map/ppermute | solution.py:306
  26.3 15.4 %collective-permute-start.9 = (bf16[512,512]{1,0:T(8,128)(2,1)S(1)}, bf16[512,512]{1,0:T(8,128)(2,1)S(1)}, u32[]{:S(2)}, u32[]{:S(2)}) collective-permute-start(bf16[512,512]{1,0:T(8,128)(2,1)S(1)} %maximum_select_fusion.own), channel_id=1, source_target_pairs={{1,4},{0,13},{5,8},{4,1},{9,12},{8,5},{13,0},{12,9},{3,6},{2,15},{... | collective-permute-start | bytes 1572872 | tf_op jit(solution)/shard_map/ppermute | solution.py:317
  29.4 13.7 %copy-start.19 = (bf16[784,256]{1,0:T(8,128)(2,1)S(1)}, bf16[784,256]{1,0:T(8,128)(2,1)}, u32[]{:S(2)}) copy-start(bf16[784,256]{1,0:T(8,128)(2,1)} %get-tuple-element.86) | copy-start | bytes 1204228
  29.4 18.2 %copy-start.4 = (bf16[2,256,512]{2,1,0:T(8,128)(2,1)S(1)}, bf16[2,256,512]{2,1,0:T(8,128)(2,1)}, u32[]{:S(2)}) copy-start(bf16[2,256,512]{2,1,0:T(8,128)(2,1)} %w2_hbm.6) | copy-start | bytes 1572868
  30.1 9.0 %collective-permute-start.6 = (bf16[512,256]{1,0:T(8,128)(2,1)S(1)}, bf16[512,256]{1,0:T(8,128)(2,1)S(1)}, u32[]{:S(2)}, u32[]{:S(2)}) collective-permute-start(bf16[512,256]{1,0:T(8,128)(2,1)S(1)} %get-tuple-element.71), channel_id=1, source_target_pairs={{0,0},{1,2},{2,1},{3,3},{4,4},{5,6},{6,5},{7,7},{8,8},{9,10},{10,9... | collective-permute-start | bytes 786440 | tf_op jit(solution)/shard_map/ppermute | solution.py:290
  34.8 12.8 %copy-start.8 = (bf16[2,256]{1,0:T(2,128)(2,1)S(1)}, bf16[2,256]{1,0:T(2,128)(2,1)}, u32[]{:S(2)}) copy-start(bf16[2,256]{1,0:T(2,128)(2,1)} %bias.6) | copy-start | bytes 3076
  34.8 12.8 %copy-start.2 = (bf16[2,512,256]{2,1,0:T(8,128)(2,1)S(1)}, bf16[2,512,256]{2,1,0:T(8,128)(2,1)}, u32[]{:S(2)}) copy-start(bf16[2,512,256]{2,1,0:T(8,128)(2,1)} %ws_hbm.6) | copy-start | bytes 1572868
  34.9 12.7 %copy-start.3 = (bf16[2,512,256]{2,1,0:T(8,128)(2,1)S(1)}, bf16[2,512,256]{2,1,0:T(8,128)(2,1)}, u32[]{:S(2)}) copy-start(bf16[2,512,256]{2,1,0:T(8,128)(2,1)} %wd_hbm.6) | copy-start | bytes 1572868
  34.9 6.1 %collective-permute-start.7 = (bf16[512,256]{1,0:T(8,128)(2,1)S(1)}, bf16[512,256]{1,0:T(8,128)(2,1)S(1)}, u32[]{:S(2)}, u32[]{:S(2)}) collective-permute-start(bf16[512,256]{1,0:T(8,128)(2,1)S(1)} %get-tuple-element.72), channel_id=1, source_target_pairs={{0,1},{1,3},{2,0},{3,2},{4,5},{5,7},{6,4},{7,6},{8,9},{9,11},{10,8... | collective-permute-start | bytes 786440 | tf_op jit(solution)/shard_map/ppermute | solution.py:291
  41.6 5.9 %collective-permute-start.10 = (bf16[784,256]{1,0:T(8,128)(2,1)S(1)}, bf16[784,256]{1,0:T(8,128)(2,1)S(1)}, u32[]{:S(2)}, u32[]{:S(2)}) collective-permute-start(bf16[784,256]{1,0:T(8,128)(2,1)S(1)} %collective-permute-done.2.near_w), channel_id=1, source_target_pairs={{0,1},{1,0},{2,3},{3,2},{4,5},{5,4},{6,7},{7,6},{8,9},{9,8},{10,11... | collective-permute-start | bytes 1204232 | tf_op jit(solution)/shard_map/ppermute | solution.py:306
  43.1 10.9 %collective-permute-start.11 = (bf16[784,256]{1,0:T(8,128)(2,1)S(1)}, bf16[784,256]{1,0:T(8,128)(2,1)S(1)}, u32[]{:S(2)}, u32[]{:S(2)}) collective-permute-start(bf16[784,256]{1,0:T(8,128)(2,1)S(1)} %copy-done.19), channel_id=1, source_target_pairs={{0,2},{2,0},{1,3},{3,1},{4,6},{6,4},{5,7},{7,5},{8,10},{10,8},{9,1... | collective-permute-start | bytes 1204232 | tf_op jit(solution)/shard_map/ppermute | solution.py:306
  44.6 11.1 %copy-start.18 = (bf16[784,256]{1,0:T(8,128)(2,1)S(1)}, bf16[784,256]{1,0:T(8,128)(2,1)}, u32[]{:S(2)}) copy-start(bf16[784,256]{1,0:T(8,128)(2,1)} %get-tuple-element.93) | copy-start | bytes 1204228
  44.7 12.1 %copy-start.5 = (bf16[2,512,256]{2,1,0:T(8,128)(2,1)S(1)}, bf16[2,512,256]{2,1,0:T(8,128)(2,1)}, u32[]{:S(2)}) copy-start(bf16[2,512,256]{2,1,0:T(8,128)(2,1)} %ws_hbm.7) | copy-start | bytes 1572868
  44.7 12.0 %copy-start.6 = (bf16[2,512,256]{2,1,0:T(8,128)(2,1)S(1)}, bf16[2,512,256]{2,1,0:T(8,128)(2,1)}, u32[]{:S(2)}) copy-start(bf16[2,512,256]{2,1,0:T(8,128)(2,1)} %wd_hbm.7) | copy-start | bytes 1572868
  44.7 12.0 %copy-start.7 = (bf16[2,256,512]{2,1,0:T(8,128)(2,1)S(1)}, bf16[2,256,512]{2,1,0:T(8,128)(2,1)}, u32[]{:S(2)}) copy-start(bf16[2,256,512]{2,1,0:T(8,128)(2,1)} %w2_hbm.7) | copy-start | bytes 1572868
  44.7 11.1 %collective-permute-start.12 = (bf16[512,512]{1,0:T(8,128)(2,1)S(1)}, bf16[512,512]{1,0:T(8,128)(2,1)S(1)}, u32[]{:S(2)}, u32[]{:S(2)}) collective-permute-start(bf16[512,512]{1,0:T(8,128)(2,1)S(1)} %maximum_select_fusion.1.own), channel_id=1, source_target_pairs={{0,1},{1,0},{2,3},{3,2},{4,5},{5,4},{6,7},{7,6},{8,9},{9,8},{10,11... | collective-permute-start | bytes 1572872 | tf_op jit(solution)/shard_map/ppermute | solution.py:306
  45.0 11.7 %collective-permute-start.13 = (bf16[512,512]{1,0:T(8,128)(2,1)S(1)}, bf16[512,512]{1,0:T(8,128)(2,1)S(1)}, u32[]{:S(2)}, u32[]{:S(2)}) collective-permute-start(bf16[512,512]{1,0:T(8,128)(2,1)S(1)} %maximum_select_fusion.1.own), channel_id=1, source_target_pairs={{1,4},{5,8},{4,1},{9,12},{8,5},{12,9},{3,6},{7,10},{6,3},{11,14},{... | collective-permute-start | bytes 1572872 | tf_op jit(solution)/shard_map/ppermute | solution.py:317
  53.9 2.8 %copy-start.9 = (bf16[2,256]{1,0:T(2,128)(2,1)S(1)}, bf16[2,256]{1,0:T(2,128)(2,1)}, u32[]{:S(2)}) copy-start(bf16[2,256]{1,0:T(2,128)(2,1)} %bias.7) | copy-start | bytes 3076
  54.1 16.7 %copy-start.17 = (bf16[784,256]{1,0:T(8,128)(2,1)S(1)}, bf16[784,256]{1,0:T(8,128)(2,1)}, u32[]{:S(2)}) copy-start(bf16[784,256]{1,0:T(8,128)(2,1)} %get-tuple-element.101) | copy-start | bytes 1204228
  54.1 2.6 %collective-permute-start.14 = (bf16[784,256]{1,0:T(8,128)(2,1)S(1)}, bf16[784,256]{1,0:T(8,128)(2,1)S(1)}, u32[]{:S(2)}, u32[]{:S(2)}) collective-permute-start(bf16[784,256]{1,0:T(8,128)(2,1)S(1)} %collective-permute-done.11.near_w), channel_id=1, source_target_pairs={{0,1},{1,0},{2,3},{3,2},{4,5},{5,4},{6,7},{7,6},{8,9},{9,8},{10,11... | collective-permute-start | bytes 1204232 | tf_op jit(solution)/shard_map/ppermute | solution.py:306
  54.9 15.9 %collective-permute-start.16 = (bf16[512,512]{1,0:T(8,128)(2,1)S(1)}, bf16[512,512]{1,0:T(8,128)(2,1)S(1)}, u32[]{:S(2)}, u32[]{:S(2)}) collective-permute-start(bf16[512,512]{1,0:T(8,128)(2,1)S(1)} %graph_layer.4.own), channel_id=1, source_target_pairs={{0,1},{1,0},{2,3},{3,2},{4,5},{5,4},{6,7},{7,6},{8,9},{9,8},{10,11... | collective-permute-start | bytes 1572872 | tf_op jit(solution)/shard_map/ppermute | solution.py:306
  54.9 16.0 %collective-permute-start.17 = (bf16[512,512]{1,0:T(8,128)(2,1)S(1)}, bf16[512,512]{1,0:T(8,128)(2,1)S(1)}, u32[]{:S(2)}, u32[]{:S(2)}) collective-permute-start(bf16[512,512]{1,0:T(8,128)(2,1)S(1)} %graph_layer.4.own), channel_id=1, source_target_pairs={{1,4},{0,13},{5,8},{4,1},{9,12},{8,5},{13,0},{12,9},{3,6},{2,15},{... | collective-permute-start | bytes 1572872 | tf_op jit(solution)/shard_map/ppermute | solution.py:317
  55.8 9.6 %collective-permute-start.15 = (bf16[784,256]{1,0:T(8,128)(2,1)S(1)}, bf16[784,256]{1,0:T(8,128)(2,1)S(1)}, u32[]{:S(2)}, u32[]{:S(2)}) collective-permute-start(bf16[784,256]{1,0:T(8,128)(2,1)S(1)} %copy-done.18), channel_id=1, source_target_pairs={{0,2},{2,0},{1,3},{3,1},{4,6},{6,4},{5,7},{7,5},{8,10},{10,8},{9,1... | collective-permute-start | bytes 1204232 | tf_op jit(solution)/shard_map/ppermute | solution.py:306
  65.3 5.5 %collective-permute-start.18 = (bf16[784,256]{1,0:T(8,128)(2,1)S(1)}, bf16[784,256]{1,0:T(8,128)(2,1)S(1)}, u32[]{:S(2)}, u32[]{:S(2)}) collective-permute-start(bf16[784,256]{1,0:T(8,128)(2,1)S(1)} %collective-permute-done.15.near_w), channel_id=1, source_target_pairs={{0,1},{1,0},{2,3},{3,2},{4,5},{5,4},{6,7},{7,6},{8,9},{9,8},{10,11... | collective-permute-start | bytes 1204232 | tf_op jit(solution)/shard_map/ppermute | solution.py:306
  67.5 16.0 %collective-permute-start.22 = (bf16[512,512]{1,0:T(8,128)(2,1)S(1)}, bf16[512,512]{1,0:T(8,128)(2,1)S(1)}, u32[]{:S(2)}, u32[]{:S(2)}) collective-permute-start(bf16[512,512]{1,0:T(8,128)(2,1)S(1)} %graph_layer.5.own), channel_id=1, source_target_pairs={{0,1},{1,0},{2,3},{3,2},{4,5},{5,4},{6,7},{7,6},{8,9},{9,8},{10,11... | collective-permute-start | bytes 1572872 | tf_op jit(solution)/shard_map/ppermute | solution.py:306
  67.5 16.0 %collective-permute-start.23 = (bf16[512,512]{1,0:T(8,128)(2,1)S(1)}, bf16[512,512]{1,0:T(8,128)(2,1)S(1)}, u32[]{:S(2)}, u32[]{:S(2)}) collective-permute-start(bf16[512,512]{1,0:T(8,128)(2,1)S(1)} %graph_layer.5.own), channel_id=1, source_target_pairs={{1,4},{5,8},{4,1},{9,12},{8,5},{12,9},{3,6},{7,10},{6,3},{11,14},{... | collective-permute-start | bytes 1572872 | tf_op jit(solution)/shard_map/ppermute | solution.py:317
  70.7 9.5 %collective-permute-start.19 = (bf16[784,256]{1,0:T(8,128)(2,1)S(1)}, bf16[784,256]{1,0:T(8,128)(2,1)S(1)}, u32[]{:S(2)}, u32[]{:S(2)}) collective-permute-start(bf16[784,256]{1,0:T(8,128)(2,1)S(1)} %copy-done.17), channel_id=1, source_target_pairs={{0,2},{2,0},{1,3},{3,1},{4,6},{6,4},{5,7},{7,5},{8,10},{10,8},{9,1... | collective-permute-start | bytes 1204232 | tf_op jit(solution)/shard_map/ppermute | solution.py:306
  80.2 3.3 %collective-permute-start.24 = (bf16[784,256]{1,0:T(8,128)(2,1)S(1)}, bf16[784,256]{1,0:T(8,128)(2,1)S(1)}, u32[]{:S(2)}, u32[]{:S(2)}) collective-permute-start(bf16[784,256]{1,0:T(8,128)(2,1)S(1)} %collective-permute-done.19.near_w), channel_id=1, source_target_pairs={{0,1},{1,0},{2,3},{3,2},{4,5},{5,4},{6,7},{7,6},{8,9},{9,8},{10,11... | collective-permute-start | bytes 1204232 | tf_op jit(solution)/shard_map/ppermute | solution.py:306
  80.2 12.0 %collective-permute-start.20 = (bf16[512,256]{1,0:T(8,128)(2,1)S(1)}, bf16[512,256]{1,0:T(8,128)(2,1)S(1)}, u32[]{:S(2)}, u32[]{:S(2)}) collective-permute-start(bf16[512,256]{1,0:T(8,128)(2,1)S(1)} %get-tuple-element.102), channel_id=1, source_target_pairs={{0,0},{1,2},{2,1},{3,3},{4,4},{5,6},{6,5},{7,7},{8,8},{9,10},{10,9... | collective-permute-start | bytes 786440 | tf_op jit(solution)/shard_map/ppermute | solution.py:296
  83.5 8.8 %collective-permute-start.21 = (bf16[512,256]{1,0:T(8,128)(2,1)S(1)}, bf16[512,256]{1,0:T(8,128)(2,1)S(1)}, u32[]{:S(2)}, u32[]{:S(2)}) collective-permute-start(bf16[512,256]{1,0:T(8,128)(2,1)S(1)} %get-tuple-element.103), channel_id=1, source_target_pairs={{0,2},{1,0},{2,3},{3,1},{4,6},{5,4},{6,7},{7,5},{8,10},{9,8},{10,1... | collective-permute-start | bytes 786440 | tf_op jit(solution)/shard_map/ppermute | solution.py:297
  89.9 10.4 %collective-permute-start.25 = (bf16[512,256]{1,0:T(8,128)(2,1)S(1)}, bf16[512,256]{1,0:T(8,128)(2,1)S(1)}, u32[]{:S(2)}, u32[]{:S(2)}) collective-permute-start(bf16[512,256]{1,0:T(8,128)(2,1)S(1)} %get-tuple-element.107), channel_id=1, source_target_pairs={{0,0},{1,2},{2,1},{3,3},{4,4},{5,6},{6,5},{7,7},{8,8},{9,10},{10,9... | collective-permute-start | bytes 786440 | tf_op jit(solution)/shard_map/ppermute | solution.py:296
  92.2 8.0 %collective-permute-start.26 = (bf16[512,256]{1,0:T(8,128)(2,1)S(1)}, bf16[512,256]{1,0:T(8,128)(2,1)S(1)}, u32[]{:S(2)}, u32[]{:S(2)}) collective-permute-start(bf16[512,256]{1,0:T(8,128)(2,1)S(1)} %get-tuple-element.108), channel_id=1, source_target_pairs={{0,2},{1,0},{2,3},{3,1},{4,6},{5,4},{6,7},{7,5},{8,10},{9,8},{10,1... | collective-permute-start | bytes 786440 | tf_op jit(solution)/shard_map/ppermute | solution.py:297

commit v15 on v13

--- a/solution.py
+++ b/solution.py
@@ -379,11 +379,12 @@
     g_weights, r_weights = (g_ws, g_wd, g_w2), (r_ws, r_wd, r_w2)
     after = lax.optimization_barrier
 
+    packs = list(pack_weights((((0, 0), (1, 0)),), core1, g_weights, g_b1, r_weights, r_b1))
+    near_w = [swap(packs[0], "mp")]
+    packs[0], g_own = after((packs[0], g_own))
     same = lax.dynamic_slice(g_own, (part * half, 0), (half, g_own.shape[1]))
     other = lax.dynamic_slice(g_own, ((1 - part) * half, 0), (half, g_own.shape[1]))
     g_a, g_b = spread_rows(same, other)
-    packs = list(pack_weights((((0, 0), (1, 0)),), core1, g_weights, g_b1, r_weights, r_b1))
-    near_w = [swap(packs[0], "mp")]
     bnd = jnp.stack([bnd_src, bnd_part[:, 0], bnd_node])
     bnd, packs[0], same, other = after((bnd, packs[0], same, other))
     pieces = pick_rows(me, bnd, g_own, parts, cap)

time: 99.9 us -> 103 us (1.031)
  starting transfers between devices: 36.8 us -> 39.9 us
  local copies, waits for them, and re-layouts: 1.88 us -> 0.82 us
    ppermute x2, waiting for transfers between devices: 4.31 us -> 15.6 us  [spread_rows(): a = lax.ppermute(same, ('mp', 'batch'), [(0, 0), (1, 2), (2, 1), (3, 3)])]
    ppermute x3, waiting for transfers between devices: 5.67 us -> 0.01 us  [by_rows(): lax.ppermute(pieces[k], 'mesh', [(i, (i + k) % parts) for i in range(part...]
    ppermute x10, waiting for transfers between devices: 3.79 us -> 0.03 us  [swap(): return lax.ppermute(values, axis, [(0, 1), (1, 0)])]
    ppermute x3, starting transfers between devices: 4.78 us -> 7.72 us  [by_rows(): lax.ppermute(pieces[k], 'mesh', [(i, (i + k) % parts) for i in range(part...]
    dynamic_slice x1, local copies, waits for them, and re-layouts: 1.07 us -> 0.03 us  [by_rows(): lax.dynamic_slice(g_own, ((1 - part) * half, 0), (half, g_own.shape[1]))]
  transfers between devices with their start and end apart: 25 -> 25, of which waited for: 6 -> 4; matrix products, arithmetic and copies ran while one was open for 1% -> 1% of each run, Pallas kernels for 34% -> 30%
where the time goes in v15:
time: 103 us; the launch traced here: 102 us
  starting transfers between devices  39.9 us (39%)
  Pallas kernels  33.9 us (33%)
  waiting for transfers between devices  24.4 us (24%)
  other arithmetic  2.41 us (2%)
  between operations  1.16 us (1%)
    pallas_call x4, Pallas kernels, run_layer(): pl.pallas_call(functools.partial(layer_kernel, layer, place, slots, last)...  25.2 us
    ppermute x2, waiting for transfers between devices, spread_rows(): a = lax.ppermute(same, ('mp', 'batch'), [(0, 0), (1, 2), (2, 1), (3, 3)])  15.6 us
    ppermute x10, starting transfers between devices, swap(): return lax.ppermute(values, axis, [(0, 1), (1, 0)])  9.91 us
    ppermute x2, starting transfers between devices, spread_rows(): a = lax.ppermute(same, ('mp', 'batch'), [(0, 0), (1, 2), (2, 1), (3, 3)])  8.86 us
    ppermute x4, starting transfers between devices, rims(): return lax.ppermute(own, ('mesh', 'batch'), pairs)  7.75 us
    ppermute x3, starting transfers between devices, by_rows(): lax.ppermute(pieces[k], 'mesh', [(i, (i + k) % parts) for i in range(part...  7.72 us
    ppermute x2, waiting for transfers between devices, gather_rows(): same = lax.ppermute(a, ('mp', 'batch'), [(0, 0), (1, 2), (2, 1), (3, 3)])  6.97 us
    pallas_call x2, Pallas kernels, pack_weights(): pl.pallas_call(functools.partial(pack_kernel, plan), out_shape=tuple((jax...  5.74 us
  transfers between devices with their start and end apart: 25, of which 4 were waited for; matrix products, arithmetic and copies ran while one was open for 1% of the time, Pallas kernels for 30%

profile of v15, /device:TPU:1, one launch (start us, length us, event | category | flops | bytes accessed | tf_op | source)
XLA Modules:
  0.0 102.5 jit_solution(6434842517027368879)
XLA Ops:
  0.6 2.9 %pack_weights.2 = bf16[1568,256]{1,0:T(8,128)(2,1)} custom-call(s32[1]{0:T(128)} %bitcast.4.core_ref, bf16[2,256]{1,0:T(2,128)(2,1)} %bias.6, bf16[2,256]{1,0:T(2,128)(2,1)} %bias.7, bf16[2,512,256]{2,1,0:T(8,128)(2,1)} %ws_hbm.6, bf16[2,512,256]{2,1,0:T(8,128)(2,1)} %wd_hbm.6, bf16[2,256,512]{2,1,0:T(8,128)(2,1)} %w2_hbm.6, bf16[2,512,256]{2,1,0:T(8,128)(2,1)} %ws_hbm.7, ...), custom_call_target="tpu_custom_call" | custom-call | flops 4294967296 | bytes 1 | tf_op jit(solution)/shard_map/pack_weights/pallas_call | solution.py:352
  3.6 2.1 %collective-permute-start.2 = (bf16[1568,256]{1,0:T(8,128)(2,1)}, bf16[1568,256]{1,0:T(8,128)(2,1)S(1)}, u32[]{:S(2)}, u32[]{:S(2)}) collective-permute-start(bf16[1568,256]{1,0:T(8,128)(2,1)} %pack_weights.2), channel_id=1, source_target_pairs={{0,2},{2,0},{1,3},{3,1},{4,6},{6,4},{5,7},{7,5},{8,10},{10,8},{9,1... | collective-permute-start | bytes 2408456 | tf_op jit(solution)/shard_map/ppermute | solution.py:308
  5.7 2.5 %collective-permute-start = (bf16[512,256]{1,0:T(8,128)(2,1)S(1)}, bf16[512,256]{1,0:T(8,128)(2,1)S(1)}, u32[]{:S(2)}, u32[]{:S(2)}) collective-permute-start(bf16[512,256]{1,0:T(8,128)(2,1)S(1)} %get-tuple-element.113), channel_id=1, source_target_pairs={{0,0},{1,2},{2,1},{3,3},{4,4},{5,6},{6,5},{7,7},{8,8},{9,10},{10,9... | collective-permute-start | bytes 786440 | tf_op jit(solution)/shard_map/ppermute | solution.py:292
  8.2 0.0 collective-permute-start.1
  8.3 0.0 copy-start.15
  8.3 0.7 copy-done.15
  9.0 0.0 copy-done.14
  9.0 0.0 copy-start.11
  9.0 2.2 %pick_rows.1 = (bf16[272,256]{1,0:T(8,128)(2,1)S(1)}, bf16[272,256]{1,0:T(8,128)(2,1)S(1)}, bf16[272,256]{1,0:T(8,128)(2,1)S(1)}, bf16[272,256]{1,0:T(8,128)(2,1)S(1)}) custom-call(s32[1]{0:T(128)} %bitcast.me_ref, s32[3,512]{1,0:T(4,128)S(1)} %pad_add_fusion.bnd_ref, bf16[1024,256]{1,0:T(8,128)(2,1)S(1)} %bitcast.30), custom_call_target="tpu_custom_call" | custom-call | flops 8589934592 | bytes 1 | tf_op jit(solution)/shard_map/pick_rows/pallas_call | solution.py:115
  11.3 0.0 copy-start.10
  11.3 1.8 %collective-permute-start.3 = (bf16[272,256]{1,0:T(8,128)(2,1)S(1)}, bf16[272,256]{1,0:T(8,128)(2,1)S(1)}, u32[]{:S(2)}, u32[]{:S(2)}) collective-permute-start(bf16[272,256]{1,0:T(8,128)(2,1)S(1)} %get-tuple-element.66), channel_id=1, source_target_pairs={{0,4},{4,8},{8,12},{12,0},{1,5},{5,9},{9,13},{13,1},{2,6},{6,10},{... | collective-permute-start | bytes 417800 | tf_op jit(solution)/shard_map/ppermute | solution.py:393
  13.1 2.3 %collective-permute-start.4 = (bf16[272,256]{1,0:T(8,128)(2,1)S(1)}, bf16[272,256]{1,0:T(8,128)(2,1)S(1)}, u32[]{:S(2)}, u32[]{:S(2)}) collective-permute-start(bf16[272,256]{1,0:T(8,128)(2,1)S(1)} %get-tuple-element.67), channel_id=1, source_target_pairs={{0,8},{4,12},{8,0},{12,4},{1,9},{5,13},{9,1},{13,5},{2,10},{6,14},... | collective-permute-start | bytes 417800 | tf_op jit(solution)/shard_map/ppermute | solution.py:393
  15.4 0.1 fusion.5
  15.6 11.3 %collective-permute-done = bf16[512,256]{1,0:T(8,128)(2,1)S(1)} collective-permute-done((bf16[512,256]{1,0:T(8,128)(2,1)S(1)}, bf16[512,256]{1,0:T(8,128)(2,1)S(1)}, u32[]{:S(2)}, u32[]{:S(2)}) %collective-permute-start) | collective-permute-done | bytes 262176 | tf_op jit(solution)/shard_map/ppermute | solution.py:292
  26.8 3.6 %collective-permute-start.5 = (bf16[272,256]{1,0:T(8,128)(2,1)S(1)}, bf16[272,256]{1,0:T(8,128)(2,1)S(1)}, u32[]{:S(2)}, u32[]{:S(2)}) collective-permute-start(bf16[272,256]{1,0:T(8,128)(2,1)S(1)} %get-tuple-element.68), channel_id=1, source_target_pairs={{0,12},{4,0},{8,4},{12,8},{1,13},{5,1},{9,5},{13,9},{2,14},{6,2},{... | collective-permute-start | bytes 417800 | tf_op jit(solution)/shard_map/ppermute | solution.py:393
  30.4 2.8 %pack_weights.3 = (bf16[784,256]{1,0:T(8,128)(2,1)}, bf16[784,256]{1,0:T(8,128)(2,1)}) custom-call(s32[1]{0:T(128)} %bitcast.4.core_ref, bf16[2,256]{1,0:T(2,128)(2,1)} %bias.6, bf16[2,256]{1,0:T(2,128)(2,1)} %bias.7, bf16[2,512,256]{2,1,0:T(8,128)(2,1)} %ws_hbm.6, bf16[2,512,256]{2,1,0:T(8,128)(2,1)} %wd_hbm.6, bf16[2,256,512]{2,1,0:T(8,128)(2,1)} %w2_hbm.6, ...), custom_call_target="tpu_custom_call" | custom-call | flops 4294967296 | bytes 1 | tf_op jit(solution)/shard_map/pack_weights/pallas_call | solution.py:352
  33.3 0.1 collective-permute-start.10
  33.4 0.1 maximum_select_fusion.own
  33.5 0.6 collective-permute-start.8
  34.1 1.4 %collective-permute-start.9 = (bf16[512,512]{1,0:T(8,128)(2,1)S(1)}, bf16[512,512]{1,0:T(8,128)(2,1)S(1)}, u32[]{:S(2)}, u32[]{:S(2)}) collective-permute-start(bf16[512,512]{1,0:T(8,128)(2,1)S(1)} %maximum_select_fusion.own), channel_id=1, source_target_pairs={{1,4},{0,13},{5,8},{4,1},{9,12},{8,5},{13,0},{12,9},{3,6},{2,15},{... | collective-permute-start | bytes 1572872 | tf_op jit(solution)/shard_map/ppermute | solution.py:319
  35.4 0.7 add_force.1
  36.2 0.0 copy-start.8
  36.2 0.0 copy-start.2
  36.2 6.3 %collective-permute-start.6 = (bf16[512,256]{1,0:T(8,128)(2,1)S(1)}, bf16[512,256]{1,0:T(8,128)(2,1)S(1)}, u32[]{:S(2)}, u32[]{:S(2)}) collective-permute-start(bf16[512,256]{1,0:T(8,128)(2,1)S(1)} %get-tuple-element.77), channel_id=1, source_target_pairs={{0,0},{1,2},{2,1},{3,3},{4,4},{5,6},{6,5},{7,7},{8,8},{9,10},{10,9... | collective-permute-start | bytes 786440 | tf_op jit(solution)/shard_map/ppermute | solution.py:292
  42.5 0.0 collective-permute-start.7
  42.6 4.3 %collective-permute-done.6 = bf16[512,256]{1,0:T(8,128)(2,1)S(1)} collective-permute-done((bf16[512,256]{1,0:T(8,128)(2,1)S(1)}, bf16[512,256]{1,0:T(8,128)(2,1)S(1)}, u32[]{:S(2)}, u32[]{:S(2)}) %collective-permute-start.6) | collective-permute-done | bytes 262176 | tf_op jit(solution)/shard_map/ppermute | solution.py:292
  46.9 1.8 %collective-permute-done.7 = bf16[512,256]{1,0:T(8,128)(2,1)S(1)} collective-permute-done((bf16[512,256]{1,0:T(8,128)(2,1)S(1)}, bf16[512,256]{1,0:T(8,128)(2,1)S(1)}, u32[]{:S(2)}, u32[]{:S(2)}) %collective-permute-start.7) | collective-permute-done | bytes 262176 | tf_op jit(solution)/shard_map/ppermute | solution.py:293
  48.7 0.1 maximum_select_fusion.1.own
  48.8 1.5 %collective-permute-start.12 = (bf16[512,512]{1,0:T(8,128)(2,1)S(1)}, bf16[512,512]{1,0:T(8,128)(2,1)S(1)}, u32[]{:S(2)}, u32[]{:S(2)}) collective-permute-start(bf16[512,512]{1,0:T(8,128)(2,1)S(1)} %maximum_select_fusion.1.own), channel_id=1, source_target_pairs={{0,1},{1,0},{2,3},{3,2},{4,5},{5,4},{6,7},{7,6},{8,9},{9,8},{10,11... | collective-permute-start | bytes 1572872 | tf_op jit(solution)/shard_map/ppermute | solution.py:308
  50.4 1.9 %collective-permute-start.13 = (bf16[512,512]{1,0:T(8,128)(2,1)S(1)}, bf16[512,512]{1,0:T(8,128)(2,1)S(1)}, u32[]{:S(2)}, u32[]{:S(2)}) collective-permute-start(bf16[512,512]{1,0:T(8,128)(2,1)S(1)} %maximum_select_fusion.1.own), channel_id=1, source_target_pairs={{1,4},{5,8},{4,1},{9,12},{8,5},{12,9},{3,6},{7,10},{6,3},{11,14},{... | collective-permute-start | bytes 1572872 | tf_op jit(solution)/shard_map/ppermute | solution.py:319
  52.3 6.3 %graph_layer.4.own = bf16[512,512]{1,0:T(8,128)(2,1)S(1)} custom-call(s32[1]{0:T(128)} %bitcast.4.core_ref, s32[4096]{0:T(1024)S(1)} %bitcast.34, bf16[512,512]{1,0:T(8,128)(2,1)S(1)} %maximum_select_fusion.own, bf16[512,512]{1,0:T(8,128)(2,1)S(1)} %collective-permute-done.8.sib, bf16[512,512]{1,0:T(8,128)(2,1)S(1)} %collective-permute-done.9.rim, ...), custom_call_target="tpu_custom_call" | custom-call | flops 8589934592 | bytes 2621440 | tf_op jit(solution)/shard_map/graph_layer/pallas_call | solution.py:254
  58.6 0.1 collective-permute-start.14
  58.7 1.8 %collective-permute-start.15 = (bf16[512,512]{1,0:T(8,128)(2,1)S(1)}, bf16[512,512]{1,0:T(8,128)(2,1)S(1)}, u32[]{:S(2)}, u32[]{:S(2)}) collective-permute-start(bf16[512,512]{1,0:T(8,128)(2,1)S(1)} %graph_layer.4.own), channel_id=1, source_target_pairs={{1,4},{0,13},{5,8},{4,1},{9,12},{8,5},{13,0},{12,9},{3,6},{2,15},{... | collective-permute-start | bytes 1572872 | tf_op jit(solution)/shard_map/ppermute | solution.py:319
  60.5 0.8 collective-permute-start.16
  61.3 1.9 %collective-permute-start.19 = (bf16[784,256]{1,0:T(8,128)(2,1)S(1)}, bf16[784,256]{1,0:T(8,128)(2,1)S(1)}, u32[]{:S(2)}, u32[]{:S(2)}) collective-permute-start(bf16[784,256]{1,0:T(8,128)(2,1)S(1)} %copy-done.17), channel_id=1, source_target_pairs={{0,2},{2,0},{1,3},{3,1},{4,6},{6,4},{5,7},{7,5},{8,10},{10,8},{9,1... | collective-permute-start | bytes 1204232 | tf_op jit(solution)/shard_map/ppermute | solution.py:308
  63.3 6.3 %graph_layer.5.own = bf16[512,512]{1,0:T(8,128)(2,1)S(1)} custom-call(s32[1]{0:T(128)} %bitcast.4.core_ref, s32[4096]{0:T(1024)S(1)} %bitcast.32, bf16[512,512]{1,0:T(8,128)(2,1)S(1)} %maximum_select_fusion.1.own, bf16[512,512]{1,0:T(8,128)(2,1)S(1)} %collective-permute-done.12.sib, bf16[512,512]{1,0:T(8,128)(2,1)S(1)} %collective-permute-done.13.rim, ...), custom_call_target="tpu_custom_call" | custom-call | flops 8589934592 | bytes 2621440 | tf_op jit(solution)/shard_map/graph_layer/pallas_call | solution.py:254
  69.6 0.4 collective-permute-start.20
  70.0 2.7 %collective-permute-start.21 = (bf16[512,512]{1,0:T(8,128)(2,1)S(1)}, bf16[512,512]{1,0:T(8,128)(2,1)S(1)}, u32[]{:S(2)}, u32[]{:S(2)}) collective-permute-start(bf16[512,512]{1,0:T(8,128)(2,1)S(1)} %graph_layer.5.own), channel_id=1, source_target_pairs={{1,4},{5,8},{4,1},{9,12},{8,5},{12,9},{3,6},{7,10},{6,3},{11,14},{... | collective-permute-start | bytes 1572872 | tf_op jit(solution)/shard_map/ppermute | solution.py:319
  72.7 6.3 %graph_layer.6 = (bf16[512,256]{1,0:T(8,128)(2,1)S(1)}, bf16[512,256]{1,0:T(8,128)(2,1)S(1)}) custom-call(s32[1]{0:T(128)} %bitcast.4.core_ref, s32[4096]{0:T(1024)S(1)} %bitcast.35, bf16[512,512]{1,0:T(8,128)(2,1)S(1)} %graph_layer.4.own, bf16[512,512]{1,0:T(8,128)(2,1)S(1)} %collective-permute-done.14.sib, ...), custom_call_target="tpu_custom_call" | custom-call | flops 8589934592 | bytes 2621440 | tf_op jit(solution)/shard_map/graph_layer/pallas_call | solution.py:254
  79.0 2.4 %collective-permute-start.22 = (bf16[784,256]{1,0:T(8,128)(2,1)S(1)}, bf16[784,256]{1,0:T(8,128)(2,1)S(1)}, u32[]{:S(2)}, u32[]{:S(2)}) collective-permute-start(bf16[784,256]{1,0:T(8,128)(2,1)S(1)} %collective-permute-done.19.near_w), channel_id=1, source_target_pairs={{0,1},{1,0},{2,3},{3,2},{4,5},{5,4},{6,7},{7,6},{8,9},{9,8},{10,11... | collective-permute-start | bytes 1204232 | tf_op jit(solution)/shard_map/ppermute | solution.py:308
  81.5 0.0 collective-permute-start.18
  81.5 3.3 %collective-permute-start.17 = (bf16[512,256]{1,0:T(8,128)(2,1)S(1)}, bf16[512,256]{1,0:T(8,128)(2,1)S(1)}, u32[]{:S(2)}, u32[]{:S(2)}) collective-permute-start(bf16[512,256]{1,0:T(8,128)(2,1)S(1)} %get-tuple-element.100), channel_id=1, source_target_pairs={{0,0},{1,2},{2,1},{3,3},{4,4},{5,6},{6,5},{7,7},{8,8},{9,10},{10,9... | collective-permute-start | bytes 786440 | tf_op jit(solution)/shard_map/ppermute | solution.py:298
  84.8 6.3 %graph_layer.7 = (bf16[512,256]{1,0:T(8,128)(2,1)S(1)}, bf16[512,256]{1,0:T(8,128)(2,1)S(1)}) custom-call(s32[1]{0:T(128)} %bitcast.4.core_ref, s32[4096]{0:T(1024)S(1)} %bitcast.33, bf16[512,512]{1,0:T(8,128)(2,1)S(1)} %graph_layer.5.own, bf16[512,512]{1,0:T(8,128)(2,1)S(1)} %collective-permute-done.20.sib, ...), custom_call_target="tpu_custom_call" | custom-call | flops 8589934592 | bytes 2621440 | tf_op jit(solution)/shard_map/graph_layer/pallas_call | solution.py:254
  91.1 2.3 %collective-permute-start.23 = (bf16[512,256]{1,0:T(8,128)(2,1)S(1)}, bf16[512,256]{1,0:T(8,128)(2,1)S(1)}, u32[]{:S(2)}, u32[]{:S(2)}) collective-permute-start(bf16[512,256]{1,0:T(8,128)(2,1)S(1)} %get-tuple-element.107), channel_id=1, source_target_pairs={{0,0},{1,2},{2,1},{3,3},{4,4},{5,6},{6,5},{7,7},{8,8},{9,10},{10,9... | collective-permute-start | bytes 786440 | tf_op jit(solution)/shard_map/ppermute | solution.py:298
  93.4 0.0 collective-permute-start.24
  93.5 1.0 maximum_select_fusion.2
  94.5 7.0 %collective-permute-done.23 = bf16[512,256]{1,0:T(8,128)(2,1)S(1)} collective-permute-done((bf16[512,256]{1,0:T(8,128)(2,1)S(1)}, bf16[512,256]{1,0:T(8,128)(2,1)S(1)}, u32[]{:S(2)}, u32[]{:S(2)}) %collective-permute-start.23) | collective-permute-done | bytes 262176 | tf_op jit(solution)/shard_map/ppermute | solution.py:298
  101.5 1.0 maximum_select_fusion.3
  (60 shorter events, 0.2 us)
Async XLA Ops:
  0.6 5.0 %copy-start = (bf16[1,1024,256]{2,1,0:T(8,128)(2,1)S(1)}, bf16[1,1024,256]{2,1,0:T(8,128)(2,1)}, u32[]{:S(2)}) copy-start(bf16[1,1024,256]{2,1,0:T(8,128)(2,1)} %param.17) | copy-start | bytes 1572868
  3.6 29.7 %collective-permute-start.2 = (bf16[1568,256]{1,0:T(8,128)(2,1)}, bf16[1568,256]{1,0:T(8,128)(2,1)S(1)}, u32[]{:S(2)}, u32[]{:S(2)}) collective-permute-start(bf16[1568,256]{1,0:T(8,128)(2,1)} %pack_weights.2), channel_id=1, source_target_pairs={{0,2},{2,0},{1,3},{3,1},{4,6},{6,4},{5,7},{7,5},{8,10},{10,8},{9,1... | collective-permute-start | bytes 2408456 | tf_op jit(solution)/shard_map/ppermute | solution.py:308
  5.7 2.6 %copy-start.16 = (s32[512]{0:T(512)S(1)}, s32[512]{0:T(512)}, u32[]{:S(2)}) copy-start(s32[512]{0:T(512)} %param.23) | copy-start | bytes 6148
  5.7 21.1 %collective-permute-start = (bf16[512,256]{1,0:T(8,128)(2,1)S(1)}, bf16[512,256]{1,0:T(8,128)(2,1)S(1)}, u32[]{:S(2)}, u32[]{:S(2)}) collective-permute-start(bf16[512,256]{1,0:T(8,128)(2,1)S(1)} %get-tuple-element.113), channel_id=1, source_target_pairs={{0,0},{1,2},{2,1},{3,3},{4,4},{5,6},{6,5},{7,7},{8,8},{9,10},{10,9... | collective-permute-start | bytes 786440 | tf_op jit(solution)/shard_map/ppermute | solution.py:292
  8.2 22.2 %collective-permute-start.1 = (bf16[512,256]{1,0:T(8,128)(2,1)S(1)}, bf16[512,256]{1,0:T(8,128)(2,1)S(1)}, u32[]{:S(2)}, u32[]{:S(2)}) collective-permute-start(bf16[512,256]{1,0:T(8,128)(2,1)S(1)} %get-tuple-element.112), channel_id=1, source_target_pairs={{0,1},{1,3},{2,0},{3,2},{4,5},{5,7},{6,4},{7,6},{8,9},{9,11},{10,8... | collective-permute-start | bytes 786440 | tf_op jit(solution)/shard_map/ppermute | solution.py:293
  8.3 0.7 copy-start.15
  8.3 0.7 copy-start.14
  9.0 6.4 %copy-start.12 = (s32[1024]{0:T(1024)S(1)}, s32[1024]{0:T(1024)}, u32[]{:S(2)}) copy-start(s32[1024]{0:T(1024)} %param.20) | copy-start | bytes 12292
  9.0 6.4 %copy-start.13 = (s32[1024]{0:T(1024)S(1)}, s32[1024]{0:T(1024)}, u32[]{:S(2)}) copy-start(s32[1024]{0:T(1024)} %param.22) | copy-start | bytes 12292
  9.0 6.5 %copy-start.11 = (s32[1024,8]{0,1:T(8,128)S(1)}, s32[1024,8]{0,1:T(8,128)}, u32[]{:S(2)}) copy-start(s32[1024,8]{0,1:T(8,128)} %param.19) | copy-start | bytes 98308
  11.3 4.3 %copy-start.10 = (s32[1024,8]{0,1:T(8,128)S(1)}, s32[1024,8]{0,1:T(8,128)}, u32[]{:S(2)}) copy-start(s32[1024,8]{0,1:T(8,128)} %param.21) | copy-start | bytes 98308
  11.3 22.0 %collective-permute-start.3 = (bf16[272,256]{1,0:T(8,128)(2,1)S(1)}, bf16[272,256]{1,0:T(8,128)(2,1)S(1)}, u32[]{:S(2)}, u32[]{:S(2)}) collective-permute-start(bf16[272,256]{1,0:T(8,128)(2,1)S(1)} %get-tuple-element.66), channel_id=1, source_target_pairs={{0,4},{4,8},{8,12},{12,0},{1,5},{5,9},{9,13},{13,1},{2,6},{6,10},{... | collective-permute-start | bytes 417800 | tf_op jit(solution)/shard_map/ppermute | solution.py:393
  13.1 20.2 %collective-permute-start.4 = (bf16[272,256]{1,0:T(8,128)(2,1)S(1)}, bf16[272,256]{1,0:T(8,128)(2,1)S(1)}, u32[]{:S(2)}, u32[]{:S(2)}) collective-permute-start(bf16[272,256]{1,0:T(8,128)(2,1)S(1)} %get-tuple-element.67), channel_id=1, source_target_pairs={{0,8},{4,12},{8,0},{12,4},{1,9},{5,13},{9,1},{13,5},{2,10},{6,14},... | collective-permute-start | bytes 417800 | tf_op jit(solution)/shard_map/ppermute | solution.py:393
  26.8 6.4 %collective-permute-start.5 = (bf16[272,256]{1,0:T(8,128)(2,1)S(1)}, bf16[272,256]{1,0:T(8,128)(2,1)S(1)}, u32[]{:S(2)}, u32[]{:S(2)}) collective-permute-start(bf16[272,256]{1,0:T(8,128)(2,1)S(1)} %get-tuple-element.68), channel_id=1, source_target_pairs={{0,12},{4,0},{8,4},{12,8},{1,13},{5,1},{9,5},{13,9},{2,14},{6,2},{... | collective-permute-start | bytes 417800 | tf_op jit(solution)/shard_map/ppermute | solution.py:393
  33.3 2.1 %copy-start.1 = (bf16[1,1024,256]{2,1,0:T(8,128)(2,1)S(1)}, bf16[1,1024,256]{2,1,0:T(8,128)(2,1)}, u32[]{:S(2)}) copy-start(bf16[1,1024,256]{2,1,0:T(8,128)(2,1)} %param.18) | copy-start | bytes 1572868
  33.3 19.0 %collective-permute-start.10 = (bf16[1568,256]{1,0:T(8,128)(2,1)S(1)}, bf16[1568,256]{1,0:T(8,128)(2,1)S(1)}, u32[]{:S(2)}, u32[]{:S(2)}) collective-permute-start(bf16[1568,256]{1,0:T(8,128)(2,1)S(1)} %collective-permute-done.2.near_w), channel_id=1, source_target_pairs={{0,1},{1,0},{2,3},{3,2},{4,5},{5,4},{6,7},{7,6},{8,9},{9,8},{10,11... | collective-permute-start | bytes 2408456 | tf_op jit(solution)/shard_map/ppermute | solution.py:308
  33.5 15.1 %collective-permute-start.8 = (bf16[512,512]{1,0:T(8,128)(2,1)S(1)}, bf16[512,512]{1,0:T(8,128)(2,1)S(1)}, u32[]{:S(2)}, u32[]{:S(2)}) collective-permute-start(bf16[512,512]{1,0:T(8,128)(2,1)S(1)} %maximum_select_fusion.own), channel_id=1, source_target_pairs={{0,1},{1,0},{2,3},{3,2},{4,5},{5,4},{6,7},{7,6},{8,9},{9,8},{10,11... | collective-permute-start | bytes 1572872 | tf_op jit(solution)/shard_map/ppermute | solution.py:308
  34.1 14.6 %collective-permute-start.9 = (bf16[512,512]{1,0:T(8,128)(2,1)S(1)}, bf16[512,512]{1,0:T(8,128)(2,1)S(1)}, u32[]{:S(2)}, u32[]{:S(2)}) collective-permute-start(bf16[512,512]{1,0:T(8,128)(2,1)S(1)} %maximum_select_fusion.own), channel_id=1, source_target_pairs={{1,4},{0,13},{5,8},{4,1},{9,12},{8,5},{13,0},{12,9},{3,6},{2,15},{... | collective-permute-start | bytes 1572872 | tf_op jit(solution)/shard_map/ppermute | solution.py:319
  35.4 11.4 %copy-start.18 = (bf16[784,256]{1,0:T(8,128)(2,1)S(1)}, bf16[784,256]{1,0:T(8,128)(2,1)}, u32[]{:S(2)}) copy-start(bf16[784,256]{1,0:T(8,128)(2,1)} %get-tuple-element.89) | copy-start | bytes 1204228
  35.4 16.9 %copy-start.4 = (bf16[2,256,512]{2,1,0:T(8,128)(2,1)S(1)}, bf16[2,256,512]{2,1,0:T(8,128)(2,1)}, u32[]{:S(2)}) copy-start(bf16[2,256,512]{2,1,0:T(8,128)(2,1)} %w2_hbm.6) | copy-start | bytes 1572868
  36.2 16.2 %copy-start.8 = (bf16[2,256]{1,0:T(2,128)(2,1)S(1)}, bf16[2,256]{1,0:T(2,128)(2,1)}, u32[]{:S(2)}) copy-start(bf16[2,256]{1,0:T(2,128)(2,1)} %bias.6) | copy-start | bytes 3076
  36.2 16.2 %copy-start.2 = (bf16[2,512,256]{2,1,0:T(8,128)(2,1)S(1)}, bf16[2,512,256]{2,1,0:T(8,128)(2,1)}, u32[]{:S(2)}) copy-start(bf16[2,512,256]{2,1,0:T(8,128)(2,1)} %ws_hbm.6) | copy-start | bytes 1572868
  36.2 16.2 %copy-start.3 = (bf16[2,512,256]{2,1,0:T(8,128)(2,1)S(1)}, bf16[2,512,256]{2,1,0:T(8,128)(2,1)}, u32[]{:S(2)}) copy-start(bf16[2,512,256]{2,1,0:T(8,128)(2,1)} %wd_hbm.6) | copy-start | bytes 1572868
  36.2 10.7 %collective-permute-start.6 = (bf16[512,256]{1,0:T(8,128)(2,1)S(1)}, bf16[512,256]{1,0:T(8,128)(2,1)S(1)}, u32[]{:S(2)}, u32[]{:S(2)}) collective-permute-start(bf16[512,256]{1,0:T(8,128)(2,1)S(1)} %get-tuple-element.77), channel_id=1, source_target_pairs={{0,0},{1,2},{2,1},{3,3},{4,4},{5,6},{6,5},{7,7},{8,8},{9,10},{10,9... | collective-permute-start | bytes 786440 | tf_op jit(solution)/shard_map/ppermute | solution.py:292
  42.5 6.1 %collective-permute-start.7 = (bf16[512,256]{1,0:T(8,128)(2,1)S(1)}, bf16[512,256]{1,0:T(8,128)(2,1)S(1)}, u32[]{:S(2)}, u32[]{:S(2)}) collective-permute-start(bf16[512,256]{1,0:T(8,128)(2,1)S(1)} %get-tuple-element.78), channel_id=1, source_target_pairs={{0,1},{1,3},{2,0},{3,2},{4,5},{5,7},{6,4},{7,6},{8,9},{9,11},{10,8... | collective-permute-start | bytes 786440 | tf_op jit(solution)/shard_map/ppermute | solution.py:293
  46.9 13.6 %collective-permute-start.11 = (bf16[784,256]{1,0:T(8,128)(2,1)S(1)}, bf16[784,256]{1,0:T(8,128)(2,1)S(1)}, u32[]{:S(2)}, u32[]{:S(2)}) collective-permute-start(bf16[784,256]{1,0:T(8,128)(2,1)S(1)} %copy-done.18), channel_id=1, source_target_pairs={{0,2},{2,0},{1,3},{3,1},{4,6},{6,4},{5,7},{7,5},{8,10},{10,8},{9,1... | collective-permute-start | bytes 1204232 | tf_op jit(solution)/shard_map/ppermute | solution.py:308
  48.8 12.5 %copy-start.17 = (bf16[784,256]{1,0:T(8,128)(2,1)S(1)}, bf16[784,256]{1,0:T(8,128)(2,1)}, u32[]{:S(2)}) copy-start(bf16[784,256]{1,0:T(8,128)(2,1)} %get-tuple-element.102) | copy-start | bytes 1204228
  48.8 14.5 %copy-start.5 = (bf16[2,512,256]{2,1,0:T(8,128)(2,1)S(1)}, bf16[2,512,256]{2,1,0:T(8,128)(2,1)}, u32[]{:S(2)}) copy-start(bf16[2,512,256]{2,1,0:T(8,128)(2,1)} %ws_hbm.7) | copy-start | bytes 1572868
  48.8 14.4 %copy-start.6 = (bf16[2,512,256]{2,1,0:T(8,128)(2,1)S(1)}, bf16[2,512,256]{2,1,0:T(8,128)(2,1)}, u32[]{:S(2)}) copy-start(bf16[2,512,256]{2,1,0:T(8,128)(2,1)} %wd_hbm.7) | copy-start | bytes 1572868
  48.8 14.4 %copy-start.7 = (bf16[2,256,512]{2,1,0:T(8,128)(2,1)S(1)}, bf16[2,256,512]{2,1,0:T(8,128)(2,1)}, u32[]{:S(2)}) copy-start(bf16[2,256,512]{2,1,0:T(8,128)(2,1)} %w2_hbm.7) | copy-start | bytes 1572868
  48.8 14.4 %copy-start.9 = (bf16[2,256]{1,0:T(2,128)(2,1)S(1)}, bf16[2,256]{1,0:T(2,128)(2,1)}, u32[]{:S(2)}) copy-start(bf16[2,256]{1,0:T(2,128)(2,1)} %bias.7) | copy-start | bytes 3076
  48.8 12.5 %collective-permute-start.12 = (bf16[512,512]{1,0:T(8,128)(2,1)S(1)}, bf16[512,512]{1,0:T(8,128)(2,1)S(1)}, u32[]{:S(2)}, u32[]{:S(2)}) collective-permute-start(bf16[512,512]{1,0:T(8,128)(2,1)S(1)} %maximum_select_fusion.1.own), channel_id=1, source_target_pairs={{0,1},{1,0},{2,3},{3,2},{4,5},{5,4},{6,7},{7,6},{8,9},{9,8},{10,11... | collective-permute-start | bytes 1572872 | tf_op jit(solution)/shard_map/ppermute | solution.py:308
  50.4 12.9 %collective-permute-start.13 = (bf16[512,512]{1,0:T(8,128)(2,1)S(1)}, bf16[512,512]{1,0:T(8,128)(2,1)S(1)}, u32[]{:S(2)}, u32[]{:S(2)}) collective-permute-start(bf16[512,512]{1,0:T(8,128)(2,1)S(1)} %maximum_select_fusion.1.own), channel_id=1, source_target_pairs={{1,4},{5,8},{4,1},{9,12},{8,5},{12,9},{3,6},{7,10},{6,3},{11,14},{... | collective-permute-start | bytes 1572872 | tf_op jit(solution)/shard_map/ppermute | solution.py:319
  58.6 14.0 %collective-permute-start.14 = (bf16[512,512]{1,0:T(8,128)(2,1)S(1)}, bf16[512,512]{1,0:T(8,128)(2,1)S(1)}, u32[]{:S(2)}, u32[]{:S(2)}) collective-permute-start(bf16[512,512]{1,0:T(8,128)(2,1)S(1)} %graph_layer.4.own), channel_id=1, source_target_pairs={{0,1},{1,0},{2,3},{3,2},{4,5},{5,4},{6,7},{7,6},{8,9},{9,8},{10,11... | collective-permute-start | bytes 1572872 | tf_op jit(solution)/shard_map/ppermute | solution.py:308
  58.7 14.0 %collective-permute-start.15 = (bf16[512,512]{1,0:T(8,128)(2,1)S(1)}, bf16[512,512]{1,0:T(8,128)(2,1)S(1)}, u32[]{:S(2)}, u32[]{:S(2)}) collective-permute-start(bf16[512,512]{1,0:T(8,128)(2,1)S(1)} %graph_layer.4.own), channel_id=1, source_target_pairs={{1,4},{0,13},{5,8},{4,1},{9,12},{8,5},{13,0},{12,9},{3,6},{2,15},{... | collective-permute-start | bytes 1572872 | tf_op jit(solution)/shard_map/ppermute | solution.py:319
  60.5 9.5 %collective-permute-start.16 = (bf16[784,256]{1,0:T(8,128)(2,1)S(1)}, bf16[784,256]{1,0:T(8,128)(2,1)S(1)}, u32[]{:S(2)}, u32[]{:S(2)}) collective-permute-start(bf16[784,256]{1,0:T(8,128)(2,1)S(1)} %collective-permute-done.11.near_w), channel_id=1, source_target_pairs={{0,1},{1,0},{2,3},{3,2},{4,5},{5,4},{6,7},{7,6},{8,9},{9,8},{10,11... | collective-permute-start | bytes 1204232 | tf_op jit(solution)/shard_map/ppermute | solution.py:308
  61.3 17.7 %collective-permute-start.19 = (bf16[784,256]{1,0:T(8,128)(2,1)S(1)}, bf16[784,256]{1,0:T(8,128)(2,1)S(1)}, u32[]{:S(2)}, u32[]{:S(2)}) collective-permute-start(bf16[784,256]{1,0:T(8,128)(2,1)S(1)} %copy-done.17), channel_id=1, source_target_pairs={{0,2},{2,0},{1,3},{3,1},{4,6},{6,4},{5,7},{7,5},{8,10},{10,8},{9,1... | collective-permute-start | bytes 1204232 | tf_op jit(solution)/shard_map/ppermute | solution.py:308
  69.6 15.2 %collective-permute-start.20 = (bf16[512,512]{1,0:T(8,128)(2,1)S(1)}, bf16[512,512]{1,0:T(8,128)(2,1)S(1)}, u32[]{:S(2)}, u32[]{:S(2)}) collective-permute-start(bf16[512,512]{1,0:T(8,128)(2,1)S(1)} %graph_layer.5.own), channel_id=1, source_target_pairs={{0,1},{1,0},{2,3},{3,2},{4,5},{5,4},{6,7},{7,6},{8,9},{9,8},{10,11... | collective-permute-start | bytes 1572872 | tf_op jit(solution)/shard_map/ppermute | solution.py:308
  70.0 14.8 %collective-permute-start.21 = (bf16[512,512]{1,0:T(8,128)(2,1)S(1)}, bf16[512,512]{1,0:T(8,128)(2,1)S(1)}, u32[]{:S(2)}, u32[]{:S(2)}) collective-permute-start(bf16[512,512]{1,0:T(8,128)(2,1)S(1)} %graph_layer.5.own), channel_id=1, source_target_pairs={{1,4},{5,8},{4,1},{9,12},{8,5},{12,9},{3,6},{7,10},{6,3},{11,14},{... | collective-permute-start | bytes 1572872 | tf_op jit(solution)/shard_map/ppermute | solution.py:319
  79.0 5.8 %collective-permute-start.22 = (bf16[784,256]{1,0:T(8,128)(2,1)S(1)}, bf16[784,256]{1,0:T(8,128)(2,1)S(1)}, u32[]{:S(2)}, u32[]{:S(2)}) collective-permute-start(bf16[784,256]{1,0:T(8,128)(2,1)S(1)} %collective-permute-done.19.near_w), channel_id=1, source_target_pairs={{0,1},{1,0},{2,3},{3,2},{4,5},{5,4},{6,7},{7,6},{8,9},{9,8},{10,11... | collective-permute-start | bytes 1204232 | tf_op jit(solution)/shard_map/ppermute | solution.py:308
  81.5 12.0 %collective-permute-start.18 = (bf16[512,256]{1,0:T(8,128)(2,1)S(1)}, bf16[512,256]{1,0:T(8,128)(2,1)S(1)}, u32[]{:S(2)}, u32[]{:S(2)}) collective-permute-start(bf16[512,256]{1,0:T(8,128)(2,1)S(1)} %get-tuple-element.101), channel_id=1, source_target_pairs={{0,2},{1,0},{2,3},{3,1},{4,6},{5,4},{6,7},{7,5},{8,10},{9,8},{10,1... | collective-permute-start | bytes 786440 | tf_op jit(solution)/shard_map/ppermute | solution.py:299
  81.5 12.0 %collective-permute-start.17 = (bf16[512,256]{1,0:T(8,128)(2,1)S(1)}, bf16[512,256]{1,0:T(8,128)(2,1)S(1)}, u32[]{:S(2)}, u32[]{:S(2)}) collective-permute-start(bf16[512,256]{1,0:T(8,128)(2,1)S(1)} %get-tuple-element.100), channel_id=1, source_target_pairs={{0,0},{1,2},{2,1},{3,3},{4,4},{5,6},{6,5},{7,7},{8,8},{9,10},{10,9... | collective-permute-start | bytes 786440 | tf_op jit(solution)/shard_map/ppermute | solution.py:298
  91.1 10.3 %collective-permute-start.23 = (bf16[512,256]{1,0:T(8,128)(2,1)S(1)}, bf16[512,256]{1,0:T(8,128)(2,1)S(1)}, u32[]{:S(2)}, u32[]{:S(2)}) collective-permute-start(bf16[512,256]{1,0:T(8,128)(2,1)S(1)} %get-tuple-element.107), channel_id=1, source_target_pairs={{0,0},{1,2},{2,1},{3,3},{4,4},{5,6},{6,5},{7,7},{8,8},{9,10},{10,9... | collective-permute-start | bytes 786440 | tf_op jit(solution)/shard_map/ppermute | solution.py:298
  93.4 8.0 %collective-permute-start.24 = (bf16[512,256]{1,0:T(8,128)(2,1)S(1)}, bf16[512,256]{1,0:T(8,128)(2,1)S(1)}, u32[]{:S(2)}, u32[]{:S(2)}) collective-permute-start(bf16[512,256]{1,0:T(8,128)(2,1)S(1)} %get-tuple-element.108), channel_id=1, source_target_pairs={{0,2},{1,0},{2,3},{3,1},{4,6},{5,4},{6,7},{7,5},{8,10},{9,8},{10,1... | collective-permute-start | bytes 786440 | tf_op jit(solution)/shard_map/ppermute | solution.py:299

commit v16 on v13

--- a/solution.py
+++ b/solution.py
@@ -239,7 +239,7 @@
             outs[1][...] = result[:, :share]
 
 
-def run_layer(layer, place, slots, last, core, idx, own, sib, rim, ws, wd, w2, bias, near_w, far_w):
+def run_layer(layer, place, slots, last, core, idx, own, sib, rim, ws, wd, w2, bias, near_w, far_w, cost=64):
     rows, width = own.shape
     share = width // 2
     chunks = width // LANES
@@ -269,7 +269,7 @@
             pltpu.SemaphoreType.DMA((3,)),
         ],
         compiler_params=pltpu.CompilerParams(vmem_limit_bytes=32 << 20),
-        cost_estimate=pl.CostEstimate(flops=64 * rows * width * width, bytes_accessed=10 * rows * width, transcendentals=0),
+        cost_estimate=pl.CostEstimate(flops=cost * rows * width * width, bytes_accessed=10 * rows * width, transcendentals=0),
         name="graph_layer",
     )(core, idx, own, sib, rim, bias, near_w, far_w, ws, wd, w2)
 
@@ -395,15 +395,13 @@
     rest = tuple(((graph, layer),) for layer in range(1, layers) for graph in (0, 1))
     packs += pack_weights(rest, core1, g_weights, g_b1, r_weights, r_b1)
     g_idx, r_idx = idx[0], idx[1]
-    g_a, g_b, g_idx, r_idx, packs[1:], near_w[0], *landed = after(
-        (g_a, g_b, g_idx, r_idx, packs[1:], near_w[0], *landed)
-    )
+    g_a, g_b, g_idx, r_idx, packs[1:], *landed = after((g_a, g_b, g_idx, r_idx, packs[1:], *landed))
     planet = ordered(core, g_a, g_b, 1)
     g_sib, g_rim = swap(planet, "batch"), rims(planet, True)
     *r_pair, packs[1:] = after((*add_force(part.reshape(1), r_own, landed, cap), packs[1:]))
     r_a, r_b = spread_rows(*r_pair)
     near_w.append(swap(packs[1], "mp"))
-    r_a, r_b, g_sib, g_rim = after((r_a, r_b, g_sib, g_rim))
+    r_a, r_b, g_sib, g_rim, near_w[0] = after((r_a, r_b, g_sib, g_rim, near_w[0]))
     regional, g_idx = after((ordered(core, r_a, r_b, 1), g_idx))
     r_sib, r_rim = swap(regional, "batch"), rims(regional, False)
     far_w = [swap(near_w[0], "batch")]
@@ -413,7 +411,8 @@
         if layer:
             far_w.append(swap(near_w[i], "batch"))
         planet = run_layer(
-            layer, 0, slots, last, core1, g_idx, planet, g_sib, g_rim, g_ws, g_wd, g_w2, g_b1, near_w[i], far_w[i]
+            layer, 0, slots, last, core1, g_idx, planet, g_sib, g_rim, g_ws, g_wd, g_w2, g_b1, near_w[i], far_w[i],
+            8 if layer else 64,
         )
         *planet, core1 = after((*(planet if last else (planet,)), core1))
         if not last:

time: 99.9 us -> 97.8 us (0.979)
  waiting for transfers between devices: 23.4 us -> 20 us
  starting transfers between devices: 36.8 us -> 38.2 us
    ppermute x10, waiting for transfers between devices: 3.79 us -> 0.03 us  [swap(): return lax.ppermute(values, axis, [(0, 1), (1, 0)])]
    ppermute x4, starting transfers between devices: 7.68 us -> 9.66 us  [rims(): return lax.ppermute(own, ('mesh', 'batch'), pairs)]
    ppermute x2, waiting for transfers between devices: 6.97 us -> 5.49 us  [gather_rows(): same = lax.ppermute(a, ('mp', 'batch'), [(0, 0), (1, 2), (2, 1), (3, 3)])]
    ppermute x4, waiting for transfers between devices: 0.91 us -> 2 us  [rims(): return lax.ppermute(own, ('mesh', 'batch'), pairs)]
  transfers between devices with their start and end apart: 25 -> 25, of which waited for: 6 -> 7; matrix products, arithmetic and copies ran while one was open for 1% -> 1% of each run, Pallas kernels for 34% -> 35%
where the time goes in v16:
time: 97.8 us; the launch traced here: 97.4 us
  starting transfers between devices  38.2 us (39%)
  Pallas kernels  33.9 us (35%)
  waiting for transfers between devices  20 us (20%)
  other arithmetic  2.41 us (2%)
  local copies, waits for them, and re-layouts  1.88 us (2%)
  between operations  1.11 us (1%)
    pallas_call x4, Pallas kernels, run_layer(): pl.pallas_call(functools.partial(layer_kernel, layer, place, slots, last)...  25.2 us
    ppermute x4, starting transfers between devices, rims(): return lax.ppermute(own, ('mesh', 'batch'), pairs)  9.66 us
    ppermute x2, starting transfers between devices, spread_rows(): a = lax.ppermute(same, ('mp', 'batch'), [(0, 0), (1, 2), (2, 1), (3, 3)])  9.31 us
    ppermute x10, starting transfers between devices, swap(): return lax.ppermute(values, axis, [(0, 1), (1, 0)])  8.75 us
    pallas_call x2, Pallas kernels, pack_weights(): pl.pallas_call(functools.partial(pack_kernel, plan), out_shape=tuple((jax...  5.74 us
    ppermute x3, waiting for transfers between devices, by_rows(): lax.ppermute(pieces[k], 'mesh', [(i, (i + k) % parts) for i in range(part...  5.67 us
    ppermute x2, starting transfers between devices, gather_rows(): same = lax.ppermute(a, ('mp', 'batch'), [(0, 0), (1, 2), (2, 1), (3, 3)])  5.55 us
    ppermute x2, waiting for transfers between devices, gather_rows(): same = lax.ppermute(a, ('mp', 'batch'), [(0, 0), (1, 2), (2, 1), (3, 3)])  5.49 us
  transfers between devices with their start and end apart: 25, of which 7 were waited for; matrix products, arithmetic and copies ran while one was open for 1% of the time, Pallas kernels for 35%

profile of v16, /device:TPU:1, one launch (start us, length us, event | category | flops | bytes accessed | tf_op | source)
XLA Modules:
  0.0 97.4 jit_solution(11178542111930678470)
XLA Ops:
  0.6 1.1 %dynamic-slice_bitcast_fusion = (bf16[512,256]{1,0:T(8,128)(2,1)S(1)}, bf16[512,256]{1,0:T(8,128)(2,1)S(1)}) fusion(bf16[1,1024,256]{2,1,0:T(8,128)(2,1)} %param.17, s32[]{:T(128)S(6)} %select_n.78, s32[]{:T(128)S(6)} %select_n.77), kind=kLoop, calls=%fused_computation.4 | loop fusion | bytes 1048584 | tf_op jit(solution)/shard_map/dynamic_slice | solution.py:383
  1.7 4.5 %collective-permute-start = (bf16[512,256]{1,0:T(8,128)(2,1)S(1)}, bf16[512,256]{1,0:T(8,128)(2,1)S(1)}, u32[]{:S(2)}, u32[]{:S(2)}) collective-permute-start(bf16[512,256]{1,0:T(8,128)(2,1)S(1)} %get-tuple-element.111), channel_id=1, source_target_pairs={{0,0},{1,2},{2,1},{3,3},{4,4},{5,6},{6,5},{7,7},{8,8},{9,10},{10,9... | collective-permute-start | bytes 786440 | tf_op jit(solution)/shard_map/ppermute | solution.py:292
  6.2 0.0 collective-permute-start.1
  6.3 2.9 %pack_weights.2 = bf16[1568,256]{1,0:T(8,128)(2,1)} custom-call(s32[1]{0:T(128)} %bitcast.4.core_ref, bf16[2,256]{1,0:T(2,128)(2,1)} %bias.6, bf16[2,256]{1,0:T(2,128)(2,1)} %bias.7, bf16[2,512,256]{2,1,0:T(8,128)(2,1)} %ws_hbm.6, bf16[2,512,256]{2,1,0:T(8,128)(2,1)} %wd_hbm.6, bf16[2,256,512]{2,1,0:T(8,128)(2,1)} %w2_hbm.6, bf16[2,512,256]{2,1,0:T(8,128)(2,1)} %ws_hbm.7, ...), custom_call_target="tpu_custom_call" | custom-call | flops 4294967296 | bytes 1 | tf_op jit(solution)/shard_map/pack_weights/pallas_call | solution.py:352
  9.2 0.2 collective-permute-start.9
  9.4 0.7 copy-done.15
  10.0 0.0 copy-done.14
  10.1 2.3 %pick_rows.1 = (bf16[272,256]{1,0:T(8,128)(2,1)S(1)}, bf16[272,256]{1,0:T(8,128)(2,1)S(1)}, bf16[272,256]{1,0:T(8,128)(2,1)S(1)}, bf16[272,256]{1,0:T(8,128)(2,1)S(1)}) custom-call(s32[1]{0:T(128)} %bitcast.me_ref, s32[3,512]{1,0:T(4,128)S(1)} %pad_add_fusion.bnd_ref, bf16[1024,256]{1,0:T(8,128)(2,1)S(1)} %bitcast.33), custom_call_target="tpu_custom_call" | custom-call | flops 8589934592 | bytes 1 | tf_op jit(solution)/shard_map/pick_rows/pallas_call | solution.py:115
  12.4 1.3 %collective-permute-start.2 = (bf16[272,256]{1,0:T(8,128)(2,1)S(1)}, bf16[272,256]{1,0:T(8,128)(2,1)S(1)}, u32[]{:S(2)}, u32[]{:S(2)}) collective-permute-start(bf16[272,256]{1,0:T(8,128)(2,1)S(1)} %get-tuple-element.64), channel_id=1, source_target_pairs={{0,4},{4,8},{8,12},{12,0},{1,5},{5,9},{9,13},{13,1},{2,6},{6,10},{... | collective-permute-start | bytes 417800 | tf_op jit(solution)/shard_map/ppermute | solution.py:392
  13.7 2.3 %collective-permute-start.3 = (bf16[272,256]{1,0:T(8,128)(2,1)S(1)}, bf16[272,256]{1,0:T(8,128)(2,1)S(1)}, u32[]{:S(2)}, u32[]{:S(2)}) collective-permute-start(bf16[272,256]{1,0:T(8,128)(2,1)S(1)} %get-tuple-element.65), channel_id=1, source_target_pairs={{0,8},{4,12},{8,0},{12,4},{1,9},{5,13},{9,1},{13,5},{2,10},{6,14},... | collective-permute-start | bytes 417800 | tf_op jit(solution)/shard_map/ppermute | solution.py:392
  16.1 0.1 fusion.5
  16.2 1.1 %collective-permute-start.4 = (bf16[272,256]{1,0:T(8,128)(2,1)S(1)}, bf16[272,256]{1,0:T(8,128)(2,1)S(1)}, u32[]{:S(2)}, u32[]{:S(2)}) collective-permute-start(bf16[272,256]{1,0:T(8,128)(2,1)S(1)} %get-tuple-element.66), channel_id=1, source_target_pairs={{0,12},{4,0},{8,4},{12,8},{1,13},{5,1},{9,5},{13,9},{2,14},{6,2},{... | collective-permute-start | bytes 417800 | tf_op jit(solution)/shard_map/ppermute | solution.py:392
  17.4 2.8 %pack_weights.3 = (bf16[784,256]{1,0:T(8,128)(2,1)}, bf16[784,256]{1,0:T(8,128)(2,1)}) custom-call(s32[1]{0:T(128)} %bitcast.4.core_ref, bf16[2,256]{1,0:T(2,128)(2,1)} %bias.6, bf16[2,256]{1,0:T(2,128)(2,1)} %bias.7, bf16[2,512,256]{2,1,0:T(8,128)(2,1)} %ws_hbm.6, bf16[2,512,256]{2,1,0:T(8,128)(2,1)} %wd_hbm.6, bf16[2,256,512]{2,1,0:T(8,128)(2,1)} %w2_hbm.6, ...), custom_call_target="tpu_custom_call" | custom-call | flops 4294967296 | bytes 1 | tf_op jit(solution)/shard_map/pack_weights/pallas_call | solution.py:352
  20.2 5.7 %collective-permute-done.3.refs_2_ = bf16[272,256]{1,0:T(8,128)(2,1)S(1)} collective-permute-done((bf16[272,256]{1,0:T(8,128)(2,1)S(1)}, bf16[272,256]{1,0:T(8,128)(2,1)S(1)}, u32[]{:S(2)}, u32[]{:S(2)}) %collective-permute-start.3) | collective-permute-done | bytes 139296 | tf_op jit(solution)/shard_map/ppermute | solution.py:392
  25.9 0.1 maximum_select_fusion.own
  26.0 0.7 collective-permute-start.7
  26.6 3.1 %collective-permute-start.8 = (bf16[512,512]{1,0:T(8,128)(2,1)S(1)}, bf16[512,512]{1,0:T(8,128)(2,1)S(1)}, u32[]{:S(2)}, u32[]{:S(2)}) collective-permute-start(bf16[512,512]{1,0:T(8,128)(2,1)S(1)} %maximum_select_fusion.own), channel_id=1, source_target_pairs={{1,4},{0,13},{5,8},{4,1},{9,12},{8,5},{13,0},{12,9},{3,6},{2,15},{... | collective-permute-start | bytes 1572872 | tf_op jit(solution)/shard_map/ppermute | solution.py:319
  29.8 0.7 add_force.1
  30.5 4.8 %collective-permute-start.5 = (bf16[512,256]{1,0:T(8,128)(2,1)S(1)}, bf16[512,256]{1,0:T(8,128)(2,1)S(1)}, u32[]{:S(2)}, u32[]{:S(2)}) collective-permute-start(bf16[512,256]{1,0:T(8,128)(2,1)S(1)} %get-tuple-element.75), channel_id=1, source_target_pairs={{0,0},{1,2},{2,1},{3,3},{4,4},{5,6},{6,5},{7,7},{8,8},{9,10},{10,9... | collective-permute-start | bytes 786440 | tf_op jit(solution)/shard_map/ppermute | solution.py:292
  35.4 0.0 collective-permute-start.6
  35.4 4.3 %collective-permute-done.5 = bf16[512,256]{1,0:T(8,128)(2,1)S(1)} collective-permute-done((bf16[512,256]{1,0:T(8,128)(2,1)S(1)}, bf16[512,256]{1,0:T(8,128)(2,1)S(1)}, u32[]{:S(2)}, u32[]{:S(2)}) %collective-permute-start.5) | collective-permute-done | bytes 262176 | tf_op jit(solution)/shard_map/ppermute | solution.py:292
  39.7 1.8 %collective-permute-done.6 = bf16[512,256]{1,0:T(8,128)(2,1)S(1)} collective-permute-done((bf16[512,256]{1,0:T(8,128)(2,1)S(1)}, bf16[512,256]{1,0:T(8,128)(2,1)S(1)}, u32[]{:S(2)}, u32[]{:S(2)}) %collective-permute-start.6) | collective-permute-done | bytes 262176 | tf_op jit(solution)/shard_map/ppermute | solution.py:293
  41.5 0.6 collective-permute-done.8.rim
  42.0 1.5 %collective-permute-start.10 = (bf16[1568,256]{1,0:T(8,128)(2,1)S(1)}, bf16[1568,256]{1,0:T(8,128)(2,1)S(1)}, u32[]{:S(2)}, u32[]{:S(2)}) collective-permute-start(bf16[1568,256]{1,0:T(8,128)(2,1)S(1)} %collective-permute-done.9.near_w), channel_id=1, source_target_pairs={{0,1},{1,0},{2,3},{3,2},{4,5},{5,4},{6,7},{7,6},{8,9},{9,8},{10,11... | collective-permute-start | bytes 2408456 | tf_op jit(solution)/shard_map/ppermute | solution.py:308
  43.5 1.4 %collective-permute-start.11 = (bf16[784,256]{1,0:T(8,128)(2,1)S(1)}, bf16[784,256]{1,0:T(8,128)(2,1)S(1)}, u32[]{:S(2)}, u32[]{:S(2)}) collective-permute-start(bf16[784,256]{1,0:T(8,128)(2,1)S(1)} %copy-done.18), channel_id=1, source_target_pairs={{0,2},{2,0},{1,3},{3,1},{4,6},{6,4},{5,7},{7,5},{8,10},{10,8},{9,1... | collective-permute-start | bytes 1204232 | tf_op jit(solution)/shard_map/ppermute | solution.py:308
  44.9 0.1 maximum_select_fusion.1.own
  45.1 0.4 collective-permute-start.12
  45.5 2.4 %collective-permute-start.13 = (bf16[512,512]{1,0:T(8,128)(2,1)S(1)}, bf16[512,512]{1,0:T(8,128)(2,1)S(1)}, u32[]{:S(2)}, u32[]{:S(2)}) collective-permute-start(bf16[512,512]{1,0:T(8,128)(2,1)S(1)} %maximum_select_fusion.1.own), channel_id=1, source_target_pairs={{1,4},{5,8},{4,1},{9,12},{8,5},{12,9},{3,6},{7,10},{6,3},{11,14},{... | collective-permute-start | bytes 1572872 | tf_op jit(solution)/shard_map/ppermute | solution.py:319
  48.0 6.3 %graph_layer.4.own = bf16[512,512]{1,0:T(8,128)(2,1)S(1)} custom-call(s32[1]{0:T(128)} %bitcast.4.core_ref, s32[4096]{0:T(1024)S(1)} %bitcast.37, bf16[512,512]{1,0:T(8,128)(2,1)S(1)} %maximum_select_fusion.own, bf16[512,512]{1,0:T(8,128)(2,1)S(1)} %collective-permute-done.7.sib, bf16[512,512]{1,0:T(8,128)(2,1)S(1)} %collective-permute-done.8.rim, ...), custom_call_target="tpu_custom_call" | custom-call | flops 8589934592 | bytes 2621440 | tf_op jit(solution)/shard_map/graph_layer/pallas_call | solution.py:254
  54.3 0.1 collective-permute-start.14
  54.4 1.4 %collective-permute-start.15 = (bf16[512,512]{1,0:T(8,128)(2,1)S(1)}, bf16[512,512]{1,0:T(8,128)(2,1)S(1)}, u32[]{:S(2)}, u32[]{:S(2)}) collective-permute-start(bf16[512,512]{1,0:T(8,128)(2,1)S(1)} %graph_layer.4.own), channel_id=1, source_target_pairs={{1,4},{0,13},{5,8},{4,1},{9,12},{8,5},{13,0},{12,9},{3,6},{2,15},{... | collective-permute-start | bytes 1572872 | tf_op jit(solution)/shard_map/ppermute | solution.py:319
  55.8 0.8 collective-permute-start.16
  56.5 0.1 collective-permute-start.19
  56.7 6.3 %graph_layer.5.own = bf16[512,512]{1,0:T(8,128)(2,1)S(1)} custom-call(s32[1]{0:T(128)} %bitcast.4.core_ref, s32[4096]{0:T(1024)S(1)} %bitcast.35, bf16[512,512]{1,0:T(8,128)(2,1)S(1)} %maximum_select_fusion.1.own, bf16[512,512]{1,0:T(8,128)(2,1)S(1)} %collective-permute-done.12.sib, bf16[512,512]{1,0:T(8,128)(2,1)S(1)} %collective-permute-done.13.rim, ...), custom_call_target="tpu_custom_call" | custom-call | flops 8589934592 | bytes 2621440 | tf_op jit(solution)/shard_map/graph_layer/pallas_call | solution.py:254
  62.9 0.4 collective-permute-start.20
  63.4 2.7 %collective-permute-start.21 = (bf16[512,512]{1,0:T(8,128)(2,1)S(1)}, bf16[512,512]{1,0:T(8,128)(2,1)S(1)}, u32[]{:S(2)}, u32[]{:S(2)}) collective-permute-start(bf16[512,512]{1,0:T(8,128)(2,1)S(1)} %graph_layer.5.own), channel_id=1, source_target_pairs={{1,4},{5,8},{4,1},{9,12},{8,5},{12,9},{3,6},{7,10},{6,3},{11,14},{... | collective-permute-start | bytes 1572872 | tf_op jit(solution)/shard_map/ppermute | solution.py:319
  66.1 1.4 %collective-permute-done.15.rim = bf16[512,512]{1,0:T(8,128)(2,1)S(1)} collective-permute-done((bf16[512,512]{1,0:T(8,128)(2,1)S(1)}, bf16[512,512]{1,0:T(8,128)(2,1)S(1)}, u32[]{:S(2)}, u32[]{:S(2)}) %collective-permute-start.15) | collective-permute-done | bytes 524320 | tf_op jit(solution)/shard_map/ppermute | solution.py:319
  67.5 6.3 %graph_layer.6 = (bf16[512,256]{1,0:T(8,128)(2,1)S(1)}, bf16[512,256]{1,0:T(8,128)(2,1)S(1)}) custom-call(s32[1]{0:T(128)} %bitcast.4.core_ref, s32[4096]{0:T(1024)S(1)} %bitcast.38, bf16[512,512]{1,0:T(8,128)(2,1)S(1)} %graph_layer.4.own, bf16[512,512]{1,0:T(8,128)(2,1)S(1)} %collective-permute-done.14.sib, ...), custom_call_target="tpu_custom_call" | custom-call | flops 1073741824 | bytes 2621440 | tf_op jit(solution)/shard_map/graph_layer/pallas_call | solution.py:254
  73.8 3.3 %collective-permute-start.22 = (bf16[784,256]{1,0:T(8,128)(2,1)S(1)}, bf16[784,256]{1,0:T(8,128)(2,1)S(1)}, u32[]{:S(2)}, u32[]{:S(2)}) collective-permute-start(bf16[784,256]{1,0:T(8,128)(2,1)S(1)} %collective-permute-done.19.near_w), channel_id=1, source_target_pairs={{0,1},{1,0},{2,3},{3,2},{4,5},{5,4},{6,7},{7,6},{8,9},{9,8},{10,11... | collective-permute-start | bytes 1204232 | tf_op jit(solution)/shard_map/ppermute | solution.py:308
  77.2 0.0 collective-permute-start.18
  77.2 2.3 %collective-permute-start.17 = (bf16[512,256]{1,0:T(8,128)(2,1)S(1)}, bf16[512,256]{1,0:T(8,128)(2,1)S(1)}, u32[]{:S(2)}, u32[]{:S(2)}) collective-permute-start(bf16[512,256]{1,0:T(8,128)(2,1)S(1)} %get-tuple-element.98), channel_id=1, source_target_pairs={{0,0},{1,2},{2,1},{3,3},{4,4},{5,6},{6,5},{7,7},{8,8},{9,10},{10,9... | collective-permute-start | bytes 786440 | tf_op jit(solution)/shard_map/ppermute | solution.py:298
  79.6 6.3 %graph_layer.7 = (bf16[512,256]{1,0:T(8,128)(2,1)S(1)}, bf16[512,256]{1,0:T(8,128)(2,1)S(1)}) custom-call(s32[1]{0:T(128)} %bitcast.4.core_ref, s32[4096]{0:T(1024)S(1)} %bitcast.36, bf16[512,512]{1,0:T(8,128)(2,1)S(1)} %graph_layer.5.own, bf16[512,512]{1,0:T(8,128)(2,1)S(1)} %collective-permute-done.20.sib, ...), custom_call_target="tpu_custom_call" | custom-call | flops 8589934592 | bytes 2621440 | tf_op jit(solution)/shard_map/graph_layer/pallas_call | solution.py:254
  85.9 3.2 %collective-permute-start.23 = (bf16[512,256]{1,0:T(8,128)(2,1)S(1)}, bf16[512,256]{1,0:T(8,128)(2,1)S(1)}, u32[]{:S(2)}, u32[]{:S(2)}) collective-permute-start(bf16[512,256]{1,0:T(8,128)(2,1)S(1)} %get-tuple-element.105), channel_id=1, source_target_pairs={{0,0},{1,2},{2,1},{3,3},{4,4},{5,6},{6,5},{7,7},{8,8},{9,10},{10,9... | collective-permute-start | bytes 786440 | tf_op jit(solution)/shard_map/ppermute | solution.py:298
  89.1 0.0 collective-permute-start.24
  89.2 1.0 %maximum_select_fusion.2 = bf16[1024,256]{1,0:T(8,128)(2,1)} fusion(bf16[512,256]{1,0:T(8,128)(2,1)S(1)} %collective-permute-done.18, bf16[512,256]{1,0:T(8,128)(2,1)S(1)} %collective-permute-done.17, pred[]{:T(512)S(6)} %eq.6), kind=kLoop, calls=%fused_computation.2 | loop fusion | flops 2359296 | bytes 1048577 | tf_op jit(solution)/shard_map/jit(_where)/select_n | solution.py:304
  90.2 5.5 %collective-permute-done.23 = bf16[512,256]{1,0:T(8,128)(2,1)S(1)} collective-permute-done((bf16[512,256]{1,0:T(8,128)(2,1)S(1)}, bf16[512,256]{1,0:T(8,128)(2,1)S(1)}, u32[]{:S(2)}, u32[]{:S(2)}) %collective-permute-start.23) | collective-permute-done | bytes 262176 | tf_op jit(solution)/shard_map/ppermute | solution.py:298
  95.7 0.7 collective-permute-done.24
  96.4 1.0 %maximum_select_fusion.3 = bf16[1,1024,256]{2,1,0:T(8,128)(2,1)} fusion(bf16[1,512,256]{2,1,0:T(8,128)(2,1)S(1)} %bitcast.41, bf16[1,512,256]{2,1,0:T(8,128)(2,1)S(1)} %bitcast.40, pred[]{:T(512)S(6)} %eq.6), kind=kLoop, calls=%fused_computation.3 | loop fusion | flops 2359296 | bytes 1048577 | tf_op jit(solution)/shard_map/jit(_where)/select_n | solution.py:304
  (60 shorter events, 0.2 us)
Async XLA Ops:
  1.7 14.5 %collective-permute-start = (bf16[512,256]{1,0:T(8,128)(2,1)S(1)}, bf16[512,256]{1,0:T(8,128)(2,1)S(1)}, u32[]{:S(2)}, u32[]{:S(2)}) collective-permute-start(bf16[512,256]{1,0:T(8,128)(2,1)S(1)} %get-tuple-element.111), channel_id=1, source_target_pairs={{0,0},{1,2},{2,1},{3,3},{4,4},{5,6},{6,5},{7,7},{8,8},{9,10},{10,9... | collective-permute-start | bytes 786440 | tf_op jit(solution)/shard_map/ppermute | solution.py:292
  6.2 11.1 %collective-permute-start.1 = (bf16[512,256]{1,0:T(8,128)(2,1)S(1)}, bf16[512,256]{1,0:T(8,128)(2,1)S(1)}, u32[]{:S(2)}, u32[]{:S(2)}) collective-permute-start(bf16[512,256]{1,0:T(8,128)(2,1)S(1)} %get-tuple-element.110), channel_id=1, source_target_pairs={{0,1},{1,3},{2,0},{3,2},{4,5},{5,7},{6,4},{7,6},{8,9},{9,11},{10,8... | collective-permute-start | bytes 786440 | tf_op jit(solution)/shard_map/ppermute | solution.py:293
  6.3 3.1 %copy-start.16 = (s32[512]{0:T(512)S(1)}, s32[512]{0:T(512)}, u32[]{:S(2)}) copy-start(s32[512]{0:T(512)} %param.23) | copy-start | bytes 6148
  6.3 3.8 %copy-start = (bf16[1,1024,256]{2,1,0:T(8,128)(2,1)S(1)}, bf16[1,1024,256]{2,1,0:T(8,128)(2,1)}, u32[]{:S(2)}) copy-start(bf16[1,1024,256]{2,1,0:T(8,128)(2,1)} %param.17) | copy-start | bytes 1572868
  9.2 32.8 %collective-permute-start.9 = (bf16[1568,256]{1,0:T(8,128)(2,1)}, bf16[1568,256]{1,0:T(8,128)(2,1)S(1)}, u32[]{:S(2)}, u32[]{:S(2)}) collective-permute-start(bf16[1568,256]{1,0:T(8,128)(2,1)} %pack_weights.2), channel_id=1, source_target_pairs={{0,2},{2,0},{1,3},{3,1},{4,6},{6,4},{5,7},{7,5},{8,10},{10,8},{9,1... | collective-permute-start | bytes 2408456 | tf_op jit(solution)/shard_map/ppermute | solution.py:308
  9.4 0.7 copy-start.15
  9.4 0.7 copy-start.14
  10.1 6.0 %copy-start.12 = (s32[1024]{0:T(1024)S(1)}, s32[1024]{0:T(1024)}, u32[]{:S(2)}) copy-start(s32[1024]{0:T(1024)} %param.20) | copy-start | bytes 12292
  10.1 6.0 %copy-start.13 = (s32[1024]{0:T(1024)S(1)}, s32[1024]{0:T(1024)}, u32[]{:S(2)}) copy-start(s32[1024]{0:T(1024)} %param.22) | copy-start | bytes 12292
  10.1 6.0 %copy-start.11 = (s32[1024,8]{0,1:T(8,128)S(1)}, s32[1024,8]{0,1:T(8,128)}, u32[]{:S(2)}) copy-start(s32[1024,8]{0,1:T(8,128)} %param.19) | copy-start | bytes 98308
  12.4 3.8 %copy-start.10 = (s32[1024,8]{0,1:T(8,128)S(1)}, s32[1024,8]{0,1:T(8,128)}, u32[]{:S(2)}) copy-start(s32[1024,8]{0,1:T(8,128)} %param.21) | copy-start | bytes 98308
  12.4 7.8 %collective-permute-start.2 = (bf16[272,256]{1,0:T(8,128)(2,1)S(1)}, bf16[272,256]{1,0:T(8,128)(2,1)S(1)}, u32[]{:S(2)}, u32[]{:S(2)}) collective-permute-start(bf16[272,256]{1,0:T(8,128)(2,1)S(1)} %get-tuple-element.64), channel_id=1, source_target_pairs={{0,4},{4,8},{8,12},{12,0},{1,5},{5,9},{9,13},{13,1},{2,6},{6,10},{... | collective-permute-start | bytes 417800 | tf_op jit(solution)/shard_map/ppermute | solution.py:392
  13.7 12.1 %collective-permute-start.3 = (bf16[272,256]{1,0:T(8,128)(2,1)S(1)}, bf16[272,256]{1,0:T(8,128)(2,1)S(1)}, u32[]{:S(2)}, u32[]{:S(2)}) collective-permute-start(bf16[272,256]{1,0:T(8,128)(2,1)S(1)} %get-tuple-element.65), channel_id=1, source_target_pairs={{0,8},{4,12},{8,0},{12,4},{1,9},{5,13},{9,1},{13,5},{2,10},{6,14},... | collective-permute-start | bytes 417800 | tf_op jit(solution)/shard_map/ppermute | solution.py:392
  16.2 9.6 %collective-permute-start.4 = (bf16[272,256]{1,0:T(8,128)(2,1)S(1)}, bf16[272,256]{1,0:T(8,128)(2,1)S(1)}, u32[]{:S(2)}, u32[]{:S(2)}) collective-permute-start(bf16[272,256]{1,0:T(8,128)(2,1)S(1)} %get-tuple-element.66), channel_id=1, source_target_pairs={{0,12},{4,0},{8,4},{12,8},{1,13},{5,1},{9,5},{13,9},{2,14},{6,2},{... | collective-permute-start | bytes 417800 | tf_op jit(solution)/shard_map/ppermute | solution.py:392
  25.9 3.9 %copy-start.1 = (bf16[1,1024,256]{2,1,0:T(8,128)(2,1)S(1)}, bf16[1,1024,256]{2,1,0:T(8,128)(2,1)}, u32[]{:S(2)}) copy-start(bf16[1,1024,256]{2,1,0:T(8,128)(2,1)} %param.18) | copy-start | bytes 1572868
  26.0 15.5 %collective-permute-start.7 = (bf16[512,512]{1,0:T(8,128)(2,1)S(1)}, bf16[512,512]{1,0:T(8,128)(2,1)S(1)}, u32[]{:S(2)}, u32[]{:S(2)}) collective-permute-start(bf16[512,512]{1,0:T(8,128)(2,1)S(1)} %maximum_select_fusion.own), channel_id=1, source_target_pairs={{0,1},{1,0},{2,3},{3,2},{4,5},{5,4},{6,7},{7,6},{8,9},{9,8},{10,11... | collective-permute-start | bytes 1572872 | tf_op jit(solution)/shard_map/ppermute | solution.py:308
  26.6 15.4 %collective-permute-start.8 = (bf16[512,512]{1,0:T(8,128)(2,1)S(1)}, bf16[512,512]{1,0:T(8,128)(2,1)S(1)}, u32[]{:S(2)}, u32[]{:S(2)}) collective-permute-start(bf16[512,512]{1,0:T(8,128)(2,1)S(1)} %maximum_select_fusion.own), channel_id=1, source_target_pairs={{1,4},{0,13},{5,8},{4,1},{9,12},{8,5},{13,0},{12,9},{3,6},{2,15},{... | collective-permute-start | bytes 1572872 | tf_op jit(solution)/shard_map/ppermute | solution.py:319
  29.8 13.7 %copy-start.18 = (bf16[784,256]{1,0:T(8,128)(2,1)S(1)}, bf16[784,256]{1,0:T(8,128)(2,1)}, u32[]{:S(2)}) copy-start(bf16[784,256]{1,0:T(8,128)(2,1)} %get-tuple-element.87) | copy-start | bytes 1204228
  29.8 18.2 %copy-start.4 = (bf16[2,256,512]{2,1,0:T(8,128)(2,1)S(1)}, bf16[2,256,512]{2,1,0:T(8,128)(2,1)}, u32[]{:S(2)}) copy-start(bf16[2,256,512]{2,1,0:T(8,128)(2,1)} %w2_hbm.6) | copy-start | bytes 1572868
  30.5 17.5 %copy-start.8 = (bf16[2,256]{1,0:T(2,128)(2,1)S(1)}, bf16[2,256]{1,0:T(2,128)(2,1)}, u32[]{:S(2)}) copy-start(bf16[2,256]{1,0:T(2,128)(2,1)} %bias.6) | copy-start | bytes 3076
  30.5 17.5 %copy-start.2 = (bf16[2,512,256]{2,1,0:T(8,128)(2,1)S(1)}, bf16[2,512,256]{2,1,0:T(8,128)(2,1)}, u32[]{:S(2)}) copy-start(bf16[2,512,256]{2,1,0:T(8,128)(2,1)} %ws_hbm.6) | copy-start | bytes 1572868
  30.5 17.5 %copy-start.3 = (bf16[2,512,256]{2,1,0:T(8,128)(2,1)S(1)}, bf16[2,512,256]{2,1,0:T(8,128)(2,1)}, u32[]{:S(2)}) copy-start(bf16[2,512,256]{2,1,0:T(8,128)(2,1)} %wd_hbm.6) | copy-start | bytes 1572868
  30.5 9.1 %collective-permute-start.5 = (bf16[512,256]{1,0:T(8,128)(2,1)S(1)}, bf16[512,256]{1,0:T(8,128)(2,1)S(1)}, u32[]{:S(2)}, u32[]{:S(2)}) collective-permute-start(bf16[512,256]{1,0:T(8,128)(2,1)S(1)} %get-tuple-element.75), channel_id=1, source_target_pairs={{0,0},{1,2},{2,1},{3,3},{4,4},{5,6},{6,5},{7,7},{8,8},{9,10},{10,9... | collective-permute-start | bytes 786440 | tf_op jit(solution)/shard_map/ppermute | solution.py:292
  35.4 6.1 %collective-permute-start.6 = (bf16[512,256]{1,0:T(8,128)(2,1)S(1)}, bf16[512,256]{1,0:T(8,128)(2,1)S(1)}, u32[]{:S(2)}, u32[]{:S(2)}) collective-permute-start(bf16[512,256]{1,0:T(8,128)(2,1)S(1)} %get-tuple-element.76), channel_id=1, source_target_pairs={{0,1},{1,3},{2,0},{3,2},{4,5},{5,7},{6,4},{7,6},{8,9},{9,11},{10,8... | collective-permute-start | bytes 786440 | tf_op jit(solution)/shard_map/ppermute | solution.py:293
  42.0 5.9 %collective-permute-start.10 = (bf16[1568,256]{1,0:T(8,128)(2,1)S(1)}, bf16[1568,256]{1,0:T(8,128)(2,1)S(1)}, u32[]{:S(2)}, u32[]{:S(2)}) collective-permute-start(bf16[1568,256]{1,0:T(8,128)(2,1)S(1)} %collective-permute-done.9.near_w), channel_id=1, source_target_pairs={{0,1},{1,0},{2,3},{3,2},{4,5},{5,4},{6,7},{7,6},{8,9},{9,8},{10,11... | collective-permute-start | bytes 2408456 | tf_op jit(solution)/shard_map/ppermute | solution.py:308
  43.5 12.2 %collective-permute-start.11 = (bf16[784,256]{1,0:T(8,128)(2,1)S(1)}, bf16[784,256]{1,0:T(8,128)(2,1)S(1)}, u32[]{:S(2)}, u32[]{:S(2)}) collective-permute-start(bf16[784,256]{1,0:T(8,128)(2,1)S(1)} %copy-done.18), channel_id=1, source_target_pairs={{0,2},{2,0},{1,3},{3,1},{4,6},{6,4},{5,7},{7,5},{8,10},{10,8},{9,1... | collective-permute-start | bytes 1204232 | tf_op jit(solution)/shard_map/ppermute | solution.py:308
  45.0 11.5 %copy-start.17 = (bf16[784,256]{1,0:T(8,128)(2,1)S(1)}, bf16[784,256]{1,0:T(8,128)(2,1)}, u32[]{:S(2)}) copy-start(bf16[784,256]{1,0:T(8,128)(2,1)} %get-tuple-element.100) | copy-start | bytes 1204228
  45.0 11.6 %copy-start.5 = (bf16[2,512,256]{2,1,0:T(8,128)(2,1)S(1)}, bf16[2,512,256]{2,1,0:T(8,128)(2,1)}, u32[]{:S(2)}) copy-start(bf16[2,512,256]{2,1,0:T(8,128)(2,1)} %ws_hbm.7) | copy-start | bytes 1572868
  45.0 11.6 %copy-start.6 = (bf16[2,512,256]{2,1,0:T(8,128)(2,1)S(1)}, bf16[2,512,256]{2,1,0:T(8,128)(2,1)}, u32[]{:S(2)}) copy-start(bf16[2,512,256]{2,1,0:T(8,128)(2,1)} %wd_hbm.7) | copy-start | bytes 1572868
  45.1 11.6 %copy-start.7 = (bf16[2,256,512]{2,1,0:T(8,128)(2,1)S(1)}, bf16[2,256,512]{2,1,0:T(8,128)(2,1)}, u32[]{:S(2)}) copy-start(bf16[2,256,512]{2,1,0:T(8,128)(2,1)} %w2_hbm.7) | copy-start | bytes 1572868
  45.1 11.6 %copy-start.9 = (bf16[2,256]{1,0:T(2,128)(2,1)S(1)}, bf16[2,256]{1,0:T(2,128)(2,1)}, u32[]{:S(2)}) copy-start(bf16[2,256]{1,0:T(2,128)(2,1)} %bias.7) | copy-start | bytes 3076
  45.1 11.5 %collective-permute-start.12 = (bf16[512,512]{1,0:T(8,128)(2,1)S(1)}, bf16[512,512]{1,0:T(8,128)(2,1)S(1)}, u32[]{:S(2)}, u32[]{:S(2)}) collective-permute-start(bf16[512,512]{1,0:T(8,128)(2,1)S(1)} %maximum_select_fusion.1.own), channel_id=1, source_target_pairs={{0,1},{1,0},{2,3},{3,2},{4,5},{5,4},{6,7},{7,6},{8,9},{9,8},{10,11... | collective-permute-start | bytes 1572872 | tf_op jit(solution)/shard_map/ppermute | solution.py:308
  45.5 11.1 %collective-permute-start.13 = (bf16[512,512]{1,0:T(8,128)(2,1)S(1)}, bf16[512,512]{1,0:T(8,128)(2,1)S(1)}, u32[]{:S(2)}, u32[]{:S(2)}) collective-permute-start(bf16[512,512]{1,0:T(8,128)(2,1)S(1)} %maximum_select_fusion.1.own), channel_id=1, source_target_pairs={{1,4},{5,8},{4,1},{9,12},{8,5},{12,9},{3,6},{7,10},{6,3},{11,14},{... | collective-permute-start | bytes 1572872 | tf_op jit(solution)/shard_map/ppermute | solution.py:319
  54.3 11.8 %collective-permute-start.14 = (bf16[512,512]{1,0:T(8,128)(2,1)S(1)}, bf16[512,512]{1,0:T(8,128)(2,1)S(1)}, u32[]{:S(2)}, u32[]{:S(2)}) collective-permute-start(bf16[512,512]{1,0:T(8,128)(2,1)S(1)} %graph_layer.4.own), channel_id=1, source_target_pairs={{0,1},{1,0},{2,3},{3,2},{4,5},{5,4},{6,7},{7,6},{8,9},{9,8},{10,11... | collective-permute-start | bytes 1572872 | tf_op jit(solution)/shard_map/ppermute | solution.py:308
  54.4 13.2 %collective-permute-start.15 = (bf16[512,512]{1,0:T(8,128)(2,1)S(1)}, bf16[512,512]{1,0:T(8,128)(2,1)S(1)}, u32[]{:S(2)}, u32[]{:S(2)}) collective-permute-start(bf16[512,512]{1,0:T(8,128)(2,1)S(1)} %graph_layer.4.own), channel_id=1, source_target_pairs={{1,4},{0,13},{5,8},{4,1},{9,12},{8,5},{13,0},{12,9},{3,6},{2,15},{... | collective-permute-start | bytes 1572872 | tf_op jit(solution)/shard_map/ppermute | solution.py:319
  55.8 7.6 %collective-permute-start.16 = (bf16[784,256]{1,0:T(8,128)(2,1)S(1)}, bf16[784,256]{1,0:T(8,128)(2,1)S(1)}, u32[]{:S(2)}, u32[]{:S(2)}) collective-permute-start(bf16[784,256]{1,0:T(8,128)(2,1)S(1)} %collective-permute-done.11.near_w), channel_id=1, source_target_pairs={{0,1},{1,0},{2,3},{3,2},{4,5},{5,4},{6,7},{7,6},{8,9},{9,8},{10,11... | collective-permute-start | bytes 1204232 | tf_op jit(solution)/shard_map/ppermute | solution.py:308
  56.5 17.3 %collective-permute-start.19 = (bf16[784,256]{1,0:T(8,128)(2,1)S(1)}, bf16[784,256]{1,0:T(8,128)(2,1)S(1)}, u32[]{:S(2)}, u32[]{:S(2)}) collective-permute-start(bf16[784,256]{1,0:T(8,128)(2,1)S(1)} %copy-done.17), channel_id=1, source_target_pairs={{0,2},{2,0},{1,3},{3,1},{4,6},{6,4},{5,7},{7,5},{8,10},{10,8},{9,1... | collective-permute-start | bytes 1204232 | tf_op jit(solution)/shard_map/ppermute | solution.py:308
  62.9 16.6 %collective-permute-start.20 = (bf16[512,512]{1,0:T(8,128)(2,1)S(1)}, bf16[512,512]{1,0:T(8,128)(2,1)S(1)}, u32[]{:S(2)}, u32[]{:S(2)}) collective-permute-start(bf16[512,512]{1,0:T(8,128)(2,1)S(1)} %graph_layer.5.own), channel_id=1, source_target_pairs={{0,1},{1,0},{2,3},{3,2},{4,5},{5,4},{6,7},{7,6},{8,9},{9,8},{10,11... | collective-permute-start | bytes 1572872 | tf_op jit(solution)/shard_map/ppermute | solution.py:308
  63.4 16.2 %collective-permute-start.21 = (bf16[512,512]{1,0:T(8,128)(2,1)S(1)}, bf16[512,512]{1,0:T(8,128)(2,1)S(1)}, u32[]{:S(2)}, u32[]{:S(2)}) collective-permute-start(bf16[512,512]{1,0:T(8,128)(2,1)S(1)} %graph_layer.5.own), channel_id=1, source_target_pairs={{1,4},{5,8},{4,1},{9,12},{8,5},{12,9},{3,6},{7,10},{6,3},{11,14},{... | collective-permute-start | bytes 1572872 | tf_op jit(solution)/shard_map/ppermute | solution.py:319
  73.8 5.7 %collective-permute-start.22 = (bf16[784,256]{1,0:T(8,128)(2,1)S(1)}, bf16[784,256]{1,0:T(8,128)(2,1)S(1)}, u32[]{:S(2)}, u32[]{:S(2)}) collective-permute-start(bf16[784,256]{1,0:T(8,128)(2,1)S(1)} %collective-permute-done.19.near_w), channel_id=1, source_target_pairs={{0,1},{1,0},{2,3},{3,2},{4,5},{5,4},{6,7},{7,6},{8,9},{9,8},{10,11... | collective-permute-start | bytes 1204232 | tf_op jit(solution)/shard_map/ppermute | solution.py:308
  77.2 12.0 %collective-permute-start.18 = (bf16[512,256]{1,0:T(8,128)(2,1)S(1)}, bf16[512,256]{1,0:T(8,128)(2,1)S(1)}, u32[]{:S(2)}, u32[]{:S(2)}) collective-permute-start(bf16[512,256]{1,0:T(8,128)(2,1)S(1)} %get-tuple-element.99), channel_id=1, source_target_pairs={{0,2},{1,0},{2,3},{3,1},{4,6},{5,4},{6,7},{7,5},{8,10},{9,8},{10,1... | collective-permute-start | bytes 786440 | tf_op jit(solution)/shard_map/ppermute | solution.py:299
  77.2 12.0 %collective-permute-start.17 = (bf16[512,256]{1,0:T(8,128)(2,1)S(1)}, bf16[512,256]{1,0:T(8,128)(2,1)S(1)}, u32[]{:S(2)}, u32[]{:S(2)}) collective-permute-start(bf16[512,256]{1,0:T(8,128)(2,1)S(1)} %get-tuple-element.98), channel_id=1, source_target_pairs={{0,0},{1,2},{2,1},{3,3},{4,4},{5,6},{6,5},{7,7},{8,8},{9,10},{10,9... | collective-permute-start | bytes 786440 | tf_op jit(solution)/shard_map/ppermute | solution.py:298
  85.9 9.8 %collective-permute-start.23 = (bf16[512,256]{1,0:T(8,128)(2,1)S(1)}, bf16[512,256]{1,0:T(8,128)(2,1)S(1)}, u32[]{:S(2)}, u32[]{:S(2)}) collective-permute-start(bf16[512,256]{1,0:T(8,128)(2,1)S(1)} %get-tuple-element.105), channel_id=1, source_target_pairs={{0,0},{1,2},{2,1},{3,3},{4,4},{5,6},{6,5},{7,7},{8,8},{9,10},{10,9... | collective-permute-start | bytes 786440 | tf_op jit(solution)/shard_map/ppermute | solution.py:298
  89.1 7.3 %collective-permute-start.24 = (bf16[512,256]{1,0:T(8,128)(2,1)S(1)}, bf16[512,256]{1,0:T(8,128)(2,1)S(1)}, u32[]{:S(2)}, u32[]{:S(2)}) collective-permute-start(bf16[512,256]{1,0:T(8,128)(2,1)S(1)} %get-tuple-element.106), channel_id=1, source_target_pairs={{0,2},{1,0},{2,3},{3,1},{4,6},{5,4},{6,7},{7,5},{8,10},{9,8},{10,1... | collective-permute-start | bytes 786440 | tf_op jit(solution)/shard_map/ppermute | solution.py:299

commit v17 on v16

--- a/solution.py
+++ b/solution.py
@@ -382,15 +382,16 @@
     same = lax.dynamic_slice(g_own, (part * half, 0), (half, g_own.shape[1]))
     other = lax.dynamic_slice(g_own, ((1 - part) * half, 0), (half, g_own.shape[1]))
     g_a, g_b = spread_rows(same, other)
+    bnd = jnp.stack([bnd_src, bnd_part[:, 0], bnd_node])
+    bnd, same, other = after((bnd, same, other))
+    pieces = list(pick_rows(me, bnd, g_own, parts, cap))
+    pieces[0], core1 = after((pieces[0], core1))
     packs = list(pack_weights((((0, 0), (1, 0)),), core1, g_weights, g_b1, r_weights, r_b1))
     near_w = [swap(packs[0], "mp")]
-    bnd = jnp.stack([bnd_src, bnd_part[:, 0], bnd_node])
-    bnd, packs[0], same, other = after((bnd, packs[0], same, other))
-    pieces = pick_rows(me, bnd, g_own, parts, cap)
     landed = [pieces[0]]
     for k in range(1, parts):
         landed.append(lax.ppermute(pieces[k], "mesh", [(i, (i + k) % parts) for i in range(parts)]))
-    landed[0], core1, g_a, g_b = after((landed[0], core1, g_a, g_b))
+    landed[0], core1, packs[0], g_a, g_b = after((landed[0], core1, packs[0], g_a, g_b))
     idx = edge_offsets(jnp.stack([g_nbr, r_nbr]), jnp.stack([g_count, r_count]), core)
     rest = tuple(((graph, layer),) for layer in range(1, layers) for graph in (0, 1))
     packs += pack_weights(rest, core1, g_weights, g_b1, r_weights, r_b1)

time: 97.8 us -> 97.3 us (level)
  starting transfers between devices: 38.2 us -> 37.2 us
    ppermute x2, waiting for transfers between devices: 4.31 us -> 9 us  [spread_rows(): a = lax.ppermute(same, ('mp', 'batch'), [(0, 0), (1, 2), (2, 1), (3, 3)])]
    ppermute x3, waiting for transfers between devices: 5.67 us -> 2.68 us  [by_rows(): lax.ppermute(pieces[k], 'mesh', [(i, (i + k) % parts) for i in range(part...]
    ppermute x2, waiting for transfers between devices: 5.49 us -> 6.97 us  [gather_rows(): same = lax.ppermute(a, ('mp', 'batch'), [(0, 0), (1, 2), (2, 1), (3, 3)])]
    ppermute x2, starting transfers between devices: 9.31 us -> 8.03 us  [spread_rows(): a = lax.ppermute(same, ('mp', 'batch'), [(0, 0), (1, 2), (2, 1), (3, 3)])]
    ppermute x4, waiting for transfers between devices: 2 us -> 0.86 us  [rims(): return lax.ppermute(own, ('mesh', 'batch'), pairs)]
    ppermute x2, waiting for transfers between devices: 1.77 us -> 0.77 us  [spread_rows(): b = lax.ppermute(other, ('mp', 'batch'), [(0, 1), (1, 3), (2, 0), (3, 2)])]
  transfers between devices with their start and end apart: 25 -> 25, of which waited for: 7 -> 6; matrix products, arithmetic and copies ran while one was open for 1% -> 1% of each run, Pallas kernels for 35% -> 35%
where the time goes in v17:
time: 97.3 us; the launch traced here: 96.9 us
  starting transfers between devices  37.2 us (38%)
  Pallas kernels  33.8 us (35%)
  waiting for transfers between devices  20.4 us (21%)
  other arithmetic  2.43 us (2%)
  local copies, waits for them, and re-layouts  1.91 us (2%)
  between operations  1.13 us (1%)
    pallas_call x4, Pallas kernels, run_layer(): pl.pallas_call(functools.partial(layer_kernel, layer, place, slots, last)...  25.2 us
    ppermute x4, starting transfers between devices, rims(): return lax.ppermute(own, ('mesh', 'batch'), pairs)  9.19 us
    ppermute x10, starting transfers between devices, swap(): return lax.ppermute(values, axis, [(0, 1), (1, 0)])  9.09 us
    ppermute x2, waiting for transfers between devices, spread_rows(): a = lax.ppermute(same, ('mp', 'batch'), [(0, 0), (1, 2), (2, 1), (3, 3)])  9 us
    ppermute x2, starting transfers between devices, spread_rows(): a = lax.ppermute(same, ('mp', 'batch'), [(0, 0), (1, 2), (2, 1), (3, 3)])  8.03 us
    ppermute x2, waiting for transfers between devices, gather_rows(): same = lax.ppermute(a, ('mp', 'batch'), [(0, 0), (1, 2), (2, 1), (3, 3)])  6.97 us
    ppermute x2, starting transfers between devices, gather_rows(): same = lax.ppermute(a, ('mp', 'batch'), [(0, 0), (1, 2), (2, 1), (3, 3)])  6.04 us
    pallas_call x2, Pallas kernels, pack_weights(): pl.pallas_call(functools.partial(pack_kernel, plan), out_shape=tuple((jax...  5.69 us
  transfers between devices with their start and end apart: 25, of which 6 were waited for; matrix products, arithmetic and copies ran while one was open for 1% of the time, Pallas kernels for 35%

profile of v17, /device:TPU:1, one launch (start us, length us, event | category | flops | bytes accessed | tf_op | source)
XLA Modules:
  0.0 96.9 jit_solution(5820485568462976869)
XLA Ops:
  0.7 1.1 %dynamic-slice_bitcast_fusion = (bf16[512,256]{1,0:T(8,128)(2,1)S(1)}, bf16[512,256]{1,0:T(8,128)(2,1)S(1)}) fusion(bf16[1,1024,256]{2,1,0:T(8,128)(2,1)} %param.17, s32[]{:T(128)S(6)} %select_n.78, s32[]{:T(128)S(6)} %select_n.77), kind=kLoop, calls=%fused_computation.4 | loop fusion | bytes 1048584 | tf_op jit(solution)/shard_map/dynamic_slice | solution.py:383
  1.8 4.5 %collective-permute-start = (bf16[512,256]{1,0:T(8,128)(2,1)S(1)}, bf16[512,256]{1,0:T(8,128)(2,1)S(1)}, u32[]{:S(2)}, u32[]{:S(2)}) collective-permute-start(bf16[512,256]{1,0:T(8,128)(2,1)S(1)} %get-tuple-element.115), channel_id=1, source_target_pairs={{0,0},{1,2},{2,1},{3,3},{4,4},{5,6},{6,5},{7,7},{8,8},{9,10},{10,9... | collective-permute-start | bytes 786440 | tf_op jit(solution)/shard_map/ppermute | solution.py:292
  6.3 0.0 collective-permute-start.1
  6.4 0.7 copy-done.15
  7.0 0.0 copy-done.14
  7.1 0.0 copy-start.13
  7.1 0.0 copy-start.11
  7.1 2.2 %pick_rows.1 = (bf16[272,256]{1,0:T(8,128)(2,1)S(1)}, bf16[272,256]{1,0:T(8,128)(2,1)S(1)}, bf16[272,256]{1,0:T(8,128)(2,1)S(1)}, bf16[272,256]{1,0:T(8,128)(2,1)S(1)}) custom-call(s32[1]{0:T(128)} %bitcast.me_ref, s32[3,512]{1,0:T(4,128)S(1)} %pad_add_fusion.bnd_ref, bf16[1024,256]{1,0:T(8,128)(2,1)S(1)} %bitcast.33), custom_call_target="tpu_custom_call" | custom-call | flops 8589934592 | bytes 1 | tf_op jit(solution)/shard_map/pick_rows/pallas_call | solution.py:115
  9.3 1.3 %collective-permute-start.2 = (bf16[272,256]{1,0:T(8,128)(2,1)S(1)}, bf16[272,256]{1,0:T(8,128)(2,1)S(1)}, u32[]{:S(2)}, u32[]{:S(2)}) collective-permute-start(bf16[272,256]{1,0:T(8,128)(2,1)S(1)} %get-tuple-element.68), channel_id=1, source_target_pairs={{0,4},{4,8},{8,12},{12,0},{1,5},{5,9},{9,13},{13,1},{2,6},{6,10},{... | collective-permute-start | bytes 417800 | tf_op jit(solution)/shard_map/ppermute | solution.py:393
  10.7 2.3 %collective-permute-start.3 = (bf16[272,256]{1,0:T(8,128)(2,1)S(1)}, bf16[272,256]{1,0:T(8,128)(2,1)S(1)}, u32[]{:S(2)}, u32[]{:S(2)}) collective-permute-start(bf16[272,256]{1,0:T(8,128)(2,1)S(1)} %get-tuple-element.69), channel_id=1, source_target_pairs={{0,8},{4,12},{8,0},{12,4},{1,9},{5,13},{9,1},{13,5},{2,10},{6,14},... | collective-permute-start | bytes 417800 | tf_op jit(solution)/shard_map/ppermute | solution.py:393
  13.0 1.1 %collective-permute-start.4 = (bf16[272,256]{1,0:T(8,128)(2,1)S(1)}, bf16[272,256]{1,0:T(8,128)(2,1)S(1)}, u32[]{:S(2)}, u32[]{:S(2)}) collective-permute-start(bf16[272,256]{1,0:T(8,128)(2,1)S(1)} %get-tuple-element.70), channel_id=1, source_target_pairs={{0,12},{4,0},{8,4},{12,8},{1,13},{5,1},{9,5},{13,9},{2,14},{6,2},{... | collective-permute-start | bytes 417800 | tf_op jit(solution)/shard_map/ppermute | solution.py:393
  14.1 0.1 fusion.5
  14.2 2.9 %pack_weights.2 = bf16[1568,256]{1,0:T(8,128)(2,1)} custom-call(s32[1]{0:T(128)} %bitcast.7.core_ref, bf16[2,256]{1,0:T(2,128)(2,1)} %bias.6, bf16[2,256]{1,0:T(2,128)(2,1)} %bias.7, bf16[2,512,256]{2,1,0:T(8,128)(2,1)} %ws_hbm.6, bf16[2,512,256]{2,1,0:T(8,128)(2,1)} %wd_hbm.6, bf16[2,256,512]{2,1,0:T(8,128)(2,1)} %w2_hbm.6, bf16[2,512,256]{2,1,0:T(8,128)(2,1)} %ws_hbm.7, ...), custom_call_target="tpu_custom_call" | custom-call | flops 4294967296 | bytes 1 | tf_op jit(solution)/shard_map/pack_weights/pallas_call | solution.py:352
  17.1 0.2 collective-permute-start.9
  17.3 2.8 %pack_weights.3 = (bf16[784,256]{1,0:T(8,128)(2,1)}, bf16[784,256]{1,0:T(8,128)(2,1)}) custom-call(s32[1]{0:T(128)} %bitcast.7.core_ref, bf16[2,256]{1,0:T(2,128)(2,1)} %bias.6, bf16[2,256]{1,0:T(2,128)(2,1)} %bias.7, bf16[2,512,256]{2,1,0:T(8,128)(2,1)} %ws_hbm.6, bf16[2,512,256]{2,1,0:T(8,128)(2,1)} %wd_hbm.6, bf16[2,256,512]{2,1,0:T(8,128)(2,1)} %w2_hbm.6, ...), custom_call_target="tpu_custom_call" | custom-call | flops 4294967296 | bytes 1 | tf_op jit(solution)/shard_map/pack_weights/pallas_call | solution.py:352
  20.1 2.7 %collective-permute-done.3.refs_2_ = bf16[272,256]{1,0:T(8,128)(2,1)S(1)} collective-permute-done((bf16[272,256]{1,0:T(8,128)(2,1)S(1)}, bf16[272,256]{1,0:T(8,128)(2,1)S(1)}, u32[]{:S(2)}, u32[]{:S(2)}) %collective-permute-start.3) | collective-permute-done | bytes 139296 | tf_op jit(solution)/shard_map/ppermute | solution.py:393
  22.8 0.1 maximum_select_fusion.own
  23.0 0.7 collective-permute-start.7
  23.6 3.1 %collective-permute-start.8 = (bf16[512,512]{1,0:T(8,128)(2,1)S(1)}, bf16[512,512]{1,0:T(8,128)(2,1)S(1)}, u32[]{:S(2)}, u32[]{:S(2)}) collective-permute-start(bf16[512,512]{1,0:T(8,128)(2,1)S(1)} %maximum_select_fusion.own), channel_id=1, source_target_pairs={{1,4},{0,13},{5,8},{4,1},{9,12},{8,5},{13,0},{12,9},{3,6},{2,15},{... | collective-permute-start | bytes 1572872 | tf_op jit(solution)/shard_map/ppermute | solution.py:319
  26.7 0.7 add_force.1
  27.5 3.5 %collective-permute-start.5 = (bf16[512,256]{1,0:T(8,128)(2,1)S(1)}, bf16[512,256]{1,0:T(8,128)(2,1)S(1)}, u32[]{:S(2)}, u32[]{:S(2)}) collective-permute-start(bf16[512,256]{1,0:T(8,128)(2,1)S(1)} %get-tuple-element.79), channel_id=1, source_target_pairs={{0,0},{1,2},{2,1},{3,3},{4,4},{5,6},{6,5},{7,7},{8,8},{9,10},{10,9... | collective-permute-start | bytes 786440 | tf_op jit(solution)/shard_map/ppermute | solution.py:292
  31.0 0.0 collective-permute-start.6
  31.1 9.0 %collective-permute-done.5 = bf16[512,256]{1,0:T(8,128)(2,1)S(1)} collective-permute-done((bf16[512,256]{1,0:T(8,128)(2,1)S(1)}, bf16[512,256]{1,0:T(8,128)(2,1)S(1)}, u32[]{:S(2)}, u32[]{:S(2)}) %collective-permute-start.5) | collective-permute-done | bytes 262176 | tf_op jit(solution)/shard_map/ppermute | solution.py:292
  40.1 0.8 collective-permute-done.6
  40.8 2.6 %collective-permute-start.10 = (bf16[1568,256]{1,0:T(8,128)(2,1)S(1)}, bf16[1568,256]{1,0:T(8,128)(2,1)S(1)}, u32[]{:S(2)}, u32[]{:S(2)}) collective-permute-start(bf16[1568,256]{1,0:T(8,128)(2,1)S(1)} %collective-permute-done.9.near_w), channel_id=1, source_target_pairs={{0,1},{1,0},{2,3},{3,2},{4,5},{5,4},{6,7},{7,6},{8,9},{9,8},{10,11... | collective-permute-start | bytes 2408456 | tf_op jit(solution)/shard_map/ppermute | solution.py:308
  43.4 0.1 maximum_select_fusion.1.own
  43.6 0.3 collective-permute-start.12
  43.9 2.6 %collective-permute-start.13 = (bf16[512,512]{1,0:T(8,128)(2,1)S(1)}, bf16[512,512]{1,0:T(8,128)(2,1)S(1)}, u32[]{:S(2)}, u32[]{:S(2)}) collective-permute-start(bf16[512,512]{1,0:T(8,128)(2,1)S(1)} %maximum_select_fusion.1.own), channel_id=1, source_target_pairs={{1,4},{5,8},{4,1},{9,12},{8,5},{12,9},{3,6},{7,10},{6,3},{11,14},{... | collective-permute-start | bytes 1572872 | tf_op jit(solution)/shard_map/ppermute | solution.py:319
  46.6 6.3 %graph_layer.4.own = bf16[512,512]{1,0:T(8,128)(2,1)S(1)} custom-call(s32[1]{0:T(128)} %bitcast.7.core_ref, s32[4096]{0:T(1024)S(1)} %bitcast.37, bf16[512,512]{1,0:T(8,128)(2,1)S(1)} %maximum_select_fusion.own, bf16[512,512]{1,0:T(8,128)(2,1)S(1)} %collective-permute-done.7.sib, bf16[512,512]{1,0:T(8,128)(2,1)S(1)} %collective-permute-done.8.rim, ...), custom_call_target="tpu_custom_call" | custom-call | flops 8589934592 | bytes 2621440 | tf_op jit(solution)/shard_map/graph_layer/pallas_call | solution.py:254
  52.8 0.1 collective-permute-start.14
  52.9 1.2 %collective-permute-start.15 = (bf16[512,512]{1,0:T(8,128)(2,1)S(1)}, bf16[512,512]{1,0:T(8,128)(2,1)S(1)}, u32[]{:S(2)}, u32[]{:S(2)}) collective-permute-start(bf16[512,512]{1,0:T(8,128)(2,1)S(1)} %graph_layer.4.own), channel_id=1, source_target_pairs={{1,4},{0,13},{5,8},{4,1},{9,12},{8,5},{13,0},{12,9},{3,6},{2,15},{... | collective-permute-start | bytes 1572872 | tf_op jit(solution)/shard_map/ppermute | solution.py:319
  54.1 0.1 collective-permute-done.11.near_w
  54.3 0.9 collective-permute-start.16
  55.1 1.0 %collective-permute-start.19 = (bf16[784,256]{1,0:T(8,128)(2,1)S(1)}, bf16[784,256]{1,0:T(8,128)(2,1)S(1)}, u32[]{:S(2)}, u32[]{:S(2)}) collective-permute-start(bf16[784,256]{1,0:T(8,128)(2,1)S(1)} %copy-done.17), channel_id=1, source_target_pairs={{0,2},{2,0},{1,3},{3,1},{4,6},{6,4},{5,7},{7,5},{8,10},{10,8},{9,1... | collective-permute-start | bytes 1204232 | tf_op jit(solution)/shard_map/ppermute | solution.py:308
  56.2 6.3 %graph_layer.5.own = bf16[512,512]{1,0:T(8,128)(2,1)S(1)} custom-call(s32[1]{0:T(128)} %bitcast.7.core_ref, s32[4096]{0:T(1024)S(1)} %bitcast.35, bf16[512,512]{1,0:T(8,128)(2,1)S(1)} %maximum_select_fusion.1.own, bf16[512,512]{1,0:T(8,128)(2,1)S(1)} %collective-permute-done.12.sib, bf16[512,512]{1,0:T(8,128)(2,1)S(1)} %collective-permute-done.13.rim, ...), custom_call_target="tpu_custom_call" | custom-call | flops 8589934592 | bytes 2621440 | tf_op jit(solution)/shard_map/graph_layer/pallas_call | solution.py:254
  62.4 0.5 collective-permute-start.20
  62.9 2.2 %collective-permute-start.21 = (bf16[512,512]{1,0:T(8,128)(2,1)S(1)}, bf16[512,512]{1,0:T(8,128)(2,1)S(1)}, u32[]{:S(2)}, u32[]{:S(2)}) collective-permute-start(bf16[512,512]{1,0:T(8,128)(2,1)S(1)} %graph_layer.5.own), channel_id=1, source_target_pairs={{1,4},{5,8},{4,1},{9,12},{8,5},{12,9},{3,6},{7,10},{6,3},{11,14},{... | collective-permute-start | bytes 1572872 | tf_op jit(solution)/shard_map/ppermute | solution.py:319
  65.2 0.8 collective-permute-done.15.rim
  66.0 6.3 %graph_layer.6 = (bf16[512,256]{1,0:T(8,128)(2,1)S(1)}, bf16[512,256]{1,0:T(8,128)(2,1)S(1)}) custom-call(s32[1]{0:T(128)} %bitcast.7.core_ref, s32[4096]{0:T(1024)S(1)} %bitcast.38, bf16[512,512]{1,0:T(8,128)(2,1)S(1)} %graph_layer.4.own, bf16[512,512]{1,0:T(8,128)(2,1)S(1)} %collective-permute-done.14.sib, ...), custom_call_target="tpu_custom_call" | custom-call | flops 1073741824 | bytes 2621440 | tf_op jit(solution)/shard_map/graph_layer/pallas_call | solution.py:254
  72.4 3.0 %collective-permute-start.22 = (bf16[784,256]{1,0:T(8,128)(2,1)S(1)}, bf16[784,256]{1,0:T(8,128)(2,1)S(1)}, u32[]{:S(2)}, u32[]{:S(2)}) collective-permute-start(bf16[784,256]{1,0:T(8,128)(2,1)S(1)} %collective-permute-done.19.near_w), channel_id=1, source_target_pairs={{0,1},{1,0},{2,3},{3,2},{4,5},{5,4},{6,7},{7,6},{8,9},{9,8},{10,11... | collective-permute-start | bytes 1204232 | tf_op jit(solution)/shard_map/ppermute | solution.py:308
  75.4 0.0 collective-permute-start.18
  75.4 4.1 %collective-permute-start.17 = (bf16[512,256]{1,0:T(8,128)(2,1)S(1)}, bf16[512,256]{1,0:T(8,128)(2,1)S(1)}, u32[]{:S(2)}, u32[]{:S(2)}) collective-permute-start(bf16[512,256]{1,0:T(8,128)(2,1)S(1)} %get-tuple-element.102), channel_id=1, source_target_pairs={{0,0},{1,2},{2,1},{3,3},{4,4},{5,6},{6,5},{7,7},{8,8},{9,10},{10,9... | collective-permute-start | bytes 786440 | tf_op jit(solution)/shard_map/ppermute | solution.py:298
  79.6 6.3 %graph_layer.7 = (bf16[512,256]{1,0:T(8,128)(2,1)S(1)}, bf16[512,256]{1,0:T(8,128)(2,1)S(1)}) custom-call(s32[1]{0:T(128)} %bitcast.7.core_ref, s32[4096]{0:T(1024)S(1)} %bitcast.36, bf16[512,512]{1,0:T(8,128)(2,1)S(1)} %graph_layer.5.own, bf16[512,512]{1,0:T(8,128)(2,1)S(1)} %collective-permute-done.20.sib, ...), custom_call_target="tpu_custom_call" | custom-call | flops 8589934592 | bytes 2621440 | tf_op jit(solution)/shard_map/graph_layer/pallas_call | solution.py:254
  85.9 1.9 %collective-permute-start.23 = (bf16[512,256]{1,0:T(8,128)(2,1)S(1)}, bf16[512,256]{1,0:T(8,128)(2,1)S(1)}, u32[]{:S(2)}, u32[]{:S(2)}) collective-permute-start(bf16[512,256]{1,0:T(8,128)(2,1)S(1)} %get-tuple-element.109), channel_id=1, source_target_pairs={{0,0},{1,2},{2,1},{3,3},{4,4},{5,6},{6,5},{7,7},{8,8},{9,10},{10,9... | collective-permute-start | bytes 786440 | tf_op jit(solution)/shard_map/ppermute | solution.py:298
  87.8 0.0 collective-permute-start.24
  87.9 1.0 %maximum_select_fusion.2 = bf16[1024,256]{1,0:T(8,128)(2,1)} fusion(bf16[512,256]{1,0:T(8,128)(2,1)S(1)} %collective-permute-done.18, bf16[512,256]{1,0:T(8,128)(2,1)S(1)} %collective-permute-done.17, pred[]{:T(512)S(6)} %eq.6), kind=kLoop, calls=%fused_computation.2 | loop fusion | flops 2359296 | bytes 1048577 | tf_op jit(solution)/shard_map/jit(_where)/select_n | solution.py:304
  88.9 7.0 %collective-permute-done.23 = bf16[512,256]{1,0:T(8,128)(2,1)S(1)} collective-permute-done((bf16[512,256]{1,0:T(8,128)(2,1)S(1)}, bf16[512,256]{1,0:T(8,128)(2,1)S(1)}, u32[]{:S(2)}, u32[]{:S(2)}) %collective-permute-start.23) | collective-permute-done | bytes 262176 | tf_op jit(solution)/shard_map/ppermute | solution.py:298
  95.9 1.0 %maximum_select_fusion.3 = bf16[1,1024,256]{2,1,0:T(8,128)(2,1)} fusion(bf16[1,512,256]{2,1,0:T(8,128)(2,1)S(1)} %bitcast.41, bf16[1,512,256]{2,1,0:T(8,128)(2,1)S(1)} %bitcast.40, pred[]{:T(512)S(6)} %eq.6), kind=kLoop, calls=%fused_computation.3 | loop fusion | flops 2359296 | bytes 1048577 | tf_op jit(solution)/shard_map/jit(_where)/select_n | solution.py:304
  (60 shorter events, 0.2 us)
Async XLA Ops:
  0.6 5.7 %copy-start.16 = (s32[512]{0:T(512)S(1)}, s32[512]{0:T(512)}, u32[]{:S(2)}) copy-start(s32[512]{0:T(512)} %param.23) | copy-start | bytes 6148
  0.6 6.4 %copy-start = (bf16[1,1024,256]{2,1,0:T(8,128)(2,1)S(1)}, bf16[1,1024,256]{2,1,0:T(8,128)(2,1)}, u32[]{:S(2)}) copy-start(bf16[1,1024,256]{2,1,0:T(8,128)(2,1)} %param.17) | copy-start | bytes 1572868
  1.8 15.3 %collective-permute-start = (bf16[512,256]{1,0:T(8,128)(2,1)S(1)}, bf16[512,256]{1,0:T(8,128)(2,1)S(1)}, u32[]{:S(2)}, u32[]{:S(2)}) collective-permute-start(bf16[512,256]{1,0:T(8,128)(2,1)S(1)} %get-tuple-element.115), channel_id=1, source_target_pairs={{0,0},{1,2},{2,1},{3,3},{4,4},{5,6},{6,5},{7,7},{8,8},{9,10},{10,9... | collective-permute-start | bytes 786440 | tf_op jit(solution)/shard_map/ppermute | solution.py:292
  6.3 11.0 %collective-permute-start.1 = (bf16[512,256]{1,0:T(8,128)(2,1)S(1)}, bf16[512,256]{1,0:T(8,128)(2,1)S(1)}, u32[]{:S(2)}, u32[]{:S(2)}) collective-permute-start(bf16[512,256]{1,0:T(8,128)(2,1)S(1)} %get-tuple-element.114), channel_id=1, source_target_pairs={{0,1},{1,3},{2,0},{3,2},{4,5},{5,7},{6,4},{7,6},{8,9},{9,11},{10,8... | collective-permute-start | bytes 786440 | tf_op jit(solution)/shard_map/ppermute | solution.py:293
  6.3 0.7 copy-start.15
  6.3 0.7 copy-start.14
  7.1 7.0 %copy-start.12 = (s32[1024]{0:T(1024)S(1)}, s32[1024]{0:T(1024)}, u32[]{:S(2)}) copy-start(s32[1024]{0:T(1024)} %param.20) | copy-start | bytes 12292
  7.1 7.0 %copy-start.13 = (s32[1024]{0:T(1024)S(1)}, s32[1024]{0:T(1024)}, u32[]{:S(2)}) copy-start(s32[1024]{0:T(1024)} %param.22) | copy-start | bytes 12292
  7.1 7.1 %copy-start.11 = (s32[1024,8]{0,1:T(8,128)S(1)}, s32[1024,8]{0,1:T(8,128)}, u32[]{:S(2)}) copy-start(s32[1024,8]{0,1:T(8,128)} %param.19) | copy-start | bytes 98308
  9.3 4.8 %copy-start.10 = (s32[1024,8]{0,1:T(8,128)S(1)}, s32[1024,8]{0,1:T(8,128)}, u32[]{:S(2)}) copy-start(s32[1024,8]{0,1:T(8,128)} %param.21) | copy-start | bytes 98308
  9.3 10.8 %collective-permute-start.2 = (bf16[272,256]{1,0:T(8,128)(2,1)S(1)}, bf16[272,256]{1,0:T(8,128)(2,1)S(1)}, u32[]{:S(2)}, u32[]{:S(2)}) collective-permute-start(bf16[272,256]{1,0:T(8,128)(2,1)S(1)} %get-tuple-element.68), channel_id=1, source_target_pairs={{0,4},{4,8},{8,12},{12,0},{1,5},{5,9},{9,13},{13,1},{2,6},{6,10},{... | collective-permute-start | bytes 417800 | tf_op jit(solution)/shard_map/ppermute | solution.py:393
  10.7 12.1 %collective-permute-start.3 = (bf16[272,256]{1,0:T(8,128)(2,1)S(1)}, bf16[272,256]{1,0:T(8,128)(2,1)S(1)}, u32[]{:S(2)}, u32[]{:S(2)}) collective-permute-start(bf16[272,256]{1,0:T(8,128)(2,1)S(1)} %get-tuple-element.69), channel_id=1, source_target_pairs={{0,8},{4,12},{8,0},{12,4},{1,9},{5,13},{9,1},{13,5},{2,10},{6,14},... | collective-permute-start | bytes 417800 | tf_op jit(solution)/shard_map/ppermute | solution.py:393
  13.0 9.8 %collective-permute-start.4 = (bf16[272,256]{1,0:T(8,128)(2,1)S(1)}, bf16[272,256]{1,0:T(8,128)(2,1)S(1)}, u32[]{:S(2)}, u32[]{:S(2)}) collective-permute-start(bf16[272,256]{1,0:T(8,128)(2,1)S(1)} %get-tuple-element.70), channel_id=1, source_target_pairs={{0,12},{4,0},{8,4},{12,8},{1,13},{5,1},{9,5},{13,9},{2,14},{6,2},{... | collective-permute-start | bytes 417800 | tf_op jit(solution)/shard_map/ppermute | solution.py:393
  17.1 23.7 %collective-permute-start.9 = (bf16[1568,256]{1,0:T(8,128)(2,1)}, bf16[1568,256]{1,0:T(8,128)(2,1)S(1)}, u32[]{:S(2)}, u32[]{:S(2)}) collective-permute-start(bf16[1568,256]{1,0:T(8,128)(2,1)} %pack_weights.2), channel_id=1, source_target_pairs={{0,2},{2,0},{1,3},{3,1},{4,6},{6,4},{5,7},{7,5},{8,10},{10,8},{9,1... | collective-permute-start | bytes 2408456 | tf_op jit(solution)/shard_map/ppermute | solution.py:308
  22.8 3.9 %copy-start.1 = (bf16[1,1024,256]{2,1,0:T(8,128)(2,1)S(1)}, bf16[1,1024,256]{2,1,0:T(8,128)(2,1)}, u32[]{:S(2)}) copy-start(bf16[1,1024,256]{2,1,0:T(8,128)(2,1)} %param.18) | copy-start | bytes 1572868
  23.0 17.9 %collective-permute-start.7 = (bf16[512,512]{1,0:T(8,128)(2,1)S(1)}, bf16[512,512]{1,0:T(8,128)(2,1)S(1)}, u32[]{:S(2)}, u32[]{:S(2)}) collective-permute-start(bf16[512,512]{1,0:T(8,128)(2,1)S(1)} %maximum_select_fusion.own), channel_id=1, source_target_pairs={{0,1},{1,0},{2,3},{3,2},{4,5},{5,4},{6,7},{7,6},{8,9},{9,8},{10,11... | collective-permute-start | bytes 1572872 | tf_op jit(solution)/shard_map/ppermute | solution.py:308
  23.6 17.2 %collective-permute-start.8 = (bf16[512,512]{1,0:T(8,128)(2,1)S(1)}, bf16[512,512]{1,0:T(8,128)(2,1)S(1)}, u32[]{:S(2)}, u32[]{:S(2)}) collective-permute-start(bf16[512,512]{1,0:T(8,128)(2,1)S(1)} %maximum_select_fusion.own), channel_id=1, source_target_pairs={{1,4},{0,13},{5,8},{4,1},{9,12},{8,5},{13,0},{12,9},{3,6},{2,15},{... | collective-permute-start | bytes 1572872 | tf_op jit(solution)/shard_map/ppermute | solution.py:319
  26.7 16.7 %copy-start.18 = (bf16[784,256]{1,0:T(8,128)(2,1)S(1)}, bf16[784,256]{1,0:T(8,128)(2,1)}, u32[]{:S(2)}) copy-start(bf16[784,256]{1,0:T(8,128)(2,1)} %get-tuple-element.91) | copy-start | bytes 1204228
  26.7 19.8 %copy-start.4 = (bf16[2,256,512]{2,1,0:T(8,128)(2,1)S(1)}, bf16[2,256,512]{2,1,0:T(8,128)(2,1)}, u32[]{:S(2)}) copy-start(bf16[2,256,512]{2,1,0:T(8,128)(2,1)} %w2_hbm.6) | copy-start | bytes 1572868
  27.5 19.1 %copy-start.8 = (bf16[2,256]{1,0:T(2,128)(2,1)S(1)}, bf16[2,256]{1,0:T(2,128)(2,1)}, u32[]{:S(2)}) copy-start(bf16[2,256]{1,0:T(2,128)(2,1)} %bias.6) | copy-start | bytes 3076
  27.5 19.1 %copy-start.2 = (bf16[2,512,256]{2,1,0:T(8,128)(2,1)S(1)}, bf16[2,512,256]{2,1,0:T(8,128)(2,1)}, u32[]{:S(2)}) copy-start(bf16[2,512,256]{2,1,0:T(8,128)(2,1)} %ws_hbm.6) | copy-start | bytes 1572868
  27.5 19.1 %copy-start.3 = (bf16[2,512,256]{2,1,0:T(8,128)(2,1)S(1)}, bf16[2,512,256]{2,1,0:T(8,128)(2,1)}, u32[]{:S(2)}) copy-start(bf16[2,512,256]{2,1,0:T(8,128)(2,1)} %wd_hbm.6) | copy-start | bytes 1572868
  27.5 12.6 %collective-permute-start.5 = (bf16[512,256]{1,0:T(8,128)(2,1)S(1)}, bf16[512,256]{1,0:T(8,128)(2,1)S(1)}, u32[]{:S(2)}, u32[]{:S(2)}) collective-permute-start(bf16[512,256]{1,0:T(8,128)(2,1)S(1)} %get-tuple-element.79), channel_id=1, source_target_pairs={{0,0},{1,2},{2,1},{3,3},{4,4},{5,6},{6,5},{7,7},{8,8},{9,10},{10,9... | collective-permute-start | bytes 786440 | tf_op jit(solution)/shard_map/ppermute | solution.py:292
  31.0 9.8 %collective-permute-start.6 = (bf16[512,256]{1,0:T(8,128)(2,1)S(1)}, bf16[512,256]{1,0:T(8,128)(2,1)S(1)}, u32[]{:S(2)}, u32[]{:S(2)}) collective-permute-start(bf16[512,256]{1,0:T(8,128)(2,1)S(1)} %get-tuple-element.80), channel_id=1, source_target_pairs={{0,1},{1,3},{2,0},{3,2},{4,5},{5,7},{6,4},{7,6},{8,9},{9,11},{10,8... | collective-permute-start | bytes 786440 | tf_op jit(solution)/shard_map/ppermute | solution.py:293
  40.8 5.7 %collective-permute-start.10 = (bf16[1568,256]{1,0:T(8,128)(2,1)S(1)}, bf16[1568,256]{1,0:T(8,128)(2,1)S(1)}, u32[]{:S(2)}, u32[]{:S(2)}) collective-permute-start(bf16[1568,256]{1,0:T(8,128)(2,1)S(1)} %collective-permute-done.9.near_w), channel_id=1, source_target_pairs={{0,1},{1,0},{2,3},{3,2},{4,5},{5,4},{6,7},{7,6},{8,9},{9,8},{10,11... | collective-permute-start | bytes 2408456 | tf_op jit(solution)/shard_map/ppermute | solution.py:308
  43.4 10.9 %collective-permute-start.11 = (bf16[784,256]{1,0:T(8,128)(2,1)S(1)}, bf16[784,256]{1,0:T(8,128)(2,1)S(1)}, u32[]{:S(2)}, u32[]{:S(2)}) collective-permute-start(bf16[784,256]{1,0:T(8,128)(2,1)S(1)} %copy-done.18), channel_id=1, source_target_pairs={{0,2},{2,0},{1,3},{3,1},{4,6},{6,4},{5,7},{7,5},{8,10},{10,8},{9,1... | collective-permute-start | bytes 1204232 | tf_op jit(solution)/shard_map/ppermute | solution.py:308
  43.6 11.6 %copy-start.17 = (bf16[784,256]{1,0:T(8,128)(2,1)S(1)}, bf16[784,256]{1,0:T(8,128)(2,1)}, u32[]{:S(2)}) copy-start(bf16[784,256]{1,0:T(8,128)(2,1)} %get-tuple-element.104) | copy-start | bytes 1204228
  43.6 12.6 %copy-start.5 = (bf16[2,512,256]{2,1,0:T(8,128)(2,1)S(1)}, bf16[2,512,256]{2,1,0:T(8,128)(2,1)}, u32[]{:S(2)}) copy-start(bf16[2,512,256]{2,1,0:T(8,128)(2,1)} %ws_hbm.7) | copy-start | bytes 1572868
  43.6 12.6 %copy-start.6 = (bf16[2,512,256]{2,1,0:T(8,128)(2,1)S(1)}, bf16[2,512,256]{2,1,0:T(8,128)(2,1)}, u32[]{:S(2)}) copy-start(bf16[2,512,256]{2,1,0:T(8,128)(2,1)} %wd_hbm.7) | copy-start | bytes 1572868
  43.6 12.5 %copy-start.7 = (bf16[2,256,512]{2,1,0:T(8,128)(2,1)S(1)}, bf16[2,256,512]{2,1,0:T(8,128)(2,1)}, u32[]{:S(2)}) copy-start(bf16[2,256,512]{2,1,0:T(8,128)(2,1)} %w2_hbm.7) | copy-start | bytes 1572868
  43.6 12.5 %copy-start.9 = (bf16[2,256]{1,0:T(2,128)(2,1)S(1)}, bf16[2,256]{1,0:T(2,128)(2,1)}, u32[]{:S(2)}) copy-start(bf16[2,256]{1,0:T(2,128)(2,1)} %bias.7) | copy-start | bytes 3076
  43.6 11.5 %collective-permute-start.12 = (bf16[512,512]{1,0:T(8,128)(2,1)S(1)}, bf16[512,512]{1,0:T(8,128)(2,1)S(1)}, u32[]{:S(2)}, u32[]{:S(2)}) collective-permute-start(bf16[512,512]{1,0:T(8,128)(2,1)S(1)} %maximum_select_fusion.1.own), channel_id=1, source_target_pairs={{0,1},{1,0},{2,3},{3,2},{4,5},{5,4},{6,7},{7,6},{8,9},{9,8},{10,11... | collective-permute-start | bytes 1572872 | tf_op jit(solution)/shard_map/ppermute | solution.py:308
  43.9 12.2 %collective-permute-start.13 = (bf16[512,512]{1,0:T(8,128)(2,1)S(1)}, bf16[512,512]{1,0:T(8,128)(2,1)S(1)}, u32[]{:S(2)}, u32[]{:S(2)}) collective-permute-start(bf16[512,512]{1,0:T(8,128)(2,1)S(1)} %maximum_select_fusion.1.own), channel_id=1, source_target_pairs={{1,4},{5,8},{4,1},{9,12},{8,5},{12,9},{3,6},{7,10},{6,3},{11,14},{... | collective-permute-start | bytes 1572872 | tf_op jit(solution)/shard_map/ppermute | solution.py:319
  52.8 12.3 %collective-permute-start.14 = (bf16[512,512]{1,0:T(8,128)(2,1)S(1)}, bf16[512,512]{1,0:T(8,128)(2,1)S(1)}, u32[]{:S(2)}, u32[]{:S(2)}) collective-permute-start(bf16[512,512]{1,0:T(8,128)(2,1)S(1)} %graph_layer.4.own), channel_id=1, source_target_pairs={{0,1},{1,0},{2,3},{3,2},{4,5},{5,4},{6,7},{7,6},{8,9},{9,8},{10,11... | collective-permute-start | bytes 1572872 | tf_op jit(solution)/shard_map/ppermute | solution.py:308
  52.9 13.1 %collective-permute-start.15 = (bf16[512,512]{1,0:T(8,128)(2,1)S(1)}, bf16[512,512]{1,0:T(8,128)(2,1)S(1)}, u32[]{:S(2)}, u32[]{:S(2)}) collective-permute-start(bf16[512,512]{1,0:T(8,128)(2,1)S(1)} %graph_layer.4.own), channel_id=1, source_target_pairs={{1,4},{0,13},{5,8},{4,1},{9,12},{8,5},{13,0},{12,9},{3,6},{2,15},{... | collective-permute-start | bytes 1572872 | tf_op jit(solution)/shard_map/ppermute | solution.py:319
  54.3 8.7 %collective-permute-start.16 = (bf16[784,256]{1,0:T(8,128)(2,1)S(1)}, bf16[784,256]{1,0:T(8,128)(2,1)S(1)}, u32[]{:S(2)}, u32[]{:S(2)}) collective-permute-start(bf16[784,256]{1,0:T(8,128)(2,1)S(1)} %collective-permute-done.11.near_w), channel_id=1, source_target_pairs={{0,1},{1,0},{2,3},{3,2},{4,5},{5,4},{6,7},{7,6},{8,9},{9,8},{10,11... | collective-permute-start | bytes 1204232 | tf_op jit(solution)/shard_map/ppermute | solution.py:308
  55.1 17.2 %collective-permute-start.19 = (bf16[784,256]{1,0:T(8,128)(2,1)S(1)}, bf16[784,256]{1,0:T(8,128)(2,1)S(1)}, u32[]{:S(2)}, u32[]{:S(2)}) collective-permute-start(bf16[784,256]{1,0:T(8,128)(2,1)S(1)} %copy-done.17), channel_id=1, source_target_pairs={{0,2},{2,0},{1,3},{3,1},{4,6},{6,4},{5,7},{7,5},{8,10},{10,8},{9,1... | collective-permute-start | bytes 1204232 | tf_op jit(solution)/shard_map/ppermute | solution.py:308
  62.4 17.1 %collective-permute-start.20 = (bf16[512,512]{1,0:T(8,128)(2,1)S(1)}, bf16[512,512]{1,0:T(8,128)(2,1)S(1)}, u32[]{:S(2)}, u32[]{:S(2)}) collective-permute-start(bf16[512,512]{1,0:T(8,128)(2,1)S(1)} %graph_layer.5.own), channel_id=1, source_target_pairs={{0,1},{1,0},{2,3},{3,2},{4,5},{5,4},{6,7},{7,6},{8,9},{9,8},{10,11... | collective-permute-start | bytes 1572872 | tf_op jit(solution)/shard_map/ppermute | solution.py:308
  62.9 16.6 %collective-permute-start.21 = (bf16[512,512]{1,0:T(8,128)(2,1)S(1)}, bf16[512,512]{1,0:T(8,128)(2,1)S(1)}, u32[]{:S(2)}, u32[]{:S(2)}) collective-permute-start(bf16[512,512]{1,0:T(8,128)(2,1)S(1)} %graph_layer.5.own), channel_id=1, source_target_pairs={{1,4},{5,8},{4,1},{9,12},{8,5},{12,9},{3,6},{7,10},{6,3},{11,14},{... | collective-permute-start | bytes 1572872 | tf_op jit(solution)/shard_map/ppermute | solution.py:319
  72.4 7.2 %collective-permute-start.22 = (bf16[784,256]{1,0:T(8,128)(2,1)S(1)}, bf16[784,256]{1,0:T(8,128)(2,1)S(1)}, u32[]{:S(2)}, u32[]{:S(2)}) collective-permute-start(bf16[784,256]{1,0:T(8,128)(2,1)S(1)} %collective-permute-done.19.near_w), channel_id=1, source_target_pairs={{0,1},{1,0},{2,3},{3,2},{4,5},{5,4},{6,7},{7,6},{8,9},{9,8},{10,11... | collective-permute-start | bytes 1204232 | tf_op jit(solution)/shard_map/ppermute | solution.py:308
  75.4 12.5 %collective-permute-start.18 = (bf16[512,256]{1,0:T(8,128)(2,1)S(1)}, bf16[512,256]{1,0:T(8,128)(2,1)S(1)}, u32[]{:S(2)}, u32[]{:S(2)}) collective-permute-start(bf16[512,256]{1,0:T(8,128)(2,1)S(1)} %get-tuple-element.103), channel_id=1, source_target_pairs={{0,2},{1,0},{2,3},{3,1},{4,6},{5,4},{6,7},{7,5},{8,10},{9,8},{10,1... | collective-permute-start | bytes 786440 | tf_op jit(solution)/shard_map/ppermute | solution.py:299
  75.4 12.5 %collective-permute-start.17 = (bf16[512,256]{1,0:T(8,128)(2,1)S(1)}, bf16[512,256]{1,0:T(8,128)(2,1)S(1)}, u32[]{:S(2)}, u32[]{:S(2)}) collective-permute-start(bf16[512,256]{1,0:T(8,128)(2,1)S(1)} %get-tuple-element.102), channel_id=1, source_target_pairs={{0,0},{1,2},{2,1},{3,3},{4,4},{5,6},{6,5},{7,7},{8,8},{9,10},{10,9... | collective-permute-start | bytes 786440 | tf_op jit(solution)/shard_map/ppermute | solution.py:298
  85.9 10.0 %collective-permute-start.23 = (bf16[512,256]{1,0:T(8,128)(2,1)S(1)}, bf16[512,256]{1,0:T(8,128)(2,1)S(1)}, u32[]{:S(2)}, u32[]{:S(2)}) collective-permute-start(bf16[512,256]{1,0:T(8,128)(2,1)S(1)} %get-tuple-element.109), channel_id=1, source_target_pairs={{0,0},{1,2},{2,1},{3,3},{4,4},{5,6},{6,5},{7,7},{8,8},{9,10},{10,9... | collective-permute-start | bytes 786440 | tf_op jit(solution)/shard_map/ppermute | solution.py:298
  87.8 8.0 %collective-permute-start.24 = (bf16[512,256]{1,0:T(8,128)(2,1)S(1)}, bf16[512,256]{1,0:T(8,128)(2,1)S(1)}, u32[]{:S(2)}, u32[]{:S(2)}) collective-permute-start(bf16[512,256]{1,0:T(8,128)(2,1)S(1)} %get-tuple-element.110), channel_id=1, source_target_pairs={{0,2},{1,0},{2,3},{3,1},{4,6},{5,4},{6,7},{7,5},{8,10},{9,8},{10,1... | collective-permute-start | bytes 786440 | tf_op jit(solution)/shard_map/ppermute | solution.py:299

commit v18 on v17

--- a/solution.py
+++ b/solution.py
@@ -392,6 +392,7 @@
     for k in range(1, parts):
         landed.append(lax.ppermute(pieces[k], "mesh", [(i, (i + k) % parts) for i in range(parts)]))
     landed[0], core1, packs[0], g_a, g_b = after((landed[0], core1, packs[0], g_a, g_b))
+    g_nbr, g_count, r_nbr, r_count, landed[1] = after((g_nbr, g_count, r_nbr, r_count, landed[1]))
     idx = edge_offsets(jnp.stack([g_nbr, r_nbr]), jnp.stack([g_count, r_count]), core)
     rest = tuple(((graph, layer),) for layer in range(1, layers) for graph in (0, 1))
     packs += pack_weights(rest, core1, g_weights, g_b1, r_weights, r_b1)

time: 97.3 us -> 97.2 us (level)
  no operation moved by 1% of the time
where the time goes in v18:
time: 97.2 us; the launch traced here: 96.7 us
  starting transfers between devices  37.2 us (38%)
  Pallas kernels  33.9 us (35%)
  waiting for transfers between devices  19.8 us (20%)
  other arithmetic  2.4 us (2%)
  local copies, waits for them, and re-layouts  2.36 us (2%)
  between operations  1.13 us (1%)
    pallas_call x4, Pallas kernels, run_layer(): pl.pallas_call(functools.partial(layer_kernel, layer, place, slots, last)...  25.2 us
    ppermute x4, starting transfers between devices, rims(): return lax.ppermute(own, ('mesh', 'batch'), pairs)  9.19 us
    ppermute x10, starting transfers between devices, swap(): return lax.ppermute(values, axis, [(0, 1), (1, 0)])  9.08 us
    ppermute x2, waiting for transfers between devices, spread_rows(): a = lax.ppermute(same, ('mp', 'batch'), [(0, 0), (1, 2), (2, 1), (3, 3)])  8.66 us
    ppermute x2, starting transfers between devices, spread_rows(): a = lax.ppermute(same, ('mp', 'batch'), [(0, 0), (1, 2), (2, 1), (3, 3)])  8.04 us
    ppermute x2, waiting for transfers between devices, gather_rows(): same = lax.ppermute(a, ('mp', 'batch'), [(0, 0), (1, 2), (2, 1), (3, 3)])  6.97 us
    ppermute x2, starting transfers between devices, gather_rows(): same = lax.ppermute(a, ('mp', 'batch'), [(0, 0), (1, 2), (2, 1), (3, 3)])  6.04 us
    pallas_call x2, Pallas kernels, pack_weights(): pl.pallas_call(functools.partial(pack_kernel, plan), out_shape=tuple((jax...  5.72 us
  transfers between devices with their start and end apart: 25, of which 6 were waited for; matrix products, arithmetic and copies ran while one was open for 1% of the time, Pallas kernels for 35%

profile of v18, /device:TPU:1, one launch (start us, length us, event | category | flops | bytes accessed | tf_op | source)
XLA Modules:
  0.0 96.7 jit_solution(6561326530405818524)
XLA Ops:
  0.7 1.1 %dynamic-slice_bitcast_fusion = (bf16[512,256]{1,0:T(8,128)(2,1)S(1)}, bf16[512,256]{1,0:T(8,128)(2,1)S(1)}) fusion(bf16[1,1024,256]{2,1,0:T(8,128)(2,1)} %param.17, s32[]{:T(128)S(6)} %select_n.78, s32[]{:T(128)S(6)} %select_n.77), kind=kLoop, calls=%fused_computation.4 | loop fusion | bytes 1048584 | tf_op jit(solution)/shard_map/dynamic_slice | solution.py:383
  1.8 4.5 %collective-permute-start = (bf16[512,256]{1,0:T(8,128)(2,1)S(1)}, bf16[512,256]{1,0:T(8,128)(2,1)S(1)}, u32[]{:S(2)}, u32[]{:S(2)}) collective-permute-start(bf16[512,256]{1,0:T(8,128)(2,1)S(1)} %get-tuple-element.125), channel_id=1, source_target_pairs={{0,0},{1,2},{2,1},{3,3},{4,4},{5,6},{6,5},{7,7},{8,8},{9,10},{10,9... | collective-permute-start | bytes 786440 | tf_op jit(solution)/shard_map/ppermute | solution.py:292
  6.3 0.0 collective-permute-start.1
  6.3 0.0 copy-start.14
  6.4 0.7 copy-done.15
  7.0 0.0 copy-done.14
  7.1 2.3 %pick_rows.1 = (bf16[272,256]{1,0:T(8,128)(2,1)S(1)}, bf16[272,256]{1,0:T(8,128)(2,1)S(1)}, bf16[272,256]{1,0:T(8,128)(2,1)S(1)}, bf16[272,256]{1,0:T(8,128)(2,1)S(1)}) custom-call(s32[1]{0:T(128)} %bitcast.me_ref, s32[3,512]{1,0:T(4,128)S(1)} %pad_add_fusion.bnd_ref, bf16[1024,256]{1,0:T(8,128)(2,1)S(1)} %bitcast.33), custom_call_target="tpu_custom_call" | custom-call | flops 8589934592 | bytes 1 | tf_op jit(solution)/shard_map/pick_rows/pallas_call | solution.py:115
  9.3 1.3 %collective-permute-start.2 = (bf16[272,256]{1,0:T(8,128)(2,1)S(1)}, bf16[272,256]{1,0:T(8,128)(2,1)S(1)}, u32[]{:S(2)}, u32[]{:S(2)}) collective-permute-start(bf16[272,256]{1,0:T(8,128)(2,1)S(1)} %get-tuple-element.70), channel_id=1, source_target_pairs={{0,4},{4,8},{8,12},{12,0},{1,5},{5,9},{9,13},{13,1},{2,6},{6,10},{... | collective-permute-start | bytes 417800 | tf_op jit(solution)/shard_map/ppermute | solution.py:393
  10.7 2.3 %collective-permute-start.3 = (bf16[272,256]{1,0:T(8,128)(2,1)S(1)}, bf16[272,256]{1,0:T(8,128)(2,1)S(1)}, u32[]{:S(2)}, u32[]{:S(2)}) collective-permute-start(bf16[272,256]{1,0:T(8,128)(2,1)S(1)} %get-tuple-element.79), channel_id=1, source_target_pairs={{0,8},{4,12},{8,0},{12,4},{1,9},{5,13},{9,1},{13,5},{2,10},{6,14},... | collective-permute-start | bytes 417800 | tf_op jit(solution)/shard_map/ppermute | solution.py:393
  13.0 1.1 %collective-permute-start.4 = (bf16[272,256]{1,0:T(8,128)(2,1)S(1)}, bf16[272,256]{1,0:T(8,128)(2,1)S(1)}, u32[]{:S(2)}, u32[]{:S(2)}) collective-permute-start(bf16[272,256]{1,0:T(8,128)(2,1)S(1)} %get-tuple-element.80), channel_id=1, source_target_pairs={{0,12},{4,0},{8,4},{12,8},{1,13},{5,1},{9,5},{13,9},{2,14},{6,2},{... | collective-permute-start | bytes 417800 | tf_op jit(solution)/shard_map/ppermute | solution.py:393
  14.1 2.9 %pack_weights.2 = bf16[1568,256]{1,0:T(8,128)(2,1)} custom-call(s32[1]{0:T(128)} %bitcast.7.core_ref, bf16[2,256]{1,0:T(2,128)(2,1)} %bias.6, bf16[2,256]{1,0:T(2,128)(2,1)} %bias.7, bf16[2,512,256]{2,1,0:T(8,128)(2,1)} %ws_hbm.6, bf16[2,512,256]{2,1,0:T(8,128)(2,1)} %wd_hbm.6, bf16[2,256,512]{2,1,0:T(8,128)(2,1)} %w2_hbm.6, bf16[2,512,256]{2,1,0:T(8,128)(2,1)} %ws_hbm.7, ...), custom_call_target="tpu_custom_call" | custom-call | flops 4294967296 | bytes 1 | tf_op jit(solution)/shard_map/pack_weights/pallas_call | solution.py:352
  17.0 0.2 collective-permute-start.9
  17.2 0.1 fusion.5
  17.3 0.5 copy-done.10
  17.8 2.8 %pack_weights.3 = (bf16[784,256]{1,0:T(8,128)(2,1)}, bf16[784,256]{1,0:T(8,128)(2,1)}) custom-call(s32[1]{0:T(128)} %bitcast.7.core_ref, bf16[2,256]{1,0:T(2,128)(2,1)} %bias.6, bf16[2,256]{1,0:T(2,128)(2,1)} %bias.7, bf16[2,512,256]{2,1,0:T(8,128)(2,1)} %ws_hbm.6, bf16[2,512,256]{2,1,0:T(8,128)(2,1)} %wd_hbm.6, bf16[2,256,512]{2,1,0:T(8,128)(2,1)} %w2_hbm.6, ...), custom_call_target="tpu_custom_call" | custom-call | flops 4294967296 | bytes 1 | tf_op jit(solution)/shard_map/pack_weights/pallas_call | solution.py:352
  20.6 2.2 %collective-permute-done.3.refs_2_ = bf16[272,256]{1,0:T(8,128)(2,1)S(1)} collective-permute-done((bf16[272,256]{1,0:T(8,128)(2,1)S(1)}, bf16[272,256]{1,0:T(8,128)(2,1)S(1)}, u32[]{:S(2)}, u32[]{:S(2)}) %collective-permute-start.3) | collective-permute-done | bytes 139296 | tf_op jit(solution)/shard_map/ppermute | solution.py:393
  22.8 0.1 maximum_select_fusion.own
  22.9 0.7 collective-permute-start.7
  23.6 3.1 %collective-permute-start.8 = (bf16[512,512]{1,0:T(8,128)(2,1)S(1)}, bf16[512,512]{1,0:T(8,128)(2,1)S(1)}, u32[]{:S(2)}, u32[]{:S(2)}) collective-permute-start(bf16[512,512]{1,0:T(8,128)(2,1)S(1)} %maximum_select_fusion.own), channel_id=1, source_target_pairs={{1,4},{0,13},{5,8},{4,1},{9,12},{8,5},{13,0},{12,9},{3,6},{2,15},{... | collective-permute-start | bytes 1572872 | tf_op jit(solution)/shard_map/ppermute | solution.py:319
  26.7 0.7 add_force.1
  27.5 3.5 %collective-permute-start.5 = (bf16[512,256]{1,0:T(8,128)(2,1)S(1)}, bf16[512,256]{1,0:T(8,128)(2,1)S(1)}, u32[]{:S(2)}, u32[]{:S(2)}) collective-permute-start(bf16[512,256]{1,0:T(8,128)(2,1)S(1)} %get-tuple-element.89), channel_id=1, source_target_pairs={{0,0},{1,2},{2,1},{3,3},{4,4},{5,6},{6,5},{7,7},{8,8},{9,10},{10,9... | collective-permute-start | bytes 786440 | tf_op jit(solution)/shard_map/ppermute | solution.py:292
  31.0 0.0 collective-permute-start.6
  31.0 8.7 %collective-permute-done.5 = bf16[512,256]{1,0:T(8,128)(2,1)S(1)} collective-permute-done((bf16[512,256]{1,0:T(8,128)(2,1)S(1)}, bf16[512,256]{1,0:T(8,128)(2,1)S(1)}, u32[]{:S(2)}, u32[]{:S(2)}) %collective-permute-start.5) | collective-permute-done | bytes 262176 | tf_op jit(solution)/shard_map/ppermute | solution.py:292
  39.7 1.0 %collective-permute-done.6 = bf16[512,256]{1,0:T(8,128)(2,1)S(1)} collective-permute-done((bf16[512,256]{1,0:T(8,128)(2,1)S(1)}, bf16[512,256]{1,0:T(8,128)(2,1)S(1)}, u32[]{:S(2)}, u32[]{:S(2)}) %collective-permute-start.6) | collective-permute-done | bytes 262176 | tf_op jit(solution)/shard_map/ppermute | solution.py:293
  40.7 2.6 %collective-permute-start.10 = (bf16[1568,256]{1,0:T(8,128)(2,1)S(1)}, bf16[1568,256]{1,0:T(8,128)(2,1)S(1)}, u32[]{:S(2)}, u32[]{:S(2)}) collective-permute-start(bf16[1568,256]{1,0:T(8,128)(2,1)S(1)} %collective-permute-done.9.near_w), channel_id=1, source_target_pairs={{0,1},{1,0},{2,3},{3,2},{4,5},{5,4},{6,7},{7,6},{8,9},{9,8},{10,11... | collective-permute-start | bytes 2408456 | tf_op jit(solution)/shard_map/ppermute | solution.py:308
  43.3 0.1 maximum_select_fusion.1.own
  43.5 0.3 collective-permute-start.12
  43.7 2.6 %collective-permute-start.13 = (bf16[512,512]{1,0:T(8,128)(2,1)S(1)}, bf16[512,512]{1,0:T(8,128)(2,1)S(1)}, u32[]{:S(2)}, u32[]{:S(2)}) collective-permute-start(bf16[512,512]{1,0:T(8,128)(2,1)S(1)} %maximum_select_fusion.1.own), channel_id=1, source_target_pairs={{1,4},{5,8},{4,1},{9,12},{8,5},{12,9},{3,6},{7,10},{6,3},{11,14},{... | collective-permute-start | bytes 1572872 | tf_op jit(solution)/shard_map/ppermute | solution.py:319
  46.4 6.3 %graph_layer.4.own = bf16[512,512]{1,0:T(8,128)(2,1)S(1)} custom-call(s32[1]{0:T(128)} %bitcast.7.core_ref, s32[4096]{0:T(1024)S(1)} %bitcast.37, bf16[512,512]{1,0:T(8,128)(2,1)S(1)} %maximum_select_fusion.own, bf16[512,512]{1,0:T(8,128)(2,1)S(1)} %collective-permute-done.7.sib, bf16[512,512]{1,0:T(8,128)(2,1)S(1)} %collective-permute-done.8.rim, ...), custom_call_target="tpu_custom_call" | custom-call | flops 8589934592 | bytes 2621440 | tf_op jit(solution)/shard_map/graph_layer/pallas_call | solution.py:254
  52.7 0.1 collective-permute-start.14
  52.8 1.2 %collective-permute-start.15 = (bf16[512,512]{1,0:T(8,128)(2,1)S(1)}, bf16[512,512]{1,0:T(8,128)(2,1)S(1)}, u32[]{:S(2)}, u32[]{:S(2)}) collective-permute-start(bf16[512,512]{1,0:T(8,128)(2,1)S(1)} %graph_layer.4.own), channel_id=1, source_target_pairs={{1,4},{0,13},{5,8},{4,1},{9,12},{8,5},{13,0},{12,9},{3,6},{2,15},{... | collective-permute-start | bytes 1572872 | tf_op jit(solution)/shard_map/ppermute | solution.py:319
  54.0 0.1 collective-permute-done.11.near_w
  54.1 0.9 collective-permute-start.16
  55.0 1.0 collective-permute-start.19
  56.0 6.3 %graph_layer.5.own = bf16[512,512]{1,0:T(8,128)(2,1)S(1)} custom-call(s32[1]{0:T(128)} %bitcast.7.core_ref, s32[4096]{0:T(1024)S(1)} %bitcast.35, bf16[512,512]{1,0:T(8,128)(2,1)S(1)} %maximum_select_fusion.1.own, bf16[512,512]{1,0:T(8,128)(2,1)S(1)} %collective-permute-done.12.sib, bf16[512,512]{1,0:T(8,128)(2,1)S(1)} %collective-permute-done.13.rim, ...), custom_call_target="tpu_custom_call" | custom-call | flops 8589934592 | bytes 2621440 | tf_op jit(solution)/shard_map/graph_layer/pallas_call | solution.py:254
  62.3 0.5 collective-permute-start.20
  62.8 2.2 %collective-permute-start.21 = (bf16[512,512]{1,0:T(8,128)(2,1)S(1)}, bf16[512,512]{1,0:T(8,128)(2,1)S(1)}, u32[]{:S(2)}, u32[]{:S(2)}) collective-permute-start(bf16[512,512]{1,0:T(8,128)(2,1)S(1)} %graph_layer.5.own), channel_id=1, source_target_pairs={{1,4},{5,8},{4,1},{9,12},{8,5},{12,9},{3,6},{7,10},{6,3},{11,14},{... | collective-permute-start | bytes 1572872 | tf_op jit(solution)/shard_map/ppermute | solution.py:319
  65.0 0.8 collective-permute-done.15.rim
  65.9 6.3 %graph_layer.6 = (bf16[512,256]{1,0:T(8,128)(2,1)S(1)}, bf16[512,256]{1,0:T(8,128)(2,1)S(1)}) custom-call(s32[1]{0:T(128)} %bitcast.7.core_ref, s32[4096]{0:T(1024)S(1)} %bitcast.38, bf16[512,512]{1,0:T(8,128)(2,1)S(1)} %graph_layer.4.own, bf16[512,512]{1,0:T(8,128)(2,1)S(1)} %collective-permute-done.14.sib, ...), custom_call_target="tpu_custom_call" | custom-call | flops 1073741824 | bytes 2621440 | tf_op jit(solution)/shard_map/graph_layer/pallas_call | solution.py:254
  72.2 3.0 %collective-permute-start.22 = (bf16[784,256]{1,0:T(8,128)(2,1)S(1)}, bf16[784,256]{1,0:T(8,128)(2,1)S(1)}, u32[]{:S(2)}, u32[]{:S(2)}) collective-permute-start(bf16[784,256]{1,0:T(8,128)(2,1)S(1)} %collective-permute-done.19.near_w), channel_id=1, source_target_pairs={{0,1},{1,0},{2,3},{3,2},{4,5},{5,4},{6,7},{7,6},{8,9},{9,8},{10,11... | collective-permute-start | bytes 1204232 | tf_op jit(solution)/shard_map/ppermute | solution.py:308
  75.2 0.0 collective-permute-start.18
  75.3 4.1 %collective-permute-start.17 = (bf16[512,256]{1,0:T(8,128)(2,1)S(1)}, bf16[512,256]{1,0:T(8,128)(2,1)S(1)}, u32[]{:S(2)}, u32[]{:S(2)}) collective-permute-start(bf16[512,256]{1,0:T(8,128)(2,1)S(1)} %get-tuple-element.112), channel_id=1, source_target_pairs={{0,0},{1,2},{2,1},{3,3},{4,4},{5,6},{6,5},{7,7},{8,8},{9,10},{10,9... | collective-permute-start | bytes 786440 | tf_op jit(solution)/shard_map/ppermute | solution.py:298
  79.4 6.3 %graph_layer.7 = (bf16[512,256]{1,0:T(8,128)(2,1)S(1)}, bf16[512,256]{1,0:T(8,128)(2,1)S(1)}) custom-call(s32[1]{0:T(128)} %bitcast.7.core_ref, s32[4096]{0:T(1024)S(1)} %bitcast.36, bf16[512,512]{1,0:T(8,128)(2,1)S(1)} %graph_layer.5.own, bf16[512,512]{1,0:T(8,128)(2,1)S(1)} %collective-permute-done.20.sib, ...), custom_call_target="tpu_custom_call" | custom-call | flops 8589934592 | bytes 2621440 | tf_op jit(solution)/shard_map/graph_layer/pallas_call | solution.py:254
  85.7 1.9 %collective-permute-start.23 = (bf16[512,256]{1,0:T(8,128)(2,1)S(1)}, bf16[512,256]{1,0:T(8,128)(2,1)S(1)}, u32[]{:S(2)}, u32[]{:S(2)}) collective-permute-start(bf16[512,256]{1,0:T(8,128)(2,1)S(1)} %get-tuple-element.119), channel_id=1, source_target_pairs={{0,0},{1,2},{2,1},{3,3},{4,4},{5,6},{6,5},{7,7},{8,8},{9,10},{10,9... | collective-permute-start | bytes 786440 | tf_op jit(solution)/shard_map/ppermute | solution.py:298
  87.7 0.0 collective-permute-start.24
  87.7 1.0 %maximum_select_fusion.2 = bf16[1024,256]{1,0:T(8,128)(2,1)} fusion(bf16[512,256]{1,0:T(8,128)(2,1)S(1)} %collective-permute-done.18, bf16[512,256]{1,0:T(8,128)(2,1)S(1)} %collective-permute-done.17, pred[]{:T(512)S(6)} %eq.6), kind=kLoop, calls=%fused_computation.2 | loop fusion | flops 2359296 | bytes 1048577 | tf_op jit(solution)/shard_map/jit(_where)/select_n | solution.py:304
  88.8 7.0 %collective-permute-done.23 = bf16[512,256]{1,0:T(8,128)(2,1)S(1)} collective-permute-done((bf16[512,256]{1,0:T(8,128)(2,1)S(1)}, bf16[512,256]{1,0:T(8,128)(2,1)S(1)}, u32[]{:S(2)}, u32[]{:S(2)}) %collective-permute-start.23) | collective-permute-done | bytes 262176 | tf_op jit(solution)/shard_map/ppermute | solution.py:298
  95.7 1.0 %maximum_select_fusion.3 = bf16[1,1024,256]{2,1,0:T(8,128)(2,1)} fusion(bf16[1,512,256]{2,1,0:T(8,128)(2,1)S(1)} %bitcast.41, bf16[1,512,256]{2,1,0:T(8,128)(2,1)S(1)} %bitcast.40, pred[]{:T(512)S(6)} %eq.6), kind=kLoop, calls=%fused_computation.3 | loop fusion | flops 2359296 | bytes 1048577 | tf_op jit(solution)/shard_map/jit(_where)/select_n | solution.py:304
  (60 shorter events, 0.2 us)
Async XLA Ops:
  0.6 5.7 %copy-start.16 = (s32[512]{0:T(512)S(1)}, s32[512]{0:T(512)}, u32[]{:S(2)}) copy-start(s32[512]{0:T(512)} %param.23) | copy-start | bytes 6148
  0.6 6.4 %copy-start = (bf16[1,1024,256]{2,1,0:T(8,128)(2,1)S(1)}, bf16[1,1024,256]{2,1,0:T(8,128)(2,1)}, u32[]{:S(2)}) copy-start(bf16[1,1024,256]{2,1,0:T(8,128)(2,1)} %param.17) | copy-start | bytes 1572868
  1.8 16.0 %collective-permute-start = (bf16[512,256]{1,0:T(8,128)(2,1)S(1)}, bf16[512,256]{1,0:T(8,128)(2,1)S(1)}, u32[]{:S(2)}, u32[]{:S(2)}) collective-permute-start(bf16[512,256]{1,0:T(8,128)(2,1)S(1)} %get-tuple-element.125), channel_id=1, source_target_pairs={{0,0},{1,2},{2,1},{3,3},{4,4},{5,6},{6,5},{7,7},{8,8},{9,10},{10,9... | collective-permute-start | bytes 786440 | tf_op jit(solution)/shard_map/ppermute | solution.py:292
  6.3 11.5 %collective-permute-start.1 = (bf16[512,256]{1,0:T(8,128)(2,1)S(1)}, bf16[512,256]{1,0:T(8,128)(2,1)S(1)}, u32[]{:S(2)}, u32[]{:S(2)}) collective-permute-start(bf16[512,256]{1,0:T(8,128)(2,1)S(1)} %get-tuple-element.124), channel_id=1, source_target_pairs={{0,1},{1,3},{2,0},{3,2},{4,5},{5,7},{6,4},{7,6},{8,9},{9,11},{10,8... | collective-permute-start | bytes 786440 | tf_op jit(solution)/shard_map/ppermute | solution.py:293
  6.3 0.7 copy-start.15
  6.3 0.7 copy-start.14
  9.3 7.7 %collective-permute-start.2 = (bf16[272,256]{1,0:T(8,128)(2,1)S(1)}, bf16[272,256]{1,0:T(8,128)(2,1)S(1)}, u32[]{:S(2)}, u32[]{:S(2)}) collective-permute-start(bf16[272,256]{1,0:T(8,128)(2,1)S(1)} %get-tuple-element.70), channel_id=1, source_target_pairs={{0,4},{4,8},{8,12},{12,0},{1,5},{5,9},{9,13},{13,1},{2,6},{6,10},{... | collective-permute-start | bytes 417800 | tf_op jit(solution)/shard_map/ppermute | solution.py:393
  10.7 12.1 %collective-permute-start.3 = (bf16[272,256]{1,0:T(8,128)(2,1)S(1)}, bf16[272,256]{1,0:T(8,128)(2,1)S(1)}, u32[]{:S(2)}, u32[]{:S(2)}) collective-permute-start(bf16[272,256]{1,0:T(8,128)(2,1)S(1)} %get-tuple-element.79), channel_id=1, source_target_pairs={{0,8},{4,12},{8,0},{12,4},{1,9},{5,13},{9,1},{13,5},{2,10},{6,14},... | collective-permute-start | bytes 417800 | tf_op jit(solution)/shard_map/ppermute | solution.py:393
  13.0 9.8 %collective-permute-start.4 = (bf16[272,256]{1,0:T(8,128)(2,1)S(1)}, bf16[272,256]{1,0:T(8,128)(2,1)S(1)}, u32[]{:S(2)}, u32[]{:S(2)}) collective-permute-start(bf16[272,256]{1,0:T(8,128)(2,1)S(1)} %get-tuple-element.80), channel_id=1, source_target_pairs={{0,12},{4,0},{8,4},{12,8},{1,13},{5,1},{9,5},{13,9},{2,14},{6,2},{... | collective-permute-start | bytes 417800 | tf_op jit(solution)/shard_map/ppermute | solution.py:393
  14.1 3.1 %copy-start.12 = (s32[1024]{0:T(1024)S(1)}, s32[1024]{0:T(1024)}, u32[]{:S(2)}) copy-start(s32[1024]{0:T(1024)} %param.20) | copy-start | bytes 12292
  14.1 3.1 %copy-start.13 = (s32[1024]{0:T(1024)S(1)}, s32[1024]{0:T(1024)}, u32[]{:S(2)}) copy-start(s32[1024]{0:T(1024)} %param.22) | copy-start | bytes 12292
  14.1 3.2 %copy-start.11 = (s32[1024,8]{0,1:T(8,128)S(1)}, s32[1024,8]{0,1:T(8,128)}, u32[]{:S(2)}) copy-start(s32[1024,8]{0,1:T(8,128)} %param.19) | copy-start | bytes 98308
  16.9 0.8 copy-start.10
  17.0 23.7 %collective-permute-start.9 = (bf16[1568,256]{1,0:T(8,128)(2,1)}, bf16[1568,256]{1,0:T(8,128)(2,1)S(1)}, u32[]{:S(2)}, u32[]{:S(2)}) collective-permute-start(bf16[1568,256]{1,0:T(8,128)(2,1)} %pack_weights.2), channel_id=1, source_target_pairs={{0,2},{2,0},{1,3},{3,1},{4,6},{6,4},{5,7},{7,5},{8,10},{10,8},{9,1... | collective-permute-start | bytes 2408456 | tf_op jit(solution)/shard_map/ppermute | solution.py:308
  22.8 3.9 %copy-start.1 = (bf16[1,1024,256]{2,1,0:T(8,128)(2,1)S(1)}, bf16[1,1024,256]{2,1,0:T(8,128)(2,1)}, u32[]{:S(2)}) copy-start(bf16[1,1024,256]{2,1,0:T(8,128)(2,1)} %param.18) | copy-start | bytes 1572868
  22.9 17.8 %collective-permute-start.7 = (bf16[512,512]{1,0:T(8,128)(2,1)S(1)}, bf16[512,512]{1,0:T(8,128)(2,1)S(1)}, u32[]{:S(2)}, u32[]{:S(2)}) collective-permute-start(bf16[512,512]{1,0:T(8,128)(2,1)S(1)} %maximum_select_fusion.own), channel_id=1, source_target_pairs={{0,1},{1,0},{2,3},{3,2},{4,5},{5,4},{6,7},{7,6},{8,9},{9,8},{10,11... | collective-permute-start | bytes 1572872 | tf_op jit(solution)/shard_map/ppermute | solution.py:308
  23.6 17.1 %collective-permute-start.8 = (bf16[512,512]{1,0:T(8,128)(2,1)S(1)}, bf16[512,512]{1,0:T(8,128)(2,1)S(1)}, u32[]{:S(2)}, u32[]{:S(2)}) collective-permute-start(bf16[512,512]{1,0:T(8,128)(2,1)S(1)} %maximum_select_fusion.own), channel_id=1, source_target_pairs={{1,4},{0,13},{5,8},{4,1},{9,12},{8,5},{13,0},{12,9},{3,6},{2,15},{... | collective-permute-start | bytes 1572872 | tf_op jit(solution)/shard_map/ppermute | solution.py:319
  26.7 16.6 %copy-start.18 = (bf16[784,256]{1,0:T(8,128)(2,1)S(1)}, bf16[784,256]{1,0:T(8,128)(2,1)}, u32[]{:S(2)}) copy-start(bf16[784,256]{1,0:T(8,128)(2,1)} %get-tuple-element.101) | copy-start | bytes 1204228
  26.7 19.7 %copy-start.4 = (bf16[2,256,512]{2,1,0:T(8,128)(2,1)S(1)}, bf16[2,256,512]{2,1,0:T(8,128)(2,1)}, u32[]{:S(2)}) copy-start(bf16[2,256,512]{2,1,0:T(8,128)(2,1)} %w2_hbm.6) | copy-start | bytes 1572868
  27.4 19.0 %copy-start.8 = (bf16[2,256]{1,0:T(2,128)(2,1)S(1)}, bf16[2,256]{1,0:T(2,128)(2,1)}, u32[]{:S(2)}) copy-start(bf16[2,256]{1,0:T(2,128)(2,1)} %bias.6) | copy-start | bytes 3076
  27.5 18.9 %copy-start.2 = (bf16[2,512,256]{2,1,0:T(8,128)(2,1)S(1)}, bf16[2,512,256]{2,1,0:T(8,128)(2,1)}, u32[]{:S(2)}) copy-start(bf16[2,512,256]{2,1,0:T(8,128)(2,1)} %ws_hbm.6) | copy-start | bytes 1572868
  27.5 18.9 %copy-start.3 = (bf16[2,512,256]{2,1,0:T(8,128)(2,1)S(1)}, bf16[2,512,256]{2,1,0:T(8,128)(2,1)}, u32[]{:S(2)}) copy-start(bf16[2,512,256]{2,1,0:T(8,128)(2,1)} %wd_hbm.6) | copy-start | bytes 1572868
  27.5 12.2 %collective-permute-start.5 = (bf16[512,256]{1,0:T(8,128)(2,1)S(1)}, bf16[512,256]{1,0:T(8,128)(2,1)S(1)}, u32[]{:S(2)}, u32[]{:S(2)}) collective-permute-start(bf16[512,256]{1,0:T(8,128)(2,1)S(1)} %get-tuple-element.89), channel_id=1, source_target_pairs={{0,0},{1,2},{2,1},{3,3},{4,4},{5,6},{6,5},{7,7},{8,8},{9,10},{10,9... | collective-permute-start | bytes 786440 | tf_op jit(solution)/shard_map/ppermute | solution.py:292
  31.0 9.7 %collective-permute-start.6 = (bf16[512,256]{1,0:T(8,128)(2,1)S(1)}, bf16[512,256]{1,0:T(8,128)(2,1)S(1)}, u32[]{:S(2)}, u32[]{:S(2)}) collective-permute-start(bf16[512,256]{1,0:T(8,128)(2,1)S(1)} %get-tuple-element.90), channel_id=1, source_target_pairs={{0,1},{1,3},{2,0},{3,2},{4,5},{5,7},{6,4},{7,6},{8,9},{9,11},{10,8... | collective-permute-start | bytes 786440 | tf_op jit(solution)/shard_map/ppermute | solution.py:293
  40.7 5.6 %collective-permute-start.10 = (bf16[1568,256]{1,0:T(8,128)(2,1)S(1)}, bf16[1568,256]{1,0:T(8,128)(2,1)S(1)}, u32[]{:S(2)}, u32[]{:S(2)}) collective-permute-start(bf16[1568,256]{1,0:T(8,128)(2,1)S(1)} %collective-permute-done.9.near_w), channel_id=1, source_target_pairs={{0,1},{1,0},{2,3},{3,2},{4,5},{5,4},{6,7},{7,6},{8,9},{9,8},{10,11... | collective-permute-start | bytes 2408456 | tf_op jit(solution)/shard_map/ppermute | solution.py:308
  43.3 10.9 %collective-permute-start.11 = (bf16[784,256]{1,0:T(8,128)(2,1)S(1)}, bf16[784,256]{1,0:T(8,128)(2,1)S(1)}, u32[]{:S(2)}, u32[]{:S(2)}) collective-permute-start(bf16[784,256]{1,0:T(8,128)(2,1)S(1)} %copy-done.18), channel_id=1, source_target_pairs={{0,2},{2,0},{1,3},{3,1},{4,6},{6,4},{5,7},{7,5},{8,10},{10,8},{9,1... | collective-permute-start | bytes 1204232 | tf_op jit(solution)/shard_map/ppermute | solution.py:308
  43.4 11.6 %copy-start.17 = (bf16[784,256]{1,0:T(8,128)(2,1)S(1)}, bf16[784,256]{1,0:T(8,128)(2,1)}, u32[]{:S(2)}) copy-start(bf16[784,256]{1,0:T(8,128)(2,1)} %get-tuple-element.114) | copy-start | bytes 1204228
  43.4 12.6 %copy-start.5 = (bf16[2,512,256]{2,1,0:T(8,128)(2,1)S(1)}, bf16[2,512,256]{2,1,0:T(8,128)(2,1)}, u32[]{:S(2)}) copy-start(bf16[2,512,256]{2,1,0:T(8,128)(2,1)} %ws_hbm.7) | copy-start | bytes 1572868
  43.4 12.5 %copy-start.6 = (bf16[2,512,256]{2,1,0:T(8,128)(2,1)S(1)}, bf16[2,512,256]{2,1,0:T(8,128)(2,1)}, u32[]{:S(2)}) copy-start(bf16[2,512,256]{2,1,0:T(8,128)(2,1)} %wd_hbm.7) | copy-start | bytes 1572868
  43.4 12.5 %copy-start.7 = (bf16[2,256,512]{2,1,0:T(8,128)(2,1)S(1)}, bf16[2,256,512]{2,1,0:T(8,128)(2,1)}, u32[]{:S(2)}) copy-start(bf16[2,256,512]{2,1,0:T(8,128)(2,1)} %w2_hbm.7) | copy-start | bytes 1572868
  43.5 12.5 %copy-start.9 = (bf16[2,256]{1,0:T(2,128)(2,1)S(1)}, bf16[2,256]{1,0:T(2,128)(2,1)}, u32[]{:S(2)}) copy-start(bf16[2,256]{1,0:T(2,128)(2,1)} %bias.7) | copy-start | bytes 3076
  43.5 11.5 %collective-permute-start.12 = (bf16[512,512]{1,0:T(8,128)(2,1)S(1)}, bf16[512,512]{1,0:T(8,128)(2,1)S(1)}, u32[]{:S(2)}, u32[]{:S(2)}) collective-permute-start(bf16[512,512]{1,0:T(8,128)(2,1)S(1)} %maximum_select_fusion.1.own), channel_id=1, source_target_pairs={{0,1},{1,0},{2,3},{3,2},{4,5},{5,4},{6,7},{7,6},{8,9},{9,8},{10,11... | collective-permute-start | bytes 1572872 | tf_op jit(solution)/shard_map/ppermute | solution.py:308
  43.7 12.2 %collective-permute-start.13 = (bf16[512,512]{1,0:T(8,128)(2,1)S(1)}, bf16[512,512]{1,0:T(8,128)(2,1)S(1)}, u32[]{:S(2)}, u32[]{:S(2)}) collective-permute-start(bf16[512,512]{1,0:T(8,128)(2,1)S(1)} %maximum_select_fusion.1.own), channel_id=1, source_target_pairs={{1,4},{5,8},{4,1},{9,12},{8,5},{12,9},{3,6},{7,10},{6,3},{11,14},{... | collective-permute-start | bytes 1572872 | tf_op jit(solution)/shard_map/ppermute | solution.py:319
  52.7 12.3 %collective-permute-start.14 = (bf16[512,512]{1,0:T(8,128)(2,1)S(1)}, bf16[512,512]{1,0:T(8,128)(2,1)S(1)}, u32[]{:S(2)}, u32[]{:S(2)}) collective-permute-start(bf16[512,512]{1,0:T(8,128)(2,1)S(1)} %graph_layer.4.own), channel_id=1, source_target_pairs={{0,1},{1,0},{2,3},{3,2},{4,5},{5,4},{6,7},{7,6},{8,9},{9,8},{10,11... | collective-permute-start | bytes 1572872 | tf_op jit(solution)/shard_map/ppermute | solution.py:308
  52.8 13.1 %collective-permute-start.15 = (bf16[512,512]{1,0:T(8,128)(2,1)S(1)}, bf16[512,512]{1,0:T(8,128)(2,1)S(1)}, u32[]{:S(2)}, u32[]{:S(2)}) collective-permute-start(bf16[512,512]{1,0:T(8,128)(2,1)S(1)} %graph_layer.4.own), channel_id=1, source_target_pairs={{1,4},{0,13},{5,8},{4,1},{9,12},{8,5},{13,0},{12,9},{3,6},{2,15},{... | collective-permute-start | bytes 1572872 | tf_op jit(solution)/shard_map/ppermute | solution.py:319
  54.1 8.7 %collective-permute-start.16 = (bf16[784,256]{1,0:T(8,128)(2,1)S(1)}, bf16[784,256]{1,0:T(8,128)(2,1)S(1)}, u32[]{:S(2)}, u32[]{:S(2)}) collective-permute-start(bf16[784,256]{1,0:T(8,128)(2,1)S(1)} %collective-permute-done.11.near_w), channel_id=1, source_target_pairs={{0,1},{1,0},{2,3},{3,2},{4,5},{5,4},{6,7},{7,6},{8,9},{9,8},{10,11... | collective-permute-start | bytes 1204232 | tf_op jit(solution)/shard_map/ppermute | solution.py:308
  55.0 17.2 %collective-permute-start.19 = (bf16[784,256]{1,0:T(8,128)(2,1)S(1)}, bf16[784,256]{1,0:T(8,128)(2,1)S(1)}, u32[]{:S(2)}, u32[]{:S(2)}) collective-permute-start(bf16[784,256]{1,0:T(8,128)(2,1)S(1)} %copy-done.17), channel_id=1, source_target_pairs={{0,2},{2,0},{1,3},{3,1},{4,6},{6,4},{5,7},{7,5},{8,10},{10,8},{9,1... | collective-permute-start | bytes 1204232 | tf_op jit(solution)/shard_map/ppermute | solution.py:308
  62.3 17.1 %collective-permute-start.20 = (bf16[512,512]{1,0:T(8,128)(2,1)S(1)}, bf16[512,512]{1,0:T(8,128)(2,1)S(1)}, u32[]{:S(2)}, u32[]{:S(2)}) collective-permute-start(bf16[512,512]{1,0:T(8,128)(2,1)S(1)} %graph_layer.5.own), channel_id=1, source_target_pairs={{0,1},{1,0},{2,3},{3,2},{4,5},{5,4},{6,7},{7,6},{8,9},{9,8},{10,11... | collective-permute-start | bytes 1572872 | tf_op jit(solution)/shard_map/ppermute | solution.py:308
  62.8 16.6 %collective-permute-start.21 = (bf16[512,512]{1,0:T(8,128)(2,1)S(1)}, bf16[512,512]{1,0:T(8,128)(2,1)S(1)}, u32[]{:S(2)}, u32[]{:S(2)}) collective-permute-start(bf16[512,512]{1,0:T(8,128)(2,1)S(1)} %graph_layer.5.own), channel_id=1, source_target_pairs={{1,4},{5,8},{4,1},{9,12},{8,5},{12,9},{3,6},{7,10},{6,3},{11,14},{... | collective-permute-start | bytes 1572872 | tf_op jit(solution)/shard_map/ppermute | solution.py:319
  72.2 7.2 %collective-permute-start.22 = (bf16[784,256]{1,0:T(8,128)(2,1)S(1)}, bf16[784,256]{1,0:T(8,128)(2,1)S(1)}, u32[]{:S(2)}, u32[]{:S(2)}) collective-permute-start(bf16[784,256]{1,0:T(8,128)(2,1)S(1)} %collective-permute-done.19.near_w), channel_id=1, source_target_pairs={{0,1},{1,0},{2,3},{3,2},{4,5},{5,4},{6,7},{7,6},{8,9},{9,8},{10,11... | collective-permute-start | bytes 1204232 | tf_op jit(solution)/shard_map/ppermute | solution.py:308
  75.2 12.5 %collective-permute-start.18 = (bf16[512,256]{1,0:T(8,128)(2,1)S(1)}, bf16[512,256]{1,0:T(8,128)(2,1)S(1)}, u32[]{:S(2)}, u32[]{:S(2)}) collective-permute-start(bf16[512,256]{1,0:T(8,128)(2,1)S(1)} %get-tuple-element.113), channel_id=1, source_target_pairs={{0,2},{1,0},{2,3},{3,1},{4,6},{5,4},{6,7},{7,5},{8,10},{9,8},{10,1... | collective-permute-start | bytes 786440 | tf_op jit(solution)/shard_map/ppermute | solution.py:299
  75.3 12.5 %collective-permute-start.17 = (bf16[512,256]{1,0:T(8,128)(2,1)S(1)}, bf16[512,256]{1,0:T(8,128)(2,1)S(1)}, u32[]{:S(2)}, u32[]{:S(2)}) collective-permute-start(bf16[512,256]{1,0:T(8,128)(2,1)S(1)} %get-tuple-element.112), channel_id=1, source_target_pairs={{0,0},{1,2},{2,1},{3,3},{4,4},{5,6},{6,5},{7,7},{8,8},{9,10},{10,9... | collective-permute-start | bytes 786440 | tf_op jit(solution)/shard_map/ppermute | solution.py:298
  85.7 10.0 %collective-permute-start.23 = (bf16[512,256]{1,0:T(8,128)(2,1)S(1)}, bf16[512,256]{1,0:T(8,128)(2,1)S(1)}, u32[]{:S(2)}, u32[]{:S(2)}) collective-permute-start(bf16[512,256]{1,0:T(8,128)(2,1)S(1)} %get-tuple-element.119), channel_id=1, source_target_pairs={{0,0},{1,2},{2,1},{3,3},{4,4},{5,6},{6,5},{7,7},{8,8},{9,10},{10,9... | collective-permute-start | bytes 786440 | tf_op jit(solution)/shard_map/ppermute | solution.py:298
  87.7 8.0 %collective-permute-start.24 = (bf16[512,256]{1,0:T(8,128)(2,1)S(1)}, bf16[512,256]{1,0:T(8,128)(2,1)S(1)}, u32[]{:S(2)}, u32[]{:S(2)}) collective-permute-start(bf16[512,256]{1,0:T(8,128)(2,1)S(1)} %get-tuple-element.120), channel_id=1, source_target_pairs={{0,2},{1,0},{2,3},{3,1},{4,6},{5,4},{6,7},{7,5},{8,10},{9,8},{10,1... | collective-permute-start | bytes 786440 | tf_op jit(solution)/shard_map/ppermute | solution.py:299
